TPU v7x, 32 devices: a whole 2x2x4 slice. The times are simulated.
32 devices in a mesh: ctx: 16 (over z, y, x), head: 2 (over core), batch: 1.
Axes of the slice: x: 2, y: 2, z: 4, core: 2. Of those that a mesh axis runs over, the one named last changes fastest.
Arguments:
- queries: bfloat16 [1, 4096, 8, 256], P('batch', 'ctx', 'head'), may hold values from -6 to 6
- keys: bfloat16 [1, 4096, 8, 256], P('batch', 'ctx', 'head'), may hold values from -6 to 6
- values: bfloat16 [1, 4096, 8, 256], P('batch', 'ctx', 'head'), may hold values from -6 to 6
- rates: float32 [1, 8, 4096], P('batch', 'head', 'ctx'), may hold values from 0.25 to 4
- head_scale: float32 [8], P('head'), may hold values from 0.3 to 3
- gain: float32 [8, 256], P('head'), may hold values from 0.25 to 1.75
- w_gate: float32 [8, 256, 256], P('head'), may hold values from -0.375 to 0.375
- w_out: float32 [8, 256, 256], P('head'), may hold values from -0.375 to 0.375
- w_up: float32 [8, 256, 256], P('head'), may hold values from -0.375 to 0.375
- cotangent: bfloat16 [1, 4096, 8, 256], P('batch', 'ctx', 'head'), may hold values from -6 to 6
Outputs:
- grad_q: bfloat16 [1, 4096, 8, 256], P('batch', 'ctx', 'head')
- grad_k: bfloat16 [1, 4096, 8, 256], P('batch', 'ctx', 'head')
- grad_v: bfloat16 [1, 4096, 8, 256], P('batch', 'ctx', 'head')
- grad_gate: float32 [8, 256, 256], P('head', ('ctx', 'batch'))
- grad_out: float32 [8, 256, 256], P('head', ('ctx', 'batch'))
- grad_up: float32 [8, 256, 256], P('head', ('ctx', 'batch'))
All inputs are finite; a program needn't handle non-finite values.
Results may differ from a plain program's by a relative error of at most 0.019.
Values sent between devices are 32-bit elements; how exact they have to be, the bound alone decides.
No kernel may reach another device: no remote copies, remote signals or barrier semaphores. Data moves between devices by JAX's collectives and lax.ppermute only.
A program may use at most 64 MiB of HBM per device.

v0:
```python
import math

import jax
import jax.numpy as jnp
from jax import lax
from jax.sharding import PartitionSpec as P


def silu(x):
    return x * jax.nn.sigmoid(x)


def update_terms(keys, values, rates, w_gate, w_out, w_up, scale):
    gate_b = w_gate.astype(jnp.bfloat16)
    up_b = w_up.astype(jnp.bfloat16)
    out_b = w_out.astype(jnp.bfloat16)
    first = jnp.dot(keys, gate_b, preferred_element_type=jnp.float32)
    third = jnp.dot(keys, up_b, preferred_element_type=jnp.float32)
    sig = jax.nn.sigmoid(first)
    activ = first * sig
    act = (activ * third).astype(jnp.bfloat16)
    scaled = (rates[:, None] * values.astype(jnp.float32)).astype(jnp.bfloat16)
    dact = jnp.dot(scaled, out_b.T, preferred_element_type=jnp.float32)
    deriv = sig * (1.0 + first * (1.0 - sig))
    dfirst = (dact * third * deriv).astype(jnp.bfloat16)
    dthird = (dact * activ).astype(jnp.bfloat16)
    upd_gate = jnp.dot(keys.T, dfirst, preferred_element_type=jnp.float32) * scale
    upd_out = jnp.dot(act.T, scaled, preferred_element_type=jnp.float32) * scale
    upd_up = jnp.dot(keys.T, dthird, preferred_element_type=jnp.float32) * scale
    return (upd_gate, upd_out, upd_up)


def update_back(keys, values, rates, w_gate, w_out, w_up, scale, cots):

    def forward(k_in, v_in, g_in, o_in, u_in):
        return update_terms(k_in, v_in, rates, g_in, o_in, u_in, scale)

    primal, pull = jax.vjp(forward, keys, values, w_gate, w_out, w_up)
    return pull(cots)


def apply_terms(queries, w_gate, w_out, w_up):
    first = jnp.dot(queries, w_gate.astype(jnp.bfloat16), preferred_element_type=jnp.float32)
    third = jnp.dot(queries, w_up.astype(jnp.bfloat16), preferred_element_type=jnp.float32)
    hidden = (silu(first) * third).astype(jnp.bfloat16)
    return jnp.dot(hidden, w_out.astype(jnp.bfloat16), preferred_element_type=jnp.float32)


def apply_back(queries, w_gate, w_out, w_up, dout):
    primal, pull = jax.vjp(apply_terms, queries, w_gate, w_out, w_up)
    return pull(dout)


def norm_back(scaled, dyg, sq, ps, count, head_scale):
    inv = lax.rsqrt(sq / count + 1e-06)
    dos = inv[None, :, None] * dyg - scaled * (inv**3 * ps / count)[None, :, None]
    return dos * head_scale[:, None, None]


def local(queries, keys, values, rates, head_scale, gain, w_gate, w_out, w_up, cotangent):
    local_heads = keys.shape[2]
    width = keys.shape[3]
    scale = 1.0 / math.sqrt(keys.shape[1] * lax.axis_size("ctx") * width)
    count = float(local_heads * lax.axis_size("head") * width)
    pieces = [
        update_terms(
            keys[0, :, hh], values[0, :, hh], rates[0, hh], w_gate[hh], w_out[hh], w_up[hh], scale
        )
        for hh in range(local_heads)
    ]
    upd = [jnp.stack([p[i] for p in pieces]) for i in range(3)]
    summed = lax.psum((upd[0], upd[1], upd[2]), "ctx")
    new_gate = w_gate + summed[0]
    new_out = w_out + summed[1]
    new_up = w_up + summed[2]
    outs = jnp.stack(
        [
            apply_terms(queries[0, :, hh], new_gate[hh], new_out[hh], new_up[hh])
            for hh in range(local_heads)
        ]
    )
    scaled = outs * head_scale[:, None, None]
    dyg = jnp.swapaxes(cotangent[0], 0, 1).astype(jnp.float32) * gain[:, None, :]
    sq, ps = lax.psum(
        (jnp.sum(scaled * scaled, axis=(0, 2)), jnp.sum(scaled * dyg, axis=(0, 2))), "head"
    )
    dout = norm_back(scaled, dyg, sq, ps, count, head_scale)
    backs = [
        apply_back(queries[0, :, hh], new_gate[hh], new_out[hh], new_up[hh], dout[hh])
        for hh in range(local_heads)
    ]
    grad_q = jnp.stack([b[0] for b in backs], axis=1)
    part = [jnp.stack([b[i] for b in backs]) for i in range(1, 4)]
    whole = lax.psum((part[0], part[1], part[2]), "ctx")
    returns = [
        update_back(
            keys[0, :, hh],
            values[0, :, hh],
            rates[0, hh],
            w_gate[hh],
            w_out[hh],
            w_up[hh],
            scale,
            (whole[0][hh], whole[1][hh], whole[2][hh]),
        )
        for hh in range(local_heads)
    ]
    grad_k = jnp.stack([b[0] for b in returns], axis=1)
    grad_v = jnp.stack([b[1] for b in returns], axis=1)
    local_gate = part[0] + jnp.stack([b[2] for b in returns])
    local_out = part[1] + jnp.stack([b[3] for b in returns])
    local_up = part[2] + jnp.stack([b[4] for b in returns])
    totals = (
        lax.psum_scatter(local_gate, ("ctx", "batch"), scatter_dimension=1, tiled=True),
        lax.psum_scatter(local_out, ("ctx", "batch"), scatter_dimension=1, tiled=True),
        lax.psum_scatter(local_up, ("ctx", "batch"), scatter_dimension=1, tiled=True),
    )
    return (grad_q[None], grad_k[None], grad_v[None], totals[0], totals[1], totals[2])


def solution(mesh):
    in_specs = (
        P("batch", "ctx", "head", None),
        P("batch", "ctx", "head", None),
        P("batch", "ctx", "head", None),
        P("batch", "head", "ctx"),
        P("head"),
        P("head", None),
        P("head", None, None),
        P("head", None, None),
        P("head", None, None),
        P("batch", "ctx", "head", None),
    )
    out_specs = (
        P("batch", "ctx", "head", None),
        P("batch", "ctx", "head", None),
        P("batch", "ctx", "head", None),
        P("head", ("ctx", "batch"), None),
        P("head", ("ctx", "batch"), None),
        P("head", ("ctx", "batch"), None),
    )
    return jax.shard_map(local, mesh=mesh, in_specs=in_specs, out_specs=out_specs, check_vma=False)
```

profile of v0, /device:TPU:0, one launch (start us, length us, event | category | flops | bytes accessed | tf_op | source)
XLA Modules:
  0.0 552.7 jit_solution(6558932636205848293)
XLA Ops:
  7.2 2.8 fusion.365
  10.8 0.8 fusion.366
  13.1 1.0 multiply_convert_fusion.12
  15.7 1.0 multiply_convert_fusion.13
  18.4 1.1 multiply_convert_fusion.14
  21.1 1.0 multiply_convert_fusion.15
  24.9 1.0 pad_maximum_fusion
  25.9 1.1 pad_maximum_fusion.1
  27.0 1.0 pad_maximum_fusion.2
  28.1 2.5 copy.106
  30.7 1.3 copy.109
  32.0 2.2 copy.120
  36.4 142.2 %all-reduce.15.cloned.1.call-done = (f32[4,256,256]{1,2,0:T(8,128)}, f32[4,256,256]{1,2,0:T(8,128)}, f32[4,256,256]{2,1,0:T(8,128)}) async-done(((f32[4,256,256]{1,2,0:T(8,128)}, f32[4,256,256]{1,2,0:T(8,128)}, f32[4,256,256]{2,1,0:T(8,128)}), (f32[4,256,256]{1,2,0:T(8,128)}, f32[4,256,256]{1,2,0:T(8,128)}, f32[4,256,256]{2,1,0:T(8,128)})) %all-reduce.15.cloned.1.call-update) | async-done | bytes 3145744 | tf_op jit(solution)/shard_map/psum | solution.py:72
  178.7 1.5 add.105
  182.4 0.9 multiply_convert_fusion
  183.3 0.9 multiply_convert_fusion.1
  186.1 0.9 multiply_convert_fusion.2
  188.2 0.9 multiply_convert_fusion.7
  190.2 0.9 multiply_reduce_fusion
  191.1 3.3 all-reduce.6
  195.8 1.7 fusion.108
  199.8 0.8 copy-done.137
  208.7 1.1 maximum_convert_fusion.2
  209.7 1.1 maximum_convert_fusion
  210.9 1.0 maximum_convert_fusion.1
  212.0 1.2 dynamic-slice
  213.9 1.1 convolution_convert_fusion.60
  215.1 1.3 fusion.43
  216.6 0.8 copy-done.135
  218.5 0.8 copy-done.144
  220.4 0.8 copy-done.141
  221.4 1.2 copy.140
  222.6 136.3 %all-reduce.13.cloned.1.call-done = (f32[4,256,256]{1,2,0:T(8,128)}, f32[4,256,256]{1,2,0:T(8,128)}, f32[4,256,256]{1,2,0:T(8,128)}) async-done(((f32[4,256,256]{1,2,0:T(8,128)}, f32[4,256,256]{1,2,0:T(8,128)}, f32[4,256,256]{1,2,0:T(8,128)}), (f32[4,256,256]{1,2,0:T(8,128)}, f32[4,256,256]{1,2,0:T(8,128)}, f32[4,256,256]{1,2,0:T(8,128)})) %all-reduce.13.cloned.1.call-update) | async-done | bytes 3145744 | tf_op jit(solution)/shard_map/psum | solution.py:94
  358.9 1.3 fusion.16
  360.2 1.8 convolution_convert_fusion.25
  362.0 1.3 fusion.21
  364.4 0.8 convolution_convert_fusion.32
  367.7 1.1 multiply_add_fusion
  369.0 0.9 convolution_convert_fusion.20
  370.8 1.1 multiply_add_fusion.1
  371.9 0.9 convolution_convert_fusion.27
  373.8 1.1 multiply_add_fusion.2
  374.8 0.9 convolution_convert_fusion.34
  375.9 0.9 convolution_convert_fusion.22
  376.8 0.9 fusion.103
  377.7 0.9 convolution_convert_fusion.29
  378.6 0.9 fusion.102
  379.5 0.9 convolution_convert_fusion.36
  380.3 0.9 fusion.101
  381.3 1.1 multiply_add_fusion.3
  384.3 1.3 copy.133
  389.8 1.3 copy.138
  392.2 1.3 convert_add_fusion
  393.5 1.4 copy.139
  394.8 1.2 copy-done.51
  396.1 1.2 fusion.71
  397.3 1.3 fusion.67
  400.7 1.2 convolution_convert_fusion.41
  404.1 1.2 copy.141
  411.9 1.2 copy.142
  413.1 128.6 %all-reduce.11.cloned.1.call-done = (f32[4,256,256]{2,0,1:T(4,128)}, f32[4,256,256]{2,0,1:T(4,128)}, f32[4,256,256]{2,0,1:T(4,128)}) async-done(((f32[4,256,256]{2,0,1:T(4,128)}, f32[4,256,256]{2,0,1:T(4,128)}, f32[4,256,256]{2,0,1:T(4,128)}), (f32[4,256,256]{2,0,1:T(4,128)}, f32[4,256,256]{2,0,1:T(4,128)}, f32[4,256,256]{2,0,1:T(4,128)})) %all-reduce.11.cloned.1.call-update) | async-done | bytes 3145744
  541.7 0.8 constant_dynamic-slice_fusion.2
  543.2 0.8 constant_dynamic-slice_fusion.1
  544.7 0.8 constant_dynamic-slice_fusion
  (442 shorter events, 57.7 us)
Async XLA Ops:
  7.2 171.5 %all-reduce.15.cloned.1.call-start = ((), (), s32[]{:S(2)}) async-start(), calls=%async_computation.2 | async-start | bytes 6291456 | tf_op jit(solution)/shard_map/psum | solution.py:72
  7.2 3.5 copy-start.22
  11.5 1.6 copy-start.5
  14.2 8.6 %copy-start.78 = (bf16[256,256]{1,0:T(8,128)(2,1)}, bf16[256,256]{1,0:T(8,128)(2,1)S(1)}, u32[]{:S(2)}) copy-start(bf16[256,256]{1,0:T(8,128)(2,1)S(1)} %get-tuple-element.68) | copy-start | bytes 393220
  14.2 9.5 %copy-start.70 = (bf16[256,256]{1,0:T(8,128)(2,1)}, bf16[256,256]{1,0:T(8,128)(2,1)S(1)}, u32[]{:S(2)}) copy-start(bf16[256,256]{1,0:T(8,128)(2,1)S(1)} %get-tuple-element.67) | copy-start | bytes 393220
  14.8 348.6 %copy-start.11 = (bf16[1,256,1,256]{3,1,2,0:T(8,128)(2,1)}, bf16[1,256,1,256]{3,1,2,0:T(8,128)(2,1)S(1)}, u32[]{:S(2)}) copy-start(bf16[1,256,1,256]{3,1,2,0:T(8,128)(2,1)S(1)} %copy.174) | copy-start | bytes 393220
  16.8 6.2 %copy-start.80 = (bf16[256,256]{1,0:T(8,128)(2,1)}, bf16[256,256]{1,0:T(8,128)(2,1)S(1)}, u32[]{:S(2)}) copy-start(bf16[256,256]{1,0:T(8,128)(2,1)S(1)} %get-tuple-element.66) | copy-start | bytes 393220
  16.8 7.2 %copy-start.72 = (bf16[256,256]{1,0:T(8,128)(2,1)}, bf16[256,256]{1,0:T(8,128)(2,1)S(1)}, u32[]{:S(2)}) copy-start(bf16[256,256]{1,0:T(8,128)(2,1)S(1)} %get-tuple-element.65) | copy-start | bytes 393220
  17.5 348.0 %copy-start.13 = (bf16[1,256,1,256]{3,1,2,0:T(8,128)(2,1)}, bf16[1,256,1,256]{3,1,2,0:T(8,128)(2,1)S(1)}, u32[]{:S(2)}) copy-start(bf16[1,256,1,256]{3,1,2,0:T(8,128)(2,1)S(1)} %copy.172) | copy-start | bytes 393220
  19.5 3.7 copy-start.82
  19.5 4.8 copy-start.74
  20.1 4.4 copy-start.15
  22.1 2.5 copy-start.76
  28.1 330.8 %all-reduce.13.cloned.1.call-start = ((), (), s32[]{:S(2)}) async-start(), calls=%async_computation.1 | async-start | bytes 6291456 | tf_op jit(solution)/shard_map/psum | solution.py:94
  32.0 2.2 copy-start.23
  178.7 1.5 copy-start.10
  178.7 1.9 copy-start.53
  180.1 9.0 %copy-start.24 = (bf16[4,256,256]{2,1,0:T(8,128)(2,1)}, bf16[4,256,256]{2,1,0:T(8,128)(2,1)S(1)}, u32[]{:S(2)}) copy-start(bf16[4,256,256]{2,1,0:T(8,128)(2,1)S(1)} %add.105) | copy-start | bytes 1572868
  180.7 1.5 copy-start.9
  181.9 1.5 copy-start.133
  182.4 5.8 %copy-start.54 = (bf16[4,256,256]{1,2,0:T(8,128)(2,1)}, bf16[4,256,256]{1,2,0:T(8,128)(2,1)S(1)}, u32[]{:S(2)}) copy-start(bf16[4,256,256]{1,2,0:T(8,128)(2,1)S(1)} %add.104) | copy-start | bytes 1572868
  184.5 4.9 copy-start.18
  185.2 4.2 copy-start.19
  187.6 1.8 copy-start.20
  188.2 1.6 copy-start.145
  195.8 1.7 copy-start.102
  198.4 10.2 %copy-start.26 = (bf16[1,256,256]{1,2,0:T(8,128)(2,1)}, bf16[1,256,256]{1,2,0:T(8,128)(2,1)S(1)}, u32[]{:S(2)}) copy-start(bf16[1,256,256]{1,2,0:T(8,128)(2,1)S(1)} %fusion.59) | copy-start | bytes 393220
  198.6 10.0 %copy-start.28 = (bf16[1,256,256]{1,2,0:T(8,128)(2,1)}, bf16[1,256,256]{1,2,0:T(8,128)(2,1)S(1)}, u32[]{:S(2)}) copy-start(bf16[1,256,256]{1,2,0:T(8,128)(2,1)S(1)} %fusion.58) | copy-start | bytes 393220
  199.6 9.0 %copy-start.30 = (bf16[1,256,256]{1,2,0:T(8,128)(2,1)}, bf16[1,256,256]{1,2,0:T(8,128)(2,1)S(1)}, u32[]{:S(2)}) copy-start(bf16[1,256,256]{1,2,0:T(8,128)(2,1)S(1)} %fusion.57) | copy-start | bytes 393220
  199.8 8.8 %copy-start.32 = (bf16[1,256,256]{1,2,0:T(8,128)(2,1)}, bf16[1,256,256]{1,2,0:T(8,128)(2,1)S(1)}, u32[]{:S(2)}) copy-start(bf16[1,256,256]{1,2,0:T(8,128)(2,1)S(1)} %fusion.56) | copy-start | bytes 393220
  200.9 3.1 copy-start.170
  200.9 6.7 %copy-start.69 = (bf16[256,256]{1,0:T(8,128)(2,1)}, bf16[256,256]{1,0:T(8,128)(2,1)S(1)}, u32[]{:S(2)}) copy-start(bf16[256,256]{1,0:T(8,128)(2,1)S(1)} %get-tuple-element.95) | copy-start | bytes 393220
  201.9 3.0 copy-start.168
  201.9 5.9 %copy-start.67 = (bf16[256,256]{1,0:T(8,128)(2,1)}, bf16[256,256]{1,0:T(8,128)(2,1)S(1)}, u32[]{:S(2)}) copy-start(bf16[256,256]{1,0:T(8,128)(2,1)S(1)} %get-tuple-element.97) | copy-start | bytes 393220
  203.0 2.9 copy-start.166
  203.0 5.2 copy-start.65
  204.0 2.7 copy-start.164
  204.0 4.4 copy-start.63
  204.9 4.8 copy-start.56
  205.8 3.9 copy-start.58
  206.7 3.0 copy-start.60
  207.6 2.1 copy-start.62
  207.9 3.0 copy-start.34
  208.1 2.7 copy-start.36
  208.4 2.5 copy-start.38
  208.6 2.2 copy-start.40
  211.9 329.8 %all-reduce.11.cloned.1.call-start = ((), (), s32[]{:S(2)}) async-start(), calls=%async_computation | async-start | bytes 6291456
  215.0 1.5 copy-start.55
  215.1 1.5 copy-start.169
  221.4 138.7 %copy-start.114 = (bf16[256,256]{1,0:T(8,128)(2,1)S(1)}, bf16[256,256]{1,0:T(8,128)(2,1)}, u32[]{:S(2)}) copy-start(bf16[256,256]{1,0:T(8,128)(2,1)} %copy-done.113) | copy-start | bytes 393220
  358.9 4.3 copy-start.3
  362.0 1.8 copy-start.7
  365.2 1.7 copy-start.157
  365.5 1.5 copy-start.50
  367.7 2.3 copy-start.155
  370.8 2.2 copy-start.159
  378.6 2.6 copy-start.153
  379.5 1.8 copy-start.126
  379.5 1.8 copy-start.152
  381.3 2.0 copy-start.41
  386.6 2.2 copy-start.33
  394.8 2.5 copy-start.81
  396.1 2.5 copy-start.8
  404.1 1.4 copy-start.4
  (110 other events, 107.7 us)
Sparse Core Ops, SparseCore 0:
  28.2 150.4 all-reduce.14
  212.1 146.8 all-reduce.12
  395.0 146.7 all-reduce.10
where the time goes:
time: 554 us; the launch traced here: 553 us
  waiting for transfers between devices  407 us (73%)
  local copies, waits for them, and re-layouts  64.4 us (12%)
  matrix products  48.8 us (9%)
  between operations  16.3 us (3%)
  other arithmetic  12.7 us (2%)
    psum x1, waiting for transfers between devices, local(): summed = lax.psum((upd[0], upd[1], upd[2]), 'ctx')  142 us
    psum x1, waiting for transfers between devices, local(): whole = lax.psum((part[0], part[1], part[2]), 'ctx')  136 us
    unnamed x4, waiting for transfers between devices  129 us
    unnamed x359, local copies, waits for them, and re-layouts  54.5 us
  transfers between devices with their start and end apart: 3, of which 3 were waited for; matrix products, arithmetic and copies ran while one was open for 4% of the time, Pallas kernels for 0%

commit v1 on v0

v1 whole, which is shorter than its diff:
```python
import functools
import math

import jax
import jax.numpy as jnp
from jax import lax
from jax.experimental import pallas as pl
from jax.experimental.pallas import tpu as pltpu
from jax.sharding import PartitionSpec as P

F32 = jnp.float32
BF16 = jnp.bfloat16
LANES = 128
VMEM_LIMIT = 40 * 1024 * 1024


def mm(a, b):
    return jnp.dot(a, b, preferred_element_type=F32)


def mm_t(a, b):
    return lax.dot_general(a, b, (((1,), (1,)), ((), ())), preferred_element_type=F32)


def tmm(a, b):
    return lax.dot_general(a, b, (((0,), (0,)), ((), ())), preferred_element_type=F32)


def call(body, out_shape, scratch, flops, *args):
    smem = pl.BlockSpec(memory_space=pltpu.SMEM)
    vmem = pl.BlockSpec(memory_space=pltpu.VMEM)
    size = sum(a.size * a.dtype.itemsize for a in args)
    size += sum(math.prod(o.shape) * o.dtype.itemsize for o in out_shape)
    return pl.pallas_call(
        body,
        out_shape=out_shape,
        in_specs=[smem] + [vmem] * (len(args) - 1),
        out_specs=[vmem] * len(out_shape),
        scratch_shapes=scratch,
        compiler_params=pltpu.CompilerParams(vmem_limit_bytes=VMEM_LIMIT),
        cost_estimate=pl.CostEstimate(flops=flops, bytes_accessed=size, transcendentals=0),
    )(*args)


def put_rows(scratch, x):
    for i in range(scratch.shape[0]):
        scratch[i] = x[:, i * LANES : (i + 1) * LANES]


def take_head(scratch, head, tokens, heads):
    parts = [scratch[i, pl.ds(head, tokens, stride=heads), :] for i in range(scratch.shape[0])]
    return jnp.concatenate(parts, axis=1)


def put_head(scratch, head, x, tokens, heads):
    for i in range(scratch.shape[0]):
        scratch[i, pl.ds(head, tokens, stride=heads), :] = x[:, i * LANES : (i + 1) * LANES]


def rows_of(scratch):
    return jnp.concatenate([scratch[i] for i in range(scratch.shape[0])], axis=1)


def partner(own, step, count):
    if count & (count - 1) == 0:
        return own ^ step
    return lax.rem(step + count - own, count)


def split_update(groups, place, k, v, r, *rest):
    outs, (sk, sv) = rest[:groups], rest[groups:]
    tokens, heads, width = k.shape
    put_rows(sk, k[...].astype(F32).reshape(tokens * heads, width))
    put_rows(sv, v[...].astype(F32).reshape(tokens * heads, width))
    for step in range(groups):
        head = partner(place[0], step, groups)
        outs[step][0] = take_head(sk, head, tokens, heads)
        rate = jnp.broadcast_to(r[pl.ds(head, 1), :], (8, tokens)).T[:, 0:1]
        scaled = take_head(sv, head, tokens, heads) * rate
        outs[step][1] = scaled.astype(BF16).astype(F32)


def split_apply(groups, place, q, cot, gain, *rest):
    outs, (sq, sc) = rest[:groups], rest[groups:]
    tokens, heads, width = q.shape
    put_rows(sq, q[...].astype(F32).reshape(tokens * heads, width))
    put_rows(sc, cot[...].astype(F32).reshape(tokens * heads, width))
    for step in range(groups):
        head = partner(place[0], step, groups)
        outs[step][0] = take_head(sq, head, tokens, heads)
        outs[step][1] = take_head(sc, head, tokens, heads) * gain[pl.ds(head, 1), :]


def send_slices(sums, outs, index, count):
    rows = sums.shape[1] // count
    for step in range(count):
        at = pl.multiple_of(partner(index, step, count) * rows, rows)
        outs[step][...] = sums[:, pl.ds(at, rows), :]


def update_kernel(groups, depth, scale, place, *refs):
    pieces = refs[:groups]
    w_gate, w_out, w_up = refs[groups : groups + 3]
    outs = refs[groups + 3 : groups + 3 + depth]
    sums = refs[groups + 3 + depth]
    gate_b, out_b, up_b = (w[...].astype(BF16) for w in (w_gate, w_out, w_up))
    total = [0.0, 0.0, 0.0]
    for piece in pieces:
        keys = piece[0].astype(BF16)
        scaled = piece[1].astype(BF16)
        first = mm(keys, gate_b)
        third = mm(keys, up_b)
        sig = jax.nn.sigmoid(first)
        activ = first * sig
        act = (activ * third).astype(BF16)
        dact = mm_t(scaled, out_b)
        deriv = sig * (1.0 + first * (1.0 - sig))
        dfirst = (dact * third * deriv).astype(BF16)
        dthird = (dact * activ).astype(BF16)
        total[0] += tmm(keys, dfirst)
        total[1] += tmm(act, scaled)
        total[2] += tmm(keys, dthird)
    for i in range(3):
        sums[i] = total[i] * scale
    send_slices(sums, outs, place[1], depth)
    rows = sums.shape[1] // depth
    at = pl.multiple_of(place[1] * rows, rows)
    for i, w in enumerate((w_gate, w_out, w_up)):
        outs[0][i] += w[pl.ds(at, rows), :]


def assemble(place, parts, whole):
    rows = parts[0].shape[1]
    for step, part in enumerate(parts):
        at = pl.multiple_of(partner(place[1], step, len(parts)) * rows, rows)
        whole[:, pl.ds(at, rows), :] = part[...]


def apply_kernel(groups, depth, place, head_scale, *refs):
    pieces = refs[:groups]
    parts = refs[groups : groups + depth]
    first_ref, third_ref, os_ref, stats, new_b = refs[groups + depth : groups + depth + 5]
    whole = refs[groups + depth + 5]
    assemble(place, parts, whole)
    new_b[...] = whole[...].astype(BF16)
    hs = head_scale[...]
    for step, piece in enumerate(pieces):
        tokens = piece.shape[1]
        queries = piece[0].astype(BF16)
        dyg = piece[1]
        first = mm(queries, new_b[0])
        third = mm(queries, new_b[2])
        hidden = (first * jax.nn.sigmoid(first) * third).astype(BF16)
        scaled = mm(hidden, new_b[1]) * hs
        first_ref[step] = first
        third_ref[step] = third
        os_ref[step] = scaled
        sq = jnp.sum(scaled * scaled, axis=1, keepdims=True)
        ps = jnp.sum(scaled * dyg, axis=1, keepdims=True)
        lane = lax.broadcasted_iota(jnp.int32, (tokens, LANES), 1)
        both = jnp.where(lane == 0, sq, jnp.where(lane == 1, ps, 0.0))
        stats[partner(place[0], step, groups)] = both.T[0:8, :]


def apply_back_kernel(groups, depth, count, place, head_scale, stats, *refs):
    pieces = refs[:groups]
    first_ref, third_ref, os_ref, new_b = refs[groups : groups + 4]
    outs = refs[groups + 4 : groups + 4 + groups]
    slices = refs[groups + 4 + groups : groups + 4 + groups + depth]
    sums = refs[groups + 4 + groups + depth]
    hs = head_scale[...]
    total = [0.0, 0.0, 0.0]
    for step, piece in enumerate(pieces):
        queries = piece[0].astype(BF16)
        dyg = piece[1]
        both = stats[partner(place[0], step, groups)].T
        sq = both[:, 0:1]
        ps = both[:, 1:2]
        inv = lax.rsqrt(sq / count + 1e-06)
        scaled = os_ref[step]
        dos = inv * dyg - scaled * (inv * inv * inv * ps / count)
        dout = (dos * hs).astype(BF16)
        first = first_ref[step]
        third = third_ref[step]
        sig = jax.nn.sigmoid(first)
        activ = first * sig
        hidden = (activ * third).astype(BF16)
        dhidden = mm_t(dout, new_b[1])
        dthird = (dhidden * activ).astype(BF16)
        dfirst = (dhidden * third * (sig * (1.0 + first * (1.0 - sig)))).astype(BF16)
        outs[step][...] = mm_t(dfirst, new_b[0]) + mm_t(dthird, new_b[2])
        total[0] += tmm(queries, dfirst)
        total[1] += tmm(hidden, dout)
        total[2] += tmm(queries, dthird)
    for i in range(3):
        sums[i] = total[i]
    send_slices(sums, slices, place[1], depth)


def update_back_kernel(groups, depth, scale, place, *refs):
    pieces = refs[:groups]
    parts = refs[groups : groups + depth]
    w_gate, w_out, w_up = refs[groups + depth : groups + depth + 3]
    base = groups + depth + 3
    outs = refs[base : base + groups]
    slices = refs[base + groups : base + groups + depth]
    whole, sums = refs[base + groups + depth :]
    assemble(place, parts, whole)
    gate_b, out_b, up_b = (w[...].astype(BF16) for w in (w_gate, w_out, w_up))
    cot_gate, cot_out, cot_up = ((whole[i] * scale).astype(BF16) for i in range(3))
    total = [0.0, 0.0, 0.0]
    for step, piece in enumerate(pieces):
        keys = piece[0].astype(BF16)
        scaled = piece[1].astype(BF16)
        first = mm(keys, gate_b)
        third = mm(keys, up_b)
        sig = jax.nn.sigmoid(first)
        activ = first * sig
        act = (activ * third).astype(BF16)
        dact = mm_t(scaled, out_b)
        slope = sig * (1.0 - sig)
        deriv = sig + first * slope
        second = slope * (2.0 + first * (1.0 - 2.0 * sig))
        third_deriv = third * deriv
        dfirst = (dact * third_deriv).astype(BF16)
        dthird = (dact * activ).astype(BF16)
        bar_dfirst = mm(keys, cot_gate)
        bar_dthird = mm(keys, cot_up)
        bar_act = mm_t(scaled, cot_out)
        bar_activ = bar_dthird * dact + bar_act * third
        bar_dact = (bar_dfirst * third_deriv + bar_dthird * activ).astype(BF16)
        bar_df_dact = bar_dfirst * dact
        bar_third = (bar_df_dact * deriv + bar_act * activ).astype(BF16)
        bar_first = (bar_activ * deriv + bar_df_dact * third * second).astype(BF16)
        outs[step][0] = (
            mm_t(dfirst, cot_gate)
            + mm_t(dthird, cot_up)
            + mm_t(bar_first, gate_b)
            + mm_t(bar_third, up_b)
        )
        outs[step][1] = mm(act, cot_out) + mm(bar_dact, out_b)
        total[0] += tmm(keys, bar_first)
        total[1] += tmm(bar_dact, scaled)
        total[2] += tmm(keys, bar_third)
    for i in range(3):
        sums[i] = total[i]
    send_slices(sums, slices, place[1], depth)


def join_query_kernel(groups, place, *refs):
    pieces, out, scratch = refs[:groups], refs[groups], refs[groups + 1]
    tokens, heads, width = out.shape
    for step, piece in enumerate(pieces):
        put_head(scratch, partner(place[0], step, groups), piece[...], tokens, heads)
    out[...] = rows_of(scratch).reshape(tokens, heads, width).astype(BF16)


def join_update_kernel(groups, place, r, *refs):
    pieces = refs[:groups]
    out_k, out_v, sk, sv = refs[groups:]
    tokens, heads, width = out_k.shape
    for step, piece in enumerate(pieces):
        head = partner(place[0], step, groups)
        put_head(sk, head, piece[0], tokens, heads)
        rate = jnp.broadcast_to(r[pl.ds(head, 1), :], (8, tokens)).T[:, 0:1]
        put_head(sv, head, piece[1] * rate, tokens, heads)
    out_k[...] = rows_of(sk).reshape(tokens, heads, width).astype(BF16)
    out_v[...] = rows_of(sv).reshape(tokens, heads, width).astype(BF16)


def rows_kernel(groups, place, *refs):
    parts, outs, total = refs[: -groups - 1], refs[-groups - 1 : -1], refs[-1]
    whole = parts[0][...]
    for part in parts[1:]:
        whole += part[...]
    total[...] = whole
    send_slices(total, outs, place[0], groups)


def join_rows_kernel(groups, place, *refs):
    parts, outs = refs[:groups], refs[groups:]
    for step, part in enumerate(parts):
        for i in range(3):
            outs[i][partner(place[0], step, groups)] = part[i]


def local(queries, keys, values, rates, head_scale, gain, w_gate, w_out, w_up, cotangent):
    tokens, heads, width = keys.shape[1:]
    hidden = w_gate.shape[2]
    ctx = lax.axis_size("ctx")
    head_axis = lax.axis_size("head")
    groups = heads
    depth = ctx // groups
    scale = 1.0 / math.sqrt(tokens * ctx * width)
    count = float(heads * head_axis * width)
    me = lax.axis_index("ctx")
    mine, layer = lax.rem(me, groups), lax.div(me, groups)
    place = jnp.stack([mine, layer]).astype(jnp.int32)

    def in_plane(x, step):
        perm = [
            (c, c // groups * groups + int(partner_of(c % groups, step, groups)))
            for c in range(ctx)
        ]
        return lax.ppermute(x, "ctx", perm)

    def in_column(x, step):
        perm = [
            (c, int(partner_of(c // groups, step, depth)) * groups + c % groups)
            for c in range(ctx)
        ]
        return lax.ppermute(x, "ctx", perm)

    def exchange(parts, move):
        return [parts[0]] + [move(p, step) for step, p in enumerate(parts) if step]

    def spread(part):
        return [part] + [in_column(part, step) for step in range(1, depth)]

    def shape(dims, dtype=F32):
        return jax.ShapeDtypeStruct(dims, dtype)

    flops = 2 * groups * tokens * width * hidden
    pair = [shape((2, tokens, width))] * groups
    slices = [shape((3, hidden // depth, width))] * depth
    scratch = pltpu.VMEM((width // LANES, tokens * heads, LANES), F32)
    square = pltpu.VMEM((3, hidden, width), F32)

    sent = call(
        functools.partial(split_update, groups), pair, [scratch] * 2, flops // 8,
        place, keys[0], values[0], rates[0],
    )
    pieces = exchange(sent, in_plane)
    own = [lax.dynamic_index_in_dim(w, mine, 0, keepdims=False) for w in (w_gate, w_out, w_up)]
    own_scale = lax.dynamic_index_in_dim(head_scale, mine, 0, keepdims=True)[None, :]
    pieces, queries, cotangent = lax.optimization_barrier((pieces, queries, cotangent))
    terms = call(
        functools.partial(update_kernel, groups, depth, scale), slices, [square], 6 * flops,
        place, *pieces, *own,
    )
    terms = exchange(terms, in_column)
    sent = call(
        functools.partial(split_apply, groups), pair, [scratch] * 2, flops // 8,
        place, queries[0], cotangent[0], gain,
    )
    q_pieces = exchange(sent, in_plane)
    new = spread(functools.reduce(jnp.add, terms))
    kept = shape((groups, tokens, width))
    first, third, scaled, stats, new_b = call(
        functools.partial(apply_kernel, groups, depth),
        [kept, kept, kept, shape((groups, 8, tokens)), shape((3, hidden, width), BF16)],
        [square], 3 * flops, place, own_scale, *q_pieces, *new,
    )
    block = groups * head_axis
    sets = [list(range(i, i + block)) for i in range(0, ctx * head_axis, block)]
    stats = lax.psum(stats, ("ctx", "head"), axis_index_groups=sets)
    out = call(
        functools.partial(apply_back_kernel, groups, depth, count),
        [shape((tokens, width))] * groups + slices, [square], 6 * flops,
        place, own_scale, stats, *q_pieces, first, third, scaled, new_b,
    )
    parts = exchange(out[groups:], in_column)
    part_sum = functools.reduce(jnp.add, parts)
    whole = spread(part_sum)
    q_back = exchange(out[:groups], in_plane)
    (grad_q,) = call(
        functools.partial(join_query_kernel, groups), [shape((tokens, heads, width), BF16)],
        [scratch], flops // 16, place, *q_back,
    )
    out = call(
        functools.partial(update_back_kernel, groups, depth, scale), pair + slices, [square] * 2,
        15 * flops, place, *pieces, *whole, *own,
    )
    ends = exchange(out[groups:], in_column)
    rows = hidden // ctx
    sent = call(
        functools.partial(rows_kernel, groups), [shape((3, rows, width))] * groups,
        [pltpu.VMEM((3, hidden // depth, width), F32)], flops // 100, place, part_sum, *ends,
    )
    back = exchange(out[:groups], in_plane)
    grad_k, grad_v = call(
        functools.partial(join_update_kernel, groups),
        [shape((tokens, heads, width), BF16)] * 2, [scratch] * 2, flops // 8,
        place, rates[0], *back,
    )
    grads = call(
        functools.partial(join_rows_kernel, groups), [shape((heads, rows, width))] * 3, [],
        flops // 100, place, *exchange(sent, in_plane),
    )
    if lax.axis_size("batch") > 1:
        grads = [lax.psum_scatter(x, "batch", scatter_dimension=1, tiled=True) for x in grads]
    return (grad_q[None], grad_k[None], grad_v[None], grads[0], grads[1], grads[2])


def partner_of(own, step, count):
    if count & (count - 1) == 0:
        return own ^ step
    return (step + count - own) % count


def solution(mesh):
    in_specs = (
        P("batch", "ctx", "head", None),
        P("batch", "ctx", "head", None),
        P("batch", "ctx", "head", None),
        P("batch", "head", "ctx"),
        P("head"),
        P("head", None),
        P("head", None, None),
        P("head", None, None),
        P("head", None, None),
        P("batch", "ctx", "head", None),
    )
    out_specs = (
        P("batch", "ctx", "head", None),
        P("batch", "ctx", "head", None),
        P("batch", "ctx", "head", None),
        P("head", ("ctx", "batch"), None),
        P("head", ("ctx", "batch"), None),
        P("head", ("ctx", "batch"), None),
    )
    return jax.shard_map(local, mesh=mesh, in_specs=in_specs, out_specs=out_specs, check_vma=False)
```

time: 554 us -> 210 us (0.38)
  waiting for transfers between devices: 407 us -> 101 us
  local copies, waits for them, and re-layouts: 64.4 us -> 12.7 us
  starting transfers between devices: 0.12 us -> 49.7 us
  matrix products: 48.8 us -> 0 us
  Pallas kernels: 0 us -> 21.1 us
  blocking collectives: 3.31 us -> 23.7 us
  between operations: 16.3 us -> 0.92 us
  other arithmetic: 12.7 us -> 0.18 us
    psum x2 -> x0, waiting for transfers between devices: 279 us -> none  [the longest x1 142 us: local(): summed = lax.psum((upd[0], upd[1], upd[2]), 'ctx')]
    unnamed x4 -> x0, waiting for transfers between devices: 129 us -> none
    ppermute x0 -> x30, waiting for transfers between devices: none -> 101 us  [the longest x15 50.8 us: in_column(): return lax.ppermute(x, 'ctx', perm)]
    ppermute x0 -> x30, starting transfers between devices: none -> 49.7 us  [the longest x15 28.7 us: in_column(): return lax.ppermute(x, 'ctx', perm)]
    dot_general x108 -> x0, matrix products: 48.8 us -> none  [the longest x12 8.86 us: update_terms(): first = jnp.dot(keys, gate_b, preferred_element_type=jnp.float32)]
    unnamed x359 -> x60, local copies, waits for them, and re-layouts: 54.5 us -> 10.9 us
    pallas_call x0 -> x10, Pallas kernels: none -> 21.1 us  [call(): pl.pallas_call(body, out_shape=out_shape, in_specs=[smem] + [vmem] * (len...]
    psum x1, blocking collectives: 3.31 us -> 23.7 us  [local(): stats = lax.psum(stats, ('ctx', 'head'), axis_index_groups=sets)]
  transfers between devices with their start and end apart: 3 -> 30, of which waited for: 3 -> 17; matrix products, arithmetic and copies ran while one was open for 4% -> 1% of each run, Pallas kernels for 0% -> 4%
where the time goes in v1:
time: 210 us; the launch traced here: 209 us
  waiting for transfers between devices  101 us (48%)
  starting transfers between devices  49.7 us (24%)
  blocking collectives  23.7 us (11%)
  Pallas kernels  21.1 us (10%)
  local copies, waits for them, and re-layouts  12.7 us (6%)
    ppermute x15, waiting for transfers between devices, in_column(): return lax.ppermute(x, 'ctx', perm)  50.8 us
    ppermute x15, waiting for transfers between devices, in_plane(): return lax.ppermute(x, 'ctx', perm)  50.1 us
    ppermute x15, starting transfers between devices, in_column(): return lax.ppermute(x, 'ctx', perm)  28.7 us
    psum x1, blocking collectives, local(): stats = lax.psum(stats, ('ctx', 'head'), axis_index_groups=sets)  23.7 us
    pallas_call x10, Pallas kernels, call(): pl.pallas_call(body, out_shape=out_shape, in_specs=[smem] + [vmem] * (len...  21.1 us
    ppermute x15, starting transfers between devices, in_plane(): return lax.ppermute(x, 'ctx', perm)  21 us
    unnamed x60, local copies, waits for them, and re-layouts  10.9 us
  transfers between devices with their start and end apart: 30, of which 17 were waited for; matrix products, arithmetic and copies ran while one was open for 1% of the time, Pallas kernels for 4%

profile of v1, /device:TPU:0, one launch (start us, length us, event | category | flops | bytes accessed | tf_op | source)
XLA Modules:
  0.0 209.1 jit_solution(17797429282755645244)
XLA Ops:
  0.7 0.7 copy-done.19
  1.4 1.0 copy-done.7
  2.5 1.0 copy-done.8
  3.5 2.4 %shard_map.145 = (f32[2,256,256]{2,1,0:T(8,128)S(1)}, f32[2,256,256]{2,1,0:T(8,128)}, f32[2,256,256]{2,1,0:T(8,128)}, f32[2,256,256]{2,1,0:T(8,128)}) custom-call(s32[2]{0:T(128)S(1)} %pad_add_fusion.place, bf16[256,4,256]{2,1,0:T(4,128)(2,1)S(1)} %bitcast.17, bf16[256,4,256]{2,1,0:T(4,128)(2,1)S(1)} %bitcast.18, f32[4,256]{1,0:T(4,128)S(1)} %bitcast.21), custom_call_target="tpu_custom_call" | custom-call | flops 16777216 | bytes 3149832 | tf_op jit(solution)/shard_map/pallas_call | solution.py:34
  5.9 2.9 %collective-permute-start = (f32[2,256,256]{2,1,0:T(8,128)}, f32[2,256,256]{2,1,0:T(8,128)S(1)}, u32[]{:S(2)}, u32[]{:S(2)}) collective-permute-start(f32[2,256,256]{2,1,0:T(8,128)} %get-tuple-element.55), channel_id=1, source_target_pairs={{0,2},{2,0},{4,6},{6,4},{8,10},{10,8},{12,14},{14,12},{16,18},{18,... | collective-permute-start | bytes 1572872 | tf_op jit(solution)/shard_map/ppermute | solution.py:305
  8.9 1.5 collective-permute-start.1
  10.4 1.2 dynamic-slice_bitcast_fusion
  11.6 10.2 %collective-permute-done.refs_1_ = f32[2,256,256]{2,1,0:T(8,128)S(1)} collective-permute-done((f32[2,256,256]{2,1,0:T(8,128)}, f32[2,256,256]{2,1,0:T(8,128)S(1)}, u32[]{:S(2)}, u32[]{:S(2)}) %collective-permute-start) | collective-permute-done | bytes 524320 | tf_op jit(solution)/shard_map/ppermute | solution.py:305
  21.8 11.9 %collective-permute-done.1.refs_2_ = f32[2,256,256]{2,1,0:T(8,128)S(1)} collective-permute-done((f32[2,256,256]{2,1,0:T(8,128)}, f32[2,256,256]{2,1,0:T(8,128)S(1)}, u32[]{:S(2)}, u32[]{:S(2)}) %collective-permute-start.1) | collective-permute-done | bytes 524320 | tf_op jit(solution)/shard_map/ppermute | solution.py:305
  33.7 2.2 %shard_map.147 = (f32[3,64,256]{2,1,0:T(8,128)S(1)}, f32[3,64,256]{2,1,0:T(8,128)S(1)}, f32[3,64,256]{2,1,0:T(8,128)S(1)}, f32[3,64,256]{2,1,0:T(8,128)S(1)}) custom-call(s32[2]{0:T(128)S(1)} %pad_add_fusion.place, f32[2,256,256]{2,1,0:T(8,128)S(1)} %get-tuple-element.64.refs_0_, f32[2,256,256]{2,1,0:T(8,128)S(1)} %collective-permute-done.refs_1_, ...), custom_call_target="tpu_custom_call" | custom-call | flops 805306368 | bytes 3670024 | tf_op jit(solution)/shard_map/pallas_call | solution.py:34
  36.0 1.6 collective-permute-start.6
  37.6 2.6 %collective-permute-start.7 = (f32[3,64,256]{2,1,0:T(8,128)S(1)}, f32[3,64,256]{2,1,0:T(8,128)S(1)}, u32[]{:S(2)}, u32[]{:S(2)}) collective-permute-start(f32[3,64,256]{2,1,0:T(8,128)S(1)} %get-tuple-element.70), channel_id=1, source_target_pairs={{0,16},{2,18},{4,20},{6,22},{8,24},{10,26},{12,28},{14,30},{16,0},... | collective-permute-start | bytes 589832 | tf_op jit(solution)/shard_map/ppermute | solution.py:312
  40.4 1.2 shard_map.146
  41.6 1.3 collective-permute-start.3
  42.9 0.8 collective-permute-start.4
  43.8 0.5 collective-permute-done.6
  44.3 1.4 collective-permute-start.5
  45.7 10.8 %collective-permute-done.7 = f32[3,64,256]{2,1,0:T(8,128)S(1)} collective-permute-done((f32[3,64,256]{2,1,0:T(8,128)S(1)}, f32[3,64,256]{2,1,0:T(8,128)S(1)}, u32[]{:S(2)}, u32[]{:S(2)}) %collective-permute-start.7) | collective-permute-done | bytes 196640 | tf_op jit(solution)/shard_map/ppermute | solution.py:312
  56.5 2.2 %collective-permute-start.11 = (f32[3,64,256]{2,1,0:T(8,128)S(1)}, f32[3,64,256]{2,1,0:T(8,128)S(1)}, u32[]{:S(2)}, u32[]{:S(2)}) collective-permute-start(f32[3,64,256]{2,1,0:T(8,128)S(1)} %add_add_fusion.1.refs_4_), channel_id=1, source_target_pairs={{0,24},{2,26},{4,28},{6,30},{8,16},{10,18},{12,20},{14,22},{16,8},... | collective-permute-start | bytes 589832 | tf_op jit(solution)/shard_map/ppermute | solution.py:312
  58.7 2.0 collective-permute-start.10
  60.7 5.4 %collective-permute-done.11.refs_7_ = f32[3,64,256]{2,1,0:T(8,128)S(1)} collective-permute-done((f32[3,64,256]{2,1,0:T(8,128)S(1)}, f32[3,64,256]{2,1,0:T(8,128)S(1)}, u32[]{:S(2)}, u32[]{:S(2)}) %collective-permute-start.11) | collective-permute-done | bytes 196640 | tf_op jit(solution)/shard_map/ppermute | solution.py:312
  66.1 6.5 %collective-permute-start.9 = (f32[3,64,256]{2,1,0:T(8,128)S(1)}, f32[3,64,256]{2,1,0:T(8,128)S(1)}, u32[]{:S(2)}, u32[]{:S(2)}) collective-permute-start(f32[3,64,256]{2,1,0:T(8,128)S(1)} %add_add_fusion.1.refs_4_), channel_id=1, source_target_pairs={{0,8},{2,10},{4,12},{6,14},{8,0},{10,2},{12,4},{14,6},{16,24},{18,... | collective-permute-start | bytes 589832 | tf_op jit(solution)/shard_map/ppermute | solution.py:312
  72.6 0.6 dynamic_slice.14
  73.2 1.1 collective-permute-done.10.refs_6_
  74.3 2.7 %collective-permute-done.9.refs_5_ = f32[3,64,256]{2,1,0:T(8,128)S(1)} collective-permute-done((f32[3,64,256]{2,1,0:T(8,128)S(1)}, f32[3,64,256]{2,1,0:T(8,128)S(1)}, u32[]{:S(2)}, u32[]{:S(2)}) %collective-permute-start.9) | collective-permute-done | bytes 196640 | tf_op jit(solution)/shard_map/ppermute | solution.py:312
  77.0 2.3 %shard_map.148 = (f32[4,256,256]{2,1,0:T(8,128)S(1)}, f32[4,256,256]{2,1,0:T(8,128)S(1)}, f32[4,256,256]{2,1,0:T(8,128)S(1)}, f32[4,8,256]{2,1,0:T(8,128)S(1)}, bf16[3,256,256]{2,1,0:T(8,128)(2,1)S(1)}) custom-call(s32[2]{0:T(128)S(1)} %pad_add_fusion.place, f32[1,1]{1,0:T(1,128)} %bitcast.2.head_scale, f32[2,256,256]{2,1,0:T(8,128)S(1)} %get-tuple-element.60.refs_0_, ...), custom_call_target="tpu_custom_call" | custom-call | flops 402653184 | bytes 6455308 | tf_op jit(solution)/shard_map/pallas_call | solution.py:34
  79.3 1.0 copy-done.1
  80.3 1.0 copy-done.3
  81.3 1.0 copy-done.5
  82.3 0.6 copy-done.18
  82.9 23.7 %psum.7.stats = f32[4,8,256]{2,1,0:T(8,128)} all-reduce(f32[4,8,256]{2,1,0:T(8,128)} %copy-done.18), channel_id=1, replica_groups={{0,1,2,3,4,5,6,7},{8,9,10,11,12,13,14,15},{16,17,18,19,20,21,22,23},{24..., use_global_device_ids=true, to_apply=%region_0.1 | all-reduce | flops 8192 | bytes 65536 | tf_op jit(solution)/shard_map/psum | solution.py:356
  106.6 1.2 copy-done.2
  107.8 1.2 copy-done.4
  109.0 1.2 copy-done.6
  110.3 0.8 copy-done.17
  111.0 3.3 %shard_map.149 = (f32[256,256]{1,0:T(8,128)S(1)}, f32[256,256]{1,0:T(8,128)S(1)}, f32[256,256]{1,0:T(8,128)S(1)}, f32[256,256]{1,0:T(8,128)S(1)}, f32[3,64,256]{...) custom-call(s32[2]{0:T(128)S(1)} %pad_add_fusion.place, ...), custom_call_target="tpu_custom_call" | custom-call | flops 805306368 | bytes 7503884 | tf_op jit(solution)/shard_map/pallas_call | solution.py:34
  114.3 1.4 collective-permute-start.15
  115.7 3.3 %collective-permute-start.16 = (f32[3,64,256]{2,1,0:T(8,128)S(1)}, f32[3,64,256]{2,1,0:T(8,128)S(1)}, u32[]{:S(2)}, u32[]{:S(2)}) collective-permute-start(f32[3,64,256]{2,1,0:T(8,128)S(1)} %get-tuple-element.83), channel_id=1, source_target_pairs={{0,16},{2,18},{4,20},{6,22},{8,24},{10,26},{12,28},{14,30},{16,0},... | collective-permute-start | bytes 589832 | tf_op jit(solution)/shard_map/ppermute | solution.py:312
  119.0 6.0 %collective-permute-done.15 = f32[3,64,256]{2,1,0:T(8,128)S(1)} collective-permute-done((f32[3,64,256]{2,1,0:T(8,128)S(1)}, f32[3,64,256]{2,1,0:T(8,128)S(1)}, u32[]{:S(2)}, u32[]{:S(2)}) %collective-permute-start.15) | collective-permute-done | bytes 196640 | tf_op jit(solution)/shard_map/ppermute | solution.py:312
  125.0 8.7 %collective-permute-done.16 = f32[3,64,256]{2,1,0:T(8,128)S(1)} collective-permute-done((f32[3,64,256]{2,1,0:T(8,128)S(1)}, f32[3,64,256]{2,1,0:T(8,128)S(1)}, u32[]{:S(2)}, u32[]{:S(2)}) %collective-permute-start.16) | collective-permute-done | bytes 196640 | tf_op jit(solution)/shard_map/ppermute | solution.py:312
  133.9 2.5 %collective-permute-start.20 = (f32[3,64,256]{2,1,0:T(8,128)S(1)}, f32[3,64,256]{2,1,0:T(8,128)S(1)}, u32[]{:S(2)}, u32[]{:S(2)}) collective-permute-start(f32[3,64,256]{2,1,0:T(8,128)S(1)} %add_add_fusion.refs_4_.refs_0_), channel_id=1, source_target_pairs={{0,24},{2,26},{4,28},{6,30},{8,16},{10,18},{12,20},{14,22},{16,8},... | collective-permute-start | bytes 589832 | tf_op jit(solution)/shard_map/ppermute | solution.py:312
  136.3 1.9 collective-permute-start.19
  138.3 1.0 collective-permute-start.12
  139.3 4.2 %collective-permute-done.20.refs_7_ = f32[3,64,256]{2,1,0:T(8,128)S(1)} collective-permute-done((f32[3,64,256]{2,1,0:T(8,128)S(1)}, f32[3,64,256]{2,1,0:T(8,128)S(1)}, u32[]{:S(2)}, u32[]{:S(2)}) %collective-permute-start.20) | collective-permute-done | bytes 196640 | tf_op jit(solution)/shard_map/ppermute | solution.py:312
  143.5 8.3 %collective-permute-done.19.refs_6_ = f32[3,64,256]{2,1,0:T(8,128)S(1)} collective-permute-done((f32[3,64,256]{2,1,0:T(8,128)S(1)}, f32[3,64,256]{2,1,0:T(8,128)S(1)}, u32[]{:S(2)}, u32[]{:S(2)}) %collective-permute-start.19) | collective-permute-done | bytes 196640 | tf_op jit(solution)/shard_map/ppermute | solution.py:312
  151.8 3.7 %shard_map.151 = (f32[2,256,256]{2,1,0:T(8,128)S(1)}, f32[2,256,256]{2,1,0:T(8,128)S(1)}, f32[2,256,256]{2,1,0:T(8,128)S(1)}, f32[2,256,256]{2,1,0:T(8,128)S(1)}...) custom-call(s32[2]{0:T(128)S(1)} %pad_add_fusion.place, ...), custom_call_target="tpu_custom_call" | custom-call | flops 2013265920 | bytes 6553608 | tf_op jit(solution)/shard_map/pallas_call | solution.py:34
  155.6 2.6 %collective-permute-start.25 = (f32[3,64,256]{2,1,0:T(8,128)S(1)}, f32[3,64,256]{2,1,0:T(8,128)S(1)}, u32[]{:S(2)}, u32[]{:S(2)}) collective-permute-start(f32[3,64,256]{2,1,0:T(8,128)S(1)} %get-tuple-element.93), channel_id=1, source_target_pairs={{0,16},{2,18},{4,20},{6,22},{8,24},{10,26},{12,28},{14,30},{16,0},... | collective-permute-start | bytes 589832 | tf_op jit(solution)/shard_map/ppermute | solution.py:312
  158.2 2.3 %collective-permute-start.21 = (f32[2,256,256]{2,1,0:T(8,128)S(1)}, f32[2,256,256]{2,1,0:T(8,128)S(1)}, u32[]{:S(2)}, u32[]{:S(2)}) collective-permute-start(f32[2,256,256]{2,1,0:T(8,128)S(1)} %get-tuple-element.86), channel_id=1, source_target_pairs={{0,2},{2,0},{4,6},{6,4},{8,10},{10,8},{12,14},{14,12},{16,18},{18,... | collective-permute-start | bytes 1572872 | tf_op jit(solution)/shard_map/ppermute | solution.py:305
  160.6 1.4 collective-permute-start.23
  162.0 2.3 %collective-permute-done.24.refs_2_ = f32[3,64,256]{2,1,0:T(8,128)S(1)} collective-permute-done((f32[3,64,256]{2,1,0:T(8,128)S(1)}, f32[3,64,256]{2,1,0:T(8,128)S(1)}, u32[]{:S(2)}, u32[]{:S(2)}) %collective-permute-start.24) | collective-permute-done | bytes 196640 | tf_op jit(solution)/shard_map/ppermute | solution.py:312
  164.3 1.7 collective-permute-start.26
  166.1 0.3 collective-permute-done.25.refs_3_
  166.3 5.1 %collective-permute-start.13 = (f32[256,256]{1,0:T(8,128)S(1)}, f32[256,256]{1,0:T(8,128)S(1)}, u32[]{:S(2)}, u32[]{:S(2)}) collective-permute-start(f32[256,256]{1,0:T(8,128)S(1)} %get-tuple-element.79), channel_id=1, source_target_pairs={{0,4},{2,6},{4,0},{6,2},{8,12},{10,14},{12,8},{14,10},{16,20},{18,... | collective-permute-start | bytes 786440 | tf_op jit(solution)/shard_map/ppermute | solution.py:305
  171.4 0.5 collective-permute-done.26.refs_4_
  171.9 2.6 %collective-permute-start.14 = (f32[256,256]{1,0:T(8,128)S(1)}, f32[256,256]{1,0:T(8,128)S(1)}, u32[]{:S(2)}, u32[]{:S(2)}) collective-permute-start(f32[256,256]{1,0:T(8,128)S(1)} %get-tuple-element.80), channel_id=1, source_target_pairs={{0,6},{2,4},{4,2},{6,0},{8,14},{10,12},{12,10},{14,8},{16,22},{18,... | collective-permute-start | bytes 786440 | tf_op jit(solution)/shard_map/ppermute | solution.py:305
  174.5 0.6 shard_map.153
  175.1 20.9 %collective-permute-done.13.refs_2_ = f32[256,256]{1,0:T(8,128)S(1)} collective-permute-done((f32[256,256]{1,0:T(8,128)S(1)}, f32[256,256]{1,0:T(8,128)S(1)}, u32[]{:S(2)}, u32[]{:S(2)}) %collective-permute-start.13) | collective-permute-done | bytes 262176 | tf_op jit(solution)/shard_map/ppermute | solution.py:305
  196.0 0.3 collective-permute-start.27
  196.3 0.3 collective-permute-start.28
  196.6 3.9 %collective-permute-done.27.refs_1_ = f32[3,16,256]{2,1,0:T(8,128)S(1)} collective-permute-done((f32[3,16,256]{2,1,0:T(8,128)S(1)}, f32[3,16,256]{2,1,0:T(8,128)S(1)}, u32[]{:S(2)}, u32[]{:S(2)}) %collective-permute-start.27) | collective-permute-done | bytes 49184 | tf_op jit(solution)/shard_map/ppermute | solution.py:305
  200.5 1.7 shard_map.150
  202.2 3.2 %collective-permute-done.29.refs_3_ = f32[3,16,256]{2,1,0:T(8,128)S(1)} collective-permute-done((f32[3,16,256]{2,1,0:T(8,128)S(1)}, f32[3,16,256]{2,1,0:T(8,128)S(1)}, u32[]{:S(2)}, u32[]{:S(2)}) %collective-permute-start.29) | collective-permute-done | bytes 49184 | tf_op jit(solution)/shard_map/ppermute | solution.py:305
  205.5 1.2 shard_map.154
  206.7 2.4 %shard_map.152 = (bf16[256,4,256]{2,1,0:T(4,128)(2,1)}, bf16[256,4,256]{2,1,0:T(4,128)(2,1)}) custom-call(s32[2]{0:T(128)S(1)} %pad_add_fusion.place, f32[4,256]{1,0:T(4,128)S(1)} %bitcast.22, f32[2,256,256]{2,1,0:T(8,128)S(1)} %get-tuple-element.85.refs_0_, f32[2,256,256]{2,1,0:T(8,128)S(1)} %collective-permute-done.21.refs_1_, ...), custom_call_target="tpu_custom_call" | custom-call | flops 16777216 | bytes 3149832 | tf_op jit(solution)/shard_map/pallas_call | solution.py:34
  (73 shorter events, 0.8 us)
Async XLA Ops:
  0.6 9.8 %copy-start = (f32[4,256,256]{2,1,0:T(8,128)S(1)}, f32[4,256,256]{2,1,0:T(8,128)}, u32[]{:S(2)}) copy-start(f32[4,256,256]{2,1,0:T(8,128)} %param.16) | copy-start | bytes 3145732
  0.7 0.8 copy-start.19
  1.4 1.0 copy-start.7
  2.5 1.0 copy-start.8
  5.9 27.8 %copy-start.21 = (f32[2,256,256]{2,1,0:T(8,128)}, f32[2,256,256]{2,1,0:T(8,128)S(1)}, u32[]{:S(2)}) copy-start(f32[2,256,256]{2,1,0:T(8,128)S(1)} %get-tuple-element.64.refs_0_) | copy-start | bytes 1572868
  5.9 15.9 %collective-permute-start = (f32[2,256,256]{2,1,0:T(8,128)}, f32[2,256,256]{2,1,0:T(8,128)S(1)}, u32[]{:S(2)}, u32[]{:S(2)}) collective-permute-start(f32[2,256,256]{2,1,0:T(8,128)} %get-tuple-element.55), channel_id=1, source_target_pairs={{0,2},{2,0},{4,6},{6,4},{8,10},{10,8},{12,14},{14,12},{16,18},{18,... | collective-permute-start | bytes 1572872 | tf_op jit(solution)/shard_map/ppermute | solution.py:305
  8.9 24.8 %collective-permute-start.1 = (f32[2,256,256]{2,1,0:T(8,128)}, f32[2,256,256]{2,1,0:T(8,128)S(1)}, u32[]{:S(2)}, u32[]{:S(2)}) collective-permute-start(f32[2,256,256]{2,1,0:T(8,128)} %get-tuple-element.56), channel_id=1, source_target_pairs={{0,4},{2,6},{4,0},{6,2},{8,12},{10,14},{12,8},{14,10},{16,20},{18,... | collective-permute-start | bytes 1572872 | tf_op jit(solution)/shard_map/ppermute | solution.py:305
  10.4 23.3 %collective-permute-start.2 = (f32[2,256,256]{2,1,0:T(8,128)}, f32[2,256,256]{2,1,0:T(8,128)S(1)}, u32[]{:S(2)}, u32[]{:S(2)}) collective-permute-start(f32[2,256,256]{2,1,0:T(8,128)} %get-tuple-element.57), channel_id=1, source_target_pairs={{0,6},{2,4},{4,2},{6,0},{8,14},{10,12},{12,10},{14,8},{16,22},{18,... | collective-permute-start | bytes 1572872 | tf_op jit(solution)/shard_map/ppermute | solution.py:305
  10.4 23.3 %copy-start.11 = (f32[256,256]{1,0:T(8,128)}, f32[256,256]{1,0:T(8,128)S(1)}, u32[]{:S(2)}) copy-start(f32[256,256]{1,0:T(8,128)S(1)} %dynamic-slice_bitcast_fusion.2.refs_4_.refs_8_) | copy-start | bytes 786436
  11.6 24.3 %copy-start.13 = (f32[256,256]{1,0:T(8,128)}, f32[256,256]{1,0:T(8,128)S(1)}, u32[]{:S(2)}) copy-start(f32[256,256]{1,0:T(8,128)S(1)} %get-tuple-element.102.refs_6_.refs_10_) | copy-start | bytes 786436
  11.6 24.3 %copy-start.15 = (f32[256,256]{1,0:T(8,128)}, f32[256,256]{1,0:T(8,128)S(1)}, u32[]{:S(2)}) copy-start(f32[256,256]{1,0:T(8,128)S(1)} %get-tuple-element.103.refs_5_.refs_9_) | copy-start | bytes 786436
  21.8 14.1 %copy-start.23 = (f32[2,256,256]{2,1,0:T(8,128)}, f32[2,256,256]{2,1,0:T(8,128)S(1)}, u32[]{:S(2)}) copy-start(f32[2,256,256]{2,1,0:T(8,128)S(1)} %collective-permute-done.refs_1_) | copy-start | bytes 1572868
  33.7 2.2 %copy-start.25 = (f32[2,256,256]{2,1,0:T(8,128)}, f32[2,256,256]{2,1,0:T(8,128)S(1)}, u32[]{:S(2)}) copy-start(f32[2,256,256]{2,1,0:T(8,128)S(1)} %collective-permute-done.1.refs_2_) | copy-start | bytes 1572868
  33.7 2.3 %copy-start.27 = (f32[2,256,256]{2,1,0:T(8,128)}, f32[2,256,256]{2,1,0:T(8,128)S(1)}, u32[]{:S(2)}) copy-start(f32[2,256,256]{2,1,0:T(8,128)S(1)} %collective-permute-done.2.refs_3_) | copy-start | bytes 1572868
  33.7 6.7 %copy-start.9 = (bf16[1,256,4,256]{3,2,1,0:T(4,128)(2,1)S(1)}, bf16[1,256,4,256]{3,2,1,0:T(4,128)(2,1)}, u32[]{:S(2)}) copy-start(bf16[1,256,4,256]{3,2,1,0:T(4,128)(2,1)} %param.10) | copy-start | bytes 1572868
  33.7 6.7 %copy-start.10 = (bf16[1,256,4,256]{3,2,1,0:T(4,128)(2,1)S(1)}, bf16[1,256,4,256]{3,2,1,0:T(4,128)(2,1)}, u32[]{:S(2)}) copy-start(bf16[1,256,4,256]{3,2,1,0:T(4,128)(2,1)} %param.19) | copy-start | bytes 1572868
  36.0 4.5 %copy-start.20 = (f32[4,256]{1,0:T(4,128)S(1)}, f32[4,256]{1,0:T(4,128)}, u32[]{:S(2)}) copy-start(f32[4,256]{1,0:T(4,128)} %gain.1) | copy-start | bytes 12292
  36.0 8.3 %collective-permute-start.6 = (f32[3,64,256]{2,1,0:T(8,128)S(1)}, f32[3,64,256]{2,1,0:T(8,128)S(1)}, u32[]{:S(2)}, u32[]{:S(2)}) collective-permute-start(f32[3,64,256]{2,1,0:T(8,128)S(1)} %get-tuple-element.69), channel_id=1, source_target_pairs={{0,8},{2,10},{4,12},{6,14},{8,0},{10,2},{12,4},{14,6},{16,24},{18,... | collective-permute-start | bytes 589832 | tf_op jit(solution)/shard_map/ppermute | solution.py:312
  37.6 18.8 %collective-permute-start.7 = (f32[3,64,256]{2,1,0:T(8,128)S(1)}, f32[3,64,256]{2,1,0:T(8,128)S(1)}, u32[]{:S(2)}, u32[]{:S(2)}) collective-permute-start(f32[3,64,256]{2,1,0:T(8,128)S(1)} %get-tuple-element.70), channel_id=1, source_target_pairs={{0,16},{2,18},{4,20},{6,22},{8,24},{10,26},{12,28},{14,30},{16,0},... | collective-permute-start | bytes 589832 | tf_op jit(solution)/shard_map/ppermute | solution.py:312
  40.2 16.3 %collective-permute-start.8 = (f32[3,64,256]{2,1,0:T(8,128)S(1)}, f32[3,64,256]{2,1,0:T(8,128)S(1)}, u32[]{:S(2)}, u32[]{:S(2)}) collective-permute-start(f32[3,64,256]{2,1,0:T(8,128)S(1)} %get-tuple-element.71), channel_id=1, source_target_pairs={{0,24},{2,26},{4,28},{6,30},{8,16},{10,18},{12,20},{14,22},{16,8},... | collective-permute-start | bytes 589832 | tf_op jit(solution)/shard_map/ppermute | solution.py:312
  41.6 35.3 %collective-permute-start.3 = (f32[2,256,256]{2,1,0:T(8,128)S(1)}, f32[2,256,256]{2,1,0:T(8,128)S(1)}, u32[]{:S(2)}, u32[]{:S(2)}) collective-permute-start(f32[2,256,256]{2,1,0:T(8,128)S(1)} %get-tuple-element.61), channel_id=1, source_target_pairs={{0,2},{2,0},{4,6},{6,4},{8,10},{10,8},{12,14},{14,12},{16,18},{18,... | collective-permute-start | bytes 1572872 | tf_op jit(solution)/shard_map/ppermute | solution.py:305
  42.9 34.0 %collective-permute-start.4 = (f32[2,256,256]{2,1,0:T(8,128)S(1)}, f32[2,256,256]{2,1,0:T(8,128)S(1)}, u32[]{:S(2)}, u32[]{:S(2)}) collective-permute-start(f32[2,256,256]{2,1,0:T(8,128)S(1)} %get-tuple-element.62), channel_id=1, source_target_pairs={{0,4},{2,6},{4,0},{6,2},{8,12},{10,14},{12,8},{14,10},{16,20},{18,... | collective-permute-start | bytes 1572872 | tf_op jit(solution)/shard_map/ppermute | solution.py:305
  44.3 32.7 %collective-permute-start.5 = (f32[2,256,256]{2,1,0:T(8,128)S(1)}, f32[2,256,256]{2,1,0:T(8,128)S(1)}, u32[]{:S(2)}, u32[]{:S(2)}) collective-permute-start(f32[2,256,256]{2,1,0:T(8,128)S(1)} %get-tuple-element.63), channel_id=1, source_target_pairs={{0,6},{2,4},{4,2},{6,0},{8,14},{10,12},{12,10},{14,8},{16,22},{18,... | collective-permute-start | bytes 1572872 | tf_op jit(solution)/shard_map/ppermute | solution.py:305
  56.5 16.2 %copy-start.29 = (f32[4]{0:T(128)S(1)}, f32[4]{0:T(128)}, u32[]{:S(2)}) copy-start(f32[4]{0:T(128)} %param.14) | copy-start | bytes 52
  56.5 9.6 %collective-permute-start.11 = (f32[3,64,256]{2,1,0:T(8,128)S(1)}, f32[3,64,256]{2,1,0:T(8,128)S(1)}, u32[]{:S(2)}, u32[]{:S(2)}) collective-permute-start(f32[3,64,256]{2,1,0:T(8,128)S(1)} %add_add_fusion.1.refs_4_), channel_id=1, source_target_pairs={{0,24},{2,26},{4,28},{6,30},{8,16},{10,18},{12,20},{14,22},{16,8},... | collective-permute-start | bytes 589832 | tf_op jit(solution)/shard_map/ppermute | solution.py:312
  58.7 15.6 %collective-permute-start.10 = (f32[3,64,256]{2,1,0:T(8,128)S(1)}, f32[3,64,256]{2,1,0:T(8,128)S(1)}, u32[]{:S(2)}, u32[]{:S(2)}) collective-permute-start(f32[3,64,256]{2,1,0:T(8,128)S(1)} %add_add_fusion.1.refs_4_), channel_id=1, source_target_pairs={{0,16},{2,18},{4,20},{6,22},{8,24},{10,26},{12,28},{14,30},{16,0},... | collective-permute-start | bytes 589832 | tf_op jit(solution)/shard_map/ppermute | solution.py:312
  66.1 10.8 %collective-permute-start.9 = (f32[3,64,256]{2,1,0:T(8,128)S(1)}, f32[3,64,256]{2,1,0:T(8,128)S(1)}, u32[]{:S(2)}, u32[]{:S(2)}) collective-permute-start(f32[3,64,256]{2,1,0:T(8,128)S(1)} %add_add_fusion.1.refs_4_), channel_id=1, source_target_pairs={{0,8},{2,10},{4,12},{6,14},{8,0},{10,2},{12,4},{14,6},{16,24},{18,... | collective-permute-start | bytes 589832 | tf_op jit(solution)/shard_map/ppermute | solution.py:312
  79.3 1.0 copy-start.1
  80.3 1.0 copy-start.3
  81.3 1.0 copy-start.5
  82.3 0.6 copy-start.18
  106.6 1.2 copy-start.2
  107.8 1.2 copy-start.4
  109.0 1.2 copy-start.6
  110.3 0.8 copy-start.17
  111.0 40.8 %copy-start.22 = (f32[2,256,256]{2,1,0:T(8,128)S(1)}, f32[2,256,256]{2,1,0:T(8,128)}, u32[]{:S(2)}) copy-start(f32[2,256,256]{2,1,0:T(8,128)} %copy-done.21) | copy-start | bytes 1572868
  111.0 40.8 %copy-start.24 = (f32[2,256,256]{2,1,0:T(8,128)S(1)}, f32[2,256,256]{2,1,0:T(8,128)}, u32[]{:S(2)}) copy-start(f32[2,256,256]{2,1,0:T(8,128)} %copy-done.23) | copy-start | bytes 1572868
  111.0 40.8 %copy-start.26 = (f32[2,256,256]{2,1,0:T(8,128)S(1)}, f32[2,256,256]{2,1,0:T(8,128)}, u32[]{:S(2)}) copy-start(f32[2,256,256]{2,1,0:T(8,128)} %copy-done.25) | copy-start | bytes 1572868
  111.0 40.8 %copy-start.28 = (f32[2,256,256]{2,1,0:T(8,128)S(1)}, f32[2,256,256]{2,1,0:T(8,128)}, u32[]{:S(2)}) copy-start(f32[2,256,256]{2,1,0:T(8,128)} %copy-done.27) | copy-start | bytes 1572868
  114.3 10.7 %collective-permute-start.15 = (f32[3,64,256]{2,1,0:T(8,128)S(1)}, f32[3,64,256]{2,1,0:T(8,128)S(1)}, u32[]{:S(2)}, u32[]{:S(2)}) collective-permute-start(f32[3,64,256]{2,1,0:T(8,128)S(1)} %get-tuple-element.82), channel_id=1, source_target_pairs={{0,8},{2,10},{4,12},{6,14},{8,0},{10,2},{12,4},{14,6},{16,24},{18,... | collective-permute-start | bytes 589832 | tf_op jit(solution)/shard_map/ppermute | solution.py:312
  115.7 18.0 %collective-permute-start.16 = (f32[3,64,256]{2,1,0:T(8,128)S(1)}, f32[3,64,256]{2,1,0:T(8,128)S(1)}, u32[]{:S(2)}, u32[]{:S(2)}) collective-permute-start(f32[3,64,256]{2,1,0:T(8,128)S(1)} %get-tuple-element.83), channel_id=1, source_target_pairs={{0,16},{2,18},{4,20},{6,22},{8,24},{10,26},{12,28},{14,30},{16,0},... | collective-permute-start | bytes 589832 | tf_op jit(solution)/shard_map/ppermute | solution.py:312
  119.0 14.8 %collective-permute-start.17 = (f32[3,64,256]{2,1,0:T(8,128)S(1)}, f32[3,64,256]{2,1,0:T(8,128)S(1)}, u32[]{:S(2)}, u32[]{:S(2)}) collective-permute-start(f32[3,64,256]{2,1,0:T(8,128)S(1)} %get-tuple-element.84), channel_id=1, source_target_pairs={{0,24},{2,26},{4,28},{6,30},{8,16},{10,18},{12,20},{14,22},{16,8},... | collective-permute-start | bytes 589832 | tf_op jit(solution)/shard_map/ppermute | solution.py:312
  133.8 18.0 %copy-start.12 = (f32[256,256]{1,0:T(8,128)S(1)}, f32[256,256]{1,0:T(8,128)}, u32[]{:S(2)}) copy-start(f32[256,256]{1,0:T(8,128)} %copy-done.11) | copy-start | bytes 786436
  133.8 18.0 %copy-start.14 = (f32[256,256]{1,0:T(8,128)S(1)}, f32[256,256]{1,0:T(8,128)}, u32[]{:S(2)}) copy-start(f32[256,256]{1,0:T(8,128)} %copy-done.13) | copy-start | bytes 786436
  133.8 18.0 %copy-start.16 = (f32[256,256]{1,0:T(8,128)S(1)}, f32[256,256]{1,0:T(8,128)}, u32[]{:S(2)}) copy-start(f32[256,256]{1,0:T(8,128)} %copy-done.15) | copy-start | bytes 786436
  133.9 9.6 %collective-permute-start.20 = (f32[3,64,256]{2,1,0:T(8,128)S(1)}, f32[3,64,256]{2,1,0:T(8,128)S(1)}, u32[]{:S(2)}, u32[]{:S(2)}) collective-permute-start(f32[3,64,256]{2,1,0:T(8,128)S(1)} %add_add_fusion.refs_4_.refs_0_), channel_id=1, source_target_pairs={{0,24},{2,26},{4,28},{6,30},{8,16},{10,18},{12,20},{14,22},{16,8},... | collective-permute-start | bytes 589832 | tf_op jit(solution)/shard_map/ppermute | solution.py:312
  136.3 15.5 %collective-permute-start.19 = (f32[3,64,256]{2,1,0:T(8,128)S(1)}, f32[3,64,256]{2,1,0:T(8,128)S(1)}, u32[]{:S(2)}, u32[]{:S(2)}) collective-permute-start(f32[3,64,256]{2,1,0:T(8,128)S(1)} %add_add_fusion.refs_4_.refs_0_), channel_id=1, source_target_pairs={{0,16},{2,18},{4,20},{6,22},{8,24},{10,26},{12,28},{14,30},{16,0},... | collective-permute-start | bytes 589832 | tf_op jit(solution)/shard_map/ppermute | solution.py:312
  138.2 13.5 %collective-permute-start.18 = (f32[3,64,256]{2,1,0:T(8,128)S(1)}, f32[3,64,256]{2,1,0:T(8,128)S(1)}, u32[]{:S(2)}, u32[]{:S(2)}) collective-permute-start(f32[3,64,256]{2,1,0:T(8,128)S(1)} %add_add_fusion.refs_4_.refs_0_), channel_id=1, source_target_pairs={{0,8},{2,10},{4,12},{6,14},{8,0},{10,2},{12,4},{14,6},{16,24},{18,... | collective-permute-start | bytes 589832 | tf_op jit(solution)/shard_map/ppermute | solution.py:312
  138.3 22.3 %collective-permute-start.12 = (f32[256,256]{1,0:T(8,128)S(1)}, f32[256,256]{1,0:T(8,128)S(1)}, u32[]{:S(2)}, u32[]{:S(2)}) collective-permute-start(f32[256,256]{1,0:T(8,128)S(1)} %get-tuple-element.78), channel_id=1, source_target_pairs={{0,2},{2,0},{4,6},{6,4},{8,10},{10,8},{12,14},{14,12},{16,18},{18,... | collective-permute-start | bytes 786440 | tf_op jit(solution)/shard_map/ppermute | solution.py:305
  155.6 8.8 %collective-permute-start.24 = (f32[3,64,256]{2,1,0:T(8,128)S(1)}, f32[3,64,256]{2,1,0:T(8,128)S(1)}, u32[]{:S(2)}, u32[]{:S(2)}) collective-permute-start(f32[3,64,256]{2,1,0:T(8,128)S(1)} %get-tuple-element.92), channel_id=1, source_target_pairs={{0,8},{2,10},{4,12},{6,14},{8,0},{10,2},{12,4},{14,6},{16,24},{18,... | collective-permute-start | bytes 589832 | tf_op jit(solution)/shard_map/ppermute | solution.py:312
  155.6 10.7 %collective-permute-start.25 = (f32[3,64,256]{2,1,0:T(8,128)S(1)}, f32[3,64,256]{2,1,0:T(8,128)S(1)}, u32[]{:S(2)}, u32[]{:S(2)}) collective-permute-start(f32[3,64,256]{2,1,0:T(8,128)S(1)} %get-tuple-element.93), channel_id=1, source_target_pairs={{0,16},{2,18},{4,20},{6,22},{8,24},{10,26},{12,28},{14,30},{16,0},... | collective-permute-start | bytes 589832 | tf_op jit(solution)/shard_map/ppermute | solution.py:312
  158.2 48.5 %collective-permute-start.21 = (f32[2,256,256]{2,1,0:T(8,128)S(1)}, f32[2,256,256]{2,1,0:T(8,128)S(1)}, u32[]{:S(2)}, u32[]{:S(2)}) collective-permute-start(f32[2,256,256]{2,1,0:T(8,128)S(1)} %get-tuple-element.86), channel_id=1, source_target_pairs={{0,2},{2,0},{4,6},{6,4},{8,10},{10,8},{12,14},{14,12},{16,18},{18,... | collective-permute-start | bytes 1572872 | tf_op jit(solution)/shard_map/ppermute | solution.py:305
  160.6 46.2 %collective-permute-start.22 = (f32[2,256,256]{2,1,0:T(8,128)S(1)}, f32[2,256,256]{2,1,0:T(8,128)S(1)}, u32[]{:S(2)}, u32[]{:S(2)}) collective-permute-start(f32[2,256,256]{2,1,0:T(8,128)S(1)} %get-tuple-element.87), channel_id=1, source_target_pairs={{0,4},{2,6},{4,0},{6,2},{8,12},{10,14},{12,8},{14,10},{16,20},{18,... | collective-permute-start | bytes 1572872 | tf_op jit(solution)/shard_map/ppermute | solution.py:305
  160.6 46.1 %collective-permute-start.23 = (f32[2,256,256]{2,1,0:T(8,128)S(1)}, f32[2,256,256]{2,1,0:T(8,128)S(1)}, u32[]{:S(2)}, u32[]{:S(2)}) collective-permute-start(f32[2,256,256]{2,1,0:T(8,128)S(1)} %get-tuple-element.88), channel_id=1, source_target_pairs={{0,6},{2,4},{4,2},{6,0},{8,14},{10,12},{12,10},{14,8},{16,22},{18,... | collective-permute-start | bytes 1572872 | tf_op jit(solution)/shard_map/ppermute | solution.py:305
  164.3 7.5 %collective-permute-start.26 = (f32[3,64,256]{2,1,0:T(8,128)S(1)}, f32[3,64,256]{2,1,0:T(8,128)S(1)}, u32[]{:S(2)}, u32[]{:S(2)}) collective-permute-start(f32[3,64,256]{2,1,0:T(8,128)S(1)} %get-tuple-element.94), channel_id=1, source_target_pairs={{0,24},{2,26},{4,28},{6,30},{8,16},{10,18},{12,20},{14,22},{16,8},... | collective-permute-start | bytes 589832 | tf_op jit(solution)/shard_map/ppermute | solution.py:312
  166.3 29.7 %collective-permute-start.13 = (f32[256,256]{1,0:T(8,128)S(1)}, f32[256,256]{1,0:T(8,128)S(1)}, u32[]{:S(2)}, u32[]{:S(2)}) collective-permute-start(f32[256,256]{1,0:T(8,128)S(1)} %get-tuple-element.79), channel_id=1, source_target_pairs={{0,4},{2,6},{4,0},{6,2},{8,12},{10,14},{12,8},{14,10},{16,20},{18,... | collective-permute-start | bytes 786440 | tf_op jit(solution)/shard_map/ppermute | solution.py:305
  171.9 24.5 %collective-permute-start.14 = (f32[256,256]{1,0:T(8,128)S(1)}, f32[256,256]{1,0:T(8,128)S(1)}, u32[]{:S(2)}, u32[]{:S(2)}) collective-permute-start(f32[256,256]{1,0:T(8,128)S(1)} %get-tuple-element.80), channel_id=1, source_target_pairs={{0,6},{2,4},{4,2},{6,0},{8,14},{10,12},{12,10},{14,8},{16,22},{18,... | collective-permute-start | bytes 786440 | tf_op jit(solution)/shard_map/ppermute | solution.py:305
  196.0 4.4 %collective-permute-start.27 = (f32[3,16,256]{2,1,0:T(8,128)S(1)}, f32[3,16,256]{2,1,0:T(8,128)S(1)}, u32[]{:S(2)}, u32[]{:S(2)}) collective-permute-start(f32[3,16,256]{2,1,0:T(8,128)S(1)} %get-tuple-element.96), channel_id=1, source_target_pairs={{0,2},{2,0},{4,6},{6,4},{8,10},{10,8},{12,14},{14,12},{16,18},{18,... | collective-permute-start | bytes 147464 | tf_op jit(solution)/shard_map/ppermute | solution.py:305
  196.3 5.9 %collective-permute-start.28 = (f32[3,16,256]{2,1,0:T(8,128)S(1)}, f32[3,16,256]{2,1,0:T(8,128)S(1)}, u32[]{:S(2)}, u32[]{:S(2)}) collective-permute-start(f32[3,16,256]{2,1,0:T(8,128)S(1)} %get-tuple-element.97), channel_id=1, source_target_pairs={{0,4},{2,6},{4,0},{6,2},{8,12},{10,14},{12,8},{14,10},{16,20},{18,... | collective-permute-start | bytes 147464 | tf_op jit(solution)/shard_map/ppermute | solution.py:305
  200.5 5.0 %collective-permute-start.29 = (f32[3,16,256]{2,1,0:T(8,128)S(1)}, f32[3,16,256]{2,1,0:T(8,128)S(1)}, u32[]{:S(2)}, u32[]{:S(2)}) collective-permute-start(f32[3,16,256]{2,1,0:T(8,128)S(1)} %get-tuple-element.98), channel_id=1, source_target_pairs={{0,6},{2,4},{4,2},{6,0},{8,14},{10,12},{12,10},{14,8},{16,22},{18,... | collective-permute-start | bytes 147464 | tf_op jit(solution)/shard_map/ppermute | solution.py:305

commit v2 on v1

v2 whole, which is shorter than its diff:
```python
import functools
import math

import jax
import jax.numpy as jnp
from jax import lax
from jax.experimental import pallas as pl
from jax.experimental.pallas import tpu as pltpu
from jax.sharding import PartitionSpec as P

F32 = jnp.float32
BF16 = jnp.bfloat16
LANES = 128
VMEM_LIMIT = 40 * 1024 * 1024


def mm(a, b):
    return jnp.dot(a, b, preferred_element_type=F32)


def mm_t(a, b):
    return lax.dot_general(a, b, (((1,), (1,)), ((), ())), preferred_element_type=F32)


def tmm(a, b):
    return lax.dot_general(a, b, (((0,), (0,)), ((), ())), preferred_element_type=F32)


def call(body, out_shape, scratch, flops, *args):
    smem = pl.BlockSpec(memory_space=pltpu.SMEM)
    vmem = pl.BlockSpec(memory_space=pltpu.VMEM)
    size = sum(a.size * a.dtype.itemsize for a in args)
    size += sum(math.prod(o.shape) * o.dtype.itemsize for o in out_shape)
    return pl.pallas_call(
        body,
        out_shape=out_shape,
        in_specs=[smem if a.dtype == jnp.int32 else vmem for a in args],
        out_specs=[vmem] * len(out_shape),
        scratch_shapes=scratch,
        compiler_params=pltpu.CompilerParams(vmem_limit_bytes=VMEM_LIMIT),
        cost_estimate=pl.CostEstimate(flops=flops, bytes_accessed=size, transcendentals=0),
    )(*args)


def put_rows(scratch, x):
    for i in range(scratch.shape[0]):
        scratch[i] = x[:, i * LANES : (i + 1) * LANES]


def take_head(scratch, head, tokens, heads):
    parts = [scratch[i, pl.ds(head, tokens, stride=heads), :] for i in range(scratch.shape[0])]
    return jnp.concatenate(parts, axis=1)


def put_head(scratch, head, x, tokens, heads):
    for i in range(scratch.shape[0]):
        scratch[i, pl.ds(head, tokens, stride=heads), :] = x[:, i * LANES : (i + 1) * LANES]


def rows_of(scratch):
    return jnp.concatenate([scratch[i] for i in range(scratch.shape[0])], axis=1)


def split_update(k, v, r, out, sk, sv):
    tokens, heads, width = k.shape
    put_rows(sk, k[...].astype(F32).reshape(tokens * heads, width))
    put_rows(sv, v[...].astype(F32).reshape(tokens * heads, width))
    for head in range(heads):
        out[head, 0] = take_head(sk, head, tokens, heads)
        scaled = take_head(sv, head, tokens, heads) * rate_column(r, head)
        out[head, 1] = scaled.astype(BF16).astype(F32)


def rate_column(r, head):
    return jnp.broadcast_to(r[head : head + 1, :], (8, r.shape[1])).T[:, 0:1]


def split_apply(groups, place, q, cot, gain, *rest):
    outs, (sq, sc) = rest[:groups], rest[groups:]
    tokens, heads, width = q.shape
    put_rows(sq, q[...].astype(F32).reshape(tokens * heads, width))
    put_rows(sc, cot[...].astype(F32).reshape(tokens * heads, width))
    for step in range(groups):
        head = place[0] ^ step
        outs[step][0] = take_head(sq, head, tokens, heads)
        outs[step][1] = take_head(sc, head, tokens, heads) * gain[pl.ds(head, 1), :]


def cut(total, i, out):
    rows = out.shape[2]
    for z in range(out.shape[0]):
        out[z, i] = total[z * rows : (z + 1) * rows]


def update_kernel(scale, place, pieces, w_gate, w_out, w_up, out):
    weights = (w_gate, w_out, w_up)
    gate_b, out_b, up_b = (w[...].astype(BF16) for w in weights)
    total = [0.0, 0.0, 0.0]
    for source in range(pieces.shape[0]):
        keys = pieces[source, 0].astype(BF16)
        scaled = pieces[source, 1].astype(BF16)
        first = mm(keys, gate_b)
        third = mm(keys, up_b)
        sig = jax.nn.sigmoid(first)
        activ = first * sig
        act = (activ * third).astype(BF16)
        dact = mm_t(scaled, out_b)
        deriv = sig * (1.0 + first * (1.0 - sig))
        dfirst = (dact * third * deriv).astype(BF16)
        dthird = (dact * activ).astype(BF16)
        total[0] += tmm(keys, dfirst)
        total[1] += tmm(act, scaled)
        total[2] += tmm(keys, dthird)
    rows = out.shape[2]
    at = pl.multiple_of(place[1] * rows, rows)
    for i in range(3):
        cut(total[i] * scale, i, out)
        out[place[1], i] += weights[i][pl.ds(at, rows), :]


def sum_spread_kernel(parts, out):
    total = parts[0]
    for z in range(1, parts.shape[0]):
        total += parts[z]
    for z in range(parts.shape[0]):
        out[z] = total


def whole(parts, i):
    return jnp.concatenate([parts[z, i] for z in range(parts.shape[0])], axis=0)


def apply_forward(queries, new_b):
    first = mm(queries, new_b[0])
    third = mm(queries, new_b[2])
    sig = jax.nn.sigmoid(first)
    activ = first * sig
    hidden = (activ * third).astype(BF16)
    return first, third, sig, activ, hidden


def apply_kernel(groups, place, head_scale, parts, *refs):
    pieces, out = refs[:groups], refs[groups]
    new_b = [whole(parts, i).astype(BF16) for i in range(3)]
    for step, piece in enumerate(pieces):
        tokens = piece.shape[1]
        hidden = apply_forward(piece[0].astype(BF16), new_b)[4]
        scaled = mm(hidden, new_b[1]) * head_scale[...]
        sq = jnp.sum(scaled * scaled, axis=1, keepdims=True)
        ps = jnp.sum(scaled * piece[1], axis=1, keepdims=True)
        lane = lax.broadcasted_iota(jnp.int32, (tokens, LANES), 1)
        both = jnp.where(lane == 0, sq, jnp.where(lane == 1, ps, 0.0)).T[0:8, :]
        for copy in range(out.shape[0]):
            out[copy, place[0] ^ step] = both


def apply_back_kernel(groups, count, place, head_scale, parts, stats, *refs):
    pieces, outs, slices = refs[:groups], refs[groups : 2 * groups], refs[2 * groups]
    new_b = [whole(parts, i).astype(BF16) for i in range(3)]
    hs = head_scale[...]
    total = [0.0, 0.0, 0.0]
    for step, piece in enumerate(pieces):
        source = place[0] ^ step
        both = stats[0, source]
        for device in range(1, stats.shape[0]):
            both += stats[device, source]
        both = both.T
        sq = both[:, 0:1]
        ps = both[:, 1:2]
        inv = lax.rsqrt(sq / count + 1e-06)
        queries = piece[0].astype(BF16)
        first, third, sig, activ, hidden = apply_forward(queries, new_b)
        scaled = mm(hidden, new_b[1]) * hs
        dos = inv * piece[1] - scaled * (inv * inv * inv * ps / count)
        dout = (dos * hs).astype(BF16)
        dhidden = mm_t(dout, new_b[1])
        dthird = (dhidden * activ).astype(BF16)
        dfirst = (dhidden * third * (sig * (1.0 + first * (1.0 - sig)))).astype(BF16)
        outs[step][...] = mm_t(dfirst, new_b[0]) + mm_t(dthird, new_b[2])
        total[0] += tmm(queries, dfirst)
        total[1] += tmm(hidden, dout)
        total[2] += tmm(queries, dthird)
    for i in range(3):
        cut(total[i], i, slices)


def update_back_kernel(groups, scale, place, pieces, parts, w_gate, w_out, w_up, *rest):
    outs, slices = rest[:groups], rest[groups]
    gate_b, out_b, up_b = (w[...].astype(BF16) for w in (w_gate, w_out, w_up))
    cot_gate, cot_out, cot_up = ((whole(parts, i) * scale).astype(BF16) for i in range(3))
    total = [0.0, 0.0, 0.0]
    for step, out in enumerate(outs):
        source = place[0] ^ step
        keys = pieces[source, 0].astype(BF16)
        scaled = pieces[source, 1].astype(BF16)
        first = mm(keys, gate_b)
        third = mm(keys, up_b)
        sig = jax.nn.sigmoid(first)
        activ = first * sig
        act = (activ * third).astype(BF16)
        dact = mm_t(scaled, out_b)
        slope = sig * (1.0 - sig)
        deriv = sig + first * slope
        second = slope * (2.0 + first * (1.0 - 2.0 * sig))
        third_deriv = third * deriv
        dfirst = (dact * third_deriv).astype(BF16)
        dthird = (dact * activ).astype(BF16)
        bar_dfirst = mm(keys, cot_gate)
        bar_dthird = mm(keys, cot_up)
        bar_act = mm_t(scaled, cot_out)
        bar_activ = bar_dthird * dact + bar_act * third
        bar_dact = (bar_dfirst * third_deriv + bar_dthird * activ).astype(BF16)
        bar_df_dact = bar_dfirst * dact
        bar_third = (bar_df_dact * deriv + bar_act * activ).astype(BF16)
        bar_first = (bar_activ * deriv + bar_df_dact * third * second).astype(BF16)
        out[0] = (
            mm_t(dfirst, cot_gate)
            + mm_t(dthird, cot_up)
            + mm_t(bar_first, gate_b)
            + mm_t(bar_third, up_b)
        )
        out[1] = mm(act, cot_out) + mm(bar_dact, out_b)
        total[0] += tmm(keys, bar_first)
        total[1] += tmm(bar_dact, scaled)
        total[2] += tmm(keys, bar_third)
    for i in range(3):
        cut(total[i], i, slices)


def join_query_kernel(groups, place, *refs):
    pieces, out, scratch = refs[:groups], refs[groups], refs[groups + 1]
    tokens, heads, width = out.shape
    for step, piece in enumerate(pieces):
        put_head(scratch, place[0] ^ step, piece[...], tokens, heads)
    out[...] = rows_of(scratch).reshape(tokens, heads, width).astype(BF16)


def join_update_kernel(groups, place, r, *refs):
    pieces, (out_k, out_v, sk, sv) = refs[:groups], refs[groups:]
    tokens, heads, width = out_k.shape
    for step, piece in enumerate(pieces):
        head = place[0] ^ step
        rate = jnp.broadcast_to(r[pl.ds(head, 1), :], (8, tokens)).T[:, 0:1]
        put_head(sk, head, piece[0], tokens, heads)
        put_head(sv, head, piece[1] * rate, tokens, heads)
    out_k[...] = rows_of(sk).reshape(tokens, heads, width).astype(BF16)
    out_v[...] = rows_of(sv).reshape(tokens, heads, width).astype(BF16)


def rows_kernel(place, first, second, out):
    total = first[place[1]]
    for z in range(second.shape[0]):
        total += second[z]
    rows = out.shape[2]
    for group in range(out.shape[0]):
        out[group] = total[:, group * rows : (group + 1) * rows]


def local(queries, keys, values, rates, head_scale, gain, w_gate, w_out, w_up, cotangent):
    tokens, heads, width = keys.shape[1:]
    hidden = w_gate.shape[2]
    ctx = lax.axis_size("ctx")
    head_axis = lax.axis_size("head")
    groups = heads
    depth = ctx // groups
    assert groups & (groups - 1) == 0 and depth * groups == ctx
    scale = 1.0 / math.sqrt(tokens * ctx * width)
    count = float(heads * head_axis * width)
    me = lax.axis_index("ctx")
    mine, layer = lax.rem(me, groups), lax.div(me, groups)
    place = jnp.stack([mine, layer]).astype(jnp.int32)
    planes = [[z * groups + p for p in range(groups)] for z in range(depth)]
    columns = [[z * groups + p for z in range(depth)] for p in range(groups)]
    block = groups * head_axis
    planes_heads = [list(range(i, i + block)) for i in range(0, ctx * head_axis, block)]

    def swap(x, axes, sets):
        return lax.all_to_all(x, axes, 0, 0, axis_index_groups=sets, tiled=True)

    def in_plane(x, step):
        return lax.ppermute(x, "ctx", [(c, c ^ step) for c in range(ctx)])

    def exchange(parts):
        return [parts[0]] + [in_plane(p, step) for step, p in enumerate(parts) if step]

    def shape(*dims, dtype=F32):
        return jax.ShapeDtypeStruct(dims, dtype)

    flops = 2 * groups * tokens * width * hidden
    pieces_shape = shape(groups, 2, tokens, width)
    slices = shape(depth, 3, hidden // depth, width)
    scratch = pltpu.VMEM((width // LANES, tokens * heads, LANES), F32)

    (sent,) = call(
        split_update, [pieces_shape], [scratch] * 2, flops // 8, keys[0], values[0], rates[0]
    )
    pieces = swap(sent, "ctx", planes)
    own = [lax.dynamic_index_in_dim(w, mine, 0, keepdims=False) for w in (w_gate, w_out, w_up)]
    own_scale = lax.dynamic_index_in_dim(head_scale, mine, 0, keepdims=True)[None, :]
    pieces, queries, cotangent = lax.optimization_barrier((pieces, queries, cotangent))
    sent = call(
        functools.partial(split_apply, groups), [shape(2, tokens, width)] * groups,
        [scratch] * 2, flops // 8, place, queries[0], cotangent[0], gain,
    )
    q_pieces = exchange(sent)
    (terms,) = call(
        functools.partial(update_kernel, scale), [slices], [], 6 * flops, place, pieces, *own
    )
    terms = swap(terms, "ctx", columns)
    new = swap(call(sum_spread_kernel, [slices], [], flops // 100, terms)[0], "ctx", columns)
    (stats,) = call(
        functools.partial(apply_kernel, groups), [shape(block, groups, 8, tokens)], [],
        3 * flops, place, own_scale, new, *q_pieces,
    )
    stats = swap(stats, ("ctx", "head"), planes_heads)
    out = call(
        functools.partial(apply_back_kernel, groups, count),
        [shape(tokens, width)] * groups + [slices], [], 9 * flops,
        place, own_scale, new, stats, *q_pieces,
    )
    q_back = exchange(out[:groups])
    parts = swap(out[groups], "ctx", columns)
    parts = swap(call(sum_spread_kernel, [slices], [], flops // 100, parts)[0], "ctx", columns)
    (grad_q,) = call(
        functools.partial(join_query_kernel, groups),
        [shape(tokens, heads, width, dtype=BF16)], [scratch], flops // 16, place, *q_back,
    )
    out = call(
        functools.partial(update_back_kernel, groups, scale),
        [shape(2, tokens, width)] * groups + [slices], [], 15 * flops, place, pieces, parts, *own,
    )
    back = exchange(out[:groups])
    ends = swap(out[groups], "ctx", columns)
    rows = hidden // ctx
    (sent,) = call(
        rows_kernel, [shape(groups, 3, rows, width)], [], flops // 100, place, parts, ends
    )
    grads = swap(sent, "ctx", planes)
    grad_k, grad_v = call(
        functools.partial(join_update_kernel, groups),
        [shape(tokens, heads, width, dtype=BF16)] * 2, [scratch] * 2, flops // 8,
        place, rates[0], *back,
    )
    grads = [grads[:, i] for i in range(3)]
    if lax.axis_size("batch") > 1:
        grads = [lax.psum_scatter(x, "batch", scatter_dimension=1, tiled=True) for x in grads]
    return (grad_q[None], grad_k[None], grad_v[None], grads[0], grads[1], grads[2])


def solution(mesh):
    in_specs = (
        P("batch", "ctx", "head", None),
        P("batch", "ctx", "head", None),
        P("batch", "ctx", "head", None),
        P("batch", "head", "ctx"),
        P("head"),
        P("head", None),
        P("head", None, None),
        P("head", None, None),
        P("head", None, None),
        P("batch", "ctx", "head", None),
    )
    out_specs = (
        P("batch", "ctx", "head", None),
        P("batch", "ctx", "head", None),
        P("batch", "ctx", "head", None),
        P("head", ("ctx", "batch"), None),
        P("head", ("ctx", "batch"), None),
        P("head", ("ctx", "batch"), None),
    )
    return jax.shard_map(local, mesh=mesh, in_specs=in_specs, out_specs=out_specs, check_vma=False)
```

time: 210 us -> 226 us (1.076)
  blocking collectives: 23.7 us -> 80.1 us
  waiting for transfers between devices: 101 us -> 69.3 us
  starting transfers between devices: 49.7 us -> 26.9 us
  local copies, waits for them, and re-layouts: 12.7 us -> 25.6 us
    all_to_all x0 -> x4, blocking collectives: none -> 80.1 us  [swap(): return lax.all_to_all(x, axes, 0, 0, axis_index_groups=sets, tiled=True)]
    ppermute x30 -> x9, waiting for transfers between devices: 101 us -> 37.9 us  [in_plane(): return lax.ppermute(x, 'ctx', [(c, c ^ step) for c in range(ctx)])]
    ppermute x30 -> x9, starting transfers between devices: 49.7 us -> 9.94 us  [in_plane(): return lax.ppermute(x, 'ctx', [(c, c ^ step) for c in range(ctx)])]
    all_to_all x0 -> x4, waiting for transfers between devices: none -> 31.3 us  [swap(): return lax.all_to_all(x, axes, 0, 0, axis_index_groups=sets, tiled=True)]
    psum x1 -> x0, blocking collectives: 23.7 us -> none  [local(): stats = lax.psum(stats, ('ctx', 'head'), axis_index_groups=sets)]
    all_to_all x0 -> x4, starting transfers between devices: none -> 17 us  [swap(): return lax.all_to_all(x, axes, 0, 0, axis_index_groups=sets, tiled=True)]
    unnamed x60 -> x72, local copies, waits for them, and re-layouts: 10.9 us -> 21.5 us
    pallas_call x10 -> x11, Pallas kernels: 21.1 us -> 21.6 us  [call(): pl.pallas_call(body, out_shape=out_shape, in_specs=[smem if a.dtype == jn...]
  transfers between devices with their start and end apart: 30 -> 13, of which waited for: 17 -> 6; matrix products, arithmetic and copies ran while one was open for 1% -> 1% of each run, Pallas kernels for 4% -> 4%
where the time goes in v2:
time: 226 us; the launch traced here: 224 us
  blocking collectives  80.1 us (35%)
  waiting for transfers between devices  69.3 us (31%)
  starting transfers between devices  26.9 us (12%)
  local copies, waits for them, and re-layouts  25.6 us (11%)
  Pallas kernels  21.6 us (10%)
    all_to_all x4, blocking collectives, swap(): return lax.all_to_all(x, axes, 0, 0, axis_index_groups=sets, tiled=True)  80.1 us
    ppermute x9, waiting for transfers between devices, in_plane(): return lax.ppermute(x, 'ctx', [(c, c ^ step) for c in range(ctx)])  37.9 us
    all_to_all x4, waiting for transfers between devices, swap(): return lax.all_to_all(x, axes, 0, 0, axis_index_groups=sets, tiled=True)  31.3 us
    pallas_call x11, Pallas kernels, call(): pl.pallas_call(body, out_shape=out_shape, in_specs=[smem if a.dtype == jn...  21.6 us
    unnamed x72, local copies, waits for them, and re-layouts  21.5 us
    all_to_all x4, starting transfers between devices, swap(): return lax.all_to_all(x, axes, 0, 0, axis_index_groups=sets, tiled=True)  17 us
    ppermute x9, starting transfers between devices, in_plane(): return lax.ppermute(x, 'ctx', [(c, c ^ step) for c in range(ctx)])  9.94 us
  transfers between devices with their start and end apart: 13, of which 6 were waited for; matrix products, arithmetic and copies ran while one was open for 1% of the time, Pallas kernels for 4%

profile of v2, /device:TPU:0, one launch (start us, length us, event | category | flops | bytes accessed | tf_op | source)
XLA Modules:
  0.0 224.5 jit_solution(10795372318794013719)
XLA Ops:
  0.6 0.0 copy-start
  0.7 1.1 copy-done.14
  1.8 1.0 copy-done.15
  2.8 0.7 copy-done.26
  3.5 0.6 shard_map.145
  4.2 1.3 copy-done.1
  5.5 5.2 %all-to-all-start = ((f32[4,2,256,256]{3,2,1,0:T(8,128)}), f32[4,2,256,256]{3,2,1,0:T(8,128)S(1)}, u32[]{:S(2)}, u32[]{:S(2)}) async-start(f32[4,2,256,256]{3,2,1,0:T(8,128)} %copy-done.1), calls=%async_computation | async-start | bytes 4194304 | tf_op jit(solution)/shard_map/all_to_all | solution.py:278
  10.7 0.1 pad_add_fusion.place
  10.8 1.9 dynamic-slice_bitcast_fusion
  12.6 22.9 %all-to-all-done.pieces = f32[4,2,256,256]{3,2,1,0:T(8,128)S(1)} async-done(((f32[4,2,256,256]{3,2,1,0:T(8,128)}), f32[4,2,256,256]{3,2,1,0:T(8,128)S(1)}, u32[]{:S(2)}, u32[]{:S(2)}) %all-to-all-start) | async-done | bytes 2097184 | tf_op jit(solution)/shard_map/all_to_all | solution.py:278
  35.5 0.9 copy-done.5
  36.5 0.9 copy-done.7
  37.4 2.1 shard_map.146
  39.5 0.0 copy-start.28
  39.5 24.1 %all_to_all.40.parts = f32[4,3,64,256]{3,2,1,0:T(8,128)S(1)} all-to-all(f32[4,3,64,256]{3,2,1,0:T(8,128)S(1)} %shard_map.146), channel_id=1, replica_groups={{0,8,16,24},{2,10,18,26},{4,12,20,28},{6,14,22,30},{1,9,17,25},{3,11,19..., dimensions={0} | all-to-all | bytes 1572864 | tf_op jit(solution)/shard_map/all_to_all | solution.py:278
  63.7 0.1 shard_map.147
  63.7 0.9 copy-done.2
  64.6 4.2 %all-to-all-start.2 = ((f32[4,3,64,256]{3,2,1,0:T(8,128)}), f32[4,3,64,256]{3,2,1,0:T(8,128)}, u32[]{:S(2)}, u32[]{:S(2)}) async-start(f32[4,3,64,256]{3,2,1,0:T(8,128)} %copy-done.2), calls=%async_computation.2 | async-start | bytes 1572864 | tf_op jit(solution)/shard_map/all_to_all | solution.py:278
  68.8 0.0 copy-start.12
  68.8 1.0 copy-done.12
  69.8 1.0 copy-done.13
  70.9 1.2 shard_map.148
  72.1 0.8 copy-done.16
  72.9 1.2 collective-permute-start
  74.1 0.7 collective-permute-start.1
  74.8 1.6 collective-permute-start.2
  76.4 0.6 dynamic_slice.14
  77.0 10.8 %collective-permute-done.refs_1_ = f32[2,256,256]{2,1,0:T(8,128)S(1)} collective-permute-done((f32[2,256,256]{2,1,0:T(8,128)S(1)}, f32[2,256,256]{2,1,0:T(8,128)S(1)}, u32[]{:S(2)}, u32[]{:S(2)}) %collective-permute-start) | collective-permute-done | bytes 524320 | tf_op jit(solution)/shard_map/ppermute | solution.py:281
  87.8 0.8 copy-done.18
  88.5 9.0 %collective-permute-done.1.refs_2_ = f32[2,256,256]{2,1,0:T(8,128)S(1)} collective-permute-done((f32[2,256,256]{2,1,0:T(8,128)S(1)}, f32[2,256,256]{2,1,0:T(8,128)S(1)}, u32[]{:S(2)}, u32[]{:S(2)}) %collective-permute-start.1) | collective-permute-done | bytes 524320 | tf_op jit(solution)/shard_map/ppermute | solution.py:281
  97.5 0.8 copy-done.20
  98.3 0.8 copy-done.22
  99.1 1.0 copy-done.17
  100.2 1.0 copy-done.19
  101.2 1.0 copy-done.21
  102.2 1.0 copy-done.23
  103.3 2.9 %shard_map.149 = f32[8,4,8,256]{3,2,1,0:T(8,128)S(1)} custom-call(s32[2]{0:T(128)S(1)} %pad_add_fusion.place, f32[1,1]{1,0:T(1,128)} %bitcast.2.head_scale, f32[4,3,64,256]{3,2,1,0:T(8,128)} %all-to-all-done.2.parts, f32[2,256,256]{2,1,0:T(8,128)S(1)} %copy-done.17, f32[2,256,256]{2,1,0:T(8,128)S(1)} %copy-done.19, f32[2,256,256]{2,1,0:T(8,128)S(1)} %copy-done.21, ...), custom_call_target="tpu_custom_call" | custom-call | flops 402653184 | bytes 3145740 | tf_op jit(solution)/shard_map/pallas_call | solution.py:34
  106.2 9.6 %all_to_all.41.stats = f32[8,4,8,256]{3,2,1,0:T(8,128)S(1)} all-to-all(f32[8,4,8,256]{3,2,1,0:T(8,128)S(1)} %shard_map.149), channel_id=1, replica_groups={{0,1,2,3,4,5,6,7},{8,9,10,11,12,13,14,15},{16,17,18,19,20,21,22,23},{24..., dimensions={0} | all-to-all | bytes 524288 | tf_op jit(solution)/shard_map/all_to_all | solution.py:278
  115.8 4.4 %shard_map.150 = (f32[256,256]{1,0:T(8,128)S(1)}, f32[256,256]{1,0:T(8,128)S(1)}, f32[256,256]{1,0:T(8,128)S(1)}, f32[256,256]{1,0:T(8,128)S(1)}, f32[4,3,64,256]{3,2,1,0:T(8,128)S(1)}) custom-call(s32[2]{0:T(128)S(1)} %pad_add_fusion.place, f32[1,1]{1,0:T(1,128)} %bitcast.2.head_scale, f32[4,3,64,256]{3,2,1,0:T(8,128)} %all-to-all-done.2.parts, ...), custom_call_target="tpu_custom_call" | custom-call | flops 1207959552 | bytes 4980748 | tf_op jit(solution)/shard_map/pallas_call | solution.py:34
  120.3 24.2 %all_to_all.42.parts = f32[4,3,64,256]{3,2,1,0:T(8,128)S(1)} all-to-all(f32[4,3,64,256]{3,2,1,0:T(8,128)S(1)} %get-tuple-element.36), channel_id=1, replica_groups={{0,8,16,24},{2,10,18,26},{4,12,20,28},{6,14,22,30},{1,9,17,25},{3,11,19..., dimensions={0} | all-to-all | bytes 1572864 | tf_op jit(solution)/shard_map/all_to_all | solution.py:278
  144.5 0.1 shard_map.152
  144.5 22.1 %all_to_all.43.parts.first = f32[4,3,64,256]{3,2,1,0:T(8,128)S(1)} all-to-all(f32[4,3,64,256]{3,2,1,0:T(8,128)S(1)} %shard_map.152), channel_id=1, replica_groups={{0,8,16,24},{2,10,18,26},{4,12,20,28},{6,14,22,30},{1,9,17,25},{3,11,19..., dimensions={0} | all-to-all | bytes 1572864 | tf_op jit(solution)/shard_map/all_to_all | solution.py:278
  166.7 3.6 %shard_map.153 = (f32[2,256,256]{2,1,0:T(8,128)S(1)}, f32[2,256,256]{2,1,0:T(8,128)S(1)}, f32[2,256,256]{2,1,0:T(8,128)S(1)}, f32[2,256,256]{2,1,0:T(8,128)S(1)}, f32[4,3,64,256]{3,2,1,0:T(8,128)S(1)}) custom-call(s32[2]{0:T(128)S(1)} %pad_add_fusion.place, f32[4,2,256,256]{3,2,1,0:T(8,128)S(1)} %all-to-all-done.pieces, ...), custom_call_target="tpu_custom_call" | custom-call | flops 2013265920 | bytes 6553608 | tf_op jit(solution)/shard_map/pallas_call | solution.py:34
  170.3 0.9 copy-done.9
  171.2 0.8 copy-done.10
  172.0 0.8 copy-done.29
  172.8 0.8 copy-done.30
  173.6 0.8 copy-done.31
  174.4 3.6 %all-to-all-start.6 = ((f32[4,3,64,256]{3,2,1,0:T(8,128)}), f32[4,3,64,256]{3,2,1,0:T(8,128)S(1)}, u32[]{:S(2)}, u32[]{:S(2)}) async-start(f32[4,3,64,256]{3,2,1,0:T(8,128)} %copy-done.9), calls=%async_computation.6 | async-start | bytes 1572864 | tf_op jit(solution)/shard_map/all_to_all | solution.py:278
  178.0 1.4 collective-permute-start.3
  179.4 0.7 collective-permute-start.6
  180.1 0.6 collective-permute-start.7
  180.7 2.2 collective-permute-start.8
  182.9 0.4 collective-permute-start.4
  183.3 4.2 %collective-permute-done.3.refs_1_ = f32[256,256]{1,0:T(8,128)S(1)} collective-permute-done((f32[256,256]{1,0:T(8,128)}, f32[256,256]{1,0:T(8,128)S(1)}, u32[]{:S(2)}, u32[]{:S(2)}) %collective-permute-start.3) | collective-permute-done | bytes 262176 | tf_op jit(solution)/shard_map/ppermute | solution.py:281
  187.5 1.2 collective-permute-start.5
  188.7 8.4 %all-to-all-done.6.second = f32[4,3,64,256]{3,2,1,0:T(8,128)S(1)} async-done(((f32[4,3,64,256]{3,2,1,0:T(8,128)}), f32[4,3,64,256]{3,2,1,0:T(8,128)S(1)}, u32[]{:S(2)}, u32[]{:S(2)}) %all-to-all-start.6) | async-done | bytes 786464 | tf_op jit(solution)/shard_map/all_to_all | solution.py:278
  197.1 1.3 shard_map.155
  198.4 4.0 %all-to-all-start.7 = ((f32[4,3,16,256]{3,2,1,0:T(8,128)}), f32[4,3,16,256]{3,2,1,0:T(8,128)}, u32[]{:S(2)}, u32[]{:S(2)}) async-start(f32[4,3,16,256]{3,2,1,0:T(8,128)} %shard_map.155), calls=%async_computation.7 | async-start | bytes 393216 | tf_op jit(solution)/shard_map/all_to_all | solution.py:278
  202.4 13.9 %collective-permute-done.4.refs_2_ = f32[256,256]{1,0:T(8,128)} collective-permute-done((f32[256,256]{1,0:T(8,128)}, f32[256,256]{1,0:T(8,128)}, u32[]{:S(2)}, u32[]{:S(2)}) %collective-permute-start.4) | collective-permute-done | bytes 262176 | tf_op jit(solution)/shard_map/ppermute | solution.py:281
  216.4 2.2 shard_map.151
  218.6 1.0 copy-done.11
  219.7 3.2 %shard_map.154 = (bf16[256,4,256]{2,1,0:T(4,128)(2,1)}, bf16[256,4,256]{2,1,0:T(4,128)(2,1)}) custom-call(s32[2]{0:T(128)S(1)} %pad_add_fusion.place, f32[4,256]{1,0:T(4,128)S(1)} %bitcast.28, f32[2,256,256]{2,1,0:T(8,128)S(1)} %copy-done.11, f32[2,256,256]{2,1,0:T(8,128)} %collective-permute-done.6.refs_1_, f32[2,256,256]{2,1,0:T(8,128)} %collective-permute-done.7.refs_2_, ...), custom_call_target="tpu_custom_call" | custom-call | flops 16777216 | bytes 3149832 | tf_op jit(solution)/shard_map/pallas_call | solution.py:34
  222.9 1.6 slice_bitcast_fusion
  (54 shorter events, 0.1 us)
Async XLA Ops:
  0.6 10.1 %copy-start = (f32[4,256,256]{2,1,0:T(8,128)S(1)}, f32[4,256,256]{2,1,0:T(8,128)}, u32[]{:S(2)}) copy-start(f32[4,256,256]{2,1,0:T(8,128)} %param.16) | copy-start | bytes 3145732
  0.6 1.1 copy-start.14
  1.8 1.0 copy-start.15
  2.8 0.7 copy-start.26
  4.2 1.3 copy-start.1
  5.5 30.0 %all-to-all-start = ((f32[4,2,256,256]{3,2,1,0:T(8,128)}), f32[4,2,256,256]{3,2,1,0:T(8,128)S(1)}, u32[]{:S(2)}, u32[]{:S(2)}) async-start(f32[4,2,256,256]{3,2,1,0:T(8,128)} %copy-done.1), calls=%async_computation | async-start | bytes 4194304 | tf_op jit(solution)/shard_map/all_to_all | solution.py:278
  35.5 1.0 copy-start.5
  36.5 0.9 copy-start.7
  39.5 29.3 %copy-start.28 = (f32[4,256]{1,0:T(4,128)S(1)}, f32[4,256]{1,0:T(4,128)}, u32[]{:S(2)}) copy-start(f32[4,256]{1,0:T(4,128)} %gain.1) | copy-start | bytes 12292
  63.7 12.7 %copy-start.35 = (f32[4]{0:T(128)S(1)}, f32[4]{0:T(128)}, u32[]{:S(2)}) copy-start(f32[4]{0:T(128)} %param.14) | copy-start | bytes 52
  63.7 0.9 copy-start.2
  64.6 34.5 %all-to-all-start.2 = ((f32[4,3,64,256]{3,2,1,0:T(8,128)}), f32[4,3,64,256]{3,2,1,0:T(8,128)}, u32[]{:S(2)}, u32[]{:S(2)}) async-start(f32[4,3,64,256]{3,2,1,0:T(8,128)} %copy-done.2), calls=%async_computation.2 | async-start | bytes 1572864 | tf_op jit(solution)/shard_map/all_to_all | solution.py:278
  68.8 1.0 copy-start.12
  69.8 1.0 copy-start.13
  72.1 0.8 copy-start.16
  72.9 14.9 %collective-permute-start = (f32[2,256,256]{2,1,0:T(8,128)S(1)}, f32[2,256,256]{2,1,0:T(8,128)S(1)}, u32[]{:S(2)}, u32[]{:S(2)}) collective-permute-start(f32[2,256,256]{2,1,0:T(8,128)S(1)} %get-tuple-element.29), channel_id=1, source_target_pairs={{0,2},{2,0},{4,6},{6,4},{8,10},{10,8},{12,14},{14,12},{16,18},{18,... | collective-permute-start | bytes 1572872 | tf_op jit(solution)/shard_map/ppermute | solution.py:281
  74.1 23.4 %collective-permute-start.1 = (f32[2,256,256]{2,1,0:T(8,128)S(1)}, f32[2,256,256]{2,1,0:T(8,128)S(1)}, u32[]{:S(2)}, u32[]{:S(2)}) collective-permute-start(f32[2,256,256]{2,1,0:T(8,128)S(1)} %get-tuple-element.30), channel_id=1, source_target_pairs={{0,4},{2,6},{4,0},{6,2},{8,12},{10,14},{12,8},{14,10},{16,20},{18,... | collective-permute-start | bytes 1572872 | tf_op jit(solution)/shard_map/ppermute | solution.py:281
  74.8 23.5 %collective-permute-start.2 = (f32[2,256,256]{2,1,0:T(8,128)S(1)}, f32[2,256,256]{2,1,0:T(8,128)S(1)}, u32[]{:S(2)}, u32[]{:S(2)}) collective-permute-start(f32[2,256,256]{2,1,0:T(8,128)S(1)} %get-tuple-element.31), channel_id=1, source_target_pairs={{0,6},{2,4},{4,2},{6,0},{8,14},{10,12},{12,10},{14,8},{16,22},{18,... | collective-permute-start | bytes 1572872 | tf_op jit(solution)/shard_map/ppermute | solution.py:281
  87.8 0.8 copy-start.18
  97.5 0.8 copy-start.20
  98.3 0.8 copy-start.22
  99.1 1.0 copy-start.17
  100.1 1.0 copy-start.19
  101.2 1.0 copy-start.21
  102.2 1.0 copy-start.23
  120.2 24.3 %copy-start.24 = (f32[256,256]{1,0:T(8,128)}, f32[256,256]{1,0:T(8,128)S(1)}, u32[]{:S(2)}) copy-start(f32[256,256]{1,0:T(8,128)S(1)} %get-tuple-element.32.refs_0_) | copy-start | bytes 786436
  120.2 24.3 %copy-start.34 = (f32[256,256]{1,0:T(8,128)}, f32[256,256]{1,0:T(8,128)S(1)}, u32[]{:S(2)}) copy-start(f32[256,256]{1,0:T(8,128)S(1)} %get-tuple-element.33) | copy-start | bytes 786436
  120.2 46.4 %copy-start.32 = (f32[256,256]{1,0:T(8,128)}, f32[256,256]{1,0:T(8,128)S(1)}, u32[]{:S(2)}) copy-start(f32[256,256]{1,0:T(8,128)S(1)} %get-tuple-element.35) | copy-start | bytes 786436
  120.2 46.4 %copy-start.33 = (f32[256,256]{1,0:T(8,128)}, f32[256,256]{1,0:T(8,128)S(1)}, u32[]{:S(2)}) copy-start(f32[256,256]{1,0:T(8,128)S(1)} %get-tuple-element.34) | copy-start | bytes 786436
  120.3 46.4 %copy-start.6 = (f32[256,256]{1,0:T(8,128)S(1)}, f32[256,256]{1,0:T(8,128)}, u32[]{:S(2)}) copy-start(f32[256,256]{1,0:T(8,128)} %get-tuple-element.47.w_up) | copy-start | bytes 786436
  120.3 46.4 %copy-start.8 = (f32[256,256]{1,0:T(8,128)S(1)}, f32[256,256]{1,0:T(8,128)}, u32[]{:S(2)}) copy-start(f32[256,256]{1,0:T(8,128)} %get-tuple-element.48.w_out) | copy-start | bytes 786436
  166.7 3.6 %copy-start.3 = (f32[4,3,64,256]{3,2,1,0:T(8,128)}, f32[4,3,64,256]{3,2,1,0:T(8,128)S(1)}, u32[]{:S(2)}) copy-start(f32[4,3,64,256]{3,2,1,0:T(8,128)S(1)} %all_to_all.43.parts.first) | copy-start | bytes 2359300
  170.3 0.9 copy-start.9
  171.2 0.8 copy-start.10
  172.0 0.8 copy-start.29
  172.8 0.8 copy-start.30
  173.6 0.8 copy-start.31
  174.4 42.0 %copy-start.25 = (f32[256,256]{1,0:T(8,128)S(1)}, f32[256,256]{1,0:T(8,128)}, u32[]{:S(2)}) copy-start(f32[256,256]{1,0:T(8,128)} %copy-done.24) | copy-start | bytes 786436
  174.4 22.8 %copy-start.4 = (f32[4,3,64,256]{3,2,1,0:T(8,128)S(1)}, f32[4,3,64,256]{3,2,1,0:T(8,128)}, u32[]{:S(2)}) copy-start(f32[4,3,64,256]{3,2,1,0:T(8,128)} %copy-done.3) | copy-start | bytes 2359300
  174.4 22.8 %all-to-all-start.6 = ((f32[4,3,64,256]{3,2,1,0:T(8,128)}), f32[4,3,64,256]{3,2,1,0:T(8,128)S(1)}, u32[]{:S(2)}, u32[]{:S(2)}) async-start(f32[4,3,64,256]{3,2,1,0:T(8,128)} %copy-done.9), calls=%async_computation.6 | async-start | bytes 1572864 | tf_op jit(solution)/shard_map/all_to_all | solution.py:278
  178.0 40.6 %copy-start.27 = (f32[1,4,256]{2,1,0:T(4,128)S(1)}, f32[1,4,256]{2,1,0:T(4,128)}, u32[]{:S(2)}) copy-start(f32[1,4,256]{2,1,0:T(4,128)} %param.13) | copy-start | bytes 12292
  178.0 9.5 %collective-permute-start.3 = (f32[256,256]{1,0:T(8,128)}, f32[256,256]{1,0:T(8,128)S(1)}, u32[]{:S(2)}, u32[]{:S(2)}) collective-permute-start(f32[256,256]{1,0:T(8,128)} %copy-done.34), channel_id=1, source_target_pairs={{0,2},{2,0},{4,6},{6,4},{8,10},{10,8},{12,14},{14,12},{16,18},{18,... | collective-permute-start | bytes 786440 | tf_op jit(solution)/shard_map/ppermute | solution.py:281
  179.4 39.2 %collective-permute-start.6 = (f32[2,256,256]{2,1,0:T(8,128)}, f32[2,256,256]{2,1,0:T(8,128)}, u32[]{:S(2)}, u32[]{:S(2)}) collective-permute-start(f32[2,256,256]{2,1,0:T(8,128)} %copy-done.31), channel_id=1, source_target_pairs={{0,2},{2,0},{4,6},{6,4},{8,10},{10,8},{12,14},{14,12},{16,18},{18,... | collective-permute-start | bytes 1572872 | tf_op jit(solution)/shard_map/ppermute | solution.py:281
  180.1 38.5 %collective-permute-start.7 = (f32[2,256,256]{2,1,0:T(8,128)}, f32[2,256,256]{2,1,0:T(8,128)}, u32[]{:S(2)}, u32[]{:S(2)}) collective-permute-start(f32[2,256,256]{2,1,0:T(8,128)} %copy-done.30), channel_id=1, source_target_pairs={{0,4},{2,6},{4,0},{6,2},{8,12},{10,14},{12,8},{14,10},{16,20},{18,... | collective-permute-start | bytes 1572872 | tf_op jit(solution)/shard_map/ppermute | solution.py:281
  180.7 37.9 %collective-permute-start.8 = (f32[2,256,256]{2,1,0:T(8,128)}, f32[2,256,256]{2,1,0:T(8,128)}, u32[]{:S(2)}, u32[]{:S(2)}) collective-permute-start(f32[2,256,256]{2,1,0:T(8,128)} %copy-done.29), channel_id=1, source_target_pairs={{0,6},{2,4},{4,2},{6,0},{8,14},{10,12},{12,10},{14,8},{16,22},{18,... | collective-permute-start | bytes 1572872 | tf_op jit(solution)/shard_map/ppermute | solution.py:281
  182.9 33.5 %collective-permute-start.4 = (f32[256,256]{1,0:T(8,128)}, f32[256,256]{1,0:T(8,128)}, u32[]{:S(2)}, u32[]{:S(2)}) collective-permute-start(f32[256,256]{1,0:T(8,128)} %copy-done.33), channel_id=1, source_target_pairs={{0,4},{2,6},{4,0},{6,2},{8,12},{10,14},{12,8},{14,10},{16,20},{18,... | collective-permute-start | bytes 786440 | tf_op jit(solution)/shard_map/ppermute | solution.py:281
  187.5 28.8 %collective-permute-start.5 = (f32[256,256]{1,0:T(8,128)}, f32[256,256]{1,0:T(8,128)}, u32[]{:S(2)}, u32[]{:S(2)}) collective-permute-start(f32[256,256]{1,0:T(8,128)} %copy-done.32), channel_id=1, source_target_pairs={{0,6},{2,4},{4,2},{6,0},{8,14},{10,12},{12,10},{14,8},{16,22},{18,... | collective-permute-start | bytes 786440 | tf_op jit(solution)/shard_map/ppermute | solution.py:281
  198.4 24.5 %all-to-all-start.7 = ((f32[4,3,16,256]{3,2,1,0:T(8,128)}), f32[4,3,16,256]{3,2,1,0:T(8,128)}, u32[]{:S(2)}, u32[]{:S(2)}) async-start(f32[4,3,16,256]{3,2,1,0:T(8,128)} %shard_map.155), calls=%async_computation.7 | async-start | bytes 393216 | tf_op jit(solution)/shard_map/all_to_all | solution.py:278
  218.6 1.0 copy-start.11

commit v3 on v1

v3 whole, which is shorter than its diff:
```python
import functools
import math

import jax
import jax.numpy as jnp
from jax import lax
from jax.experimental import pallas as pl
from jax.experimental.pallas import tpu as pltpu
from jax.sharding import PartitionSpec as P

F32 = jnp.float32
BF16 = jnp.bfloat16
LANES = 128
VMEM_LIMIT = 40 * 1024 * 1024


def mm(a, b):
    return jnp.dot(a, b, preferred_element_type=F32)


def mm_t(a, b):
    return lax.dot_general(a, b, (((1,), (1,)), ((), ())), preferred_element_type=F32)


def tmm(a, b):
    return lax.dot_general(a, b, (((0,), (0,)), ((), ())), preferred_element_type=F32)


def call(body, out_shape, scratch, flops, *args):
    smem = pl.BlockSpec(memory_space=pltpu.SMEM)
    vmem = pl.BlockSpec(memory_space=pltpu.VMEM)
    size = sum(a.size * a.dtype.itemsize for a in args)
    size += sum(math.prod(o.shape) * o.dtype.itemsize for o in out_shape)
    return pl.pallas_call(
        body,
        out_shape=out_shape,
        in_specs=[smem if a.dtype == jnp.int32 else vmem for a in args],
        out_specs=[vmem] * len(out_shape),
        scratch_shapes=scratch,
        compiler_params=pltpu.CompilerParams(vmem_limit_bytes=VMEM_LIMIT),
        cost_estimate=pl.CostEstimate(flops=flops, bytes_accessed=size, transcendentals=0),
    )(*args)


def put_rows(scratch, x):
    for i in range(scratch.shape[0]):
        scratch[i] = x[:, i * LANES : (i + 1) * LANES]


def take_head(scratch, head, tokens, heads):
    parts = [scratch[i, pl.ds(head, tokens, stride=heads), :] for i in range(scratch.shape[0])]
    return jnp.concatenate(parts, axis=1)


def put_head(scratch, head, x, tokens, heads):
    for i in range(scratch.shape[0]):
        scratch[i, pl.ds(head, tokens, stride=heads), :] = x[:, i * LANES : (i + 1) * LANES]


def rows_of(scratch):
    return jnp.concatenate([scratch[i] for i in range(scratch.shape[0])], axis=1)


def split_kernel(groups, place, x, *rest):
    outs, scratch = rest[:groups], rest[groups]
    tokens, heads, width = x.shape
    put_rows(scratch, x[...].astype(F32).reshape(tokens * heads, width))
    for step in range(groups):
        outs[step][...] = take_head(scratch, place[0] ^ step, tokens, heads)


def split_scaled_kernel(groups, place, x, r, *rest):
    outs = rest[:groups]
    split_kernel(groups, place, x, *rest)
    for step in range(groups):
        scaled = outs[step][...] * rate_column(r, place[0] ^ step)
        outs[step][...] = scaled.astype(BF16).astype(F32)


def split_apply_kernel(groups, place, q, cot, gain, *rest):
    outs, scratch = rest[:groups], rest[groups]
    split_kernel(groups, place, q, *[out.at[0] for out in outs], scratch)
    split_kernel(groups, place, cot, *[out.at[1] for out in outs], scratch)
    for step in range(groups):
        outs[step][1] *= gain[pl.ds(place[0] ^ step, 1), :]


def rate_column(r, head):
    return jnp.broadcast_to(r[pl.ds(head, 1), :], (8, r.shape[1])).T[:, 0:1]


def send_slices(sums, outs, layer):
    rows = sums.shape[1] // len(outs)
    for step, out in enumerate(outs):
        at = pl.multiple_of((layer ^ step) * rows, rows)
        out[...] = sums[:, pl.ds(at, rows), :]


def update_kernel(groups, depth, scale, place, *refs):
    keys_in, scaled_in = refs[:groups], refs[groups : 2 * groups]
    w_gate, w_out, w_up = refs[2 * groups : 2 * groups + 3]
    outs, sums = refs[2 * groups + 3 : -1], refs[-1]
    gate_b, out_b, up_b = (w[...].astype(BF16) for w in (w_gate, w_out, w_up))
    total = [0.0, 0.0, 0.0]
    for key, value in zip(keys_in, scaled_in):
        keys = key[...].astype(BF16)
        scaled = value[...].astype(BF16)
        first = mm(keys, gate_b)
        third = mm(keys, up_b)
        sig = jax.nn.sigmoid(first)
        activ = first * sig
        act = (activ * third).astype(BF16)
        dact = mm_t(scaled, out_b)
        deriv = sig * (1.0 + first * (1.0 - sig))
        dfirst = (dact * third * deriv).astype(BF16)
        dthird = (dact * activ).astype(BF16)
        total[0] += tmm(keys, dfirst)
        total[1] += tmm(act, scaled)
        total[2] += tmm(keys, dthird)
    for i in range(3):
        sums[i] = total[i] * scale
    send_slices(sums, outs, place[1])
    rows = sums.shape[1] // depth
    at = pl.multiple_of(place[1] * rows, rows)
    for i, w in enumerate((w_gate, w_out, w_up)):
        outs[0][i] += w[pl.ds(at, rows), :]


def assemble(place, parts, whole):
    rows = parts[0].shape[1]
    for step, part in enumerate(parts):
        at = pl.multiple_of((place[1] ^ step) * rows, rows)
        whole[:, pl.ds(at, rows), :] = part[...]


def apply_kernel(groups, depth, place, head_scale, *refs):
    pieces = refs[:groups]
    parts = refs[groups : groups + depth]
    first_ref, third_ref, os_ref, new_b, stats, whole = refs[groups + depth :]
    assemble(place, parts, whole)
    new_b[...] = whole[...].astype(BF16)
    for step in range(groups):
        queries = pieces[step][0].astype(BF16)
        tokens = queries.shape[0]
        first = mm(queries, new_b[0])
        third = mm(queries, new_b[2])
        hidden = (first * jax.nn.sigmoid(first) * third).astype(BF16)
        scaled = mm(hidden, new_b[1]) * head_scale[...]
        first_ref[step] = first
        third_ref[step] = third
        os_ref[step] = scaled
        sq = jnp.sum(scaled * scaled, axis=1, keepdims=True)
        ps = jnp.sum(scaled * pieces[step][1], axis=1, keepdims=True)
        lane = lax.broadcasted_iota(jnp.int32, (tokens, LANES), 1)
        both = jnp.where(lane == 0, sq, jnp.where(lane == 1, ps, 0.0)).T
        source = place[0] ^ step
        stats[0, pl.ds(source, 1), :] = both[0:1, :]
        stats[1, pl.ds(source, 1), :] = both[1:2, :]


def apply_back_kernel(groups, count, place, head_scale, *refs):
    pieces = refs[:groups]
    stats = refs[groups : 2 * groups]
    first_ref, third_ref, os_ref, new_b = refs[2 * groups : 2 * groups + 4]
    outs = refs[2 * groups + 4 : 3 * groups + 4]
    slices, sums, both = refs[3 * groups + 4 : -2], refs[-2], refs[-1]
    hs = head_scale[...]
    total_stats = stats[0][...]
    for other in stats[1:]:
        total_stats += other[...]
    both[...] = total_stats
    total = [0.0, 0.0, 0.0]
    for step in range(groups):
        queries = pieces[step][0].astype(BF16)
        source = place[0] ^ step
        sq = rate_column(both.at[0], source)
        ps = rate_column(both.at[1], source)
        inv = lax.rsqrt(sq / count + 1e-06)
        scaled = os_ref[step]
        dos = inv * pieces[step][1] - scaled * (inv * inv * inv * ps / count)
        dout = (dos * hs).astype(BF16)
        first = first_ref[step]
        third = third_ref[step]
        sig = jax.nn.sigmoid(first)
        activ = first * sig
        hidden = (activ * third).astype(BF16)
        dhidden = mm_t(dout, new_b[1])
        dthird = (dhidden * activ).astype(BF16)
        dfirst = (dhidden * third * (sig * (1.0 + first * (1.0 - sig)))).astype(BF16)
        outs[step][...] = mm_t(dfirst, new_b[0]) + mm_t(dthird, new_b[2])
        total[0] += tmm(queries, dfirst)
        total[1] += tmm(hidden, dout)
        total[2] += tmm(queries, dthird)
    for i in range(3):
        sums[i] = total[i]
    send_slices(sums, slices, place[1])


def halving_order(depth):
    sets, bit = [], 1
    while bit < depth:
        sets.append(list(range(bit, depth, 2 * bit)))
        bit *= 2
    return sets


def update_back_kernel(groups, depth, scale, place, *refs):
    keys_in, scaled_in = refs[:groups], refs[groups : 2 * groups]
    parts = refs[2 * groups : 2 * groups + depth]
    w_gate, w_out, w_up = refs[2 * groups + depth : 2 * groups + depth + 3]
    base = 2 * groups + depth + 3
    outs = refs[base : base + groups]
    slices = refs[base + groups : -2]
    whole, sums = refs[-2:]
    assemble(place, parts, whole)
    gate_b, out_b, up_b = (w[...].astype(BF16) for w in (w_gate, w_out, w_up))
    cot_gate, cot_out, cot_up = ((whole[i] * scale).astype(BF16) for i in range(3))
    total = [0.0, 0.0, 0.0]
    for step in range(groups):
        keys = keys_in[step][...].astype(BF16)
        scaled = scaled_in[step][...].astype(BF16)
        first = mm(keys, gate_b)
        third = mm(keys, up_b)
        sig = jax.nn.sigmoid(first)
        activ = first * sig
        act = (activ * third).astype(BF16)
        dact = mm_t(scaled, out_b)
        slope = sig * (1.0 - sig)
        deriv = sig + first * slope
        second = slope * (2.0 + first * (1.0 - 2.0 * sig))
        third_deriv = third * deriv
        dfirst = (dact * third_deriv).astype(BF16)
        dthird = (dact * activ).astype(BF16)
        bar_dfirst = mm(keys, cot_gate)
        bar_dthird = mm(keys, cot_up)
        bar_act = mm_t(scaled, cot_out)
        bar_activ = bar_dthird * dact + bar_act * third
        bar_dact = (bar_dfirst * third_deriv + bar_dthird * activ).astype(BF16)
        bar_df_dact = bar_dfirst * dact
        bar_third = (bar_df_dact * deriv + bar_act * activ).astype(BF16)
        bar_first = (bar_activ * deriv + bar_df_dact * third * second).astype(BF16)
        outs[step][0] = (
            mm_t(dfirst, cot_gate)
            + mm_t(dthird, cot_up)
            + mm_t(bar_first, gate_b)
            + mm_t(bar_third, up_b)
        )
        outs[step][1] = mm(act, cot_out) + mm(bar_dact, out_b)
        total[0] += tmm(keys, bar_first)
        total[1] += tmm(bar_dact, scaled)
        total[2] += tmm(keys, bar_third)
    for i in range(3):
        sums[i] = total[i]
    rows = sums.shape[1] // depth
    for out, members in zip(slices, halving_order(depth) + [[0]]):
        for i, step in enumerate(members):
            at = pl.multiple_of((place[1] ^ step) * rows, rows)
            out[i] = sums[:, pl.ds(at, rows), :]


def join_query_kernel(groups, place, *refs):
    pieces, out, scratch = refs[:groups], refs[groups], refs[groups + 1]
    tokens, heads, width = out.shape
    for step, piece in enumerate(pieces):
        put_head(scratch, place[0] ^ step, piece[...], tokens, heads)
    out[...] = rows_of(scratch).reshape(tokens, heads, width).astype(BF16)


def join_update_kernel(groups, place, r, *refs):
    pieces, (out_k, out_v, sk, sv) = refs[:groups], refs[groups:]
    tokens, heads, width = out_k.shape
    for step, piece in enumerate(pieces):
        head = place[0] ^ step
        put_head(sk, head, piece[0], tokens, heads)
        put_head(sv, head, piece[1] * rate_column(r, head), tokens, heads)
    out_k[...] = rows_of(sk).reshape(tokens, heads, width).astype(BF16)
    out_v[...] = rows_of(sv).reshape(tokens, heads, width).astype(BF16)


def rows_kernel(groups, place, *refs):
    parts, outs, total = refs[: -groups - 1], refs[-groups - 1 : -1], refs[-1]
    summed = parts[0][...]
    for part in parts[1:]:
        summed += part[0]
    total[...] = summed
    send_slices(total, outs, place[0])


def join_rows_kernel(groups, place, *refs):
    parts, outs = refs[:groups], refs[groups:]
    for step, part in enumerate(parts):
        for i, out in enumerate(outs):
            out[place[0] ^ step] = part[i]


def local(queries, keys, values, rates, head_scale, gain, w_gate, w_out, w_up, cotangent):
    tokens, heads, width = keys.shape[1:]
    hidden = w_gate.shape[2]
    ctx = lax.axis_size("ctx")
    head_axis = lax.axis_size("head")
    groups = heads
    depth = ctx // groups
    assert groups & (groups - 1) == 0 and depth & (depth - 1) == 0
    scale = 1.0 / math.sqrt(tokens * ctx * width)
    count = float(heads * head_axis * width)
    me = lax.axis_index("ctx")
    mine, layer = lax.rem(me, groups), lax.div(me, groups)
    place = jnp.stack([mine, layer]).astype(jnp.int32)

    def move(x, axis, step):
        return lax.ppermute(x, axis, [(c, c ^ step) for c in range(lax.axis_size(axis))])

    def in_plane(parts):
        return [parts[0]] + [move(p, "ctx", step) for step, p in enumerate(parts) if step]

    def in_column(parts):
        return [parts[0]] + [move(p, "ctx", i * groups) for i, p in enumerate(parts) if i]

    def after(x, *others):
        return lax.optimization_barrier((x, *others))

    def shape(*dims, dtype=F32):
        return jax.ShapeDtypeStruct(dims, dtype)

    flops = 2 * groups * tokens * width * hidden
    pieces = [shape(tokens, width)] * groups
    slices = [shape(3, hidden // depth, width)] * depth
    joined = shape(tokens, heads, width, dtype=BF16)
    scratch = pltpu.VMEM((width // LANES, tokens * heads, LANES), F32)
    square = pltpu.VMEM((3, hidden, width), F32)

    def split(body, *args):
        return call(functools.partial(body, groups), pieces, [scratch], flops // 16, place, *args)

    k_in = in_plane(split(split_kernel, keys[0]))
    s_in = in_plane(split(split_scaled_kernel, values[0], rates[0]))
    own = [lax.dynamic_index_in_dim(w, mine, 0, keepdims=False) for w in (w_gate, w_out, w_up)]
    own_scale = lax.dynamic_index_in_dim(head_scale, mine, 0, keepdims=True)[None, :]
    q_out = call(
        functools.partial(split_apply_kernel, groups), [shape(2, tokens, width)] * groups,
        [scratch], flops // 8, place, queries[0], cotangent[0], gain,
    )
    k_in, s_in, q_out = after(k_in, s_in, q_out)
    terms = call(
        functools.partial(update_kernel, groups, depth, scale), slices, [square], 6 * flops,
        place, *k_in, *s_in, *own,
    )
    q_in = in_plane(q_out)
    new = functools.reduce(jnp.add, in_column(terms))
    new, q_in[:-1] = after(new, q_in[:-1])
    new = in_column([new] * depth)
    kept = shape(groups, tokens, width)
    first, third, scaled, new_b, stats = call(
        functools.partial(apply_kernel, groups, depth),
        [kept, kept, kept, shape(3, hidden, width, dtype=BF16), shape(2, groups, tokens)],
        [square], 3 * flops, place, own_scale, *q_in, *new,
    )
    bit = 1
    while bit < head_axis:
        stats = stats + move(stats, "head", bit)
        bit *= 2
    out = call(
        functools.partial(apply_back_kernel, groups, count), pieces + slices,
        [square, pltpu.VMEM((2, groups, tokens), F32)], 6 * flops,
        place, own_scale, *q_in, *in_plane([stats] * groups),
        first, third, scaled, new_b,
    )
    part = functools.reduce(jnp.add, in_column(out[groups:]))
    part, q_back = after(part, in_plane(out[:groups]))
    parts = in_column([part] * depth)
    (grad_q,) = call(
        functools.partial(join_query_kernel, groups), [joined], [scratch], flops // 16,
        place, *q_back,
    )
    rows = hidden // depth
    sets = halving_order(depth)
    out = call(
        functools.partial(update_back_kernel, groups, depth, scale),
        [shape(2, tokens, width)] * groups
        + [shape(len(members), 3, rows, width) for members in sets + [[0]]],
        [square] * 2, 15 * flops, place, *k_in, *s_in, *parts, *own,
    )
    back = in_plane(out[:groups])
    ends, rest = list(out[groups:-1]), [part, out[-1]]
    for i in range(len(ends)):
        got = move(ends[i], "ctx", groups << i)
        for j in range(i + 1, len(ends)):
            ends[j] = ends[j] + got[1 << (j - i - 1) :: 1 << (j - i)]
        rest.append(got[:1])
    own_rows = rows // groups
    sent = call(
        functools.partial(rows_kernel, groups), [shape(3, own_rows, width)] * groups,
        [pltpu.VMEM((3, rows, width), F32)], flops // 100, place, *rest,
    )
    grads = call(
        functools.partial(join_rows_kernel, groups), [shape(heads, own_rows, width)] * 3, [],
        flops // 100, place, *in_plane(sent),
    )
    grad_k, grad_v = call(
        functools.partial(join_update_kernel, groups), [joined] * 2, [scratch] * 2, flops // 8,
        place, rates[0], *back,
    )
    if lax.axis_size("batch") > 1:
        grads = [lax.psum_scatter(x, "batch", scatter_dimension=1, tiled=True) for x in grads]
    return (grad_q[None], grad_k[None], grad_v[None], grads[0], grads[1], grads[2])


def solution(mesh):
    in_specs = (
        P("batch", "ctx", "head", None),
        P("batch", "ctx", "head", None),
        P("batch", "ctx", "head", None),
        P("batch", "head", "ctx"),
        P("head"),
        P("head", None),
        P("head", None, None),
        P("head", None, None),
        P("head", None, None),
        P("batch", "ctx", "head", None),
    )
    out_specs = (
        P("batch", "ctx", "head", None),
        P("batch", "ctx", "head", None),
        P("batch", "ctx", "head", None),
        P("head", ("ctx", "batch"), None),
        P("head", ("ctx", "batch"), None),
        P("head", ("ctx", "batch"), None),
    )
    return jax.shard_map(local, mesh=mesh, in_specs=in_specs, out_specs=out_specs, check_vma=False)
```

time: 210 us -> 159 us (0.76)
  blocking collectives: 23.7 us -> 0 us
  waiting for transfers between devices: 101 us -> 80 us
  local copies, waits for them, and re-layouts: 12.7 us -> 4.54 us
    psum x1 -> x0, blocking collectives: 23.7 us -> none  [local(): stats = lax.psum(stats, ('ctx', 'head'), axis_index_groups=sets)]
    ppermute x30 -> x36, waiting for transfers between devices: 101 us -> 80 us  [move(): lax.ppermute(x, axis, [(c, c ^ step) for c in range(lax.axis_size(axis))])]
    unnamed x60 -> x16, local copies, waits for them, and re-layouts: 10.9 us -> 2.86 us
    pallas_call x10 -> x11, Pallas kernels: 21.1 us -> 23 us  [call(): pl.pallas_call(body, out_shape=out_shape, in_specs=[smem if a.dtype == jn...]
    ppermute x30 -> x36, starting transfers between devices: 49.7 us -> 49.8 us  [move(): lax.ppermute(x, axis, [(c, c ^ step) for c in range(lax.axis_size(axis))])]
  transfers between devices with their start and end apart: 30 -> 36, of which waited for: 17 -> 20; matrix products, arithmetic and copies ran while one was open for 1% -> 1% of each run, Pallas kernels for 4% -> 7%
where the time goes in v3:
time: 159 us; the launch traced here: 158 us
  waiting for transfers between devices  80 us (50%)
  starting transfers between devices  49.8 us (31%)
  Pallas kernels  23 us (14%)
  local copies, waits for them, and re-layouts  4.54 us (3%)
    ppermute x36, waiting for transfers between devices, move(): lax.ppermute(x, axis, [(c, c ^ step) for c in range(lax.axis_size(axis))])  80 us
    ppermute x36, starting transfers between devices, move(): lax.ppermute(x, axis, [(c, c ^ step) for c in range(lax.axis_size(axis))])  49.8 us
    pallas_call x11, Pallas kernels, call(): pl.pallas_call(body, out_shape=out_shape, in_specs=[smem if a.dtype == jn...  23 us
  transfers between devices with their start and end apart: 36, of which 20 were waited for; matrix products, arithmetic and copies ran while one was open for 1% of the time, Pallas kernels for 7%

profile of v3, /device:TPU:0, one launch (start us, length us, event | category | flops | bytes accessed | tf_op | source)
XLA Modules:
  0.0 158.4 jit_solution(10716867244277413478)
XLA Ops:
  0.7 1.1 copy-done.1
  1.9 1.7 %shard_map.145 = (f32[256,256]{1,0:T(8,128)S(1)}, f32[256,256]{1,0:T(8,128)S(1)}, f32[256,256]{1,0:T(8,128)}, f32[256,256]{1,0:T(8,128)}) custom-call(s32[2]{0:T(128)S(1)} %pad_add_fusion.place, bf16[256,4,256]{2,1,0:T(4,128)(2,1)S(1)} %bitcast.17), custom_call_target="tpu_custom_call" | custom-call | flops 8388608 | bytes 1572872 | tf_op jit(solution)/shard_map/pallas_call | solution.py:34
  3.5 2.9 %collective-permute-start = (f32[256,256]{1,0:T(8,128)S(1)}, f32[256,256]{1,0:T(8,128)S(1)}, u32[]{:S(2)}, u32[]{:S(2)}) collective-permute-start(f32[256,256]{1,0:T(8,128)S(1)} %get-tuple-element.73), channel_id=1, source_target_pairs={{0,2},{2,0},{4,6},{6,4},{8,10},{10,8},{12,14},{14,12},{16,18},{18,... | collective-permute-start | bytes 786440 | tf_op jit(solution)/shard_map/ppermute | solution.py:311
  6.5 1.5 collective-permute-start.1
  8.0 1.9 %shard_map.146 = (f32[256,256]{1,0:T(8,128)S(1)}, f32[256,256]{1,0:T(8,128)}, f32[256,256]{1,0:T(8,128)}, f32[256,256]{1,0:T(8,128)}) custom-call(s32[2]{0:T(128)S(1)} %pad_add_fusion.place, bf16[256,4,256]{2,1,0:T(4,128)(2,1)S(1)} %bitcast.18, f32[4,256]{1,0:T(4,128)S(1)} %bitcast.21), custom_call_target="tpu_custom_call" | custom-call | flops 8388608 | bytes 1576968 | tf_op jit(solution)/shard_map/pallas_call | solution.py:34
  9.9 2.0 %collective-permute-start.3 = (f32[256,256]{1,0:T(8,128)}, f32[256,256]{1,0:T(8,128)S(1)}, u32[]{:S(2)}, u32[]{:S(2)}) collective-permute-start(f32[256,256]{1,0:T(8,128)} %get-tuple-element.77), channel_id=1, source_target_pairs={{0,2},{2,0},{4,6},{6,4},{8,10},{10,8},{12,14},{14,12},{16,18},{18,... | collective-permute-start | bytes 786440 | tf_op jit(solution)/shard_map/ppermute | solution.py:311
  11.9 1.5 collective-permute-start.4
  13.6 3.0 %collective-permute-start.5 = (f32[256,256]{1,0:T(8,128)}, f32[256,256]{1,0:T(8,128)}, u32[]{:S(2)}, u32[]{:S(2)}) collective-permute-start(f32[256,256]{1,0:T(8,128)} %get-tuple-element.79), channel_id=1, source_target_pairs={{0,6},{2,4},{4,2},{6,0},{8,14},{10,12},{12,10},{14,8},{16,22},{18,... | collective-permute-start | bytes 786440 | tf_op jit(solution)/shard_map/ppermute | solution.py:311
  16.6 0.7 copy-done.6
  17.3 1.0 copy-done.4
  18.4 1.3 shard_map.147
  19.7 1.1 dynamic-slice_bitcast_fusion
  20.8 0.6 collective-permute-done.1.refs_2_
  21.3 3.5 %collective-permute-done.3.refs_5_ = f32[256,256]{1,0:T(8,128)S(1)} collective-permute-done((f32[256,256]{1,0:T(8,128)}, f32[256,256]{1,0:T(8,128)S(1)}, u32[]{:S(2)}, u32[]{:S(2)}) %collective-permute-start.3) | collective-permute-done | bytes 262176 | tf_op jit(solution)/shard_map/ppermute | solution.py:311
  24.9 6.4 %collective-permute-done.4.refs_6_ = f32[256,256]{1,0:T(8,128)S(1)} collective-permute-done((f32[256,256]{1,0:T(8,128)}, f32[256,256]{1,0:T(8,128)S(1)}, u32[]{:S(2)}, u32[]{:S(2)}) %collective-permute-start.4) | collective-permute-done | bytes 262176 | tf_op jit(solution)/shard_map/ppermute | solution.py:311
  31.3 1.2 collective-permute-start.9
  32.5 0.9 collective-permute-start.10
  33.4 2.6 %shard_map.148 = (f32[3,64,256]{2,1,0:T(8,128)S(1)}, f32[3,64,256]{2,1,0:T(8,128)S(1)}, f32[3,64,256]{2,1,0:T(8,128)S(1)}, f32[3,64,256]{2,1,0:T(8,128)S(1)}) custom-call(s32[2]{0:T(128)S(1)} %pad_add_fusion.place, f32[256,256]{1,0:T(8,128)S(1)} %get-tuple-element.84.refs_0_, f32[256,256]{1,0:T(8,128)S(1)} %collective-permute-done.refs_1_, ...), custom_call_target="tpu_custom_call" | custom-call | flops 805306368 | bytes 3670024 | tf_op jit(solution)/shard_map/pallas_call | solution.py:34
  35.9 1.6 %collective-permute-start.6 = (f32[3,64,256]{2,1,0:T(8,128)S(1)}, f32[3,64,256]{2,1,0:T(8,128)S(1)}, u32[]{:S(2)}, u32[]{:S(2)}) collective-permute-start(f32[3,64,256]{2,1,0:T(8,128)S(1)} %get-tuple-element.93), channel_id=1, source_target_pairs={{0,8},{2,10},{4,12},{6,14},{8,0},{10,2},{12,4},{14,6},{16,24},{18,... | collective-permute-start | bytes 589832 | tf_op jit(solution)/shard_map/ppermute | solution.py:311
  37.6 2.6 %collective-permute-start.7 = (f32[3,64,256]{2,1,0:T(8,128)S(1)}, f32[3,64,256]{2,1,0:T(8,128)S(1)}, u32[]{:S(2)}, u32[]{:S(2)}) collective-permute-start(f32[3,64,256]{2,1,0:T(8,128)S(1)} %get-tuple-element.94), channel_id=1, source_target_pairs={{0,16},{2,18},{4,20},{6,22},{8,24},{10,26},{12,28},{14,30},{16,0},... | collective-permute-start | bytes 589832 | tf_op jit(solution)/shard_map/ppermute | solution.py:311
  40.4 3.0 %collective-permute-done.6 = f32[3,64,256]{2,1,0:T(8,128)S(1)} collective-permute-done((f32[3,64,256]{2,1,0:T(8,128)S(1)}, f32[3,64,256]{2,1,0:T(8,128)S(1)}, u32[]{:S(2)}, u32[]{:S(2)}) %collective-permute-start.6) | collective-permute-done | bytes 196640 | tf_op jit(solution)/shard_map/ppermute | solution.py:311
  43.4 1.5 collective-permute-start.11
  44.9 10.8 %collective-permute-done.7 = f32[3,64,256]{2,1,0:T(8,128)S(1)} collective-permute-done((f32[3,64,256]{2,1,0:T(8,128)S(1)}, f32[3,64,256]{2,1,0:T(8,128)S(1)}, u32[]{:S(2)}, u32[]{:S(2)}) %collective-permute-start.7) | collective-permute-done | bytes 196640 | tf_op jit(solution)/shard_map/ppermute | solution.py:311
  55.8 0.4 collective-permute-done.10.refs_2_
  56.2 3.6 %collective-permute-start.14 = (f32[3,64,256]{2,1,0:T(8,128)S(1)}, f32[3,64,256]{2,1,0:T(8,128)S(1)}, u32[]{:S(2)}, u32[]{:S(2)}) collective-permute-start(f32[3,64,256]{2,1,0:T(8,128)S(1)} %add_add_fusion.1.refs_4_), channel_id=1, source_target_pairs={{0,24},{2,26},{4,28},{6,30},{8,16},{10,18},{12,20},{14,22},{16,8},... | collective-permute-start | bytes 589832 | tf_op jit(solution)/shard_map/ppermute | solution.py:311
  60.0 0.6 collective-permute-start.12
  60.6 0.6 dynamic_slice.14
  61.2 4.6 %collective-permute-done.14.refs_7_ = f32[3,64,256]{2,1,0:T(8,128)S(1)} collective-permute-done((f32[3,64,256]{2,1,0:T(8,128)S(1)}, f32[3,64,256]{2,1,0:T(8,128)S(1)}, u32[]{:S(2)}, u32[]{:S(2)}) %collective-permute-start.14) | collective-permute-done | bytes 196640 | tf_op jit(solution)/shard_map/ppermute | solution.py:311
  65.8 7.7 %collective-permute-done.13.refs_6_ = f32[3,64,256]{2,1,0:T(8,128)S(1)} collective-permute-done((f32[3,64,256]{2,1,0:T(8,128)S(1)}, f32[3,64,256]{2,1,0:T(8,128)S(1)}, u32[]{:S(2)}, u32[]{:S(2)}) %collective-permute-start.13) | collective-permute-done | bytes 196640 | tf_op jit(solution)/shard_map/ppermute | solution.py:311
  73.5 2.3 %shard_map.149 = (f32[4,256,256]{2,1,0:T(8,128)S(1)}, f32[4,256,256]{2,1,0:T(8,128)S(1)}, f32[4,256,256]{2,1,0:T(8,128)S(1)}, bf16[3,256,256]{2,1,0:T(8,128)(2,1)S(1)}, f32[2,4,256]{2,1,0:T(4,128)S(1)}) custom-call(s32[2]{0:T(128)S(1)} %pad_add_fusion.place, f32[1,1]{1,0:T(1,128)} %bitcast.2.head_scale, f32[2,256,256]{2,1,0:T(8,128)S(1)} %get-tuple-element.99.refs_0_, ...), custom_call_target="tpu_custom_call" | custom-call | flops 402653184 | bytes 6430732 | tf_op jit(solution)/shard_map/pallas_call | solution.py:34
  75.9 1.2 collective-permute-done.15
  77.0 1.5 collective-permute-start.18
  78.5 0.6 collective-permute-start.17
  79.1 1.4 collective-permute-start.16
  80.5 1.1 collective-permute-done.18.refs_7_
  81.6 0.6 collective-permute-done.17.refs_6_
  82.2 0.6 collective-permute-done.16.refs_5_
  82.7 3.1 %shard_map.150 = (f32[256,256]{1,0:T(8,128)S(1)}, f32[256,256]{1,0:T(8,128)S(1)}, f32[256,256]{1,0:T(8,128)S(1)}, f32[256,256]{1,0:T(8,128)S(1)}, f32[3,64,256]{...) custom-call(s32[2]{0:T(128)S(1)} %pad_add_fusion.place, ...), custom_call_target="tpu_custom_call" | custom-call | flops 805306368 | bytes 7503884 | tf_op jit(solution)/shard_map/pallas_call | solution.py:34
  85.9 3.2 %collective-permute-start.20 = (f32[3,64,256]{2,1,0:T(8,128)S(1)}, f32[3,64,256]{2,1,0:T(8,128)S(1)}, u32[]{:S(2)}, u32[]{:S(2)}) collective-permute-start(f32[3,64,256]{2,1,0:T(8,128)S(1)} %get-tuple-element.111), channel_id=1, source_target_pairs={{0,16},{2,18},{4,20},{6,22},{8,24},{10,26},{12,28},{14,30},{16,0},... | collective-permute-start | bytes 589832 | tf_op jit(solution)/shard_map/ppermute | solution.py:311
  89.1 1.2 collective-permute-start.21
  90.3 1.4 collective-permute-start.22
  91.7 1.5 collective-permute-start.23
  93.2 1.3 collective-permute-done.19
  94.5 2.2 %collective-permute-start.24 = (f32[256,256]{1,0:T(8,128)S(1)}, f32[256,256]{1,0:T(8,128)S(1)}, u32[]{:S(2)}, u32[]{:S(2)}) collective-permute-start(f32[256,256]{1,0:T(8,128)S(1)} %get-tuple-element.116), channel_id=1, source_target_pairs={{0,6},{2,4},{4,2},{6,0},{8,14},{10,12},{12,10},{14,8},{16,22},{18,... | collective-permute-start | bytes 786440 | tf_op jit(solution)/shard_map/ppermute | solution.py:311
  96.7 6.5 %collective-permute-done.20 = f32[3,64,256]{2,1,0:T(8,128)S(1)} collective-permute-done((f32[3,64,256]{2,1,0:T(8,128)S(1)}, f32[3,64,256]{2,1,0:T(8,128)S(1)}, u32[]{:S(2)}, u32[]{:S(2)}) %collective-permute-start.20) | collective-permute-done | bytes 196640 | tf_op jit(solution)/shard_map/ppermute | solution.py:311
  103.3 0.4 collective-permute-done.23.refs_2_
  103.7 2.6 %collective-permute-start.27 = (f32[3,64,256]{2,1,0:T(8,128)S(1)}, f32[3,64,256]{2,1,0:T(8,128)S(1)}, u32[]{:S(2)}, u32[]{:S(2)}) collective-permute-start(f32[3,64,256]{2,1,0:T(8,128)S(1)} %add_add_fusion.refs_8_.refs_0_), channel_id=1, source_target_pairs={{0,24},{2,26},{4,28},{6,30},{8,16},{10,18},{12,20},{14,22},{16,8},... | collective-permute-start | bytes 589832 | tf_op jit(solution)/shard_map/ppermute | solution.py:311
  106.4 1.1 collective-permute-start.26
  107.5 0.6 collective-permute-start.25
  108.1 5.1 %collective-permute-done.27.refs_11_ = f32[3,64,256]{2,1,0:T(8,128)S(1)} collective-permute-done((f32[3,64,256]{2,1,0:T(8,128)S(1)}, f32[3,64,256]{2,1,0:T(8,128)S(1)}, u32[]{:S(2)}, u32[]{:S(2)}) %collective-permute-start.27) | collective-permute-done | bytes 196640 | tf_op jit(solution)/shard_map/ppermute | solution.py:311
  113.2 9.9 %collective-permute-done.26.refs_10_ = f32[3,64,256]{2,1,0:T(8,128)S(1)} collective-permute-done((f32[3,64,256]{2,1,0:T(8,128)S(1)}, f32[3,64,256]{2,1,0:T(8,128)S(1)}, u32[]{:S(2)}, u32[]{:S(2)}) %collective-permute-start.26) | collective-permute-done | bytes 196640 | tf_op jit(solution)/shard_map/ppermute | solution.py:311
  123.1 4.1 %shard_map.152 = (f32[2,256,256]{2,1,0:T(8,128)S(1)}, f32[2,256,256]{2,1,0:T(8,128)S(1)}, f32[2,256,256]{2,1,0:T(8,128)S(1)}, f32[2,256,256]{2,1,0:T(8,128)S(1)}...) custom-call(s32[2]{0:T(128)S(1)} %pad_add_fusion.place, ...), custom_call_target="tpu_custom_call" | custom-call | flops 2013265920 | bytes 6553608 | tf_op jit(solution)/shard_map/pallas_call | solution.py:34
  127.3 1.2 collective-permute-start.28
  128.5 0.8 collective-permute-start.29
  129.3 1.6 %collective-permute-start.30 = (f32[2,256,256]{2,1,0:T(8,128)S(1)}, f32[2,256,256]{2,1,0:T(8,128)S(1)}, u32[]{:S(2)}, u32[]{:S(2)}) collective-permute-start(f32[2,256,256]{2,1,0:T(8,128)S(1)} %get-tuple-element.125), channel_id=1, source_target_pairs={{0,6},{2,4},{4,2},{6,0},{8,14},{10,12},{12,10},{14,8},{16,22},{18,... | collective-permute-start | bytes 1572872 | tf_op jit(solution)/shard_map/ppermute | solution.py:311
  130.9 7.1 %collective-permute-done.31 = f32[2,3,64,256]{3,2,1,0:T(8,128)S(1)} collective-permute-done((f32[2,3,64,256]{3,2,1,0:T(8,128)S(1)}, f32[2,3,64,256]{3,2,1,0:T(8,128)S(1)}, u32[]{:S(2)}, u32[]{:S(2)}) %collective-permute-start.31) | collective-permute-done | bytes 393248 | tf_op jit(solution)/shard_map/ppermute | solution.py:311
  138.1 1.8 %collective-permute-start.32 = (f32[1,3,64,256]{3,2,1,0:T(8,128)S(1)}, f32[1,3,64,256]{3,2,1,0:T(8,128)S(1)}, u32[]{:S(2)}, u32[]{:S(2)}) collective-permute-start(f32[1,3,64,256]{3,2,1,0:T(8,128)S(1)} %get-tuple-element.138), channel_id=1, source_target_pairs={{0,16},{2,18},{4,20},{6,22},{8,24},{10,26},{12,28},{14,30},{16,0},... | collective-permute-start | bytes 589832 | tf_op jit(solution)/shard_map/ppermute | solution.py:311
  139.8 9.0 %collective-permute-done.32.refs_3_ = f32[1,3,64,256]{3,2,1,0:T(8,128)S(1)} collective-permute-done((f32[1,3,64,256]{3,2,1,0:T(8,128)S(1)}, f32[1,3,64,256]{3,2,1,0:T(8,128)S(1)}, u32[]{:S(2)}, u32[]{:S(2)}) %collective-permute-start.32) | collective-permute-done | bytes 196640 | tf_op jit(solution)/shard_map/ppermute | solution.py:311
  148.8 0.6 shard_map.154
  149.4 1.4 collective-permute-start.33
  150.9 2.1 %collective-permute-start.35 = (f32[3,16,256]{2,1,0:T(8,128)S(1)}, f32[3,16,256]{2,1,0:T(8,128)S(1)}, u32[]{:S(2)}, u32[]{:S(2)}) collective-permute-start(f32[3,16,256]{2,1,0:T(8,128)S(1)} %get-tuple-element.134), channel_id=1, source_target_pairs={{0,6},{2,4},{4,2},{6,0},{8,14},{10,12},{12,10},{14,8},{16,22},{18,... | collective-permute-start | bytes 147464 | tf_op jit(solution)/shard_map/ppermute | solution.py:311
  153.0 1.7 %shard_map.151 = bf16[256,4,256]{2,1,0:T(4,128)(2,1)} custom-call(s32[2]{0:T(128)S(1)} %pad_add_fusion.place, f32[256,256]{1,0:T(8,128)S(1)} %get-tuple-element.117.refs_0_, f32[256,256]{1,0:T(8,128)S(1)} %collective-permute-done.22.refs_1_, f32[256,256]{1,0:T(8,128)S(1)} %collective-permute-done.23.refs_2_, f32[256,256]{1,0:T(8,128)S(1)} %collective-permute-done.24.refs_3_), custom_call_target="tpu_custom_call" | custom-call | flops 8388608 | bytes 1572872 | tf_op jit(solution)/shard_map/pallas_call | solution.py:34
  154.7 2.4 %shard_map.153 = (bf16[256,4,256]{2,1,0:T(4,128)(2,1)}, bf16[256,4,256]{2,1,0:T(4,128)(2,1)}) custom-call(s32[2]{0:T(128)S(1)} %pad_add_fusion.place, f32[4,256]{1,0:T(4,128)S(1)} %bitcast.22, f32[2,256,256]{2,1,0:T(8,128)S(1)} %get-tuple-element.122.refs_0_, f32[2,256,256]{2,1,0:T(8,128)S(1)} %collective-permute-done.28.refs_1_, ...), custom_call_target="tpu_custom_call" | custom-call | flops 16777216 | bytes 3149832 | tf_op jit(solution)/shard_map/pallas_call | solution.py:34
  157.2 1.2 shard_map.155
  (43 shorter events, 1.1 us)
Async XLA Ops:
  0.6 19.0 %copy-start = (f32[4,256,256]{2,1,0:T(8,128)S(1)}, f32[4,256,256]{2,1,0:T(8,128)}, u32[]{:S(2)}) copy-start(f32[4,256,256]{2,1,0:T(8,128)} %param.16) | copy-start | bytes 3145732
  0.7 7.3 %copy-start.5 = (f32[1,4,256]{2,1,0:T(4,128)S(1)}, f32[1,4,256]{2,1,0:T(4,128)}, u32[]{:S(2)}) copy-start(f32[1,4,256]{2,1,0:T(4,128)} %param.13) | copy-start | bytes 12292
  0.7 1.1 copy-start.1
  1.9 6.2 %copy-start.2 = (bf16[1,256,4,256]{3,2,1,0:T(4,128)(2,1)S(1)}, bf16[1,256,4,256]{3,2,1,0:T(4,128)(2,1)}, u32[]{:S(2)}) copy-start(bf16[1,256,4,256]{3,2,1,0:T(4,128)(2,1)} %param.12) | copy-start | bytes 1572868
  1.9 14.8 %copy-start.3 = (bf16[1,256,4,256]{3,2,1,0:T(4,128)(2,1)S(1)}, bf16[1,256,4,256]{3,2,1,0:T(4,128)(2,1)}, u32[]{:S(2)}) copy-start(bf16[1,256,4,256]{3,2,1,0:T(4,128)(2,1)} %param.10) | copy-start | bytes 1572868
  3.5 10.1 %collective-permute-start = (f32[256,256]{1,0:T(8,128)S(1)}, f32[256,256]{1,0:T(8,128)S(1)}, u32[]{:S(2)}, u32[]{:S(2)}) collective-permute-start(f32[256,256]{1,0:T(8,128)S(1)} %get-tuple-element.73), channel_id=1, source_target_pairs={{0,2},{2,0},{4,6},{6,4},{8,10},{10,8},{12,14},{14,12},{16,18},{18,... | collective-permute-start | bytes 786440 | tf_op jit(solution)/shard_map/ppermute | solution.py:311
  6.5 14.9 %collective-permute-start.1 = (f32[256,256]{1,0:T(8,128)}, f32[256,256]{1,0:T(8,128)S(1)}, u32[]{:S(2)}, u32[]{:S(2)}) collective-permute-start(f32[256,256]{1,0:T(8,128)} %get-tuple-element.74), channel_id=1, source_target_pairs={{0,4},{2,6},{4,0},{6,2},{8,12},{10,14},{12,8},{14,10},{16,20},{18,... | collective-permute-start | bytes 786440 | tf_op jit(solution)/shard_map/ppermute | solution.py:311
  8.0 13.3 %collective-permute-start.2 = (f32[256,256]{1,0:T(8,128)}, f32[256,256]{1,0:T(8,128)S(1)}, u32[]{:S(2)}, u32[]{:S(2)}) collective-permute-start(f32[256,256]{1,0:T(8,128)} %get-tuple-element.75), channel_id=1, source_target_pairs={{0,6},{2,4},{4,2},{6,0},{8,14},{10,12},{12,10},{14,8},{16,22},{18,... | collective-permute-start | bytes 786440 | tf_op jit(solution)/shard_map/ppermute | solution.py:311
  9.9 15.0 %collective-permute-start.3 = (f32[256,256]{1,0:T(8,128)}, f32[256,256]{1,0:T(8,128)S(1)}, u32[]{:S(2)}, u32[]{:S(2)}) collective-permute-start(f32[256,256]{1,0:T(8,128)} %get-tuple-element.77), channel_id=1, source_target_pairs={{0,2},{2,0},{4,6},{6,4},{8,10},{10,8},{12,14},{14,12},{16,18},{18,... | collective-permute-start | bytes 786440 | tf_op jit(solution)/shard_map/ppermute | solution.py:311
  11.9 19.4 %collective-permute-start.4 = (f32[256,256]{1,0:T(8,128)}, f32[256,256]{1,0:T(8,128)S(1)}, u32[]{:S(2)}, u32[]{:S(2)}) collective-permute-start(f32[256,256]{1,0:T(8,128)} %get-tuple-element.78), channel_id=1, source_target_pairs={{0,4},{2,6},{4,0},{6,2},{8,12},{10,14},{12,8},{14,10},{16,20},{18,... | collective-permute-start | bytes 786440 | tf_op jit(solution)/shard_map/ppermute | solution.py:311
  13.6 17.7 %collective-permute-start.5 = (f32[256,256]{1,0:T(8,128)}, f32[256,256]{1,0:T(8,128)}, u32[]{:S(2)}, u32[]{:S(2)}) collective-permute-start(f32[256,256]{1,0:T(8,128)} %get-tuple-element.79), channel_id=1, source_target_pairs={{0,6},{2,4},{4,2},{6,0},{8,14},{10,12},{12,10},{14,8},{16,22},{18,... | collective-permute-start | bytes 786440 | tf_op jit(solution)/shard_map/ppermute | solution.py:311
  16.6 0.7 copy-start.6
  17.3 1.0 copy-start.4
  31.3 24.5 %collective-permute-start.9 = (f32[2,256,256]{2,1,0:T(8,128)S(1)}, f32[2,256,256]{2,1,0:T(8,128)S(1)}, u32[]{:S(2)}, u32[]{:S(2)}) collective-permute-start(f32[2,256,256]{2,1,0:T(8,128)S(1)} %get-tuple-element.97), channel_id=1, source_target_pairs={{0,2},{2,0},{4,6},{6,4},{8,10},{10,8},{12,14},{14,12},{16,18},{18,... | collective-permute-start | bytes 1572872 | tf_op jit(solution)/shard_map/ppermute | solution.py:311
  32.5 23.7 %collective-permute-start.10 = (f32[2,256,256]{2,1,0:T(8,128)S(1)}, f32[2,256,256]{2,1,0:T(8,128)S(1)}, u32[]{:S(2)}, u32[]{:S(2)}) collective-permute-start(f32[2,256,256]{2,1,0:T(8,128)S(1)} %get-tuple-element.98), channel_id=1, source_target_pairs={{0,4},{2,6},{4,0},{6,2},{8,12},{10,14},{12,8},{14,10},{16,20},{18,... | collective-permute-start | bytes 1572872 | tf_op jit(solution)/shard_map/ppermute | solution.py:311
  35.9 7.4 %collective-permute-start.6 = (f32[3,64,256]{2,1,0:T(8,128)S(1)}, f32[3,64,256]{2,1,0:T(8,128)S(1)}, u32[]{:S(2)}, u32[]{:S(2)}) collective-permute-start(f32[3,64,256]{2,1,0:T(8,128)S(1)} %get-tuple-element.93), channel_id=1, source_target_pairs={{0,8},{2,10},{4,12},{6,14},{8,0},{10,2},{12,4},{14,6},{16,24},{18,... | collective-permute-start | bytes 589832 | tf_op jit(solution)/shard_map/ppermute | solution.py:311
  37.6 18.1 %collective-permute-start.7 = (f32[3,64,256]{2,1,0:T(8,128)S(1)}, f32[3,64,256]{2,1,0:T(8,128)S(1)}, u32[]{:S(2)}, u32[]{:S(2)}) collective-permute-start(f32[3,64,256]{2,1,0:T(8,128)S(1)} %get-tuple-element.94), channel_id=1, source_target_pairs={{0,16},{2,18},{4,20},{6,22},{8,24},{10,26},{12,28},{14,30},{16,0},... | collective-permute-start | bytes 589832 | tf_op jit(solution)/shard_map/ppermute | solution.py:311
  40.2 15.5 %collective-permute-start.8 = (f32[3,64,256]{2,1,0:T(8,128)S(1)}, f32[3,64,256]{2,1,0:T(8,128)S(1)}, u32[]{:S(2)}, u32[]{:S(2)}) collective-permute-start(f32[3,64,256]{2,1,0:T(8,128)S(1)} %get-tuple-element.95), channel_id=1, source_target_pairs={{0,24},{2,26},{4,28},{6,30},{8,16},{10,18},{12,20},{14,22},{16,8},... | collective-permute-start | bytes 589832 | tf_op jit(solution)/shard_map/ppermute | solution.py:311
  43.4 17.8 %collective-permute-start.11 = (f32[2,256,256]{2,1,0:T(8,128)S(1)}, f32[2,256,256]{2,1,0:T(8,128)S(1)}, u32[]{:S(2)}, u32[]{:S(2)}) collective-permute-start(f32[2,256,256]{2,1,0:T(8,128)S(1)} %get-tuple-element.102), channel_id=1, source_target_pairs={{0,6},{2,4},{4,2},{6,0},{8,14},{10,12},{12,10},{14,8},{16,22},{18,... | collective-permute-start | bytes 1572872 | tf_op jit(solution)/shard_map/ppermute | solution.py:311
  55.7 4.9 %copy-start.7 = (f32[4]{0:T(128)S(1)}, f32[4]{0:T(128)}, u32[]{:S(2)}) copy-start(f32[4]{0:T(128)} %param.14) | copy-start | bytes 52
  56.2 9.6 %collective-permute-start.14 = (f32[3,64,256]{2,1,0:T(8,128)S(1)}, f32[3,64,256]{2,1,0:T(8,128)S(1)}, u32[]{:S(2)}, u32[]{:S(2)}) collective-permute-start(f32[3,64,256]{2,1,0:T(8,128)S(1)} %add_add_fusion.1.refs_4_), channel_id=1, source_target_pairs={{0,24},{2,26},{4,28},{6,30},{8,16},{10,18},{12,20},{14,22},{16,8},... | collective-permute-start | bytes 589832 | tf_op jit(solution)/shard_map/ppermute | solution.py:311
  59.8 13.6 %collective-permute-start.13 = (f32[3,64,256]{2,1,0:T(8,128)S(1)}, f32[3,64,256]{2,1,0:T(8,128)S(1)}, u32[]{:S(2)}, u32[]{:S(2)}) collective-permute-start(f32[3,64,256]{2,1,0:T(8,128)S(1)} %add_add_fusion.1.refs_4_), channel_id=1, source_target_pairs={{0,16},{2,18},{4,20},{6,22},{8,24},{10,26},{12,28},{14,30},{16,0},... | collective-permute-start | bytes 589832 | tf_op jit(solution)/shard_map/ppermute | solution.py:311
  60.0 13.5 %collective-permute-start.12 = (f32[3,64,256]{2,1,0:T(8,128)S(1)}, f32[3,64,256]{2,1,0:T(8,128)S(1)}, u32[]{:S(2)}, u32[]{:S(2)}) collective-permute-start(f32[3,64,256]{2,1,0:T(8,128)S(1)} %add_add_fusion.1.refs_4_), channel_id=1, source_target_pairs={{0,8},{2,10},{4,12},{6,14},{8,0},{10,2},{12,4},{14,6},{16,24},{18,... | collective-permute-start | bytes 589832 | tf_op jit(solution)/shard_map/ppermute | solution.py:311
  75.8 1.2 collective-permute-start.15
  77.0 4.5 %collective-permute-start.18 = (f32[2,4,256]{2,1,0:T(4,128)S(1)}, f32[2,4,256]{2,1,0:T(4,128)S(1)}, u32[]{:S(2)}, u32[]{:S(2)}) collective-permute-start(f32[2,4,256]{2,1,0:T(4,128)S(1)} %add.36.refs_4_), channel_id=1, source_target_pairs={{0,6},{2,4},{4,2},{6,0},{8,14},{10,12},{12,10},{14,8},{16,22},{18,... | collective-permute-start | bytes 24584 | tf_op jit(solution)/shard_map/ppermute | solution.py:311
  78.5 3.7 %collective-permute-start.17 = (f32[2,4,256]{2,1,0:T(4,128)S(1)}, f32[2,4,256]{2,1,0:T(4,128)S(1)}, u32[]{:S(2)}, u32[]{:S(2)}) collective-permute-start(f32[2,4,256]{2,1,0:T(4,128)S(1)} %add.36.refs_4_), channel_id=1, source_target_pairs={{0,4},{2,6},{4,0},{6,2},{8,12},{10,14},{12,8},{14,10},{16,20},{18,... | collective-permute-start | bytes 24584 | tf_op jit(solution)/shard_map/ppermute | solution.py:311
  79.1 3.7 %collective-permute-start.16 = (f32[2,4,256]{2,1,0:T(4,128)S(1)}, f32[2,4,256]{2,1,0:T(4,128)S(1)}, u32[]{:S(2)}, u32[]{:S(2)}) collective-permute-start(f32[2,4,256]{2,1,0:T(4,128)S(1)} %add.36.refs_4_), channel_id=1, source_target_pairs={{0,2},{2,0},{4,6},{6,4},{8,10},{10,8},{12,14},{14,12},{16,18},{18,... | collective-permute-start | bytes 24584 | tf_op jit(solution)/shard_map/ppermute | solution.py:311
  85.8 8.7 %collective-permute-start.19 = (f32[3,64,256]{2,1,0:T(8,128)S(1)}, f32[3,64,256]{2,1,0:T(8,128)S(1)}, u32[]{:S(2)}, u32[]{:S(2)}) collective-permute-start(f32[3,64,256]{2,1,0:T(8,128)S(1)} %get-tuple-element.110), channel_id=1, source_target_pairs={{0,8},{2,10},{4,12},{6,14},{8,0},{10,2},{12,4},{14,6},{16,24},{18,... | collective-permute-start | bytes 589832 | tf_op jit(solution)/shard_map/ppermute | solution.py:311
  85.9 17.3 %collective-permute-start.20 = (f32[3,64,256]{2,1,0:T(8,128)S(1)}, f32[3,64,256]{2,1,0:T(8,128)S(1)}, u32[]{:S(2)}, u32[]{:S(2)}) collective-permute-start(f32[3,64,256]{2,1,0:T(8,128)S(1)} %get-tuple-element.111), channel_id=1, source_target_pairs={{0,16},{2,18},{4,20},{6,22},{8,24},{10,26},{12,28},{14,30},{16,0},... | collective-permute-start | bytes 589832 | tf_op jit(solution)/shard_map/ppermute | solution.py:311
  89.1 14.1 %collective-permute-start.21 = (f32[3,64,256]{2,1,0:T(8,128)S(1)}, f32[3,64,256]{2,1,0:T(8,128)S(1)}, u32[]{:S(2)}, u32[]{:S(2)}) collective-permute-start(f32[3,64,256]{2,1,0:T(8,128)S(1)} %get-tuple-element.112), channel_id=1, source_target_pairs={{0,24},{2,26},{4,28},{6,30},{8,16},{10,18},{12,20},{14,22},{16,8},... | collective-permute-start | bytes 589832 | tf_op jit(solution)/shard_map/ppermute | solution.py:311
  90.3 13.0 %collective-permute-start.22 = (f32[256,256]{1,0:T(8,128)S(1)}, f32[256,256]{1,0:T(8,128)S(1)}, u32[]{:S(2)}, u32[]{:S(2)}) collective-permute-start(f32[256,256]{1,0:T(8,128)S(1)} %get-tuple-element.114), channel_id=1, source_target_pairs={{0,2},{2,0},{4,6},{6,4},{8,10},{10,8},{12,14},{14,12},{16,18},{18,... | collective-permute-start | bytes 786440 | tf_op jit(solution)/shard_map/ppermute | solution.py:311
  91.7 12.0 %collective-permute-start.23 = (f32[256,256]{1,0:T(8,128)S(1)}, f32[256,256]{1,0:T(8,128)S(1)}, u32[]{:S(2)}, u32[]{:S(2)}) collective-permute-start(f32[256,256]{1,0:T(8,128)S(1)} %get-tuple-element.115), channel_id=1, source_target_pairs={{0,4},{2,6},{4,0},{6,2},{8,12},{10,14},{12,8},{14,10},{16,20},{18,... | collective-permute-start | bytes 786440 | tf_op jit(solution)/shard_map/ppermute | solution.py:311
  94.5 9.2 %collective-permute-start.24 = (f32[256,256]{1,0:T(8,128)S(1)}, f32[256,256]{1,0:T(8,128)S(1)}, u32[]{:S(2)}, u32[]{:S(2)}) collective-permute-start(f32[256,256]{1,0:T(8,128)S(1)} %get-tuple-element.116), channel_id=1, source_target_pairs={{0,6},{2,4},{4,2},{6,0},{8,14},{10,12},{12,10},{14,8},{16,22},{18,... | collective-permute-start | bytes 786440 | tf_op jit(solution)/shard_map/ppermute | solution.py:311
  103.7 9.5 %collective-permute-start.27 = (f32[3,64,256]{2,1,0:T(8,128)S(1)}, f32[3,64,256]{2,1,0:T(8,128)S(1)}, u32[]{:S(2)}, u32[]{:S(2)}) collective-permute-start(f32[3,64,256]{2,1,0:T(8,128)S(1)} %add_add_fusion.refs_8_.refs_0_), channel_id=1, source_target_pairs={{0,24},{2,26},{4,28},{6,30},{8,16},{10,18},{12,20},{14,22},{16,8},... | collective-permute-start | bytes 589832 | tf_op jit(solution)/shard_map/ppermute | solution.py:311
  106.4 16.7 %collective-permute-start.26 = (f32[3,64,256]{2,1,0:T(8,128)S(1)}, f32[3,64,256]{2,1,0:T(8,128)S(1)}, u32[]{:S(2)}, u32[]{:S(2)}) collective-permute-start(f32[3,64,256]{2,1,0:T(8,128)S(1)} %add_add_fusion.refs_8_.refs_0_), channel_id=1, source_target_pairs={{0,16},{2,18},{4,20},{6,22},{8,24},{10,26},{12,28},{14,30},{16,0},... | collective-permute-start | bytes 589832 | tf_op jit(solution)/shard_map/ppermute | solution.py:311
  107.5 15.6 %collective-permute-start.25 = (f32[3,64,256]{2,1,0:T(8,128)S(1)}, f32[3,64,256]{2,1,0:T(8,128)S(1)}, u32[]{:S(2)}, u32[]{:S(2)}) collective-permute-start(f32[3,64,256]{2,1,0:T(8,128)S(1)} %add_add_fusion.refs_8_.refs_0_), channel_id=1, source_target_pairs={{0,8},{2,10},{4,12},{6,14},{8,0},{10,2},{12,4},{14,6},{16,24},{18,... | collective-permute-start | bytes 589832 | tf_op jit(solution)/shard_map/ppermute | solution.py:311
  127.2 10.8 %collective-permute-start.31 = (f32[2,3,64,256]{3,2,1,0:T(8,128)S(1)}, f32[2,3,64,256]{3,2,1,0:T(8,128)S(1)}, u32[]{:S(2)}, u32[]{:S(2)}) collective-permute-start(f32[2,3,64,256]{3,2,1,0:T(8,128)S(1)} %get-tuple-element.129), channel_id=1, source_target_pairs={{0,8},{2,10},{4,12},{6,14},{8,0},{10,2},{12,4},{14,6},{16,24},{18,... | collective-permute-start | bytes 1179656 | tf_op jit(solution)/shard_map/ppermute | solution.py:311
  127.3 23.6 %collective-permute-start.28 = (f32[2,256,256]{2,1,0:T(8,128)S(1)}, f32[2,256,256]{2,1,0:T(8,128)S(1)}, u32[]{:S(2)}, u32[]{:S(2)}) collective-permute-start(f32[2,256,256]{2,1,0:T(8,128)S(1)} %get-tuple-element.123), channel_id=1, source_target_pairs={{0,2},{2,0},{4,6},{6,4},{8,10},{10,8},{12,14},{14,12},{16,18},{18,... | collective-permute-start | bytes 1572872 | tf_op jit(solution)/shard_map/ppermute | solution.py:311
  128.5 26.3 %collective-permute-start.29 = (f32[2,256,256]{2,1,0:T(8,128)S(1)}, f32[2,256,256]{2,1,0:T(8,128)S(1)}, u32[]{:S(2)}, u32[]{:S(2)}) collective-permute-start(f32[2,256,256]{2,1,0:T(8,128)S(1)} %get-tuple-element.124), channel_id=1, source_target_pairs={{0,4},{2,6},{4,0},{6,2},{8,12},{10,14},{12,8},{14,10},{16,20},{18,... | collective-permute-start | bytes 1572872 | tf_op jit(solution)/shard_map/ppermute | solution.py:311
  129.3 25.5 %collective-permute-start.30 = (f32[2,256,256]{2,1,0:T(8,128)S(1)}, f32[2,256,256]{2,1,0:T(8,128)S(1)}, u32[]{:S(2)}, u32[]{:S(2)}) collective-permute-start(f32[2,256,256]{2,1,0:T(8,128)S(1)} %get-tuple-element.125), channel_id=1, source_target_pairs={{0,6},{2,4},{4,2},{6,0},{8,14},{10,12},{12,10},{14,8},{16,22},{18,... | collective-permute-start | bytes 1572872 | tf_op jit(solution)/shard_map/ppermute | solution.py:311
  138.1 10.8 %collective-permute-start.32 = (f32[1,3,64,256]{3,2,1,0:T(8,128)S(1)}, f32[1,3,64,256]{3,2,1,0:T(8,128)S(1)}, u32[]{:S(2)}, u32[]{:S(2)}) collective-permute-start(f32[1,3,64,256]{3,2,1,0:T(8,128)S(1)} %get-tuple-element.138), channel_id=1, source_target_pairs={{0,16},{2,18},{4,20},{6,22},{8,24},{10,26},{12,28},{14,30},{16,0},... | collective-permute-start | bytes 589832 | tf_op jit(solution)/shard_map/ppermute | solution.py:311
  149.4 7.7 %collective-permute-start.33 = (f32[3,16,256]{2,1,0:T(8,128)S(1)}, f32[3,16,256]{2,1,0:T(8,128)S(1)}, u32[]{:S(2)}, u32[]{:S(2)}) collective-permute-start(f32[3,16,256]{2,1,0:T(8,128)S(1)} %get-tuple-element.132), channel_id=1, source_target_pairs={{0,2},{2,0},{4,6},{6,4},{8,10},{10,8},{12,14},{14,12},{16,18},{18,... | collective-permute-start | bytes 147464 | tf_op jit(solution)/shard_map/ppermute | solution.py:311
  150.9 6.3 %collective-permute-start.34 = (f32[3,16,256]{2,1,0:T(8,128)S(1)}, f32[3,16,256]{2,1,0:T(8,128)S(1)}, u32[]{:S(2)}, u32[]{:S(2)}) collective-permute-start(f32[3,16,256]{2,1,0:T(8,128)S(1)} %get-tuple-element.133), channel_id=1, source_target_pairs={{0,4},{2,6},{4,0},{6,2},{8,12},{10,14},{12,8},{14,10},{16,20},{18,... | collective-permute-start | bytes 147464 | tf_op jit(solution)/shard_map/ppermute | solution.py:311
  150.9 6.3 %collective-permute-start.35 = (f32[3,16,256]{2,1,0:T(8,128)S(1)}, f32[3,16,256]{2,1,0:T(8,128)S(1)}, u32[]{:S(2)}, u32[]{:S(2)}) collective-permute-start(f32[3,16,256]{2,1,0:T(8,128)S(1)} %get-tuple-element.134), channel_id=1, source_target_pairs={{0,6},{2,4},{4,2},{6,0},{8,14},{10,12},{12,10},{14,8},{16,22},{18,... | collective-permute-start | bytes 147464 | tf_op jit(solution)/shard_map/ppermute | solution.py:311

commit v4 on v3

v4 whole, which is shorter than its diff:
```python
import functools
import math

import jax
import jax.numpy as jnp
from jax import lax
from jax.experimental import pallas as pl
from jax.experimental.pallas import tpu as pltpu
from jax.sharding import PartitionSpec as P

F32 = jnp.float32
BF16 = jnp.bfloat16
LANES = 128
VMEM_LIMIT = 40 * 1024 * 1024
WHOLE_VMEM = 60 * 1024 * 1024


def mm(a, b):
    return jnp.dot(a, b, preferred_element_type=F32)


def mm_t(a, b):
    return lax.dot_general(a, b, (((1,), (1,)), ((), ())), preferred_element_type=F32)


def tmm(a, b):
    return lax.dot_general(a, b, (((0,), (0,)), ((), ())), preferred_element_type=F32)


def place_of(i, array, left):
    if array.dtype == jnp.int32:
        return pl.BlockSpec(memory_space=pltpu.SMEM)
    return pl.BlockSpec(memory_space=pltpu.HBM if i in left else pltpu.VMEM)


def call(body, out_shape, scratch, flops, *args, left=()):
    vmem = pl.BlockSpec(memory_space=pltpu.VMEM)
    size = sum(a.size * a.dtype.itemsize for a in args)
    size += sum(math.prod(o.shape) * o.dtype.itemsize for o in out_shape)
    return pl.pallas_call(
        body,
        out_shape=out_shape,
        in_specs=[place_of(i, a, left) for i, a in enumerate(args)],
        out_specs=[vmem] * len(out_shape),
        scratch_shapes=scratch,
        compiler_params=pltpu.CompilerParams(
            vmem_limit_bytes=WHOLE_VMEM if left else VMEM_LIMIT
        ),
        cost_estimate=pl.CostEstimate(flops=flops, bytes_accessed=size, transcendentals=0),
    )(*args)


def put_rows(scratch, x):
    for i in range(scratch.shape[0]):
        scratch[i] = x[:, i * LANES : (i + 1) * LANES]


def take_head(scratch, head, tokens, heads):
    parts = [scratch[i, pl.ds(head, tokens, stride=heads), :] for i in range(scratch.shape[0])]
    return jnp.concatenate(parts, axis=1)


def put_head(scratch, head, x, tokens, heads):
    for i in range(scratch.shape[0]):
        scratch[i, pl.ds(head, tokens, stride=heads), :] = x[:, i * LANES : (i + 1) * LANES]


def rows_of(scratch):
    return jnp.concatenate([scratch[i] for i in range(scratch.shape[0])], axis=1)


def split_kernel(groups, place, x, *rest):
    outs, scratch = rest[:groups], rest[groups]
    tokens, heads, width = x.shape
    put_rows(scratch, x[...].astype(F32).reshape(tokens * heads, width))
    for step in range(groups):
        outs[step][...] = take_head(scratch, place[0] ^ step, tokens, heads)


def split_update_kernel(groups, place, r, scales, k, v, w_gate, w_out, w_up, *rest):
    outs, own = rest[:groups], rest[groups]
    scratch, k_here, v_here, sems = rest[groups + 1 :]
    width = k.shape[2]
    first = pltpu.make_async_copy(k, k_here, sems.at[0])
    second = pltpu.make_async_copy(v, v_here, sems.at[1])
    first.start()
    second.start()
    copies = []
    for i, w in enumerate((w_gate, w_out, w_up)):
        to = own.at[pl.ds(i * width, width)]
        copies.append(pltpu.make_async_copy(w.at[place[0]], to, sems.at[2 + i]))
        copies[-1].start()
    own[3 * width :, :] = jnp.broadcast_to(scales[pl.ds(place[0], 1), :], (8, width))
    first.wait()
    split_kernel(groups, place, k_here, *[out.at[0] for out in outs], scratch)
    second.wait()
    split_kernel(groups, place, v_here, *[out.at[1] for out in outs], scratch)
    for step in range(groups):
        scaled = outs[step][1] * rate_column(r, place[0] ^ step)
        outs[step][1] = scaled.astype(BF16).astype(F32)
    for copy in copies:
        copy.wait()


def split_apply_kernel(groups, place, q, cot, gain, *rest):
    outs, scratch = rest[:groups], rest[groups]
    split_kernel(groups, place, q, *[out.at[0] for out in outs], scratch)
    split_kernel(groups, place, cot, *[out.at[1] for out in outs], scratch)
    for step in range(groups):
        outs[step][1] *= gain[pl.ds(place[0] ^ step, 1), :]


def rate_column(r, head):
    return jnp.broadcast_to(r[pl.ds(head, 1), :], (8, r.shape[1])).T[:, 0:1]


def halving_order(depth):
    sets, bit = [], 1
    while bit < depth:
        sets.append(list(range(bit, depth, 2 * bit)))
        bit *= 2
    return sets + [[0]]


def send_slices(sums, outs, rank, depth):
    rows = sums.shape[1] // depth
    for out, members in zip(outs, halving_order(depth)):
        for i, step in enumerate(members):
            at = pl.multiple_of((rank ^ step) * rows, rows)
            out[i] = sums[:, pl.ds(at, rows), :]


def weights_of(own, width):
    return [own[i * width : (i + 1) * width, :].astype(BF16) for i in range(3)]


def update_kernel(groups, depth, scale, place, own, *refs):
    pieces, outs, sums = refs[:groups], refs[groups:-1], refs[-1]
    width = sums.shape[1]
    gate_b, out_b, up_b = weights_of(own, width)
    total = [0.0, 0.0, 0.0]
    for piece in pieces:
        keys = piece[0].astype(BF16)
        scaled = piece[1].astype(BF16)
        first = mm(keys, gate_b)
        third = mm(keys, up_b)
        sig = jax.nn.sigmoid(first)
        activ = first * sig
        act = (activ * third).astype(BF16)
        dact = mm_t(scaled, out_b)
        deriv = sig * (1.0 + first * (1.0 - sig))
        dfirst = (dact * third * deriv).astype(BF16)
        dthird = (dact * activ).astype(BF16)
        total[0] += tmm(keys, dfirst)
        total[1] += tmm(act, scaled)
        total[2] += tmm(keys, dthird)
    for i in range(3):
        sums[i] = total[i] * scale
    send_slices(sums, outs, place[1], depth)
    rows = width // depth
    for i in range(3):
        at = pl.multiple_of(i * width + place[1] * rows, rows)
        outs[-1][0, i] += own[pl.ds(at, rows), :]


def assemble(place, depth, parts, whole):
    rows = whole.shape[1] // depth
    for part, members in zip(parts, gathered_order(depth)):
        for i, step in enumerate(members):
            at = pl.multiple_of((place[1] ^ step) * rows, rows)
            whole[:, pl.ds(at, rows), :] = part[i]


def gathered_order(depth):
    held, bit = [0], depth // 2
    while bit > 1:
        held = held + [step ^ bit for step in held]
        bit //= 2
    return [held, [step ^ 1 for step in held]] if depth > 1 else [held]


def apply_kernel(groups, depth, place, own, *refs):
    pieces = refs[:groups]
    parts = refs[groups:-6]
    first_ref, third_ref, os_ref, new_b, stats, whole = refs[-6:]
    assemble(place, depth, parts, whole)
    new_b[...] = whole[...].astype(BF16)
    for step in range(groups):
        queries = pieces[step][0].astype(BF16)
        tokens = queries.shape[0]
        first = mm(queries, new_b[0])
        third = mm(queries, new_b[2])
        hidden = (first * jax.nn.sigmoid(first) * third).astype(BF16)
        scaled = mm(hidden, new_b[1]) * own[-8:-7, :]
        first_ref[step] = first
        third_ref[step] = third
        os_ref[step] = scaled
        sq = jnp.sum(scaled * scaled, axis=1, keepdims=True)
        ps = jnp.sum(scaled * pieces[step][1], axis=1, keepdims=True)
        lane = lax.broadcasted_iota(jnp.int32, (tokens, LANES), 1)
        both = jnp.where(lane == 0, sq, jnp.where(lane == 1, ps, 0.0)).T
        source = place[0] ^ step
        stats[0, pl.ds(source, 1), :] = both[0:1, :]
        stats[1, pl.ds(source, 1), :] = both[1:2, :]


def apply_back_kernel(groups, depth, count, place, own, *refs):
    pieces = refs[:groups]
    stats = refs[groups : 2 * groups]
    first_ref, third_ref, os_ref, new_b = refs[2 * groups : 2 * groups + 4]
    outs = refs[2 * groups + 4 : 3 * groups + 4]
    slices, sums, both = refs[3 * groups + 4 : -2], refs[-2], refs[-1]
    hs = own[-8:-7, :]
    total_stats = stats[0][...]
    for other in stats[1:]:
        total_stats += other[...]
    both[...] = total_stats
    total = [0.0, 0.0, 0.0]
    for step in range(groups):
        queries = pieces[step][0].astype(BF16)
        source = place[0] ^ step
        sq = rate_column(both.at[0], source)
        ps = rate_column(both.at[1], source)
        inv = lax.rsqrt(sq / count + 1e-06)
        scaled = os_ref[step]
        dos = inv * pieces[step][1] - scaled * (inv * inv * inv * ps / count)
        dout = (dos * hs).astype(BF16)
        first = first_ref[step]
        third = third_ref[step]
        sig = jax.nn.sigmoid(first)
        activ = first * sig
        hidden = (activ * third).astype(BF16)
        dhidden = mm_t(dout, new_b[1])
        dthird = (dhidden * activ).astype(BF16)
        dfirst = (dhidden * third * (sig * (1.0 + first * (1.0 - sig)))).astype(BF16)
        outs[step][...] = mm_t(dfirst, new_b[0]) + mm_t(dthird, new_b[2])
        total[0] += tmm(queries, dfirst)
        total[1] += tmm(hidden, dout)
        total[2] += tmm(queries, dthird)
    for i in range(3):
        sums[i] = total[i]
    send_slices(sums, slices, place[1], depth)


def update_back_kernel(groups, depth, scale, place, own, *refs):
    pieces = refs[:groups]
    count = len(gathered_order(depth))
    parts, refs = refs[groups : groups + count], refs[groups + count :]
    outs, slices = refs[:groups], refs[groups:-2]
    whole, sums = refs[-2:]
    assemble(place, depth, parts, whole)
    gate_b, out_b, up_b = weights_of(own, whole.shape[1])
    cot_gate, cot_out, cot_up = ((whole[i] * scale).astype(BF16) for i in range(3))
    total = [0.0, 0.0, 0.0]
    for step in range(groups):
        keys = pieces[step][0].astype(BF16)
        scaled = pieces[step][1].astype(BF16)
        first = mm(keys, gate_b)
        third = mm(keys, up_b)
        sig = jax.nn.sigmoid(first)
        activ = first * sig
        act = (activ * third).astype(BF16)
        dact = mm_t(scaled, out_b)
        slope = sig * (1.0 - sig)
        deriv = sig + first * slope
        second = slope * (2.0 + first * (1.0 - 2.0 * sig))
        third_deriv = third * deriv
        dfirst = (dact * third_deriv).astype(BF16)
        dthird = (dact * activ).astype(BF16)
        bar_dfirst = mm(keys, cot_gate)
        bar_dthird = mm(keys, cot_up)
        bar_act = mm_t(scaled, cot_out)
        bar_activ = bar_dthird * dact + bar_act * third
        bar_dact = (bar_dfirst * third_deriv + bar_dthird * activ).astype(BF16)
        bar_df_dact = bar_dfirst * dact
        bar_third = (bar_df_dact * deriv + bar_act * activ).astype(BF16)
        bar_first = (bar_activ * deriv + bar_df_dact * third * second).astype(BF16)
        outs[step][0] = (
            mm_t(dfirst, cot_gate)
            + mm_t(dthird, cot_up)
            + mm_t(bar_first, gate_b)
            + mm_t(bar_third, up_b)
        )
        outs[step][1] = mm(act, cot_out) + mm(bar_dact, out_b)
        total[0] += tmm(keys, bar_first)
        total[1] += tmm(bar_dact, scaled)
        total[2] += tmm(keys, bar_third)
    for i in range(3):
        sums[i] = total[i]
    send_slices(sums, slices, place[1], depth)


def join_query_kernel(groups, place, *refs):
    pieces, out, scratch = refs[:groups], refs[groups], refs[groups + 1]
    tokens, heads, width = out.shape
    for step, piece in enumerate(pieces):
        put_head(scratch, place[0] ^ step, piece[...], tokens, heads)
    out[...] = rows_of(scratch).reshape(tokens, heads, width).astype(BF16)


def join_update_kernel(groups, place, r, *refs):
    pieces, (out_k, out_v, sk, sv) = refs[:groups], refs[groups:]
    tokens, heads, width = out_k.shape
    for step, piece in enumerate(pieces):
        head = place[0] ^ step
        put_head(sk, head, piece[0], tokens, heads)
        put_head(sv, head, piece[1] * rate_column(r, head), tokens, heads)
    out_k[...] = rows_of(sk).reshape(tokens, heads, width).astype(BF16)
    out_v[...] = rows_of(sv).reshape(tokens, heads, width).astype(BF16)


def rows_kernel(groups, place, *refs):
    parts, outs, total = refs[: -groups - 1], refs[-groups - 1 : -1], refs[-1]
    summed = parts[0][0]
    for part in parts[1:]:
        summed += part[0]
    total[...] = summed
    rows = total.shape[1] // groups
    for step, out in enumerate(outs):
        at = pl.multiple_of((place[0] ^ step) * rows, rows)
        out[...] = total[:, pl.ds(at, rows), :]


def join_rows_kernel(groups, place, *refs):
    parts, outs = refs[:groups], refs[groups:]
    for step, part in enumerate(parts):
        for i, out in enumerate(outs):
            out[place[0] ^ step] = part[i]


def local(queries, keys, values, rates, head_scale, gain, w_gate, w_out, w_up, cotangent):
    tokens, heads, width = keys.shape[1:]
    hidden = w_gate.shape[2]
    ctx = lax.axis_size("ctx")
    blocks = lax.axis_size("head")
    groups = heads
    depth = ctx // groups
    assert groups & (groups - 1) == 0 and depth & (depth - 1) == 0
    assert blocks & (blocks - 1) == 0 and depth % blocks == 0 and hidden == width
    scale = 1.0 / math.sqrt(tokens * ctx * width)
    count = float(heads * blocks * width)
    me, block = lax.axis_index("ctx"), lax.axis_index("head")
    mine = lax.rem(me, groups)
    low = lax.rem(lax.div(me, groups), blocks)
    rank = lax.div(me, groups * blocks) * blocks + block
    place = jnp.stack([mine, rank]).astype(jnp.int32)

    def shift(x, axis, step):
        return lax.ppermute(x, axis, [(c, c ^ step) for c in range(lax.axis_size(axis))])

    def in_rank(x, bit):
        return shift(x, "head", bit) if bit < blocks else shift(x, "ctx", bit * groups)

    def swap(x, step):
        pairs = []
        for c in range(ctx):
            hi, a, p = c // (groups * blocks), c // groups % blocks, c % groups
            for b in range(blocks):
                to = (hi * blocks + b) * groups + (p ^ step)
                pairs.append((c * blocks + b, to * blocks + a))
        return lax.ppermute(x, ("ctx", "head"), pairs)

    def exchange(parts):
        return [swap(part, step) for step, part in enumerate(parts)]

    def scatter(stacks):
        stacks = list(stacks)
        for i in range(len(stacks) - 1):
            got = in_rank(stacks[i], 1 << i)
            for j in range(i + 1, len(stacks) - 1):
                stacks[j] = stacks[j] + got[1 << (j - i - 1) :: 1 << (j - i)]
            stacks[-1] = stacks[-1] + got[:1]
        return stacks[-1]

    def gather(held, beside):
        bit = depth // 2
        while bit > 1:
            held = jnp.concatenate([held, in_rank(held, bit)])
            bit //= 2
        held, beside = after(held, beside)
        return ([held, in_rank(held, bit)] if bit else [held]), beside

    def fetch(bundle):
        own = jnp.where(block == low, bundle, 0.0)
        for step in range(1, blocks):
            pairs = [
                (c * blocks + a, c * blocks + (a ^ step))
                for c in range(ctx)
                for a in [c // groups % blocks]
            ]
            own = own + lax.ppermute(bundle, ("ctx", "head"), pairs)
        return own

    def after(x, *others):
        return lax.optimization_barrier((x, *others))

    def shape(*dims, dtype=F32):
        return jax.ShapeDtypeStruct(dims, dtype)

    flops = 2 * groups * tokens * width * hidden
    rows = hidden // depth
    pieces = [shape(2, tokens, width)] * groups
    stacks = [shape(len(members), 3, rows, width) for members in halving_order(depth)]
    joined = shape(tokens, heads, width, dtype=BF16)
    scratch = pltpu.VMEM((width // LANES, tokens * heads, LANES), F32)
    square = pltpu.VMEM((3, hidden, width), F32)

    scales = jnp.broadcast_to(head_scale[:, None], (heads, width))
    sent = call(
        functools.partial(split_update_kernel, groups), pieces + [shape(3 * width + 8, width)],
        [scratch] + [pltpu.VMEM((tokens, heads, width), BF16)] * 2
        + [pltpu.SemaphoreType.DMA((5,))], flops // 8,
        place, rates[0], scales, keys[0], values[0], w_gate, w_out, w_up, left=(3, 4, 5, 6, 7),
    )
    own = fetch(sent[-1])
    k_in = exchange(sent[:-1])
    q_out = call(
        functools.partial(split_apply_kernel, groups), pieces, [scratch], flops // 8,
        place, queries[0], cotangent[0], gain,
    )
    terms = call(
        functools.partial(update_kernel, groups, depth, scale), stacks, [square], 6 * flops,
        place, own, *k_in,
    )
    terms, q_out = after(terms, q_out)
    new, q_in = gather(scatter(terms), exchange(q_out))
    kept = shape(groups, tokens, width)
    first, third, scaled, new_b, stats = call(
        functools.partial(apply_kernel, groups, depth),
        [kept, kept, kept, shape(3, hidden, width, dtype=BF16), shape(2, groups, tokens)],
        [square], 3 * flops, place, own, *q_in, *new,
    )
    bit = 1
    while bit < blocks:
        stats = stats + shift(stats, "ctx", bit * groups)
        bit *= 2
    stats = [stats] + [shift(stats, "ctx", step) for step in range(1, groups)]
    out = call(
        functools.partial(apply_back_kernel, groups, depth, count),
        [shape(tokens, width)] * groups + stacks,
        [square, pltpu.VMEM((2, groups, tokens), F32)], 6 * flops,
        place, own, *q_in, *stats, first, third, scaled, new_b,
    )
    q_back = exchange(out[:groups])
    half = groups // 2
    part, q_back[:half] = after(scatter(out[groups:]), q_back[:half])
    parts, q_back[half:] = gather(part, q_back[half:])
    (grad_q,) = call(
        functools.partial(join_query_kernel, groups), [joined], [scratch], flops // 16,
        place, *q_back,
    )
    parts, grad_q = after(parts, grad_q)
    out = call(
        functools.partial(update_back_kernel, groups, depth, scale), pieces + stacks,
        [square] * 2, 15 * flops, place, own, *k_in, *parts,
    )
    back = exchange(out[:groups])
    own_rows = rows // groups
    sent = call(
        functools.partial(rows_kernel, groups), [shape(3, own_rows, width)] * groups,
        [pltpu.VMEM((3, rows, width), F32)], flops // 100, place, part, scatter(out[groups:]),
    )
    grads = call(
        functools.partial(join_rows_kernel, groups), [shape(heads, own_rows, width)] * 3, [],
        flops // 100, place, *exchange(sent),
    )
    grad_k, grad_v = call(
        functools.partial(join_update_kernel, groups), [joined] * 2, [scratch] * 2, flops // 8,
        place, rates[0], *back,
    )
    if lax.axis_size("batch") > 1:
        grads = [lax.psum_scatter(x, "batch", scatter_dimension=1, tiled=True) for x in grads]
    return (grad_q[None], grad_k[None], grad_v[None], grads[0], grads[1], grads[2])


def solution(mesh):
    in_specs = (
        P("batch", "ctx", "head", None),
        P("batch", "ctx", "head", None),
        P("batch", "ctx", "head", None),
        P("batch", "head", "ctx"),
        P("head"),
        P("head", None),
        P("head", None, None),
        P("head", None, None),
        P("head", None, None),
        P("batch", "ctx", "head", None),
    )
    out_specs = (
        P("batch", "ctx", "head", None),
        P("batch", "ctx", "head", None),
        P("batch", "ctx", "head", None),
        P("head", ("ctx", "batch"), None),
        P("head", ("ctx", "batch"), None),
        P("head", ("ctx", "batch"), None),
    )
    return jax.shard_map(local, mesh=mesh, in_specs=in_specs, out_specs=out_specs, check_vma=False)
```

time: 159 us -> 186 us (1.17)
  the two profiles are of different devices: /device:TPU:0 before, /device:TPU:1 now
where the time goes in v4:
time: 186 us
  waiting for transfers between devices  104 us (56%)
  starting transfers between devices  54.9 us (30%)
  Pallas kernels  21.6 us (12%)
  other arithmetic  2.1 us (1%)
  local copies, waits for them, and re-layouts  2 us (1%)
    ppermute x14, waiting for transfers between devices, shift(): lax.ppermute(x, axis, [(c, c ^ step) for c in range(lax.axis_size(axis))])  66.4 us
    ppermute x20, starting transfers between devices, swap(): return lax.ppermute(x, ('ctx', 'head'), pairs)  40.8 us
    ppermute x20, waiting for transfers between devices, swap(): return lax.ppermute(x, ('ctx', 'head'), pairs)  37.6 us
    pallas_call x10, Pallas kernels, call(): pl.pallas_call(body, out_shape=out_shape, in_specs=[place_of(i, a, left)...  21.6 us
    ppermute x14, starting transfers between devices, shift(): lax.ppermute(x, axis, [(c, c ^ step) for c in range(lax.axis_size(axis))])  12.8 us
  transfers between devices with their start and end apart: 35, of which 22 were waited for; matrix products, arithmetic and copies ran while one was open for 1% of the time, Pallas kernels for 3%

profile of v4, /device:TPU:1, one launch (start us, length us, event | category | flops | bytes accessed | tf_op | source)
XLA Modules:
  0.0 185.5 jit_solution(928567667293998016)
XLA Ops:
  0.6 0.6 pad_add_fusion.place
  1.2 0.7 copy-done.6
  1.9 0.7 broadcast_in_dim.19.scales
  2.5 4.3 %shard_map.145 = (f32[2,256,256]{2,1,0:T(8,128)}, f32[2,256,256]{2,1,0:T(8,128)}, f32[2,256,256]{2,1,0:T(8,128)}, f32[2,256,256]{2,1,0:T(8,128)}, f32[776,256]{1,0:T(8,128)}) custom-call(s32[2]{0:T(128)} %pad_add_fusion.place, f32[4,256]{1,0:T(4,128)} %bitcast.12, f32[4,256]{1,0:T(4,128)} %broadcast_in_dim.19.scales, bf16[256,4,256]{2,1,0:T(4,128)(2,1)} %bitcast.14, ...), custom_call_target="tpu_custom_call" | custom-call | flops 16777216 | bytes 7094280 | tf_op jit(solution)/shard_map/pallas_call | solution.py:40
  6.9 1.3 collective-permute-start
  8.2 4.6 %collective-permute-start.1 = (f32[2,256,256]{2,1,0:T(8,128)}, f32[2,256,256]{2,1,0:T(8,128)S(1)}, u32[]{:S(2)}, u32[]{:S(2)}) collective-permute-start(f32[2,256,256]{2,1,0:T(8,128)} %get-tuple-element.68), channel_id=1, source_target_pairs={{0,0},{1,8},{2,2},{3,10},{4,4},{5,12},{6,6},{7,14},{8,1},{9,9},{10... | collective-permute-start | bytes 1572872 | tf_op jit(solution)/shard_map/ppermute | solution.py:361
  12.8 1.0 collective-permute-start.2
  13.8 2.7 %collective-permute-start.3 = (f32[2,256,256]{2,1,0:T(8,128)}, f32[2,256,256]{2,1,0:T(8,128)S(1)}, u32[]{:S(2)}, u32[]{:S(2)}) collective-permute-start(f32[2,256,256]{2,1,0:T(8,128)} %get-tuple-element.70), channel_id=1, source_target_pairs={{0,4},{1,12},{2,6},{3,14},{4,0},{5,8},{6,2},{7,10},{8,5},{9,13},{1... | collective-permute-start | bytes 1572872 | tf_op jit(solution)/shard_map/ppermute | solution.py:361
  16.5 0.7 copy-done.4
  17.2 1.3 shard_map.147
  18.5 1.2 select_add_fusion.own
  19.7 0.4 collective-permute-done.1.refs_0_
  20.1 6.4 %collective-permute-done.2.refs_1_ = f32[2,256,256]{2,1,0:T(8,128)S(1)} collective-permute-done((f32[2,256,256]{2,1,0:T(8,128)}, f32[2,256,256]{2,1,0:T(8,128)S(1)}, u32[]{:S(2)}, u32[]{:S(2)}) %collective-permute-start.2) | collective-permute-done | bytes 524320 | tf_op jit(solution)/shard_map/ppermute | solution.py:361
  26.5 9.7 %collective-permute-done.3.refs_2_ = f32[2,256,256]{2,1,0:T(8,128)S(1)} collective-permute-done((f32[2,256,256]{2,1,0:T(8,128)}, f32[2,256,256]{2,1,0:T(8,128)S(1)}, u32[]{:S(2)}, u32[]{:S(2)}) %collective-permute-start.3) | collective-permute-done | bytes 524320 | tf_op jit(solution)/shard_map/ppermute | solution.py:361
  36.1 6.2 %collective-permute-done.4.refs_3_ = f32[2,256,256]{2,1,0:T(8,128)S(1)} collective-permute-done((f32[2,256,256]{2,1,0:T(8,128)}, f32[2,256,256]{2,1,0:T(8,128)S(1)}, u32[]{:S(2)}, u32[]{:S(2)}) %collective-permute-start.4) | collective-permute-done | bytes 524320 | tf_op jit(solution)/shard_map/ppermute | solution.py:361
  42.3 2.2 %shard_map.146 = (f32[2,3,64,256]{3,2,1,0:T(8,128)S(1)}, f32[1,3,64,256]{3,2,1,0:T(8,128)S(1)}, f32[1,3,64,256]{3,2,1,0:T(8,128)S(1)}) custom-call(s32[2]{0:T(128)S(1)} %copy-done.2, f32[776,256]{1,0:T(8,128)S(1)} %select_add_fusion.own, f32[2,256,256]{2,1,0:T(8,128)S(1)} %collective-permute-done.1.refs_0_, ...), custom_call_target="tpu_custom_call" | custom-call | flops 805306368 | bytes 3678216 | tf_op jit(solution)/shard_map/pallas_call | solution.py:40
  44.5 1.7 collective-permute-start.5
  46.2 1.3 collective-permute-done.5
  47.6 2.4 %collective-permute-start.6 = (f32[1,3,64,256]{3,2,1,0:T(8,128)S(1)}, f32[1,3,64,256]{3,2,1,0:T(8,128)S(1)}, u32[]{:S(2)}, u32[]{:S(2)}) collective-permute-start(f32[1,3,64,256]{3,2,1,0:T(8,128)S(1)} %slice_add_fusion.4), channel_id=1, source_target_pairs={{0,16},{2,18},{4,20},{6,22},{8,24},{10,26},{12,28},{14,30},{16,0},... | collective-permute-start | bytes 589832 | tf_op jit(solution)/shard_map/ppermute | solution.py:349
  50.0 3.1 %collective-permute-start.8 = (f32[2,256,256]{2,1,0:T(8,128)S(1)}, f32[2,256,256]{2,1,0:T(8,128)S(1)}, u32[]{:S(2)}, u32[]{:S(2)}) collective-permute-start(f32[2,256,256]{2,1,0:T(8,128)S(1)} %get-tuple-element.82), channel_id=1, source_target_pairs={{0,0},{1,8},{2,2},{3,10},{4,4},{5,12},{6,6},{7,14},{8,1},{9,9},{10... | collective-permute-start | bytes 1572872 | tf_op jit(solution)/shard_map/ppermute | solution.py:361
  53.0 1.6 collective-permute-start.9
  54.6 1.1 collective-permute-start.10
  55.7 1.5 collective-permute-start.11
  57.2 1.9 %collective-permute-done.6 = f32[1,3,64,256]{3,2,1,0:T(8,128)S(1)} collective-permute-done((f32[1,3,64,256]{3,2,1,0:T(8,128)S(1)}, f32[1,3,64,256]{3,2,1,0:T(8,128)S(1)}, u32[]{:S(2)}, u32[]{:S(2)}) %collective-permute-start.6) | collective-permute-done | bytes 196640 | tf_op jit(solution)/shard_map/ppermute | solution.py:349
  59.2 23.0 %collective-permute-done.7 = f32[1,3,64,256]{3,2,1,0:T(8,128)S(1)} collective-permute-done((f32[1,3,64,256]{3,2,1,0:T(8,128)S(1)}, f32[1,3,64,256]{3,2,1,0:T(8,128)S(1)}, u32[]{:S(2)}, u32[]{:S(2)}) %collective-permute-start.7) | collective-permute-done | bytes 196640 | tf_op jit(solution)/shard_map/ppermute | solution.py:349
  82.3 3.7 %collective-permute-done.11.refs_3_ = f32[2,256,256]{2,1,0:T(8,128)S(1)} collective-permute-done((f32[2,256,256]{2,1,0:T(8,128)S(1)}, f32[2,256,256]{2,1,0:T(8,128)S(1)}, u32[]{:S(2)}, u32[]{:S(2)}) %collective-permute-start.11) | collective-permute-done | bytes 524320 | tf_op jit(solution)/shard_map/ppermute | solution.py:361
  86.0 1.7 collective-permute-done.12.refs_5_
  87.7 1.7 shard_map.148
  89.4 2.5 %collective-permute-done.13 = f32[2,4,256]{2,1,0:T(4,128)S(1)} collective-permute-done((f32[2,4,256]{2,1,0:T(4,128)S(1)}, f32[2,4,256]{2,1,0:T(4,128)S(1)}, u32[]{:S(2)}, u32[]{:S(2)}) %collective-permute-start.13) | collective-permute-done | bytes 8224 | tf_op jit(solution)/shard_map/ppermute | solution.py:349
  91.9 1.2 collective-permute-start.16
  93.2 0.2 collective-permute-start.15
  93.4 1.2 collective-permute-start.14
  94.6 0.8 collective-permute-done.16.refs_7_
  95.3 0.3 collective-permute-done.15.refs_6_
  95.7 0.2 collective-permute-done.14.refs_5_
  95.9 2.4 %shard_map.149 = (f32[256,256]{1,0:T(8,128)S(1)}, f32[256,256]{1,0:T(8,128)S(1)}, f32[256,256]{1,0:T(8,128)S(1)}, f32[256,256]{1,0:T(8,128)S(1)}, f32[2,3,64,256...) custom-call(s32[2]{0:T(128)S(1)} %copy-done.2, f32[776,256]{1,0:T(8,128)S(1)} %select_add_fusion.own, ...), custom_call_target="tpu_custom_call" | custom-call | flops 805306368 | bytes 8298504 | tf_op jit(solution)/shard_map/pallas_call | solution.py:40
  98.3 3.1 %collective-permute-start.17 = (f32[2,3,64,256]{3,2,1,0:T(8,128)S(1)}, f32[2,3,64,256]{3,2,1,0:T(8,128)S(1)}, u32[]{:S(2)}, u32[]{:S(2)}) collective-permute-start(f32[2,3,64,256]{3,2,1,0:T(8,128)S(1)} %get-tuple-element.97), channel_id=1, source_target_pairs={{0,1},{1,0},{2,3},{3,2},{4,5},{5,4},{6,7},{7,6},{8,9},{9,8},{10,11... | collective-permute-start | bytes 1179656 | tf_op jit(solution)/shard_map/ppermute | solution.py:349
  101.4 1.3 collective-permute-done.17
  102.8 0.2 collective-permute-start.18
  103.0 3.7 %collective-permute-start.19 = (f32[256,256]{1,0:T(8,128)S(1)}, f32[256,256]{1,0:T(8,128)S(1)}, u32[]{:S(2)}, u32[]{:S(2)}) collective-permute-start(f32[256,256]{1,0:T(8,128)S(1)} %get-tuple-element.99), channel_id=1, source_target_pairs={{0,0},{1,8},{2,2},{3,10},{4,4},{5,12},{6,6},{7,14},{8,1},{9,9},{10... | collective-permute-start | bytes 786440 | tf_op jit(solution)/shard_map/ppermute | solution.py:361
  106.7 1.0 collective-permute-start.20
  107.7 7.0 %collective-permute-done.18 = f32[1,3,64,256]{3,2,1,0:T(8,128)S(1)} collective-permute-done((f32[1,3,64,256]{3,2,1,0:T(8,128)S(1)}, f32[1,3,64,256]{3,2,1,0:T(8,128)S(1)}, u32[]{:S(2)}, u32[]{:S(2)}) %collective-permute-start.18) | collective-permute-done | bytes 196640 | tf_op jit(solution)/shard_map/ppermute | solution.py:349
  114.7 0.1 collective-permute-done.19.refs_0_
  114.9 3.7 %collective-permute-done.20.refs_1_ = f32[256,256]{1,0:T(8,128)S(1)} collective-permute-done((f32[256,256]{1,0:T(8,128)S(1)}, f32[256,256]{1,0:T(8,128)S(1)}, u32[]{:S(2)}, u32[]{:S(2)}) %collective-permute-start.20) | collective-permute-done | bytes 262176 | tf_op jit(solution)/shard_map/ppermute | solution.py:361
  118.6 3.7 %collective-permute-start.22 = (f32[256,256]{1,0:T(8,128)S(1)}, f32[256,256]{1,0:T(8,128)S(1)}, u32[]{:S(2)}, u32[]{:S(2)}) collective-permute-start(f32[256,256]{1,0:T(8,128)S(1)} %get-tuple-element.102), channel_id=1, source_target_pairs={{0,4},{1,12},{2,6},{3,14},{4,0},{5,8},{6,2},{7,10},{8,5},{9,13},{1... | collective-permute-start | bytes 786440 | tf_op jit(solution)/shard_map/ppermute | solution.py:361
  122.3 3.9 %collective-permute-done.21 = f32[1,3,64,256]{3,2,1,0:T(8,128)S(1)} collective-permute-done((f32[1,3,64,256]{3,2,1,0:T(8,128)S(1)}, f32[1,3,64,256]{3,2,1,0:T(8,128)S(1)}, u32[]{:S(2)}, u32[]{:S(2)}) %collective-permute-start.21) | collective-permute-done | bytes 196640 | tf_op jit(solution)/shard_map/ppermute | solution.py:349
  126.2 2.0 %collective-permute-done.22.refs_2_ = f32[256,256]{1,0:T(8,128)S(1)} collective-permute-done((f32[256,256]{1,0:T(8,128)S(1)}, f32[256,256]{1,0:T(8,128)S(1)}, u32[]{:S(2)}, u32[]{:S(2)}) %collective-permute-start.22) | collective-permute-done | bytes 262176 | tf_op jit(solution)/shard_map/ppermute | solution.py:361
  128.2 3.2 %collective-permute-done.23.refs_3_ = f32[256,256]{1,0:T(8,128)S(1)} collective-permute-done((f32[256,256]{1,0:T(8,128)S(1)}, f32[256,256]{1,0:T(8,128)S(1)}, u32[]{:S(2)}, u32[]{:S(2)}) %collective-permute-start.23) | collective-permute-done | bytes 262176 | tf_op jit(solution)/shard_map/ppermute | solution.py:361
  131.4 1.7 shard_map.150
  133.2 3.7 %shard_map.151 = (f32[2,256,256]{2,1,0:T(8,128)S(1)}, f32[2,256,256]{2,1,0:T(8,128)S(1)}, f32[2,256,256]{2,1,0:T(8,128)S(1)}, f32[2,256,256]{2,1,0:T(8,128)S(1)}...) custom-call(s32[2]{0:T(128)S(1)} %copy-done.2, ...), custom_call_target="tpu_custom_call" | custom-call | flops 2013265920 | bytes 6561800 | tf_op jit(solution)/shard_map/pallas_call | solution.py:40
  136.9 0.6 collective-permute-start.29
  137.4 2.3 %collective-permute-start.25 = (f32[2,256,256]{2,1,0:T(8,128)S(1)}, f32[2,256,256]{2,1,0:T(8,128)S(1)}, u32[]{:S(2)}, u32[]{:S(2)}) collective-permute-start(f32[2,256,256]{2,1,0:T(8,128)S(1)} %get-tuple-element.112), channel_id=1, source_target_pairs={{0,0},{1,8},{2,2},{3,10},{4,4},{5,12},{6,6},{7,14},{8,1},{9,9},{10... | collective-permute-start | bytes 1572872 | tf_op jit(solution)/shard_map/ppermute | solution.py:361
  139.7 2.0 %collective-permute-start.26 = (f32[2,256,256]{2,1,0:T(8,128)S(1)}, f32[2,256,256]{2,1,0:T(8,128)S(1)}, u32[]{:S(2)}, u32[]{:S(2)}) collective-permute-start(f32[2,256,256]{2,1,0:T(8,128)S(1)} %get-tuple-element.113), channel_id=1, source_target_pairs={{0,2},{1,10},{2,0},{3,8},{4,6},{5,14},{6,4},{7,12},{8,3},{9,11},{1... | collective-permute-start | bytes 1572872 | tf_op jit(solution)/shard_map/ppermute | solution.py:361
  141.7 0.7 collective-permute-start.27
  142.4 2.3 %collective-permute-start.28 = (f32[2,256,256]{2,1,0:T(8,128)S(1)}, f32[2,256,256]{2,1,0:T(8,128)S(1)}, u32[]{:S(2)}, u32[]{:S(2)}) collective-permute-start(f32[2,256,256]{2,1,0:T(8,128)S(1)} %get-tuple-element.115), channel_id=1, source_target_pairs={{0,6},{1,14},{2,4},{3,12},{4,2},{5,10},{6,0},{7,8},{8,7},{9,15},{1... | collective-permute-start | bytes 1572872 | tf_op jit(solution)/shard_map/ppermute | solution.py:361
  144.7 2.1 %collective-permute-start.30 = (f32[1,3,64,256]{3,2,1,0:T(8,128)S(1)}, f32[1,3,64,256]{3,2,1,0:T(8,128)S(1)}, u32[]{:S(2)}, u32[]{:S(2)}) collective-permute-start(f32[1,3,64,256]{3,2,1,0:T(8,128)S(1)} %slice_add_fusion), channel_id=1, source_target_pairs={{0,16},{2,18},{4,20},{6,22},{8,24},{10,26},{12,28},{14,30},{16,0},... | collective-permute-start | bytes 589832 | tf_op jit(solution)/shard_map/ppermute | solution.py:349
  146.8 22.4 %collective-permute-done.30 = f32[1,3,64,256]{3,2,1,0:T(8,128)S(1)} collective-permute-done((f32[1,3,64,256]{3,2,1,0:T(8,128)S(1)}, f32[1,3,64,256]{3,2,1,0:T(8,128)S(1)}, u32[]{:S(2)}, u32[]{:S(2)}) %collective-permute-start.30) | collective-permute-done | bytes 196640 | tf_op jit(solution)/shard_map/ppermute | solution.py:349
  169.2 0.6 shard_map.153
  169.8 6.0 %collective-permute-start.31 = (f32[3,16,256]{2,1,0:T(8,128)S(1)}, f32[3,16,256]{2,1,0:T(8,128)S(1)}, u32[]{:S(2)}, u32[]{:S(2)}) collective-permute-start(f32[3,16,256]{2,1,0:T(8,128)S(1)} %get-tuple-element.121), channel_id=1, source_target_pairs={{0,0},{1,8},{2,2},{3,10},{4,4},{5,12},{6,6},{7,14},{8,1},{9,9},{10... | collective-permute-start | bytes 147464 | tf_op jit(solution)/shard_map/ppermute | solution.py:361
  176.0 3.0 %collective-permute-start.33 = (f32[3,16,256]{2,1,0:T(8,128)S(1)}, f32[3,16,256]{2,1,0:T(8,128)S(1)}, u32[]{:S(2)}, u32[]{:S(2)}) collective-permute-start(f32[3,16,256]{2,1,0:T(8,128)S(1)} %get-tuple-element.123), channel_id=1, source_target_pairs={{0,4},{1,12},{2,6},{3,14},{4,0},{5,8},{6,2},{7,10},{8,5},{9,13},{1... | collective-permute-start | bytes 147464 | tf_op jit(solution)/shard_map/ppermute | solution.py:361
  179.0 0.6 collective-permute-start.34
  179.5 2.4 %shard_map.152 = (bf16[256,4,256]{2,1,0:T(4,128)(2,1)}, bf16[256,4,256]{2,1,0:T(4,128)(2,1)}) custom-call(s32[2]{0:T(128)S(1)} %copy-done.2, f32[4,256]{1,0:T(4,128)S(1)} %bitcast.13, f32[2,256,256]{2,1,0:T(8,128)S(1)} %collective-permute-done.25.refs_0_, f32[2,256,256]{2,1,0:T(8,128)S(1)} %collective-permute-done.26.refs_1_, ...), custom_call_target="tpu_custom_call" | custom-call | flops 16777216 | bytes 3149832 | tf_op jit(solution)/shard_map/pallas_call | solution.py:40
  182.0 2.3 %collective-permute-done.34.refs_3_ = f32[3,16,256]{2,1,0:T(8,128)S(1)} collective-permute-done((f32[3,16,256]{2,1,0:T(8,128)S(1)}, f32[3,16,256]{2,1,0:T(8,128)S(1)}, u32[]{:S(2)}, u32[]{:S(2)}) %collective-permute-start.34) | collective-permute-done | bytes 49184 | tf_op jit(solution)/shard_map/ppermute | solution.py:361
  184.3 1.2 shard_map.154
  (42 shorter events, 0.6 us)
Async XLA Ops:
  1.2 0.7 copy-start.6
  2.5 13.9 %copy-start = (bf16[1,256,4,256]{3,2,1,0:T(4,128)(2,1)S(1)}, bf16[1,256,4,256]{3,2,1,0:T(4,128)(2,1)}, u32[]{:S(2)}) copy-start(bf16[1,256,4,256]{3,2,1,0:T(4,128)(2,1)} %param.10) | copy-start | bytes 1572868
  2.5 13.9 %copy-start.1 = (bf16[1,256,4,256]{3,2,1,0:T(4,128)(2,1)S(1)}, bf16[1,256,4,256]{3,2,1,0:T(4,128)(2,1)}, u32[]{:S(2)}) copy-start(bf16[1,256,4,256]{3,2,1,0:T(4,128)(2,1)} %param.19) | copy-start | bytes 1572868
  6.9 11.6 %collective-permute-start = (f32[776,256]{1,0:T(8,128)}, f32[776,256]{1,0:T(8,128)}, u32[]{:S(2)}, u32[]{:S(2)}) collective-permute-start(f32[776,256]{1,0:T(8,128)} %get-tuple-element.67), channel_id=1, source_target_pairs={{0,1},{2,3},{4,5},{6,7},{9,8},{11,10},{13,12},{15,14},{16,17},{18,... | collective-permute-start | bytes 2383880 | tf_op jit(solution)/shard_map/ppermute | solution.py:391
  8.2 12.0 %collective-permute-start.1 = (f32[2,256,256]{2,1,0:T(8,128)}, f32[2,256,256]{2,1,0:T(8,128)S(1)}, u32[]{:S(2)}, u32[]{:S(2)}) collective-permute-start(f32[2,256,256]{2,1,0:T(8,128)} %get-tuple-element.68), channel_id=1, source_target_pairs={{0,0},{1,8},{2,2},{3,10},{4,4},{5,12},{6,6},{7,14},{8,1},{9,9},{10... | collective-permute-start | bytes 1572872 | tf_op jit(solution)/shard_map/ppermute | solution.py:361
  12.8 13.7 %collective-permute-start.2 = (f32[2,256,256]{2,1,0:T(8,128)}, f32[2,256,256]{2,1,0:T(8,128)S(1)}, u32[]{:S(2)}, u32[]{:S(2)}) collective-permute-start(f32[2,256,256]{2,1,0:T(8,128)} %get-tuple-element.69), channel_id=1, source_target_pairs={{0,2},{1,10},{2,0},{3,8},{4,6},{5,14},{6,4},{7,12},{8,3},{9,11},{1... | collective-permute-start | bytes 1572872 | tf_op jit(solution)/shard_map/ppermute | solution.py:361
  13.8 22.4 %collective-permute-start.3 = (f32[2,256,256]{2,1,0:T(8,128)}, f32[2,256,256]{2,1,0:T(8,128)S(1)}, u32[]{:S(2)}, u32[]{:S(2)}) collective-permute-start(f32[2,256,256]{2,1,0:T(8,128)} %get-tuple-element.70), channel_id=1, source_target_pairs={{0,4},{1,12},{2,6},{3,14},{4,0},{5,8},{6,2},{7,10},{8,5},{9,13},{1... | collective-permute-start | bytes 1572872 | tf_op jit(solution)/shard_map/ppermute | solution.py:361
  16.5 25.9 %collective-permute-start.4 = (f32[2,256,256]{2,1,0:T(8,128)}, f32[2,256,256]{2,1,0:T(8,128)S(1)}, u32[]{:S(2)}, u32[]{:S(2)}) collective-permute-start(f32[2,256,256]{2,1,0:T(8,128)} %get-tuple-element.71), channel_id=1, source_target_pairs={{0,6},{1,14},{2,4},{3,12},{4,2},{5,10},{6,0},{7,8},{8,7},{9,15},{1... | collective-permute-start | bytes 1572872 | tf_op jit(solution)/shard_map/ppermute | solution.py:361
  16.5 0.7 copy-start.4
  16.5 0.7 copy-start.2
  16.5 2.0 %copy-start.5 = (f32[776,256]{1,0:T(8,128)S(1)}, f32[776,256]{1,0:T(8,128)}, u32[]{:S(2)}) copy-start(f32[776,256]{1,0:T(8,128)} %get-tuple-element.67) | copy-start | bytes 2383876
  44.5 3.1 %collective-permute-start.5 = (f32[2,3,64,256]{3,2,1,0:T(8,128)S(1)}, f32[2,3,64,256]{3,2,1,0:T(8,128)S(1)}, u32[]{:S(2)}, u32[]{:S(2)}) collective-permute-start(f32[2,3,64,256]{3,2,1,0:T(8,128)S(1)} %get-tuple-element.80), channel_id=1, source_target_pairs={{0,1},{1,0},{2,3},{3,2},{4,5},{5,4},{6,7},{7,6},{8,9},{9,8},{10,11... | collective-permute-start | bytes 1179656 | tf_op jit(solution)/shard_map/ppermute | solution.py:349
  47.6 11.5 %collective-permute-start.6 = (f32[1,3,64,256]{3,2,1,0:T(8,128)S(1)}, f32[1,3,64,256]{3,2,1,0:T(8,128)S(1)}, u32[]{:S(2)}, u32[]{:S(2)}) collective-permute-start(f32[1,3,64,256]{3,2,1,0:T(8,128)S(1)} %slice_add_fusion.4), channel_id=1, source_target_pairs={{0,16},{2,18},{4,20},{6,22},{8,24},{10,26},{12,28},{14,30},{16,0},... | collective-permute-start | bytes 589832 | tf_op jit(solution)/shard_map/ppermute | solution.py:349
  50.0 32.3 %collective-permute-start.8 = (f32[2,256,256]{2,1,0:T(8,128)S(1)}, f32[2,256,256]{2,1,0:T(8,128)S(1)}, u32[]{:S(2)}, u32[]{:S(2)}) collective-permute-start(f32[2,256,256]{2,1,0:T(8,128)S(1)} %get-tuple-element.82), channel_id=1, source_target_pairs={{0,0},{1,8},{2,2},{3,10},{4,4},{5,12},{6,6},{7,14},{8,1},{9,9},{10... | collective-permute-start | bytes 1572872 | tf_op jit(solution)/shard_map/ppermute | solution.py:361
  53.0 29.2 %collective-permute-start.9 = (f32[2,256,256]{2,1,0:T(8,128)S(1)}, f32[2,256,256]{2,1,0:T(8,128)S(1)}, u32[]{:S(2)}, u32[]{:S(2)}) collective-permute-start(f32[2,256,256]{2,1,0:T(8,128)S(1)} %get-tuple-element.83), channel_id=1, source_target_pairs={{0,2},{1,10},{2,0},{3,8},{4,6},{5,14},{6,4},{7,12},{8,3},{9,11},{1... | collective-permute-start | bytes 1572872 | tf_op jit(solution)/shard_map/ppermute | solution.py:361
  54.6 27.6 %collective-permute-start.10 = (f32[2,256,256]{2,1,0:T(8,128)S(1)}, f32[2,256,256]{2,1,0:T(8,128)S(1)}, u32[]{:S(2)}, u32[]{:S(2)}) collective-permute-start(f32[2,256,256]{2,1,0:T(8,128)S(1)} %get-tuple-element.84), channel_id=1, source_target_pairs={{0,4},{1,12},{2,6},{3,14},{4,0},{5,8},{6,2},{7,10},{8,5},{9,13},{1... | collective-permute-start | bytes 1572872 | tf_op jit(solution)/shard_map/ppermute | solution.py:361
  55.7 30.2 %collective-permute-start.11 = (f32[2,256,256]{2,1,0:T(8,128)S(1)}, f32[2,256,256]{2,1,0:T(8,128)S(1)}, u32[]{:S(2)}, u32[]{:S(2)}) collective-permute-start(f32[2,256,256]{2,1,0:T(8,128)S(1)} %get-tuple-element.85), channel_id=1, source_target_pairs={{0,6},{1,14},{2,4},{3,12},{4,2},{5,10},{6,0},{7,8},{8,7},{9,15},{1... | collective-permute-start | bytes 1572872 | tf_op jit(solution)/shard_map/ppermute | solution.py:361
  59.2 23.0 %collective-permute-start.7 = (f32[1,3,64,256]{3,2,1,0:T(8,128)S(1)}, f32[1,3,64,256]{3,2,1,0:T(8,128)S(1)}, u32[]{:S(2)}, u32[]{:S(2)}) collective-permute-start(f32[1,3,64,256]{3,2,1,0:T(8,128)S(1)} %fusion.2), channel_id=1, source_target_pairs={{0,16},{2,18},{4,20},{6,22},{8,24},{10,26},{12,28},{14,30},{16,0},... | collective-permute-start | bytes 589832 | tf_op jit(solution)/shard_map/ppermute | solution.py:349
  85.9 1.7 collective-permute-start.12
  89.4 2.5 %collective-permute-start.13 = (f32[2,4,256]{2,1,0:T(4,128)S(1)}, f32[2,4,256]{2,1,0:T(4,128)S(1)}, u32[]{:S(2)}, u32[]{:S(2)}) collective-permute-start(f32[2,4,256]{2,1,0:T(4,128)S(1)} %get-tuple-element.91), channel_id=1, source_target_pairs={{0,8},{2,10},{4,12},{6,14},{8,0},{10,2},{12,4},{14,6},{16,24},{18,... | collective-permute-start | bytes 24584 | tf_op jit(solution)/shard_map/ppermute | solution.py:349
  91.9 3.4 %collective-permute-start.16 = (f32[2,4,256]{2,1,0:T(4,128)S(1)}, f32[2,4,256]{2,1,0:T(4,128)S(1)}, u32[]{:S(2)}, u32[]{:S(2)}) collective-permute-start(f32[2,4,256]{2,1,0:T(4,128)S(1)} %add.41.refs_4_), channel_id=1, source_target_pairs={{0,6},{2,4},{4,2},{6,0},{8,14},{10,12},{12,10},{14,8},{16,22},{18,... | collective-permute-start | bytes 24584 | tf_op jit(solution)/shard_map/ppermute | solution.py:349
  93.2 2.5 %collective-permute-start.15 = (f32[2,4,256]{2,1,0:T(4,128)S(1)}, f32[2,4,256]{2,1,0:T(4,128)S(1)}, u32[]{:S(2)}, u32[]{:S(2)}) collective-permute-start(f32[2,4,256]{2,1,0:T(4,128)S(1)} %add.41.refs_4_), channel_id=1, source_target_pairs={{0,4},{2,6},{4,0},{6,2},{8,12},{10,14},{12,8},{14,10},{16,20},{18,... | collective-permute-start | bytes 24584 | tf_op jit(solution)/shard_map/ppermute | solution.py:349
  93.4 2.5 %collective-permute-start.14 = (f32[2,4,256]{2,1,0:T(4,128)S(1)}, f32[2,4,256]{2,1,0:T(4,128)S(1)}, u32[]{:S(2)}, u32[]{:S(2)}) collective-permute-start(f32[2,4,256]{2,1,0:T(4,128)S(1)} %add.41.refs_4_), channel_id=1, source_target_pairs={{0,2},{2,0},{4,6},{6,4},{8,10},{10,8},{12,14},{14,12},{16,18},{18,... | collective-permute-start | bytes 24584 | tf_op jit(solution)/shard_map/ppermute | solution.py:349
  98.3 4.4 %collective-permute-start.17 = (f32[2,3,64,256]{3,2,1,0:T(8,128)S(1)}, f32[2,3,64,256]{3,2,1,0:T(8,128)S(1)}, u32[]{:S(2)}, u32[]{:S(2)}) collective-permute-start(f32[2,3,64,256]{3,2,1,0:T(8,128)S(1)} %get-tuple-element.97), channel_id=1, source_target_pairs={{0,1},{1,0},{2,3},{3,2},{4,5},{5,4},{6,7},{7,6},{8,9},{9,8},{10,11... | collective-permute-start | bytes 1179656 | tf_op jit(solution)/shard_map/ppermute | solution.py:349
  102.8 11.9 %collective-permute-start.18 = (f32[1,3,64,256]{3,2,1,0:T(8,128)S(1)}, f32[1,3,64,256]{3,2,1,0:T(8,128)S(1)}, u32[]{:S(2)}, u32[]{:S(2)}) collective-permute-start(f32[1,3,64,256]{3,2,1,0:T(8,128)S(1)} %slice_add_fusion.2), channel_id=1, source_target_pairs={{0,16},{2,18},{4,20},{6,22},{8,24},{10,26},{12,28},{14,30},{16,0},... | collective-permute-start | bytes 589832 | tf_op jit(solution)/shard_map/ppermute | solution.py:349
  103.0 11.9 %collective-permute-start.19 = (f32[256,256]{1,0:T(8,128)S(1)}, f32[256,256]{1,0:T(8,128)S(1)}, u32[]{:S(2)}, u32[]{:S(2)}) collective-permute-start(f32[256,256]{1,0:T(8,128)S(1)} %get-tuple-element.99), channel_id=1, source_target_pairs={{0,0},{1,8},{2,2},{3,10},{4,4},{5,12},{6,6},{7,14},{8,1},{9,9},{10... | collective-permute-start | bytes 786440 | tf_op jit(solution)/shard_map/ppermute | solution.py:361
  106.7 11.8 %collective-permute-start.20 = (f32[256,256]{1,0:T(8,128)S(1)}, f32[256,256]{1,0:T(8,128)S(1)}, u32[]{:S(2)}, u32[]{:S(2)}) collective-permute-start(f32[256,256]{1,0:T(8,128)S(1)} %get-tuple-element.100), channel_id=1, source_target_pairs={{0,2},{1,10},{2,0},{3,8},{4,6},{5,14},{6,4},{7,12},{8,3},{9,11},{1... | collective-permute-start | bytes 786440 | tf_op jit(solution)/shard_map/ppermute | solution.py:361
  118.5 7.6 %collective-permute-start.21 = (f32[1,3,64,256]{3,2,1,0:T(8,128)S(1)}, f32[1,3,64,256]{3,2,1,0:T(8,128)S(1)}, u32[]{:S(2)}, u32[]{:S(2)}) collective-permute-start(f32[1,3,64,256]{3,2,1,0:T(8,128)S(1)} %fusion.1.refs_0_), channel_id=1, source_target_pairs={{0,16},{2,18},{4,20},{6,22},{8,24},{10,26},{12,28},{14,30},{16,0},... | collective-permute-start | bytes 589832 | tf_op jit(solution)/shard_map/ppermute | solution.py:349
  118.6 9.7 %collective-permute-start.22 = (f32[256,256]{1,0:T(8,128)S(1)}, f32[256,256]{1,0:T(8,128)S(1)}, u32[]{:S(2)}, u32[]{:S(2)}) collective-permute-start(f32[256,256]{1,0:T(8,128)S(1)} %get-tuple-element.102), channel_id=1, source_target_pairs={{0,4},{1,12},{2,6},{3,14},{4,0},{5,8},{6,2},{7,10},{8,5},{9,13},{1... | collective-permute-start | bytes 786440 | tf_op jit(solution)/shard_map/ppermute | solution.py:361
  122.3 9.2 %collective-permute-start.23 = (f32[256,256]{1,0:T(8,128)S(1)}, f32[256,256]{1,0:T(8,128)S(1)}, u32[]{:S(2)}, u32[]{:S(2)}) collective-permute-start(f32[256,256]{1,0:T(8,128)S(1)} %get-tuple-element.103), channel_id=1, source_target_pairs={{0,6},{1,14},{2,4},{3,12},{4,2},{5,10},{6,0},{7,8},{8,7},{9,15},{1... | collective-permute-start | bytes 786440 | tf_op jit(solution)/shard_map/ppermute | solution.py:361
  131.4 1.7 collective-permute-start.24
  136.9 7.8 %collective-permute-start.29 = (f32[2,3,64,256]{3,2,1,0:T(8,128)S(1)}, f32[2,3,64,256]{3,2,1,0:T(8,128)S(1)}, u32[]{:S(2)}, u32[]{:S(2)}) collective-permute-start(f32[2,3,64,256]{3,2,1,0:T(8,128)S(1)} %get-tuple-element.119), channel_id=1, source_target_pairs={{0,1},{1,0},{2,3},{3,2},{4,5},{5,4},{6,7},{7,6},{8,9},{9,8},{10,11... | collective-permute-start | bytes 1179656 | tf_op jit(solution)/shard_map/ppermute | solution.py:349
  137.4 38.4 %collective-permute-start.25 = (f32[2,256,256]{2,1,0:T(8,128)S(1)}, f32[2,256,256]{2,1,0:T(8,128)S(1)}, u32[]{:S(2)}, u32[]{:S(2)}) collective-permute-start(f32[2,256,256]{2,1,0:T(8,128)S(1)} %get-tuple-element.112), channel_id=1, source_target_pairs={{0,0},{1,8},{2,2},{3,10},{4,4},{5,12},{6,6},{7,14},{8,1},{9,9},{10... | collective-permute-start | bytes 1572872 | tf_op jit(solution)/shard_map/ppermute | solution.py:361
  139.7 36.3 %collective-permute-start.26 = (f32[2,256,256]{2,1,0:T(8,128)S(1)}, f32[2,256,256]{2,1,0:T(8,128)S(1)}, u32[]{:S(2)}, u32[]{:S(2)}) collective-permute-start(f32[2,256,256]{2,1,0:T(8,128)S(1)} %get-tuple-element.113), channel_id=1, source_target_pairs={{0,2},{1,10},{2,0},{3,8},{4,6},{5,14},{6,4},{7,12},{8,3},{9,11},{1... | collective-permute-start | bytes 1572872 | tf_op jit(solution)/shard_map/ppermute | solution.py:361
  141.7 37.3 %collective-permute-start.27 = (f32[2,256,256]{2,1,0:T(8,128)S(1)}, f32[2,256,256]{2,1,0:T(8,128)S(1)}, u32[]{:S(2)}, u32[]{:S(2)}) collective-permute-start(f32[2,256,256]{2,1,0:T(8,128)S(1)} %get-tuple-element.114), channel_id=1, source_target_pairs={{0,4},{1,12},{2,6},{3,14},{4,0},{5,8},{6,2},{7,10},{8,5},{9,13},{1... | collective-permute-start | bytes 1572872 | tf_op jit(solution)/shard_map/ppermute | solution.py:361
  142.4 37.1 %collective-permute-start.28 = (f32[2,256,256]{2,1,0:T(8,128)S(1)}, f32[2,256,256]{2,1,0:T(8,128)S(1)}, u32[]{:S(2)}, u32[]{:S(2)}) collective-permute-start(f32[2,256,256]{2,1,0:T(8,128)S(1)} %get-tuple-element.115), channel_id=1, source_target_pairs={{0,6},{1,14},{2,4},{3,12},{4,2},{5,10},{6,0},{7,8},{8,7},{9,15},{1... | collective-permute-start | bytes 1572872 | tf_op jit(solution)/shard_map/ppermute | solution.py:361
  144.7 24.5 %collective-permute-start.30 = (f32[1,3,64,256]{3,2,1,0:T(8,128)S(1)}, f32[1,3,64,256]{3,2,1,0:T(8,128)S(1)}, u32[]{:S(2)}, u32[]{:S(2)}) collective-permute-start(f32[1,3,64,256]{3,2,1,0:T(8,128)S(1)} %slice_add_fusion), channel_id=1, source_target_pairs={{0,16},{2,18},{4,20},{6,22},{8,24},{10,26},{12,28},{14,30},{16,0},... | collective-permute-start | bytes 589832 | tf_op jit(solution)/shard_map/ppermute | solution.py:349
  169.8 9.7 %copy-start.3 = (f32[1,4,256]{2,1,0:T(4,128)S(1)}, f32[1,4,256]{2,1,0:T(4,128)}, u32[]{:S(2)}) copy-start(f32[1,4,256]{2,1,0:T(4,128)} %param.13) | copy-start | bytes 12292
  169.8 12.1 %collective-permute-start.31 = (f32[3,16,256]{2,1,0:T(8,128)S(1)}, f32[3,16,256]{2,1,0:T(8,128)S(1)}, u32[]{:S(2)}, u32[]{:S(2)}) collective-permute-start(f32[3,16,256]{2,1,0:T(8,128)S(1)} %get-tuple-element.121), channel_id=1, source_target_pairs={{0,0},{1,8},{2,2},{3,10},{4,4},{5,12},{6,6},{7,14},{8,1},{9,9},{10... | collective-permute-start | bytes 147464 | tf_op jit(solution)/shard_map/ppermute | solution.py:361
  175.9 6.0 %collective-permute-start.32 = (f32[3,16,256]{2,1,0:T(8,128)S(1)}, f32[3,16,256]{2,1,0:T(8,128)S(1)}, u32[]{:S(2)}, u32[]{:S(2)}) collective-permute-start(f32[3,16,256]{2,1,0:T(8,128)S(1)} %get-tuple-element.122), channel_id=1, source_target_pairs={{0,2},{1,10},{2,0},{3,8},{4,6},{5,14},{6,4},{7,12},{8,3},{9,11},{1... | collective-permute-start | bytes 147464 | tf_op jit(solution)/shard_map/ppermute | solution.py:361
  176.0 5.9 %collective-permute-start.33 = (f32[3,16,256]{2,1,0:T(8,128)S(1)}, f32[3,16,256]{2,1,0:T(8,128)S(1)}, u32[]{:S(2)}, u32[]{:S(2)}) collective-permute-start(f32[3,16,256]{2,1,0:T(8,128)S(1)} %get-tuple-element.123), channel_id=1, source_target_pairs={{0,4},{1,12},{2,6},{3,14},{4,0},{5,8},{6,2},{7,10},{8,5},{9,13},{1... | collective-permute-start | bytes 147464 | tf_op jit(solution)/shard_map/ppermute | solution.py:361
  179.0 5.3 %collective-permute-start.34 = (f32[3,16,256]{2,1,0:T(8,128)S(1)}, f32[3,16,256]{2,1,0:T(8,128)S(1)}, u32[]{:S(2)}, u32[]{:S(2)}) collective-permute-start(f32[3,16,256]{2,1,0:T(8,128)S(1)} %get-tuple-element.124), channel_id=1, source_target_pairs={{0,6},{1,14},{2,4},{3,12},{4,2},{5,10},{6,0},{7,8},{8,7},{9,15},{1... | collective-permute-start | bytes 147464 | tf_op jit(solution)/shard_map/ppermute | solution.py:361

commit v5 on v3

--- a/solution.py
+++ b/solution.py
@@ -96,15 +96,25 @@
         out[...] = sums[:, pl.ds(at, rows), :]
 
 
-def update_kernel(groups, depth, scale, place, *refs):
-    keys_in, scaled_in = refs[:groups], refs[groups : 2 * groups]
-    w_gate, w_out, w_up = refs[2 * groups : 2 * groups + 3]
-    outs, sums = refs[2 * groups + 3 : -1], refs[-1]
+def merge(own, early, late, kept):
+    kept[0] = own[...].astype(BF16)
+    for step, (one, two) in enumerate(zip(early, late)):
+        kept[step + 1] = (one[...] + two[...]).astype(BF16)
+
+
+def update_kernel(groups, depth, scale, place, mark, *refs):
+    each = 2 * groups - 1
+    keys_in, scaled_in = refs[:each], refs[each : 2 * each]
+    w_gate, w_out, w_up = refs[2 * each : 2 * each + 3]
+    key_kept, scaled_kept = refs[2 * each + 3 : 2 * each + 5]
+    outs, sums = refs[2 * each + 5 : -1], refs[-1]
     gate_b, out_b, up_b = (w[...].astype(BF16) for w in (w_gate, w_out, w_up))
+    merge(keys_in[0], keys_in[1:groups], keys_in[groups:], key_kept)
+    merge(scaled_in[0], scaled_in[1:groups], scaled_in[groups:], scaled_kept)
     total = [0.0, 0.0, 0.0]
-    for key, value in zip(keys_in, scaled_in):
-        keys = key[...].astype(BF16)
-        scaled = value[...].astype(BF16)
+    for step in range(groups):
+        keys = key_kept[step]
+        scaled = scaled_kept[step]
         first = mm(keys, gate_b)
         third = mm(keys, up_b)
         sig = jax.nn.sigmoid(first)
@@ -204,11 +214,11 @@
     return sets
 
 
-def update_back_kernel(groups, depth, scale, place, *refs):
-    keys_in, scaled_in = refs[:groups], refs[groups : 2 * groups]
-    parts = refs[2 * groups : 2 * groups + depth]
-    w_gate, w_out, w_up = refs[2 * groups + depth : 2 * groups + depth + 3]
-    base = 2 * groups + depth + 3
+def update_back_kernel(groups, depth, scale, place, mark, *refs):
+    keys_in, scaled_in = refs[:2]
+    parts = refs[2 : depth + 2]
+    w_gate, w_out, w_up = refs[depth + 2 : depth + 5]
+    base = depth + 5
     outs = refs[base : base + groups]
     slices = refs[base + groups : -2]
     whole, sums = refs[-2:]
@@ -217,8 +227,8 @@
     cot_gate, cot_out, cot_up = ((whole[i] * scale).astype(BF16) for i in range(3))
     total = [0.0, 0.0, 0.0]
     for step in range(groups):
-        keys = keys_in[step][...].astype(BF16)
-        scaled = scaled_in[step][...].astype(BF16)
+        keys = keys_in[step]
+        scaled = scaled_in[step]
         first = mm(keys, gate_b)
         third = mm(keys, up_b)
         sig = jax.nn.sigmoid(first)
@@ -310,6 +320,29 @@
     def move(x, axis, step):
         return lax.ppermute(x, axis, [(c, c ^ step) for c in range(lax.axis_size(axis))])
 
+    blocks = lax.axis_size("head")
+    half = max(blocks // 2, 1)
+
+    def half_move(x, step, late):
+        heads_of = range(half, blocks) if late else range(half)
+        pairs = [(c * blocks + b, (c ^ step) * blocks + b) for c in range(ctx) for b in heads_of]
+        return lax.ppermute(x, ("ctx", "head"), pairs)
+
+    def tell(early, x):
+        early = lax.optimization_barrier(early)
+        mark = jax.tree.leaves(early)[-1][..., :8, :LANES].reshape(-1, LANES)[:8]
+        if blocks < 2:
+            return early, mark, x
+        pairs = [
+            (c * blocks + b, c * blocks + b + half) for c in range(ctx) for b in range(blocks - half)
+        ]
+        return early, *after(lax.ppermute(mark, ("ctx", "head"), pairs), x)
+
+    def half_plane(parts, late):
+        if late and blocks < 2:
+            return [jnp.zeros_like(p) for p in parts[1:]]
+        return [half_move(p, step, late) for step, p in enumerate(parts) if step]
+
     def in_plane(parts):
         return [parts[0]] + [move(p, "ctx", step) for step, p in enumerate(parts) if step]
 
@@ -332,22 +365,27 @@
     def split(body, *args):
         return call(functools.partial(body, groups), pieces, [scratch], flops // 16, place, *args)
 
-    k_in = in_plane(split(split_kernel, keys[0]))
-    s_in = in_plane(split(split_scaled_kernel, values[0], rates[0]))
+    k_out = split(split_kernel, keys[0])
+    k_early = half_plane(k_out, False)
+    s_out = split(split_scaled_kernel, values[0], rates[0])
+    s_early = half_plane(s_out, False)
+    (k_early, s_early), first_mark, (k_late, s_late) = tell((k_early, s_early), (k_out, s_out))
+    k_late, s_late = half_plane(k_late, True), half_plane(s_late, True)
     own = [lax.dynamic_index_in_dim(w, mine, 0, keepdims=False) for w in (w_gate, w_out, w_up)]
     own_scale = lax.dynamic_index_in_dim(head_scale, mine, 0, keepdims=True)[None, :]
     q_out = call(
         functools.partial(split_apply_kernel, groups), [shape(2, tokens, width)] * groups,
         [scratch], flops // 8, place, queries[0], cotangent[0], gain,
     )
-    k_in, s_in, q_out = after(k_in, s_in, q_out)
-    terms = call(
-        functools.partial(update_kernel, groups, depth, scale), slices, [square], 6 * flops,
-        place, *k_in, *s_in, *own,
-    )
+    kept_b = shape(groups, tokens, width, dtype=BF16)
+    out = call(
+        functools.partial(update_kernel, groups, depth, scale), [kept_b] * 2 + slices, [square],
+        6 * flops, place, first_mark, k_out[0], *k_early, *k_late, s_out[0], *s_early, *s_late, *own,
+    )
+    k_in, s_in, terms = out[0], out[1], out[2:]
+    new = functools.reduce(jnp.add, in_column(terms))
+    new, q_out = after(new, q_out)
     q_in = in_plane(q_out)
-    new = functools.reduce(jnp.add, in_column(terms))
-    new, q_in[:-1] = after(new, q_in[:-1])
     new = in_column([new] * depth)
     kept = shape(groups, tokens, width)
     first, third, scaled, new_b, stats = call(
@@ -365,20 +403,26 @@
         place, own_scale, *q_in, *in_plane([stats] * groups),
         first, third, scaled, new_b,
     )
-    part = functools.reduce(jnp.add, in_column(out[groups:]))
-    part, q_back = after(part, in_plane(out[:groups]))
+    q_back = in_plane(out[:groups])
+    parts = out[groups:]
+    early = [half_move(p, i * groups, False) for i, p in enumerate(parts) if i]
+    early, second_mark, later = tell(early, parts[1:])
+    if blocks > 1:
+        early += [half_move(p, (i + 1) * groups, True) for i, p in enumerate(later)]
+    part = functools.reduce(jnp.add, [parts[0]] + early)
     parts = in_column([part] * depth)
     (grad_q,) = call(
         functools.partial(join_query_kernel, groups), [joined], [scratch], flops // 16,
         place, *q_back,
     )
+    parts, grad_q = after(parts, grad_q)
     rows = hidden // depth
     sets = halving_order(depth)
     out = call(
         functools.partial(update_back_kernel, groups, depth, scale),
         [shape(2, tokens, width)] * groups
         + [shape(len(members), 3, rows, width) for members in sets + [[0]]],
-        [square] * 2, 15 * flops, place, *k_in, *s_in, *parts, *own,
+        [square] * 2, 15 * flops, place, second_mark, k_in, s_in, *parts, *own,
     )
     back = in_plane(out[:groups])
     ends, rest = list(out[groups:-1]), [part, out[-1]]

time: 159 us -> 188 us (1.18); the launches traced: 158 us -> 185 us
  starting transfers between devices: 49.8 us -> 88.3 us
  waiting for transfers between devices: 80 us -> 69.3 us
    ppermute x0 -> x20, starting transfers between devices: none -> 41.9 us  [the longest x18 39.3 us: half_move(): return lax.ppermute(x, ('ctx', 'head'), pairs)]
    ppermute x36 -> x27, waiting for transfers between devices: 80 us -> 53.2 us  [move(): lax.ppermute(x, axis, [(c, c ^ step) for c in range(lax.axis_size(axis))])]
    ppermute x0 -> x20, waiting for transfers between devices: none -> 16.1 us  [the longest x18 14.5 us: half_move(): return lax.ppermute(x, ('ctx', 'head'), pairs)]
    ppermute x36 -> x27, starting transfers between devices: 49.8 us -> 46.5 us  [move(): lax.ppermute(x, axis, [(c, c ^ step) for c in range(lax.axis_size(axis))])]
  transfers between devices with their start and end apart: 36 -> 47, of which waited for: 20 -> 21; matrix products, arithmetic and copies ran while one was open for 1% -> 1% of each run, Pallas kernels for 7% -> 4%
where the time goes in v5:
time: 188 us; the launch traced here: 185 us
  starting transfers between devices  88.3 us (47%)
  waiting for transfers between devices  69.3 us (37%)
  Pallas kernels  23.1 us (12%)
  local copies, waits for them, and re-layouts  2.83 us (2%)
    ppermute x27, waiting for transfers between devices, move(): lax.ppermute(x, axis, [(c, c ^ step) for c in range(lax.axis_size(axis))])  53.2 us
    ppermute x27, starting transfers between devices, move(): lax.ppermute(x, axis, [(c, c ^ step) for c in range(lax.axis_size(axis))])  46.5 us
    ppermute x18, starting transfers between devices, half_move(): return lax.ppermute(x, ('ctx', 'head'), pairs)  39.3 us
    pallas_call x11, Pallas kernels, call(): pl.pallas_call(body, out_shape=out_shape, in_specs=[smem if a.dtype == jn...  23.1 us
    ppermute x18, waiting for transfers between devices, half_move(): return lax.ppermute(x, ('ctx', 'head'), pairs)  14.5 us
  transfers between devices with their start and end apart: 47, of which 21 were waited for; matrix products, arithmetic and copies ran while one was open for 1% of the time, Pallas kernels for 4%

profile of v5, /device:TPU:0, one launch (start us, length us, event | category | flops | bytes accessed | tf_op | source)
XLA Modules:
  0.0 184.8 jit_solution(14660114714264765562)
XLA Ops:
  0.7 1.1 copy-done.1
  1.8 1.7 shard_map.145
  3.5 5.0 %collective-permute-start = (f32[256,256]{1,0:T(8,128)S(1)}, f32[256,256]{1,0:T(8,128)S(1)}, u32[]{:S(2)}, u32[]{:S(2)}) collective-permute-start(f32[256,256]{1,0:T(8,128)S(1)} %get-tuple-element.96), channel_id=1, source_target_pairs={{0,2},{2,0},{4,6},{6,4},{8,10},{10,8},{12,14},{14,12},{16,18},{18,... | collective-permute-start | bytes 786440 | tf_op jit(solution)/shard_map/ppermute | solution.py:329
  8.5 3.4 %collective-permute-start.1 = (f32[256,256]{1,0:T(8,128)}, f32[256,256]{1,0:T(8,128)S(1)}, u32[]{:S(2)}, u32[]{:S(2)}) collective-permute-start(f32[256,256]{1,0:T(8,128)} %get-tuple-element.97), channel_id=1, source_target_pairs={{0,4},{2,6},{4,0},{6,2},{8,12},{10,14},{12,8},{14,10},{16,20},{18,... | collective-permute-start | bytes 786440 | tf_op jit(solution)/shard_map/ppermute | solution.py:329
  11.9 1.9 %collective-permute-start.2 = (f32[256,256]{1,0:T(8,128)}, f32[256,256]{1,0:T(8,128)S(1)}, u32[]{:S(2)}, u32[]{:S(2)}) collective-permute-start(f32[256,256]{1,0:T(8,128)} %get-tuple-element.98), channel_id=1, source_target_pairs={{0,6},{2,4},{4,2},{6,0},{8,14},{10,12},{12,10},{14,8},{16,22},{18,... | collective-permute-start | bytes 786440 | tf_op jit(solution)/shard_map/ppermute | solution.py:329
  13.9 1.9 %shard_map.146 = (f32[256,256]{1,0:T(8,128)S(1)}, f32[256,256]{1,0:T(8,128)}, f32[256,256]{1,0:T(8,128)}, f32[256,256]{1,0:T(8,128)}) custom-call(s32[2]{0:T(128)S(1)} %pad_add_fusion.place, bf16[256,4,256]{2,1,0:T(4,128)(2,1)S(1)} %bitcast.20, f32[4,256]{1,0:T(4,128)S(1)} %bitcast.23), custom_call_target="tpu_custom_call" | custom-call | flops 8388608 | bytes 1576968 | tf_op jit(solution)/shard_map/pallas_call | solution.py:34
  15.8 3.9 %collective-permute-start.3 = (f32[256,256]{1,0:T(8,128)}, f32[256,256]{1,0:T(8,128)S(1)}, u32[]{:S(2)}, u32[]{:S(2)}) collective-permute-start(f32[256,256]{1,0:T(8,128)} %get-tuple-element.101), channel_id=1, source_target_pairs={{0,2},{2,0},{4,6},{6,4},{8,10},{10,8},{12,14},{14,12},{16,18},{18,... | collective-permute-start | bytes 786440 | tf_op jit(solution)/shard_map/ppermute | solution.py:329
  19.7 3.4 %collective-permute-start.4 = (f32[256,256]{1,0:T(8,128)}, f32[256,256]{1,0:T(8,128)S(1)}, u32[]{:S(2)}, u32[]{:S(2)}) collective-permute-start(f32[256,256]{1,0:T(8,128)} %get-tuple-element.102), channel_id=1, source_target_pairs={{0,4},{2,6},{4,0},{6,2},{8,12},{10,14},{12,8},{14,10},{16,20},{18,... | collective-permute-start | bytes 786440 | tf_op jit(solution)/shard_map/ppermute | solution.py:329
  23.1 1.9 %collective-permute-start.5 = (f32[256,256]{1,0:T(8,128)}, f32[256,256]{1,0:T(8,128)S(1)}, u32[]{:S(2)}, u32[]{:S(2)}) collective-permute-start(f32[256,256]{1,0:T(8,128)} %get-tuple-element.103), channel_id=1, source_target_pairs={{0,6},{2,4},{4,2},{6,0},{8,14},{10,12},{12,10},{14,8},{16,22},{18,... | collective-permute-start | bytes 786440 | tf_op jit(solution)/shard_map/ppermute | solution.py:329
  25.1 3.1 %collective-permute-done.4.refs_9_ = f32[256,256]{1,0:T(8,128)S(1)} collective-permute-done((f32[256,256]{1,0:T(8,128)}, f32[256,256]{1,0:T(8,128)S(1)}, u32[]{:S(2)}, u32[]{:S(2)}) %collective-permute-start.4) | collective-permute-done | bytes 262176 | tf_op jit(solution)/shard_map/ppermute | solution.py:329
  28.1 4.3 %collective-permute-done.5.refs_10_ = f32[256,256]{1,0:T(8,128)S(1)} collective-permute-done((f32[256,256]{1,0:T(8,128)}, f32[256,256]{1,0:T(8,128)S(1)}, u32[]{:S(2)}, u32[]{:S(2)}) %collective-permute-start.5) | collective-permute-done | bytes 262176 | tf_op jit(solution)/shard_map/ppermute | solution.py:329
  32.5 1.3 collective-permute-start.6
  33.8 0.8 collective-permute-done.6.mark
  35.2 1.4 collective-permute-start.8
  36.6 1.4 collective-permute-start.9
  38.0 1.4 collective-permute-start.10
  39.3 1.4 collective-permute-start.11
  40.7 1.4 collective-permute-start.12
  42.1 1.1 dynamic-slice_bitcast_fusion
  43.3 3.0 %shard_map.147 = (bf16[4,256,256]{2,1,0:T(8,128)(2,1)S(1)}, bf16[4,256,256]{2,1,0:T(8,128)(2,1)S(1)}, f32[3,64,256]{2,1,0:T(8,128)S(1)}, f32[3,64,256]{2,1,0:T(8...) custom-call(s32[2]{0:T(128)S(1)} %pad_add_fusion.place, f32[8,128]{1,0:T(8,128)S(1)} %collective-permute-done.6.mark, ...), custom_call_target="tpu_custom_call" | custom-call | flops 805306368 | bytes 6295560 | tf_op jit(solution)/shard_map/pallas_call | solution.py:34
  46.3 1.6 collective-permute-start.13
  47.9 2.6 %collective-permute-start.14 = (f32[3,64,256]{2,1,0:T(8,128)S(1)}, f32[3,64,256]{2,1,0:T(8,128)S(1)}, u32[]{:S(2)}, u32[]{:S(2)}) collective-permute-start(f32[3,64,256]{2,1,0:T(8,128)S(1)} %get-tuple-element.106), channel_id=1, source_target_pairs={{0,16},{2,18},{4,20},{6,22},{8,24},{10,26},{12,28},{14,30},{16,0},... | collective-permute-start | bytes 589832 | tf_op jit(solution)/shard_map/ppermute | solution.py:321
  50.8 1.3 shard_map.148
  52.1 6.7 %collective-permute-done.14 = f32[3,64,256]{2,1,0:T(8,128)S(1)} collective-permute-done((f32[3,64,256]{2,1,0:T(8,128)S(1)}, f32[3,64,256]{2,1,0:T(8,128)S(1)}, u32[]{:S(2)}, u32[]{:S(2)}) %collective-permute-start.14) | collective-permute-done | bytes 196640 | tf_op jit(solution)/shard_map/ppermute | solution.py:321
  59.9 2.4 %collective-permute-start.18 = (f32[2,256,256]{2,1,0:T(8,128)S(1)}, f32[2,256,256]{2,1,0:T(8,128)S(1)}, u32[]{:S(2)}, u32[]{:S(2)}) collective-permute-start(f32[2,256,256]{2,1,0:T(8,128)S(1)} %get-tuple-element.115), channel_id=1, source_target_pairs={{0,6},{2,4},{4,2},{6,0},{8,14},{10,12},{12,10},{14,8},{16,22},{18,... | collective-permute-start | bytes 1572872 | tf_op jit(solution)/shard_map/ppermute | solution.py:321
  62.4 2.5 %collective-permute-start.21 = (f32[3,64,256]{2,1,0:T(8,128)S(1)}, f32[3,64,256]{2,1,0:T(8,128)S(1)}, u32[]{:S(2)}, u32[]{:S(2)}) collective-permute-start(f32[3,64,256]{2,1,0:T(8,128)S(1)} %add_add_fusion.1.refs_4_), channel_id=1, source_target_pairs={{0,24},{2,26},{4,28},{6,30},{8,16},{10,18},{12,20},{14,22},{16,8},... | collective-permute-start | bytes 589832 | tf_op jit(solution)/shard_map/ppermute | solution.py:321
  64.9 1.6 collective-permute-start.20
  66.5 5.6 %collective-permute-done.21.refs_7_ = f32[3,64,256]{2,1,0:T(8,128)S(1)} collective-permute-done((f32[3,64,256]{2,1,0:T(8,128)S(1)}, f32[3,64,256]{2,1,0:T(8,128)S(1)}, u32[]{:S(2)}, u32[]{:S(2)}) %collective-permute-start.21) | collective-permute-done | bytes 196640 | tf_op jit(solution)/shard_map/ppermute | solution.py:321
  72.1 7.1 %collective-permute-start.19 = (f32[3,64,256]{2,1,0:T(8,128)S(1)}, f32[3,64,256]{2,1,0:T(8,128)S(1)}, u32[]{:S(2)}, u32[]{:S(2)}) collective-permute-start(f32[3,64,256]{2,1,0:T(8,128)S(1)} %add_add_fusion.1.refs_4_), channel_id=1, source_target_pairs={{0,8},{2,10},{4,12},{6,14},{8,0},{10,2},{12,4},{14,6},{16,24},{18,... | collective-permute-start | bytes 589832 | tf_op jit(solution)/shard_map/ppermute | solution.py:321
  79.8 1.1 collective-permute-done.20.refs_6_
  80.9 4.2 %collective-permute-done.19.refs_5_ = f32[3,64,256]{2,1,0:T(8,128)S(1)} collective-permute-done((f32[3,64,256]{2,1,0:T(8,128)S(1)}, f32[3,64,256]{2,1,0:T(8,128)S(1)}, u32[]{:S(2)}, u32[]{:S(2)}) %collective-permute-start.19) | collective-permute-done | bytes 196640 | tf_op jit(solution)/shard_map/ppermute | solution.py:321
  85.0 2.3 %shard_map.149 = (f32[4,256,256]{2,1,0:T(8,128)S(1)}, f32[4,256,256]{2,1,0:T(8,128)S(1)}, f32[4,256,256]{2,1,0:T(8,128)S(1)}, bf16[3,256,256]{2,1,0:T(8,128)(2,1)S(1)}, f32[2,4,256]{2,1,0:T(4,128)S(1)}) custom-call(s32[2]{0:T(128)S(1)} %pad_add_fusion.place, f32[1,1]{1,0:T(1,128)} %bitcast.2.head_scale, f32[2,256,256]{2,1,0:T(8,128)S(1)} %get-tuple-element.112.refs_0_, ...), custom_call_target="tpu_custom_call" | custom-call | flops 402653184 | bytes 6430732 | tf_op jit(solution)/shard_map/pallas_call | solution.py:34
  87.4 8.1 %collective-permute-start.22 = (f32[2,4,256]{2,1,0:T(4,128)S(1)}, f32[2,4,256]{2,1,0:T(4,128)S(1)}, u32[]{:S(2)}, u32[]{:S(2)}) collective-permute-start(f32[2,4,256]{2,1,0:T(4,128)S(1)} %get-tuple-element.117), channel_id=1, source_target_pairs={{0,1},{1,0},{2,3},{3,2},{4,5},{5,4},{6,7},{7,6},{8,9},{9,8},{10,11... | collective-permute-start | bytes 24584 | tf_op jit(solution)/shard_map/ppermute | solution.py:321
  95.5 0.8 collective-permute-done.22
  96.4 2.4 %collective-permute-start.25 = (f32[2,4,256]{2,1,0:T(4,128)S(1)}, f32[2,4,256]{2,1,0:T(4,128)S(1)}, u32[]{:S(2)}, u32[]{:S(2)}) collective-permute-start(f32[2,4,256]{2,1,0:T(4,128)S(1)} %add.45.refs_4_), channel_id=1, source_target_pairs={{0,6},{2,4},{4,2},{6,0},{8,14},{10,12},{12,10},{14,8},{16,22},{18,... | collective-permute-start | bytes 24584 | tf_op jit(solution)/shard_map/ppermute | solution.py:321
  99.8 1.1 collective-permute-done.25.refs_7_
  100.9 1.5 collective-permute-done.24.refs_6_
  103.0 3.1 %shard_map.150 = (f32[256,256]{1,0:T(8,128)S(1)}, f32[256,256]{1,0:T(8,128)S(1)}, f32[256,256]{1,0:T(8,128)S(1)}, f32[256,256]{1,0:T(8,128)S(1)}, f32[3,64,256]{...) custom-call(s32[2]{0:T(128)S(1)} %pad_add_fusion.place, ...), custom_call_target="tpu_custom_call" | custom-call | flops 805306368 | bytes 7503884 | tf_op jit(solution)/shard_map/pallas_call | solution.py:34
  106.1 3.0 %collective-permute-start.26 = (f32[3,64,256]{2,1,0:T(8,128)S(1)}, f32[3,64,256]{2,1,0:T(8,128)S(1)}, u32[]{:S(2)}, u32[]{:S(2)}) collective-permute-start(f32[3,64,256]{2,1,0:T(8,128)S(1)} %get-tuple-element.129), channel_id=1, source_target_pairs={{0,8},{2,10},{4,12},{6,14},{8,0},{10,2},{12,4},{14,6},{16,24},{18,... | collective-permute-start | bytes 589832 | tf_op jit(solution)/shard_map/ppermute | solution.py:329
  109.0 4.7 %collective-permute-start.27 = (f32[3,64,256]{2,1,0:T(8,128)S(1)}, f32[3,64,256]{2,1,0:T(8,128)S(1)}, u32[]{:S(2)}, u32[]{:S(2)}) collective-permute-start(f32[3,64,256]{2,1,0:T(8,128)S(1)} %get-tuple-element.130), channel_id=1, source_target_pairs={{0,16},{2,18},{4,20},{6,22},{8,24},{10,26},{12,28},{14,30},{16,0},... | collective-permute-start | bytes 589832 | tf_op jit(solution)/shard_map/ppermute | solution.py:329
  113.7 2.4 %collective-permute-start.28 = (f32[3,64,256]{2,1,0:T(8,128)S(1)}, f32[3,64,256]{2,1,0:T(8,128)S(1)}, u32[]{:S(2)}, u32[]{:S(2)}) collective-permute-start(f32[3,64,256]{2,1,0:T(8,128)S(1)} %get-tuple-element.131), channel_id=1, source_target_pairs={{0,24},{2,26},{4,28},{6,30},{8,16},{10,18},{12,20},{14,22},{16,8},... | collective-permute-start | bytes 589832 | tf_op jit(solution)/shard_map/ppermute | solution.py:329
  116.2 3.4 %collective-permute-done.27 = f32[3,64,256]{2,1,0:T(8,128)S(1)} collective-permute-done((f32[3,64,256]{2,1,0:T(8,128)S(1)}, f32[3,64,256]{2,1,0:T(8,128)S(1)}, u32[]{:S(2)}, u32[]{:S(2)}) %collective-permute-start.27) | collective-permute-done | bytes 196640 | tf_op jit(solution)/shard_map/ppermute | solution.py:329
  119.6 3.6 %collective-permute-done.28 = f32[3,64,256]{2,1,0:T(8,128)S(1)} collective-permute-done((f32[3,64,256]{2,1,0:T(8,128)S(1)}, f32[3,64,256]{2,1,0:T(8,128)S(1)}, u32[]{:S(2)}, u32[]{:S(2)}) %collective-permute-start.28) | collective-permute-done | bytes 196640 | tf_op jit(solution)/shard_map/ppermute | solution.py:329
  123.2 1.3 collective-permute-start.29
  126.7 0.9 collective-permute-start.32
  128.1 1.5 collective-permute-start.37
  129.6 1.4 collective-permute-start.38
  131.2 1.7 collective-permute-start.35
  132.9 1.3 collective-permute-start.34
  134.1 1.5 collective-permute-start.33
  136.4 1.3 collective-permute-done.38.refs_3_
  137.7 1.7 shard_map.151
  139.5 13.3 %collective-permute-done.34.refs_4_ = f32[3,64,256]{2,1,0:T(8,128)S(1)} collective-permute-done((f32[3,64,256]{2,1,0:T(8,128)S(1)}, f32[3,64,256]{2,1,0:T(8,128)S(1)}, u32[]{:S(2)}, u32[]{:S(2)}) %collective-permute-start.34) | collective-permute-done | bytes 196640 | tf_op jit(solution)/shard_map/ppermute | solution.py:321
  152.8 3.8 %shard_map.152 = (f32[2,256,256]{2,1,0:T(8,128)S(1)}, f32[2,256,256]{2,1,0:T(8,128)S(1)}, f32[2,256,256]{2,1,0:T(8,128)S(1)}, f32[2,256,256]{2,1,0:T(8,128)S(1)}...) custom-call(s32[2]{0:T(128)S(1)} %pad_add_fusion.place, ...), custom_call_target="tpu_custom_call" | custom-call | flops 2013265920 | bytes 5509128 | tf_op jit(solution)/shard_map/pallas_call | solution.py:34
  157.4 1.5 collective-permute-start.40
  159.0 1.2 collective-permute-start.41
  160.2 4.2 %collective-permute-done.42 = f32[2,3,64,256]{3,2,1,0:T(8,128)S(1)} collective-permute-done((f32[2,3,64,256]{3,2,1,0:T(8,128)S(1)}, f32[2,3,64,256]{3,2,1,0:T(8,128)S(1)}, u32[]{:S(2)}, u32[]{:S(2)}) %collective-permute-start.42) | collective-permute-done | bytes 393248 | tf_op jit(solution)/shard_map/ppermute | solution.py:321
  164.9 8.1 %collective-permute-done.43.refs_3_ = f32[1,3,64,256]{3,2,1,0:T(8,128)S(1)} collective-permute-done((f32[1,3,64,256]{3,2,1,0:T(8,128)S(1)}, f32[1,3,64,256]{3,2,1,0:T(8,128)S(1)}, u32[]{:S(2)}, u32[]{:S(2)}) %collective-permute-start.43) | collective-permute-done | bytes 196640 | tf_op jit(solution)/shard_map/ppermute | solution.py:321
  174.3 1.5 collective-permute-start.45
  175.9 1.2 collective-permute-start.46
  177.1 0.8 collective-permute-done.41.refs_3_
  177.9 2.4 %shard_map.153 = (bf16[256,4,256]{2,1,0:T(4,128)(2,1)}, bf16[256,4,256]{2,1,0:T(4,128)(2,1)}) custom-call(s32[2]{0:T(128)S(1)} %pad_add_fusion.place, f32[4,256]{1,0:T(4,128)S(1)} %bitcast.24, f32[2,256,256]{2,1,0:T(8,128)S(1)} %get-tuple-element.144.refs_0_, f32[2,256,256]{2,1,0:T(8,128)S(1)} %collective-permute-done.39.refs_1_, ...), custom_call_target="tpu_custom_call" | custom-call | flops 16777216 | bytes 3149832 | tf_op jit(solution)/shard_map/pallas_call | solution.py:34
  180.3 3.3 %collective-permute-done.45.refs_2_ = f32[3,16,256]{2,1,0:T(8,128)S(1)} collective-permute-done((f32[3,16,256]{2,1,0:T(8,128)S(1)}, f32[3,16,256]{2,1,0:T(8,128)S(1)}, u32[]{:S(2)}, u32[]{:S(2)}) %collective-permute-start.45) | collective-permute-done | bytes 49184 | tf_op jit(solution)/shard_map/ppermute | solution.py:321
  183.6 1.2 shard_map.155
  (67 shorter events, 10.8 us)
Async XLA Ops:
  0.6 41.5 %copy-start = (f32[4,256,256]{2,1,0:T(8,128)S(1)}, f32[4,256,256]{2,1,0:T(8,128)}, u32[]{:S(2)}) copy-start(f32[4,256,256]{2,1,0:T(8,128)} %param.16) | copy-start | bytes 3145732
  0.7 1.1 copy-start.1
  1.8 12.0 %copy-start.2 = (bf16[1,256,4,256]{3,2,1,0:T(4,128)(2,1)S(1)}, bf16[1,256,4,256]{3,2,1,0:T(4,128)(2,1)}, u32[]{:S(2)}) copy-start(bf16[1,256,4,256]{3,2,1,0:T(4,128)(2,1)} %param.12) | copy-start | bytes 1572868
  3.5 10.4 %copy-start.5 = (f32[1,4,256]{2,1,0:T(4,128)S(1)}, f32[1,4,256]{2,1,0:T(4,128)}, u32[]{:S(2)}) copy-start(f32[1,4,256]{2,1,0:T(4,128)} %param.13) | copy-start | bytes 12292
  3.5 19.6 %collective-permute-start = (f32[256,256]{1,0:T(8,128)S(1)}, f32[256,256]{1,0:T(8,128)S(1)}, u32[]{:S(2)}, u32[]{:S(2)}) collective-permute-start(f32[256,256]{1,0:T(8,128)S(1)} %get-tuple-element.96), channel_id=1, source_target_pairs={{0,2},{2,0},{4,6},{6,4},{8,10},{10,8},{12,14},{14,12},{16,18},{18,... | collective-permute-start | bytes 786440 | tf_op jit(solution)/shard_map/ppermute | solution.py:329
  8.5 16.5 %collective-permute-start.1 = (f32[256,256]{1,0:T(8,128)}, f32[256,256]{1,0:T(8,128)S(1)}, u32[]{:S(2)}, u32[]{:S(2)}) collective-permute-start(f32[256,256]{1,0:T(8,128)} %get-tuple-element.97), channel_id=1, source_target_pairs={{0,4},{2,6},{4,0},{6,2},{8,12},{10,14},{12,8},{14,10},{16,20},{18,... | collective-permute-start | bytes 786440 | tf_op jit(solution)/shard_map/ppermute | solution.py:329
  11.9 13.1 %collective-permute-start.2 = (f32[256,256]{1,0:T(8,128)}, f32[256,256]{1,0:T(8,128)S(1)}, u32[]{:S(2)}, u32[]{:S(2)}) collective-permute-start(f32[256,256]{1,0:T(8,128)} %get-tuple-element.98), channel_id=1, source_target_pairs={{0,6},{2,4},{4,2},{6,0},{8,14},{10,12},{12,10},{14,8},{16,22},{18,... | collective-permute-start | bytes 786440 | tf_op jit(solution)/shard_map/ppermute | solution.py:329
  15.8 9.3 %collective-permute-start.3 = (f32[256,256]{1,0:T(8,128)}, f32[256,256]{1,0:T(8,128)S(1)}, u32[]{:S(2)}, u32[]{:S(2)}) collective-permute-start(f32[256,256]{1,0:T(8,128)} %get-tuple-element.101), channel_id=1, source_target_pairs={{0,2},{2,0},{4,6},{6,4},{8,10},{10,8},{12,14},{14,12},{16,18},{18,... | collective-permute-start | bytes 786440 | tf_op jit(solution)/shard_map/ppermute | solution.py:329
  19.7 8.5 %collective-permute-start.4 = (f32[256,256]{1,0:T(8,128)}, f32[256,256]{1,0:T(8,128)S(1)}, u32[]{:S(2)}, u32[]{:S(2)}) collective-permute-start(f32[256,256]{1,0:T(8,128)} %get-tuple-element.102), channel_id=1, source_target_pairs={{0,4},{2,6},{4,0},{6,2},{8,12},{10,14},{12,8},{14,10},{16,20},{18,... | collective-permute-start | bytes 786440 | tf_op jit(solution)/shard_map/ppermute | solution.py:329
  23.1 9.4 %collective-permute-start.5 = (f32[256,256]{1,0:T(8,128)}, f32[256,256]{1,0:T(8,128)S(1)}, u32[]{:S(2)}, u32[]{:S(2)}) collective-permute-start(f32[256,256]{1,0:T(8,128)} %get-tuple-element.103), channel_id=1, source_target_pairs={{0,6},{2,4},{4,2},{6,0},{8,14},{10,12},{12,10},{14,8},{16,22},{18,... | collective-permute-start | bytes 786440 | tf_op jit(solution)/shard_map/ppermute | solution.py:329
  32.5 2.1 %collective-permute-start.6 = (f32[8,128]{1,0:T(8,128)S(1)}, f32[8,128]{1,0:T(8,128)S(1)}, u32[]{:S(2)}, u32[]{:S(2)}) collective-permute-start(f32[8,128]{1,0:T(8,128)S(1)} %slice.18), channel_id=1, source_target_pairs={{0,1},{2,3},{4,5},{6,7},{8,9},{10,11},{12,13},{14,15},{16,17},{18,... | collective-permute-start | bytes 12296 | tf_op jit(solution)/shard_map/ppermute | solution.py:339
  34.6 6.1 %collective-permute-start.7 = (f32[256,256]{1,0:T(8,128)S(1)}, f32[256,256]{1,0:T(8,128)S(1)}, u32[]{:S(2)}, u32[]{:S(2)}) collective-permute-start(f32[256,256]{1,0:T(8,128)S(1)} %get-tuple-element.96), channel_id=1, source_target_pairs={{1,3},{3,1},{5,7},{7,5},{9,11},{11,9},{13,15},{15,13},{17,19},{19,... | collective-permute-start | bytes 786440 | tf_op jit(solution)/shard_map/ppermute | solution.py:329
  35.2 7.9 %collective-permute-start.8 = (f32[256,256]{1,0:T(8,128)}, f32[256,256]{1,0:T(8,128)}, u32[]{:S(2)}, u32[]{:S(2)}) collective-permute-start(f32[256,256]{1,0:T(8,128)} %get-tuple-element.97), channel_id=1, source_target_pairs={{1,5},{3,7},{5,1},{7,3},{9,13},{11,15},{13,9},{15,11},{17,21},{19,... | collective-permute-start | bytes 786440 | tf_op jit(solution)/shard_map/ppermute | solution.py:329
  36.6 6.6 %collective-permute-start.9 = (f32[256,256]{1,0:T(8,128)}, f32[256,256]{1,0:T(8,128)}, u32[]{:S(2)}, u32[]{:S(2)}) collective-permute-start(f32[256,256]{1,0:T(8,128)} %get-tuple-element.98), channel_id=1, source_target_pairs={{1,7},{3,5},{5,3},{7,1},{9,15},{11,13},{13,11},{15,9},{17,23},{19,... | collective-permute-start | bytes 786440 | tf_op jit(solution)/shard_map/ppermute | solution.py:329
  38.0 5.2 %collective-permute-start.10 = (f32[256,256]{1,0:T(8,128)}, f32[256,256]{1,0:T(8,128)}, u32[]{:S(2)}, u32[]{:S(2)}) collective-permute-start(f32[256,256]{1,0:T(8,128)} %get-tuple-element.101), channel_id=1, source_target_pairs={{1,3},{3,1},{5,7},{7,5},{9,11},{11,9},{13,15},{15,13},{17,19},{19,... | collective-permute-start | bytes 786440 | tf_op jit(solution)/shard_map/ppermute | solution.py:329
  39.3 3.9 %collective-permute-start.11 = (f32[256,256]{1,0:T(8,128)}, f32[256,256]{1,0:T(8,128)}, u32[]{:S(2)}, u32[]{:S(2)}) collective-permute-start(f32[256,256]{1,0:T(8,128)} %get-tuple-element.102), channel_id=1, source_target_pairs={{1,5},{3,7},{5,1},{7,3},{9,13},{11,15},{13,9},{15,11},{17,21},{19,... | collective-permute-start | bytes 786440 | tf_op jit(solution)/shard_map/ppermute | solution.py:329
  40.7 2.5 %collective-permute-start.12 = (f32[256,256]{1,0:T(8,128)}, f32[256,256]{1,0:T(8,128)}, u32[]{:S(2)}, u32[]{:S(2)}) collective-permute-start(f32[256,256]{1,0:T(8,128)} %get-tuple-element.103), channel_id=1, source_target_pairs={{1,7},{3,5},{5,3},{7,1},{9,15},{11,13},{13,11},{15,9},{17,23},{19,... | collective-permute-start | bytes 786440 | tf_op jit(solution)/shard_map/ppermute | solution.py:329
  43.2 7.5 %copy-start.3 = (bf16[1,256,4,256]{3,2,1,0:T(4,128)(2,1)S(1)}, bf16[1,256,4,256]{3,2,1,0:T(4,128)(2,1)}, u32[]{:S(2)}) copy-start(bf16[1,256,4,256]{3,2,1,0:T(4,128)(2,1)} %param.10) | copy-start | bytes 1572868
  43.2 7.5 %copy-start.4 = (bf16[1,256,4,256]{3,2,1,0:T(4,128)(2,1)S(1)}, bf16[1,256,4,256]{3,2,1,0:T(4,128)(2,1)}, u32[]{:S(2)}) copy-start(bf16[1,256,4,256]{3,2,1,0:T(4,128)(2,1)} %param.19) | copy-start | bytes 1572868
  46.3 4.5 %copy-start.6 = (f32[4,256]{1,0:T(4,128)S(1)}, f32[4,256]{1,0:T(4,128)}, u32[]{:S(2)}) copy-start(f32[4,256]{1,0:T(4,128)} %gain.1) | copy-start | bytes 12292
  46.3 5.8 %collective-permute-start.13 = (f32[3,64,256]{2,1,0:T(8,128)S(1)}, f32[3,64,256]{2,1,0:T(8,128)S(1)}, u32[]{:S(2)}, u32[]{:S(2)}) collective-permute-start(f32[3,64,256]{2,1,0:T(8,128)S(1)} %get-tuple-element.105), channel_id=1, source_target_pairs={{0,8},{2,10},{4,12},{6,14},{8,0},{10,2},{12,4},{14,6},{16,24},{18,... | collective-permute-start | bytes 589832 | tf_op jit(solution)/shard_map/ppermute | solution.py:321
  47.9 10.8 %collective-permute-start.14 = (f32[3,64,256]{2,1,0:T(8,128)S(1)}, f32[3,64,256]{2,1,0:T(8,128)S(1)}, u32[]{:S(2)}, u32[]{:S(2)}) collective-permute-start(f32[3,64,256]{2,1,0:T(8,128)S(1)} %get-tuple-element.106), channel_id=1, source_target_pairs={{0,16},{2,18},{4,20},{6,22},{8,24},{10,26},{12,28},{14,30},{16,0},... | collective-permute-start | bytes 589832 | tf_op jit(solution)/shard_map/ppermute | solution.py:321
  50.5 8.2 %collective-permute-start.15 = (f32[3,64,256]{2,1,0:T(8,128)S(1)}, f32[3,64,256]{2,1,0:T(8,128)S(1)}, u32[]{:S(2)}, u32[]{:S(2)}) collective-permute-start(f32[3,64,256]{2,1,0:T(8,128)S(1)} %get-tuple-element.107), channel_id=1, source_target_pairs={{0,24},{2,26},{4,28},{6,30},{8,16},{10,18},{12,20},{14,22},{16,8},... | collective-permute-start | bytes 589832 | tf_op jit(solution)/shard_map/ppermute | solution.py:321
  58.8 20.4 %copy-start.7 = (f32[4]{0:T(128)S(1)}, f32[4]{0:T(128)}, u32[]{:S(2)}) copy-start(f32[4]{0:T(128)} %param.14) | copy-start | bytes 52
  58.8 26.2 %collective-permute-start.16 = (f32[2,256,256]{2,1,0:T(8,128)S(1)}, f32[2,256,256]{2,1,0:T(8,128)S(1)}, u32[]{:S(2)}, u32[]{:S(2)}) collective-permute-start(f32[2,256,256]{2,1,0:T(8,128)S(1)} %get-tuple-element.113), channel_id=1, source_target_pairs={{0,2},{2,0},{4,6},{6,4},{8,10},{10,8},{12,14},{14,12},{16,18},{18,... | collective-permute-start | bytes 1572872 | tf_op jit(solution)/shard_map/ppermute | solution.py:321
  59.4 25.6 %collective-permute-start.17 = (f32[2,256,256]{2,1,0:T(8,128)S(1)}, f32[2,256,256]{2,1,0:T(8,128)S(1)}, u32[]{:S(2)}, u32[]{:S(2)}) collective-permute-start(f32[2,256,256]{2,1,0:T(8,128)S(1)} %get-tuple-element.114), channel_id=1, source_target_pairs={{0,4},{2,6},{4,0},{6,2},{8,12},{10,14},{12,8},{14,10},{16,20},{18,... | collective-permute-start | bytes 1572872 | tf_op jit(solution)/shard_map/ppermute | solution.py:321
  59.9 25.1 %collective-permute-start.18 = (f32[2,256,256]{2,1,0:T(8,128)S(1)}, f32[2,256,256]{2,1,0:T(8,128)S(1)}, u32[]{:S(2)}, u32[]{:S(2)}) collective-permute-start(f32[2,256,256]{2,1,0:T(8,128)S(1)} %get-tuple-element.115), channel_id=1, source_target_pairs={{0,6},{2,4},{4,2},{6,0},{8,14},{10,12},{12,10},{14,8},{16,22},{18,... | collective-permute-start | bytes 1572872 | tf_op jit(solution)/shard_map/ppermute | solution.py:321
  62.4 9.7 %collective-permute-start.21 = (f32[3,64,256]{2,1,0:T(8,128)S(1)}, f32[3,64,256]{2,1,0:T(8,128)S(1)}, u32[]{:S(2)}, u32[]{:S(2)}) collective-permute-start(f32[3,64,256]{2,1,0:T(8,128)S(1)} %add_add_fusion.1.refs_4_), channel_id=1, source_target_pairs={{0,24},{2,26},{4,28},{6,30},{8,16},{10,18},{12,20},{14,22},{16,8},... | collective-permute-start | bytes 589832 | tf_op jit(solution)/shard_map/ppermute | solution.py:321
  64.9 16.0 %collective-permute-start.20 = (f32[3,64,256]{2,1,0:T(8,128)S(1)}, f32[3,64,256]{2,1,0:T(8,128)S(1)}, u32[]{:S(2)}, u32[]{:S(2)}) collective-permute-start(f32[3,64,256]{2,1,0:T(8,128)S(1)} %add_add_fusion.1.refs_4_), channel_id=1, source_target_pairs={{0,16},{2,18},{4,20},{6,22},{8,24},{10,26},{12,28},{14,30},{16,0},... | collective-permute-start | bytes 589832 | tf_op jit(solution)/shard_map/ppermute | solution.py:321
  72.1 13.0 %collective-permute-start.19 = (f32[3,64,256]{2,1,0:T(8,128)S(1)}, f32[3,64,256]{2,1,0:T(8,128)S(1)}, u32[]{:S(2)}, u32[]{:S(2)}) collective-permute-start(f32[3,64,256]{2,1,0:T(8,128)S(1)} %add_add_fusion.1.refs_4_), channel_id=1, source_target_pairs={{0,8},{2,10},{4,12},{6,14},{8,0},{10,2},{12,4},{14,6},{16,24},{18,... | collective-permute-start | bytes 589832 | tf_op jit(solution)/shard_map/ppermute | solution.py:321
  87.4 9.0 %collective-permute-start.22 = (f32[2,4,256]{2,1,0:T(4,128)S(1)}, f32[2,4,256]{2,1,0:T(4,128)S(1)}, u32[]{:S(2)}, u32[]{:S(2)}) collective-permute-start(f32[2,4,256]{2,1,0:T(4,128)S(1)} %get-tuple-element.117), channel_id=1, source_target_pairs={{0,1},{1,0},{2,3},{3,2},{4,5},{5,4},{6,7},{7,6},{8,9},{9,8},{10,11... | collective-permute-start | bytes 24584 | tf_op jit(solution)/shard_map/ppermute | solution.py:321
  96.4 4.5 %collective-permute-start.25 = (f32[2,4,256]{2,1,0:T(4,128)S(1)}, f32[2,4,256]{2,1,0:T(4,128)S(1)}, u32[]{:S(2)}, u32[]{:S(2)}) collective-permute-start(f32[2,4,256]{2,1,0:T(4,128)S(1)} %add.45.refs_4_), channel_id=1, source_target_pairs={{0,6},{2,4},{4,2},{6,0},{8,14},{10,12},{12,10},{14,8},{16,22},{18,... | collective-permute-start | bytes 24584 | tf_op jit(solution)/shard_map/ppermute | solution.py:321
  98.7 3.7 %collective-permute-start.24 = (f32[2,4,256]{2,1,0:T(4,128)S(1)}, f32[2,4,256]{2,1,0:T(4,128)S(1)}, u32[]{:S(2)}, u32[]{:S(2)}) collective-permute-start(f32[2,4,256]{2,1,0:T(4,128)S(1)} %add.45.refs_4_), channel_id=1, source_target_pairs={{0,4},{2,6},{4,0},{6,2},{8,12},{10,14},{12,8},{14,10},{16,20},{18,... | collective-permute-start | bytes 24584 | tf_op jit(solution)/shard_map/ppermute | solution.py:321
  99.3 3.7 %collective-permute-start.23 = (f32[2,4,256]{2,1,0:T(4,128)S(1)}, f32[2,4,256]{2,1,0:T(4,128)S(1)}, u32[]{:S(2)}, u32[]{:S(2)}) collective-permute-start(f32[2,4,256]{2,1,0:T(4,128)S(1)} %add.45.refs_4_), channel_id=1, source_target_pairs={{0,2},{2,0},{4,6},{6,4},{8,10},{10,8},{12,14},{14,12},{16,18},{18,... | collective-permute-start | bytes 24584 | tf_op jit(solution)/shard_map/ppermute | solution.py:321
  106.1 10.1 %collective-permute-start.26 = (f32[3,64,256]{2,1,0:T(8,128)S(1)}, f32[3,64,256]{2,1,0:T(8,128)S(1)}, u32[]{:S(2)}, u32[]{:S(2)}) collective-permute-start(f32[3,64,256]{2,1,0:T(8,128)S(1)} %get-tuple-element.129), channel_id=1, source_target_pairs={{0,8},{2,10},{4,12},{6,14},{8,0},{10,2},{12,4},{14,6},{16,24},{18,... | collective-permute-start | bytes 589832 | tf_op jit(solution)/shard_map/ppermute | solution.py:329
  109.0 10.6 %collective-permute-start.27 = (f32[3,64,256]{2,1,0:T(8,128)S(1)}, f32[3,64,256]{2,1,0:T(8,128)S(1)}, u32[]{:S(2)}, u32[]{:S(2)}) collective-permute-start(f32[3,64,256]{2,1,0:T(8,128)S(1)} %get-tuple-element.130), channel_id=1, source_target_pairs={{0,16},{2,18},{4,20},{6,22},{8,24},{10,26},{12,28},{14,30},{16,0},... | collective-permute-start | bytes 589832 | tf_op jit(solution)/shard_map/ppermute | solution.py:329
  113.7 9.5 %collective-permute-start.28 = (f32[3,64,256]{2,1,0:T(8,128)S(1)}, f32[3,64,256]{2,1,0:T(8,128)S(1)}, u32[]{:S(2)}, u32[]{:S(2)}) collective-permute-start(f32[3,64,256]{2,1,0:T(8,128)S(1)} %get-tuple-element.131), channel_id=1, source_target_pairs={{0,24},{2,26},{4,28},{6,30},{8,16},{10,18},{12,20},{14,22},{16,8},... | collective-permute-start | bytes 589832 | tf_op jit(solution)/shard_map/ppermute | solution.py:329
  123.2 2.1 %collective-permute-start.29 = (f32[8,128]{1,0:T(8,128)S(1)}, f32[8,128]{1,0:T(8,128)S(1)}, u32[]{:S(2)}, u32[]{:S(2)}) collective-permute-start(f32[8,128]{1,0:T(8,128)S(1)} %slice_bitcast_fusion), channel_id=1, source_target_pairs={{0,1},{2,3},{4,5},{6,7},{8,9},{10,11},{12,13},{14,15},{16,17},{18,... | collective-permute-start | bytes 12296 | tf_op jit(solution)/shard_map/ppermute | solution.py:339
  125.3 4.3 %collective-permute-start.30 = (f32[3,64,256]{2,1,0:T(8,128)S(1)}, f32[3,64,256]{2,1,0:T(8,128)S(1)}, u32[]{:S(2)}, u32[]{:S(2)}) collective-permute-start(f32[3,64,256]{2,1,0:T(8,128)S(1)} %get-tuple-element.129), channel_id=1, source_target_pairs={{1,9},{3,11},{5,13},{7,15},{9,1},{11,3},{13,5},{15,7},{17,25},{19,... | collective-permute-start | bytes 589832 | tf_op jit(solution)/shard_map/ppermute | solution.py:329
  126.0 5.1 %collective-permute-start.31 = (f32[3,64,256]{2,1,0:T(8,128)S(1)}, f32[3,64,256]{2,1,0:T(8,128)S(1)}, u32[]{:S(2)}, u32[]{:S(2)}) collective-permute-start(f32[3,64,256]{2,1,0:T(8,128)S(1)} %get-tuple-element.130), channel_id=1, source_target_pairs={{1,17},{3,19},{5,21},{7,23},{9,25},{11,27},{13,29},{15,31},{17,1},... | collective-permute-start | bytes 589832 | tf_op jit(solution)/shard_map/ppermute | solution.py:329
  126.7 4.4 %collective-permute-start.32 = (f32[3,64,256]{2,1,0:T(8,128)S(1)}, f32[3,64,256]{2,1,0:T(8,128)S(1)}, u32[]{:S(2)}, u32[]{:S(2)}) collective-permute-start(f32[3,64,256]{2,1,0:T(8,128)S(1)} %get-tuple-element.131), channel_id=1, source_target_pairs={{1,25},{3,27},{5,29},{7,31},{9,17},{11,19},{13,21},{15,23},{17,9},... | collective-permute-start | bytes 589832 | tf_op jit(solution)/shard_map/ppermute | solution.py:329
  127.5 6.6 %collective-permute-start.36 = (f32[256,256]{1,0:T(8,128)S(1)}, f32[256,256]{1,0:T(8,128)S(1)}, u32[]{:S(2)}, u32[]{:S(2)}) collective-permute-start(f32[256,256]{1,0:T(8,128)S(1)} %get-tuple-element.133), channel_id=1, source_target_pairs={{0,2},{2,0},{4,6},{6,4},{8,10},{10,8},{12,14},{14,12},{16,18},{18,... | collective-permute-start | bytes 786440 | tf_op jit(solution)/shard_map/ppermute | solution.py:321
  128.1 8.3 %collective-permute-start.37 = (f32[256,256]{1,0:T(8,128)S(1)}, f32[256,256]{1,0:T(8,128)S(1)}, u32[]{:S(2)}, u32[]{:S(2)}) collective-permute-start(f32[256,256]{1,0:T(8,128)S(1)} %get-tuple-element.134), channel_id=1, source_target_pairs={{0,4},{2,6},{4,0},{6,2},{8,12},{10,14},{12,8},{14,10},{16,20},{18,... | collective-permute-start | bytes 786440 | tf_op jit(solution)/shard_map/ppermute | solution.py:321
  129.6 8.1 %collective-permute-start.38 = (f32[256,256]{1,0:T(8,128)S(1)}, f32[256,256]{1,0:T(8,128)S(1)}, u32[]{:S(2)}, u32[]{:S(2)}) collective-permute-start(f32[256,256]{1,0:T(8,128)S(1)} %get-tuple-element.135), channel_id=1, source_target_pairs={{0,6},{2,4},{4,2},{6,0},{8,14},{10,12},{12,10},{14,8},{16,22},{18,... | collective-permute-start | bytes 786440 | tf_op jit(solution)/shard_map/ppermute | solution.py:321
  131.2 8.3 %collective-permute-start.35 = (f32[3,64,256]{2,1,0:T(8,128)S(1)}, f32[3,64,256]{2,1,0:T(8,128)S(1)}, u32[]{:S(2)}, u32[]{:S(2)}) collective-permute-start(f32[3,64,256]{2,1,0:T(8,128)S(1)} %add_add_fusion.refs_2_.refs_0_), channel_id=1, source_target_pairs={{0,24},{2,26},{4,28},{6,30},{8,16},{10,18},{12,20},{14,22},{16,8},... | collective-permute-start | bytes 589832 | tf_op jit(solution)/shard_map/ppermute | solution.py:321
  132.9 19.9 %collective-permute-start.34 = (f32[3,64,256]{2,1,0:T(8,128)S(1)}, f32[3,64,256]{2,1,0:T(8,128)S(1)}, u32[]{:S(2)}, u32[]{:S(2)}) collective-permute-start(f32[3,64,256]{2,1,0:T(8,128)S(1)} %add_add_fusion.refs_2_.refs_0_), channel_id=1, source_target_pairs={{0,16},{2,18},{4,20},{6,22},{8,24},{10,26},{12,28},{14,30},{16,0},... | collective-permute-start | bytes 589832 | tf_op jit(solution)/shard_map/ppermute | solution.py:321
  134.1 18.7 %collective-permute-start.33 = (f32[3,64,256]{2,1,0:T(8,128)S(1)}, f32[3,64,256]{2,1,0:T(8,128)S(1)}, u32[]{:S(2)}, u32[]{:S(2)}) collective-permute-start(f32[3,64,256]{2,1,0:T(8,128)S(1)} %add_add_fusion.refs_2_.refs_0_), channel_id=1, source_target_pairs={{0,8},{2,10},{4,12},{6,14},{8,0},{10,2},{12,4},{14,6},{16,24},{18,... | collective-permute-start | bytes 589832 | tf_op jit(solution)/shard_map/ppermute | solution.py:321
  156.6 7.8 %collective-permute-start.42 = (f32[2,3,64,256]{3,2,1,0:T(8,128)S(1)}, f32[2,3,64,256]{3,2,1,0:T(8,128)S(1)}, u32[]{:S(2)}, u32[]{:S(2)}) collective-permute-start(f32[2,3,64,256]{3,2,1,0:T(8,128)S(1)} %get-tuple-element.151), channel_id=1, source_target_pairs={{0,8},{2,10},{4,12},{6,14},{8,0},{10,2},{12,4},{14,6},{16,24},{18,... | collective-permute-start | bytes 1179656 | tf_op jit(solution)/shard_map/ppermute | solution.py:321
  156.7 19.2 %collective-permute-start.39 = (f32[2,256,256]{2,1,0:T(8,128)S(1)}, f32[2,256,256]{2,1,0:T(8,128)S(1)}, u32[]{:S(2)}, u32[]{:S(2)}) collective-permute-start(f32[2,256,256]{2,1,0:T(8,128)S(1)} %get-tuple-element.145), channel_id=1, source_target_pairs={{0,2},{2,0},{4,6},{6,4},{8,10},{10,8},{12,14},{14,12},{16,18},{18,... | collective-permute-start | bytes 1572872 | tf_op jit(solution)/shard_map/ppermute | solution.py:321
  157.4 19.7 %collective-permute-start.40 = (f32[2,256,256]{2,1,0:T(8,128)S(1)}, f32[2,256,256]{2,1,0:T(8,128)S(1)}, u32[]{:S(2)}, u32[]{:S(2)}) collective-permute-start(f32[2,256,256]{2,1,0:T(8,128)S(1)} %get-tuple-element.146), channel_id=1, source_target_pairs={{0,4},{2,6},{4,0},{6,2},{8,12},{10,14},{12,8},{14,10},{16,20},{18,... | collective-permute-start | bytes 1572872 | tf_op jit(solution)/shard_map/ppermute | solution.py:321
  159.0 18.9 %collective-permute-start.41 = (f32[2,256,256]{2,1,0:T(8,128)S(1)}, f32[2,256,256]{2,1,0:T(8,128)S(1)}, u32[]{:S(2)}, u32[]{:S(2)}) collective-permute-start(f32[2,256,256]{2,1,0:T(8,128)S(1)} %get-tuple-element.147), channel_id=1, source_target_pairs={{0,6},{2,4},{4,2},{6,0},{8,14},{10,12},{12,10},{14,8},{16,22},{18,... | collective-permute-start | bytes 1572872 | tf_op jit(solution)/shard_map/ppermute | solution.py:321
  164.5 8.5 %collective-permute-start.43 = (f32[1,3,64,256]{3,2,1,0:T(8,128)S(1)}, f32[1,3,64,256]{3,2,1,0:T(8,128)S(1)}, u32[]{:S(2)}, u32[]{:S(2)}) collective-permute-start(f32[1,3,64,256]{3,2,1,0:T(8,128)S(1)} %get-tuple-element.160), channel_id=1, source_target_pairs={{0,16},{2,18},{4,20},{6,22},{8,24},{10,26},{12,28},{14,30},{16,0},... | collective-permute-start | bytes 589832 | tf_op jit(solution)/shard_map/ppermute | solution.py:321
  173.5 6.8 %collective-permute-start.44 = (f32[3,16,256]{2,1,0:T(8,128)S(1)}, f32[3,16,256]{2,1,0:T(8,128)S(1)}, u32[]{:S(2)}, u32[]{:S(2)}) collective-permute-start(f32[3,16,256]{2,1,0:T(8,128)S(1)} %get-tuple-element.154), channel_id=1, source_target_pairs={{0,2},{2,0},{4,6},{6,4},{8,10},{10,8},{12,14},{14,12},{16,18},{18,... | collective-permute-start | bytes 147464 | tf_op jit(solution)/shard_map/ppermute | solution.py:321
  174.3 9.3 %collective-permute-start.45 = (f32[3,16,256]{2,1,0:T(8,128)S(1)}, f32[3,16,256]{2,1,0:T(8,128)S(1)}, u32[]{:S(2)}, u32[]{:S(2)}) collective-permute-start(f32[3,16,256]{2,1,0:T(8,128)S(1)} %get-tuple-element.155), channel_id=1, source_target_pairs={{0,4},{2,6},{4,0},{6,2},{8,12},{10,14},{12,8},{14,10},{16,20},{18,... | collective-permute-start | bytes 147464 | tf_op jit(solution)/shard_map/ppermute | solution.py:321
  175.9 7.8 %collective-permute-start.46 = (f32[3,16,256]{2,1,0:T(8,128)S(1)}, f32[3,16,256]{2,1,0:T(8,128)S(1)}, u32[]{:S(2)}, u32[]{:S(2)}) collective-permute-start(f32[3,16,256]{2,1,0:T(8,128)S(1)} %get-tuple-element.156), channel_id=1, source_target_pairs={{0,6},{2,4},{4,2},{6,0},{8,14},{10,12},{12,10},{14,8},{16,22},{18,... | collective-permute-start | bytes 147464 | tf_op jit(solution)/shard_map/ppermute | solution.py:321

commit v6 on v3

--- a/solution.py
+++ b/solution.py
@@ -69,9 +69,11 @@
         outs[step][...] = take_head(scratch, place[0] ^ step, tokens, heads)
 
 
-def split_scaled_kernel(groups, place, x, r, *rest):
-    outs = rest[:groups]
-    split_kernel(groups, place, x, *rest)
+def split_scaled_kernel(groups, place, x, r, key, *rest):
+    outs = list(rest[:groups])
+    outs[1][0] = key[...]
+    outs[1] = outs[1].at[1]
+    split_kernel(groups, place, x, *outs, *rest[groups:])
     for step in range(groups):
         scaled = outs[step][...] * rate_column(r, place[0] ^ step)
         outs[step][...] = scaled.astype(BF16).astype(F32)
@@ -97,14 +99,19 @@
 
 
 def update_kernel(groups, depth, scale, place, *refs):
-    keys_in, scaled_in = refs[:groups], refs[groups : 2 * groups]
-    w_gate, w_out, w_up = refs[2 * groups : 2 * groups + 3]
-    outs, sums = refs[2 * groups + 3 : -1], refs[-1]
+    pieces = list(zip(refs[:groups], refs[groups : 2 * groups]))
+    pieces[1] = (refs[1].at[0], refs[1].at[1])
+    refs = refs[2 * groups :]
+    w_gate, w_out, w_up = refs[:3]
+    key_kept, scaled_kept = refs[3:5]
+    outs, sums = refs[5:-1], refs[-1]
     gate_b, out_b, up_b = (w[...].astype(BF16) for w in (w_gate, w_out, w_up))
     total = [0.0, 0.0, 0.0]
-    for key, value in zip(keys_in, scaled_in):
+    for step, (key, value) in enumerate(pieces):
         keys = key[...].astype(BF16)
         scaled = value[...].astype(BF16)
+        key_kept[step] = keys
+        scaled_kept[step] = scaled
         first = mm(keys, gate_b)
         third = mm(keys, up_b)
         sig = jax.nn.sigmoid(first)
@@ -196,6 +203,20 @@
     send_slices(sums, slices, place[1])
 
 
+def paired(groups):
+    return [True, True, True, False, False] if groups == 4 else [True] * groups
+
+
+def back_refs(groups, refs):
+    pairs, singles = [], []
+    for ref, both in zip(refs, paired(groups)):
+        if both:
+            pairs.append((ref.at[0], ref.at[1]))
+        else:
+            singles.append(ref)
+    return pairs + ([tuple(singles)] if singles else [])
+
+
 def halving_order(depth):
     sets, bit = [], 1
     while bit < depth:
@@ -205,20 +226,20 @@
 
 
 def update_back_kernel(groups, depth, scale, place, *refs):
-    keys_in, scaled_in = refs[:groups], refs[groups : 2 * groups]
-    parts = refs[2 * groups : 2 * groups + depth]
-    w_gate, w_out, w_up = refs[2 * groups + depth : 2 * groups + depth + 3]
-    base = 2 * groups + depth + 3
-    outs = refs[base : base + groups]
-    slices = refs[base + groups : -2]
+    keys_in, scaled_in = refs[:2]
+    parts = refs[2 : depth + 2]
+    w_gate, w_out, w_up = refs[depth + 2 : depth + 5]
+    refs = refs[depth + 5 :]
+    count = len(paired(groups))
+    outs, slices = back_refs(groups, refs[:count]), refs[count:-2]
     whole, sums = refs[-2:]
     assemble(place, parts, whole)
     gate_b, out_b, up_b = (w[...].astype(BF16) for w in (w_gate, w_out, w_up))
     cot_gate, cot_out, cot_up = ((whole[i] * scale).astype(BF16) for i in range(3))
     total = [0.0, 0.0, 0.0]
     for step in range(groups):
-        keys = keys_in[step][...].astype(BF16)
-        scaled = scaled_in[step][...].astype(BF16)
+        keys = keys_in[step]
+        scaled = scaled_in[step]
         first = mm(keys, gate_b)
         third = mm(keys, up_b)
         sig = jax.nn.sigmoid(first)
@@ -239,13 +260,13 @@
         bar_df_dact = bar_dfirst * dact
         bar_third = (bar_df_dact * deriv + bar_act * activ).astype(BF16)
         bar_first = (bar_activ * deriv + bar_df_dact * third * second).astype(BF16)
-        outs[step][0] = (
+        outs[step][0][...] = (
             mm_t(dfirst, cot_gate)
             + mm_t(dthird, cot_up)
             + mm_t(bar_first, gate_b)
             + mm_t(bar_third, up_b)
         )
-        outs[step][1] = mm(act, cot_out) + mm(bar_dact, out_b)
+        outs[step][1][...] = mm(act, cot_out) + mm(bar_dact, out_b)
         total[0] += tmm(keys, bar_first)
         total[1] += tmm(bar_dact, scaled)
         total[2] += tmm(keys, bar_third)
@@ -267,12 +288,12 @@
 
 
 def join_update_kernel(groups, place, r, *refs):
-    pieces, (out_k, out_v, sk, sv) = refs[:groups], refs[groups:]
+    pieces, (out_k, out_v, sk, sv) = back_refs(groups, refs[:-4]), refs[-4:]
     tokens, heads, width = out_k.shape
-    for step, piece in enumerate(pieces):
+    for step, (key, value) in enumerate(pieces):
         head = place[0] ^ step
-        put_head(sk, head, piece[0], tokens, heads)
-        put_head(sv, head, piece[1] * rate_column(r, head), tokens, heads)
+        put_head(sk, head, key[...], tokens, heads)
+        put_head(sv, head, value[...] * rate_column(r, head), tokens, heads)
     out_k[...] = rows_of(sk).reshape(tokens, heads, width).astype(BF16)
     out_v[...] = rows_of(sv).reshape(tokens, heads, width).astype(BF16)
 
@@ -329,24 +350,37 @@
     scratch = pltpu.VMEM((width // LANES, tokens * heads, LANES), F32)
     square = pltpu.VMEM((3, hidden, width), F32)
 
-    def split(body, *args):
-        return call(functools.partial(body, groups), pieces, [scratch], flops // 16, place, *args)
-
-    k_in = in_plane(split(split_kernel, keys[0]))
-    s_in = in_plane(split(split_scaled_kernel, values[0], rates[0]))
+    def split(body, out, *args):
+        return call(functools.partial(body, groups), out, [scratch], flops // 16, place, *args)
+
+    both = [shape(2, tokens, width)]
+    k_out = split(split_kernel, pieces, keys[0])
+    s_out = split(
+        split_scaled_kernel, pieces[:1] + both + pieces[2:], values[0], rates[0], k_out[1]
+    )
+    k_in = [k_out[0], move(s_out[1], "ctx", 1)]
+    s_in = [s_out[0], s_out[0]]
+    if groups == 4:
+        k_in += [move(k_out[2], "ctx", 2), move(move(k_out[3], "ctx", 1), "ctx", 2)]
+        s_in += [move(s_out[2], "ctx", 2), move(move(s_out[3], "ctx", 2), "ctx", 1)]
+    else:
+        k_in += [move(k_out[step], "ctx", step) for step in range(2, groups)]
+        s_in += [move(s_out[step], "ctx", step) for step in range(2, groups)]
     own = [lax.dynamic_index_in_dim(w, mine, 0, keepdims=False) for w in (w_gate, w_out, w_up)]
     own_scale = lax.dynamic_index_in_dim(head_scale, mine, 0, keepdims=True)[None, :]
     q_out = call(
-        functools.partial(split_apply_kernel, groups), [shape(2, tokens, width)] * groups,
+        functools.partial(split_apply_kernel, groups), both * groups,
         [scratch], flops // 8, place, queries[0], cotangent[0], gain,
     )
     k_in, s_in, q_out = after(k_in, s_in, q_out)
-    terms = call(
-        functools.partial(update_kernel, groups, depth, scale), slices, [square], 6 * flops,
-        place, *k_in, *s_in, *own,
-    )
+    kept_b = shape(groups, tokens, width, dtype=BF16)
+    out = call(
+        functools.partial(update_kernel, groups, depth, scale), [kept_b] * 2 + slices, [square],
+        6 * flops, place, *k_in, *s_in, *own,
+    )
+    k_in, s_in, terms = out[0], out[1], in_column(out[2:])
     q_in = in_plane(q_out)
-    new = functools.reduce(jnp.add, in_column(terms))
+    new = functools.reduce(jnp.add, terms)
     new, q_in[:-1] = after(new, q_in[:-1])
     new = in_column([new] * depth)
     kept = shape(groups, tokens, width)
@@ -372,16 +406,21 @@
         functools.partial(join_query_kernel, groups), [joined], [scratch], flops // 16,
         place, *q_back,
     )
+    parts, grad_q = after(parts, grad_q)
     rows = hidden // depth
     sets = halving_order(depth)
     out = call(
         functools.partial(update_back_kernel, groups, depth, scale),
-        [shape(2, tokens, width)] * groups
+        [both[0] if two else pieces[0] for two in paired(groups)]
         + [shape(len(members), 3, rows, width) for members in sets + [[0]]],
-        [square] * 2, 15 * flops, place, *k_in, *s_in, *parts, *own,
-    )
-    back = in_plane(out[:groups])
-    ends, rest = list(out[groups:-1]), [part, out[-1]]
+        [square] * 2, 15 * flops, place, k_in, s_in, *parts, *own,
+    )
+    sent, out = out[: len(paired(groups))], out[len(paired(groups)) :]
+    back = in_plane(sent[:groups] if len(sent) == groups else sent[: groups - 1])
+    if len(sent) > groups:
+        back.append(move(move(sent[-2], "ctx", 1), "ctx", 2))
+        back.append(move(move(sent[-1], "ctx", 2), "ctx", 1))
+    ends, rest = list(out[:-1]), [part, out[-1]]
     for i in range(len(ends)):
         got = move(ends[i], "ctx", groups << i)
         for j in range(i + 1, len(ends)):

time: 159 us -> 162 us (1.019)
  starting transfers between devices: 49.8 us -> 54.8 us
    ppermute x36 -> x40, starting transfers between devices: 49.8 us -> 54.8 us  [move(): lax.ppermute(x, axis, [(c, c ^ step) for c in range(lax.axis_size(axis))])]
    ppermute x36 -> x40, waiting for transfers between devices: 80 us -> 78.6 us  [move(): lax.ppermute(x, axis, [(c, c ^ step) for c in range(lax.axis_size(axis))])]
  transfers between devices with their start and end apart: 36 -> 40, of which waited for: 20 -> 20; matrix products, arithmetic and copies ran while one was open for 1% -> 1% of each run, Pallas kernels for 7% -> 7%
where the time goes in v6:
time: 162 us; the launch traced here: 161 us
  waiting for transfers between devices  78.6 us (49%)
  starting transfers between devices  54.8 us (34%)
  Pallas kernels  22.6 us (14%)
  local copies, waits for them, and re-layouts  4.54 us (3%)
    ppermute x40, waiting for transfers between devices, move(): lax.ppermute(x, axis, [(c, c ^ step) for c in range(lax.axis_size(axis))])  78.6 us
    ppermute x40, starting transfers between devices, move(): lax.ppermute(x, axis, [(c, c ^ step) for c in range(lax.axis_size(axis))])  54.8 us
    pallas_call x11, Pallas kernels, call(): pl.pallas_call(body, out_shape=out_shape, in_specs=[smem if a.dtype == jn...  22.6 us
  transfers between devices with their start and end apart: 40, of which 20 were waited for; matrix products, arithmetic and copies ran while one was open for 1% of the time, Pallas kernels for 7%

profile of v6, /device:TPU:0, one launch (start us, length us, event | category | flops | bytes accessed | tf_op | source)
XLA Modules:
  0.0 161.5 jit_solution(861730380306939729)
XLA Ops:
  0.7 1.1 copy-done.1
  1.8 1.6 shard_map.145
  3.4 2.9 %collective-permute-start.2 = (f32[256,256]{1,0:T(8,128)S(1)}, f32[256,256]{1,0:T(8,128)}, u32[]{:S(2)}, u32[]{:S(2)}) collective-permute-start(f32[256,256]{1,0:T(8,128)S(1)} %get-tuple-element.84), channel_id=1, source_target_pairs={{0,2},{2,0},{4,6},{6,4},{8,10},{10,8},{12,14},{14,12},{16,18},{18,... | collective-permute-start | bytes 786440 | tf_op jit(solution)/shard_map/ppermute | solution.py:332
  6.4 1.9 %shard_map.146 = (f32[256,256]{1,0:T(8,128)S(1)}, f32[2,256,256]{2,1,0:T(8,128)}, f32[256,256]{1,0:T(8,128)}, f32[256,256]{1,0:T(8,128)S(1)}) custom-call(s32[2]{0:T(128)S(1)} %pad_add_fusion.place, bf16[256,4,256]{2,1,0:T(4,128)(2,1)S(1)} %bitcast.18, f32[4,256]{1,0:T(4,128)S(1)} %bitcast.21, f32[256,256]{1,0:T(8,128)S(1)} %get-tuple-element.81.key), custom_call_target="tpu_custom_call" | custom-call | flops 8388608 | bytes 2101256 | tf_op jit(solution)/shard_map/pallas_call | solution.py:34
  8.3 1.5 collective-permute-start.5
  9.8 0.5 collective-permute-start
  10.4 2.0 %collective-permute-start.4 = (f32[256,256]{1,0:T(8,128)}, f32[256,256]{1,0:T(8,128)S(1)}, u32[]{:S(2)}, u32[]{:S(2)}) collective-permute-start(f32[256,256]{1,0:T(8,128)} %get-tuple-element.86), channel_id=1, source_target_pairs={{0,4},{2,6},{4,0},{6,2},{8,12},{10,14},{12,8},{14,10},{16,20},{18,... | collective-permute-start | bytes 786440 | tf_op jit(solution)/shard_map/ppermute | solution.py:332
  12.4 1.1 collective-permute-done.2
  13.5 2.2 %collective-permute-start.3 = (f32[256,256]{1,0:T(8,128)}, f32[256,256]{1,0:T(8,128)S(1)}, u32[]{:S(2)}, u32[]{:S(2)}) collective-permute-start(f32[256,256]{1,0:T(8,128)} %collective-permute-done.2), channel_id=1, source_target_pairs={{0,4},{2,6},{4,0},{6,2},{8,12},{10,14},{12,8},{14,10},{16,20},{18,... | collective-permute-start | bytes 786440 | tf_op jit(solution)/shard_map/ppermute | solution.py:332
  15.7 1.9 %collective-permute-done.5 = f32[256,256]{1,0:T(8,128)} collective-permute-done((f32[256,256]{1,0:T(8,128)S(1)}, f32[256,256]{1,0:T(8,128)}, u32[]{:S(2)}, u32[]{:S(2)}) %collective-permute-start.5) | collective-permute-done | bytes 262176 | tf_op jit(solution)/shard_map/ppermute | solution.py:332
  17.7 0.7 copy-done.6
  18.3 1.0 copy-done.4
  19.4 1.3 shard_map.147
  20.7 1.1 dynamic-slice_bitcast_fusion
  21.8 1.4 collective-permute-done.1.refs_2_
  23.2 5.6 %collective-permute-done.4.refs_6_ = f32[256,256]{1,0:T(8,128)S(1)} collective-permute-done((f32[256,256]{1,0:T(8,128)}, f32[256,256]{1,0:T(8,128)S(1)}, u32[]{:S(2)}, u32[]{:S(2)}) %collective-permute-start.4) | collective-permute-done | bytes 262176 | tf_op jit(solution)/shard_map/ppermute | solution.py:332
  28.8 4.2 %collective-permute-done.3.refs_3_ = f32[256,256]{1,0:T(8,128)S(1)} collective-permute-done((f32[256,256]{1,0:T(8,128)}, f32[256,256]{1,0:T(8,128)S(1)}, u32[]{:S(2)}, u32[]{:S(2)}) %collective-permute-start.3) | collective-permute-done | bytes 262176 | tf_op jit(solution)/shard_map/ppermute | solution.py:332
  33.3 1.7 %collective-permute-start.11 = (f32[2,256,256]{2,1,0:T(8,128)S(1)}, f32[2,256,256]{2,1,0:T(8,128)S(1)}, u32[]{:S(2)}, u32[]{:S(2)}) collective-permute-start(f32[2,256,256]{2,1,0:T(8,128)S(1)} %get-tuple-element.106), channel_id=1, source_target_pairs={{0,4},{2,6},{4,0},{6,2},{8,12},{10,14},{12,8},{14,10},{16,20},{18,... | collective-permute-start | bytes 1572872 | tf_op jit(solution)/shard_map/ppermute | solution.py:332
  35.0 2.6 %shard_map.148 = (bf16[4,256,256]{2,1,0:T(8,128)(2,1)S(1)}, bf16[4,256,256]{2,1,0:T(8,128)(2,1)S(1)}, f32[3,64,256]{2,1,0:T(8,128)S(1)}, f32[3,64,256]{2,1,0:T(8...) custom-call(s32[2]{0:T(128)S(1)} %pad_add_fusion.place, f32[256,256]{1,0:T(8,128)S(1)} %get-tuple-element.92.refs_0_, ...), custom_call_target="tpu_custom_call" | custom-call | flops 805306368 | bytes 4980744 | tf_op jit(solution)/shard_map/pallas_call | solution.py:34
  37.6 1.6 %collective-permute-start.7 = (f32[3,64,256]{2,1,0:T(8,128)S(1)}, f32[3,64,256]{2,1,0:T(8,128)S(1)}, u32[]{:S(2)}, u32[]{:S(2)}) collective-permute-start(f32[3,64,256]{2,1,0:T(8,128)S(1)} %get-tuple-element.101), channel_id=1, source_target_pairs={{0,8},{2,10},{4,12},{6,14},{8,0},{10,2},{12,4},{14,6},{16,24},{18,... | collective-permute-start | bytes 589832 | tf_op jit(solution)/shard_map/ppermute | solution.py:332
  39.2 2.6 %collective-permute-start.8 = (f32[3,64,256]{2,1,0:T(8,128)S(1)}, f32[3,64,256]{2,1,0:T(8,128)S(1)}, u32[]{:S(2)}, u32[]{:S(2)}) collective-permute-start(f32[3,64,256]{2,1,0:T(8,128)S(1)} %get-tuple-element.102), channel_id=1, source_target_pairs={{0,16},{2,18},{4,20},{6,22},{8,24},{10,26},{12,28},{14,30},{16,0},... | collective-permute-start | bytes 589832 | tf_op jit(solution)/shard_map/ppermute | solution.py:332
  42.0 3.0 %collective-permute-done.7 = f32[3,64,256]{2,1,0:T(8,128)S(1)} collective-permute-done((f32[3,64,256]{2,1,0:T(8,128)S(1)}, f32[3,64,256]{2,1,0:T(8,128)S(1)}, u32[]{:S(2)}, u32[]{:S(2)}) %collective-permute-start.7) | collective-permute-done | bytes 196640 | tf_op jit(solution)/shard_map/ppermute | solution.py:332
  45.0 1.4 collective-permute-start.12
  46.5 10.9 %collective-permute-done.8 = f32[3,64,256]{2,1,0:T(8,128)S(1)} collective-permute-done((f32[3,64,256]{2,1,0:T(8,128)S(1)}, f32[3,64,256]{2,1,0:T(8,128)S(1)}, u32[]{:S(2)}, u32[]{:S(2)}) %collective-permute-start.8) | collective-permute-done | bytes 196640 | tf_op jit(solution)/shard_map/ppermute | solution.py:332
  57.5 2.3 %collective-permute-start.15 = (f32[3,64,256]{2,1,0:T(8,128)S(1)}, f32[3,64,256]{2,1,0:T(8,128)S(1)}, u32[]{:S(2)}, u32[]{:S(2)}) collective-permute-start(f32[3,64,256]{2,1,0:T(8,128)S(1)} %add_add_fusion.1.refs_4_), channel_id=1, source_target_pairs={{0,24},{2,26},{4,28},{6,30},{8,16},{10,18},{12,20},{14,22},{16,8},... | collective-permute-start | bytes 589832 | tf_op jit(solution)/shard_map/ppermute | solution.py:332
  59.8 1.9 %collective-permute-start.14 = (f32[3,64,256]{2,1,0:T(8,128)S(1)}, f32[3,64,256]{2,1,0:T(8,128)S(1)}, u32[]{:S(2)}, u32[]{:S(2)}) collective-permute-start(f32[3,64,256]{2,1,0:T(8,128)S(1)} %add_add_fusion.1.refs_4_), channel_id=1, source_target_pairs={{0,16},{2,18},{4,20},{6,22},{8,24},{10,26},{12,28},{14,30},{16,0},... | collective-permute-start | bytes 589832 | tf_op jit(solution)/shard_map/ppermute | solution.py:332
  61.9 0.6 dynamic_slice.14
  62.5 4.7 %collective-permute-done.15.refs_7_ = f32[3,64,256]{2,1,0:T(8,128)S(1)} collective-permute-done((f32[3,64,256]{2,1,0:T(8,128)S(1)}, f32[3,64,256]{2,1,0:T(8,128)S(1)}, u32[]{:S(2)}, u32[]{:S(2)}) %collective-permute-start.15) | collective-permute-done | bytes 196640 | tf_op jit(solution)/shard_map/ppermute | solution.py:332
  67.2 8.0 %collective-permute-done.14.refs_6_ = f32[3,64,256]{2,1,0:T(8,128)S(1)} collective-permute-done((f32[3,64,256]{2,1,0:T(8,128)S(1)}, f32[3,64,256]{2,1,0:T(8,128)S(1)}, u32[]{:S(2)}, u32[]{:S(2)}) %collective-permute-start.14) | collective-permute-done | bytes 196640 | tf_op jit(solution)/shard_map/ppermute | solution.py:332
  75.1 2.3 %shard_map.149 = (f32[4,256,256]{2,1,0:T(8,128)S(1)}, f32[4,256,256]{2,1,0:T(8,128)S(1)}, f32[4,256,256]{2,1,0:T(8,128)S(1)}, bf16[3,256,256]{2,1,0:T(8,128)(2,1)S(1)}, f32[2,4,256]{2,1,0:T(4,128)S(1)}) custom-call(s32[2]{0:T(128)S(1)} %pad_add_fusion.place, f32[1,1]{1,0:T(1,128)} %bitcast.2.head_scale, f32[2,256,256]{2,1,0:T(8,128)S(1)} %get-tuple-element.107.refs_0_, ...), custom_call_target="tpu_custom_call" | custom-call | flops 402653184 | bytes 6430732 | tf_op jit(solution)/shard_map/pallas_call | solution.py:34
  77.5 1.2 collective-permute-done.16
  78.7 1.4 collective-permute-start.19
  80.1 1.5 collective-permute-start.18
  82.2 1.1 collective-permute-done.19.refs_7_
  83.2 0.5 collective-permute-done.18.refs_6_
  83.8 1.5 collective-permute-done.17.refs_5_
  85.3 3.1 %shard_map.150 = (f32[256,256]{1,0:T(8,128)S(1)}, f32[256,256]{1,0:T(8,128)S(1)}, f32[256,256]{1,0:T(8,128)S(1)}, f32[256,256]{1,0:T(8,128)S(1)}, f32[3,64,256]{...) custom-call(s32[2]{0:T(128)S(1)} %pad_add_fusion.place, ...), custom_call_target="tpu_custom_call" | custom-call | flops 805306368 | bytes 7503884 | tf_op jit(solution)/shard_map/pallas_call | solution.py:34
  88.5 3.2 %collective-permute-start.21 = (f32[3,64,256]{2,1,0:T(8,128)S(1)}, f32[3,64,256]{2,1,0:T(8,128)S(1)}, u32[]{:S(2)}, u32[]{:S(2)}) collective-permute-start(f32[3,64,256]{2,1,0:T(8,128)S(1)} %get-tuple-element.119), channel_id=1, source_target_pairs={{0,16},{2,18},{4,20},{6,22},{8,24},{10,26},{12,28},{14,30},{16,0},... | collective-permute-start | bytes 589832 | tf_op jit(solution)/shard_map/ppermute | solution.py:332
  91.7 1.2 collective-permute-start.22
  93.9 3.0 %collective-permute-done.20 = f32[3,64,256]{2,1,0:T(8,128)S(1)} collective-permute-done((f32[3,64,256]{2,1,0:T(8,128)S(1)}, f32[3,64,256]{2,1,0:T(8,128)S(1)}, u32[]{:S(2)}, u32[]{:S(2)}) %collective-permute-start.20) | collective-permute-done | bytes 196640 | tf_op jit(solution)/shard_map/ppermute | solution.py:332
  96.9 0.7 collective-permute-start.25
  97.5 8.1 %collective-permute-done.21 = f32[3,64,256]{2,1,0:T(8,128)S(1)} collective-permute-done((f32[3,64,256]{2,1,0:T(8,128)S(1)}, f32[3,64,256]{2,1,0:T(8,128)S(1)}, u32[]{:S(2)}, u32[]{:S(2)}) %collective-permute-start.21) | collective-permute-done | bytes 196640 | tf_op jit(solution)/shard_map/ppermute | solution.py:332
  105.7 2.3 %collective-permute-start.28 = (f32[3,64,256]{2,1,0:T(8,128)S(1)}, f32[3,64,256]{2,1,0:T(8,128)S(1)}, u32[]{:S(2)}, u32[]{:S(2)}) collective-permute-start(f32[3,64,256]{2,1,0:T(8,128)S(1)} %add_add_fusion.refs_2_.refs_0_), channel_id=1, source_target_pairs={{0,24},{2,26},{4,28},{6,30},{8,16},{10,18},{12,20},{14,22},{16,8},... | collective-permute-start | bytes 589832 | tf_op jit(solution)/shard_map/ppermute | solution.py:332
  108.0 7.3 %collective-permute-start.27 = (f32[3,64,256]{2,1,0:T(8,128)S(1)}, f32[3,64,256]{2,1,0:T(8,128)S(1)}, u32[]{:S(2)}, u32[]{:S(2)}) collective-permute-start(f32[3,64,256]{2,1,0:T(8,128)S(1)} %add_add_fusion.refs_2_.refs_0_), channel_id=1, source_target_pairs={{0,16},{2,18},{4,20},{6,22},{8,24},{10,26},{12,28},{14,30},{16,0},... | collective-permute-start | bytes 589832 | tf_op jit(solution)/shard_map/ppermute | solution.py:332
  115.8 1.7 %shard_map.151 = bf16[256,4,256]{2,1,0:T(4,128)(2,1)} custom-call(s32[2]{0:T(128)S(1)} %pad_add_fusion.place, f32[256,256]{1,0:T(8,128)S(1)} %get-tuple-element.126.refs_0_, f32[256,256]{1,0:T(8,128)S(1)} %collective-permute-done.23.refs_1_, f32[256,256]{1,0:T(8,128)S(1)} %collective-permute-done.24.refs_2_, f32[256,256]{1,0:T(8,128)S(1)} %collective-permute-done.25.refs_3_), custom_call_target="tpu_custom_call" | custom-call | flops 8388608 | bytes 1572872 | tf_op jit(solution)/shard_map/pallas_call | solution.py:34
  117.5 7.0 %collective-permute-done.27.refs_4_ = f32[3,64,256]{2,1,0:T(8,128)S(1)} collective-permute-done((f32[3,64,256]{2,1,0:T(8,128)S(1)}, f32[3,64,256]{2,1,0:T(8,128)S(1)}, u32[]{:S(2)}, u32[]{:S(2)}) %collective-permute-start.27) | collective-permute-done | bytes 196640 | tf_op jit(solution)/shard_map/ppermute | solution.py:332
  124.6 3.7 %shard_map.152 = (f32[2,256,256]{2,1,0:T(8,128)S(1)}, f32[2,256,256]{2,1,0:T(8,128)S(1)}, f32[2,256,256]{2,1,0:T(8,128)S(1)}, f32[256,256]{1,0:T(8,128)S(1)}, f3...) custom-call(s32[2]{0:T(128)S(1)} %pad_add_fusion.place, ...), custom_call_target="tpu_custom_call" | custom-call | flops 2013265920 | bytes 5505032 | tf_op jit(solution)/shard_map/pallas_call | solution.py:34
  128.4 0.8 collective-permute-start.31
  129.2 1.5 collective-permute-start.33
  130.7 1.1 collective-permute-start.29
  131.7 0.8 collective-permute-start.30
  132.5 4.7 %collective-permute-done.31 = f32[256,256]{1,0:T(8,128)S(1)} collective-permute-done((f32[256,256]{1,0:T(8,128)S(1)}, f32[256,256]{1,0:T(8,128)S(1)}, u32[]{:S(2)}, u32[]{:S(2)}) %collective-permute-start.31) | collective-permute-done | bytes 262176 | tf_op jit(solution)/shard_map/ppermute | solution.py:332
  137.2 1.7 %collective-permute-start.32 = (f32[256,256]{1,0:T(8,128)S(1)}, f32[256,256]{1,0:T(8,128)S(1)}, u32[]{:S(2)}, u32[]{:S(2)}) collective-permute-start(f32[256,256]{1,0:T(8,128)S(1)} %collective-permute-done.31), channel_id=1, source_target_pairs={{0,4},{2,6},{4,0},{6,2},{8,12},{10,14},{12,8},{14,10},{16,20},{18,... | collective-permute-start | bytes 786440 | tf_op jit(solution)/shard_map/ppermute | solution.py:332
  138.9 0.9 collective-permute-start.34
  139.9 3.1 %collective-permute-start.36 = (f32[1,3,64,256]{3,2,1,0:T(8,128)S(1)}, f32[1,3,64,256]{3,2,1,0:T(8,128)S(1)}, u32[]{:S(2)}, u32[]{:S(2)}) collective-permute-start(f32[1,3,64,256]{3,2,1,0:T(8,128)S(1)} %get-tuple-element.154), channel_id=1, source_target_pairs={{0,16},{2,18},{4,20},{6,22},{8,24},{10,26},{12,28},{14,30},{16,0},... | collective-permute-start | bytes 589832 | tf_op jit(solution)/shard_map/ppermute | solution.py:332
  143.0 6.3 %collective-permute-done.36.refs_3_ = f32[1,3,64,256]{3,2,1,0:T(8,128)S(1)} collective-permute-done((f32[1,3,64,256]{3,2,1,0:T(8,128)S(1)}, f32[1,3,64,256]{3,2,1,0:T(8,128)S(1)}, u32[]{:S(2)}, u32[]{:S(2)}) %collective-permute-start.36) | collective-permute-done | bytes 196640 | tf_op jit(solution)/shard_map/ppermute | solution.py:332
  149.4 0.6 shard_map.154
  150.0 0.9 collective-permute-start.37
  150.8 2.7 %collective-permute-done.32.refs_3_ = f32[256,256]{1,0:T(8,128)S(1)} collective-permute-done((f32[256,256]{1,0:T(8,128)S(1)}, f32[256,256]{1,0:T(8,128)S(1)}, u32[]{:S(2)}, u32[]{:S(2)}) %collective-permute-start.32) | collective-permute-done | bytes 262176 | tf_op jit(solution)/shard_map/ppermute | solution.py:332
  153.5 1.7 %collective-permute-start.38 = (f32[3,16,256]{2,1,0:T(8,128)S(1)}, f32[3,16,256]{2,1,0:T(8,128)S(1)}, u32[]{:S(2)}, u32[]{:S(2)}) collective-permute-start(f32[3,16,256]{2,1,0:T(8,128)S(1)} %get-tuple-element.149), channel_id=1, source_target_pairs={{0,4},{2,6},{4,0},{6,2},{8,12},{10,14},{12,8},{14,10},{16,20},{18,... | collective-permute-start | bytes 147464 | tf_op jit(solution)/shard_map/ppermute | solution.py:332
  155.3 0.8 collective-permute-start.39
  156.1 2.4 %shard_map.153 = (bf16[256,4,256]{2,1,0:T(4,128)(2,1)}, bf16[256,4,256]{2,1,0:T(4,128)(2,1)}) custom-call(s32[2]{0:T(128)S(1)} %pad_add_fusion.place, f32[4,256]{1,0:T(4,128)S(1)} %bitcast.22, f32[2,256,256]{2,1,0:T(8,128)S(1)} %get-tuple-element.137.refs_0_, f32[2,256,256]{2,1,0:T(8,128)S(1)} %collective-permute-done.29.refs_1_, ...), custom_call_target="tpu_custom_call" | custom-call | flops 16777216 | bytes 3149832 | tf_op jit(solution)/shard_map/pallas_call | solution.py:34
  158.5 1.8 %collective-permute-done.39.refs_3_ = f32[3,16,256]{2,1,0:T(8,128)S(1)} collective-permute-done((f32[3,16,256]{2,1,0:T(8,128)S(1)}, f32[3,16,256]{2,1,0:T(8,128)S(1)}, u32[]{:S(2)}, u32[]{:S(2)}) %collective-permute-start.39) | collective-permute-done | bytes 49184 | tf_op jit(solution)/shard_map/ppermute | solution.py:332
  160.3 1.2 shard_map.155
  (51 shorter events, 3.4 us)
Async XLA Ops:
  0.6 20.1 %copy-start = (f32[4,256,256]{2,1,0:T(8,128)S(1)}, f32[4,256,256]{2,1,0:T(8,128)}, u32[]{:S(2)}) copy-start(f32[4,256,256]{2,1,0:T(8,128)} %param.16) | copy-start | bytes 3145732
  0.7 1.1 copy-start.1
  1.8 4.5 %copy-start.2 = (bf16[1,256,4,256]{3,2,1,0:T(4,128)(2,1)S(1)}, bf16[1,256,4,256]{3,2,1,0:T(4,128)(2,1)}, u32[]{:S(2)}) copy-start(bf16[1,256,4,256]{3,2,1,0:T(4,128)(2,1)} %param.12) | copy-start | bytes 1572868
  1.8 4.5 %copy-start.5 = (f32[1,4,256]{2,1,0:T(4,128)S(1)}, f32[1,4,256]{2,1,0:T(4,128)}, u32[]{:S(2)}) copy-start(f32[1,4,256]{2,1,0:T(4,128)} %param.13) | copy-start | bytes 12292
  3.4 14.2 %copy-start.3 = (bf16[1,256,4,256]{3,2,1,0:T(4,128)(2,1)S(1)}, bf16[1,256,4,256]{3,2,1,0:T(4,128)(2,1)}, u32[]{:S(2)}) copy-start(bf16[1,256,4,256]{3,2,1,0:T(4,128)(2,1)} %param.10) | copy-start | bytes 1572868
  3.4 10.1 %collective-permute-start.2 = (f32[256,256]{1,0:T(8,128)S(1)}, f32[256,256]{1,0:T(8,128)}, u32[]{:S(2)}, u32[]{:S(2)}) collective-permute-start(f32[256,256]{1,0:T(8,128)S(1)} %get-tuple-element.84), channel_id=1, source_target_pairs={{0,2},{2,0},{4,6},{6,4},{8,10},{10,8},{12,14},{14,12},{16,18},{18,... | collective-permute-start | bytes 786440 | tf_op jit(solution)/shard_map/ppermute | solution.py:332
  8.3 9.3 %collective-permute-start.5 = (f32[256,256]{1,0:T(8,128)S(1)}, f32[256,256]{1,0:T(8,128)}, u32[]{:S(2)}, u32[]{:S(2)}) collective-permute-start(f32[256,256]{1,0:T(8,128)S(1)} %get-tuple-element.87), channel_id=1, source_target_pairs={{0,4},{2,6},{4,0},{6,2},{8,12},{10,14},{12,8},{14,10},{16,20},{18,... | collective-permute-start | bytes 786440 | tf_op jit(solution)/shard_map/ppermute | solution.py:332
  9.8 23.1 %collective-permute-start = (f32[2,256,256]{2,1,0:T(8,128)}, f32[2,256,256]{2,1,0:T(8,128)S(1)}, u32[]{:S(2)}, u32[]{:S(2)}) collective-permute-start(f32[2,256,256]{2,1,0:T(8,128)} %get-tuple-element.82), channel_id=1, source_target_pairs={{0,2},{2,0},{4,6},{6,4},{8,10},{10,8},{12,14},{14,12},{16,18},{18,... | collective-permute-start | bytes 1572872 | tf_op jit(solution)/shard_map/ppermute | solution.py:332
  10.4 12.8 %collective-permute-start.1 = (f32[256,256]{1,0:T(8,128)}, f32[256,256]{1,0:T(8,128)S(1)}, u32[]{:S(2)}, u32[]{:S(2)}) collective-permute-start(f32[256,256]{1,0:T(8,128)} %get-tuple-element.83), channel_id=1, source_target_pairs={{0,4},{2,6},{4,0},{6,2},{8,12},{10,14},{12,8},{14,10},{16,20},{18,... | collective-permute-start | bytes 786440 | tf_op jit(solution)/shard_map/ppermute | solution.py:332
  10.4 18.4 %collective-permute-start.4 = (f32[256,256]{1,0:T(8,128)}, f32[256,256]{1,0:T(8,128)S(1)}, u32[]{:S(2)}, u32[]{:S(2)}) collective-permute-start(f32[256,256]{1,0:T(8,128)} %get-tuple-element.86), channel_id=1, source_target_pairs={{0,4},{2,6},{4,0},{6,2},{8,12},{10,14},{12,8},{14,10},{16,20},{18,... | collective-permute-start | bytes 786440 | tf_op jit(solution)/shard_map/ppermute | solution.py:332
  13.5 19.4 %collective-permute-start.3 = (f32[256,256]{1,0:T(8,128)}, f32[256,256]{1,0:T(8,128)S(1)}, u32[]{:S(2)}, u32[]{:S(2)}) collective-permute-start(f32[256,256]{1,0:T(8,128)} %collective-permute-done.2), channel_id=1, source_target_pairs={{0,4},{2,6},{4,0},{6,2},{8,12},{10,14},{12,8},{14,10},{16,20},{18,... | collective-permute-start | bytes 786440 | tf_op jit(solution)/shard_map/ppermute | solution.py:332
  17.6 15.3 %collective-permute-start.6 = (f32[256,256]{1,0:T(8,128)}, f32[256,256]{1,0:T(8,128)}, u32[]{:S(2)}, u32[]{:S(2)}) collective-permute-start(f32[256,256]{1,0:T(8,128)} %collective-permute-done.5), channel_id=1, source_target_pairs={{0,2},{2,0},{4,6},{6,4},{8,10},{10,8},{12,14},{14,12},{16,18},{18,... | collective-permute-start | bytes 786440 | tf_op jit(solution)/shard_map/ppermute | solution.py:332
  17.7 0.7 copy-start.6
  18.3 1.0 copy-start.4
  32.9 24.5 %collective-permute-start.10 = (f32[2,256,256]{2,1,0:T(8,128)S(1)}, f32[2,256,256]{2,1,0:T(8,128)S(1)}, u32[]{:S(2)}, u32[]{:S(2)}) collective-permute-start(f32[2,256,256]{2,1,0:T(8,128)S(1)} %get-tuple-element.105), channel_id=1, source_target_pairs={{0,2},{2,0},{4,6},{6,4},{8,10},{10,8},{12,14},{14,12},{16,18},{18,... | collective-permute-start | bytes 1572872 | tf_op jit(solution)/shard_map/ppermute | solution.py:332
  33.3 24.2 %collective-permute-start.11 = (f32[2,256,256]{2,1,0:T(8,128)S(1)}, f32[2,256,256]{2,1,0:T(8,128)S(1)}, u32[]{:S(2)}, u32[]{:S(2)}) collective-permute-start(f32[2,256,256]{2,1,0:T(8,128)S(1)} %get-tuple-element.106), channel_id=1, source_target_pairs={{0,4},{2,6},{4,0},{6,2},{8,12},{10,14},{12,8},{14,10},{16,20},{18,... | collective-permute-start | bytes 1572872 | tf_op jit(solution)/shard_map/ppermute | solution.py:332
  37.6 7.5 %collective-permute-start.7 = (f32[3,64,256]{2,1,0:T(8,128)S(1)}, f32[3,64,256]{2,1,0:T(8,128)S(1)}, u32[]{:S(2)}, u32[]{:S(2)}) collective-permute-start(f32[3,64,256]{2,1,0:T(8,128)S(1)} %get-tuple-element.101), channel_id=1, source_target_pairs={{0,8},{2,10},{4,12},{6,14},{8,0},{10,2},{12,4},{14,6},{16,24},{18,... | collective-permute-start | bytes 589832 | tf_op jit(solution)/shard_map/ppermute | solution.py:332
  39.2 18.1 %collective-permute-start.8 = (f32[3,64,256]{2,1,0:T(8,128)S(1)}, f32[3,64,256]{2,1,0:T(8,128)S(1)}, u32[]{:S(2)}, u32[]{:S(2)}) collective-permute-start(f32[3,64,256]{2,1,0:T(8,128)S(1)} %get-tuple-element.102), channel_id=1, source_target_pairs={{0,16},{2,18},{4,20},{6,22},{8,24},{10,26},{12,28},{14,30},{16,0},... | collective-permute-start | bytes 589832 | tf_op jit(solution)/shard_map/ppermute | solution.py:332
  41.8 15.6 %collective-permute-start.9 = (f32[3,64,256]{2,1,0:T(8,128)S(1)}, f32[3,64,256]{2,1,0:T(8,128)S(1)}, u32[]{:S(2)}, u32[]{:S(2)}) collective-permute-start(f32[3,64,256]{2,1,0:T(8,128)S(1)} %get-tuple-element.103), channel_id=1, source_target_pairs={{0,24},{2,26},{4,28},{6,30},{8,16},{10,18},{12,20},{14,22},{16,8},... | collective-permute-start | bytes 589832 | tf_op jit(solution)/shard_map/ppermute | solution.py:332
  45.0 17.5 %collective-permute-start.12 = (f32[2,256,256]{2,1,0:T(8,128)S(1)}, f32[2,256,256]{2,1,0:T(8,128)S(1)}, u32[]{:S(2)}, u32[]{:S(2)}) collective-permute-start(f32[2,256,256]{2,1,0:T(8,128)S(1)} %get-tuple-element.110), channel_id=1, source_target_pairs={{0,6},{2,4},{4,2},{6,0},{8,14},{10,12},{12,10},{14,8},{16,22},{18,... | collective-permute-start | bytes 1572872 | tf_op jit(solution)/shard_map/ppermute | solution.py:332
  57.4 4.5 %copy-start.7 = (f32[4]{0:T(128)S(1)}, f32[4]{0:T(128)}, u32[]{:S(2)}) copy-start(f32[4]{0:T(128)} %param.14) | copy-start | bytes 52
  57.5 9.7 %collective-permute-start.15 = (f32[3,64,256]{2,1,0:T(8,128)S(1)}, f32[3,64,256]{2,1,0:T(8,128)S(1)}, u32[]{:S(2)}, u32[]{:S(2)}) collective-permute-start(f32[3,64,256]{2,1,0:T(8,128)S(1)} %add_add_fusion.1.refs_4_), channel_id=1, source_target_pairs={{0,24},{2,26},{4,28},{6,30},{8,16},{10,18},{12,20},{14,22},{16,8},... | collective-permute-start | bytes 589832 | tf_op jit(solution)/shard_map/ppermute | solution.py:332
  59.8 15.3 %collective-permute-start.14 = (f32[3,64,256]{2,1,0:T(8,128)S(1)}, f32[3,64,256]{2,1,0:T(8,128)S(1)}, u32[]{:S(2)}, u32[]{:S(2)}) collective-permute-start(f32[3,64,256]{2,1,0:T(8,128)S(1)} %add_add_fusion.1.refs_4_), channel_id=1, source_target_pairs={{0,16},{2,18},{4,20},{6,22},{8,24},{10,26},{12,28},{14,30},{16,0},... | collective-permute-start | bytes 589832 | tf_op jit(solution)/shard_map/ppermute | solution.py:332
  61.7 13.5 %collective-permute-start.13 = (f32[3,64,256]{2,1,0:T(8,128)S(1)}, f32[3,64,256]{2,1,0:T(8,128)S(1)}, u32[]{:S(2)}, u32[]{:S(2)}) collective-permute-start(f32[3,64,256]{2,1,0:T(8,128)S(1)} %add_add_fusion.1.refs_4_), channel_id=1, source_target_pairs={{0,8},{2,10},{4,12},{6,14},{8,0},{10,2},{12,4},{14,6},{16,24},{18,... | collective-permute-start | bytes 589832 | tf_op jit(solution)/shard_map/ppermute | solution.py:332
  77.5 1.2 collective-permute-start.16
  78.7 4.5 %collective-permute-start.19 = (f32[2,4,256]{2,1,0:T(4,128)S(1)}, f32[2,4,256]{2,1,0:T(4,128)S(1)}, u32[]{:S(2)}, u32[]{:S(2)}) collective-permute-start(f32[2,4,256]{2,1,0:T(4,128)S(1)} %add.36.refs_4_), channel_id=1, source_target_pairs={{0,6},{2,4},{4,2},{6,0},{8,14},{10,12},{12,10},{14,8},{16,22},{18,... | collective-permute-start | bytes 24584 | tf_op jit(solution)/shard_map/ppermute | solution.py:332
  80.1 3.7 %collective-permute-start.18 = (f32[2,4,256]{2,1,0:T(4,128)S(1)}, f32[2,4,256]{2,1,0:T(4,128)S(1)}, u32[]{:S(2)}, u32[]{:S(2)}) collective-permute-start(f32[2,4,256]{2,1,0:T(4,128)S(1)} %add.36.refs_4_), channel_id=1, source_target_pairs={{0,4},{2,6},{4,0},{6,2},{8,12},{10,14},{12,8},{14,10},{16,20},{18,... | collective-permute-start | bytes 24584 | tf_op jit(solution)/shard_map/ppermute | solution.py:332
  81.6 3.7 %collective-permute-start.17 = (f32[2,4,256]{2,1,0:T(4,128)S(1)}, f32[2,4,256]{2,1,0:T(4,128)S(1)}, u32[]{:S(2)}, u32[]{:S(2)}) collective-permute-start(f32[2,4,256]{2,1,0:T(4,128)S(1)} %add.36.refs_4_), channel_id=1, source_target_pairs={{0,2},{2,0},{4,6},{6,4},{8,10},{10,8},{12,14},{14,12},{16,18},{18,... | collective-permute-start | bytes 24584 | tf_op jit(solution)/shard_map/ppermute | solution.py:332
  88.4 8.5 %collective-permute-start.20 = (f32[3,64,256]{2,1,0:T(8,128)S(1)}, f32[3,64,256]{2,1,0:T(8,128)S(1)}, u32[]{:S(2)}, u32[]{:S(2)}) collective-permute-start(f32[3,64,256]{2,1,0:T(8,128)S(1)} %get-tuple-element.118), channel_id=1, source_target_pairs={{0,8},{2,10},{4,12},{6,14},{8,0},{10,2},{12,4},{14,6},{16,24},{18,... | collective-permute-start | bytes 589832 | tf_op jit(solution)/shard_map/ppermute | solution.py:332
  88.5 17.1 %collective-permute-start.21 = (f32[3,64,256]{2,1,0:T(8,128)S(1)}, f32[3,64,256]{2,1,0:T(8,128)S(1)}, u32[]{:S(2)}, u32[]{:S(2)}) collective-permute-start(f32[3,64,256]{2,1,0:T(8,128)S(1)} %get-tuple-element.119), channel_id=1, source_target_pairs={{0,16},{2,18},{4,20},{6,22},{8,24},{10,26},{12,28},{14,30},{16,0},... | collective-permute-start | bytes 589832 | tf_op jit(solution)/shard_map/ppermute | solution.py:332
  91.7 13.9 %collective-permute-start.22 = (f32[3,64,256]{2,1,0:T(8,128)S(1)}, f32[3,64,256]{2,1,0:T(8,128)S(1)}, u32[]{:S(2)}, u32[]{:S(2)}) collective-permute-start(f32[3,64,256]{2,1,0:T(8,128)S(1)} %get-tuple-element.120), channel_id=1, source_target_pairs={{0,24},{2,26},{4,28},{6,30},{8,16},{10,18},{12,20},{14,22},{16,8},... | collective-permute-start | bytes 589832 | tf_op jit(solution)/shard_map/ppermute | solution.py:332
  92.8 12.8 %collective-permute-start.23 = (f32[256,256]{1,0:T(8,128)S(1)}, f32[256,256]{1,0:T(8,128)S(1)}, u32[]{:S(2)}, u32[]{:S(2)}) collective-permute-start(f32[256,256]{1,0:T(8,128)S(1)} %get-tuple-element.122), channel_id=1, source_target_pairs={{0,2},{2,0},{4,6},{6,4},{8,10},{10,8},{12,14},{14,12},{16,18},{18,... | collective-permute-start | bytes 786440 | tf_op jit(solution)/shard_map/ppermute | solution.py:332
  93.4 12.3 %collective-permute-start.24 = (f32[256,256]{1,0:T(8,128)S(1)}, f32[256,256]{1,0:T(8,128)S(1)}, u32[]{:S(2)}, u32[]{:S(2)}) collective-permute-start(f32[256,256]{1,0:T(8,128)S(1)} %get-tuple-element.123), channel_id=1, source_target_pairs={{0,4},{2,6},{4,0},{6,2},{8,12},{10,14},{12,8},{14,10},{16,20},{18,... | collective-permute-start | bytes 786440 | tf_op jit(solution)/shard_map/ppermute | solution.py:332
  96.9 8.8 %collective-permute-start.25 = (f32[256,256]{1,0:T(8,128)S(1)}, f32[256,256]{1,0:T(8,128)S(1)}, u32[]{:S(2)}, u32[]{:S(2)}) collective-permute-start(f32[256,256]{1,0:T(8,128)S(1)} %get-tuple-element.124), channel_id=1, source_target_pairs={{0,6},{2,4},{4,2},{6,0},{8,14},{10,12},{12,10},{14,8},{16,22},{18,... | collective-permute-start | bytes 786440 | tf_op jit(solution)/shard_map/ppermute | solution.py:332
  105.7 11.9 %collective-permute-start.28 = (f32[3,64,256]{2,1,0:T(8,128)S(1)}, f32[3,64,256]{2,1,0:T(8,128)S(1)}, u32[]{:S(2)}, u32[]{:S(2)}) collective-permute-start(f32[3,64,256]{2,1,0:T(8,128)S(1)} %add_add_fusion.refs_2_.refs_0_), channel_id=1, source_target_pairs={{0,24},{2,26},{4,28},{6,30},{8,16},{10,18},{12,20},{14,22},{16,8},... | collective-permute-start | bytes 589832 | tf_op jit(solution)/shard_map/ppermute | solution.py:332
  108.0 16.6 %collective-permute-start.27 = (f32[3,64,256]{2,1,0:T(8,128)S(1)}, f32[3,64,256]{2,1,0:T(8,128)S(1)}, u32[]{:S(2)}, u32[]{:S(2)}) collective-permute-start(f32[3,64,256]{2,1,0:T(8,128)S(1)} %add_add_fusion.refs_2_.refs_0_), channel_id=1, source_target_pairs={{0,16},{2,18},{4,20},{6,22},{8,24},{10,26},{12,28},{14,30},{16,0},... | collective-permute-start | bytes 589832 | tf_op jit(solution)/shard_map/ppermute | solution.py:332
  115.3 9.3 %collective-permute-start.26 = (f32[3,64,256]{2,1,0:T(8,128)S(1)}, f32[3,64,256]{2,1,0:T(8,128)S(1)}, u32[]{:S(2)}, u32[]{:S(2)}) collective-permute-start(f32[3,64,256]{2,1,0:T(8,128)S(1)} %add_add_fusion.refs_2_.refs_0_), channel_id=1, source_target_pairs={{0,8},{2,10},{4,12},{6,14},{8,0},{10,2},{12,4},{14,6},{16,24},{18,... | collective-permute-start | bytes 589832 | tf_op jit(solution)/shard_map/ppermute | solution.py:332
  128.3 11.5 %collective-permute-start.35 = (f32[2,3,64,256]{3,2,1,0:T(8,128)S(1)}, f32[2,3,64,256]{3,2,1,0:T(8,128)S(1)}, u32[]{:S(2)}, u32[]{:S(2)}) collective-permute-start(f32[2,3,64,256]{3,2,1,0:T(8,128)S(1)} %get-tuple-element.145), channel_id=1, source_target_pairs={{0,8},{2,10},{4,12},{6,14},{8,0},{10,2},{12,4},{14,6},{16,24},{18,... | collective-permute-start | bytes 1179656 | tf_op jit(solution)/shard_map/ppermute | solution.py:332
  128.4 8.8 %collective-permute-start.31 = (f32[256,256]{1,0:T(8,128)S(1)}, f32[256,256]{1,0:T(8,128)S(1)}, u32[]{:S(2)}, u32[]{:S(2)}) collective-permute-start(f32[256,256]{1,0:T(8,128)S(1)} %get-tuple-element.140), channel_id=1, source_target_pairs={{0,2},{2,0},{4,6},{6,4},{8,10},{10,8},{12,14},{14,12},{16,18},{18,... | collective-permute-start | bytes 786440 | tf_op jit(solution)/shard_map/ppermute | solution.py:332
  129.2 9.8 %collective-permute-start.33 = (f32[256,256]{1,0:T(8,128)S(1)}, f32[256,256]{1,0:T(8,128)S(1)}, u32[]{:S(2)}, u32[]{:S(2)}) collective-permute-start(f32[256,256]{1,0:T(8,128)S(1)} %get-tuple-element.141), channel_id=1, source_target_pairs={{0,4},{2,6},{4,0},{6,2},{8,12},{10,14},{12,8},{14,10},{16,20},{18,... | collective-permute-start | bytes 786440 | tf_op jit(solution)/shard_map/ppermute | solution.py:332
  130.7 25.4 %collective-permute-start.29 = (f32[2,256,256]{2,1,0:T(8,128)S(1)}, f32[2,256,256]{2,1,0:T(8,128)S(1)}, u32[]{:S(2)}, u32[]{:S(2)}) collective-permute-start(f32[2,256,256]{2,1,0:T(8,128)S(1)} %get-tuple-element.138), channel_id=1, source_target_pairs={{0,2},{2,0},{4,6},{6,4},{8,10},{10,8},{12,14},{14,12},{16,18},{18,... | collective-permute-start | bytes 1572872 | tf_op jit(solution)/shard_map/ppermute | solution.py:332
  131.7 24.3 %collective-permute-start.30 = (f32[2,256,256]{2,1,0:T(8,128)S(1)}, f32[2,256,256]{2,1,0:T(8,128)S(1)}, u32[]{:S(2)}, u32[]{:S(2)}) collective-permute-start(f32[2,256,256]{2,1,0:T(8,128)S(1)} %get-tuple-element.139), channel_id=1, source_target_pairs={{0,4},{2,6},{4,0},{6,2},{8,12},{10,14},{12,8},{14,10},{16,20},{18,... | collective-permute-start | bytes 1572872 | tf_op jit(solution)/shard_map/ppermute | solution.py:332
  137.2 16.3 %collective-permute-start.32 = (f32[256,256]{1,0:T(8,128)S(1)}, f32[256,256]{1,0:T(8,128)S(1)}, u32[]{:S(2)}, u32[]{:S(2)}) collective-permute-start(f32[256,256]{1,0:T(8,128)S(1)} %collective-permute-done.31), channel_id=1, source_target_pairs={{0,4},{2,6},{4,0},{6,2},{8,12},{10,14},{12,8},{14,10},{16,20},{18,... | collective-permute-start | bytes 786440 | tf_op jit(solution)/shard_map/ppermute | solution.py:332
  138.9 16.4 %collective-permute-start.34 = (f32[256,256]{1,0:T(8,128)S(1)}, f32[256,256]{1,0:T(8,128)S(1)}, u32[]{:S(2)}, u32[]{:S(2)}) collective-permute-start(f32[256,256]{1,0:T(8,128)S(1)} %collective-permute-done.33), channel_id=1, source_target_pairs={{0,2},{2,0},{4,6},{6,4},{8,10},{10,8},{12,14},{14,12},{16,18},{18,... | collective-permute-start | bytes 786440 | tf_op jit(solution)/shard_map/ppermute | solution.py:332
  139.9 9.5 %collective-permute-start.36 = (f32[1,3,64,256]{3,2,1,0:T(8,128)S(1)}, f32[1,3,64,256]{3,2,1,0:T(8,128)S(1)}, u32[]{:S(2)}, u32[]{:S(2)}) collective-permute-start(f32[1,3,64,256]{3,2,1,0:T(8,128)S(1)} %get-tuple-element.154), channel_id=1, source_target_pairs={{0,16},{2,18},{4,20},{6,22},{8,24},{10,26},{12,28},{14,30},{16,0},... | collective-permute-start | bytes 589832 | tf_op jit(solution)/shard_map/ppermute | solution.py:332
  150.0 8.5 %collective-permute-start.37 = (f32[3,16,256]{2,1,0:T(8,128)S(1)}, f32[3,16,256]{2,1,0:T(8,128)S(1)}, u32[]{:S(2)}, u32[]{:S(2)}) collective-permute-start(f32[3,16,256]{2,1,0:T(8,128)S(1)} %get-tuple-element.148), channel_id=1, source_target_pairs={{0,2},{2,0},{4,6},{6,4},{8,10},{10,8},{12,14},{14,12},{16,18},{18,... | collective-permute-start | bytes 147464 | tf_op jit(solution)/shard_map/ppermute | solution.py:332
  153.5 4.9 %collective-permute-start.38 = (f32[3,16,256]{2,1,0:T(8,128)S(1)}, f32[3,16,256]{2,1,0:T(8,128)S(1)}, u32[]{:S(2)}, u32[]{:S(2)}) collective-permute-start(f32[3,16,256]{2,1,0:T(8,128)S(1)} %get-tuple-element.149), channel_id=1, source_target_pairs={{0,4},{2,6},{4,0},{6,2},{8,12},{10,14},{12,8},{14,10},{16,20},{18,... | collective-permute-start | bytes 147464 | tf_op jit(solution)/shard_map/ppermute | solution.py:332
  155.3 5.0 %collective-permute-start.39 = (f32[3,16,256]{2,1,0:T(8,128)S(1)}, f32[3,16,256]{2,1,0:T(8,128)S(1)}, u32[]{:S(2)}, u32[]{:S(2)}) collective-permute-start(f32[3,16,256]{2,1,0:T(8,128)S(1)} %get-tuple-element.150), channel_id=1, source_target_pairs={{0,6},{2,4},{4,2},{6,0},{8,14},{10,12},{12,10},{14,8},{16,22},{18,... | collective-permute-start | bytes 147464 | tf_op jit(solution)/shard_map/ppermute | solution.py:332

commit v7 on v3

--- a/solution.py
+++ b/solution.py
@@ -11,7 +11,7 @@
 F32 = jnp.float32
 BF16 = jnp.bfloat16
 LANES = 128
-VMEM_LIMIT = 40 * 1024 * 1024
+VMEM_LIMIT = 24 * 1024 * 1024
 
 
 def mm(a, b):
@@ -89,22 +89,31 @@
     return jnp.broadcast_to(r[pl.ds(head, 1), :], (8, r.shape[1])).T[:, 0:1]
 
 
-def send_slices(sums, outs, layer):
-    rows = sums.shape[1] // len(outs)
-    for step, out in enumerate(outs):
-        at = pl.multiple_of((layer ^ step) * rows, rows)
-        out[...] = sums[:, pl.ds(at, rows), :]
+def send_groups(count):
+    odd = list(range(3, count, 2))
+    return ([odd] if odd else []) + [[r] for r in [1] + list(range(2, count, 2)) if r < count] + [[0]]
+
+
+def send_slices(sums, outs, own, count):
+    rows = sums.shape[1] // count
+    for out, members in zip(outs, send_groups(count)):
+        for i, step in enumerate(members):
+            at = pl.multiple_of((own ^ step) * rows, rows)
+            out[i] = sums[:, pl.ds(at, rows), :]
 
 
 def update_kernel(groups, depth, scale, place, *refs):
     keys_in, scaled_in = refs[:groups], refs[groups : 2 * groups]
     w_gate, w_out, w_up = refs[2 * groups : 2 * groups + 3]
-    outs, sums = refs[2 * groups + 3 : -1], refs[-1]
+    key_kept, scaled_kept = refs[2 * groups + 3 : 2 * groups + 5]
+    outs, sums = refs[2 * groups + 5 : -1], refs[-1]
     gate_b, out_b, up_b = (w[...].astype(BF16) for w in (w_gate, w_out, w_up))
     total = [0.0, 0.0, 0.0]
-    for key, value in zip(keys_in, scaled_in):
-        keys = key[...].astype(BF16)
-        scaled = value[...].astype(BF16)
+    for step in range(groups):
+        keys = keys_in[step][...].astype(BF16)
+        scaled = scaled_in[step][...].astype(BF16)
+        key_kept[step] = keys
+        scaled_kept[step] = scaled
         first = mm(keys, gate_b)
         third = mm(keys, up_b)
         sig = jax.nn.sigmoid(first)
@@ -119,18 +128,18 @@
         total[2] += tmm(keys, dthird)
     for i in range(3):
         sums[i] = total[i] * scale
-    send_slices(sums, outs, place[1])
+    send_slices(sums, outs, place[1], depth)
     rows = sums.shape[1] // depth
     at = pl.multiple_of(place[1] * rows, rows)
     for i, w in enumerate((w_gate, w_out, w_up)):
-        outs[0][i] += w[pl.ds(at, rows), :]
+        outs[-1][0, i] += w[pl.ds(at, rows), :]
 
 
 def assemble(place, parts, whole):
-    rows = parts[0].shape[1]
+    rows = parts[0].shape[2]
     for step, part in enumerate(parts):
         at = pl.multiple_of((place[1] ^ step) * rows, rows)
-        whole[:, pl.ds(at, rows), :] = part[...]
+        whole[:, pl.ds(at, rows), :] = part[0]
 
 
 def apply_kernel(groups, depth, place, head_scale, *refs):
@@ -158,7 +167,7 @@
         stats[1, pl.ds(source, 1), :] = both[1:2, :]
 
 
-def apply_back_kernel(groups, count, place, head_scale, *refs):
+def apply_back_kernel(groups, depth, count, place, head_scale, *refs):
     pieces = refs[:groups]
     stats = refs[groups : 2 * groups]
     first_ref, third_ref, os_ref, new_b = refs[2 * groups : 2 * groups + 4]
@@ -193,22 +202,14 @@
         total[2] += tmm(queries, dthird)
     for i in range(3):
         sums[i] = total[i]
-    send_slices(sums, slices, place[1])
-
-
-def halving_order(depth):
-    sets, bit = [], 1
-    while bit < depth:
-        sets.append(list(range(bit, depth, 2 * bit)))
-        bit *= 2
-    return sets
+    send_slices(sums, slices, place[1], depth)
 
 
 def update_back_kernel(groups, depth, scale, place, *refs):
-    keys_in, scaled_in = refs[:groups], refs[groups : 2 * groups]
-    parts = refs[2 * groups : 2 * groups + depth]
-    w_gate, w_out, w_up = refs[2 * groups + depth : 2 * groups + depth + 3]
-    base = 2 * groups + depth + 3
+    keys_in, scaled_in = refs[:2]
+    parts = refs[2 : depth + 2]
+    w_gate, w_out, w_up = refs[depth + 2 : depth + 5]
+    base = depth + 5
     outs = refs[base : base + groups]
     slices = refs[base + groups : -2]
     whole, sums = refs[-2:]
@@ -217,8 +218,8 @@
     cot_gate, cot_out, cot_up = ((whole[i] * scale).astype(BF16) for i in range(3))
     total = [0.0, 0.0, 0.0]
     for step in range(groups):
-        keys = keys_in[step][...].astype(BF16)
-        scaled = scaled_in[step][...].astype(BF16)
+        keys = keys_in[step]
+        scaled = scaled_in[step]
         first = mm(keys, gate_b)
         third = mm(keys, up_b)
         sig = jax.nn.sigmoid(first)
@@ -251,11 +252,7 @@
         total[2] += tmm(keys, bar_third)
     for i in range(3):
         sums[i] = total[i]
-    rows = sums.shape[1] // depth
-    for out, members in zip(slices, halving_order(depth) + [[0]]):
-        for i, step in enumerate(members):
-            at = pl.multiple_of((place[1] ^ step) * rows, rows)
-            out[i] = sums[:, pl.ds(at, rows), :]
+    send_slices(sums, slices, place[1], depth)
 
 
 def join_query_kernel(groups, place, *refs):
@@ -267,30 +264,28 @@
 
 
 def join_update_kernel(groups, place, r, *refs):
-    pieces, (out_k, out_v, sk, sv) = refs[:groups], refs[groups:]
+    pieces, parts = refs[:groups], refs[groups : 2 * groups]
+    out_k, out_v = refs[2 * groups : 2 * groups + 2]
+    grads, (sk, sv) = refs[2 * groups + 2 : -2], refs[-2:]
     tokens, heads, width = out_k.shape
     for step, piece in enumerate(pieces):
         head = place[0] ^ step
         put_head(sk, head, piece[0], tokens, heads)
         put_head(sv, head, piece[1] * rate_column(r, head), tokens, heads)
+        for i, grad in enumerate(grads):
+            grad[head] = parts[step][0, i]
     out_k[...] = rows_of(sk).reshape(tokens, heads, width).astype(BF16)
     out_v[...] = rows_of(sv).reshape(tokens, heads, width).astype(BF16)
 
 
 def rows_kernel(groups, place, *refs):
-    parts, outs, total = refs[: -groups - 1], refs[-groups - 1 : -1], refs[-1]
-    summed = parts[0][...]
+    count = len(send_groups(groups))
+    parts, outs, total = refs[: -count - 1], refs[-count - 1 : -1], refs[-1]
+    summed = parts[0][0]
     for part in parts[1:]:
         summed += part[0]
     total[...] = summed
-    send_slices(total, outs, place[0])
-
-
-def join_rows_kernel(groups, place, *refs):
-    parts, outs = refs[:groups], refs[groups:]
-    for step, part in enumerate(parts):
-        for i, out in enumerate(outs):
-            out[place[0] ^ step] = part[i]
+    send_slices(total, outs, place[0], groups)
 
 
 def local(queries, keys, values, rates, head_scale, gain, w_gate, w_out, w_up, cotangent):
@@ -313,8 +308,33 @@
     def in_plane(parts):
         return [parts[0]] + [move(p, "ctx", step) for step, p in enumerate(parts) if step]
 
-    def in_column(parts):
-        return [parts[0]] + [move(p, "ctx", i * groups) for i, p in enumerate(parts) if i]
+    def forwarded(got):
+        return [got[:1]] if got.shape[0] == 1 else [got[i : i + 1] for i in range(got.shape[0])]
+
+    def scatter(outs, count, unit):
+        outs = list(outs)
+        evens = list(range(2, count, 2))
+        via = forwarded(move(outs.pop(0), "ctx", unit)) if evens else []
+        first = [move(outs[0], "ctx", unit)] if count > 1 else []
+        even = [move(p + v, "ctx", r * unit) for p, v, r in zip(outs[1:], via, evens)]
+        return [outs[-1]] + first + even
+
+    def gather(part, count, unit):
+        got = [part] * count
+        for r in [2 * i for i in range(1, count // 2)]:
+            got[r] = move(part, "ctx", r * unit)
+            got[r + 1] = move(got[r], "ctx", unit)
+        if count > 1:
+            got[1] = move(part, "ctx", unit)
+        return got
+
+    def rows_exchange(outs):
+        outs, evens = list(outs), list(range(2, groups, 2))
+        via = forwarded(move(outs.pop(0), "ctx", 1)) if evens else []
+        got = [outs[-1]] + [move(outs[0], "ctx", 1)] * (groups > 1)
+        for i, r in enumerate(evens):
+            got += [move(outs[1 + i], "ctx", r), move(via[i], "ctx", r)]
+        return got
 
     def after(x, *others):
         return lax.optimization_barrier((x, *others))
@@ -324,7 +344,7 @@
 
     flops = 2 * groups * tokens * width * hidden
     pieces = [shape(tokens, width)] * groups
-    slices = [shape(3, hidden // depth, width)] * depth
+    slices = [shape(len(m), 3, hidden // depth, width) for m in send_groups(depth)]
     joined = shape(tokens, heads, width, dtype=BF16)
     scratch = pltpu.VMEM((width // LANES, tokens * heads, LANES), F32)
     square = pltpu.VMEM((3, hidden, width), F32)
@@ -336,19 +356,20 @@
     s_in = in_plane(split(split_scaled_kernel, values[0], rates[0]))
     own = [lax.dynamic_index_in_dim(w, mine, 0, keepdims=False) for w in (w_gate, w_out, w_up)]
     own_scale = lax.dynamic_index_in_dim(head_scale, mine, 0, keepdims=True)[None, :]
+    k_in, s_in, queries, cotangent = after(k_in, s_in, queries, cotangent)
+    kept_b = shape(groups, tokens, width, dtype=BF16)
+    out = call(
+        functools.partial(update_kernel, groups, depth, scale), [kept_b] * 2 + slices, [square],
+        6 * flops, place, *k_in, *s_in, *own,
+    )
+    k_in, s_in, terms = out[0], out[1], out[2:]
     q_out = call(
         functools.partial(split_apply_kernel, groups), [shape(2, tokens, width)] * groups,
         [scratch], flops // 8, place, queries[0], cotangent[0], gain,
     )
-    k_in, s_in, q_out = after(k_in, s_in, q_out)
-    terms = call(
-        functools.partial(update_kernel, groups, depth, scale), slices, [square], 6 * flops,
-        place, *k_in, *s_in, *own,
-    )
     q_in = in_plane(q_out)
-    new = functools.reduce(jnp.add, in_column(terms))
-    new, q_in[:-1] = after(new, q_in[:-1])
-    new = in_column([new] * depth)
+    new = functools.reduce(jnp.add, scatter(terms, depth, groups))
+    new = gather(new, depth, groups)
     kept = shape(groups, tokens, width)
     first, third, scaled, new_b, stats = call(
         functools.partial(apply_kernel, groups, depth),
@@ -360,45 +381,36 @@
         stats = stats + move(stats, "head", bit)
         bit *= 2
     out = call(
-        functools.partial(apply_back_kernel, groups, count), pieces + slices,
+        functools.partial(apply_back_kernel, groups, depth, count), pieces + slices,
         [square, pltpu.VMEM((2, groups, tokens), F32)], 6 * flops,
         place, own_scale, *q_in, *in_plane([stats] * groups),
         first, third, scaled, new_b,
     )
-    part = functools.reduce(jnp.add, in_column(out[groups:]))
-    part, q_back = after(part, in_plane(out[:groups]))
-    parts = in_column([part] * depth)
+    part = functools.reduce(jnp.add, scatter(out[groups:], depth, groups))
+    parts = gather(part, depth, groups)
     (grad_q,) = call(
         functools.partial(join_query_kernel, groups), [joined], [scratch], flops // 16,
-        place, *q_back,
-    )
+        place, *in_plane(out[:groups]),
+    )
+    parts, grad_q = after(parts, grad_q)
     rows = hidden // depth
-    sets = halving_order(depth)
     out = call(
         functools.partial(update_back_kernel, groups, depth, scale),
-        [shape(2, tokens, width)] * groups
-        + [shape(len(members), 3, rows, width) for members in sets + [[0]]],
-        [square] * 2, 15 * flops, place, *k_in, *s_in, *parts, *own,
+        [shape(2, tokens, width)] * groups + slices, [square] * 2, 15 * flops,
+        place, k_in, s_in, *parts, *own,
     )
     back = in_plane(out[:groups])
-    ends, rest = list(out[groups:-1]), [part, out[-1]]
-    for i in range(len(ends)):
-        got = move(ends[i], "ctx", groups << i)
-        for j in range(i + 1, len(ends)):
-            ends[j] = ends[j] + got[1 << (j - i - 1) :: 1 << (j - i)]
-        rest.append(got[:1])
+    ends = scatter(out[groups:], depth, groups)
     own_rows = rows // groups
     sent = call(
-        functools.partial(rows_kernel, groups), [shape(3, own_rows, width)] * groups,
-        [pltpu.VMEM((3, rows, width), F32)], flops // 100, place, *rest,
-    )
-    grads = call(
-        functools.partial(join_rows_kernel, groups), [shape(heads, own_rows, width)] * 3, [],
-        flops // 100, place, *in_plane(sent),
-    )
-    grad_k, grad_v = call(
-        functools.partial(join_update_kernel, groups), [joined] * 2, [scratch] * 2, flops // 8,
-        place, rates[0], *back,
+        functools.partial(rows_kernel, groups),
+        [shape(len(m), 3, own_rows, width) for m in send_groups(groups)],
+        [pltpu.VMEM((3, rows, width), F32)], flops // 100, place, part, *ends,
+    )
+    grad_k, grad_v, *grads = call(
+        functools.partial(join_update_kernel, groups),
+        [joined] * 2 + [shape(heads, own_rows, width)] * 3, [scratch] * 2, flops // 8,
+        place, rates[0], *back, *rows_exchange(sent),
     )
     if lax.axis_size("batch") > 1:
         grads = [lax.psum_scatter(x, "batch", scatter_dimension=1, tiled=True) for x in grads]

time: 159 us -> 152 us (0.956)
  starting transfers between devices: 49.8 us -> 42.5 us
  waiting for transfers between devices: 80 us -> 84.6 us
  Pallas kernels: 23 us -> 20.9 us
  local copies, waits for them, and re-layouts: 4.54 us -> 2.82 us
    ppermute x36 -> x38, starting transfers between devices: 49.8 us -> 42.5 us  [move(): lax.ppermute(x, axis, [(c, c ^ step) for c in range(lax.axis_size(axis))])]
    ppermute x36 -> x38, waiting for transfers between devices: 80 us -> 84.6 us  [move(): lax.ppermute(x, axis, [(c, c ^ step) for c in range(lax.axis_size(axis))])]
    pallas_call x11 -> x10, Pallas kernels: 23 us -> 20.9 us  [call(): pl.pallas_call(body, out_shape=out_shape, in_specs=[smem if a.dtype == jn...]
    unnamed x16, local copies, waits for them, and re-layouts: 2.86 us -> 1.15 us
  transfers between devices with their start and end apart: 36 -> 38, of which waited for: 20 -> 26; matrix products, arithmetic and copies ran while one was open for 1% -> 1% of each run, Pallas kernels for 7% -> 4%
where the time goes in v7:
time: 152 us
  waiting for transfers between devices  84.6 us (56%)
  starting transfers between devices  42.5 us (28%)
  Pallas kernels  20.9 us (14%)
  local copies, waits for them, and re-layouts  2.82 us (2%)
    ppermute x38, waiting for transfers between devices, move(): lax.ppermute(x, axis, [(c, c ^ step) for c in range(lax.axis_size(axis))])  84.6 us
    ppermute x38, starting transfers between devices, move(): lax.ppermute(x, axis, [(c, c ^ step) for c in range(lax.axis_size(axis))])  42.5 us
    pallas_call x10, Pallas kernels, call(): pl.pallas_call(body, out_shape=out_shape, in_specs=[smem if a.dtype == jn...  20.9 us
  transfers between devices with their start and end apart: 38, of which 26 were waited for; matrix products, arithmetic and copies ran while one was open for 1% of the time, Pallas kernels for 4%

profile of v7, /device:TPU:0, one launch (start us, length us, event | category | flops | bytes accessed | tf_op | source)
XLA Modules:
  0.0 151.9 jit_solution(7159098556356528355)
XLA Ops:
  0.7 1.1 copy-done.1
  1.8 1.6 %shard_map.145 = (f32[256,256]{1,0:T(8,128)S(1)}, f32[256,256]{1,0:T(8,128)S(1)}, f32[256,256]{1,0:T(8,128)}, f32[256,256]{1,0:T(8,128)S(1)}) custom-call(s32[2]{0:T(128)S(1)} %pad_add_fusion.place, bf16[256,4,256]{2,1,0:T(4,128)(2,1)S(1)} %bitcast.17), custom_call_target="tpu_custom_call" | custom-call | flops 8388608 | bytes 1572872 | tf_op jit(solution)/shard_map/pallas_call | solution.py:34
  3.4 2.9 %collective-permute-start = (f32[256,256]{1,0:T(8,128)S(1)}, f32[256,256]{1,0:T(8,128)S(1)}, u32[]{:S(2)}, u32[]{:S(2)}) collective-permute-start(f32[256,256]{1,0:T(8,128)S(1)} %get-tuple-element.70), channel_id=1, source_target_pairs={{0,2},{2,0},{4,6},{6,4},{8,10},{10,8},{12,14},{14,12},{16,18},{18,... | collective-permute-start | bytes 786440 | tf_op jit(solution)/shard_map/ppermute | solution.py:306
  6.4 1.5 %collective-permute-start.1 = (f32[256,256]{1,0:T(8,128)}, f32[256,256]{1,0:T(8,128)S(1)}, u32[]{:S(2)}, u32[]{:S(2)}) collective-permute-start(f32[256,256]{1,0:T(8,128)} %get-tuple-element.71), channel_id=1, source_target_pairs={{0,4},{2,6},{4,0},{6,2},{8,12},{10,14},{12,8},{14,10},{16,20},{18,... | collective-permute-start | bytes 786440 | tf_op jit(solution)/shard_map/ppermute | solution.py:306
  7.9 1.9 %shard_map.146 = (f32[256,256]{1,0:T(8,128)S(1)}, f32[256,256]{1,0:T(8,128)}, f32[256,256]{1,0:T(8,128)}, f32[256,256]{1,0:T(8,128)}) custom-call(s32[2]{0:T(128)S(1)} %pad_add_fusion.place, bf16[256,4,256]{2,1,0:T(4,128)(2,1)S(1)} %bitcast.18, f32[4,256]{1,0:T(4,128)S(1)} %bitcast.21), custom_call_target="tpu_custom_call" | custom-call | flops 8388608 | bytes 1576968 | tf_op jit(solution)/shard_map/pallas_call | solution.py:34
  9.8 2.0 %collective-permute-start.3 = (f32[256,256]{1,0:T(8,128)}, f32[256,256]{1,0:T(8,128)S(1)}, u32[]{:S(2)}, u32[]{:S(2)}) collective-permute-start(f32[256,256]{1,0:T(8,128)} %get-tuple-element.74), channel_id=1, source_target_pairs={{0,2},{2,0},{4,6},{6,4},{8,10},{10,8},{12,14},{14,12},{16,18},{18,... | collective-permute-start | bytes 786440 | tf_op jit(solution)/shard_map/ppermute | solution.py:306
  11.8 1.5 %collective-permute-start.4 = (f32[256,256]{1,0:T(8,128)}, f32[256,256]{1,0:T(8,128)S(1)}, u32[]{:S(2)}, u32[]{:S(2)}) collective-permute-start(f32[256,256]{1,0:T(8,128)} %get-tuple-element.75), channel_id=1, source_target_pairs={{0,4},{2,6},{4,0},{6,2},{8,12},{10,14},{12,8},{14,10},{16,20},{18,... | collective-permute-start | bytes 786440 | tf_op jit(solution)/shard_map/ppermute | solution.py:306
  13.5 3.0 %collective-permute-start.5 = (f32[256,256]{1,0:T(8,128)}, f32[256,256]{1,0:T(8,128)S(1)}, u32[]{:S(2)}, u32[]{:S(2)}) collective-permute-start(f32[256,256]{1,0:T(8,128)} %get-tuple-element.76), channel_id=1, source_target_pairs={{0,6},{2,4},{4,2},{6,0},{8,14},{10,12},{12,10},{14,8},{16,22},{18,... | collective-permute-start | bytes 786440 | tf_op jit(solution)/shard_map/ppermute | solution.py:306
  16.6 1.1 dynamic-slice_bitcast_fusion
  17.6 3.6 %collective-permute-done.1.refs_2_ = f32[256,256]{1,0:T(8,128)S(1)} collective-permute-done((f32[256,256]{1,0:T(8,128)}, f32[256,256]{1,0:T(8,128)S(1)}, u32[]{:S(2)}, u32[]{:S(2)}) %collective-permute-start.1) | collective-permute-done | bytes 262176 | tf_op jit(solution)/shard_map/ppermute | solution.py:306
  21.3 3.5 %collective-permute-done.3.refs_5_ = f32[256,256]{1,0:T(8,128)S(1)} collective-permute-done((f32[256,256]{1,0:T(8,128)}, f32[256,256]{1,0:T(8,128)S(1)}, u32[]{:S(2)}, u32[]{:S(2)}) %collective-permute-start.3) | collective-permute-done | bytes 262176 | tf_op jit(solution)/shard_map/ppermute | solution.py:306
  24.8 6.4 %collective-permute-done.4.refs_6_ = f32[256,256]{1,0:T(8,128)S(1)} collective-permute-done((f32[256,256]{1,0:T(8,128)}, f32[256,256]{1,0:T(8,128)S(1)}, u32[]{:S(2)}, u32[]{:S(2)}) %collective-permute-start.4) | collective-permute-done | bytes 262176 | tf_op jit(solution)/shard_map/ppermute | solution.py:306
  31.2 2.2 %shard_map.148 = (bf16[4,256,256]{2,1,0:T(8,128)(2,1)S(1)}, bf16[4,256,256]{2,1,0:T(8,128)(2,1)S(1)}, f32[1,3,64,256]{3,2,1,0:T(8,128)S(1)}, f32[1,3,64,256]{3,2...) custom-call(s32[2]{0:T(128)S(1)} %pad_add_fusion.place, ...), custom_call_target="tpu_custom_call" | custom-call | flops 805306368 | bytes 4718600 | tf_op jit(solution)/shard_map/pallas_call | solution.py:34
  33.4 1.6 %collective-permute-start.10 = (f32[1,3,64,256]{3,2,1,0:T(8,128)S(1)}, f32[1,3,64,256]{3,2,1,0:T(8,128)S(1)}, u32[]{:S(2)}, u32[]{:S(2)}) collective-permute-start(f32[1,3,64,256]{3,2,1,0:T(8,128)S(1)} %get-tuple-element.94), channel_id=1, source_target_pairs={{0,8},{2,10},{4,12},{6,14},{8,0},{10,2},{12,4},{14,6},{16,24},{18,... | collective-permute-start | bytes 589832 | tf_op jit(solution)/shard_map/ppermute | solution.py:306
  35.5 7.6 %collective-permute-done.10 = f32[1,3,64,256]{3,2,1,0:T(8,128)S(1)} collective-permute-done((f32[1,3,64,256]{3,2,1,0:T(8,128)S(1)}, f32[1,3,64,256]{3,2,1,0:T(8,128)S(1)}, u32[]{:S(2)}, u32[]{:S(2)}) %collective-permute-start.10) | collective-permute-done | bytes 196640 | tf_op jit(solution)/shard_map/ppermute | solution.py:306
  43.1 0.9 collective-permute-start.11
  44.0 1.3 shard_map.147
  45.3 1.2 collective-permute-start.6
  46.6 0.9 collective-permute-start.7
  47.4 1.4 collective-permute-start.8
  48.9 6.7 %collective-permute-done.11 = f32[1,3,64,256]{3,2,1,0:T(8,128)S(1)} collective-permute-done((f32[1,3,64,256]{3,2,1,0:T(8,128)S(1)}, f32[1,3,64,256]{3,2,1,0:T(8,128)S(1)}, u32[]{:S(2)}, u32[]{:S(2)}) %collective-permute-start.11) | collective-permute-done | bytes 196640 | tf_op jit(solution)/shard_map/ppermute | solution.py:306
  55.8 2.7 %collective-permute-start.12 = (f32[1,3,64,256]{3,2,1,0:T(8,128)S(1)}, f32[1,3,64,256]{3,2,1,0:T(8,128)S(1)}, u32[]{:S(2)}, u32[]{:S(2)}) collective-permute-start(f32[1,3,64,256]{3,2,1,0:T(8,128)S(1)} %add_add_fusion.1.refs_4_), channel_id=1, source_target_pairs={{0,8},{2,10},{4,12},{6,14},{8,0},{10,2},{12,4},{14,6},{16,24},{18,... | collective-permute-start | bytes 589832 | tf_op jit(solution)/shard_map/ppermute | solution.py:306
  58.5 5.7 %collective-permute-done.13.refs_6_ = f32[1,3,64,256]{3,2,1,0:T(8,128)S(1)} collective-permute-done((f32[1,3,64,256]{3,2,1,0:T(8,128)S(1)}, f32[1,3,64,256]{3,2,1,0:T(8,128)S(1)}, u32[]{:S(2)}, u32[]{:S(2)}) %collective-permute-start.13) | collective-permute-done | bytes 196640 | tf_op jit(solution)/shard_map/ppermute | solution.py:306
  64.1 0.6 dynamic_slice.14
  64.7 2.2 %collective-permute-done.7.refs_2_ = f32[2,256,256]{2,1,0:T(8,128)S(1)} collective-permute-done((f32[2,256,256]{2,1,0:T(8,128)S(1)}, f32[2,256,256]{2,1,0:T(8,128)S(1)}, u32[]{:S(2)}, u32[]{:S(2)}) %collective-permute-start.7) | collective-permute-done | bytes 524320 | tf_op jit(solution)/shard_map/ppermute | solution.py:306
  66.9 2.9 %collective-permute-done.14.refs_7_ = f32[1,3,64,256]{3,2,1,0:T(8,128)S(1)} collective-permute-done((f32[1,3,64,256]{3,2,1,0:T(8,128)S(1)}, f32[1,3,64,256]{3,2,1,0:T(8,128)S(1)}, u32[]{:S(2)}, u32[]{:S(2)}) %collective-permute-start.14) | collective-permute-done | bytes 196640 | tf_op jit(solution)/shard_map/ppermute | solution.py:306
  69.8 2.3 %shard_map.149 = (f32[4,256,256]{2,1,0:T(8,128)S(1)}, f32[4,256,256]{2,1,0:T(8,128)S(1)}, f32[4,256,256]{2,1,0:T(8,128)S(1)}, bf16[3,256,256]{2,1,0:T(8,128)(2,1)S(1)}, f32[2,4,256]{2,1,0:T(4,128)S(1)}) custom-call(s32[2]{0:T(128)S(1)} %pad_add_fusion.place, f32[1,1]{1,0:T(1,128)} %bitcast.2.head_scale, f32[2,256,256]{2,1,0:T(8,128)S(1)} %get-tuple-element.79.refs_0_, ...), custom_call_target="tpu_custom_call" | custom-call | flops 402653184 | bytes 6430732 | tf_op jit(solution)/shard_map/pallas_call | solution.py:34
  72.2 1.2 collective-permute-done.15
  73.4 1.5 collective-permute-start.18
  74.8 1.0 collective-permute-start.17
  75.8 1.0 collective-permute-start.16
  76.8 1.1 collective-permute-done.18.refs_7_
  78.5 1.0 collective-permute-done.16.refs_5_
  79.5 3.1 %shard_map.150 = (f32[256,256]{1,0:T(8,128)S(1)}, f32[256,256]{1,0:T(8,128)S(1)}, f32[256,256]{1,0:T(8,128)S(1)}, f32[256,256]{1,0:T(8,128)S(1)}, f32[1,3,64,256...) custom-call(s32[2]{0:T(128)S(1)} %pad_add_fusion.place, ...), custom_call_target="tpu_custom_call" | custom-call | flops 805306368 | bytes 7503884 | tf_op jit(solution)/shard_map/pallas_call | solution.py:34
  82.6 2.0 %collective-permute-start.19 = (f32[1,3,64,256]{3,2,1,0:T(8,128)S(1)}, f32[1,3,64,256]{3,2,1,0:T(8,128)S(1)}, u32[]{:S(2)}, u32[]{:S(2)}) collective-permute-start(f32[1,3,64,256]{3,2,1,0:T(8,128)S(1)} %get-tuple-element.101), channel_id=1, source_target_pairs={{0,8},{2,10},{4,12},{6,14},{8,0},{10,2},{12,4},{14,6},{16,24},{18,... | collective-permute-start | bytes 589832 | tf_op jit(solution)/shard_map/ppermute | solution.py:306
  84.7 7.1 %collective-permute-done.20 = f32[1,3,64,256]{3,2,1,0:T(8,128)S(1)} collective-permute-done((f32[1,3,64,256]{3,2,1,0:T(8,128)S(1)}, f32[1,3,64,256]{3,2,1,0:T(8,128)S(1)}, u32[]{:S(2)}, u32[]{:S(2)}) %collective-permute-start.20) | collective-permute-done | bytes 196640 | tf_op jit(solution)/shard_map/ppermute | solution.py:306
  91.9 2.5 %collective-permute-done.19 = f32[1,3,64,256]{3,2,1,0:T(8,128)S(1)} collective-permute-done((f32[1,3,64,256]{3,2,1,0:T(8,128)S(1)}, f32[1,3,64,256]{3,2,1,0:T(8,128)S(1)}, u32[]{:S(2)}, u32[]{:S(2)}) %collective-permute-start.19) | collective-permute-done | bytes 196640 | tf_op jit(solution)/shard_map/ppermute | solution.py:306
  94.3 9.6 %collective-permute-done.21 = f32[1,3,64,256]{3,2,1,0:T(8,128)S(1)} collective-permute-done((f32[1,3,64,256]{3,2,1,0:T(8,128)S(1)}, f32[1,3,64,256]{3,2,1,0:T(8,128)S(1)}, u32[]{:S(2)}, u32[]{:S(2)}) %collective-permute-start.21) | collective-permute-done | bytes 196640 | tf_op jit(solution)/shard_map/ppermute | solution.py:306
  104.0 1.0 collective-permute-start.25
  105.0 0.8 collective-permute-start.26
  105.8 1.7 %collective-permute-start.27 = (f32[256,256]{1,0:T(8,128)S(1)}, f32[256,256]{1,0:T(8,128)S(1)}, u32[]{:S(2)}, u32[]{:S(2)}) collective-permute-start(f32[256,256]{1,0:T(8,128)S(1)} %get-tuple-element.107), channel_id=1, source_target_pairs={{0,6},{2,4},{4,2},{6,0},{8,14},{10,12},{12,10},{14,8},{16,22},{18,... | collective-permute-start | bytes 786440 | tf_op jit(solution)/shard_map/ppermute | solution.py:306
  107.6 2.3 %collective-permute-start.22 = (f32[1,3,64,256]{3,2,1,0:T(8,128)S(1)}, f32[1,3,64,256]{3,2,1,0:T(8,128)S(1)}, u32[]{:S(2)}, u32[]{:S(2)}) collective-permute-start(f32[1,3,64,256]{3,2,1,0:T(8,128)S(1)} %add_add_fusion.refs_2_.refs_0_), channel_id=1, source_target_pairs={{0,8},{2,10},{4,12},{6,14},{8,0},{10,2},{12,4},{14,6},{16,24},{18,... | collective-permute-start | bytes 589832 | tf_op jit(solution)/shard_map/ppermute | solution.py:306
  109.9 2.3 %collective-permute-done.23.refs_4_ = f32[1,3,64,256]{3,2,1,0:T(8,128)S(1)} collective-permute-done((f32[1,3,64,256]{3,2,1,0:T(8,128)S(1)}, f32[1,3,64,256]{3,2,1,0:T(8,128)S(1)}, u32[]{:S(2)}, u32[]{:S(2)}) %collective-permute-start.23) | collective-permute-done | bytes 196640 | tf_op jit(solution)/shard_map/ppermute | solution.py:306
  112.2 2.0 %collective-permute-done.26.refs_2_ = f32[256,256]{1,0:T(8,128)S(1)} collective-permute-done((f32[256,256]{1,0:T(8,128)S(1)}, f32[256,256]{1,0:T(8,128)S(1)}, u32[]{:S(2)}, u32[]{:S(2)}) %collective-permute-start.26) | collective-permute-done | bytes 262176 | tf_op jit(solution)/shard_map/ppermute | solution.py:306
  114.2 1.7 %shard_map.151 = bf16[256,4,256]{2,1,0:T(4,128)(2,1)} custom-call(s32[2]{0:T(128)S(1)} %pad_add_fusion.place, f32[256,256]{1,0:T(8,128)S(1)} %get-tuple-element.104.refs_0_, f32[256,256]{1,0:T(8,128)S(1)} %collective-permute-done.25.refs_1_, f32[256,256]{1,0:T(8,128)S(1)} %collective-permute-done.26.refs_2_, f32[256,256]{1,0:T(8,128)S(1)} %collective-permute-done.27.refs_3_), custom_call_target="tpu_custom_call" | custom-call | flops 8388608 | bytes 1572872 | tf_op jit(solution)/shard_map/pallas_call | solution.py:34
  116.0 1.9 %collective-permute-done.24.refs_5_ = f32[1,3,64,256]{3,2,1,0:T(8,128)S(1)} collective-permute-done((f32[1,3,64,256]{3,2,1,0:T(8,128)S(1)}, f32[1,3,64,256]{3,2,1,0:T(8,128)S(1)}, u32[]{:S(2)}, u32[]{:S(2)}) %collective-permute-start.24) | collective-permute-done | bytes 196640 | tf_op jit(solution)/shard_map/ppermute | solution.py:306
  117.9 3.8 %shard_map.152 = (f32[2,256,256]{2,1,0:T(8,128)S(1)}, f32[2,256,256]{2,1,0:T(8,128)S(1)}, f32[2,256,256]{2,1,0:T(8,128)S(1)}, f32[2,256,256]{2,1,0:T(8,128)S(1)}...) custom-call(s32[2]{0:T(128)S(1)} %pad_add_fusion.place, ...), custom_call_target="tpu_custom_call" | custom-call | flops 2013265920 | bytes 5505032 | tf_op jit(solution)/shard_map/pallas_call | solution.py:34
  121.6 1.1 collective-permute-start.28
  122.7 0.8 collective-permute-start.29
  123.5 1.7 %collective-permute-start.30 = (f32[2,256,256]{2,1,0:T(8,128)S(1)}, f32[2,256,256]{2,1,0:T(8,128)S(1)}, u32[]{:S(2)}, u32[]{:S(2)}) collective-permute-start(f32[2,256,256]{2,1,0:T(8,128)S(1)} %get-tuple-element.118), channel_id=1, source_target_pairs={{0,6},{2,4},{4,2},{6,0},{8,14},{10,12},{12,10},{14,8},{16,22},{18,... | collective-permute-start | bytes 1572872 | tf_op jit(solution)/shard_map/ppermute | solution.py:306
  125.8 1.5 collective-permute-start.31
  127.2 3.6 %collective-permute-done.32 = f32[1,3,64,256]{3,2,1,0:T(8,128)S(1)} collective-permute-done((f32[1,3,64,256]{3,2,1,0:T(8,128)S(1)}, f32[1,3,64,256]{3,2,1,0:T(8,128)S(1)}, u32[]{:S(2)}, u32[]{:S(2)}) %collective-permute-start.32) | collective-permute-done | bytes 196640 | tf_op jit(solution)/shard_map/ppermute | solution.py:306
  130.9 1.0 collective-permute-start.33
  131.9 1.1 collective-permute-done.31.refs_2_
  133.0 6.7 %collective-permute-done.33.refs_3_ = f32[1,3,64,256]{3,2,1,0:T(8,128)S(1)} collective-permute-done((f32[1,3,64,256]{3,2,1,0:T(8,128)S(1)}, f32[1,3,64,256]{3,2,1,0:T(8,128)S(1)}, u32[]{:S(2)}, u32[]{:S(2)}) %collective-permute-start.33) | collective-permute-done | bytes 196640 | tf_op jit(solution)/shard_map/ppermute | solution.py:306
  139.6 0.6 shard_map.153
  140.2 1.0 collective-permute-start.34
  141.3 1.1 collective-permute-start.36
  142.3 2.1 %collective-permute-done.34.refs_5_ = f32[1,3,16,256]{3,2,1,0:T(8,128)S(1)} collective-permute-done((f32[1,3,16,256]{3,2,1,0:T(8,128)S(1)}, f32[1,3,16,256]{3,2,1,0:T(8,128)S(1)}, u32[]{:S(2)}, u32[]{:S(2)}) %collective-permute-start.34) | collective-permute-done | bytes 49184 | tf_op jit(solution)/shard_map/ppermute | solution.py:306
  144.4 0.8 collective-permute-start.35
  145.3 1.1 collective-permute-start.37
  146.4 2.1 %collective-permute-done.35.refs_6_ = f32[1,3,16,256]{3,2,1,0:T(8,128)S(1)} collective-permute-done((f32[1,3,16,256]{3,2,1,0:T(8,128)S(1)}, f32[1,3,16,256]{3,2,1,0:T(8,128)S(1)}, u32[]{:S(2)}, u32[]{:S(2)}) %collective-permute-start.35) | collective-permute-done | bytes 49184 | tf_op jit(solution)/shard_map/ppermute | solution.py:306
  148.5 0.9 collective-permute-done.37.refs_7_
  149.4 2.4 %shard_map.154 = (bf16[256,4,256]{2,1,0:T(4,128)(2,1)}, bf16[256,4,256]{2,1,0:T(4,128)(2,1)}, f32[4,16,256]{2,1,0:T(8,128)}, f32[4,16,256]{2,1,0:T(8,128)}, f32[4,16,256]{2,1,0:T(8,128)}) custom-call(s32[2]{0:T(128)S(1)} %pad_add_fusion.place, f32[4,256]{1,0:T(4,128)S(1)} %bitcast.22, f32[2,256,256]{2,1,0:T(8,128)S(1)} %get-tuple-element.115.refs_0_, ...), custom_call_target="tpu_custom_call" | custom-call | flops 16777216 | bytes 3543048 | tf_op jit(solution)/shard_map/pallas_call | solution.py:34
  (48 shorter events, 2.6 us)
Async XLA Ops:
  0.6 15.9 %copy-start = (f32[4,256,256]{2,1,0:T(8,128)S(1)}, f32[4,256,256]{2,1,0:T(8,128)}, u32[]{:S(2)}) copy-start(f32[4,256,256]{2,1,0:T(8,128)} %param.16) | copy-start | bytes 3145732
  0.7 1.1 copy-start.1
  1.8 6.1 %copy-start.2 = (bf16[1,256,4,256]{3,2,1,0:T(4,128)(2,1)S(1)}, bf16[1,256,4,256]{3,2,1,0:T(4,128)(2,1)}, u32[]{:S(2)}) copy-start(bf16[1,256,4,256]{3,2,1,0:T(4,128)(2,1)} %param.12) | copy-start | bytes 1572868
  3.4 4.5 %copy-start.5 = (f32[1,4,256]{2,1,0:T(4,128)S(1)}, f32[1,4,256]{2,1,0:T(4,128)}, u32[]{:S(2)}) copy-start(f32[1,4,256]{2,1,0:T(4,128)} %param.13) | copy-start | bytes 12292
  3.4 10.1 %collective-permute-start = (f32[256,256]{1,0:T(8,128)S(1)}, f32[256,256]{1,0:T(8,128)S(1)}, u32[]{:S(2)}, u32[]{:S(2)}) collective-permute-start(f32[256,256]{1,0:T(8,128)S(1)} %get-tuple-element.70), channel_id=1, source_target_pairs={{0,2},{2,0},{4,6},{6,4},{8,10},{10,8},{12,14},{14,12},{16,18},{18,... | collective-permute-start | bytes 786440 | tf_op jit(solution)/shard_map/ppermute | solution.py:306
  6.4 14.9 %collective-permute-start.1 = (f32[256,256]{1,0:T(8,128)}, f32[256,256]{1,0:T(8,128)S(1)}, u32[]{:S(2)}, u32[]{:S(2)}) collective-permute-start(f32[256,256]{1,0:T(8,128)} %get-tuple-element.71), channel_id=1, source_target_pairs={{0,4},{2,6},{4,0},{6,2},{8,12},{10,14},{12,8},{14,10},{16,20},{18,... | collective-permute-start | bytes 786440 | tf_op jit(solution)/shard_map/ppermute | solution.py:306
  7.9 13.4 %collective-permute-start.2 = (f32[256,256]{1,0:T(8,128)S(1)}, f32[256,256]{1,0:T(8,128)S(1)}, u32[]{:S(2)}, u32[]{:S(2)}) collective-permute-start(f32[256,256]{1,0:T(8,128)S(1)} %get-tuple-element.72), channel_id=1, source_target_pairs={{0,6},{2,4},{4,2},{6,0},{8,14},{10,12},{12,10},{14,8},{16,22},{18,... | collective-permute-start | bytes 786440 | tf_op jit(solution)/shard_map/ppermute | solution.py:306
  9.8 15.0 %collective-permute-start.3 = (f32[256,256]{1,0:T(8,128)}, f32[256,256]{1,0:T(8,128)S(1)}, u32[]{:S(2)}, u32[]{:S(2)}) collective-permute-start(f32[256,256]{1,0:T(8,128)} %get-tuple-element.74), channel_id=1, source_target_pairs={{0,2},{2,0},{4,6},{6,4},{8,10},{10,8},{12,14},{14,12},{16,18},{18,... | collective-permute-start | bytes 786440 | tf_op jit(solution)/shard_map/ppermute | solution.py:306
  11.8 19.4 %collective-permute-start.4 = (f32[256,256]{1,0:T(8,128)}, f32[256,256]{1,0:T(8,128)S(1)}, u32[]{:S(2)}, u32[]{:S(2)}) collective-permute-start(f32[256,256]{1,0:T(8,128)} %get-tuple-element.75), channel_id=1, source_target_pairs={{0,4},{2,6},{4,0},{6,2},{8,12},{10,14},{12,8},{14,10},{16,20},{18,... | collective-permute-start | bytes 786440 | tf_op jit(solution)/shard_map/ppermute | solution.py:306
  13.5 17.7 %collective-permute-start.5 = (f32[256,256]{1,0:T(8,128)}, f32[256,256]{1,0:T(8,128)S(1)}, u32[]{:S(2)}, u32[]{:S(2)}) collective-permute-start(f32[256,256]{1,0:T(8,128)} %get-tuple-element.76), channel_id=1, source_target_pairs={{0,6},{2,4},{4,2},{6,0},{8,14},{10,12},{12,10},{14,8},{16,22},{18,... | collective-permute-start | bytes 786440 | tf_op jit(solution)/shard_map/ppermute | solution.py:306
  31.2 12.8 %copy-start.4 = (bf16[1,256,4,256]{3,2,1,0:T(4,128)(2,1)S(1)}, bf16[1,256,4,256]{3,2,1,0:T(4,128)(2,1)}, u32[]{:S(2)}) copy-start(bf16[1,256,4,256]{3,2,1,0:T(4,128)(2,1)} %param.19) | copy-start | bytes 1572868
  33.4 10.6 %copy-start.3 = (bf16[1,256,4,256]{3,2,1,0:T(4,128)(2,1)S(1)}, bf16[1,256,4,256]{3,2,1,0:T(4,128)(2,1)}, u32[]{:S(2)}) copy-start(bf16[1,256,4,256]{3,2,1,0:T(4,128)(2,1)} %param.10) | copy-start | bytes 1572868
  33.4 9.7 %collective-permute-start.10 = (f32[1,3,64,256]{3,2,1,0:T(8,128)S(1)}, f32[1,3,64,256]{3,2,1,0:T(8,128)S(1)}, u32[]{:S(2)}, u32[]{:S(2)}) collective-permute-start(f32[1,3,64,256]{3,2,1,0:T(8,128)S(1)} %get-tuple-element.94), channel_id=1, source_target_pairs={{0,8},{2,10},{4,12},{6,14},{8,0},{10,2},{12,4},{14,6},{16,24},{18,... | collective-permute-start | bytes 589832 | tf_op jit(solution)/shard_map/ppermute | solution.py:306
  35.1 13.8 %collective-permute-start.9 = (f32[1,3,64,256]{3,2,1,0:T(8,128)S(1)}, f32[1,3,64,256]{3,2,1,0:T(8,128)S(1)}, u32[]{:S(2)}, u32[]{:S(2)}) collective-permute-start(f32[1,3,64,256]{3,2,1,0:T(8,128)S(1)} %get-tuple-element.92), channel_id=1, source_target_pairs={{0,8},{2,10},{4,12},{6,14},{8,0},{10,2},{12,4},{14,6},{16,24},{18,... | collective-permute-start | bytes 589832 | tf_op jit(solution)/shard_map/ppermute | solution.py:306
  43.1 0.9 copy-start.6
  43.1 12.5 %collective-permute-start.11 = (f32[1,3,64,256]{3,2,1,0:T(8,128)S(1)}, f32[1,3,64,256]{3,2,1,0:T(8,128)S(1)}, u32[]{:S(2)}, u32[]{:S(2)}) collective-permute-start(f32[1,3,64,256]{3,2,1,0:T(8,128)S(1)} %add.34), channel_id=1, source_target_pairs={{0,16},{2,18},{4,20},{6,22},{8,24},{10,26},{12,28},{14,30},{16,0},... | collective-permute-start | bytes 589832 | tf_op jit(solution)/shard_map/ppermute | solution.py:306
  45.3 19.4 %collective-permute-start.6 = (f32[2,256,256]{2,1,0:T(8,128)S(1)}, f32[2,256,256]{2,1,0:T(8,128)S(1)}, u32[]{:S(2)}, u32[]{:S(2)}) collective-permute-start(f32[2,256,256]{2,1,0:T(8,128)S(1)} %get-tuple-element.80), channel_id=1, source_target_pairs={{0,2},{2,0},{4,6},{6,4},{8,10},{10,8},{12,14},{14,12},{16,18},{18,... | collective-permute-start | bytes 1572872 | tf_op jit(solution)/shard_map/ppermute | solution.py:306
  46.6 20.4 %collective-permute-start.7 = (f32[2,256,256]{2,1,0:T(8,128)S(1)}, f32[2,256,256]{2,1,0:T(8,128)S(1)}, u32[]{:S(2)}, u32[]{:S(2)}) collective-permute-start(f32[2,256,256]{2,1,0:T(8,128)S(1)} %get-tuple-element.81), channel_id=1, source_target_pairs={{0,4},{2,6},{4,0},{6,2},{8,12},{10,14},{12,8},{14,10},{16,20},{18,... | collective-permute-start | bytes 1572872 | tf_op jit(solution)/shard_map/ppermute | solution.py:306
  47.4 19.5 %collective-permute-start.8 = (f32[2,256,256]{2,1,0:T(8,128)S(1)}, f32[2,256,256]{2,1,0:T(8,128)S(1)}, u32[]{:S(2)}, u32[]{:S(2)}) collective-permute-start(f32[2,256,256]{2,1,0:T(8,128)S(1)} %get-tuple-element.82), channel_id=1, source_target_pairs={{0,6},{2,4},{4,2},{6,0},{8,14},{10,12},{12,10},{14,8},{16,22},{18,... | collective-permute-start | bytes 1572872 | tf_op jit(solution)/shard_map/ppermute | solution.py:306
  55.6 8.5 %copy-start.7 = (f32[4]{0:T(128)S(1)}, f32[4]{0:T(128)}, u32[]{:S(2)}) copy-start(f32[4]{0:T(128)} %param.14) | copy-start | bytes 52
  55.7 8.5 %collective-permute-start.13 = (f32[1,3,64,256]{3,2,1,0:T(8,128)S(1)}, f32[1,3,64,256]{3,2,1,0:T(8,128)S(1)}, u32[]{:S(2)}, u32[]{:S(2)}) collective-permute-start(f32[1,3,64,256]{3,2,1,0:T(8,128)S(1)} %add_add_fusion.1.refs_4_), channel_id=1, source_target_pairs={{0,16},{2,18},{4,20},{6,22},{8,24},{10,26},{12,28},{14,30},{16,0},... | collective-permute-start | bytes 589832 | tf_op jit(solution)/shard_map/ppermute | solution.py:306
  55.8 11.2 %collective-permute-start.12 = (f32[1,3,64,256]{3,2,1,0:T(8,128)S(1)}, f32[1,3,64,256]{3,2,1,0:T(8,128)S(1)}, u32[]{:S(2)}, u32[]{:S(2)}) collective-permute-start(f32[1,3,64,256]{3,2,1,0:T(8,128)S(1)} %add_add_fusion.1.refs_4_), channel_id=1, source_target_pairs={{0,8},{2,10},{4,12},{6,14},{8,0},{10,2},{12,4},{14,6},{16,24},{18,... | collective-permute-start | bytes 589832 | tf_op jit(solution)/shard_map/ppermute | solution.py:306
  64.1 5.7 %collective-permute-start.14 = (f32[1,3,64,256]{3,2,1,0:T(8,128)S(1)}, f32[1,3,64,256]{3,2,1,0:T(8,128)S(1)}, u32[]{:S(2)}, u32[]{:S(2)}) collective-permute-start(f32[1,3,64,256]{3,2,1,0:T(8,128)S(1)} %collective-permute-done.13.refs_6_), channel_id=1, source_target_pairs={{0,8},{2,10},{4,12},{6,14},{8,0},{10,2},{12,4},{14,6},{16,24},{18,... | collective-permute-start | bytes 589832 | tf_op jit(solution)/shard_map/ppermute | solution.py:306
  72.1 1.2 collective-permute-start.15
  73.4 4.5 %collective-permute-start.18 = (f32[2,4,256]{2,1,0:T(4,128)S(1)}, f32[2,4,256]{2,1,0:T(4,128)S(1)}, u32[]{:S(2)}, u32[]{:S(2)}) collective-permute-start(f32[2,4,256]{2,1,0:T(4,128)S(1)} %add.36.refs_4_), channel_id=1, source_target_pairs={{0,6},{2,4},{4,2},{6,0},{8,14},{10,12},{12,10},{14,8},{16,22},{18,... | collective-permute-start | bytes 24584 | tf_op jit(solution)/shard_map/ppermute | solution.py:306
  74.8 3.7 %collective-permute-start.17 = (f32[2,4,256]{2,1,0:T(4,128)S(1)}, f32[2,4,256]{2,1,0:T(4,128)S(1)}, u32[]{:S(2)}, u32[]{:S(2)}) collective-permute-start(f32[2,4,256]{2,1,0:T(4,128)S(1)} %add.36.refs_4_), channel_id=1, source_target_pairs={{0,4},{2,6},{4,0},{6,2},{8,12},{10,14},{12,8},{14,10},{16,20},{18,... | collective-permute-start | bytes 24584 | tf_op jit(solution)/shard_map/ppermute | solution.py:306
  75.8 3.7 %collective-permute-start.16 = (f32[2,4,256]{2,1,0:T(4,128)S(1)}, f32[2,4,256]{2,1,0:T(4,128)S(1)}, u32[]{:S(2)}, u32[]{:S(2)}) collective-permute-start(f32[2,4,256]{2,1,0:T(4,128)S(1)} %add.36.refs_4_), channel_id=1, source_target_pairs={{0,2},{2,0},{4,6},{6,4},{8,10},{10,8},{12,14},{14,12},{16,18},{18,... | collective-permute-start | bytes 24584 | tf_op jit(solution)/shard_map/ppermute | solution.py:306
  82.6 9.2 %collective-permute-start.20 = (f32[1,3,64,256]{3,2,1,0:T(8,128)S(1)}, f32[1,3,64,256]{3,2,1,0:T(8,128)S(1)}, u32[]{:S(2)}, u32[]{:S(2)}) collective-permute-start(f32[1,3,64,256]{3,2,1,0:T(8,128)S(1)} %get-tuple-element.103), channel_id=1, source_target_pairs={{0,8},{2,10},{4,12},{6,14},{8,0},{10,2},{12,4},{14,6},{16,24},{18,... | collective-permute-start | bytes 589832 | tf_op jit(solution)/shard_map/ppermute | solution.py:306
  82.6 11.7 %collective-permute-start.19 = (f32[1,3,64,256]{3,2,1,0:T(8,128)S(1)}, f32[1,3,64,256]{3,2,1,0:T(8,128)S(1)}, u32[]{:S(2)}, u32[]{:S(2)}) collective-permute-start(f32[1,3,64,256]{3,2,1,0:T(8,128)S(1)} %get-tuple-element.101), channel_id=1, source_target_pairs={{0,8},{2,10},{4,12},{6,14},{8,0},{10,2},{12,4},{14,6},{16,24},{18,... | collective-permute-start | bytes 589832 | tf_op jit(solution)/shard_map/ppermute | solution.py:306
  91.8 12.1 %collective-permute-start.21 = (f32[1,3,64,256]{3,2,1,0:T(8,128)S(1)}, f32[1,3,64,256]{3,2,1,0:T(8,128)S(1)}, u32[]{:S(2)}, u32[]{:S(2)}) collective-permute-start(f32[1,3,64,256]{3,2,1,0:T(8,128)S(1)} %add.38), channel_id=1, source_target_pairs={{0,16},{2,18},{4,20},{6,22},{8,24},{10,26},{12,28},{14,30},{16,0},... | collective-permute-start | bytes 589832 | tf_op jit(solution)/shard_map/ppermute | solution.py:306
  103.9 8.3 %collective-permute-start.23 = (f32[1,3,64,256]{3,2,1,0:T(8,128)S(1)}, f32[1,3,64,256]{3,2,1,0:T(8,128)S(1)}, u32[]{:S(2)}, u32[]{:S(2)}) collective-permute-start(f32[1,3,64,256]{3,2,1,0:T(8,128)S(1)} %add_add_fusion.refs_2_.refs_0_), channel_id=1, source_target_pairs={{0,16},{2,18},{4,20},{6,22},{8,24},{10,26},{12,28},{14,30},{16,0},... | collective-permute-start | bytes 589832 | tf_op jit(solution)/shard_map/ppermute | solution.py:306
  104.0 8.2 %collective-permute-start.25 = (f32[256,256]{1,0:T(8,128)S(1)}, f32[256,256]{1,0:T(8,128)S(1)}, u32[]{:S(2)}, u32[]{:S(2)}) collective-permute-start(f32[256,256]{1,0:T(8,128)S(1)} %get-tuple-element.105), channel_id=1, source_target_pairs={{0,2},{2,0},{4,6},{6,4},{8,10},{10,8},{12,14},{14,12},{16,18},{18,... | collective-permute-start | bytes 786440 | tf_op jit(solution)/shard_map/ppermute | solution.py:306
  105.0 9.2 %collective-permute-start.26 = (f32[256,256]{1,0:T(8,128)S(1)}, f32[256,256]{1,0:T(8,128)S(1)}, u32[]{:S(2)}, u32[]{:S(2)}) collective-permute-start(f32[256,256]{1,0:T(8,128)S(1)} %get-tuple-element.106), channel_id=1, source_target_pairs={{0,4},{2,6},{4,0},{6,2},{8,12},{10,14},{12,8},{14,10},{16,20},{18,... | collective-permute-start | bytes 786440 | tf_op jit(solution)/shard_map/ppermute | solution.py:306
  105.8 8.4 %collective-permute-start.27 = (f32[256,256]{1,0:T(8,128)S(1)}, f32[256,256]{1,0:T(8,128)S(1)}, u32[]{:S(2)}, u32[]{:S(2)}) collective-permute-start(f32[256,256]{1,0:T(8,128)S(1)} %get-tuple-element.107), channel_id=1, source_target_pairs={{0,6},{2,4},{4,2},{6,0},{8,14},{10,12},{12,10},{14,8},{16,22},{18,... | collective-permute-start | bytes 786440 | tf_op jit(solution)/shard_map/ppermute | solution.py:306
  107.6 8.4 %collective-permute-start.22 = (f32[1,3,64,256]{3,2,1,0:T(8,128)S(1)}, f32[1,3,64,256]{3,2,1,0:T(8,128)S(1)}, u32[]{:S(2)}, u32[]{:S(2)}) collective-permute-start(f32[1,3,64,256]{3,2,1,0:T(8,128)S(1)} %add_add_fusion.refs_2_.refs_0_), channel_id=1, source_target_pairs={{0,8},{2,10},{4,12},{6,14},{8,0},{10,2},{12,4},{14,6},{16,24},{18,... | collective-permute-start | bytes 589832 | tf_op jit(solution)/shard_map/ppermute | solution.py:306
  112.2 5.7 %collective-permute-start.24 = (f32[1,3,64,256]{3,2,1,0:T(8,128)S(1)}, f32[1,3,64,256]{3,2,1,0:T(8,128)S(1)}, u32[]{:S(2)}, u32[]{:S(2)}) collective-permute-start(f32[1,3,64,256]{3,2,1,0:T(8,128)S(1)} %collective-permute-done.23.refs_4_), channel_id=1, source_target_pairs={{0,8},{2,10},{4,12},{6,14},{8,0},{10,2},{12,4},{14,6},{16,24},{18,... | collective-permute-start | bytes 589832 | tf_op jit(solution)/shard_map/ppermute | solution.py:306
  121.6 27.8 %collective-permute-start.28 = (f32[2,256,256]{2,1,0:T(8,128)S(1)}, f32[2,256,256]{2,1,0:T(8,128)S(1)}, u32[]{:S(2)}, u32[]{:S(2)}) collective-permute-start(f32[2,256,256]{2,1,0:T(8,128)S(1)} %get-tuple-element.116), channel_id=1, source_target_pairs={{0,2},{2,0},{4,6},{6,4},{8,10},{10,8},{12,14},{14,12},{16,18},{18,... | collective-permute-start | bytes 1572872 | tf_op jit(solution)/shard_map/ppermute | solution.py:306
  122.7 26.7 %collective-permute-start.29 = (f32[2,256,256]{2,1,0:T(8,128)S(1)}, f32[2,256,256]{2,1,0:T(8,128)S(1)}, u32[]{:S(2)}, u32[]{:S(2)}) collective-permute-start(f32[2,256,256]{2,1,0:T(8,128)S(1)} %get-tuple-element.117), channel_id=1, source_target_pairs={{0,4},{2,6},{4,0},{6,2},{8,12},{10,14},{12,8},{14,10},{16,20},{18,... | collective-permute-start | bytes 1572872 | tf_op jit(solution)/shard_map/ppermute | solution.py:306
  123.5 25.9 %collective-permute-start.30 = (f32[2,256,256]{2,1,0:T(8,128)S(1)}, f32[2,256,256]{2,1,0:T(8,128)S(1)}, u32[]{:S(2)}, u32[]{:S(2)}) collective-permute-start(f32[2,256,256]{2,1,0:T(8,128)S(1)} %get-tuple-element.118), channel_id=1, source_target_pairs={{0,6},{2,4},{4,2},{6,0},{8,14},{10,12},{12,10},{14,8},{16,22},{18,... | collective-permute-start | bytes 1572872 | tf_op jit(solution)/shard_map/ppermute | solution.py:306
  125.2 5.7 %collective-permute-start.32 = (f32[1,3,64,256]{3,2,1,0:T(8,128)S(1)}, f32[1,3,64,256]{3,2,1,0:T(8,128)S(1)}, u32[]{:S(2)}, u32[]{:S(2)}) collective-permute-start(f32[1,3,64,256]{3,2,1,0:T(8,128)S(1)} %get-tuple-element.122), channel_id=1, source_target_pairs={{0,8},{2,10},{4,12},{6,14},{8,0},{10,2},{12,4},{14,6},{16,24},{18,... | collective-permute-start | bytes 589832 | tf_op jit(solution)/shard_map/ppermute | solution.py:306
  125.8 7.2 %collective-permute-start.31 = (f32[1,3,64,256]{3,2,1,0:T(8,128)S(1)}, f32[1,3,64,256]{3,2,1,0:T(8,128)S(1)}, u32[]{:S(2)}, u32[]{:S(2)}) collective-permute-start(f32[1,3,64,256]{3,2,1,0:T(8,128)S(1)} %get-tuple-element.120), channel_id=1, source_target_pairs={{0,8},{2,10},{4,12},{6,14},{8,0},{10,2},{12,4},{14,6},{16,24},{18,... | collective-permute-start | bytes 589832 | tf_op jit(solution)/shard_map/ppermute | solution.py:306
  130.9 8.7 %collective-permute-start.33 = (f32[1,3,64,256]{3,2,1,0:T(8,128)S(1)}, f32[1,3,64,256]{3,2,1,0:T(8,128)S(1)}, u32[]{:S(2)}, u32[]{:S(2)}) collective-permute-start(f32[1,3,64,256]{3,2,1,0:T(8,128)S(1)} %add.40), channel_id=1, source_target_pairs={{0,16},{2,18},{4,20},{6,22},{8,24},{10,26},{12,28},{14,30},{16,0},... | collective-permute-start | bytes 589832 | tf_op jit(solution)/shard_map/ppermute | solution.py:306
  140.2 4.2 %collective-permute-start.34 = (f32[1,3,16,256]{3,2,1,0:T(8,128)S(1)}, f32[1,3,16,256]{3,2,1,0:T(8,128)S(1)}, u32[]{:S(2)}, u32[]{:S(2)}) collective-permute-start(f32[1,3,16,256]{3,2,1,0:T(8,128)S(1)} %get-tuple-element.124), channel_id=1, source_target_pairs={{0,2},{2,0},{4,6},{6,4},{8,10},{10,8},{12,14},{14,12},{16,18},{18,... | collective-permute-start | bytes 147464 | tf_op jit(solution)/shard_map/ppermute | solution.py:306
  141.3 4.1 %collective-permute-start.36 = (f32[1,3,16,256]{3,2,1,0:T(8,128)S(1)}, f32[1,3,16,256]{3,2,1,0:T(8,128)S(1)}, u32[]{:S(2)}, u32[]{:S(2)}) collective-permute-start(f32[1,3,16,256]{3,2,1,0:T(8,128)S(1)} %get-tuple-element.126), channel_id=1, source_target_pairs={{0,2},{2,0},{4,6},{6,4},{8,10},{10,8},{12,14},{14,12},{16,18},{18,... | collective-permute-start | bytes 147464 | tf_op jit(solution)/shard_map/ppermute | solution.py:306
  144.4 4.1 %collective-permute-start.35 = (f32[1,3,16,256]{3,2,1,0:T(8,128)S(1)}, f32[1,3,16,256]{3,2,1,0:T(8,128)S(1)}, u32[]{:S(2)}, u32[]{:S(2)}) collective-permute-start(f32[1,3,16,256]{3,2,1,0:T(8,128)S(1)} %get-tuple-element.125), channel_id=1, source_target_pairs={{0,4},{2,6},{4,0},{6,2},{8,12},{10,14},{12,8},{14,10},{16,20},{18,... | collective-permute-start | bytes 147464 | tf_op jit(solution)/shard_map/ppermute | solution.py:306
  145.3 4.1 %collective-permute-start.37 = (f32[1,3,16,256]{3,2,1,0:T(8,128)S(1)}, f32[1,3,16,256]{3,2,1,0:T(8,128)S(1)}, u32[]{:S(2)}, u32[]{:S(2)}) collective-permute-start(f32[1,3,16,256]{3,2,1,0:T(8,128)S(1)} %collective-permute-done.36), channel_id=1, source_target_pairs={{0,4},{2,6},{4,0},{6,2},{8,12},{10,14},{12,8},{14,10},{16,20},{18,... | collective-permute-start | bytes 147464 | tf_op jit(solution)/shard_map/ppermute | solution.py:306

commit v8 on v7

--- a/solution.py
+++ b/solution.py
@@ -77,8 +77,9 @@
         outs[step][...] = scaled.astype(BF16).astype(F32)
 
 
-def split_apply_kernel(groups, place, q, cot, gain, *rest):
-    outs, scratch = rest[:groups], rest[groups]
+def split_apply_kernel(groups, place, q, cot, gain, scale, *rest):
+    outs, scale_row, scratch = rest[:groups], rest[groups], rest[groups + 1]
+    scale_row[...] = jnp.broadcast_to(scale[...], scale_row.shape)
     split_kernel(groups, place, q, *[out.at[0] for out in outs], scratch)
     split_kernel(groups, place, cot, *[out.at[1] for out in outs], scratch)
     for step in range(groups):
@@ -102,16 +103,12 @@
             out[i] = sums[:, pl.ds(at, rows), :]
 
 
-def update_kernel(groups, depth, scale, place, *refs):
-    keys_in, scaled_in = refs[:groups], refs[groups : 2 * groups]
-    w_gate, w_out, w_up = refs[2 * groups : 2 * groups + 3]
-    key_kept, scaled_kept = refs[2 * groups + 3 : 2 * groups + 5]
-    outs, sums = refs[2 * groups + 5 : -1], refs[-1]
-    gate_b, out_b, up_b = (w[...].astype(BF16) for w in (w_gate, w_out, w_up))
+def update_sums(keys_in, scaled_in, weights, key_kept, scaled_kept):
+    gate_b, out_b, up_b = (w[...].astype(BF16) for w in weights)
     total = [0.0, 0.0, 0.0]
-    for step in range(groups):
-        keys = keys_in[step][...].astype(BF16)
-        scaled = scaled_in[step][...].astype(BF16)
+    for step, (key, value) in enumerate(zip(keys_in, scaled_in)):
+        keys = key[...].astype(BF16)
+        scaled = value[...].astype(BF16)
         key_kept[step] = keys
         scaled_kept[step] = scaled
         first = mm(keys, gate_b)
@@ -126,12 +123,20 @@
         total[0] += tmm(keys, dfirst)
         total[1] += tmm(act, scaled)
         total[2] += tmm(keys, dthird)
+    return total
+
+
+def update_kernel(count, depth, scale, place, *refs):
+    keys_in, scaled_in, weights = refs[:count], refs[count : 2 * count], refs[2 * count :][:3]
+    key_kept, scaled_kept = refs[2 * count + 3 : 2 * count + 5]
+    outs, sums = refs[2 * count + 5 : -1], refs[-1]
+    total = update_sums(keys_in, scaled_in, weights, key_kept, scaled_kept)
     for i in range(3):
         sums[i] = total[i] * scale
     send_slices(sums, outs, place[1], depth)
     rows = sums.shape[1] // depth
     at = pl.multiple_of(place[1] * rows, rows)
-    for i, w in enumerate((w_gate, w_out, w_up)):
+    for i, w in enumerate(weights):
         outs[-1][0, i] += w[pl.ds(at, rows), :]
 
 
@@ -142,10 +147,10 @@
         whole[:, pl.ds(at, rows), :] = part[0]
 
 
-def apply_kernel(groups, depth, place, head_scale, *refs):
+def apply_kernel(groups, depth, place, scale_row, *refs):
     pieces = refs[:groups]
     parts = refs[groups : groups + depth]
-    first_ref, third_ref, os_ref, new_b, stats, whole = refs[groups + depth :]
+    activ_ref, slope_ref, hidden_ref, os_ref, new_b, stats, whole = refs[groups + depth :]
     assemble(place, parts, whole)
     new_b[...] = whole[...].astype(BF16)
     for step in range(groups):
@@ -153,10 +158,13 @@
         tokens = queries.shape[0]
         first = mm(queries, new_b[0])
         third = mm(queries, new_b[2])
-        hidden = (first * jax.nn.sigmoid(first) * third).astype(BF16)
-        scaled = mm(hidden, new_b[1]) * head_scale[...]
-        first_ref[step] = first
-        third_ref[step] = third
+        sig = jax.nn.sigmoid(first)
+        activ = first * sig
+        hidden = (activ * third).astype(BF16)
+        scaled = mm(hidden, new_b[1]) * scale_row[0:1, :]
+        activ_ref[step] = activ
+        slope_ref[step] = third * (sig * (1.0 + first * (1.0 - sig)))
+        hidden_ref[step] = hidden
         os_ref[step] = scaled
         sq = jnp.sum(scaled * scaled, axis=1, keepdims=True)
         ps = jnp.sum(scaled * pieces[step][1], axis=1, keepdims=True)
@@ -167,13 +175,11 @@
         stats[1, pl.ds(source, 1), :] = both[1:2, :]
 
 
-def apply_back_kernel(groups, depth, count, place, head_scale, *refs):
-    pieces = refs[:groups]
-    stats = refs[groups : 2 * groups]
-    first_ref, third_ref, os_ref, new_b = refs[2 * groups : 2 * groups + 4]
-    outs = refs[2 * groups + 4 : 3 * groups + 4]
-    slices, sums, both = refs[3 * groups + 4 : -2], refs[-2], refs[-1]
-    hs = head_scale[...]
+def apply_back_kernel(groups, depth, count, place, scale_row, *refs):
+    pieces, stats = refs[:groups], refs[groups : 2 * groups]
+    activ_ref, slope_ref, hidden_ref, os_ref, new_b = refs[2 * groups : 2 * groups + 5]
+    outs = refs[2 * groups + 5 : 3 * groups + 5]
+    slices, sums, both = refs[3 * groups + 5 : -2], refs[-2], refs[-1]
     total_stats = stats[0][...]
     for other in stats[1:]:
         total_stats += other[...]
@@ -185,68 +191,74 @@
         sq = rate_column(both.at[0], source)
         ps = rate_column(both.at[1], source)
         inv = lax.rsqrt(sq / count + 1e-06)
-        scaled = os_ref[step]
-        dos = inv * pieces[step][1] - scaled * (inv * inv * inv * ps / count)
-        dout = (dos * hs).astype(BF16)
-        first = first_ref[step]
-        third = third_ref[step]
-        sig = jax.nn.sigmoid(first)
-        activ = first * sig
-        hidden = (activ * third).astype(BF16)
+        dos = inv * pieces[step][1] - os_ref[step] * (inv * inv * inv * ps / count)
+        dout = (dos * scale_row[0:1, :]).astype(BF16)
         dhidden = mm_t(dout, new_b[1])
-        dthird = (dhidden * activ).astype(BF16)
-        dfirst = (dhidden * third * (sig * (1.0 + first * (1.0 - sig)))).astype(BF16)
+        dthird = (dhidden * activ_ref[step]).astype(BF16)
+        dfirst = (dhidden * slope_ref[step]).astype(BF16)
         outs[step][...] = mm_t(dfirst, new_b[0]) + mm_t(dthird, new_b[2])
         total[0] += tmm(queries, dfirst)
-        total[1] += tmm(hidden, dout)
+        total[1] += tmm(hidden_ref[step], dout)
         total[2] += tmm(queries, dthird)
     for i in range(3):
         sums[i] = total[i]
     send_slices(sums, slices, place[1], depth)
 
 
+def update_keep_kernel(k_kept, s_kept, w_gate, w_out, w_up, *outs):
+    dact_r, third_r, activ_r, deriv_r, slope_r, second_r, dfirst_r, dthird_r, act_r = outs
+    gate_b, out_b, up_b = (w[...].astype(BF16) for w in (w_gate, w_out, w_up))
+    for step in range(k_kept.shape[0]):
+        keys, scaled = k_kept[step], s_kept[step]
+        first = mm(keys, gate_b)
+        third = mm(keys, up_b)
+        dact = mm_t(scaled, out_b)
+        sig = jax.nn.sigmoid(first)
+        activ = first * sig
+        slope = sig * (1.0 - sig)
+        deriv = sig + first * slope
+        third_deriv = third * deriv
+        dact_r[step] = dact
+        third_r[step] = third
+        activ_r[step] = activ
+        deriv_r[step] = deriv
+        slope_r[step] = third_deriv
+        second_r[step] = third * (slope * (2.0 + first * (1.0 - 2.0 * sig)))
+        dfirst_r[step] = (dact * third_deriv).astype(BF16)
+        dthird_r[step] = (dact * activ).astype(BF16)
+        act_r[step] = (activ * third).astype(BF16)
+
+
 def update_back_kernel(groups, depth, scale, place, *refs):
-    keys_in, scaled_in = refs[:2]
-    parts = refs[2 : depth + 2]
-    w_gate, w_out, w_up = refs[depth + 2 : depth + 5]
-    base = depth + 5
-    outs = refs[base : base + groups]
-    slices = refs[base + groups : -2]
+    (k_kept, s_kept), refs = refs[:2], refs[2:]
+    kept, refs = refs[:9], refs[9:]
+    dact_r, third_r, activ_r, deriv_r, slope_r, second_r, dfirst_r, dthird_r, act_r = kept
+    parts, refs = refs[:depth], refs[depth:]
+    w_gate, w_out, w_up = refs[:3]
+    outs, slices = refs[3 : groups + 3], refs[groups + 3 : -2]
     whole, sums = refs[-2:]
     assemble(place, parts, whole)
     gate_b, out_b, up_b = (w[...].astype(BF16) for w in (w_gate, w_out, w_up))
     cot_gate, cot_out, cot_up = ((whole[i] * scale).astype(BF16) for i in range(3))
     total = [0.0, 0.0, 0.0]
     for step in range(groups):
-        keys = keys_in[step]
-        scaled = scaled_in[step]
-        first = mm(keys, gate_b)
-        third = mm(keys, up_b)
-        sig = jax.nn.sigmoid(first)
-        activ = first * sig
-        act = (activ * third).astype(BF16)
-        dact = mm_t(scaled, out_b)
-        slope = sig * (1.0 - sig)
-        deriv = sig + first * slope
-        second = slope * (2.0 + first * (1.0 - 2.0 * sig))
-        third_deriv = third * deriv
-        dfirst = (dact * third_deriv).astype(BF16)
-        dthird = (dact * activ).astype(BF16)
+        keys, scaled = k_kept[step], s_kept[step]
         bar_dfirst = mm(keys, cot_gate)
         bar_dthird = mm(keys, cot_up)
         bar_act = mm_t(scaled, cot_out)
-        bar_activ = bar_dthird * dact + bar_act * third
-        bar_dact = (bar_dfirst * third_deriv + bar_dthird * activ).astype(BF16)
+        dact, activ, deriv = dact_r[step], activ_r[step], deriv_r[step]
+        bar_activ = bar_dthird * dact + bar_act * third_r[step]
+        bar_dact = (bar_dfirst * slope_r[step] + bar_dthird * activ).astype(BF16)
         bar_df_dact = bar_dfirst * dact
         bar_third = (bar_df_dact * deriv + bar_act * activ).astype(BF16)
-        bar_first = (bar_activ * deriv + bar_df_dact * third * second).astype(BF16)
+        bar_first = (bar_activ * deriv + bar_df_dact * second_r[step]).astype(BF16)
         outs[step][0] = (
-            mm_t(dfirst, cot_gate)
-            + mm_t(dthird, cot_up)
+            mm_t(dfirst_r[step], cot_gate)
+            + mm_t(dthird_r[step], cot_up)
             + mm_t(bar_first, gate_b)
             + mm_t(bar_third, up_b)
         )
-        outs[step][1] = mm(act, cot_out) + mm(bar_dact, out_b)
+        outs[step][1] = mm(act_r[step], cot_out) + mm(bar_dact, out_b)
         total[0] += tmm(keys, bar_first)
         total[1] += tmm(bar_dact, scaled)
         total[2] += tmm(keys, bar_third)
@@ -279,13 +291,15 @@
 
 
 def rows_kernel(groups, place, *refs):
-    count = len(send_groups(groups))
-    parts, outs, total = refs[: -count - 1], refs[-count - 1 : -1], refs[-1]
+    parts, outs, total = refs[: -groups - 1], refs[-groups - 1 : -1], refs[-1]
     summed = parts[0][0]
     for part in parts[1:]:
         summed += part[0]
     total[...] = summed
-    send_slices(total, outs, place[0], groups)
+    rows = total.shape[1] // groups
+    for step, out in enumerate(outs):
+        at = pl.multiple_of((place[0] ^ step) * rows, rows)
+        out[0] = total[:, pl.ds(at, rows), :]
 
 
 def local(queries, keys, values, rates, head_scale, gain, w_gate, w_out, w_up, cotangent):
@@ -311,10 +325,12 @@
     def forwarded(got):
         return [got[:1]] if got.shape[0] == 1 else [got[i : i + 1] for i in range(got.shape[0])]
 
-    def scatter(outs, count, unit):
+    def scatter(outs, count, unit, one_by_one=True):
         outs = list(outs)
         evens = list(range(2, count, 2))
         via = forwarded(move(outs.pop(0), "ctx", unit)) if evens else []
+        if one_by_one:
+            via, outs[0] = after(via, outs[0])
         first = [move(outs[0], "ctx", unit)] if count > 1 else []
         even = [move(p + v, "ctx", r * unit) for p, v, r in zip(outs[1:], via, evens)]
         return [outs[-1]] + first + even
@@ -328,14 +344,6 @@
             got[1] = move(part, "ctx", unit)
         return got
 
-    def rows_exchange(outs):
-        outs, evens = list(outs), list(range(2, groups, 2))
-        via = forwarded(move(outs.pop(0), "ctx", 1)) if evens else []
-        got = [outs[-1]] + [move(outs[0], "ctx", 1)] * (groups > 1)
-        for i, r in enumerate(evens):
-            got += [move(outs[1 + i], "ctx", r), move(via[i], "ctx", r)]
-        return got
-
     def after(x, *others):
         return lax.optimization_barrier((x, *others))
 
@@ -350,31 +358,36 @@
     square = pltpu.VMEM((3, hidden, width), F32)
 
     def split(body, *args):
-        return call(functools.partial(body, groups), pieces, [scratch], flops // 16, place, *args)
+        return call(functools.partial(body, groups), pieces, [scratch], 16 * flops, place, *args)
 
     k_in = in_plane(split(split_kernel, keys[0]))
     s_in = in_plane(split(split_scaled_kernel, values[0], rates[0]))
     own = [lax.dynamic_index_in_dim(w, mine, 0, keepdims=False) for w in (w_gate, w_out, w_up)]
     own_scale = lax.dynamic_index_in_dim(head_scale, mine, 0, keepdims=True)[None, :]
     k_in, s_in, queries, cotangent = after(k_in, s_in, queries, cotangent)
-    kept_b = shape(groups, tokens, width, dtype=BF16)
+
+    def kept(*dims, dtype=F32):
+        return shape(*dims, tokens, width, dtype=dtype)
+
     out = call(
-        functools.partial(update_kernel, groups, depth, scale), [kept_b] * 2 + slices, [square],
-        6 * flops, place, *k_in, *s_in, *own,
-    )
-    k_in, s_in, terms = out[0], out[1], out[2:]
-    q_out = call(
-        functools.partial(split_apply_kernel, groups), [shape(2, tokens, width)] * groups,
-        [scratch], flops // 8, place, queries[0], cotangent[0], gain,
+        functools.partial(update_kernel, groups, depth, scale),
+        [kept(groups, dtype=BF16)] * 2 + slices, [square], 6 * flops,
+        place, *k_in, *s_in, *own,
+    )
+    early, terms = out[:2], out[2:]
+    *q_out, scale_row = call(
+        functools.partial(split_apply_kernel, groups),
+        [shape(2, tokens, width)] * groups + [shape(8, width)],
+        [scratch], flops // 8, place, queries[0], cotangent[0], gain, own_scale,
     )
     q_in = in_plane(q_out)
     new = functools.reduce(jnp.add, scatter(terms, depth, groups))
     new = gather(new, depth, groups)
-    kept = shape(groups, tokens, width)
-    first, third, scaled, new_b, stats = call(
+    *passed, stats = call(
         functools.partial(apply_kernel, groups, depth),
-        [kept, kept, kept, shape(3, hidden, width, dtype=BF16), shape(2, groups, tokens)],
-        [square], 3 * flops, place, own_scale, *q_in, *new,
+        [kept(groups), kept(groups), kept(groups, dtype=BF16), kept(groups)]
+        + [shape(3, hidden, width, dtype=BF16), shape(2, groups, tokens)],
+        [square], 3 * flops, place, scale_row, *q_in, *new,
     )
     bit = 1
     while bit < head_axis:
@@ -383,8 +396,12 @@
     out = call(
         functools.partial(apply_back_kernel, groups, depth, count), pieces + slices,
         [square, pltpu.VMEM((2, groups, tokens), F32)], 6 * flops,
-        place, own_scale, *q_in, *in_plane([stats] * groups),
-        first, third, scaled, new_b,
+        place, scale_row, *q_in, *in_plane([stats] * groups), *passed,
+    )
+    out, early = after(out, early)
+    saved = call(
+        update_keep_kernel, [kept(groups)] * 6 + [kept(groups, dtype=BF16)] * 3, [], 3 * flops,
+        *early, *own,
     )
     part = functools.reduce(jnp.add, scatter(out[groups:], depth, groups))
     parts = gather(part, depth, groups)
@@ -392,25 +409,25 @@
         functools.partial(join_query_kernel, groups), [joined], [scratch], flops // 16,
         place, *in_plane(out[:groups]),
     )
-    parts, grad_q = after(parts, grad_q)
+    parts, grad_q, saved = after(parts, grad_q, saved)
     rows = hidden // depth
     out = call(
         functools.partial(update_back_kernel, groups, depth, scale),
-        [shape(2, tokens, width)] * groups + slices, [square] * 2, 15 * flops,
-        place, k_in, s_in, *parts, *own,
+        [shape(2, tokens, width)] * groups + slices, [square] * 2, 12 * flops,
+        place, *early, *saved, *parts, *own,
     )
     back = in_plane(out[:groups])
-    ends = scatter(out[groups:], depth, groups)
+    ends = scatter(out[groups:], depth, groups, one_by_one=False)
     own_rows = rows // groups
     sent = call(
         functools.partial(rows_kernel, groups),
-        [shape(len(m), 3, own_rows, width) for m in send_groups(groups)],
+        [shape(1, 3, own_rows, width)] * groups,
         [pltpu.VMEM((3, rows, width), F32)], flops // 100, place, part, *ends,
     )
     grad_k, grad_v, *grads = call(
         functools.partial(join_update_kernel, groups),
         [joined] * 2 + [shape(heads, own_rows, width)] * 3, [scratch] * 2, flops // 8,
-        place, rates[0], *back, *rows_exchange(sent),
+        place, rates[0], *back, *in_plane(sent),
     )
     if lax.axis_size("batch") > 1:
         grads = [lax.psum_scatter(x, "batch", scatter_dimension=1, tiled=True) for x in grads]

time: 152 us -> 146 us (0.961)
  waiting for transfers between devices: 84.6 us -> 75 us
  starting transfers between devices: 42.5 us -> 46.3 us
    ppermute x38 -> x37, waiting for transfers between devices: 84.6 us -> 75 us  [move(): lax.ppermute(x, axis, [(c, c ^ step) for c in range(lax.axis_size(axis))])]
    ppermute x38 -> x37, starting transfers between devices: 42.5 us -> 46.3 us  [move(): lax.ppermute(x, axis, [(c, c ^ step) for c in range(lax.axis_size(axis))])]
    pallas_call x10 -> x11, Pallas kernels: 20.9 us -> 19.5 us  [call(): pl.pallas_call(body, out_shape=out_shape, in_specs=[smem if a.dtype == jn...]
  transfers between devices with their start and end apart: 38 -> 37, of which waited for: 26 -> 22; matrix products, arithmetic and copies ran while one was open for 1% -> 1% of each run, Pallas kernels for 4% -> 5%
where the time goes in v8:
time: 146 us; the launch traced here: 145 us
  waiting for transfers between devices  75 us (51%)
  starting transfers between devices  46.3 us (32%)
  Pallas kernels  19.5 us (13%)
  local copies, waits for them, and re-layouts  3.6 us (2%)
    ppermute x37, waiting for transfers between devices, move(): lax.ppermute(x, axis, [(c, c ^ step) for c in range(lax.axis_size(axis))])  75 us
    ppermute x37, starting transfers between devices, move(): lax.ppermute(x, axis, [(c, c ^ step) for c in range(lax.axis_size(axis))])  46.3 us
    pallas_call x11, Pallas kernels, call(): pl.pallas_call(body, out_shape=out_shape, in_specs=[smem if a.dtype == jn...  19.5 us
  transfers between devices with their start and end apart: 37, of which 22 were waited for; matrix products, arithmetic and copies ran while one was open for 1% of the time, Pallas kernels for 5%

profile of v8, /device:TPU:0, one launch (start us, length us, event | category | flops | bytes accessed | tf_op | source)
XLA Modules:
  0.0 145.4 jit_solution(6691174951592592546)
XLA Ops:
  0.7 1.1 copy-done.5
  1.8 0.9 shard_map.145
  2.8 3.0 %collective-permute-start = (f32[256,256]{1,0:T(8,128)S(1)}, f32[256,256]{1,0:T(8,128)S(1)}, u32[]{:S(2)}, u32[]{:S(2)}) collective-permute-start(f32[256,256]{1,0:T(8,128)S(1)} %get-tuple-element.104), channel_id=1, source_target_pairs={{0,2},{2,0},{4,6},{6,4},{8,10},{10,8},{12,14},{14,12},{16,18},{18,... | collective-permute-start | bytes 786440 | tf_op jit(solution)/shard_map/ppermute | solution.py:320
  5.8 1.5 %collective-permute-start.1 = (f32[256,256]{1,0:T(8,128)S(1)}, f32[256,256]{1,0:T(8,128)S(1)}, u32[]{:S(2)}, u32[]{:S(2)}) collective-permute-start(f32[256,256]{1,0:T(8,128)S(1)} %get-tuple-element.105), channel_id=1, source_target_pairs={{0,4},{2,6},{4,0},{6,2},{8,12},{10,14},{12,8},{14,10},{16,20},{18,... | collective-permute-start | bytes 786440 | tf_op jit(solution)/shard_map/ppermute | solution.py:320
  7.3 1.8 %shard_map.146 = (f32[256,256]{1,0:T(8,128)S(1)}, f32[256,256]{1,0:T(8,128)}, f32[256,256]{1,0:T(8,128)}, f32[256,256]{1,0:T(8,128)S(1)}) custom-call(s32[2]{0:T(128)S(1)} %pad_add_fusion.place, bf16[256,4,256]{2,1,0:T(4,128)(2,1)S(1)} %bitcast.22, f32[4,256]{1,0:T(4,128)S(1)} %bitcast.19), custom_call_target="tpu_custom_call" | custom-call | flops 2147483648 | bytes 1576968 | tf_op jit(solution)/shard_map/pallas_call | solution.py:34
  9.1 0.7 copy-done.9
  9.8 1.9 %collective-permute-start.3 = (f32[256,256]{1,0:T(8,128)}, f32[256,256]{1,0:T(8,128)S(1)}, u32[]{:S(2)}, u32[]{:S(2)}) collective-permute-start(f32[256,256]{1,0:T(8,128)} %get-tuple-element.108), channel_id=1, source_target_pairs={{0,2},{2,0},{4,6},{6,4},{8,10},{10,8},{12,14},{14,12},{16,18},{18,... | collective-permute-start | bytes 786440 | tf_op jit(solution)/shard_map/ppermute | solution.py:320
  11.8 1.5 %collective-permute-start.4 = (f32[256,256]{1,0:T(8,128)}, f32[256,256]{1,0:T(8,128)S(1)}, u32[]{:S(2)}, u32[]{:S(2)}) collective-permute-start(f32[256,256]{1,0:T(8,128)} %get-tuple-element.109), channel_id=1, source_target_pairs={{0,4},{2,6},{4,0},{6,2},{8,12},{10,14},{12,8},{14,10},{16,20},{18,... | collective-permute-start | bytes 786440 | tf_op jit(solution)/shard_map/ppermute | solution.py:320
  13.3 2.6 %collective-permute-start.5 = (f32[256,256]{1,0:T(8,128)S(1)}, f32[256,256]{1,0:T(8,128)S(1)}, u32[]{:S(2)}, u32[]{:S(2)}) collective-permute-start(f32[256,256]{1,0:T(8,128)S(1)} %get-tuple-element.110), channel_id=1, source_target_pairs={{0,6},{2,4},{4,2},{6,0},{8,14},{10,12},{12,10},{14,8},{16,22},{18,... | collective-permute-start | bytes 786440 | tf_op jit(solution)/shard_map/ppermute | solution.py:320
  16.0 1.1 dynamic-slice_bitcast_fusion
  17.1 2.6 %collective-permute-done.1.refs_2_ = f32[256,256]{1,0:T(8,128)S(1)} collective-permute-done((f32[256,256]{1,0:T(8,128)S(1)}, f32[256,256]{1,0:T(8,128)S(1)}, u32[]{:S(2)}, u32[]{:S(2)}) %collective-permute-start.1) | collective-permute-done | bytes 262176 | tf_op jit(solution)/shard_map/ppermute | solution.py:320
  20.1 4.1 %collective-permute-done.3.refs_5_ = f32[256,256]{1,0:T(8,128)S(1)} collective-permute-done((f32[256,256]{1,0:T(8,128)}, f32[256,256]{1,0:T(8,128)S(1)}, u32[]{:S(2)}, u32[]{:S(2)}) %collective-permute-start.3) | collective-permute-done | bytes 262176 | tf_op jit(solution)/shard_map/ppermute | solution.py:320
  24.2 6.2 %collective-permute-done.4.refs_6_ = f32[256,256]{1,0:T(8,128)S(1)} collective-permute-done((f32[256,256]{1,0:T(8,128)}, f32[256,256]{1,0:T(8,128)S(1)}, u32[]{:S(2)}, u32[]{:S(2)}) %collective-permute-start.4) | collective-permute-done | bytes 262176 | tf_op jit(solution)/shard_map/ppermute | solution.py:320
  30.4 2.2 %shard_map.148 = (bf16[4,256,256]{2,1,0:T(8,128)(2,1)S(1)}, bf16[4,256,256]{2,1,0:T(8,128)(2,1)S(1)}, f32[1,3,64,256]{3,2,1,0:T(8,128)S(1)}, f32[1,3,64,256]{3,2...) custom-call(s32[2]{0:T(128)S(1)} %pad_add_fusion.place, f32[256,256]{1,0:T(8,128)S(1)} %copy-done.8, ...), custom_call_target="tpu_custom_call" | custom-call | flops 805306368 | bytes 4718600 | tf_op jit(solution)/shard_map/pallas_call | solution.py:34
  32.6 1.6 %collective-permute-start.9 = (f32[1,3,64,256]{3,2,1,0:T(8,128)S(1)}, f32[1,3,64,256]{3,2,1,0:T(8,128)S(1)}, u32[]{:S(2)}, u32[]{:S(2)}) collective-permute-start(f32[1,3,64,256]{3,2,1,0:T(8,128)S(1)} %get-tuple-element.127), channel_id=1, source_target_pairs={{0,8},{2,10},{4,12},{6,14},{8,0},{10,2},{12,4},{14,6},{16,24},{18,... | collective-permute-start | bytes 589832 | tf_op jit(solution)/shard_map/ppermute | solution.py:320
  34.3 4.1 %collective-permute-done.9 = f32[1,3,64,256]{3,2,1,0:T(8,128)S(1)} collective-permute-done((f32[1,3,64,256]{3,2,1,0:T(8,128)S(1)}, f32[1,3,64,256]{3,2,1,0:T(8,128)S(1)}, u32[]{:S(2)}, u32[]{:S(2)}) %collective-permute-start.9) | collective-permute-done | bytes 196640 | tf_op jit(solution)/shard_map/ppermute | solution.py:320
  38.4 2.7 %collective-permute-start.11 = (f32[1,3,64,256]{3,2,1,0:T(8,128)S(1)}, f32[1,3,64,256]{3,2,1,0:T(8,128)S(1)}, u32[]{:S(2)}, u32[]{:S(2)}) collective-permute-start(f32[1,3,64,256]{3,2,1,0:T(8,128)S(1)} %add.34), channel_id=1, source_target_pairs={{0,16},{2,18},{4,20},{6,22},{8,24},{10,26},{12,28},{14,30},{16,0},... | collective-permute-start | bytes 589832 | tf_op jit(solution)/shard_map/ppermute | solution.py:320
  41.1 1.6 %collective-permute-start.10 = (f32[1,3,64,256]{3,2,1,0:T(8,128)S(1)}, f32[1,3,64,256]{3,2,1,0:T(8,128)S(1)}, u32[]{:S(2)}, u32[]{:S(2)}) collective-permute-start(f32[1,3,64,256]{3,2,1,0:T(8,128)S(1)} %get-tuple-element.129), channel_id=1, source_target_pairs={{0,8},{2,10},{4,12},{6,14},{8,0},{10,2},{12,4},{14,6},{16,24},{18,... | collective-permute-start | bytes 589832 | tf_op jit(solution)/shard_map/ppermute | solution.py:320
  42.6 0.6 dynamic_slice.14
  43.2 1.9 %shard_map.147 = (f32[2,256,256]{2,1,0:T(8,128)S(1)}, f32[2,256,256]{2,1,0:T(8,128)S(1)}, f32[2,256,256]{2,1,0:T(8,128)S(1)}, f32[2,256,256]{2,1,0:T(8,128)S(1)}, f32[8,256]{1,0:T(8,128)S(1)}) custom-call(s32[2]{0:T(128)S(1)} %pad_add_fusion.place, bf16[256,4,256]{2,1,0:T(4,128)(2,1)S(1)} %bitcast.17, bf16[256,4,256]{2,1,0:T(4,128)(2,1)S(1)} %bitcast.18, ...), custom_call_target="tpu_custom_call" | custom-call | flops 16777216 | bytes 3158028 | tf_op jit(solution)/shard_map/pallas_call | solution.py:34
  45.2 1.4 collective-permute-start.6
  46.6 0.8 collective-permute-start.7
  47.4 1.4 collective-permute-start.8
  48.9 0.9 collective-permute-start.13
  49.8 2.9 %collective-permute-start.12 = (f32[1,3,64,256]{3,2,1,0:T(8,128)S(1)}, f32[1,3,64,256]{3,2,1,0:T(8,128)S(1)}, u32[]{:S(2)}, u32[]{:S(2)}) collective-permute-start(f32[1,3,64,256]{3,2,1,0:T(8,128)S(1)} %add_add_fusion.1.refs_4_), channel_id=1, source_target_pairs={{0,8},{2,10},{4,12},{6,14},{8,0},{10,2},{12,4},{14,6},{16,24},{18,... | collective-permute-start | bytes 589832 | tf_op jit(solution)/shard_map/ppermute | solution.py:320
  52.7 5.0 %collective-permute-done.13.refs_6_ = f32[1,3,64,256]{3,2,1,0:T(8,128)S(1)} collective-permute-done((f32[1,3,64,256]{3,2,1,0:T(8,128)S(1)}, f32[1,3,64,256]{3,2,1,0:T(8,128)S(1)}, u32[]{:S(2)}, u32[]{:S(2)}) %collective-permute-start.13) | collective-permute-done | bytes 196640 | tf_op jit(solution)/shard_map/ppermute | solution.py:320
  58.2 1.9 %collective-permute-done.6.refs_1_ = f32[2,256,256]{2,1,0:T(8,128)S(1)} collective-permute-done((f32[2,256,256]{2,1,0:T(8,128)S(1)}, f32[2,256,256]{2,1,0:T(8,128)S(1)}, u32[]{:S(2)}, u32[]{:S(2)}) %collective-permute-start.6) | collective-permute-done | bytes 524320 | tf_op jit(solution)/shard_map/ppermute | solution.py:320
  60.1 8.8 %collective-permute-done.7.refs_2_ = f32[2,256,256]{2,1,0:T(8,128)S(1)} collective-permute-done((f32[2,256,256]{2,1,0:T(8,128)S(1)}, f32[2,256,256]{2,1,0:T(8,128)S(1)}, u32[]{:S(2)}, u32[]{:S(2)}) %collective-permute-start.7) | collective-permute-done | bytes 524320 | tf_op jit(solution)/shard_map/ppermute | solution.py:320
  68.9 1.8 %shard_map.149 = (f32[4,256,256]{2,1,0:T(8,128)S(1)}, f32[4,256,256]{2,1,0:T(8,128)S(1)}, bf16[4,256,256]{2,1,0:T(8,128)(2,1)S(1)}, f32[4,256,256]{2,1,0:T(8,128...) custom-call(s32[2]{0:T(128)S(1)} %pad_add_fusion.place, f32[8,256]{1,0:T(8,128)S(1)} %get-tuple-element.113.scale_row, ...), custom_call_target="tpu_custom_call" | custom-call | flops 402653184 | bytes 6963208 | tf_op jit(solution)/shard_map/pallas_call | solution.py:34
  70.7 1.2 collective-permute-done.15
  71.9 1.2 collective-permute-start.18
  73.0 0.7 collective-permute-start.17
  73.7 1.7 %collective-permute-start.16 = (f32[2,4,256]{2,1,0:T(4,128)S(1)}, f32[2,4,256]{2,1,0:T(4,128)S(1)}, u32[]{:S(2)}, u32[]{:S(2)}) collective-permute-start(f32[2,4,256]{2,1,0:T(4,128)S(1)} %add.36.refs_4_), channel_id=1, source_target_pairs={{0,2},{2,0},{4,6},{6,4},{8,10},{10,8},{12,14},{14,12},{16,18},{18,... | collective-permute-start | bytes 24584 | tf_op jit(solution)/shard_map/ppermute | solution.py:320
  75.4 1.1 collective-permute-done.18.refs_7_
  76.7 0.7 collective-permute-done.16.refs_5_
  77.3 2.1 %shard_map.150 = (f32[256,256]{1,0:T(8,128)S(1)}, f32[256,256]{1,0:T(8,128)S(1)}, f32[256,256]{1,0:T(8,128)S(1)}, f32[256,256]{1,0:T(8,128)S(1)}, f32[1,3,64,256...) custom-call(s32[2]{0:T(128)S(1)} %pad_add_fusion.place, ...), custom_call_target="tpu_custom_call" | custom-call | flops 805306368 | bytes 8036360 | tf_op jit(solution)/shard_map/pallas_call | solution.py:34
  79.4 0.5 collective-permute-start.19
  80.0 5.2 %collective-permute-done.19 = f32[1,3,64,256]{3,2,1,0:T(8,128)S(1)} collective-permute-done((f32[1,3,64,256]{3,2,1,0:T(8,128)S(1)}, f32[1,3,64,256]{3,2,1,0:T(8,128)S(1)}, u32[]{:S(2)}, u32[]{:S(2)}) %collective-permute-start.19) | collective-permute-done | bytes 196640 | tf_op jit(solution)/shard_map/ppermute | solution.py:320
  85.6 0.8 collective-permute-start.20
  86.4 8.8 %collective-permute-done.21 = f32[1,3,64,256]{3,2,1,0:T(8,128)S(1)} collective-permute-done((f32[1,3,64,256]{3,2,1,0:T(8,128)S(1)}, f32[1,3,64,256]{3,2,1,0:T(8,128)S(1)}, u32[]{:S(2)}, u32[]{:S(2)}) %collective-permute-start.21) | collective-permute-done | bytes 196640 | tf_op jit(solution)/shard_map/ppermute | solution.py:320
  95.3 0.8 collective-permute-start.23
  96.1 1.5 %collective-permute-start.25 = (f32[256,256]{1,0:T(8,128)S(1)}, f32[256,256]{1,0:T(8,128)S(1)}, u32[]{:S(2)}, u32[]{:S(2)}) collective-permute-start(f32[256,256]{1,0:T(8,128)S(1)} %get-tuple-element.155), channel_id=1, source_target_pairs={{0,2},{2,0},{4,6},{6,4},{8,10},{10,8},{12,14},{14,12},{16,18},{18,... | collective-permute-start | bytes 786440 | tf_op jit(solution)/shard_map/ppermute | solution.py:320
  97.6 0.5 collective-permute-start.26
  98.0 1.5 %collective-permute-start.27 = (f32[256,256]{1,0:T(8,128)S(1)}, f32[256,256]{1,0:T(8,128)S(1)}, u32[]{:S(2)}, u32[]{:S(2)}) collective-permute-start(f32[256,256]{1,0:T(8,128)S(1)} %get-tuple-element.157), channel_id=1, source_target_pairs={{0,6},{2,4},{4,2},{6,0},{8,14},{10,12},{12,10},{14,8},{16,22},{18,... | collective-permute-start | bytes 786440 | tf_op jit(solution)/shard_map/ppermute | solution.py:320
  99.8 3.6 %collective-permute-done.23.refs_13_ = f32[1,3,64,256]{3,2,1,0:T(8,128)S(1)} collective-permute-done((f32[1,3,64,256]{3,2,1,0:T(8,128)S(1)}, f32[1,3,64,256]{3,2,1,0:T(8,128)S(1)}, u32[]{:S(2)}, u32[]{:S(2)}) %collective-permute-start.23) | collective-permute-done | bytes 196640 | tf_op jit(solution)/shard_map/ppermute | solution.py:320
  103.4 1.1 shard_map.152
  104.6 3.9 %collective-permute-done.26.refs_2_ = f32[256,256]{1,0:T(8,128)S(1)} collective-permute-done((f32[256,256]{1,0:T(8,128)S(1)}, f32[256,256]{1,0:T(8,128)S(1)}, u32[]{:S(2)}, u32[]{:S(2)}) %collective-permute-start.26) | collective-permute-done | bytes 262176 | tf_op jit(solution)/shard_map/ppermute | solution.py:320
  108.5 1.7 %shard_map.151 = bf16[256,4,256]{2,1,0:T(4,128)(2,1)} custom-call(s32[2]{0:T(128)S(1)} %pad_add_fusion.place, f32[256,256]{1,0:T(8,128)S(1)} %get-tuple-element.154.refs_0_, f32[256,256]{1,0:T(8,128)S(1)} %collective-permute-done.25.refs_1_, f32[256,256]{1,0:T(8,128)S(1)} %collective-permute-done.26.refs_2_, f32[256,256]{1,0:T(8,128)S(1)} %collective-permute-done.27.refs_3_), custom_call_target="tpu_custom_call" | custom-call | flops 8388608 | bytes 1572872 | tf_op jit(solution)/shard_map/pallas_call | solution.py:34
  110.2 3.0 %shard_map.153 = (f32[2,256,256]{2,1,0:T(8,128)S(1)}, f32[2,256,256]{2,1,0:T(8,128)S(1)}, f32[2,256,256]{2,1,0:T(8,128)S(1)}, f32[2,256,256]{2,1,0:T(8,128)S(1)}...) custom-call(s32[2]{0:T(128)S(1)} %pad_add_fusion.place, ...), custom_call_target="tpu_custom_call" | custom-call | flops 1610612736 | bytes 13369352 | tf_op jit(solution)/shard_map/pallas_call | solution.py:34
  113.2 0.7 collective-permute-start.28
  114.0 1.3 collective-permute-start.29
  115.3 1.5 %collective-permute-start.30 = (f32[2,256,256]{2,1,0:T(8,128)S(1)}, f32[2,256,256]{2,1,0:T(8,128)S(1)}, u32[]{:S(2)}, u32[]{:S(2)}) collective-permute-start(f32[2,256,256]{2,1,0:T(8,128)S(1)} %get-tuple-element.186), channel_id=1, source_target_pairs={{0,6},{2,4},{4,2},{6,0},{8,14},{10,12},{12,10},{14,8},{16,22},{18,... | collective-permute-start | bytes 1572872 | tf_op jit(solution)/shard_map/ppermute | solution.py:320
  116.8 2.0 %collective-permute-start.31 = (f32[1,3,64,256]{3,2,1,0:T(8,128)S(1)}, f32[1,3,64,256]{3,2,1,0:T(8,128)S(1)}, u32[]{:S(2)}, u32[]{:S(2)}) collective-permute-start(f32[1,3,64,256]{3,2,1,0:T(8,128)S(1)} %get-tuple-element.188), channel_id=1, source_target_pairs={{0,8},{2,10},{4,12},{6,14},{8,0},{10,2},{12,4},{14,6},{16,24},{18,... | collective-permute-start | bytes 589832 | tf_op jit(solution)/shard_map/ppermute | solution.py:320
  118.8 5.1 %collective-permute-done.32 = f32[1,3,64,256]{3,2,1,0:T(8,128)S(1)} collective-permute-done((f32[1,3,64,256]{3,2,1,0:T(8,128)S(1)}, f32[1,3,64,256]{3,2,1,0:T(8,128)S(1)}, u32[]{:S(2)}, u32[]{:S(2)}) %collective-permute-start.32) | collective-permute-done | bytes 196640 | tf_op jit(solution)/shard_map/ppermute | solution.py:320
  124.0 3.0 %collective-permute-start.33 = (f32[1,3,64,256]{3,2,1,0:T(8,128)S(1)}, f32[1,3,64,256]{3,2,1,0:T(8,128)S(1)}, u32[]{:S(2)}, u32[]{:S(2)}) collective-permute-start(f32[1,3,64,256]{3,2,1,0:T(8,128)S(1)} %add.40), channel_id=1, source_target_pairs={{0,16},{2,18},{4,20},{6,22},{8,24},{10,26},{12,28},{14,30},{16,0},... | collective-permute-start | bytes 589832 | tf_op jit(solution)/shard_map/ppermute | solution.py:320
  126.9 0.7 collective-permute-done.31.refs_2_
  127.6 5.1 %collective-permute-done.33.refs_3_ = f32[1,3,64,256]{3,2,1,0:T(8,128)S(1)} collective-permute-done((f32[1,3,64,256]{3,2,1,0:T(8,128)S(1)}, f32[1,3,64,256]{3,2,1,0:T(8,128)S(1)}, u32[]{:S(2)}, u32[]{:S(2)}) %collective-permute-start.33) | collective-permute-done | bytes 196640 | tf_op jit(solution)/shard_map/ppermute | solution.py:320
  132.7 0.6 shard_map.154
  133.3 0.8 collective-permute-start.34
  134.1 1.3 collective-permute-start.35
  135.4 2.6 %collective-permute-done.34.refs_5_ = f32[1,3,16,256]{3,2,1,0:T(8,128)S(1)} collective-permute-done((f32[1,3,16,256]{3,2,1,0:T(8,128)S(1)}, f32[1,3,16,256]{3,2,1,0:T(8,128)S(1)}, u32[]{:S(2)}, u32[]{:S(2)}) %collective-permute-start.34) | collective-permute-done | bytes 49184 | tf_op jit(solution)/shard_map/ppermute | solution.py:320
  138.0 1.4 collective-permute-start.36
  139.4 3.6 %collective-permute-done.36.refs_7_ = f32[1,3,16,256]{3,2,1,0:T(8,128)S(1)} collective-permute-done((f32[1,3,16,256]{3,2,1,0:T(8,128)S(1)}, f32[1,3,16,256]{3,2,1,0:T(8,128)S(1)}, u32[]{:S(2)}, u32[]{:S(2)}) %collective-permute-start.36) | collective-permute-done | bytes 49184 | tf_op jit(solution)/shard_map/ppermute | solution.py:320
  143.0 2.4 %shard_map.155 = (bf16[256,4,256]{2,1,0:T(4,128)(2,1)}, bf16[256,4,256]{2,1,0:T(4,128)(2,1)}, f32[4,16,256]{2,1,0:T(8,128)}, f32[4,16,256]{2,1,0:T(8,128)}, f32[4,16,256]{2,1,0:T(8,128)}) custom-call(s32[2]{0:T(128)S(1)} %pad_add_fusion.place, f32[4,256]{1,0:T(4,128)S(1)} %bitcast.20, f32[2,256,256]{2,1,0:T(8,128)S(1)} %get-tuple-element.183.refs_0_, ...), custom_call_target="tpu_custom_call" | custom-call | flops 16777216 | bytes 3543048 | tf_op jit(solution)/shard_map/pallas_call | solution.py:34
  (55 shorter events, 2.3 us)
Async XLA Ops:
  0.6 15.3 %copy-start = (f32[4,256,256]{2,1,0:T(8,128)S(1)}, f32[4,256,256]{2,1,0:T(8,128)}, u32[]{:S(2)}) copy-start(f32[4,256,256]{2,1,0:T(8,128)} %param.16) | copy-start | bytes 3145732
  0.7 1.1 copy-start.5
  1.8 5.5 %copy-start.6 = (bf16[1,256,4,256]{3,2,1,0:T(4,128)(2,1)S(1)}, bf16[1,256,4,256]{3,2,1,0:T(4,128)(2,1)}, u32[]{:S(2)}) copy-start(bf16[1,256,4,256]{3,2,1,0:T(4,128)(2,1)} %param.12) | copy-start | bytes 1572868
  2.7 6.4 %copy-start.7 = (f32[256,256]{1,0:T(8,128)}, f32[256,256]{1,0:T(8,128)S(1)}, u32[]{:S(2)}) copy-start(f32[256,256]{1,0:T(8,128)S(1)} %get-tuple-element.118.refs_0_) | copy-start | bytes 786436
  2.8 4.6 %copy-start.4 = (f32[1,4,256]{2,1,0:T(4,128)S(1)}, f32[1,4,256]{2,1,0:T(4,128)}, u32[]{:S(2)}) copy-start(f32[1,4,256]{2,1,0:T(4,128)} %param.13) | copy-start | bytes 12292
  2.8 10.5 %collective-permute-start = (f32[256,256]{1,0:T(8,128)S(1)}, f32[256,256]{1,0:T(8,128)S(1)}, u32[]{:S(2)}, u32[]{:S(2)}) collective-permute-start(f32[256,256]{1,0:T(8,128)S(1)} %get-tuple-element.104), channel_id=1, source_target_pairs={{0,2},{2,0},{4,6},{6,4},{8,10},{10,8},{12,14},{14,12},{16,18},{18,... | collective-permute-start | bytes 786440 | tf_op jit(solution)/shard_map/ppermute | solution.py:320
  5.8 13.9 %collective-permute-start.1 = (f32[256,256]{1,0:T(8,128)S(1)}, f32[256,256]{1,0:T(8,128)S(1)}, u32[]{:S(2)}, u32[]{:S(2)}) collective-permute-start(f32[256,256]{1,0:T(8,128)S(1)} %get-tuple-element.105), channel_id=1, source_target_pairs={{0,4},{2,6},{4,0},{6,2},{8,12},{10,14},{12,8},{14,10},{16,20},{18,... | collective-permute-start | bytes 786440 | tf_op jit(solution)/shard_map/ppermute | solution.py:320
  7.3 12.8 %collective-permute-start.2 = (f32[256,256]{1,0:T(8,128)S(1)}, f32[256,256]{1,0:T(8,128)S(1)}, u32[]{:S(2)}, u32[]{:S(2)}) collective-permute-start(f32[256,256]{1,0:T(8,128)S(1)} %get-tuple-element.106), channel_id=1, source_target_pairs={{0,6},{2,4},{4,2},{6,0},{8,14},{10,12},{12,10},{14,8},{16,22},{18,... | collective-permute-start | bytes 786440 | tf_op jit(solution)/shard_map/ppermute | solution.py:320
  9.1 0.7 copy-start.9
  9.8 14.4 %collective-permute-start.3 = (f32[256,256]{1,0:T(8,128)}, f32[256,256]{1,0:T(8,128)S(1)}, u32[]{:S(2)}, u32[]{:S(2)}) collective-permute-start(f32[256,256]{1,0:T(8,128)} %get-tuple-element.108), channel_id=1, source_target_pairs={{0,2},{2,0},{4,6},{6,4},{8,10},{10,8},{12,14},{14,12},{16,18},{18,... | collective-permute-start | bytes 786440 | tf_op jit(solution)/shard_map/ppermute | solution.py:320
  11.8 18.6 %collective-permute-start.4 = (f32[256,256]{1,0:T(8,128)}, f32[256,256]{1,0:T(8,128)S(1)}, u32[]{:S(2)}, u32[]{:S(2)}) collective-permute-start(f32[256,256]{1,0:T(8,128)} %get-tuple-element.109), channel_id=1, source_target_pairs={{0,4},{2,6},{4,0},{6,2},{8,12},{10,14},{12,8},{14,10},{16,20},{18,... | collective-permute-start | bytes 786440 | tf_op jit(solution)/shard_map/ppermute | solution.py:320
  13.3 17.1 %collective-permute-start.5 = (f32[256,256]{1,0:T(8,128)S(1)}, f32[256,256]{1,0:T(8,128)S(1)}, u32[]{:S(2)}, u32[]{:S(2)}) collective-permute-start(f32[256,256]{1,0:T(8,128)S(1)} %get-tuple-element.110), channel_id=1, source_target_pairs={{0,6},{2,4},{4,2},{6,0},{8,14},{10,12},{12,10},{14,8},{16,22},{18,... | collective-permute-start | bytes 786440 | tf_op jit(solution)/shard_map/ppermute | solution.py:320
  15.9 14.5 %copy-start.8 = (f32[256,256]{1,0:T(8,128)S(1)}, f32[256,256]{1,0:T(8,128)}, u32[]{:S(2)}) copy-start(f32[256,256]{1,0:T(8,128)} %copy-done.7) | copy-start | bytes 786436
  16.0 14.4 %copy-start.10 = (f32[256,256]{1,0:T(8,128)S(1)}, f32[256,256]{1,0:T(8,128)}, u32[]{:S(2)}) copy-start(f32[256,256]{1,0:T(8,128)} %copy-done.9) | copy-start | bytes 786436
  30.4 12.8 %copy-start.2 = (bf16[1,256,4,256]{3,2,1,0:T(4,128)(2,1)S(1)}, bf16[1,256,4,256]{3,2,1,0:T(4,128)(2,1)}, u32[]{:S(2)}) copy-start(bf16[1,256,4,256]{3,2,1,0:T(4,128)(2,1)} %param.19) | copy-start | bytes 1572868
  32.6 10.6 %copy-start.1 = (bf16[1,256,4,256]{3,2,1,0:T(4,128)(2,1)S(1)}, bf16[1,256,4,256]{3,2,1,0:T(4,128)(2,1)}, u32[]{:S(2)}) copy-start(bf16[1,256,4,256]{3,2,1,0:T(4,128)(2,1)} %param.10) | copy-start | bytes 1572868
  32.6 5.7 %collective-permute-start.9 = (f32[1,3,64,256]{3,2,1,0:T(8,128)S(1)}, f32[1,3,64,256]{3,2,1,0:T(8,128)S(1)}, u32[]{:S(2)}, u32[]{:S(2)}) collective-permute-start(f32[1,3,64,256]{3,2,1,0:T(8,128)S(1)} %get-tuple-element.127), channel_id=1, source_target_pairs={{0,8},{2,10},{4,12},{6,14},{8,0},{10,2},{12,4},{14,6},{16,24},{18,... | collective-permute-start | bytes 589832 | tf_op jit(solution)/shard_map/ppermute | solution.py:320
  38.4 4.3 %copy-start.11 = (f32[4]{0:T(128)S(1)}, f32[4]{0:T(128)}, u32[]{:S(2)}) copy-start(f32[4]{0:T(128)} %param.14) | copy-start | bytes 52
  38.4 4.8 %copy-start.3 = (f32[4,256]{1,0:T(4,128)S(1)}, f32[4,256]{1,0:T(4,128)}, u32[]{:S(2)}) copy-start(f32[4,256]{1,0:T(4,128)} %gain.1) | copy-start | bytes 12292
  38.4 10.4 %collective-permute-start.11 = (f32[1,3,64,256]{3,2,1,0:T(8,128)S(1)}, f32[1,3,64,256]{3,2,1,0:T(8,128)S(1)}, u32[]{:S(2)}, u32[]{:S(2)}) collective-permute-start(f32[1,3,64,256]{3,2,1,0:T(8,128)S(1)} %add.34), channel_id=1, source_target_pairs={{0,16},{2,18},{4,20},{6,22},{8,24},{10,26},{12,28},{14,30},{16,0},... | collective-permute-start | bytes 589832 | tf_op jit(solution)/shard_map/ppermute | solution.py:320
  41.1 7.8 %collective-permute-start.10 = (f32[1,3,64,256]{3,2,1,0:T(8,128)S(1)}, f32[1,3,64,256]{3,2,1,0:T(8,128)S(1)}, u32[]{:S(2)}, u32[]{:S(2)}) collective-permute-start(f32[1,3,64,256]{3,2,1,0:T(8,128)S(1)} %get-tuple-element.129), channel_id=1, source_target_pairs={{0,8},{2,10},{4,12},{6,14},{8,0},{10,2},{12,4},{14,6},{16,24},{18,... | collective-permute-start | bytes 589832 | tf_op jit(solution)/shard_map/ppermute | solution.py:320
  45.2 14.9 %collective-permute-start.6 = (f32[2,256,256]{2,1,0:T(8,128)S(1)}, f32[2,256,256]{2,1,0:T(8,128)S(1)}, u32[]{:S(2)}, u32[]{:S(2)}) collective-permute-start(f32[2,256,256]{2,1,0:T(8,128)S(1)} %get-tuple-element.115), channel_id=1, source_target_pairs={{0,2},{2,0},{4,6},{6,4},{8,10},{10,8},{12,14},{14,12},{16,18},{18,... | collective-permute-start | bytes 1572872 | tf_op jit(solution)/shard_map/ppermute | solution.py:320
  46.6 22.3 %collective-permute-start.7 = (f32[2,256,256]{2,1,0:T(8,128)S(1)}, f32[2,256,256]{2,1,0:T(8,128)S(1)}, u32[]{:S(2)}, u32[]{:S(2)}) collective-permute-start(f32[2,256,256]{2,1,0:T(8,128)S(1)} %get-tuple-element.116), channel_id=1, source_target_pairs={{0,4},{2,6},{4,0},{6,2},{8,12},{10,14},{12,8},{14,10},{16,20},{18,... | collective-permute-start | bytes 1572872 | tf_op jit(solution)/shard_map/ppermute | solution.py:320
  47.4 21.5 %collective-permute-start.8 = (f32[2,256,256]{2,1,0:T(8,128)S(1)}, f32[2,256,256]{2,1,0:T(8,128)S(1)}, u32[]{:S(2)}, u32[]{:S(2)}) collective-permute-start(f32[2,256,256]{2,1,0:T(8,128)S(1)} %get-tuple-element.117), channel_id=1, source_target_pairs={{0,6},{2,4},{4,2},{6,0},{8,14},{10,12},{12,10},{14,8},{16,22},{18,... | collective-permute-start | bytes 1572872 | tf_op jit(solution)/shard_map/ppermute | solution.py:320
  48.9 8.9 %collective-permute-start.13 = (f32[1,3,64,256]{3,2,1,0:T(8,128)S(1)}, f32[1,3,64,256]{3,2,1,0:T(8,128)S(1)}, u32[]{:S(2)}, u32[]{:S(2)}) collective-permute-start(f32[1,3,64,256]{3,2,1,0:T(8,128)S(1)} %add_add_fusion.1.refs_4_), channel_id=1, source_target_pairs={{0,16},{2,18},{4,20},{6,22},{8,24},{10,26},{12,28},{14,30},{16,0},... | collective-permute-start | bytes 589832 | tf_op jit(solution)/shard_map/ppermute | solution.py:320
  49.8 19.1 %collective-permute-start.12 = (f32[1,3,64,256]{3,2,1,0:T(8,128)S(1)}, f32[1,3,64,256]{3,2,1,0:T(8,128)S(1)}, u32[]{:S(2)}, u32[]{:S(2)}) collective-permute-start(f32[1,3,64,256]{3,2,1,0:T(8,128)S(1)} %add_add_fusion.1.refs_4_), channel_id=1, source_target_pairs={{0,8},{2,10},{4,12},{6,14},{8,0},{10,2},{12,4},{14,6},{16,24},{18,... | collective-permute-start | bytes 589832 | tf_op jit(solution)/shard_map/ppermute | solution.py:320
  57.7 11.1 %collective-permute-start.14 = (f32[1,3,64,256]{3,2,1,0:T(8,128)S(1)}, f32[1,3,64,256]{3,2,1,0:T(8,128)S(1)}, u32[]{:S(2)}, u32[]{:S(2)}) collective-permute-start(f32[1,3,64,256]{3,2,1,0:T(8,128)S(1)} %collective-permute-done.13.refs_6_), channel_id=1, source_target_pairs={{0,8},{2,10},{4,12},{6,14},{8,0},{10,2},{12,4},{14,6},{16,24},{18,... | collective-permute-start | bytes 589832 | tf_op jit(solution)/shard_map/ppermute | solution.py:320
  70.7 1.2 collective-permute-start.15
  71.9 4.5 %collective-permute-start.18 = (f32[2,4,256]{2,1,0:T(4,128)S(1)}, f32[2,4,256]{2,1,0:T(4,128)S(1)}, u32[]{:S(2)}, u32[]{:S(2)}) collective-permute-start(f32[2,4,256]{2,1,0:T(4,128)S(1)} %add.36.refs_4_), channel_id=1, source_target_pairs={{0,6},{2,4},{4,2},{6,0},{8,14},{10,12},{12,10},{14,8},{16,22},{18,... | collective-permute-start | bytes 24584 | tf_op jit(solution)/shard_map/ppermute | solution.py:320
  73.0 3.7 %collective-permute-start.17 = (f32[2,4,256]{2,1,0:T(4,128)S(1)}, f32[2,4,256]{2,1,0:T(4,128)S(1)}, u32[]{:S(2)}, u32[]{:S(2)}) collective-permute-start(f32[2,4,256]{2,1,0:T(4,128)S(1)} %add.36.refs_4_), channel_id=1, source_target_pairs={{0,4},{2,6},{4,0},{6,2},{8,12},{10,14},{12,8},{14,10},{16,20},{18,... | collective-permute-start | bytes 24584 | tf_op jit(solution)/shard_map/ppermute | solution.py:320
  73.7 3.7 %collective-permute-start.16 = (f32[2,4,256]{2,1,0:T(4,128)S(1)}, f32[2,4,256]{2,1,0:T(4,128)S(1)}, u32[]{:S(2)}, u32[]{:S(2)}) collective-permute-start(f32[2,4,256]{2,1,0:T(4,128)S(1)} %add.36.refs_4_), channel_id=1, source_target_pairs={{0,2},{2,0},{4,6},{6,4},{8,10},{10,8},{12,14},{14,12},{16,18},{18,... | collective-permute-start | bytes 24584 | tf_op jit(solution)/shard_map/ppermute | solution.py:320
  79.4 5.7 %collective-permute-start.19 = (f32[1,3,64,256]{3,2,1,0:T(8,128)S(1)}, f32[1,3,64,256]{3,2,1,0:T(8,128)S(1)}, u32[]{:S(2)}, u32[]{:S(2)}) collective-permute-start(f32[1,3,64,256]{3,2,1,0:T(8,128)S(1)} %get-tuple-element.149), channel_id=1, source_target_pairs={{0,8},{2,10},{4,12},{6,14},{8,0},{10,2},{12,4},{14,6},{16,24},{18,... | collective-permute-start | bytes 589832 | tf_op jit(solution)/shard_map/ppermute | solution.py:320
  85.2 10.0 %collective-permute-start.21 = (f32[1,3,64,256]{3,2,1,0:T(8,128)S(1)}, f32[1,3,64,256]{3,2,1,0:T(8,128)S(1)}, u32[]{:S(2)}, u32[]{:S(2)}) collective-permute-start(f32[1,3,64,256]{3,2,1,0:T(8,128)S(1)} %add.38), channel_id=1, source_target_pairs={{0,16},{2,18},{4,20},{6,22},{8,24},{10,26},{12,28},{14,30},{16,0},... | collective-permute-start | bytes 589832 | tf_op jit(solution)/shard_map/ppermute | solution.py:320
  85.6 9.6 %collective-permute-start.20 = (f32[1,3,64,256]{3,2,1,0:T(8,128)S(1)}, f32[1,3,64,256]{3,2,1,0:T(8,128)S(1)}, u32[]{:S(2)}, u32[]{:S(2)}) collective-permute-start(f32[1,3,64,256]{3,2,1,0:T(8,128)S(1)} %get-tuple-element.151), channel_id=1, source_target_pairs={{0,8},{2,10},{4,12},{6,14},{8,0},{10,2},{12,4},{14,6},{16,24},{18,... | collective-permute-start | bytes 589832 | tf_op jit(solution)/shard_map/ppermute | solution.py:320
  95.3 8.1 %collective-permute-start.23 = (f32[1,3,64,256]{3,2,1,0:T(8,128)S(1)}, f32[1,3,64,256]{3,2,1,0:T(8,128)S(1)}, u32[]{:S(2)}, u32[]{:S(2)}) collective-permute-start(f32[1,3,64,256]{3,2,1,0:T(8,128)S(1)} %add_add_fusion.refs_11_.refs_0_), channel_id=1, source_target_pairs={{0,16},{2,18},{4,20},{6,22},{8,24},{10,26},{12,28},{14,30},{16,0},... | collective-permute-start | bytes 589832 | tf_op jit(solution)/shard_map/ppermute | solution.py:320
  96.1 8.5 %collective-permute-start.25 = (f32[256,256]{1,0:T(8,128)S(1)}, f32[256,256]{1,0:T(8,128)S(1)}, u32[]{:S(2)}, u32[]{:S(2)}) collective-permute-start(f32[256,256]{1,0:T(8,128)S(1)} %get-tuple-element.155), channel_id=1, source_target_pairs={{0,2},{2,0},{4,6},{6,4},{8,10},{10,8},{12,14},{14,12},{16,18},{18,... | collective-permute-start | bytes 786440 | tf_op jit(solution)/shard_map/ppermute | solution.py:320
  97.6 10.9 %collective-permute-start.26 = (f32[256,256]{1,0:T(8,128)S(1)}, f32[256,256]{1,0:T(8,128)S(1)}, u32[]{:S(2)}, u32[]{:S(2)}) collective-permute-start(f32[256,256]{1,0:T(8,128)S(1)} %get-tuple-element.156), channel_id=1, source_target_pairs={{0,4},{2,6},{4,0},{6,2},{8,12},{10,14},{12,8},{14,10},{16,20},{18,... | collective-permute-start | bytes 786440 | tf_op jit(solution)/shard_map/ppermute | solution.py:320
  98.0 10.5 %collective-permute-start.27 = (f32[256,256]{1,0:T(8,128)S(1)}, f32[256,256]{1,0:T(8,128)S(1)}, u32[]{:S(2)}, u32[]{:S(2)}) collective-permute-start(f32[256,256]{1,0:T(8,128)S(1)} %get-tuple-element.157), channel_id=1, source_target_pairs={{0,6},{2,4},{4,2},{6,0},{8,14},{10,12},{12,10},{14,8},{16,22},{18,... | collective-permute-start | bytes 786440 | tf_op jit(solution)/shard_map/ppermute | solution.py:320
  99.6 10.7 %collective-permute-start.22 = (f32[1,3,64,256]{3,2,1,0:T(8,128)S(1)}, f32[1,3,64,256]{3,2,1,0:T(8,128)S(1)}, u32[]{:S(2)}, u32[]{:S(2)}) collective-permute-start(f32[1,3,64,256]{3,2,1,0:T(8,128)S(1)} %add_add_fusion.refs_11_.refs_0_), channel_id=1, source_target_pairs={{0,8},{2,10},{4,12},{6,14},{8,0},{10,2},{12,4},{14,6},{16,24},{18,... | collective-permute-start | bytes 589832 | tf_op jit(solution)/shard_map/ppermute | solution.py:320
  103.4 6.8 %collective-permute-start.24 = (f32[1,3,64,256]{3,2,1,0:T(8,128)S(1)}, f32[1,3,64,256]{3,2,1,0:T(8,128)S(1)}, u32[]{:S(2)}, u32[]{:S(2)}) collective-permute-start(f32[1,3,64,256]{3,2,1,0:T(8,128)S(1)} %collective-permute-done.23.refs_13_), channel_id=1, source_target_pairs={{0,8},{2,10},{4,12},{6,14},{8,0},{10,2},{12,4},{14,6},{16,24},{18,... | collective-permute-start | bytes 589832 | tf_op jit(solution)/shard_map/ppermute | solution.py:320
  113.2 29.8 %collective-permute-start.28 = (f32[2,256,256]{2,1,0:T(8,128)S(1)}, f32[2,256,256]{2,1,0:T(8,128)S(1)}, u32[]{:S(2)}, u32[]{:S(2)}) collective-permute-start(f32[2,256,256]{2,1,0:T(8,128)S(1)} %get-tuple-element.184), channel_id=1, source_target_pairs={{0,2},{2,0},{4,6},{6,4},{8,10},{10,8},{12,14},{14,12},{16,18},{18,... | collective-permute-start | bytes 1572872 | tf_op jit(solution)/shard_map/ppermute | solution.py:320
  114.0 29.0 %collective-permute-start.29 = (f32[2,256,256]{2,1,0:T(8,128)S(1)}, f32[2,256,256]{2,1,0:T(8,128)S(1)}, u32[]{:S(2)}, u32[]{:S(2)}) collective-permute-start(f32[2,256,256]{2,1,0:T(8,128)S(1)} %get-tuple-element.185), channel_id=1, source_target_pairs={{0,4},{2,6},{4,0},{6,2},{8,12},{10,14},{12,8},{14,10},{16,20},{18,... | collective-permute-start | bytes 1572872 | tf_op jit(solution)/shard_map/ppermute | solution.py:320
  115.3 27.7 %collective-permute-start.30 = (f32[2,256,256]{2,1,0:T(8,128)S(1)}, f32[2,256,256]{2,1,0:T(8,128)S(1)}, u32[]{:S(2)}, u32[]{:S(2)}) collective-permute-start(f32[2,256,256]{2,1,0:T(8,128)S(1)} %get-tuple-element.186), channel_id=1, source_target_pairs={{0,6},{2,4},{4,2},{6,0},{8,14},{10,12},{12,10},{14,8},{16,22},{18,... | collective-permute-start | bytes 1572872 | tf_op jit(solution)/shard_map/ppermute | solution.py:320
  116.8 7.2 %collective-permute-start.32 = (f32[1,3,64,256]{3,2,1,0:T(8,128)S(1)}, f32[1,3,64,256]{3,2,1,0:T(8,128)S(1)}, u32[]{:S(2)}, u32[]{:S(2)}) collective-permute-start(f32[1,3,64,256]{3,2,1,0:T(8,128)S(1)} %get-tuple-element.190), channel_id=1, source_target_pairs={{0,8},{2,10},{4,12},{6,14},{8,0},{10,2},{12,4},{14,6},{16,24},{18,... | collective-permute-start | bytes 589832 | tf_op jit(solution)/shard_map/ppermute | solution.py:320
  116.8 10.9 %collective-permute-start.31 = (f32[1,3,64,256]{3,2,1,0:T(8,128)S(1)}, f32[1,3,64,256]{3,2,1,0:T(8,128)S(1)}, u32[]{:S(2)}, u32[]{:S(2)}) collective-permute-start(f32[1,3,64,256]{3,2,1,0:T(8,128)S(1)} %get-tuple-element.188), channel_id=1, source_target_pairs={{0,8},{2,10},{4,12},{6,14},{8,0},{10,2},{12,4},{14,6},{16,24},{18,... | collective-permute-start | bytes 589832 | tf_op jit(solution)/shard_map/ppermute | solution.py:320
  124.0 8.7 %collective-permute-start.33 = (f32[1,3,64,256]{3,2,1,0:T(8,128)S(1)}, f32[1,3,64,256]{3,2,1,0:T(8,128)S(1)}, u32[]{:S(2)}, u32[]{:S(2)}) collective-permute-start(f32[1,3,64,256]{3,2,1,0:T(8,128)S(1)} %add.40), channel_id=1, source_target_pairs={{0,16},{2,18},{4,20},{6,22},{8,24},{10,26},{12,28},{14,30},{16,0},... | collective-permute-start | bytes 589832 | tf_op jit(solution)/shard_map/ppermute | solution.py:320
  133.3 4.7 %collective-permute-start.34 = (f32[1,3,16,256]{3,2,1,0:T(8,128)S(1)}, f32[1,3,16,256]{3,2,1,0:T(8,128)S(1)}, u32[]{:S(2)}, u32[]{:S(2)}) collective-permute-start(f32[1,3,16,256]{3,2,1,0:T(8,128)S(1)} %get-tuple-element.192), channel_id=1, source_target_pairs={{0,2},{2,0},{4,6},{6,4},{8,10},{10,8},{12,14},{14,12},{16,18},{18,... | collective-permute-start | bytes 147464 | tf_op jit(solution)/shard_map/ppermute | solution.py:320
  134.1 5.4 %collective-permute-start.35 = (f32[1,3,16,256]{3,2,1,0:T(8,128)S(1)}, f32[1,3,16,256]{3,2,1,0:T(8,128)S(1)}, u32[]{:S(2)}, u32[]{:S(2)}) collective-permute-start(f32[1,3,16,256]{3,2,1,0:T(8,128)S(1)} %get-tuple-element.193), channel_id=1, source_target_pairs={{0,4},{2,6},{4,0},{6,2},{8,12},{10,14},{12,8},{14,10},{16,20},{18,... | collective-permute-start | bytes 147464 | tf_op jit(solution)/shard_map/ppermute | solution.py:320
  138.0 5.0 %collective-permute-start.36 = (f32[1,3,16,256]{3,2,1,0:T(8,128)S(1)}, f32[1,3,16,256]{3,2,1,0:T(8,128)S(1)}, u32[]{:S(2)}, u32[]{:S(2)}) collective-permute-start(f32[1,3,16,256]{3,2,1,0:T(8,128)S(1)} %get-tuple-element.194), channel_id=1, source_target_pairs={{0,6},{2,4},{4,2},{6,0},{8,14},{10,12},{12,10},{14,8},{16,22},{18,... | collective-permute-start | bytes 147464 | tf_op jit(solution)/shard_map/ppermute | solution.py:320

commit v9 on v8

--- a/solution.py
+++ b/solution.py
@@ -325,24 +325,26 @@
     def forwarded(got):
         return [got[:1]] if got.shape[0] == 1 else [got[i : i + 1] for i in range(got.shape[0])]
 
-    def scatter(outs, count, unit, one_by_one=True):
+    def scatter(outs, count, unit):
         outs = list(outs)
         evens = list(range(2, count, 2))
         via = forwarded(move(outs.pop(0), "ctx", unit)) if evens else []
-        if one_by_one:
-            via, outs[0] = after(via, outs[0])
+        via, outs[0] = after(via, outs[0])
         first = [move(outs[0], "ctx", unit)] if count > 1 else []
         even = [move(p + v, "ctx", r * unit) for p, v, r in zip(outs[1:], via, evens)]
         return [outs[-1]] + first + even
 
-    def gather(part, count, unit):
+    def gather(part, count, unit, beside):
         got = [part] * count
-        for r in [2 * i for i in range(1, count // 2)]:
+        evens = range(2, count, 2)
+        for r in evens:
             got[r] = move(part, "ctx", r * unit)
-            got[r + 1] = move(got[r], "ctx", unit)
         if count > 1:
             got[1] = move(part, "ctx", unit)
-        return got
+        got, beside = after(got, beside)
+        for r in evens:
+            got[r + 1] = move(got[r], "ctx", unit)
+        return got, beside
 
     def after(x, *others):
         return lax.optimization_barrier((x, *others))
@@ -364,7 +366,12 @@
     s_in = in_plane(split(split_scaled_kernel, values[0], rates[0]))
     own = [lax.dynamic_index_in_dim(w, mine, 0, keepdims=False) for w in (w_gate, w_out, w_up)]
     own_scale = lax.dynamic_index_in_dim(head_scale, mine, 0, keepdims=True)[None, :]
-    k_in, s_in, queries, cotangent = after(k_in, s_in, queries, cotangent)
+    *q_out, scale_row = call(
+        functools.partial(split_apply_kernel, groups),
+        [shape(2, tokens, width)] * groups + [shape(8, width)],
+        [scratch], flops // 8, place, queries[0], cotangent[0], gain, own_scale,
+    )
+    k_in, s_in, q_out = after(k_in, s_in, q_out)
 
     def kept(*dims, dtype=F32):
         return shape(*dims, tokens, width, dtype=dtype)
@@ -375,14 +382,10 @@
         place, *k_in, *s_in, *own,
     )
     early, terms = out[:2], out[2:]
-    *q_out, scale_row = call(
-        functools.partial(split_apply_kernel, groups),
-        [shape(2, tokens, width)] * groups + [shape(8, width)],
-        [scratch], flops // 8, place, queries[0], cotangent[0], gain, own_scale,
-    )
     q_in = in_plane(q_out)
     new = functools.reduce(jnp.add, scatter(terms, depth, groups))
-    new = gather(new, depth, groups)
+    new, q_in[:-1] = after(new, q_in[:-1])
+    new, q_in[-1] = gather(new, depth, groups, q_in[-1])
     *passed, stats = call(
         functools.partial(apply_kernel, groups, depth),
         [kept(groups), kept(groups), kept(groups, dtype=BF16), kept(groups)]
@@ -404,10 +407,10 @@
         *early, *own,
     )
     part = functools.reduce(jnp.add, scatter(out[groups:], depth, groups))
-    parts = gather(part, depth, groups)
+    parts, q_back = gather(part, depth, groups, in_plane(out[:groups]))
     (grad_q,) = call(
         functools.partial(join_query_kernel, groups), [joined], [scratch], flops // 16,
-        place, *in_plane(out[:groups]),
+        place, *q_back,
     )
     parts, grad_q, saved = after(parts, grad_q, saved)
     rows = hidden // depth
@@ -417,7 +420,7 @@
         place, *early, *saved, *parts, *own,
     )
     back = in_plane(out[:groups])
-    ends = scatter(out[groups:], depth, groups, one_by_one=False)
+    ends = scatter(out[groups:], depth, groups)
     own_rows = rows // groups
     sent = call(
         functools.partial(rows_kernel, groups),

time: 146 us -> 153 us (1.048)
  waiting for transfers between devices: 75 us -> 83.9 us
  starting transfers between devices: 46.3 us -> 41.9 us
  Pallas kernels: 19.5 us -> 21.1 us
    ppermute x37, waiting for transfers between devices: 75 us -> 83.9 us  [move(): lax.ppermute(x, axis, [(c, c ^ step) for c in range(lax.axis_size(axis))])]
    ppermute x37, starting transfers between devices: 46.3 us -> 41.9 us  [move(): lax.ppermute(x, axis, [(c, c ^ step) for c in range(lax.axis_size(axis))])]
    pallas_call x11, Pallas kernels: 19.5 us -> 21.1 us  [call(): pl.pallas_call(body, out_shape=out_shape, in_specs=[smem if a.dtype == jn...]
  transfers between devices with their start and end apart: 37 -> 37, of which waited for: 22 -> 25; matrix products, arithmetic and copies ran while one was open for 1% -> 1% of each run, Pallas kernels for 5% -> 5%
where the time goes in v9:
time: 153 us
  waiting for transfers between devices  83.9 us (55%)
  starting transfers between devices  41.9 us (27%)
  Pallas kernels  21.1 us (14%)
  local copies, waits for them, and re-layouts  5.04 us (3%)
    ppermute x37, waiting for transfers between devices, move(): lax.ppermute(x, axis, [(c, c ^ step) for c in range(lax.axis_size(axis))])  83.9 us
    ppermute x37, starting transfers between devices, move(): lax.ppermute(x, axis, [(c, c ^ step) for c in range(lax.axis_size(axis))])  41.9 us
    pallas_call x11, Pallas kernels, call(): pl.pallas_call(body, out_shape=out_shape, in_specs=[smem if a.dtype == jn...  21.1 us
    unnamed x24, local copies, waits for them, and re-layouts  3.31 us
  transfers between devices with their start and end apart: 37, of which 25 were waited for; matrix products, arithmetic and copies ran while one was open for 1% of the time, Pallas kernels for 5%

profile of v9, /device:TPU:0, one launch (start us, length us, event | category | flops | bytes accessed | tf_op | source)
XLA Modules:
  0.0 153.0 jit_solution(12316641802411308672)
XLA Ops:
  0.7 1.1 copy-done.5
  1.8 1.7 %shard_map.146 = (f32[256,256]{1,0:T(8,128)S(1)}, f32[256,256]{1,0:T(8,128)S(1)}, f32[256,256]{1,0:T(8,128)}, f32[256,256]{1,0:T(8,128)}) custom-call(s32[2]{0:T(128)S(1)} %pad_add_fusion.place, bf16[256,4,256]{2,1,0:T(4,128)(2,1)S(1)} %bitcast.21), custom_call_target="tpu_custom_call" | custom-call | flops 2147483648 | bytes 1572872 | tf_op jit(solution)/shard_map/pallas_call | solution.py:34
  3.5 0.7 copy-done.7
  4.2 2.9 %collective-permute-start = (f32[256,256]{1,0:T(8,128)S(1)}, f32[256,256]{1,0:T(8,128)S(1)}, u32[]{:S(2)}, u32[]{:S(2)}) collective-permute-start(f32[256,256]{1,0:T(8,128)S(1)} %get-tuple-element.124), channel_id=1, source_target_pairs={{0,2},{2,0},{4,6},{6,4},{8,10},{10,8},{12,14},{14,12},{16,18},{18,... | collective-permute-start | bytes 786440 | tf_op jit(solution)/shard_map/ppermute | solution.py:320
  7.2 1.5 collective-permute-start.1
  8.7 1.9 %shard_map.147 = (f32[256,256]{1,0:T(8,128)S(1)}, f32[256,256]{1,0:T(8,128)}, f32[256,256]{1,0:T(8,128)}, f32[256,256]{1,0:T(8,128)}) custom-call(s32[2]{0:T(128)S(1)} %pad_add_fusion.place, bf16[256,4,256]{2,1,0:T(4,128)(2,1)S(1)} %bitcast.22, f32[4,256]{1,0:T(4,128)S(1)} %bitcast.19), custom_call_target="tpu_custom_call" | custom-call | flops 2147483648 | bytes 1576968 | tf_op jit(solution)/shard_map/pallas_call | solution.py:34
  10.7 0.7 copy-done.9
  11.4 1.9 %collective-permute-start.3 = (f32[256,256]{1,0:T(8,128)}, f32[256,256]{1,0:T(8,128)S(1)}, u32[]{:S(2)}, u32[]{:S(2)}) collective-permute-start(f32[256,256]{1,0:T(8,128)} %get-tuple-element.128), channel_id=1, source_target_pairs={{0,2},{2,0},{4,6},{6,4},{8,10},{10,8},{12,14},{14,12},{16,18},{18,... | collective-permute-start | bytes 786440 | tf_op jit(solution)/shard_map/ppermute | solution.py:320
  13.3 1.5 collective-permute-start.4
  14.8 2.5 %collective-permute-start.5 = (f32[256,256]{1,0:T(8,128)}, f32[256,256]{1,0:T(8,128)}, u32[]{:S(2)}, u32[]{:S(2)}) collective-permute-start(f32[256,256]{1,0:T(8,128)} %get-tuple-element.130), channel_id=1, source_target_pairs={{0,6},{2,4},{4,2},{6,0},{8,14},{10,12},{12,10},{14,8},{16,22},{18,... | collective-permute-start | bytes 786440 | tf_op jit(solution)/shard_map/ppermute | solution.py:320
  17.3 0.7 copy-done.11
  18.0 0.6 dynamic_slice.14
  18.7 1.9 %shard_map.145 = (f32[2,256,256]{2,1,0:T(8,128)S(1)}, f32[2,256,256]{2,1,0:T(8,128)S(1)}, f32[2,256,256]{2,1,0:T(8,128)S(1)}, f32[2,256,256]{2,1,0:T(8,128)S(1)}, f32[8,256]{1,0:T(8,128)S(1)}) custom-call(s32[2]{0:T(128)S(1)} %pad_add_fusion.place, bf16[256,4,256]{2,1,0:T(4,128)(2,1)S(1)} %bitcast.17, bf16[256,4,256]{2,1,0:T(4,128)(2,1)S(1)} %bitcast.18, ...), custom_call_target="tpu_custom_call" | custom-call | flops 16777216 | bytes 3158028 | tf_op jit(solution)/shard_map/pallas_call | solution.py:34
  20.7 1.1 dynamic-slice_bitcast_fusion
  21.8 3.8 %collective-permute-done.3.refs_5_ = f32[256,256]{1,0:T(8,128)S(1)} collective-permute-done((f32[256,256]{1,0:T(8,128)}, f32[256,256]{1,0:T(8,128)S(1)}, u32[]{:S(2)}, u32[]{:S(2)}) %collective-permute-start.3) | collective-permute-done | bytes 262176 | tf_op jit(solution)/shard_map/ppermute | solution.py:320
  25.6 6.4 %collective-permute-done.4.refs_6_ = f32[256,256]{1,0:T(8,128)S(1)} collective-permute-done((f32[256,256]{1,0:T(8,128)}, f32[256,256]{1,0:T(8,128)S(1)}, u32[]{:S(2)}, u32[]{:S(2)}) %collective-permute-start.4) | collective-permute-done | bytes 262176 | tf_op jit(solution)/shard_map/ppermute | solution.py:320
  32.0 2.6 %shard_map.148 = (bf16[4,256,256]{2,1,0:T(8,128)(2,1)S(1)}, bf16[4,256,256]{2,1,0:T(8,128)(2,1)S(1)}, f32[1,3,64,256]{3,2,1,0:T(8,128)S(1)}, f32[1,3,64,256]{3,2...) custom-call(s32[2]{0:T(128)S(1)} %pad_add_fusion.place, f32[256,256]{1,0:T(8,128)S(1)} %copy-done.8, ...), custom_call_target="tpu_custom_call" | custom-call | flops 805306368 | bytes 4718600 | tf_op jit(solution)/shard_map/pallas_call | solution.py:34
  34.6 1.6 %collective-permute-start.6 = (f32[1,3,64,256]{3,2,1,0:T(8,128)S(1)}, f32[1,3,64,256]{3,2,1,0:T(8,128)S(1)}, u32[]{:S(2)}, u32[]{:S(2)}) collective-permute-start(f32[1,3,64,256]{3,2,1,0:T(8,128)S(1)} %get-tuple-element.144), channel_id=1, source_target_pairs={{0,8},{2,10},{4,12},{6,14},{8,0},{10,2},{12,4},{14,6},{16,24},{18,... | collective-permute-start | bytes 589832 | tf_op jit(solution)/shard_map/ppermute | solution.py:320
  36.3 1.2 collective-permute-start.9
  37.4 0.9 collective-permute-start.10
  38.3 2.0 %collective-permute-done.6 = f32[1,3,64,256]{3,2,1,0:T(8,128)S(1)} collective-permute-done((f32[1,3,64,256]{3,2,1,0:T(8,128)S(1)}, f32[1,3,64,256]{3,2,1,0:T(8,128)S(1)}, u32[]{:S(2)}, u32[]{:S(2)}) %collective-permute-start.6) | collective-permute-done | bytes 196640 | tf_op jit(solution)/shard_map/ppermute | solution.py:320
  40.4 2.7 %collective-permute-start.8 = (f32[1,3,64,256]{3,2,1,0:T(8,128)S(1)}, f32[1,3,64,256]{3,2,1,0:T(8,128)S(1)}, u32[]{:S(2)}, u32[]{:S(2)}) collective-permute-start(f32[1,3,64,256]{3,2,1,0:T(8,128)S(1)} %add.34), channel_id=1, source_target_pairs={{0,16},{2,18},{4,20},{6,22},{8,24},{10,26},{12,28},{14,30},{16,0},... | collective-permute-start | bytes 589832 | tf_op jit(solution)/shard_map/ppermute | solution.py:320
  43.0 1.6 %collective-permute-start.7 = (f32[1,3,64,256]{3,2,1,0:T(8,128)S(1)}, f32[1,3,64,256]{3,2,1,0:T(8,128)S(1)}, u32[]{:S(2)}, u32[]{:S(2)}) collective-permute-start(f32[1,3,64,256]{3,2,1,0:T(8,128)S(1)} %get-tuple-element.146), channel_id=1, source_target_pairs={{0,8},{2,10},{4,12},{6,14},{8,0},{10,2},{12,4},{14,6},{16,24},{18,... | collective-permute-start | bytes 589832 | tf_op jit(solution)/shard_map/ppermute | solution.py:320
  44.6 1.5 collective-permute-start.13
  46.1 3.9 %collective-permute-done.8 = f32[1,3,64,256]{3,2,1,0:T(8,128)S(1)} collective-permute-done((f32[1,3,64,256]{3,2,1,0:T(8,128)S(1)}, f32[1,3,64,256]{3,2,1,0:T(8,128)S(1)}, u32[]{:S(2)}, u32[]{:S(2)}) %collective-permute-start.8) | collective-permute-done | bytes 196640 | tf_op jit(solution)/shard_map/ppermute | solution.py:320
  50.3 0.8 collective-permute-done.9.refs_1_
  51.1 9.8 %collective-permute-done.10.refs_2_ = f32[2,256,256]{2,1,0:T(8,128)S(1)} collective-permute-done((f32[2,256,256]{2,1,0:T(8,128)S(1)}, f32[2,256,256]{2,1,0:T(8,128)S(1)}, u32[]{:S(2)}, u32[]{:S(2)}) %collective-permute-start.10) | collective-permute-done | bytes 524320 | tf_op jit(solution)/shard_map/ppermute | solution.py:320
  60.9 2.6 %collective-permute-start.12 = (f32[1,3,64,256]{3,2,1,0:T(8,128)S(1)}, f32[1,3,64,256]{3,2,1,0:T(8,128)S(1)}, u32[]{:S(2)}, u32[]{:S(2)}) collective-permute-start(f32[1,3,64,256]{3,2,1,0:T(8,128)S(1)} %add_add_fusion.1.refs_4_), channel_id=1, source_target_pairs={{0,16},{2,18},{4,20},{6,22},{8,24},{10,26},{12,28},{14,30},{16,0},... | collective-permute-start | bytes 589832 | tf_op jit(solution)/shard_map/ppermute | solution.py:320
  63.9 5.6 %collective-permute-done.12.refs_6_ = f32[1,3,64,256]{3,2,1,0:T(8,128)S(1)} collective-permute-done((f32[1,3,64,256]{3,2,1,0:T(8,128)S(1)}, f32[1,3,64,256]{3,2,1,0:T(8,128)S(1)}, u32[]{:S(2)}, u32[]{:S(2)}) %collective-permute-start.12) | collective-permute-done | bytes 196640 | tf_op jit(solution)/shard_map/ppermute | solution.py:320
  69.6 1.6 %collective-permute-done.11.refs_5_ = f32[1,3,64,256]{3,2,1,0:T(8,128)S(1)} collective-permute-done((f32[1,3,64,256]{3,2,1,0:T(8,128)S(1)}, f32[1,3,64,256]{3,2,1,0:T(8,128)S(1)}, u32[]{:S(2)}, u32[]{:S(2)}) %collective-permute-start.11) | collective-permute-done | bytes 196640 | tf_op jit(solution)/shard_map/ppermute | solution.py:320
  71.3 5.5 %collective-permute-done.14.refs_7_ = f32[1,3,64,256]{3,2,1,0:T(8,128)S(1)} collective-permute-done((f32[1,3,64,256]{3,2,1,0:T(8,128)S(1)}, f32[1,3,64,256]{3,2,1,0:T(8,128)S(1)}, u32[]{:S(2)}, u32[]{:S(2)}) %collective-permute-start.14) | collective-permute-done | bytes 196640 | tf_op jit(solution)/shard_map/ppermute | solution.py:320
  76.8 1.8 %shard_map.149 = (f32[4,256,256]{2,1,0:T(8,128)S(1)}, f32[4,256,256]{2,1,0:T(8,128)S(1)}, bf16[4,256,256]{2,1,0:T(8,128)(2,1)S(1)}, f32[4,256,256]{2,1,0:T(8,128...) custom-call(s32[2]{0:T(128)S(1)} %pad_add_fusion.place, f32[8,256]{1,0:T(8,128)S(1)} %get-tuple-element.122.scale_row, ...), custom_call_target="tpu_custom_call" | custom-call | flops 402653184 | bytes 6963208 | tf_op jit(solution)/shard_map/pallas_call | solution.py:34
  78.7 1.2 collective-permute-done.15
  79.8 2.0 %collective-permute-start.17 = (f32[2,4,256]{2,1,0:T(4,128)S(1)}, f32[2,4,256]{2,1,0:T(4,128)S(1)}, u32[]{:S(2)}, u32[]{:S(2)}) collective-permute-start(f32[2,4,256]{2,1,0:T(4,128)S(1)} %add.36.refs_4_), channel_id=1, source_target_pairs={{0,4},{2,6},{4,0},{6,2},{8,12},{10,14},{12,8},{14,10},{16,20},{18,... | collective-permute-start | bytes 24584 | tf_op jit(solution)/shard_map/ppermute | solution.py:320
  81.9 1.5 collective-permute-start.16
  83.3 1.1 collective-permute-done.18.refs_7_
  84.4 1.1 collective-permute-done.16.refs_5_
  85.5 2.1 %shard_map.150 = (f32[256,256]{1,0:T(8,128)S(1)}, f32[256,256]{1,0:T(8,128)S(1)}, f32[256,256]{1,0:T(8,128)S(1)}, f32[256,256]{1,0:T(8,128)S(1)}, f32[1,3,64,256...) custom-call(s32[2]{0:T(128)S(1)} %pad_add_fusion.place, ...), custom_call_target="tpu_custom_call" | custom-call | flops 805306368 | bytes 8036360 | tf_op jit(solution)/shard_map/pallas_call | solution.py:34
  87.9 5.5 %collective-permute-done.19 = f32[1,3,64,256]{3,2,1,0:T(8,128)S(1)} collective-permute-done((f32[1,3,64,256]{3,2,1,0:T(8,128)S(1)}, f32[1,3,64,256]{3,2,1,0:T(8,128)S(1)}, u32[]{:S(2)}, u32[]{:S(2)}) %collective-permute-start.19) | collective-permute-done | bytes 196640 | tf_op jit(solution)/shard_map/ppermute | solution.py:320
  93.5 1.5 collective-permute-start.20
  95.0 1.5 collective-permute-start.24
  96.4 0.5 collective-permute-start.25
  97.0 1.5 collective-permute-start.26
  98.5 4.3 %collective-permute-done.21 = f32[1,3,64,256]{3,2,1,0:T(8,128)S(1)} collective-permute-done((f32[1,3,64,256]{3,2,1,0:T(8,128)S(1)}, f32[1,3,64,256]{3,2,1,0:T(8,128)S(1)}, u32[]{:S(2)}, u32[]{:S(2)}) %collective-permute-start.21) | collective-permute-done | bytes 196640 | tf_op jit(solution)/shard_map/ppermute | solution.py:320
  102.8 0.7 collective-permute-start.23
  103.5 1.5 collective-permute-start.22
  104.9 1.9 %collective-permute-done.25.refs_2_ = f32[256,256]{1,0:T(8,128)S(1)} collective-permute-done((f32[256,256]{1,0:T(8,128)S(1)}, f32[256,256]{1,0:T(8,128)S(1)}, u32[]{:S(2)}, u32[]{:S(2)}) %collective-permute-start.25) | collective-permute-done | bytes 262176 | tf_op jit(solution)/shard_map/ppermute | solution.py:320
  106.9 5.3 %collective-permute-done.23.refs_13_ = f32[1,3,64,256]{3,2,1,0:T(8,128)S(1)} collective-permute-done((f32[1,3,64,256]{3,2,1,0:T(8,128)S(1)}, f32[1,3,64,256]{3,2,1,0:T(8,128)S(1)}, u32[]{:S(2)}, u32[]{:S(2)}) %collective-permute-start.23) | collective-permute-done | bytes 196640 | tf_op jit(solution)/shard_map/ppermute | solution.py:320
  112.9 1.1 shard_map.152
  114.0 1.7 %shard_map.151 = bf16[256,4,256]{2,1,0:T(4,128)(2,1)} custom-call(s32[2]{0:T(128)S(1)} %pad_add_fusion.place, f32[256,256]{1,0:T(8,128)S(1)} %get-tuple-element.190.refs_0_, f32[256,256]{1,0:T(8,128)S(1)} %collective-permute-done.24.refs_1_, f32[256,256]{1,0:T(8,128)S(1)} %collective-permute-done.25.refs_2_, f32[256,256]{1,0:T(8,128)S(1)} %collective-permute-done.26.refs_3_), custom_call_target="tpu_custom_call" | custom-call | flops 8388608 | bytes 1572872 | tf_op jit(solution)/shard_map/pallas_call | solution.py:34
  115.7 2.6 %collective-permute-done.27.refs_14_ = f32[1,3,64,256]{3,2,1,0:T(8,128)S(1)} collective-permute-done((f32[1,3,64,256]{3,2,1,0:T(8,128)S(1)}, f32[1,3,64,256]{3,2,1,0:T(8,128)S(1)}, u32[]{:S(2)}, u32[]{:S(2)}) %collective-permute-start.27) | collective-permute-done | bytes 196640 | tf_op jit(solution)/shard_map/ppermute | solution.py:320
  118.3 3.2 %shard_map.153 = (f32[2,256,256]{2,1,0:T(8,128)S(1)}, f32[2,256,256]{2,1,0:T(8,128)S(1)}, f32[2,256,256]{2,1,0:T(8,128)S(1)}, f32[2,256,256]{2,1,0:T(8,128)S(1)}...) custom-call(s32[2]{0:T(128)S(1)} %pad_add_fusion.place, ...), custom_call_target="tpu_custom_call" | custom-call | flops 1610612736 | bytes 13369352 | tf_op jit(solution)/shard_map/pallas_call | solution.py:34
  121.4 1.3 collective-permute-start.28
  122.9 2.1 %collective-permute-start.30 = (f32[2,256,256]{2,1,0:T(8,128)S(1)}, f32[2,256,256]{2,1,0:T(8,128)S(1)}, u32[]{:S(2)}, u32[]{:S(2)}) collective-permute-start(f32[2,256,256]{2,1,0:T(8,128)S(1)} %get-tuple-element.222), channel_id=1, source_target_pairs={{0,6},{2,4},{4,2},{6,0},{8,14},{10,12},{12,10},{14,8},{16,22},{18,... | collective-permute-start | bytes 1572872 | tf_op jit(solution)/shard_map/ppermute | solution.py:320
  125.2 7.2 %collective-permute-done.31 = f32[1,3,64,256]{3,2,1,0:T(8,128)S(1)} collective-permute-done((f32[1,3,64,256]{3,2,1,0:T(8,128)S(1)}, f32[1,3,64,256]{3,2,1,0:T(8,128)S(1)}, u32[]{:S(2)}, u32[]{:S(2)}) %collective-permute-start.31) | collective-permute-done | bytes 196640 | tf_op jit(solution)/shard_map/ppermute | solution.py:320
  132.9 1.8 %collective-permute-start.32 = (f32[1,3,64,256]{3,2,1,0:T(8,128)S(1)}, f32[1,3,64,256]{3,2,1,0:T(8,128)S(1)}, u32[]{:S(2)}, u32[]{:S(2)}) collective-permute-start(f32[1,3,64,256]{3,2,1,0:T(8,128)S(1)} %get-tuple-element.226), channel_id=1, source_target_pairs={{0,8},{2,10},{4,12},{6,14},{8,0},{10,2},{12,4},{14,6},{16,24},{18,... | collective-permute-start | bytes 589832 | tf_op jit(solution)/shard_map/ppermute | solution.py:320
  134.6 5.5 %collective-permute-done.33.refs_3_ = f32[1,3,64,256]{3,2,1,0:T(8,128)S(1)} collective-permute-done((f32[1,3,64,256]{3,2,1,0:T(8,128)S(1)}, f32[1,3,64,256]{3,2,1,0:T(8,128)S(1)}, u32[]{:S(2)}, u32[]{:S(2)}) %collective-permute-start.33) | collective-permute-done | bytes 196640 | tf_op jit(solution)/shard_map/ppermute | solution.py:320
  140.1 0.5 collective-permute-done.32.refs_2_
  140.6 0.6 shard_map.154
  141.2 1.3 collective-permute-start.34
  142.6 3.0 %collective-permute-done.34.refs_5_ = f32[1,3,16,256]{3,2,1,0:T(8,128)S(1)} collective-permute-done((f32[1,3,16,256]{3,2,1,0:T(8,128)S(1)}, f32[1,3,16,256]{3,2,1,0:T(8,128)S(1)}, u32[]{:S(2)}, u32[]{:S(2)}) %collective-permute-start.34) | collective-permute-done | bytes 49184 | tf_op jit(solution)/shard_map/ppermute | solution.py:320
  145.9 0.8 collective-permute-done.35.refs_6_
  146.7 3.9 %collective-permute-done.36.refs_7_ = f32[1,3,16,256]{3,2,1,0:T(8,128)S(1)} collective-permute-done((f32[1,3,16,256]{3,2,1,0:T(8,128)S(1)}, f32[1,3,16,256]{3,2,1,0:T(8,128)S(1)}, u32[]{:S(2)}, u32[]{:S(2)}) %collective-permute-start.36) | collective-permute-done | bytes 49184 | tf_op jit(solution)/shard_map/ppermute | solution.py:320
  150.5 2.4 %shard_map.155 = (bf16[256,4,256]{2,1,0:T(4,128)(2,1)}, bf16[256,4,256]{2,1,0:T(4,128)(2,1)}, f32[4,16,256]{2,1,0:T(8,128)}, f32[4,16,256]{2,1,0:T(8,128)}, f32[4,16,256]{2,1,0:T(8,128)}) custom-call(s32[2]{0:T(128)S(1)} %pad_add_fusion.place, f32[4,256]{1,0:T(4,128)S(1)} %bitcast.20, f32[2,256,256]{2,1,0:T(8,128)S(1)} %get-tuple-element.219.refs_0_, ...), custom_call_target="tpu_custom_call" | custom-call | flops 16777216 | bytes 3543048 | tf_op jit(solution)/shard_map/pallas_call | solution.py:34
  (55 shorter events, 3.4 us)
Async XLA Ops:
  0.6 20.0 %copy-start = (f32[4,256,256]{2,1,0:T(8,128)S(1)}, f32[4,256,256]{2,1,0:T(8,128)}, u32[]{:S(2)}) copy-start(f32[4,256,256]{2,1,0:T(8,128)} %param.16) | copy-start | bytes 3145732
  0.7 1.1 copy-start.5
  1.8 6.9 %copy-start.6 = (bf16[1,256,4,256]{3,2,1,0:T(4,128)(2,1)S(1)}, bf16[1,256,4,256]{3,2,1,0:T(4,128)(2,1)}, u32[]{:S(2)}) copy-start(bf16[1,256,4,256]{3,2,1,0:T(4,128)(2,1)} %param.12) | copy-start | bytes 1572868
  3.5 0.7 copy-start.7
  4.2 4.5 %copy-start.4 = (f32[1,4,256]{2,1,0:T(4,128)S(1)}, f32[1,4,256]{2,1,0:T(4,128)}, u32[]{:S(2)}) copy-start(f32[1,4,256]{2,1,0:T(4,128)} %param.13) | copy-start | bytes 12292
  4.2 10.6 %collective-permute-start = (f32[256,256]{1,0:T(8,128)S(1)}, f32[256,256]{1,0:T(8,128)S(1)}, u32[]{:S(2)}, u32[]{:S(2)}) collective-permute-start(f32[256,256]{1,0:T(8,128)S(1)} %get-tuple-element.124), channel_id=1, source_target_pairs={{0,2},{2,0},{4,6},{6,4},{8,10},{10,8},{12,14},{14,12},{16,18},{18,... | collective-permute-start | bytes 786440 | tf_op jit(solution)/shard_map/ppermute | solution.py:320
  7.2 14.6 %collective-permute-start.1 = (f32[256,256]{1,0:T(8,128)}, f32[256,256]{1,0:T(8,128)S(1)}, u32[]{:S(2)}, u32[]{:S(2)}) collective-permute-start(f32[256,256]{1,0:T(8,128)} %get-tuple-element.125), channel_id=1, source_target_pairs={{0,4},{2,6},{4,0},{6,2},{8,12},{10,14},{12,8},{14,10},{16,20},{18,... | collective-permute-start | bytes 786440 | tf_op jit(solution)/shard_map/ppermute | solution.py:320
  8.7 13.1 %collective-permute-start.2 = (f32[256,256]{1,0:T(8,128)}, f32[256,256]{1,0:T(8,128)S(1)}, u32[]{:S(2)}, u32[]{:S(2)}) collective-permute-start(f32[256,256]{1,0:T(8,128)} %get-tuple-element.126), channel_id=1, source_target_pairs={{0,6},{2,4},{4,2},{6,0},{8,14},{10,12},{12,10},{14,8},{16,22},{18,... | collective-permute-start | bytes 786440 | tf_op jit(solution)/shard_map/ppermute | solution.py:320
  8.7 9.9 %copy-start.1 = (bf16[1,256,4,256]{3,2,1,0:T(4,128)(2,1)S(1)}, bf16[1,256,4,256]{3,2,1,0:T(4,128)(2,1)}, u32[]{:S(2)}) copy-start(bf16[1,256,4,256]{3,2,1,0:T(4,128)(2,1)} %param.10) | copy-start | bytes 1572868
  8.7 9.9 %copy-start.2 = (bf16[1,256,4,256]{3,2,1,0:T(4,128)(2,1)S(1)}, bf16[1,256,4,256]{3,2,1,0:T(4,128)(2,1)}, u32[]{:S(2)}) copy-start(bf16[1,256,4,256]{3,2,1,0:T(4,128)(2,1)} %param.19) | copy-start | bytes 1572868
  10.7 0.7 copy-start.9
  11.4 14.2 %collective-permute-start.3 = (f32[256,256]{1,0:T(8,128)}, f32[256,256]{1,0:T(8,128)S(1)}, u32[]{:S(2)}, u32[]{:S(2)}) collective-permute-start(f32[256,256]{1,0:T(8,128)} %get-tuple-element.128), channel_id=1, source_target_pairs={{0,2},{2,0},{4,6},{6,4},{8,10},{10,8},{12,14},{14,12},{16,18},{18,... | collective-permute-start | bytes 786440 | tf_op jit(solution)/shard_map/ppermute | solution.py:320
  13.3 18.7 %collective-permute-start.4 = (f32[256,256]{1,0:T(8,128)}, f32[256,256]{1,0:T(8,128)S(1)}, u32[]{:S(2)}, u32[]{:S(2)}) collective-permute-start(f32[256,256]{1,0:T(8,128)} %get-tuple-element.129), channel_id=1, source_target_pairs={{0,4},{2,6},{4,0},{6,2},{8,12},{10,14},{12,8},{14,10},{16,20},{18,... | collective-permute-start | bytes 786440 | tf_op jit(solution)/shard_map/ppermute | solution.py:320
  14.8 17.2 %collective-permute-start.5 = (f32[256,256]{1,0:T(8,128)}, f32[256,256]{1,0:T(8,128)}, u32[]{:S(2)}, u32[]{:S(2)}) collective-permute-start(f32[256,256]{1,0:T(8,128)} %get-tuple-element.130), channel_id=1, source_target_pairs={{0,6},{2,4},{4,2},{6,0},{8,14},{10,12},{12,10},{14,8},{16,22},{18,... | collective-permute-start | bytes 786440 | tf_op jit(solution)/shard_map/ppermute | solution.py:320
  17.3 0.7 copy-start.11
  18.0 0.7 copy-start.3
  20.7 11.3 %copy-start.8 = (f32[256,256]{1,0:T(8,128)S(1)}, f32[256,256]{1,0:T(8,128)}, u32[]{:S(2)}) copy-start(f32[256,256]{1,0:T(8,128)} %copy-done.7) | copy-start | bytes 786436
  20.7 11.3 %copy-start.10 = (f32[256,256]{1,0:T(8,128)S(1)}, f32[256,256]{1,0:T(8,128)}, u32[]{:S(2)}) copy-start(f32[256,256]{1,0:T(8,128)} %copy-done.9) | copy-start | bytes 786436
  34.6 5.7 %collective-permute-start.6 = (f32[1,3,64,256]{3,2,1,0:T(8,128)S(1)}, f32[1,3,64,256]{3,2,1,0:T(8,128)S(1)}, u32[]{:S(2)}, u32[]{:S(2)}) collective-permute-start(f32[1,3,64,256]{3,2,1,0:T(8,128)S(1)} %get-tuple-element.144), channel_id=1, source_target_pairs={{0,8},{2,10},{4,12},{6,14},{8,0},{10,2},{12,4},{14,6},{16,24},{18,... | collective-permute-start | bytes 589832 | tf_op jit(solution)/shard_map/ppermute | solution.py:320
  36.3 14.9 %collective-permute-start.9 = (f32[2,256,256]{2,1,0:T(8,128)S(1)}, f32[2,256,256]{2,1,0:T(8,128)S(1)}, u32[]{:S(2)}, u32[]{:S(2)}) collective-permute-start(f32[2,256,256]{2,1,0:T(8,128)S(1)} %get-tuple-element.150), channel_id=1, source_target_pairs={{0,2},{2,0},{4,6},{6,4},{8,10},{10,8},{12,14},{14,12},{16,18},{18,... | collective-permute-start | bytes 1572872 | tf_op jit(solution)/shard_map/ppermute | solution.py:320
  37.4 23.5 %collective-permute-start.10 = (f32[2,256,256]{2,1,0:T(8,128)S(1)}, f32[2,256,256]{2,1,0:T(8,128)S(1)}, u32[]{:S(2)}, u32[]{:S(2)}) collective-permute-start(f32[2,256,256]{2,1,0:T(8,128)S(1)} %get-tuple-element.151), channel_id=1, source_target_pairs={{0,4},{2,6},{4,0},{6,2},{8,12},{10,14},{12,8},{14,10},{16,20},{18,... | collective-permute-start | bytes 1572872 | tf_op jit(solution)/shard_map/ppermute | solution.py:320
  40.4 9.7 %collective-permute-start.8 = (f32[1,3,64,256]{3,2,1,0:T(8,128)S(1)}, f32[1,3,64,256]{3,2,1,0:T(8,128)S(1)}, u32[]{:S(2)}, u32[]{:S(2)}) collective-permute-start(f32[1,3,64,256]{3,2,1,0:T(8,128)S(1)} %add.34), channel_id=1, source_target_pairs={{0,16},{2,18},{4,20},{6,22},{8,24},{10,26},{12,28},{14,30},{16,0},... | collective-permute-start | bytes 589832 | tf_op jit(solution)/shard_map/ppermute | solution.py:320
  43.0 7.2 %collective-permute-start.7 = (f32[1,3,64,256]{3,2,1,0:T(8,128)S(1)}, f32[1,3,64,256]{3,2,1,0:T(8,128)S(1)}, u32[]{:S(2)}, u32[]{:S(2)}) collective-permute-start(f32[1,3,64,256]{3,2,1,0:T(8,128)S(1)} %get-tuple-element.146), channel_id=1, source_target_pairs={{0,8},{2,10},{4,12},{6,14},{8,0},{10,2},{12,4},{14,6},{16,24},{18,... | collective-permute-start | bytes 589832 | tf_op jit(solution)/shard_map/ppermute | solution.py:320
  44.6 19.3 %collective-permute-start.13 = (f32[2,256,256]{2,1,0:T(8,128)S(1)}, f32[2,256,256]{2,1,0:T(8,128)S(1)}, u32[]{:S(2)}, u32[]{:S(2)}) collective-permute-start(f32[2,256,256]{2,1,0:T(8,128)S(1)} %get-tuple-element.156), channel_id=1, source_target_pairs={{0,6},{2,4},{4,2},{6,0},{8,14},{10,12},{12,10},{14,8},{16,22},{18,... | collective-permute-start | bytes 1572872 | tf_op jit(solution)/shard_map/ppermute | solution.py:320
  60.9 8.7 %collective-permute-start.12 = (f32[1,3,64,256]{3,2,1,0:T(8,128)S(1)}, f32[1,3,64,256]{3,2,1,0:T(8,128)S(1)}, u32[]{:S(2)}, u32[]{:S(2)}) collective-permute-start(f32[1,3,64,256]{3,2,1,0:T(8,128)S(1)} %add_add_fusion.1.refs_4_), channel_id=1, source_target_pairs={{0,16},{2,18},{4,20},{6,22},{8,24},{10,26},{12,28},{14,30},{16,0},... | collective-permute-start | bytes 589832 | tf_op jit(solution)/shard_map/ppermute | solution.py:320
  63.5 7.7 %collective-permute-start.11 = (f32[1,3,64,256]{3,2,1,0:T(8,128)S(1)}, f32[1,3,64,256]{3,2,1,0:T(8,128)S(1)}, u32[]{:S(2)}, u32[]{:S(2)}) collective-permute-start(f32[1,3,64,256]{3,2,1,0:T(8,128)S(1)} %add_add_fusion.1.refs_4_), channel_id=1, source_target_pairs={{0,8},{2,10},{4,12},{6,14},{8,0},{10,2},{12,4},{14,6},{16,24},{18,... | collective-permute-start | bytes 589832 | tf_op jit(solution)/shard_map/ppermute | solution.py:320
  71.2 5.7 %collective-permute-start.14 = (f32[1,3,64,256]{3,2,1,0:T(8,128)S(1)}, f32[1,3,64,256]{3,2,1,0:T(8,128)S(1)}, u32[]{:S(2)}, u32[]{:S(2)}) collective-permute-start(f32[1,3,64,256]{3,2,1,0:T(8,128)S(1)} %collective-permute-done.12.refs_6_), channel_id=1, source_target_pairs={{0,8},{2,10},{4,12},{6,14},{8,0},{10,2},{12,4},{14,6},{16,24},{18,... | collective-permute-start | bytes 589832 | tf_op jit(solution)/shard_map/ppermute | solution.py:320
  78.6 1.2 collective-permute-start.15
  79.8 4.5 %collective-permute-start.18 = (f32[2,4,256]{2,1,0:T(4,128)S(1)}, f32[2,4,256]{2,1,0:T(4,128)S(1)}, u32[]{:S(2)}, u32[]{:S(2)}) collective-permute-start(f32[2,4,256]{2,1,0:T(4,128)S(1)} %add.36.refs_4_), channel_id=1, source_target_pairs={{0,6},{2,4},{4,2},{6,0},{8,14},{10,12},{12,10},{14,8},{16,22},{18,... | collective-permute-start | bytes 24584 | tf_op jit(solution)/shard_map/ppermute | solution.py:320
  79.8 4.5 %collective-permute-start.17 = (f32[2,4,256]{2,1,0:T(4,128)S(1)}, f32[2,4,256]{2,1,0:T(4,128)S(1)}, u32[]{:S(2)}, u32[]{:S(2)}) collective-permute-start(f32[2,4,256]{2,1,0:T(4,128)S(1)} %add.36.refs_4_), channel_id=1, source_target_pairs={{0,4},{2,6},{4,0},{6,2},{8,12},{10,14},{12,8},{14,10},{16,20},{18,... | collective-permute-start | bytes 24584 | tf_op jit(solution)/shard_map/ppermute | solution.py:320
  81.9 3.7 %collective-permute-start.16 = (f32[2,4,256]{2,1,0:T(4,128)S(1)}, f32[2,4,256]{2,1,0:T(4,128)S(1)}, u32[]{:S(2)}, u32[]{:S(2)}) collective-permute-start(f32[2,4,256]{2,1,0:T(4,128)S(1)} %add.36.refs_4_), channel_id=1, source_target_pairs={{0,2},{2,0},{4,6},{6,4},{8,10},{10,8},{12,14},{14,12},{16,18},{18,... | collective-permute-start | bytes 24584 | tf_op jit(solution)/shard_map/ppermute | solution.py:320
  87.6 5.7 %collective-permute-start.19 = (f32[1,3,64,256]{3,2,1,0:T(8,128)S(1)}, f32[1,3,64,256]{3,2,1,0:T(8,128)S(1)}, u32[]{:S(2)}, u32[]{:S(2)}) collective-permute-start(f32[1,3,64,256]{3,2,1,0:T(8,128)S(1)} %get-tuple-element.178), channel_id=1, source_target_pairs={{0,8},{2,10},{4,12},{6,14},{8,0},{10,2},{12,4},{14,6},{16,24},{18,... | collective-permute-start | bytes 589832 | tf_op jit(solution)/shard_map/ppermute | solution.py:320
  93.4 9.3 %collective-permute-start.21 = (f32[1,3,64,256]{3,2,1,0:T(8,128)S(1)}, f32[1,3,64,256]{3,2,1,0:T(8,128)S(1)}, u32[]{:S(2)}, u32[]{:S(2)}) collective-permute-start(f32[1,3,64,256]{3,2,1,0:T(8,128)S(1)} %add.38), channel_id=1, source_target_pairs={{0,16},{2,18},{4,20},{6,22},{8,24},{10,26},{12,28},{14,30},{16,0},... | collective-permute-start | bytes 589832 | tf_op jit(solution)/shard_map/ppermute | solution.py:320
  93.5 9.2 %collective-permute-start.20 = (f32[1,3,64,256]{3,2,1,0:T(8,128)S(1)}, f32[1,3,64,256]{3,2,1,0:T(8,128)S(1)}, u32[]{:S(2)}, u32[]{:S(2)}) collective-permute-start(f32[1,3,64,256]{3,2,1,0:T(8,128)S(1)} %get-tuple-element.180), channel_id=1, source_target_pairs={{0,8},{2,10},{4,12},{6,14},{8,0},{10,2},{12,4},{14,6},{16,24},{18,... | collective-permute-start | bytes 589832 | tf_op jit(solution)/shard_map/ppermute | solution.py:320
  95.0 10.0 %collective-permute-start.24 = (f32[256,256]{1,0:T(8,128)S(1)}, f32[256,256]{1,0:T(8,128)S(1)}, u32[]{:S(2)}, u32[]{:S(2)}) collective-permute-start(f32[256,256]{1,0:T(8,128)S(1)} %get-tuple-element.184), channel_id=1, source_target_pairs={{0,2},{2,0},{4,6},{6,4},{8,10},{10,8},{12,14},{14,12},{16,18},{18,... | collective-permute-start | bytes 786440 | tf_op jit(solution)/shard_map/ppermute | solution.py:320
  96.4 10.5 %collective-permute-start.25 = (f32[256,256]{1,0:T(8,128)S(1)}, f32[256,256]{1,0:T(8,128)S(1)}, u32[]{:S(2)}, u32[]{:S(2)}) collective-permute-start(f32[256,256]{1,0:T(8,128)S(1)} %get-tuple-element.185), channel_id=1, source_target_pairs={{0,4},{2,6},{4,0},{6,2},{8,12},{10,14},{12,8},{14,10},{16,20},{18,... | collective-permute-start | bytes 786440 | tf_op jit(solution)/shard_map/ppermute | solution.py:320
  97.0 9.9 %collective-permute-start.26 = (f32[256,256]{1,0:T(8,128)S(1)}, f32[256,256]{1,0:T(8,128)S(1)}, u32[]{:S(2)}, u32[]{:S(2)}) collective-permute-start(f32[256,256]{1,0:T(8,128)S(1)} %get-tuple-element.186), channel_id=1, source_target_pairs={{0,6},{2,4},{4,2},{6,0},{8,14},{10,12},{12,10},{14,8},{16,22},{18,... | collective-permute-start | bytes 786440 | tf_op jit(solution)/shard_map/ppermute | solution.py:320
  102.8 9.4 %collective-permute-start.23 = (f32[1,3,64,256]{3,2,1,0:T(8,128)S(1)}, f32[1,3,64,256]{3,2,1,0:T(8,128)S(1)}, u32[]{:S(2)}, u32[]{:S(2)}) collective-permute-start(f32[1,3,64,256]{3,2,1,0:T(8,128)S(1)} %add_add_fusion.refs_11_.refs_0_), channel_id=1, source_target_pairs={{0,16},{2,18},{4,20},{6,22},{8,24},{10,26},{12,28},{14,30},{16,0},... | collective-permute-start | bytes 589832 | tf_op jit(solution)/shard_map/ppermute | solution.py:320
  103.5 9.1 %collective-permute-start.22 = (f32[1,3,64,256]{3,2,1,0:T(8,128)S(1)}, f32[1,3,64,256]{3,2,1,0:T(8,128)S(1)}, u32[]{:S(2)}, u32[]{:S(2)}) collective-permute-start(f32[1,3,64,256]{3,2,1,0:T(8,128)S(1)} %add_add_fusion.refs_11_.refs_0_), channel_id=1, source_target_pairs={{0,8},{2,10},{4,12},{6,14},{8,0},{10,2},{12,4},{14,6},{16,24},{18,... | collective-permute-start | bytes 589832 | tf_op jit(solution)/shard_map/ppermute | solution.py:320
  112.6 5.7 %collective-permute-start.27 = (f32[1,3,64,256]{3,2,1,0:T(8,128)S(1)}, f32[1,3,64,256]{3,2,1,0:T(8,128)S(1)}, u32[]{:S(2)}, u32[]{:S(2)}) collective-permute-start(f32[1,3,64,256]{3,2,1,0:T(8,128)S(1)} %collective-permute-done.23.refs_13_), channel_id=1, source_target_pairs={{0,8},{2,10},{4,12},{6,14},{8,0},{10,2},{12,4},{14,6},{16,24},{18,... | collective-permute-start | bytes 589832 | tf_op jit(solution)/shard_map/ppermute | solution.py:320
  121.4 29.1 %collective-permute-start.28 = (f32[2,256,256]{2,1,0:T(8,128)S(1)}, f32[2,256,256]{2,1,0:T(8,128)S(1)}, u32[]{:S(2)}, u32[]{:S(2)}) collective-permute-start(f32[2,256,256]{2,1,0:T(8,128)S(1)} %get-tuple-element.220), channel_id=1, source_target_pairs={{0,2},{2,0},{4,6},{6,4},{8,10},{10,8},{12,14},{14,12},{16,18},{18,... | collective-permute-start | bytes 1572872 | tf_op jit(solution)/shard_map/ppermute | solution.py:320
  122.7 27.8 %collective-permute-start.29 = (f32[2,256,256]{2,1,0:T(8,128)S(1)}, f32[2,256,256]{2,1,0:T(8,128)S(1)}, u32[]{:S(2)}, u32[]{:S(2)}) collective-permute-start(f32[2,256,256]{2,1,0:T(8,128)S(1)} %get-tuple-element.221), channel_id=1, source_target_pairs={{0,4},{2,6},{4,0},{6,2},{8,12},{10,14},{12,8},{14,10},{16,20},{18,... | collective-permute-start | bytes 1572872 | tf_op jit(solution)/shard_map/ppermute | solution.py:320
  122.9 27.6 %collective-permute-start.30 = (f32[2,256,256]{2,1,0:T(8,128)S(1)}, f32[2,256,256]{2,1,0:T(8,128)S(1)}, u32[]{:S(2)}, u32[]{:S(2)}) collective-permute-start(f32[2,256,256]{2,1,0:T(8,128)S(1)} %get-tuple-element.222), channel_id=1, source_target_pairs={{0,6},{2,4},{4,2},{6,0},{8,14},{10,12},{12,10},{14,8},{16,22},{18,... | collective-permute-start | bytes 1572872 | tf_op jit(solution)/shard_map/ppermute | solution.py:320
  125.0 7.5 %collective-permute-start.31 = (f32[1,3,64,256]{3,2,1,0:T(8,128)S(1)}, f32[1,3,64,256]{3,2,1,0:T(8,128)S(1)}, u32[]{:S(2)}, u32[]{:S(2)}) collective-permute-start(f32[1,3,64,256]{3,2,1,0:T(8,128)S(1)} %get-tuple-element.224), channel_id=1, source_target_pairs={{0,8},{2,10},{4,12},{6,14},{8,0},{10,2},{12,4},{14,6},{16,24},{18,... | collective-permute-start | bytes 589832 | tf_op jit(solution)/shard_map/ppermute | solution.py:320
  132.5 7.7 %collective-permute-start.33 = (f32[1,3,64,256]{3,2,1,0:T(8,128)S(1)}, f32[1,3,64,256]{3,2,1,0:T(8,128)S(1)}, u32[]{:S(2)}, u32[]{:S(2)}) collective-permute-start(f32[1,3,64,256]{3,2,1,0:T(8,128)S(1)} %add.40), channel_id=1, source_target_pairs={{0,16},{2,18},{4,20},{6,22},{8,24},{10,26},{12,28},{14,30},{16,0},... | collective-permute-start | bytes 589832 | tf_op jit(solution)/shard_map/ppermute | solution.py:320
  132.9 7.8 %collective-permute-start.32 = (f32[1,3,64,256]{3,2,1,0:T(8,128)S(1)}, f32[1,3,64,256]{3,2,1,0:T(8,128)S(1)}, u32[]{:S(2)}, u32[]{:S(2)}) collective-permute-start(f32[1,3,64,256]{3,2,1,0:T(8,128)S(1)} %get-tuple-element.226), channel_id=1, source_target_pairs={{0,8},{2,10},{4,12},{6,14},{8,0},{10,2},{12,4},{14,6},{16,24},{18,... | collective-permute-start | bytes 589832 | tf_op jit(solution)/shard_map/ppermute | solution.py:320
  141.2 4.3 %collective-permute-start.34 = (f32[1,3,16,256]{3,2,1,0:T(8,128)S(1)}, f32[1,3,16,256]{3,2,1,0:T(8,128)S(1)}, u32[]{:S(2)}, u32[]{:S(2)}) collective-permute-start(f32[1,3,16,256]{3,2,1,0:T(8,128)S(1)} %get-tuple-element.230), channel_id=1, source_target_pairs={{0,2},{2,0},{4,6},{6,4},{8,10},{10,8},{12,14},{14,12},{16,18},{18,... | collective-permute-start | bytes 147464 | tf_op jit(solution)/shard_map/ppermute | solution.py:320
  142.6 4.1 %collective-permute-start.35 = (f32[1,3,16,256]{3,2,1,0:T(8,128)S(1)}, f32[1,3,16,256]{3,2,1,0:T(8,128)S(1)}, u32[]{:S(2)}, u32[]{:S(2)}) collective-permute-start(f32[1,3,16,256]{3,2,1,0:T(8,128)S(1)} %get-tuple-element.231), channel_id=1, source_target_pairs={{0,4},{2,6},{4,0},{6,2},{8,12},{10,14},{12,8},{14,10},{16,20},{18,... | collective-permute-start | bytes 147464 | tf_op jit(solution)/shard_map/ppermute | solution.py:320
  145.5 5.0 %collective-permute-start.36 = (f32[1,3,16,256]{3,2,1,0:T(8,128)S(1)}, f32[1,3,16,256]{3,2,1,0:T(8,128)S(1)}, u32[]{:S(2)}, u32[]{:S(2)}) collective-permute-start(f32[1,3,16,256]{3,2,1,0:T(8,128)S(1)} %get-tuple-element.232), channel_id=1, source_target_pairs={{0,6},{2,4},{4,2},{6,0},{8,14},{10,12},{12,10},{14,8},{16,22},{18,... | collective-permute-start | bytes 147464 | tf_op jit(solution)/shard_map/ppermute | solution.py:320

commit v10 on v9

--- a/solution.py
+++ b/solution.py
@@ -26,14 +26,14 @@
     return lax.dot_general(a, b, (((0,), (0,)), ((), ())), preferred_element_type=F32)
 
 
-def call(body, out_shape, scratch, flops, *args):
+def call(body, out_shape, scratch, flops, *args, final=False):
     smem = pl.BlockSpec(memory_space=pltpu.SMEM)
     vmem = pl.BlockSpec(memory_space=pltpu.VMEM)
     size = sum(a.size * a.dtype.itemsize for a in args)
     size += sum(math.prod(o.shape) * o.dtype.itemsize for o in out_shape)
     return pl.pallas_call(
         body,
-        out_shape=out_shape,
+        out_shape=out_shape if final else [pltpu.VMEM(o.shape, o.dtype) for o in out_shape],
         in_specs=[smem if a.dtype == jnp.int32 else vmem for a in args],
         out_specs=[vmem] * len(out_shape),
         scratch_shapes=scratch,
@@ -77,13 +77,34 @@
         outs[step][...] = scaled.astype(BF16).astype(F32)
 
 
+def packing(groups):
+    if groups == 4:
+        return [[(0, 0), (0, 1)], [(1, 0), (1, 1), (3, 0)], [(2, 0), (2, 1), (3, 1)]]
+    return [[(step, 0), (step, 1)] for step in range(groups)]
+
+
+def unpacked(groups, refs):
+    found = {}
+    for ref, members in zip(refs, packing(groups)):
+        for i, member in enumerate(members):
+            found[member] = ref.at[i]
+    for i, ref in enumerate(refs[len(packing(groups)) :]):
+        found[(groups - 1, i)] = ref
+    return [found[(step, 0)] for step in range(groups)], [found[(step, 1)] for step in range(groups)]
+
+
 def split_apply_kernel(groups, place, q, cot, gain, scale, *rest):
-    outs, scale_row, scratch = rest[:groups], rest[groups], rest[groups + 1]
+    outs, scale_row, scratch = rest[:-2], rest[-2], rest[-1]
     scale_row[...] = jnp.broadcast_to(scale[...], scale_row.shape)
-    split_kernel(groups, place, q, *[out.at[0] for out in outs], scratch)
-    split_kernel(groups, place, cot, *[out.at[1] for out in outs], scratch)
-    for step in range(groups):
-        outs[step][1] *= gain[pl.ds(place[0] ^ step, 1), :]
+    to_q, to_dyg = unpacked(groups, outs)
+    split_kernel(groups, place, q, *to_q, scratch)
+    split_kernel(groups, place, cot, *to_dyg, scratch)
+    for step in range(groups):
+        to_dyg[step][...] *= gain[pl.ds(place[0] ^ step, 1), :]
+
+
+def packed_count(groups):
+    return len(packing(groups)) + 2 * (groups == 4)
 
 
 def rate_column(r, head):
@@ -148,13 +169,13 @@
 
 
 def apply_kernel(groups, depth, place, scale_row, *refs):
-    pieces = refs[:groups]
-    parts = refs[groups : groups + depth]
-    activ_ref, slope_ref, hidden_ref, os_ref, new_b, stats, whole = refs[groups + depth :]
+    count = packed_count(groups)
+    (q_in, dyg_in), parts = unpacked(groups, refs[:count]), refs[count : count + depth]
+    activ_ref, slope_ref, hidden_ref, os_ref, new_b, stats, whole = refs[count + depth :]
     assemble(place, parts, whole)
     new_b[...] = whole[...].astype(BF16)
     for step in range(groups):
-        queries = pieces[step][0].astype(BF16)
+        queries = q_in[step][...].astype(BF16)
         tokens = queries.shape[0]
         first = mm(queries, new_b[0])
         third = mm(queries, new_b[2])
@@ -167,7 +188,7 @@
         hidden_ref[step] = hidden
         os_ref[step] = scaled
         sq = jnp.sum(scaled * scaled, axis=1, keepdims=True)
-        ps = jnp.sum(scaled * pieces[step][1], axis=1, keepdims=True)
+        ps = jnp.sum(scaled * dyg_in[step][...], axis=1, keepdims=True)
         lane = lax.broadcasted_iota(jnp.int32, (tokens, LANES), 1)
         both = jnp.where(lane == 0, sq, jnp.where(lane == 1, ps, 0.0)).T
         source = place[0] ^ step
@@ -176,22 +197,24 @@
 
 
 def apply_back_kernel(groups, depth, count, place, scale_row, *refs):
-    pieces, stats = refs[:groups], refs[groups : 2 * groups]
-    activ_ref, slope_ref, hidden_ref, os_ref, new_b = refs[2 * groups : 2 * groups + 5]
-    outs = refs[2 * groups + 5 : 3 * groups + 5]
-    slices, sums, both = refs[3 * groups + 5 : -2], refs[-2], refs[-1]
+    packed = packed_count(groups)
+    q_in, dyg_in = unpacked(groups, refs[:packed])
+    refs = refs[packed:]
+    stats, refs = refs[:groups], refs[groups:]
+    activ_ref, slope_ref, hidden_ref, os_ref, new_b = refs[:5]
+    outs, slices, sums, both = refs[5 : groups + 5], refs[groups + 5 : -2], refs[-2], refs[-1]
     total_stats = stats[0][...]
     for other in stats[1:]:
         total_stats += other[...]
     both[...] = total_stats
     total = [0.0, 0.0, 0.0]
     for step in range(groups):
-        queries = pieces[step][0].astype(BF16)
+        queries = q_in[step][...].astype(BF16)
         source = place[0] ^ step
         sq = rate_column(both.at[0], source)
         ps = rate_column(both.at[1], source)
         inv = lax.rsqrt(sq / count + 1e-06)
-        dos = inv * pieces[step][1] - os_ref[step] * (inv * inv * inv * ps / count)
+        dos = inv * dyg_in[step][...] - os_ref[step] * (inv * inv * inv * ps / count)
         dout = (dos * scale_row[0:1, :]).astype(BF16)
         dhidden = mm_t(dout, new_b[1])
         dthird = (dhidden * activ_ref[step]).astype(BF16)
@@ -325,11 +348,12 @@
     def forwarded(got):
         return [got[:1]] if got.shape[0] == 1 else [got[i : i + 1] for i in range(got.shape[0])]
 
-    def scatter(outs, count, unit):
+    def scatter(outs, count, unit, one_by_one=True):
         outs = list(outs)
         evens = list(range(2, count, 2))
         via = forwarded(move(outs.pop(0), "ctx", unit)) if evens else []
-        via, outs[0] = after(via, outs[0])
+        if one_by_one:
+            via, outs[0] = after(via, outs[0])
         first = [move(outs[0], "ctx", unit)] if count > 1 else []
         even = [move(p + v, "ctx", r * unit) for p, v, r in zip(outs[1:], via, evens)]
         return [outs[-1]] + first + even
@@ -366,26 +390,26 @@
     s_in = in_plane(split(split_scaled_kernel, values[0], rates[0]))
     own = [lax.dynamic_index_in_dim(w, mine, 0, keepdims=False) for w in (w_gate, w_out, w_up)]
     own_scale = lax.dynamic_index_in_dim(head_scale, mine, 0, keepdims=True)[None, :]
+    def kept(*dims, dtype=F32):
+        return shape(*dims, tokens, width, dtype=dtype)
+
     *q_out, scale_row = call(
         functools.partial(split_apply_kernel, groups),
-        [shape(2, tokens, width)] * groups + [shape(8, width)],
+        [kept(len(members)) for members in packing(groups)] + [shape(8, width)],
         [scratch], flops // 8, place, queries[0], cotangent[0], gain, own_scale,
     )
     k_in, s_in, q_out = after(k_in, s_in, q_out)
-
-    def kept(*dims, dtype=F32):
-        return shape(*dims, tokens, width, dtype=dtype)
-
+    q_in = q_out[:1] + [move(q_out[i], "ctx", i) for i in range(1, len(q_out))]
     out = call(
         functools.partial(update_kernel, groups, depth, scale),
         [kept(groups, dtype=BF16)] * 2 + slices, [square], 6 * flops,
         place, *k_in, *s_in, *own,
     )
     early, terms = out[:2], out[2:]
-    q_in = in_plane(q_out)
     new = functools.reduce(jnp.add, scatter(terms, depth, groups))
-    new, q_in[:-1] = after(new, q_in[:-1])
-    new, q_in[-1] = gather(new, depth, groups, q_in[-1])
+    new, q_in[1:] = gather(new, depth, groups, q_in[1:])
+    if groups == 4:
+        q_in += [move(q_in[1][2], "ctx", 2), move(q_in[2][2], "ctx", 1)]
     *passed, stats = call(
         functools.partial(apply_kernel, groups, depth),
         [kept(groups), kept(groups), kept(groups, dtype=BF16), kept(groups)]
@@ -410,7 +434,7 @@
     parts, q_back = gather(part, depth, groups, in_plane(out[:groups]))
     (grad_q,) = call(
         functools.partial(join_query_kernel, groups), [joined], [scratch], flops // 16,
-        place, *q_back,
+        place, *q_back, final=True,
     )
     parts, grad_q, saved = after(parts, grad_q, saved)
     rows = hidden // depth
@@ -420,7 +444,7 @@
         place, *early, *saved, *parts, *own,
     )
     back = in_plane(out[:groups])
-    ends = scatter(out[groups:], depth, groups)
+    ends = scatter(out[groups:], depth, groups, one_by_one=False)
     own_rows = rows // groups
     sent = call(
         functools.partial(rows_kernel, groups),
@@ -430,7 +454,7 @@
     grad_k, grad_v, *grads = call(
         functools.partial(join_update_kernel, groups),
         [joined] * 2 + [shape(heads, own_rows, width)] * 3, [scratch] * 2, flops // 8,
-        place, rates[0], *back, *in_plane(sent),
+        place, rates[0], *back, *in_plane(sent), final=True,
     )
     if lax.axis_size("batch") > 1:
         grads = [lax.psum_scatter(x, "batch", scatter_dimension=1, tiled=True) for x in grads]

time: 153 us -> 152 us (level)
  waiting for transfers between devices: 83.9 us -> 72.6 us
  starting transfers between devices: 41.9 us -> 51.7 us
    ppermute x37 -> x38, waiting for transfers between devices: 83.9 us -> 72.6 us  [move(): lax.ppermute(x, axis, [(c, c ^ step) for c in range(lax.axis_size(axis))])]
    ppermute x37 -> x38, starting transfers between devices: 41.9 us -> 51.7 us  [move(): lax.ppermute(x, axis, [(c, c ^ step) for c in range(lax.axis_size(axis))])]
  transfers between devices with their start and end apart: 37 -> 38, of which waited for: 25 -> 23; matrix products, arithmetic and copies ran while one was open for 1% -> 1% of each run, Pallas kernels for 5% -> 5%
where the time goes in v10:
time: 152 us
  waiting for transfers between devices  72.6 us (48%)
  starting transfers between devices  51.7 us (34%)
  Pallas kernels  21 us (14%)
  local copies, waits for them, and re-layouts  5.09 us (3%)
    ppermute x38, waiting for transfers between devices, move(): lax.ppermute(x, axis, [(c, c ^ step) for c in range(lax.axis_size(axis))])  72.6 us
    ppermute x38, starting transfers between devices, move(): lax.ppermute(x, axis, [(c, c ^ step) for c in range(lax.axis_size(axis))])  51.7 us
    pallas_call x11, Pallas kernels, call(): pl.pallas_call(body, out_shape=out_shape if final else [pltpu.VMEM(o.shap...  21 us
    unnamed x24, local copies, waits for them, and re-layouts  3.32 us
  transfers between devices with their start and end apart: 38, of which 23 were waited for; matrix products, arithmetic and copies ran while one was open for 1% of the time, Pallas kernels for 5%

profile of v10, /device:TPU:0, one launch (start us, length us, event | category | flops | bytes accessed | tf_op | source)
XLA Modules:
  0.0 151.6 jit_solution(18330193452167909925)
XLA Ops:
  0.7 1.1 copy-done.5
  1.8 1.7 %shard_map.146 = (f32[256,256]{1,0:T(8,128)S(1)}, f32[256,256]{1,0:T(8,128)S(1)}, f32[256,256]{1,0:T(8,128)}, f32[256,256]{1,0:T(8,128)}) custom-call(s32[2]{0:T(128)S(1)} %pad_add_fusion.place, bf16[256,4,256]{2,1,0:T(4,128)(2,1)S(1)} %bitcast.25), custom_call_target="tpu_custom_call" | custom-call | flops 2147483648 | bytes 1572872 | tf_op jit(solution)/shard_map/pallas_call | solution.py:34
  3.5 0.7 copy-done.7
  4.2 2.9 %collective-permute-start = (f32[256,256]{1,0:T(8,128)S(1)}, f32[256,256]{1,0:T(8,128)S(1)}, u32[]{:S(2)}, u32[]{:S(2)}) collective-permute-start(f32[256,256]{1,0:T(8,128)S(1)} %get-tuple-element.117), channel_id=1, source_target_pairs={{0,2},{2,0},{4,6},{6,4},{8,10},{10,8},{12,14},{14,12},{16,18},{18,... | collective-permute-start | bytes 786440 | tf_op jit(solution)/shard_map/ppermute | solution.py:343
  7.2 1.5 %collective-permute-start.1 = (f32[256,256]{1,0:T(8,128)}, f32[256,256]{1,0:T(8,128)S(1)}, u32[]{:S(2)}, u32[]{:S(2)}) collective-permute-start(f32[256,256]{1,0:T(8,128)} %get-tuple-element.118), channel_id=1, source_target_pairs={{0,4},{2,6},{4,0},{6,2},{8,12},{10,14},{12,8},{14,10},{16,20},{18,... | collective-permute-start | bytes 786440 | tf_op jit(solution)/shard_map/ppermute | solution.py:343
  8.7 1.9 %shard_map.147 = (f32[256,256]{1,0:T(8,128)S(1)}, f32[256,256]{1,0:T(8,128)}, f32[256,256]{1,0:T(8,128)}, f32[256,256]{1,0:T(8,128)}) custom-call(s32[2]{0:T(128)S(1)} %pad_add_fusion.place, bf16[256,4,256]{2,1,0:T(4,128)(2,1)S(1)} %bitcast.26, f32[4,256]{1,0:T(4,128)S(1)} %bitcast.23), custom_call_target="tpu_custom_call" | custom-call | flops 2147483648 | bytes 1576968 | tf_op jit(solution)/shard_map/pallas_call | solution.py:34
  10.7 0.7 copy-done.9
  11.4 1.9 %collective-permute-start.3 = (f32[256,256]{1,0:T(8,128)}, f32[256,256]{1,0:T(8,128)S(1)}, u32[]{:S(2)}, u32[]{:S(2)}) collective-permute-start(f32[256,256]{1,0:T(8,128)} %get-tuple-element.121), channel_id=1, source_target_pairs={{0,2},{2,0},{4,6},{6,4},{8,10},{10,8},{12,14},{14,12},{16,18},{18,... | collective-permute-start | bytes 786440 | tf_op jit(solution)/shard_map/ppermute | solution.py:343
  13.3 1.5 %collective-permute-start.4 = (f32[256,256]{1,0:T(8,128)}, f32[256,256]{1,0:T(8,128)S(1)}, u32[]{:S(2)}, u32[]{:S(2)}) collective-permute-start(f32[256,256]{1,0:T(8,128)} %get-tuple-element.122), channel_id=1, source_target_pairs={{0,4},{2,6},{4,0},{6,2},{8,12},{10,14},{12,8},{14,10},{16,20},{18,... | collective-permute-start | bytes 786440 | tf_op jit(solution)/shard_map/ppermute | solution.py:343
  14.8 2.5 %collective-permute-start.5 = (f32[256,256]{1,0:T(8,128)}, f32[256,256]{1,0:T(8,128)}, u32[]{:S(2)}, u32[]{:S(2)}) collective-permute-start(f32[256,256]{1,0:T(8,128)} %get-tuple-element.123), channel_id=1, source_target_pairs={{0,6},{2,4},{4,2},{6,0},{8,14},{10,12},{12,10},{14,8},{16,22},{18,... | collective-permute-start | bytes 786440 | tf_op jit(solution)/shard_map/ppermute | solution.py:343
  17.3 0.7 copy-done.11
  18.0 0.6 dynamic_slice.14
  18.7 1.9 %shard_map.145 = (f32[2,256,256]{2,1,0:T(8,128)S(1)}, f32[3,256,256]{2,1,0:T(8,128)S(1)}, f32[3,256,256]{2,1,0:T(8,128)S(1)}, f32[8,256]{1,0:T(8,128)S(1)}) custom-call(s32[2]{0:T(128)S(1)} %pad_add_fusion.place, bf16[256,4,256]{2,1,0:T(4,128)(2,1)S(1)} %bitcast.21, bf16[256,4,256]{2,1,0:T(4,128)(2,1)S(1)} %bitcast.22, f32[4,256]{1,0:T(4,128)S(1)} %copy-done.3, ...), custom_call_target="tpu_custom_call" | custom-call | flops 16777216 | bytes 3158028 | tf_op jit(solution)/shard_map/pallas_call | solution.py:34
  20.7 1.1 dynamic-slice_bitcast_fusion
  21.8 3.8 %collective-permute-done.3.refs_5_ = f32[256,256]{1,0:T(8,128)S(1)} collective-permute-done((f32[256,256]{1,0:T(8,128)}, f32[256,256]{1,0:T(8,128)S(1)}, u32[]{:S(2)}, u32[]{:S(2)}) %collective-permute-start.3) | collective-permute-done | bytes 262176 | tf_op jit(solution)/shard_map/ppermute | solution.py:343
  25.6 6.4 %collective-permute-done.4.refs_6_ = f32[256,256]{1,0:T(8,128)S(1)} collective-permute-done((f32[256,256]{1,0:T(8,128)}, f32[256,256]{1,0:T(8,128)S(1)}, u32[]{:S(2)}, u32[]{:S(2)}) %collective-permute-start.4) | collective-permute-done | bytes 262176 | tf_op jit(solution)/shard_map/ppermute | solution.py:343
  32.0 2.6 %shard_map.148 = (bf16[4,256,256]{2,1,0:T(8,128)(2,1)S(1)}, bf16[4,256,256]{2,1,0:T(8,128)(2,1)S(1)}, f32[1,3,64,256]{3,2,1,0:T(8,128)S(1)}, f32[1,3,64,256]{3,2...) custom-call(s32[2]{0:T(128)S(1)} %pad_add_fusion.place, f32[256,256]{1,0:T(8,128)S(1)} %copy-done.8, ...), custom_call_target="tpu_custom_call" | custom-call | flops 805306368 | bytes 4718600 | tf_op jit(solution)/shard_map/pallas_call | solution.py:34
  34.6 1.6 %collective-permute-start.6 = (f32[1,3,64,256]{3,2,1,0:T(8,128)S(1)}, f32[1,3,64,256]{3,2,1,0:T(8,128)S(1)}, u32[]{:S(2)}, u32[]{:S(2)}) collective-permute-start(f32[1,3,64,256]{3,2,1,0:T(8,128)S(1)} %get-tuple-element.137), channel_id=1, source_target_pairs={{0,8},{2,10},{4,12},{6,14},{8,0},{10,2},{12,4},{14,6},{16,24},{18,... | collective-permute-start | bytes 589832 | tf_op jit(solution)/shard_map/ppermute | solution.py:343
  36.3 1.2 collective-permute-start.11
  37.4 0.9 collective-permute-start.12
  38.3 2.0 %collective-permute-done.6 = f32[1,3,64,256]{3,2,1,0:T(8,128)S(1)} collective-permute-done((f32[1,3,64,256]{3,2,1,0:T(8,128)S(1)}, f32[1,3,64,256]{3,2,1,0:T(8,128)S(1)}, u32[]{:S(2)}, u32[]{:S(2)}) %collective-permute-start.6) | collective-permute-done | bytes 196640 | tf_op jit(solution)/shard_map/ppermute | solution.py:343
  40.4 2.7 %collective-permute-start.8 = (f32[1,3,64,256]{3,2,1,0:T(8,128)S(1)}, f32[1,3,64,256]{3,2,1,0:T(8,128)S(1)}, u32[]{:S(2)}, u32[]{:S(2)}) collective-permute-start(f32[1,3,64,256]{3,2,1,0:T(8,128)S(1)} %add.34), channel_id=1, source_target_pairs={{0,16},{2,18},{4,20},{6,22},{8,24},{10,26},{12,28},{14,30},{16,0},... | collective-permute-start | bytes 589832 | tf_op jit(solution)/shard_map/ppermute | solution.py:343
  43.0 1.6 %collective-permute-start.7 = (f32[1,3,64,256]{3,2,1,0:T(8,128)S(1)}, f32[1,3,64,256]{3,2,1,0:T(8,128)S(1)}, u32[]{:S(2)}, u32[]{:S(2)}) collective-permute-start(f32[1,3,64,256]{3,2,1,0:T(8,128)S(1)} %get-tuple-element.139), channel_id=1, source_target_pairs={{0,8},{2,10},{4,12},{6,14},{8,0},{10,2},{12,4},{14,6},{16,24},{18,... | collective-permute-start | bytes 589832 | tf_op jit(solution)/shard_map/ppermute | solution.py:343
  44.6 5.4 %collective-permute-done.8 = f32[1,3,64,256]{3,2,1,0:T(8,128)S(1)} collective-permute-done((f32[1,3,64,256]{3,2,1,0:T(8,128)S(1)}, f32[1,3,64,256]{3,2,1,0:T(8,128)S(1)}, u32[]{:S(2)}, u32[]{:S(2)}) %collective-permute-start.8) | collective-permute-done | bytes 196640 | tf_op jit(solution)/shard_map/ppermute | solution.py:343
  50.3 1.4 collective-permute-start.10
  51.7 3.0 %collective-permute-start.9 = (f32[1,3,64,256]{3,2,1,0:T(8,128)S(1)}, f32[1,3,64,256]{3,2,1,0:T(8,128)S(1)}, u32[]{:S(2)}, u32[]{:S(2)}) collective-permute-start(f32[1,3,64,256]{3,2,1,0:T(8,128)S(1)} %add_add_fusion.1.refs_5_), channel_id=1, source_target_pairs={{0,8},{2,10},{4,12},{6,14},{8,0},{10,2},{12,4},{14,6},{16,24},{18,... | collective-permute-start | bytes 589832 | tf_op jit(solution)/shard_map/ppermute | solution.py:343
  54.7 3.2 %collective-permute-done.10.refs_7_ = f32[1,3,64,256]{3,2,1,0:T(8,128)S(1)} collective-permute-done((f32[1,3,64,256]{3,2,1,0:T(8,128)S(1)}, f32[1,3,64,256]{3,2,1,0:T(8,128)S(1)}, u32[]{:S(2)}, u32[]{:S(2)}) %collective-permute-start.10) | collective-permute-done | bytes 196640 | tf_op jit(solution)/shard_map/ppermute | solution.py:343
  57.9 1.6 %collective-permute-done.9.refs_6_ = f32[1,3,64,256]{3,2,1,0:T(8,128)S(1)} collective-permute-done((f32[1,3,64,256]{3,2,1,0:T(8,128)S(1)}, f32[1,3,64,256]{3,2,1,0:T(8,128)S(1)}, u32[]{:S(2)}, u32[]{:S(2)}) %collective-permute-start.9) | collective-permute-done | bytes 196640 | tf_op jit(solution)/shard_map/ppermute | solution.py:343
  59.6 2.4 %collective-permute-start.14 = (f32[256,256]{1,0:T(8,128)S(1)}, f32[256,256]{1,0:T(8,128)S(1)}, u32[]{:S(2)}, u32[]{:S(2)}) collective-permute-start(f32[256,256]{1,0:T(8,128)S(1)} %slice_bitcast_fusion), channel_id=1, source_target_pairs={{0,2},{2,0},{4,6},{6,4},{8,10},{10,8},{12,14},{14,12},{16,18},{18,... | collective-permute-start | bytes 786440 | tf_op jit(solution)/shard_map/ppermute | solution.py:343
  62.1 1.4 collective-permute-start.13
  63.5 2.0 %collective-permute-start.15 = (f32[1,3,64,256]{3,2,1,0:T(8,128)S(1)}, f32[1,3,64,256]{3,2,1,0:T(8,128)S(1)}, u32[]{:S(2)}, u32[]{:S(2)}) collective-permute-start(f32[1,3,64,256]{3,2,1,0:T(8,128)S(1)} %collective-permute-done.10.refs_7_), channel_id=1, source_target_pairs={{0,8},{2,10},{4,12},{6,14},{8,0},{10,2},{12,4},{14,6},{16,24},{18,... | collective-permute-start | bytes 589832 | tf_op jit(solution)/shard_map/ppermute | solution.py:343
  65.5 3.6 %collective-permute-done.15.refs_8_ = f32[1,3,64,256]{3,2,1,0:T(8,128)S(1)} collective-permute-done((f32[1,3,64,256]{3,2,1,0:T(8,128)S(1)}, f32[1,3,64,256]{3,2,1,0:T(8,128)S(1)}, u32[]{:S(2)}, u32[]{:S(2)}) %collective-permute-start.15) | collective-permute-done | bytes 196640 | tf_op jit(solution)/shard_map/ppermute | solution.py:343
  69.2 1.8 %shard_map.149 = (f32[4,256,256]{2,1,0:T(8,128)S(1)}, f32[4,256,256]{2,1,0:T(8,128)S(1)}, bf16[4,256,256]{2,1,0:T(8,128)(2,1)S(1)}, f32[4,256,256]{2,1,0:T(8,128...) custom-call(s32[2]{0:T(128)S(1)} %pad_add_fusion.place, f32[8,256]{1,0:T(8,128)S(1)} %get-tuple-element.115.scale_row, ...), custom_call_target="tpu_custom_call" | custom-call | flops 402653184 | bytes 7487496 | tf_op jit(solution)/shard_map/pallas_call | solution.py:34
  71.0 1.2 collective-permute-done.16
  72.1 2.1 %collective-permute-start.19 = (f32[2,4,256]{2,1,0:T(4,128)S(1)}, f32[2,4,256]{2,1,0:T(4,128)S(1)}, u32[]{:S(2)}, u32[]{:S(2)}) collective-permute-start(f32[2,4,256]{2,1,0:T(4,128)S(1)} %add.36.refs_5_), channel_id=1, source_target_pairs={{0,6},{2,4},{4,2},{6,0},{8,14},{10,12},{12,10},{14,8},{16,22},{18,... | collective-permute-start | bytes 24584 | tf_op jit(solution)/shard_map/ppermute | solution.py:343
  74.2 1.3 collective-permute-start.18
  75.6 1.1 collective-permute-done.19.refs_8_
  76.7 1.2 collective-permute-done.18.refs_7_
  77.9 1.3 collective-permute-done.17.refs_6_
  79.2 2.1 %shard_map.150 = (f32[256,256]{1,0:T(8,128)S(1)}, f32[256,256]{1,0:T(8,128)S(1)}, f32[256,256]{1,0:T(8,128)S(1)}, f32[256,256]{1,0:T(8,128)S(1)}, f32[1,3,64,256...) custom-call(s32[2]{0:T(128)S(1)} %pad_add_fusion.place, ...), custom_call_target="tpu_custom_call" | custom-call | flops 805306368 | bytes 8560648 | tf_op jit(solution)/shard_map/pallas_call | solution.py:34
  81.3 2.1 %collective-permute-start.20 = (f32[1,3,64,256]{3,2,1,0:T(8,128)S(1)}, f32[1,3,64,256]{3,2,1,0:T(8,128)S(1)}, u32[]{:S(2)}, u32[]{:S(2)}) collective-permute-start(f32[1,3,64,256]{3,2,1,0:T(8,128)S(1)} %get-tuple-element.166), channel_id=1, source_target_pairs={{0,8},{2,10},{4,12},{6,14},{8,0},{10,2},{12,4},{14,6},{16,24},{18,... | collective-permute-start | bytes 589832 | tf_op jit(solution)/shard_map/ppermute | solution.py:343
  83.4 3.8 %collective-permute-done.20 = f32[1,3,64,256]{3,2,1,0:T(8,128)S(1)} collective-permute-done((f32[1,3,64,256]{3,2,1,0:T(8,128)S(1)}, f32[1,3,64,256]{3,2,1,0:T(8,128)S(1)}, u32[]{:S(2)}, u32[]{:S(2)}) %collective-permute-start.20) | collective-permute-done | bytes 196640 | tf_op jit(solution)/shard_map/ppermute | solution.py:343
  87.3 2.2 %collective-permute-start.22 = (f32[1,3,64,256]{3,2,1,0:T(8,128)S(1)}, f32[1,3,64,256]{3,2,1,0:T(8,128)S(1)}, u32[]{:S(2)}, u32[]{:S(2)}) collective-permute-start(f32[1,3,64,256]{3,2,1,0:T(8,128)S(1)} %add.38), channel_id=1, source_target_pairs={{0,16},{2,18},{4,20},{6,22},{8,24},{10,26},{12,28},{14,30},{16,0},... | collective-permute-start | bytes 589832 | tf_op jit(solution)/shard_map/ppermute | solution.py:343
  89.5 1.9 %collective-permute-start.21 = (f32[1,3,64,256]{3,2,1,0:T(8,128)S(1)}, f32[1,3,64,256]{3,2,1,0:T(8,128)S(1)}, u32[]{:S(2)}, u32[]{:S(2)}) collective-permute-start(f32[1,3,64,256]{3,2,1,0:T(8,128)S(1)} %get-tuple-element.168), channel_id=1, source_target_pairs={{0,8},{2,10},{4,12},{6,14},{8,0},{10,2},{12,4},{14,6},{16,24},{18,... | collective-permute-start | bytes 589832 | tf_op jit(solution)/shard_map/ppermute | solution.py:343
  91.4 0.7 collective-permute-start.26
  92.1 2.7 %collective-permute-start.27 = (f32[256,256]{1,0:T(8,128)S(1)}, f32[256,256]{1,0:T(8,128)S(1)}, u32[]{:S(2)}, u32[]{:S(2)}) collective-permute-start(f32[256,256]{1,0:T(8,128)S(1)} %get-tuple-element.174), channel_id=1, source_target_pairs={{0,6},{2,4},{4,2},{6,0},{8,14},{10,12},{12,10},{14,8},{16,22},{18,... | collective-permute-start | bytes 786440 | tf_op jit(solution)/shard_map/ppermute | solution.py:343
  94.8 2.6 %collective-permute-done.22 = f32[1,3,64,256]{3,2,1,0:T(8,128)S(1)} collective-permute-done((f32[1,3,64,256]{3,2,1,0:T(8,128)S(1)}, f32[1,3,64,256]{3,2,1,0:T(8,128)S(1)}, u32[]{:S(2)}, u32[]{:S(2)}) %collective-permute-start.22) | collective-permute-done | bytes 196640 | tf_op jit(solution)/shard_map/ppermute | solution.py:343
  97.5 1.4 collective-permute-start.24
  98.9 2.2 %collective-permute-start.23 = (f32[1,3,64,256]{3,2,1,0:T(8,128)S(1)}, f32[1,3,64,256]{3,2,1,0:T(8,128)S(1)}, u32[]{:S(2)}, u32[]{:S(2)}) collective-permute-start(f32[1,3,64,256]{3,2,1,0:T(8,128)S(1)} %add_add_fusion.refs_11_.refs_0_), channel_id=1, source_target_pairs={{0,8},{2,10},{4,12},{6,14},{8,0},{10,2},{12,4},{14,6},{16,24},{18,... | collective-permute-start | bytes 589832 | tf_op jit(solution)/shard_map/ppermute | solution.py:343
  101.1 1.2 collective-permute-done.26.refs_2_
  102.2 6.4 %collective-permute-done.24.refs_13_ = f32[1,3,64,256]{3,2,1,0:T(8,128)S(1)} collective-permute-done((f32[1,3,64,256]{3,2,1,0:T(8,128)S(1)}, f32[1,3,64,256]{3,2,1,0:T(8,128)S(1)}, u32[]{:S(2)}, u32[]{:S(2)}) %collective-permute-start.24) | collective-permute-done | bytes 196640 | tf_op jit(solution)/shard_map/ppermute | solution.py:343
  108.8 1.1 shard_map.152
  109.9 1.7 %shard_map.151 = bf16[256,4,256]{2,1,0:T(4,128)(2,1)} custom-call(s32[2]{0:T(128)S(1)} %pad_add_fusion.place, f32[256,256]{1,0:T(8,128)S(1)} %get-tuple-element.178.refs_0_, f32[256,256]{1,0:T(8,128)S(1)} %collective-permute-done.25.refs_1_, f32[256,256]{1,0:T(8,128)S(1)} %collective-permute-done.26.refs_2_, f32[256,256]{1,0:T(8,128)S(1)} %collective-permute-done.27.refs_3_), custom_call_target="tpu_custom_call" | custom-call | flops 8388608 | bytes 1572872 | tf_op jit(solution)/shard_map/pallas_call | solution.py:34
  111.6 3.7 %collective-permute-done.28.refs_14_ = f32[1,3,64,256]{3,2,1,0:T(8,128)S(1)} collective-permute-done((f32[1,3,64,256]{3,2,1,0:T(8,128)S(1)}, f32[1,3,64,256]{3,2,1,0:T(8,128)S(1)}, u32[]{:S(2)}, u32[]{:S(2)}) %collective-permute-start.28) | collective-permute-done | bytes 196640 | tf_op jit(solution)/shard_map/ppermute | solution.py:343
  115.3 3.2 %shard_map.153 = (f32[2,256,256]{2,1,0:T(8,128)S(1)}, f32[2,256,256]{2,1,0:T(8,128)S(1)}, f32[2,256,256]{2,1,0:T(8,128)S(1)}, f32[2,256,256]{2,1,0:T(8,128)S(1)}...) custom-call(s32[2]{0:T(128)S(1)} %pad_add_fusion.place, ...), custom_call_target="tpu_custom_call" | custom-call | flops 1610612736 | bytes 13369352 | tf_op jit(solution)/shard_map/pallas_call | solution.py:34
  118.8 3.2 %collective-permute-start.31 = (f32[2,256,256]{2,1,0:T(8,128)S(1)}, f32[2,256,256]{2,1,0:T(8,128)S(1)}, u32[]{:S(2)}, u32[]{:S(2)}) collective-permute-start(f32[2,256,256]{2,1,0:T(8,128)S(1)} %get-tuple-element.210), channel_id=1, source_target_pairs={{0,6},{2,4},{4,2},{6,0},{8,14},{10,12},{12,10},{14,8},{16,22},{18,... | collective-permute-start | bytes 1572872 | tf_op jit(solution)/shard_map/ppermute | solution.py:343
  122.3 1.7 %collective-permute-start.32 = (f32[1,3,64,256]{3,2,1,0:T(8,128)S(1)}, f32[1,3,64,256]{3,2,1,0:T(8,128)S(1)}, u32[]{:S(2)}, u32[]{:S(2)}) collective-permute-start(f32[1,3,64,256]{3,2,1,0:T(8,128)S(1)} %get-tuple-element.212), channel_id=1, source_target_pairs={{0,8},{2,10},{4,12},{6,14},{8,0},{10,2},{12,4},{14,6},{16,24},{18,... | collective-permute-start | bytes 589832 | tf_op jit(solution)/shard_map/ppermute | solution.py:343
  124.1 5.5 %collective-permute-done.33 = f32[1,3,64,256]{3,2,1,0:T(8,128)S(1)} collective-permute-done((f32[1,3,64,256]{3,2,1,0:T(8,128)S(1)}, f32[1,3,64,256]{3,2,1,0:T(8,128)S(1)}, u32[]{:S(2)}, u32[]{:S(2)}) %collective-permute-start.33) | collective-permute-done | bytes 196640 | tf_op jit(solution)/shard_map/ppermute | solution.py:343
  129.7 3.6 %collective-permute-done.32.refs_2_ = f32[1,3,64,256]{3,2,1,0:T(8,128)S(1)} collective-permute-done((f32[1,3,64,256]{3,2,1,0:T(8,128)S(1)}, f32[1,3,64,256]{3,2,1,0:T(8,128)S(1)}, u32[]{:S(2)}, u32[]{:S(2)}) %collective-permute-start.32) | collective-permute-done | bytes 196640 | tf_op jit(solution)/shard_map/ppermute | solution.py:343
  133.2 5.1 %collective-permute-done.34.refs_3_ = f32[1,3,64,256]{3,2,1,0:T(8,128)S(1)} collective-permute-done((f32[1,3,64,256]{3,2,1,0:T(8,128)S(1)}, f32[1,3,64,256]{3,2,1,0:T(8,128)S(1)}, u32[]{:S(2)}, u32[]{:S(2)}) %collective-permute-start.34) | collective-permute-done | bytes 196640 | tf_op jit(solution)/shard_map/ppermute | solution.py:343
  138.3 0.6 shard_map.154
  139.6 4.5 %collective-permute-done.35.refs_5_ = f32[1,3,16,256]{3,2,1,0:T(8,128)S(1)} collective-permute-done((f32[1,3,16,256]{3,2,1,0:T(8,128)S(1)}, f32[1,3,16,256]{3,2,1,0:T(8,128)S(1)}, u32[]{:S(2)}, u32[]{:S(2)}) %collective-permute-start.35) | collective-permute-done | bytes 49184 | tf_op jit(solution)/shard_map/ppermute | solution.py:343
  144.2 5.0 %collective-permute-done.37.refs_7_ = f32[1,3,16,256]{3,2,1,0:T(8,128)S(1)} collective-permute-done((f32[1,3,16,256]{3,2,1,0:T(8,128)S(1)}, f32[1,3,16,256]{3,2,1,0:T(8,128)S(1)}, u32[]{:S(2)}, u32[]{:S(2)}) %collective-permute-start.37) | collective-permute-done | bytes 49184 | tf_op jit(solution)/shard_map/ppermute | solution.py:343
  149.2 2.4 %shard_map.155 = (bf16[256,4,256]{2,1,0:T(4,128)(2,1)}, bf16[256,4,256]{2,1,0:T(4,128)(2,1)}, f32[4,16,256]{2,1,0:T(8,128)}, f32[4,16,256]{2,1,0:T(8,128)}, f32[4,16,256]{2,1,0:T(8,128)}) custom-call(s32[2]{0:T(128)S(1)} %pad_add_fusion.place, f32[4,256]{1,0:T(4,128)S(1)} %bitcast.24, f32[2,256,256]{2,1,0:T(8,128)S(1)} %get-tuple-element.207.refs_0_, ...), custom_call_target="tpu_custom_call" | custom-call | flops 16777216 | bytes 3543048 | tf_op jit(solution)/shard_map/pallas_call | solution.py:34
  (59 shorter events, 2.4 us)
Async XLA Ops:
  0.6 20.0 %copy-start = (f32[4,256,256]{2,1,0:T(8,128)S(1)}, f32[4,256,256]{2,1,0:T(8,128)}, u32[]{:S(2)}) copy-start(f32[4,256,256]{2,1,0:T(8,128)} %param.16) | copy-start | bytes 3145732
  0.7 1.1 copy-start.5
  1.8 6.9 %copy-start.6 = (bf16[1,256,4,256]{3,2,1,0:T(4,128)(2,1)S(1)}, bf16[1,256,4,256]{3,2,1,0:T(4,128)(2,1)}, u32[]{:S(2)}) copy-start(bf16[1,256,4,256]{3,2,1,0:T(4,128)(2,1)} %param.12) | copy-start | bytes 1572868
  3.5 0.7 copy-start.7
  4.2 4.5 %copy-start.4 = (f32[1,4,256]{2,1,0:T(4,128)S(1)}, f32[1,4,256]{2,1,0:T(4,128)}, u32[]{:S(2)}) copy-start(f32[1,4,256]{2,1,0:T(4,128)} %param.13) | copy-start | bytes 12292
  4.2 10.6 %collective-permute-start = (f32[256,256]{1,0:T(8,128)S(1)}, f32[256,256]{1,0:T(8,128)S(1)}, u32[]{:S(2)}, u32[]{:S(2)}) collective-permute-start(f32[256,256]{1,0:T(8,128)S(1)} %get-tuple-element.117), channel_id=1, source_target_pairs={{0,2},{2,0},{4,6},{6,4},{8,10},{10,8},{12,14},{14,12},{16,18},{18,... | collective-permute-start | bytes 786440 | tf_op jit(solution)/shard_map/ppermute | solution.py:343
  7.2 14.6 %collective-permute-start.1 = (f32[256,256]{1,0:T(8,128)}, f32[256,256]{1,0:T(8,128)S(1)}, u32[]{:S(2)}, u32[]{:S(2)}) collective-permute-start(f32[256,256]{1,0:T(8,128)} %get-tuple-element.118), channel_id=1, source_target_pairs={{0,4},{2,6},{4,0},{6,2},{8,12},{10,14},{12,8},{14,10},{16,20},{18,... | collective-permute-start | bytes 786440 | tf_op jit(solution)/shard_map/ppermute | solution.py:343
  8.7 13.1 %collective-permute-start.2 = (f32[256,256]{1,0:T(8,128)}, f32[256,256]{1,0:T(8,128)S(1)}, u32[]{:S(2)}, u32[]{:S(2)}) collective-permute-start(f32[256,256]{1,0:T(8,128)} %get-tuple-element.119), channel_id=1, source_target_pairs={{0,6},{2,4},{4,2},{6,0},{8,14},{10,12},{12,10},{14,8},{16,22},{18,... | collective-permute-start | bytes 786440 | tf_op jit(solution)/shard_map/ppermute | solution.py:343
  8.7 9.9 %copy-start.1 = (bf16[1,256,4,256]{3,2,1,0:T(4,128)(2,1)S(1)}, bf16[1,256,4,256]{3,2,1,0:T(4,128)(2,1)}, u32[]{:S(2)}) copy-start(bf16[1,256,4,256]{3,2,1,0:T(4,128)(2,1)} %param.10) | copy-start | bytes 1572868
  8.7 9.9 %copy-start.2 = (bf16[1,256,4,256]{3,2,1,0:T(4,128)(2,1)S(1)}, bf16[1,256,4,256]{3,2,1,0:T(4,128)(2,1)}, u32[]{:S(2)}) copy-start(bf16[1,256,4,256]{3,2,1,0:T(4,128)(2,1)} %param.19) | copy-start | bytes 1572868
  10.7 0.7 copy-start.9
  11.4 14.2 %collective-permute-start.3 = (f32[256,256]{1,0:T(8,128)}, f32[256,256]{1,0:T(8,128)S(1)}, u32[]{:S(2)}, u32[]{:S(2)}) collective-permute-start(f32[256,256]{1,0:T(8,128)} %get-tuple-element.121), channel_id=1, source_target_pairs={{0,2},{2,0},{4,6},{6,4},{8,10},{10,8},{12,14},{14,12},{16,18},{18,... | collective-permute-start | bytes 786440 | tf_op jit(solution)/shard_map/ppermute | solution.py:343
  13.3 18.7 %collective-permute-start.4 = (f32[256,256]{1,0:T(8,128)}, f32[256,256]{1,0:T(8,128)S(1)}, u32[]{:S(2)}, u32[]{:S(2)}) collective-permute-start(f32[256,256]{1,0:T(8,128)} %get-tuple-element.122), channel_id=1, source_target_pairs={{0,4},{2,6},{4,0},{6,2},{8,12},{10,14},{12,8},{14,10},{16,20},{18,... | collective-permute-start | bytes 786440 | tf_op jit(solution)/shard_map/ppermute | solution.py:343
  14.8 17.2 %collective-permute-start.5 = (f32[256,256]{1,0:T(8,128)}, f32[256,256]{1,0:T(8,128)}, u32[]{:S(2)}, u32[]{:S(2)}) collective-permute-start(f32[256,256]{1,0:T(8,128)} %get-tuple-element.123), channel_id=1, source_target_pairs={{0,6},{2,4},{4,2},{6,0},{8,14},{10,12},{12,10},{14,8},{16,22},{18,... | collective-permute-start | bytes 786440 | tf_op jit(solution)/shard_map/ppermute | solution.py:343
  17.3 0.7 copy-start.11
  18.0 0.7 copy-start.3
  20.7 11.4 %copy-start.8 = (f32[256,256]{1,0:T(8,128)S(1)}, f32[256,256]{1,0:T(8,128)}, u32[]{:S(2)}) copy-start(f32[256,256]{1,0:T(8,128)} %copy-done.7) | copy-start | bytes 786436
  20.7 11.3 %copy-start.10 = (f32[256,256]{1,0:T(8,128)S(1)}, f32[256,256]{1,0:T(8,128)}, u32[]{:S(2)}) copy-start(f32[256,256]{1,0:T(8,128)} %copy-done.9) | copy-start | bytes 786436
  34.6 5.7 %collective-permute-start.6 = (f32[1,3,64,256]{3,2,1,0:T(8,128)S(1)}, f32[1,3,64,256]{3,2,1,0:T(8,128)S(1)}, u32[]{:S(2)}, u32[]{:S(2)}) collective-permute-start(f32[1,3,64,256]{3,2,1,0:T(8,128)S(1)} %get-tuple-element.137), channel_id=1, source_target_pairs={{0,8},{2,10},{4,12},{6,14},{8,0},{10,2},{12,4},{14,6},{16,24},{18,... | collective-permute-start | bytes 589832 | tf_op jit(solution)/shard_map/ppermute | solution.py:343
  36.3 23.3 %collective-permute-start.11 = (f32[3,256,256]{2,1,0:T(8,128)S(1)}, f32[3,256,256]{2,1,0:T(8,128)S(1)}, u32[]{:S(2)}, u32[]{:S(2)}) collective-permute-start(f32[3,256,256]{2,1,0:T(8,128)S(1)} %get-tuple-element.142), channel_id=1, source_target_pairs={{0,2},{2,0},{4,6},{6,4},{8,10},{10,8},{12,14},{14,12},{16,18},{18,... | collective-permute-start | bytes 2359304 | tf_op jit(solution)/shard_map/ppermute | solution.py:343
  37.4 22.2 %collective-permute-start.12 = (f32[3,256,256]{2,1,0:T(8,128)S(1)}, f32[3,256,256]{2,1,0:T(8,128)S(1)}, u32[]{:S(2)}, u32[]{:S(2)}) collective-permute-start(f32[3,256,256]{2,1,0:T(8,128)S(1)} %get-tuple-element.143), channel_id=1, source_target_pairs={{0,4},{2,6},{4,0},{6,2},{8,12},{10,14},{12,8},{14,10},{16,20},{18,... | collective-permute-start | bytes 2359304 | tf_op jit(solution)/shard_map/ppermute | solution.py:343
  40.4 9.7 %collective-permute-start.8 = (f32[1,3,64,256]{3,2,1,0:T(8,128)S(1)}, f32[1,3,64,256]{3,2,1,0:T(8,128)S(1)}, u32[]{:S(2)}, u32[]{:S(2)}) collective-permute-start(f32[1,3,64,256]{3,2,1,0:T(8,128)S(1)} %add.34), channel_id=1, source_target_pairs={{0,16},{2,18},{4,20},{6,22},{8,24},{10,26},{12,28},{14,30},{16,0},... | collective-permute-start | bytes 589832 | tf_op jit(solution)/shard_map/ppermute | solution.py:343
  43.0 7.2 %collective-permute-start.7 = (f32[1,3,64,256]{3,2,1,0:T(8,128)S(1)}, f32[1,3,64,256]{3,2,1,0:T(8,128)S(1)}, u32[]{:S(2)}, u32[]{:S(2)}) collective-permute-start(f32[1,3,64,256]{3,2,1,0:T(8,128)S(1)} %get-tuple-element.139), channel_id=1, source_target_pairs={{0,8},{2,10},{4,12},{6,14},{8,0},{10,2},{12,4},{14,6},{16,24},{18,... | collective-permute-start | bytes 589832 | tf_op jit(solution)/shard_map/ppermute | solution.py:343
  50.3 7.6 %collective-permute-start.10 = (f32[1,3,64,256]{3,2,1,0:T(8,128)S(1)}, f32[1,3,64,256]{3,2,1,0:T(8,128)S(1)}, u32[]{:S(2)}, u32[]{:S(2)}) collective-permute-start(f32[1,3,64,256]{3,2,1,0:T(8,128)S(1)} %add_add_fusion.1.refs_5_), channel_id=1, source_target_pairs={{0,16},{2,18},{4,20},{6,22},{8,24},{10,26},{12,28},{14,30},{16,0},... | collective-permute-start | bytes 589832 | tf_op jit(solution)/shard_map/ppermute | solution.py:343
  51.7 7.9 %collective-permute-start.9 = (f32[1,3,64,256]{3,2,1,0:T(8,128)S(1)}, f32[1,3,64,256]{3,2,1,0:T(8,128)S(1)}, u32[]{:S(2)}, u32[]{:S(2)}) collective-permute-start(f32[1,3,64,256]{3,2,1,0:T(8,128)S(1)} %add_add_fusion.1.refs_5_), channel_id=1, source_target_pairs={{0,8},{2,10},{4,12},{6,14},{8,0},{10,2},{12,4},{14,6},{16,24},{18,... | collective-permute-start | bytes 589832 | tf_op jit(solution)/shard_map/ppermute | solution.py:343
  59.6 9.5 %collective-permute-start.14 = (f32[256,256]{1,0:T(8,128)S(1)}, f32[256,256]{1,0:T(8,128)S(1)}, u32[]{:S(2)}, u32[]{:S(2)}) collective-permute-start(f32[256,256]{1,0:T(8,128)S(1)} %slice_bitcast_fusion), channel_id=1, source_target_pairs={{0,2},{2,0},{4,6},{6,4},{8,10},{10,8},{12,14},{14,12},{16,18},{18,... | collective-permute-start | bytes 786440 | tf_op jit(solution)/shard_map/ppermute | solution.py:343
  62.1 7.1 %collective-permute-start.13 = (f32[256,256]{1,0:T(8,128)S(1)}, f32[256,256]{1,0:T(8,128)S(1)}, u32[]{:S(2)}, u32[]{:S(2)}) collective-permute-start(f32[256,256]{1,0:T(8,128)S(1)} %slice_bitcast_fusion.1), channel_id=1, source_target_pairs={{0,4},{2,6},{4,0},{6,2},{8,12},{10,14},{12,8},{14,10},{16,20},{18,... | collective-permute-start | bytes 786440 | tf_op jit(solution)/shard_map/ppermute | solution.py:343
  63.5 5.7 %collective-permute-start.15 = (f32[1,3,64,256]{3,2,1,0:T(8,128)S(1)}, f32[1,3,64,256]{3,2,1,0:T(8,128)S(1)}, u32[]{:S(2)}, u32[]{:S(2)}) collective-permute-start(f32[1,3,64,256]{3,2,1,0:T(8,128)S(1)} %collective-permute-done.10.refs_7_), channel_id=1, source_target_pairs={{0,8},{2,10},{4,12},{6,14},{8,0},{10,2},{12,4},{14,6},{16,24},{18,... | collective-permute-start | bytes 589832 | tf_op jit(solution)/shard_map/ppermute | solution.py:343
  70.9 1.2 collective-permute-start.16
  72.1 4.5 %collective-permute-start.19 = (f32[2,4,256]{2,1,0:T(4,128)S(1)}, f32[2,4,256]{2,1,0:T(4,128)S(1)}, u32[]{:S(2)}, u32[]{:S(2)}) collective-permute-start(f32[2,4,256]{2,1,0:T(4,128)S(1)} %add.36.refs_5_), channel_id=1, source_target_pairs={{0,6},{2,4},{4,2},{6,0},{8,14},{10,12},{12,10},{14,8},{16,22},{18,... | collective-permute-start | bytes 24584 | tf_op jit(solution)/shard_map/ppermute | solution.py:343
  74.2 3.7 %collective-permute-start.18 = (f32[2,4,256]{2,1,0:T(4,128)S(1)}, f32[2,4,256]{2,1,0:T(4,128)S(1)}, u32[]{:S(2)}, u32[]{:S(2)}) collective-permute-start(f32[2,4,256]{2,1,0:T(4,128)S(1)} %add.36.refs_5_), channel_id=1, source_target_pairs={{0,4},{2,6},{4,0},{6,2},{8,12},{10,14},{12,8},{14,10},{16,20},{18,... | collective-permute-start | bytes 24584 | tf_op jit(solution)/shard_map/ppermute | solution.py:343
  75.6 3.7 %collective-permute-start.17 = (f32[2,4,256]{2,1,0:T(4,128)S(1)}, f32[2,4,256]{2,1,0:T(4,128)S(1)}, u32[]{:S(2)}, u32[]{:S(2)}) collective-permute-start(f32[2,4,256]{2,1,0:T(4,128)S(1)} %add.36.refs_5_), channel_id=1, source_target_pairs={{0,2},{2,0},{4,6},{6,4},{8,10},{10,8},{12,14},{14,12},{16,18},{18,... | collective-permute-start | bytes 24584 | tf_op jit(solution)/shard_map/ppermute | solution.py:343
  81.3 5.9 %collective-permute-start.20 = (f32[1,3,64,256]{3,2,1,0:T(8,128)S(1)}, f32[1,3,64,256]{3,2,1,0:T(8,128)S(1)}, u32[]{:S(2)}, u32[]{:S(2)}) collective-permute-start(f32[1,3,64,256]{3,2,1,0:T(8,128)S(1)} %get-tuple-element.166), channel_id=1, source_target_pairs={{0,8},{2,10},{4,12},{6,14},{8,0},{10,2},{12,4},{14,6},{16,24},{18,... | collective-permute-start | bytes 589832 | tf_op jit(solution)/shard_map/ppermute | solution.py:343
  87.3 10.2 %collective-permute-start.22 = (f32[1,3,64,256]{3,2,1,0:T(8,128)S(1)}, f32[1,3,64,256]{3,2,1,0:T(8,128)S(1)}, u32[]{:S(2)}, u32[]{:S(2)}) collective-permute-start(f32[1,3,64,256]{3,2,1,0:T(8,128)S(1)} %add.38), channel_id=1, source_target_pairs={{0,16},{2,18},{4,20},{6,22},{8,24},{10,26},{12,28},{14,30},{16,0},... | collective-permute-start | bytes 589832 | tf_op jit(solution)/shard_map/ppermute | solution.py:343
  89.5 8.0 %collective-permute-start.21 = (f32[1,3,64,256]{3,2,1,0:T(8,128)S(1)}, f32[1,3,64,256]{3,2,1,0:T(8,128)S(1)}, u32[]{:S(2)}, u32[]{:S(2)}) collective-permute-start(f32[1,3,64,256]{3,2,1,0:T(8,128)S(1)} %get-tuple-element.168), channel_id=1, source_target_pairs={{0,8},{2,10},{4,12},{6,14},{8,0},{10,2},{12,4},{14,6},{16,24},{18,... | collective-permute-start | bytes 589832 | tf_op jit(solution)/shard_map/ppermute | solution.py:343
  91.4 9.7 %collective-permute-start.25 = (f32[256,256]{1,0:T(8,128)S(1)}, f32[256,256]{1,0:T(8,128)S(1)}, u32[]{:S(2)}, u32[]{:S(2)}) collective-permute-start(f32[256,256]{1,0:T(8,128)S(1)} %get-tuple-element.172), channel_id=1, source_target_pairs={{0,2},{2,0},{4,6},{6,4},{8,10},{10,8},{12,14},{14,12},{16,18},{18,... | collective-permute-start | bytes 786440 | tf_op jit(solution)/shard_map/ppermute | solution.py:343
  91.4 10.8 %collective-permute-start.26 = (f32[256,256]{1,0:T(8,128)S(1)}, f32[256,256]{1,0:T(8,128)S(1)}, u32[]{:S(2)}, u32[]{:S(2)}) collective-permute-start(f32[256,256]{1,0:T(8,128)S(1)} %get-tuple-element.173), channel_id=1, source_target_pairs={{0,4},{2,6},{4,0},{6,2},{8,12},{10,14},{12,8},{14,10},{16,20},{18,... | collective-permute-start | bytes 786440 | tf_op jit(solution)/shard_map/ppermute | solution.py:343
  92.1 10.1 %collective-permute-start.27 = (f32[256,256]{1,0:T(8,128)S(1)}, f32[256,256]{1,0:T(8,128)S(1)}, u32[]{:S(2)}, u32[]{:S(2)}) collective-permute-start(f32[256,256]{1,0:T(8,128)S(1)} %get-tuple-element.174), channel_id=1, source_target_pairs={{0,6},{2,4},{4,2},{6,0},{8,14},{10,12},{12,10},{14,8},{16,22},{18,... | collective-permute-start | bytes 786440 | tf_op jit(solution)/shard_map/ppermute | solution.py:343
  97.5 11.1 %collective-permute-start.24 = (f32[1,3,64,256]{3,2,1,0:T(8,128)S(1)}, f32[1,3,64,256]{3,2,1,0:T(8,128)S(1)}, u32[]{:S(2)}, u32[]{:S(2)}) collective-permute-start(f32[1,3,64,256]{3,2,1,0:T(8,128)S(1)} %add_add_fusion.refs_11_.refs_0_), channel_id=1, source_target_pairs={{0,16},{2,18},{4,20},{6,22},{8,24},{10,26},{12,28},{14,30},{16,0},... | collective-permute-start | bytes 589832 | tf_op jit(solution)/shard_map/ppermute | solution.py:343
  98.9 9.9 %collective-permute-start.23 = (f32[1,3,64,256]{3,2,1,0:T(8,128)S(1)}, f32[1,3,64,256]{3,2,1,0:T(8,128)S(1)}, u32[]{:S(2)}, u32[]{:S(2)}) collective-permute-start(f32[1,3,64,256]{3,2,1,0:T(8,128)S(1)} %add_add_fusion.refs_11_.refs_0_), channel_id=1, source_target_pairs={{0,8},{2,10},{4,12},{6,14},{8,0},{10,2},{12,4},{14,6},{16,24},{18,... | collective-permute-start | bytes 589832 | tf_op jit(solution)/shard_map/ppermute | solution.py:343
  108.8 6.6 %collective-permute-start.28 = (f32[1,3,64,256]{3,2,1,0:T(8,128)S(1)}, f32[1,3,64,256]{3,2,1,0:T(8,128)S(1)}, u32[]{:S(2)}, u32[]{:S(2)}) collective-permute-start(f32[1,3,64,256]{3,2,1,0:T(8,128)S(1)} %collective-permute-done.24.refs_13_), channel_id=1, source_target_pairs={{0,8},{2,10},{4,12},{6,14},{8,0},{10,2},{12,4},{14,6},{16,24},{18,... | collective-permute-start | bytes 589832 | tf_op jit(solution)/shard_map/ppermute | solution.py:343
  118.5 30.6 %collective-permute-start.29 = (f32[2,256,256]{2,1,0:T(8,128)S(1)}, f32[2,256,256]{2,1,0:T(8,128)S(1)}, u32[]{:S(2)}, u32[]{:S(2)}) collective-permute-start(f32[2,256,256]{2,1,0:T(8,128)S(1)} %get-tuple-element.208), channel_id=1, source_target_pairs={{0,2},{2,0},{4,6},{6,4},{8,10},{10,8},{12,14},{14,12},{16,18},{18,... | collective-permute-start | bytes 1572872 | tf_op jit(solution)/shard_map/ppermute | solution.py:343
  118.8 30.4 %collective-permute-start.30 = (f32[2,256,256]{2,1,0:T(8,128)S(1)}, f32[2,256,256]{2,1,0:T(8,128)S(1)}, u32[]{:S(2)}, u32[]{:S(2)}) collective-permute-start(f32[2,256,256]{2,1,0:T(8,128)S(1)} %get-tuple-element.209), channel_id=1, source_target_pairs={{0,4},{2,6},{4,0},{6,2},{8,12},{10,14},{12,8},{14,10},{16,20},{18,... | collective-permute-start | bytes 1572872 | tf_op jit(solution)/shard_map/ppermute | solution.py:343
  118.8 30.3 %collective-permute-start.31 = (f32[2,256,256]{2,1,0:T(8,128)S(1)}, f32[2,256,256]{2,1,0:T(8,128)S(1)}, u32[]{:S(2)}, u32[]{:S(2)}) collective-permute-start(f32[2,256,256]{2,1,0:T(8,128)S(1)} %get-tuple-element.210), channel_id=1, source_target_pairs={{0,6},{2,4},{4,2},{6,0},{8,14},{10,12},{12,10},{14,8},{16,22},{18,... | collective-permute-start | bytes 1572872 | tf_op jit(solution)/shard_map/ppermute | solution.py:343
  122.1 7.5 %collective-permute-start.33 = (f32[1,3,64,256]{3,2,1,0:T(8,128)S(1)}, f32[1,3,64,256]{3,2,1,0:T(8,128)S(1)}, u32[]{:S(2)}, u32[]{:S(2)}) collective-permute-start(f32[1,3,64,256]{3,2,1,0:T(8,128)S(1)} %get-tuple-element.214), channel_id=1, source_target_pairs={{0,8},{2,10},{4,12},{6,14},{8,0},{10,2},{12,4},{14,6},{16,24},{18,... | collective-permute-start | bytes 589832 | tf_op jit(solution)/shard_map/ppermute | solution.py:343
  122.3 10.9 %collective-permute-start.32 = (f32[1,3,64,256]{3,2,1,0:T(8,128)S(1)}, f32[1,3,64,256]{3,2,1,0:T(8,128)S(1)}, u32[]{:S(2)}, u32[]{:S(2)}) collective-permute-start(f32[1,3,64,256]{3,2,1,0:T(8,128)S(1)} %get-tuple-element.212), channel_id=1, source_target_pairs={{0,8},{2,10},{4,12},{6,14},{8,0},{10,2},{12,4},{14,6},{16,24},{18,... | collective-permute-start | bytes 589832 | tf_op jit(solution)/shard_map/ppermute | solution.py:343
  129.6 8.7 %collective-permute-start.34 = (f32[1,3,64,256]{3,2,1,0:T(8,128)S(1)}, f32[1,3,64,256]{3,2,1,0:T(8,128)S(1)}, u32[]{:S(2)}, u32[]{:S(2)}) collective-permute-start(f32[1,3,64,256]{3,2,1,0:T(8,128)S(1)} %add.40), channel_id=1, source_target_pairs={{0,16},{2,18},{4,20},{6,22},{8,24},{10,26},{12,28},{14,30},{16,0},... | collective-permute-start | bytes 589832 | tf_op jit(solution)/shard_map/ppermute | solution.py:343
  138.9 5.2 %collective-permute-start.35 = (f32[1,3,16,256]{3,2,1,0:T(8,128)S(1)}, f32[1,3,16,256]{3,2,1,0:T(8,128)S(1)}, u32[]{:S(2)}, u32[]{:S(2)}) collective-permute-start(f32[1,3,16,256]{3,2,1,0:T(8,128)S(1)} %get-tuple-element.216), channel_id=1, source_target_pairs={{0,2},{2,0},{4,6},{6,4},{8,10},{10,8},{12,14},{14,12},{16,18},{18,... | collective-permute-start | bytes 147464 | tf_op jit(solution)/shard_map/ppermute | solution.py:343
  139.3 4.9 %collective-permute-start.36 = (f32[1,3,16,256]{3,2,1,0:T(8,128)S(1)}, f32[1,3,16,256]{3,2,1,0:T(8,128)S(1)}, u32[]{:S(2)}, u32[]{:S(2)}) collective-permute-start(f32[1,3,16,256]{3,2,1,0:T(8,128)S(1)} %get-tuple-element.217), channel_id=1, source_target_pairs={{0,4},{2,6},{4,0},{6,2},{8,12},{10,14},{12,8},{14,10},{16,20},{18,... | collective-permute-start | bytes 147464 | tf_op jit(solution)/shard_map/ppermute | solution.py:343
  144.2 5.0 %collective-permute-start.37 = (f32[1,3,16,256]{3,2,1,0:T(8,128)S(1)}, f32[1,3,16,256]{3,2,1,0:T(8,128)S(1)}, u32[]{:S(2)}, u32[]{:S(2)}) collective-permute-start(f32[1,3,16,256]{3,2,1,0:T(8,128)S(1)} %get-tuple-element.218), channel_id=1, source_target_pairs={{0,6},{2,4},{4,2},{6,0},{8,14},{10,12},{12,10},{14,8},{16,22},{18,... | collective-permute-start | bytes 147464 | tf_op jit(solution)/shard_map/ppermute | solution.py:343

commit v11 on v10

--- a/solution.py
+++ b/solution.py
@@ -11,7 +11,7 @@
 F32 = jnp.float32
 BF16 = jnp.bfloat16
 LANES = 128
-VMEM_LIMIT = 24 * 1024 * 1024
+MIB = 1024 * 1024
 
 
 def mm(a, b):
@@ -26,7 +26,7 @@
     return lax.dot_general(a, b, (((0,), (0,)), ((), ())), preferred_element_type=F32)
 
 
-def call(body, out_shape, scratch, flops, *args, final=False):
+def call(body, out_shape, scratch, flops, *args, final=False, mib=16):
     smem = pl.BlockSpec(memory_space=pltpu.SMEM)
     vmem = pl.BlockSpec(memory_space=pltpu.VMEM)
     size = sum(a.size * a.dtype.itemsize for a in args)
@@ -37,7 +37,7 @@
         in_specs=[smem if a.dtype == jnp.int32 else vmem for a in args],
         out_specs=[vmem] * len(out_shape),
         scratch_shapes=scratch,
-        compiler_params=pltpu.CompilerParams(vmem_limit_bytes=VMEM_LIMIT),
+        compiler_params=pltpu.CompilerParams(vmem_limit_bytes=mib * MIB),
         cost_estimate=pl.CostEstimate(flops=flops, bytes_accessed=size, transcendentals=0),
     )(*args)
 
@@ -65,16 +65,16 @@
     outs, scratch = rest[:groups], rest[groups]
     tokens, heads, width = x.shape
     put_rows(scratch, x[...].astype(F32).reshape(tokens * heads, width))
-    for step in range(groups):
-        outs[step][...] = take_head(scratch, place[0] ^ step, tokens, heads)
+    for step, out in enumerate(outs):
+        out[...] = take_head(scratch, place[0] ^ step, tokens, heads).astype(out.dtype)
 
 
 def split_scaled_kernel(groups, place, x, r, *rest):
     outs = rest[:groups]
     split_kernel(groups, place, x, *rest)
     for step in range(groups):
-        scaled = outs[step][...] * rate_column(r, place[0] ^ step)
-        outs[step][...] = scaled.astype(BF16).astype(F32)
+        scaled = outs[step][...].astype(F32) * rate_column(r, place[0] ^ step)
+        outs[step][...] = scaled.astype(BF16).astype(outs[step].dtype)
 
 
 def packing(groups):
@@ -358,14 +358,14 @@
         even = [move(p + v, "ctx", r * unit) for p, v, r in zip(outs[1:], via, evens)]
         return [outs[-1]] + first + even
 
-    def gather(part, count, unit, beside):
+    def gather(part, count, unit, beside=()):
         got = [part] * count
         evens = range(2, count, 2)
         for r in evens:
             got[r] = move(part, "ctx", r * unit)
         if count > 1:
             got[1] = move(part, "ctx", unit)
-        got, beside = after(got, beside)
+            got[1], beside = after(got[1], beside)
         for r in evens:
             got[r + 1] = move(got[r], "ctx", unit)
         return got, beside
@@ -384,7 +384,9 @@
     square = pltpu.VMEM((3, hidden, width), F32)
 
     def split(body, *args):
-        return call(functools.partial(body, groups), pieces, [scratch], 16 * flops, place, *args)
+        outs = [shape(tokens, width, dtype=BF16)] + pieces[1:]
+        body = functools.partial(body, groups)
+        return call(body, outs, [scratch], 16 * flops, place, *args, mib=8)
 
     k_in = in_plane(split(split_kernel, keys[0]))
     s_in = in_plane(split(split_scaled_kernel, values[0], rates[0]))
@@ -396,7 +398,7 @@
     *q_out, scale_row = call(
         functools.partial(split_apply_kernel, groups),
         [kept(len(members)) for members in packing(groups)] + [shape(8, width)],
-        [scratch], flops // 8, place, queries[0], cotangent[0], gain, own_scale,
+        [scratch], flops // 8, place, queries[0], cotangent[0], gain, own_scale, mib=8,
     )
     k_in, s_in, q_out = after(k_in, s_in, q_out)
     q_in = q_out[:1] + [move(q_out[i], "ctx", i) for i in range(1, len(q_out))]
@@ -431,17 +433,18 @@
         *early, *own,
     )
     part = functools.reduce(jnp.add, scatter(out[groups:], depth, groups))
-    parts, q_back = gather(part, depth, groups, in_plane(out[:groups]))
+    parts, _ = gather(part, depth, groups)
+    q_back = in_plane(out[:groups])
     (grad_q,) = call(
         functools.partial(join_query_kernel, groups), [joined], [scratch], flops // 16,
-        place, *q_back, final=True,
+        place, *q_back, final=True, mib=8,
     )
     parts, grad_q, saved = after(parts, grad_q, saved)
     rows = hidden // depth
     out = call(
         functools.partial(update_back_kernel, groups, depth, scale),
         [shape(2, tokens, width)] * groups + slices, [square] * 2, 12 * flops,
-        place, *early, *saved, *parts, *own,
+        place, *early, *saved, *parts, *own, mib=24,
     )
     back = in_plane(out[:groups])
     ends = scatter(out[groups:], depth, groups, one_by_one=False)
@@ -449,12 +452,12 @@
     sent = call(
         functools.partial(rows_kernel, groups),
         [shape(1, 3, own_rows, width)] * groups,
-        [pltpu.VMEM((3, rows, width), F32)], flops // 100, place, part, *ends,
+        [pltpu.VMEM((3, rows, width), F32)], flops // 100, place, part, *ends, mib=8,
     )
     grad_k, grad_v, *grads = call(
         functools.partial(join_update_kernel, groups),
         [joined] * 2 + [shape(heads, own_rows, width)] * 3, [scratch] * 2, flops // 8,
-        place, rates[0], *back, *in_plane(sent), final=True,
+        place, rates[0], *back, *in_plane(sent), final=True, mib=8,
     )
     if lax.axis_size("batch") > 1:
         grads = [lax.psum_scatter(x, "batch", scatter_dimension=1, tiled=True) for x in grads]

time: 152 us -> 150 us (0.987)
  starting transfers between devices: 51.7 us -> 45.1 us
  waiting for transfers between devices: 72.6 us -> 78 us
    ppermute x38, starting transfers between devices: 51.7 us -> 45.1 us  [move(): lax.ppermute(x, axis, [(c, c ^ step) for c in range(lax.axis_size(axis))])]
    ppermute x38, waiting for transfers between devices: 72.6 us -> 78 us  [move(): lax.ppermute(x, axis, [(c, c ^ step) for c in range(lax.axis_size(axis))])]
    unnamed x24 -> x20, local copies, waits for them, and re-layouts: 3.32 us -> 2.55 us
  transfers between devices with their start and end apart: 38 -> 38, of which waited for: 23 -> 21; matrix products, arithmetic and copies ran while one was open for 1% -> 1% of each run, Pallas kernels for 5% -> 5%
where the time goes in v11:
time: 150 us; the launch traced here: 149 us
  waiting for transfers between devices  78 us (52%)
  starting transfers between devices  45.1 us (30%)
  Pallas kernels  20.8 us (14%)
  local copies, waits for them, and re-layouts  4.3 us (3%)
    ppermute x38, waiting for transfers between devices, move(): lax.ppermute(x, axis, [(c, c ^ step) for c in range(lax.axis_size(axis))])  78 us
    ppermute x38, starting transfers between devices, move(): lax.ppermute(x, axis, [(c, c ^ step) for c in range(lax.axis_size(axis))])  45.1 us
    pallas_call x11, Pallas kernels, call(): pl.pallas_call(body, out_shape=out_shape if final else [pltpu.VMEM(o.shap...  20.8 us
  transfers between devices with their start and end apart: 38, of which 21 were waited for; matrix products, arithmetic and copies ran while one was open for 1% of the time, Pallas kernels for 5%

profile of v11, /device:TPU:0, one launch (start us, length us, event | category | flops | bytes accessed | tf_op | source)
XLA Modules:
  0.0 149.3 jit_solution(1592148458550322606)
XLA Ops:
  0.7 1.1 copy-done.5
  1.8 1.7 %shard_map.146 = (bf16[256,256]{1,0:T(8,128)(2,1)S(1)}, f32[256,256]{1,0:T(8,128)S(1)}, f32[256,256]{1,0:T(8,128)}, f32[256,256]{1,0:T(8,128)}) custom-call(s32[2]{0:T(128)S(1)} %pad_add_fusion.place, bf16[256,4,256]{2,1,0:T(4,128)(2,1)S(1)} %bitcast.25), custom_call_target="tpu_custom_call" | custom-call | flops 2147483648 | bytes 1441800 | tf_op jit(solution)/shard_map/pallas_call | solution.py:34
  3.5 2.9 %collective-permute-start = (f32[256,256]{1,0:T(8,128)S(1)}, f32[256,256]{1,0:T(8,128)S(1)}, u32[]{:S(2)}, u32[]{:S(2)}) collective-permute-start(f32[256,256]{1,0:T(8,128)S(1)} %get-tuple-element.108), channel_id=1, source_target_pairs={{0,2},{2,0},{4,6},{6,4},{8,10},{10,8},{12,14},{14,12},{16,18},{18,... | collective-permute-start | bytes 786440 | tf_op jit(solution)/shard_map/ppermute | solution.py:343
  6.5 1.5 %collective-permute-start.1 = (f32[256,256]{1,0:T(8,128)}, f32[256,256]{1,0:T(8,128)S(1)}, u32[]{:S(2)}, u32[]{:S(2)}) collective-permute-start(f32[256,256]{1,0:T(8,128)} %get-tuple-element.109), channel_id=1, source_target_pairs={{0,4},{2,6},{4,0},{6,2},{8,12},{10,14},{12,8},{14,10},{16,20},{18,... | collective-permute-start | bytes 786440 | tf_op jit(solution)/shard_map/ppermute | solution.py:343
  8.0 1.9 %shard_map.147 = (bf16[256,256]{1,0:T(8,128)(2,1)S(1)}, f32[256,256]{1,0:T(8,128)}, f32[256,256]{1,0:T(8,128)}, f32[256,256]{1,0:T(8,128)}) custom-call(s32[2]{0:T(128)S(1)} %pad_add_fusion.place, bf16[256,4,256]{2,1,0:T(4,128)(2,1)S(1)} %bitcast.26, f32[4,256]{1,0:T(4,128)S(1)} %bitcast.23), custom_call_target="tpu_custom_call" | custom-call | flops 2147483648 | bytes 1445896 | tf_op jit(solution)/shard_map/pallas_call | solution.py:34
  9.9 0.6 copy-done.7
  10.6 1.9 %collective-permute-start.3 = (f32[256,256]{1,0:T(8,128)}, f32[256,256]{1,0:T(8,128)S(1)}, u32[]{:S(2)}, u32[]{:S(2)}) collective-permute-start(f32[256,256]{1,0:T(8,128)} %get-tuple-element.112), channel_id=1, source_target_pairs={{0,2},{2,0},{4,6},{6,4},{8,10},{10,8},{12,14},{14,12},{16,18},{18,... | collective-permute-start | bytes 786440 | tf_op jit(solution)/shard_map/ppermute | solution.py:343
  12.5 1.5 %collective-permute-start.4 = (f32[256,256]{1,0:T(8,128)}, f32[256,256]{1,0:T(8,128)S(1)}, u32[]{:S(2)}, u32[]{:S(2)}) collective-permute-start(f32[256,256]{1,0:T(8,128)} %get-tuple-element.113), channel_id=1, source_target_pairs={{0,4},{2,6},{4,0},{6,2},{8,12},{10,14},{12,8},{14,10},{16,20},{18,... | collective-permute-start | bytes 786440 | tf_op jit(solution)/shard_map/ppermute | solution.py:343
  14.0 2.6 %collective-permute-start.5 = (f32[256,256]{1,0:T(8,128)}, f32[256,256]{1,0:T(8,128)}, u32[]{:S(2)}, u32[]{:S(2)}) collective-permute-start(f32[256,256]{1,0:T(8,128)} %get-tuple-element.114), channel_id=1, source_target_pairs={{0,6},{2,4},{4,2},{6,0},{8,14},{10,12},{12,10},{14,8},{16,22},{18,... | collective-permute-start | bytes 786440 | tf_op jit(solution)/shard_map/ppermute | solution.py:343
  16.6 0.7 copy-done.9
  17.3 0.6 dynamic_slice.14
  18.0 1.9 %shard_map.145 = (f32[2,256,256]{2,1,0:T(8,128)S(1)}, f32[3,256,256]{2,1,0:T(8,128)S(1)}, f32[3,256,256]{2,1,0:T(8,128)S(1)}, f32[8,256]{1,0:T(8,128)S(1)}) custom-call(s32[2]{0:T(128)S(1)} %pad_add_fusion.place, bf16[256,4,256]{2,1,0:T(4,128)(2,1)S(1)} %bitcast.21, bf16[256,4,256]{2,1,0:T(4,128)(2,1)S(1)} %bitcast.22, f32[4,256]{1,0:T(4,128)S(1)} %copy-done.3, ...), custom_call_target="tpu_custom_call" | custom-call | flops 16777216 | bytes 3158028 | tf_op jit(solution)/shard_map/pallas_call | solution.py:34
  20.0 1.1 dynamic-slice_bitcast_fusion
  21.1 3.8 %collective-permute-done.3.refs_5_ = f32[256,256]{1,0:T(8,128)S(1)} collective-permute-done((f32[256,256]{1,0:T(8,128)}, f32[256,256]{1,0:T(8,128)S(1)}, u32[]{:S(2)}, u32[]{:S(2)}) %collective-permute-start.3) | collective-permute-done | bytes 262176 | tf_op jit(solution)/shard_map/ppermute | solution.py:343
  24.9 6.4 %collective-permute-done.4.refs_6_ = f32[256,256]{1,0:T(8,128)S(1)} collective-permute-done((f32[256,256]{1,0:T(8,128)}, f32[256,256]{1,0:T(8,128)S(1)}, u32[]{:S(2)}, u32[]{:S(2)}) %collective-permute-start.4) | collective-permute-done | bytes 262176 | tf_op jit(solution)/shard_map/ppermute | solution.py:343
  31.3 2.6 %shard_map.148 = (bf16[4,256,256]{2,1,0:T(8,128)(2,1)S(1)}, bf16[4,256,256]{2,1,0:T(8,128)(2,1)S(1)}, f32[1,3,64,256]{3,2,1,0:T(8,128)S(1)}, f32[1,3,64,256]{3,2...) custom-call(s32[2]{0:T(128)S(1)} %pad_add_fusion.place, ...), custom_call_target="tpu_custom_call" | custom-call | flops 805306368 | bytes 4456456 | tf_op jit(solution)/shard_map/pallas_call | solution.py:34
  33.9 1.6 %collective-permute-start.6 = (f32[1,3,64,256]{3,2,1,0:T(8,128)S(1)}, f32[1,3,64,256]{3,2,1,0:T(8,128)S(1)}, u32[]{:S(2)}, u32[]{:S(2)}) collective-permute-start(f32[1,3,64,256]{3,2,1,0:T(8,128)S(1)} %get-tuple-element.128), channel_id=1, source_target_pairs={{0,8},{2,10},{4,12},{6,14},{8,0},{10,2},{12,4},{14,6},{16,24},{18,... | collective-permute-start | bytes 589832 | tf_op jit(solution)/shard_map/ppermute | solution.py:343
  35.6 1.2 collective-permute-start.10
  36.7 0.9 collective-permute-start.11
  37.6 2.0 %collective-permute-done.6 = f32[1,3,64,256]{3,2,1,0:T(8,128)S(1)} collective-permute-done((f32[1,3,64,256]{3,2,1,0:T(8,128)S(1)}, f32[1,3,64,256]{3,2,1,0:T(8,128)S(1)}, u32[]{:S(2)}, u32[]{:S(2)}) %collective-permute-start.6) | collective-permute-done | bytes 196640 | tf_op jit(solution)/shard_map/ppermute | solution.py:343
  39.7 2.7 %collective-permute-start.8 = (f32[1,3,64,256]{3,2,1,0:T(8,128)S(1)}, f32[1,3,64,256]{3,2,1,0:T(8,128)S(1)}, u32[]{:S(2)}, u32[]{:S(2)}) collective-permute-start(f32[1,3,64,256]{3,2,1,0:T(8,128)S(1)} %add.34), channel_id=1, source_target_pairs={{0,16},{2,18},{4,20},{6,22},{8,24},{10,26},{12,28},{14,30},{16,0},... | collective-permute-start | bytes 589832 | tf_op jit(solution)/shard_map/ppermute | solution.py:343
  42.3 1.6 %collective-permute-start.7 = (f32[1,3,64,256]{3,2,1,0:T(8,128)S(1)}, f32[1,3,64,256]{3,2,1,0:T(8,128)S(1)}, u32[]{:S(2)}, u32[]{:S(2)}) collective-permute-start(f32[1,3,64,256]{3,2,1,0:T(8,128)S(1)} %get-tuple-element.130), channel_id=1, source_target_pairs={{0,8},{2,10},{4,12},{6,14},{8,0},{10,2},{12,4},{14,6},{16,24},{18,... | collective-permute-start | bytes 589832 | tf_op jit(solution)/shard_map/ppermute | solution.py:343
  43.9 5.4 %collective-permute-done.8 = f32[1,3,64,256]{3,2,1,0:T(8,128)S(1)} collective-permute-done((f32[1,3,64,256]{3,2,1,0:T(8,128)S(1)}, f32[1,3,64,256]{3,2,1,0:T(8,128)S(1)}, u32[]{:S(2)}, u32[]{:S(2)}) %collective-permute-start.8) | collective-permute-done | bytes 196640 | tf_op jit(solution)/shard_map/ppermute | solution.py:343
  49.7 1.4 collective-permute-start.9
  51.1 2.3 %collective-permute-start.14 = (f32[1,3,64,256]{3,2,1,0:T(8,128)S(1)}, f32[1,3,64,256]{3,2,1,0:T(8,128)S(1)}, u32[]{:S(2)}, u32[]{:S(2)}) collective-permute-start(f32[1,3,64,256]{3,2,1,0:T(8,128)S(1)} %add_add_fusion.1.refs_5_), channel_id=1, source_target_pairs={{0,16},{2,18},{4,20},{6,22},{8,24},{10,26},{12,28},{14,30},{16,0},... | collective-permute-start | bytes 589832 | tf_op jit(solution)/shard_map/ppermute | solution.py:343
  53.4 4.6 %collective-permute-done.9.refs_6_ = f32[1,3,64,256]{3,2,1,0:T(8,128)S(1)} collective-permute-done((f32[1,3,64,256]{3,2,1,0:T(8,128)S(1)}, f32[1,3,64,256]{3,2,1,0:T(8,128)S(1)}, u32[]{:S(2)}, u32[]{:S(2)}) %collective-permute-start.9) | collective-permute-done | bytes 196640 | tf_op jit(solution)/shard_map/ppermute | solution.py:343
  58.1 2.8 %collective-permute-start.13 = (f32[256,256]{1,0:T(8,128)S(1)}, f32[256,256]{1,0:T(8,128)S(1)}, u32[]{:S(2)}, u32[]{:S(2)}) collective-permute-start(f32[256,256]{1,0:T(8,128)S(1)} %slice_bitcast_fusion), channel_id=1, source_target_pairs={{0,2},{2,0},{4,6},{6,4},{8,10},{10,8},{12,14},{14,12},{16,18},{18,... | collective-permute-start | bytes 786440 | tf_op jit(solution)/shard_map/ppermute | solution.py:343
  60.8 3.0 %collective-permute-start.12 = (f32[256,256]{1,0:T(8,128)S(1)}, f32[256,256]{1,0:T(8,128)S(1)}, u32[]{:S(2)}, u32[]{:S(2)}) collective-permute-start(f32[256,256]{1,0:T(8,128)S(1)} %slice_bitcast_fusion.1), channel_id=1, source_target_pairs={{0,4},{2,6},{4,0},{6,2},{8,12},{10,14},{12,8},{14,10},{16,20},{18,... | collective-permute-start | bytes 786440 | tf_op jit(solution)/shard_map/ppermute | solution.py:343
  63.8 5.7 %collective-permute-done.15.refs_8_ = f32[1,3,64,256]{3,2,1,0:T(8,128)S(1)} collective-permute-done((f32[1,3,64,256]{3,2,1,0:T(8,128)S(1)}, f32[1,3,64,256]{3,2,1,0:T(8,128)S(1)}, u32[]{:S(2)}, u32[]{:S(2)}) %collective-permute-start.15) | collective-permute-done | bytes 196640 | tf_op jit(solution)/shard_map/ppermute | solution.py:343
  69.5 1.8 %shard_map.149 = (f32[4,256,256]{2,1,0:T(8,128)S(1)}, f32[4,256,256]{2,1,0:T(8,128)S(1)}, bf16[4,256,256]{2,1,0:T(8,128)(2,1)S(1)}, f32[4,256,256]{2,1,0:T(8,128...) custom-call(s32[2]{0:T(128)S(1)} %pad_add_fusion.place, f32[8,256]{1,0:T(8,128)S(1)} %get-tuple-element.106.scale_row, ...), custom_call_target="tpu_custom_call" | custom-call | flops 402653184 | bytes 7487496 | tf_op jit(solution)/shard_map/pallas_call | solution.py:34
  71.3 1.2 collective-permute-done.16
  72.5 2.1 %collective-permute-start.19 = (f32[2,4,256]{2,1,0:T(4,128)S(1)}, f32[2,4,256]{2,1,0:T(4,128)S(1)}, u32[]{:S(2)}, u32[]{:S(2)}) collective-permute-start(f32[2,4,256]{2,1,0:T(4,128)S(1)} %add.36.refs_5_), channel_id=1, source_target_pairs={{0,6},{2,4},{4,2},{6,0},{8,14},{10,12},{12,10},{14,8},{16,22},{18,... | collective-permute-start | bytes 24584 | tf_op jit(solution)/shard_map/ppermute | solution.py:343
  74.6 1.3 collective-permute-start.18
  76.0 1.1 collective-permute-done.19.refs_8_
  77.0 1.2 collective-permute-done.18.refs_7_
  78.2 1.3 collective-permute-done.17.refs_6_
  79.6 2.1 %shard_map.150 = (f32[256,256]{1,0:T(8,128)S(1)}, f32[256,256]{1,0:T(8,128)S(1)}, f32[256,256]{1,0:T(8,128)S(1)}, f32[256,256]{1,0:T(8,128)S(1)}, f32[1,3,64,256...) custom-call(s32[2]{0:T(128)S(1)} %pad_add_fusion.place, ...), custom_call_target="tpu_custom_call" | custom-call | flops 805306368 | bytes 8560648 | tf_op jit(solution)/shard_map/pallas_call | solution.py:34
  81.7 5.7 %collective-permute-done.20 = f32[1,3,64,256]{3,2,1,0:T(8,128)S(1)} collective-permute-done((f32[1,3,64,256]{3,2,1,0:T(8,128)S(1)}, f32[1,3,64,256]{3,2,1,0:T(8,128)S(1)}, u32[]{:S(2)}, u32[]{:S(2)}) %collective-permute-start.20) | collective-permute-done | bytes 196640 | tf_op jit(solution)/shard_map/ppermute | solution.py:343
  87.5 0.6 collective-permute-start.21
  88.1 8.9 %collective-permute-done.22 = f32[1,3,64,256]{3,2,1,0:T(8,128)S(1)} collective-permute-done((f32[1,3,64,256]{3,2,1,0:T(8,128)S(1)}, f32[1,3,64,256]{3,2,1,0:T(8,128)S(1)}, u32[]{:S(2)}, u32[]{:S(2)}) %collective-permute-start.22) | collective-permute-done | bytes 196640 | tf_op jit(solution)/shard_map/ppermute | solution.py:343
  97.1 0.8 collective-permute-start.24
  97.8 0.8 collective-permute-start.26
  98.6 0.6 collective-permute-start.27
  99.2 2.1 %collective-permute-start.28 = (f32[256,256]{1,0:T(8,128)S(1)}, f32[256,256]{1,0:T(8,128)S(1)}, u32[]{:S(2)}, u32[]{:S(2)}) collective-permute-start(f32[256,256]{1,0:T(8,128)S(1)} %get-tuple-element.163), channel_id=1, source_target_pairs={{0,6},{2,4},{4,2},{6,0},{8,14},{10,12},{12,10},{14,8},{16,22},{18,... | collective-permute-start | bytes 786440 | tf_op jit(solution)/shard_map/ppermute | solution.py:343
  101.3 0.8 collective-permute-start.23
  102.1 3.9 %collective-permute-done.24.refs_13_ = f32[1,3,64,256]{3,2,1,0:T(8,128)S(1)} collective-permute-done((f32[1,3,64,256]{3,2,1,0:T(8,128)S(1)}, f32[1,3,64,256]{3,2,1,0:T(8,128)S(1)}, u32[]{:S(2)}, u32[]{:S(2)}) %collective-permute-start.24) | collective-permute-done | bytes 196640 | tf_op jit(solution)/shard_map/ppermute | solution.py:343
  106.1 1.0 shard_map.152
  107.1 2.9 %collective-permute-done.27.refs_2_ = f32[256,256]{1,0:T(8,128)S(1)} collective-permute-done((f32[256,256]{1,0:T(8,128)S(1)}, f32[256,256]{1,0:T(8,128)S(1)}, u32[]{:S(2)}, u32[]{:S(2)}) %collective-permute-start.27) | collective-permute-done | bytes 262176 | tf_op jit(solution)/shard_map/ppermute | solution.py:343
  110.1 1.7 %shard_map.151 = bf16[256,4,256]{2,1,0:T(4,128)(2,1)} custom-call(s32[2]{0:T(128)S(1)} %pad_add_fusion.place, f32[256,256]{1,0:T(8,128)S(1)} %get-tuple-element.160.refs_0_, f32[256,256]{1,0:T(8,128)S(1)} %collective-permute-done.26.refs_1_, f32[256,256]{1,0:T(8,128)S(1)} %collective-permute-done.27.refs_2_, f32[256,256]{1,0:T(8,128)S(1)} %collective-permute-done.28.refs_3_), custom_call_target="tpu_custom_call" | custom-call | flops 8388608 | bytes 1572872 | tf_op jit(solution)/shard_map/pallas_call | solution.py:34
  111.8 1.3 collective-permute-done.25.refs_14_
  113.1 3.0 %shard_map.153 = (f32[2,256,256]{2,1,0:T(8,128)S(1)}, f32[2,256,256]{2,1,0:T(8,128)S(1)}, f32[2,256,256]{2,1,0:T(8,128)S(1)}, f32[2,256,256]{2,1,0:T(8,128)S(1)}...) custom-call(s32[2]{0:T(128)S(1)} %pad_add_fusion.place, ...), custom_call_target="tpu_custom_call" | custom-call | flops 1610612736 | bytes 13369352 | tf_op jit(solution)/shard_map/pallas_call | solution.py:34
  116.1 0.4 collective-permute-start.29
  116.8 2.9 %collective-permute-start.31 = (f32[2,256,256]{2,1,0:T(8,128)S(1)}, f32[2,256,256]{2,1,0:T(8,128)S(1)}, u32[]{:S(2)}, u32[]{:S(2)}) collective-permute-start(f32[2,256,256]{2,1,0:T(8,128)S(1)} %get-tuple-element.192), channel_id=1, source_target_pairs={{0,6},{2,4},{4,2},{6,0},{8,14},{10,12},{12,10},{14,8},{16,22},{18,... | collective-permute-start | bytes 1572872 | tf_op jit(solution)/shard_map/ppermute | solution.py:343
  119.7 2.0 %collective-permute-start.32 = (f32[1,3,64,256]{3,2,1,0:T(8,128)S(1)}, f32[1,3,64,256]{3,2,1,0:T(8,128)S(1)}, u32[]{:S(2)}, u32[]{:S(2)}) collective-permute-start(f32[1,3,64,256]{3,2,1,0:T(8,128)S(1)} %get-tuple-element.194), channel_id=1, source_target_pairs={{0,8},{2,10},{4,12},{6,14},{8,0},{10,2},{12,4},{14,6},{16,24},{18,... | collective-permute-start | bytes 589832 | tf_op jit(solution)/shard_map/ppermute | solution.py:343
  121.7 5.7 %collective-permute-done.33 = f32[1,3,64,256]{3,2,1,0:T(8,128)S(1)} collective-permute-done((f32[1,3,64,256]{3,2,1,0:T(8,128)S(1)}, f32[1,3,64,256]{3,2,1,0:T(8,128)S(1)}, u32[]{:S(2)}, u32[]{:S(2)}) %collective-permute-start.33) | collective-permute-done | bytes 196640 | tf_op jit(solution)/shard_map/ppermute | solution.py:343
  127.5 1.3 collective-permute-start.34
  128.8 2.2 %collective-permute-done.32.refs_2_ = f32[1,3,64,256]{3,2,1,0:T(8,128)S(1)} collective-permute-done((f32[1,3,64,256]{3,2,1,0:T(8,128)S(1)}, f32[1,3,64,256]{3,2,1,0:T(8,128)S(1)}, u32[]{:S(2)}, u32[]{:S(2)}) %collective-permute-start.32) | collective-permute-done | bytes 196640 | tf_op jit(solution)/shard_map/ppermute | solution.py:343
  131.0 4.7 %collective-permute-done.34.refs_3_ = f32[1,3,64,256]{3,2,1,0:T(8,128)S(1)} collective-permute-done((f32[1,3,64,256]{3,2,1,0:T(8,128)S(1)}, f32[1,3,64,256]{3,2,1,0:T(8,128)S(1)}, u32[]{:S(2)}, u32[]{:S(2)}) %collective-permute-start.34) | collective-permute-done | bytes 196640 | tf_op jit(solution)/shard_map/ppermute | solution.py:343
  135.7 0.6 shard_map.154
  136.4 0.5 collective-permute-start.35
  136.9 0.5 collective-permute-start.36
  137.4 4.5 %collective-permute-done.35.refs_5_ = f32[1,3,16,256]{3,2,1,0:T(8,128)S(1)} collective-permute-done((f32[1,3,16,256]{3,2,1,0:T(8,128)S(1)}, f32[1,3,16,256]{3,2,1,0:T(8,128)S(1)}, u32[]{:S(2)}, u32[]{:S(2)}) %collective-permute-start.35) | collective-permute-done | bytes 49184 | tf_op jit(solution)/shard_map/ppermute | solution.py:343
  141.9 5.0 %collective-permute-done.37.refs_7_ = f32[1,3,16,256]{3,2,1,0:T(8,128)S(1)} collective-permute-done((f32[1,3,16,256]{3,2,1,0:T(8,128)S(1)}, f32[1,3,16,256]{3,2,1,0:T(8,128)S(1)}, u32[]{:S(2)}, u32[]{:S(2)}) %collective-permute-start.37) | collective-permute-done | bytes 49184 | tf_op jit(solution)/shard_map/ppermute | solution.py:343
  146.9 2.4 %shard_map.155 = (bf16[256,4,256]{2,1,0:T(4,128)(2,1)}, bf16[256,4,256]{2,1,0:T(4,128)(2,1)}, f32[4,16,256]{2,1,0:T(8,128)}, f32[4,16,256]{2,1,0:T(8,128)}, f32[4,16,256]{2,1,0:T(8,128)}) custom-call(s32[2]{0:T(128)S(1)} %pad_add_fusion.place, f32[4,256]{1,0:T(4,128)S(1)} %bitcast.24, f32[2,256,256]{2,1,0:T(8,128)S(1)} %get-tuple-element.189.refs_0_, ...), custom_call_target="tpu_custom_call" | custom-call | flops 16777216 | bytes 3543048 | tf_op jit(solution)/shard_map/pallas_call | solution.py:34
  (55 shorter events, 1.4 us)
Async XLA Ops:
  0.6 19.3 %copy-start = (f32[4,256,256]{2,1,0:T(8,128)S(1)}, f32[4,256,256]{2,1,0:T(8,128)}, u32[]{:S(2)}) copy-start(f32[4,256,256]{2,1,0:T(8,128)} %param.16) | copy-start | bytes 3145732
  0.7 1.1 copy-start.5
  1.8 6.2 %copy-start.6 = (bf16[1,256,4,256]{3,2,1,0:T(4,128)(2,1)S(1)}, bf16[1,256,4,256]{3,2,1,0:T(4,128)(2,1)}, u32[]{:S(2)}) copy-start(bf16[1,256,4,256]{3,2,1,0:T(4,128)(2,1)} %param.12) | copy-start | bytes 1572868
  3.5 4.5 %copy-start.4 = (f32[1,4,256]{2,1,0:T(4,128)S(1)}, f32[1,4,256]{2,1,0:T(4,128)}, u32[]{:S(2)}) copy-start(f32[1,4,256]{2,1,0:T(4,128)} %param.13) | copy-start | bytes 12292
  3.5 10.5 %collective-permute-start = (f32[256,256]{1,0:T(8,128)S(1)}, f32[256,256]{1,0:T(8,128)S(1)}, u32[]{:S(2)}, u32[]{:S(2)}) collective-permute-start(f32[256,256]{1,0:T(8,128)S(1)} %get-tuple-element.108), channel_id=1, source_target_pairs={{0,2},{2,0},{4,6},{6,4},{8,10},{10,8},{12,14},{14,12},{16,18},{18,... | collective-permute-start | bytes 786440 | tf_op jit(solution)/shard_map/ppermute | solution.py:343
  6.5 14.6 %collective-permute-start.1 = (f32[256,256]{1,0:T(8,128)}, f32[256,256]{1,0:T(8,128)S(1)}, u32[]{:S(2)}, u32[]{:S(2)}) collective-permute-start(f32[256,256]{1,0:T(8,128)} %get-tuple-element.109), channel_id=1, source_target_pairs={{0,4},{2,6},{4,0},{6,2},{8,12},{10,14},{12,8},{14,10},{16,20},{18,... | collective-permute-start | bytes 786440 | tf_op jit(solution)/shard_map/ppermute | solution.py:343
  8.0 13.1 %collective-permute-start.2 = (f32[256,256]{1,0:T(8,128)}, f32[256,256]{1,0:T(8,128)S(1)}, u32[]{:S(2)}, u32[]{:S(2)}) collective-permute-start(f32[256,256]{1,0:T(8,128)} %get-tuple-element.110), channel_id=1, source_target_pairs={{0,6},{2,4},{4,2},{6,0},{8,14},{10,12},{12,10},{14,8},{16,22},{18,... | collective-permute-start | bytes 786440 | tf_op jit(solution)/shard_map/ppermute | solution.py:343
  8.0 9.9 %copy-start.1 = (bf16[1,256,4,256]{3,2,1,0:T(4,128)(2,1)S(1)}, bf16[1,256,4,256]{3,2,1,0:T(4,128)(2,1)}, u32[]{:S(2)}) copy-start(bf16[1,256,4,256]{3,2,1,0:T(4,128)(2,1)} %param.10) | copy-start | bytes 1572868
  8.0 9.9 %copy-start.2 = (bf16[1,256,4,256]{3,2,1,0:T(4,128)(2,1)S(1)}, bf16[1,256,4,256]{3,2,1,0:T(4,128)(2,1)}, u32[]{:S(2)}) copy-start(bf16[1,256,4,256]{3,2,1,0:T(4,128)(2,1)} %param.19) | copy-start | bytes 1572868
  9.9 0.7 copy-start.7
  10.6 14.3 %collective-permute-start.3 = (f32[256,256]{1,0:T(8,128)}, f32[256,256]{1,0:T(8,128)S(1)}, u32[]{:S(2)}, u32[]{:S(2)}) collective-permute-start(f32[256,256]{1,0:T(8,128)} %get-tuple-element.112), channel_id=1, source_target_pairs={{0,2},{2,0},{4,6},{6,4},{8,10},{10,8},{12,14},{14,12},{16,18},{18,... | collective-permute-start | bytes 786440 | tf_op jit(solution)/shard_map/ppermute | solution.py:343
  12.5 18.8 %collective-permute-start.4 = (f32[256,256]{1,0:T(8,128)}, f32[256,256]{1,0:T(8,128)S(1)}, u32[]{:S(2)}, u32[]{:S(2)}) collective-permute-start(f32[256,256]{1,0:T(8,128)} %get-tuple-element.113), channel_id=1, source_target_pairs={{0,4},{2,6},{4,0},{6,2},{8,12},{10,14},{12,8},{14,10},{16,20},{18,... | collective-permute-start | bytes 786440 | tf_op jit(solution)/shard_map/ppermute | solution.py:343
  14.0 17.3 %collective-permute-start.5 = (f32[256,256]{1,0:T(8,128)}, f32[256,256]{1,0:T(8,128)}, u32[]{:S(2)}, u32[]{:S(2)}) collective-permute-start(f32[256,256]{1,0:T(8,128)} %get-tuple-element.114), channel_id=1, source_target_pairs={{0,6},{2,4},{4,2},{6,0},{8,14},{10,12},{12,10},{14,8},{16,22},{18,... | collective-permute-start | bytes 786440 | tf_op jit(solution)/shard_map/ppermute | solution.py:343
  16.6 0.7 copy-start.9
  17.3 0.7 copy-start.3
  20.0 11.4 %copy-start.8 = (bf16[256,256]{1,0:T(8,128)(2,1)S(1)}, bf16[256,256]{1,0:T(8,128)(2,1)}, u32[]{:S(2)}) copy-start(bf16[256,256]{1,0:T(8,128)(2,1)} %copy-done.7) | copy-start | bytes 393220
  33.9 5.7 %collective-permute-start.6 = (f32[1,3,64,256]{3,2,1,0:T(8,128)S(1)}, f32[1,3,64,256]{3,2,1,0:T(8,128)S(1)}, u32[]{:S(2)}, u32[]{:S(2)}) collective-permute-start(f32[1,3,64,256]{3,2,1,0:T(8,128)S(1)} %get-tuple-element.128), channel_id=1, source_target_pairs={{0,8},{2,10},{4,12},{6,14},{8,0},{10,2},{12,4},{14,6},{16,24},{18,... | collective-permute-start | bytes 589832 | tf_op jit(solution)/shard_map/ppermute | solution.py:343
  35.6 22.4 %collective-permute-start.10 = (f32[3,256,256]{2,1,0:T(8,128)S(1)}, f32[3,256,256]{2,1,0:T(8,128)S(1)}, u32[]{:S(2)}, u32[]{:S(2)}) collective-permute-start(f32[3,256,256]{2,1,0:T(8,128)S(1)} %get-tuple-element.133), channel_id=1, source_target_pairs={{0,2},{2,0},{4,6},{6,4},{8,10},{10,8},{12,14},{14,12},{16,18},{18,... | collective-permute-start | bytes 2359304 | tf_op jit(solution)/shard_map/ppermute | solution.py:343
  36.7 21.3 %collective-permute-start.11 = (f32[3,256,256]{2,1,0:T(8,128)S(1)}, f32[3,256,256]{2,1,0:T(8,128)S(1)}, u32[]{:S(2)}, u32[]{:S(2)}) collective-permute-start(f32[3,256,256]{2,1,0:T(8,128)S(1)} %get-tuple-element.134), channel_id=1, source_target_pairs={{0,4},{2,6},{4,0},{6,2},{8,12},{10,14},{12,8},{14,10},{16,20},{18,... | collective-permute-start | bytes 2359304 | tf_op jit(solution)/shard_map/ppermute | solution.py:343
  39.7 9.7 %collective-permute-start.8 = (f32[1,3,64,256]{3,2,1,0:T(8,128)S(1)}, f32[1,3,64,256]{3,2,1,0:T(8,128)S(1)}, u32[]{:S(2)}, u32[]{:S(2)}) collective-permute-start(f32[1,3,64,256]{3,2,1,0:T(8,128)S(1)} %add.34), channel_id=1, source_target_pairs={{0,16},{2,18},{4,20},{6,22},{8,24},{10,26},{12,28},{14,30},{16,0},... | collective-permute-start | bytes 589832 | tf_op jit(solution)/shard_map/ppermute | solution.py:343
  42.3 7.4 %collective-permute-start.7 = (f32[1,3,64,256]{3,2,1,0:T(8,128)S(1)}, f32[1,3,64,256]{3,2,1,0:T(8,128)S(1)}, u32[]{:S(2)}, u32[]{:S(2)}) collective-permute-start(f32[1,3,64,256]{3,2,1,0:T(8,128)S(1)} %get-tuple-element.130), channel_id=1, source_target_pairs={{0,8},{2,10},{4,12},{6,14},{8,0},{10,2},{12,4},{14,6},{16,24},{18,... | collective-permute-start | bytes 589832 | tf_op jit(solution)/shard_map/ppermute | solution.py:343
  49.7 8.3 %collective-permute-start.9 = (f32[1,3,64,256]{3,2,1,0:T(8,128)S(1)}, f32[1,3,64,256]{3,2,1,0:T(8,128)S(1)}, u32[]{:S(2)}, u32[]{:S(2)}) collective-permute-start(f32[1,3,64,256]{3,2,1,0:T(8,128)S(1)} %add_add_fusion.1.refs_5_), channel_id=1, source_target_pairs={{0,8},{2,10},{4,12},{6,14},{8,0},{10,2},{12,4},{14,6},{16,24},{18,... | collective-permute-start | bytes 589832 | tf_op jit(solution)/shard_map/ppermute | solution.py:343
  51.1 12.7 %collective-permute-start.14 = (f32[1,3,64,256]{3,2,1,0:T(8,128)S(1)}, f32[1,3,64,256]{3,2,1,0:T(8,128)S(1)}, u32[]{:S(2)}, u32[]{:S(2)}) collective-permute-start(f32[1,3,64,256]{3,2,1,0:T(8,128)S(1)} %add_add_fusion.1.refs_5_), channel_id=1, source_target_pairs={{0,16},{2,18},{4,20},{6,22},{8,24},{10,26},{12,28},{14,30},{16,0},... | collective-permute-start | bytes 589832 | tf_op jit(solution)/shard_map/ppermute | solution.py:343
  58.1 11.4 %collective-permute-start.13 = (f32[256,256]{1,0:T(8,128)S(1)}, f32[256,256]{1,0:T(8,128)S(1)}, u32[]{:S(2)}, u32[]{:S(2)}) collective-permute-start(f32[256,256]{1,0:T(8,128)S(1)} %slice_bitcast_fusion), channel_id=1, source_target_pairs={{0,2},{2,0},{4,6},{6,4},{8,10},{10,8},{12,14},{14,12},{16,18},{18,... | collective-permute-start | bytes 786440 | tf_op jit(solution)/shard_map/ppermute | solution.py:343
  60.8 8.7 %collective-permute-start.12 = (f32[256,256]{1,0:T(8,128)S(1)}, f32[256,256]{1,0:T(8,128)S(1)}, u32[]{:S(2)}, u32[]{:S(2)}) collective-permute-start(f32[256,256]{1,0:T(8,128)S(1)} %slice_bitcast_fusion.1), channel_id=1, source_target_pairs={{0,4},{2,6},{4,0},{6,2},{8,12},{10,14},{12,8},{14,10},{16,20},{18,... | collective-permute-start | bytes 786440 | tf_op jit(solution)/shard_map/ppermute | solution.py:343
  63.8 5.7 %collective-permute-start.15 = (f32[1,3,64,256]{3,2,1,0:T(8,128)S(1)}, f32[1,3,64,256]{3,2,1,0:T(8,128)S(1)}, u32[]{:S(2)}, u32[]{:S(2)}) collective-permute-start(f32[1,3,64,256]{3,2,1,0:T(8,128)S(1)} %collective-permute-done.14.refs_7_), channel_id=1, source_target_pairs={{0,8},{2,10},{4,12},{6,14},{8,0},{10,2},{12,4},{14,6},{16,24},{18,... | collective-permute-start | bytes 589832 | tf_op jit(solution)/shard_map/ppermute | solution.py:343
  71.3 1.2 collective-permute-start.16
  72.5 4.5 %collective-permute-start.19 = (f32[2,4,256]{2,1,0:T(4,128)S(1)}, f32[2,4,256]{2,1,0:T(4,128)S(1)}, u32[]{:S(2)}, u32[]{:S(2)}) collective-permute-start(f32[2,4,256]{2,1,0:T(4,128)S(1)} %add.36.refs_5_), channel_id=1, source_target_pairs={{0,6},{2,4},{4,2},{6,0},{8,14},{10,12},{12,10},{14,8},{16,22},{18,... | collective-permute-start | bytes 24584 | tf_op jit(solution)/shard_map/ppermute | solution.py:343
  74.6 3.7 %collective-permute-start.18 = (f32[2,4,256]{2,1,0:T(4,128)S(1)}, f32[2,4,256]{2,1,0:T(4,128)S(1)}, u32[]{:S(2)}, u32[]{:S(2)}) collective-permute-start(f32[2,4,256]{2,1,0:T(4,128)S(1)} %add.36.refs_5_), channel_id=1, source_target_pairs={{0,4},{2,6},{4,0},{6,2},{8,12},{10,14},{12,8},{14,10},{16,20},{18,... | collective-permute-start | bytes 24584 | tf_op jit(solution)/shard_map/ppermute | solution.py:343
  75.9 3.7 %collective-permute-start.17 = (f32[2,4,256]{2,1,0:T(4,128)S(1)}, f32[2,4,256]{2,1,0:T(4,128)S(1)}, u32[]{:S(2)}, u32[]{:S(2)}) collective-permute-start(f32[2,4,256]{2,1,0:T(4,128)S(1)} %add.36.refs_5_), channel_id=1, source_target_pairs={{0,2},{2,0},{4,6},{6,4},{8,10},{10,8},{12,14},{14,12},{16,18},{18,... | collective-permute-start | bytes 24584 | tf_op jit(solution)/shard_map/ppermute | solution.py:343
  81.7 5.7 %collective-permute-start.20 = (f32[1,3,64,256]{3,2,1,0:T(8,128)S(1)}, f32[1,3,64,256]{3,2,1,0:T(8,128)S(1)}, u32[]{:S(2)}, u32[]{:S(2)}) collective-permute-start(f32[1,3,64,256]{3,2,1,0:T(8,128)S(1)} %get-tuple-element.155), channel_id=1, source_target_pairs={{0,8},{2,10},{4,12},{6,14},{8,0},{10,2},{12,4},{14,6},{16,24},{18,... | collective-permute-start | bytes 589832 | tf_op jit(solution)/shard_map/ppermute | solution.py:343
  87.4 9.6 %collective-permute-start.22 = (f32[1,3,64,256]{3,2,1,0:T(8,128)S(1)}, f32[1,3,64,256]{3,2,1,0:T(8,128)S(1)}, u32[]{:S(2)}, u32[]{:S(2)}) collective-permute-start(f32[1,3,64,256]{3,2,1,0:T(8,128)S(1)} %add.38), channel_id=1, source_target_pairs={{0,16},{2,18},{4,20},{6,22},{8,24},{10,26},{12,28},{14,30},{16,0},... | collective-permute-start | bytes 589832 | tf_op jit(solution)/shard_map/ppermute | solution.py:343
  87.5 9.5 %collective-permute-start.21 = (f32[1,3,64,256]{3,2,1,0:T(8,128)S(1)}, f32[1,3,64,256]{3,2,1,0:T(8,128)S(1)}, u32[]{:S(2)}, u32[]{:S(2)}) collective-permute-start(f32[1,3,64,256]{3,2,1,0:T(8,128)S(1)} %get-tuple-element.157), channel_id=1, source_target_pairs={{0,8},{2,10},{4,12},{6,14},{8,0},{10,2},{12,4},{14,6},{16,24},{18,... | collective-permute-start | bytes 589832 | tf_op jit(solution)/shard_map/ppermute | solution.py:343
  97.1 9.0 %collective-permute-start.24 = (f32[1,3,64,256]{3,2,1,0:T(8,128)S(1)}, f32[1,3,64,256]{3,2,1,0:T(8,128)S(1)}, u32[]{:S(2)}, u32[]{:S(2)}) collective-permute-start(f32[1,3,64,256]{3,2,1,0:T(8,128)S(1)} %add_add_fusion.refs_11_.refs_0_), channel_id=1, source_target_pairs={{0,16},{2,18},{4,20},{6,22},{8,24},{10,26},{12,28},{14,30},{16,0},... | collective-permute-start | bytes 589832 | tf_op jit(solution)/shard_map/ppermute | solution.py:343
  97.8 9.3 %collective-permute-start.26 = (f32[256,256]{1,0:T(8,128)S(1)}, f32[256,256]{1,0:T(8,128)S(1)}, u32[]{:S(2)}, u32[]{:S(2)}) collective-permute-start(f32[256,256]{1,0:T(8,128)S(1)} %get-tuple-element.161), channel_id=1, source_target_pairs={{0,2},{2,0},{4,6},{6,4},{8,10},{10,8},{12,14},{14,12},{16,18},{18,... | collective-permute-start | bytes 786440 | tf_op jit(solution)/shard_map/ppermute | solution.py:343
  98.6 11.5 %collective-permute-start.27 = (f32[256,256]{1,0:T(8,128)S(1)}, f32[256,256]{1,0:T(8,128)S(1)}, u32[]{:S(2)}, u32[]{:S(2)}) collective-permute-start(f32[256,256]{1,0:T(8,128)S(1)} %get-tuple-element.162), channel_id=1, source_target_pairs={{0,4},{2,6},{4,0},{6,2},{8,12},{10,14},{12,8},{14,10},{16,20},{18,... | collective-permute-start | bytes 786440 | tf_op jit(solution)/shard_map/ppermute | solution.py:343
  99.2 10.9 %collective-permute-start.28 = (f32[256,256]{1,0:T(8,128)S(1)}, f32[256,256]{1,0:T(8,128)S(1)}, u32[]{:S(2)}, u32[]{:S(2)}) collective-permute-start(f32[256,256]{1,0:T(8,128)S(1)} %get-tuple-element.163), channel_id=1, source_target_pairs={{0,6},{2,4},{4,2},{6,0},{8,14},{10,12},{12,10},{14,8},{16,22},{18,... | collective-permute-start | bytes 786440 | tf_op jit(solution)/shard_map/ppermute | solution.py:343
  101.3 10.5 %collective-permute-start.23 = (f32[1,3,64,256]{3,2,1,0:T(8,128)S(1)}, f32[1,3,64,256]{3,2,1,0:T(8,128)S(1)}, u32[]{:S(2)}, u32[]{:S(2)}) collective-permute-start(f32[1,3,64,256]{3,2,1,0:T(8,128)S(1)} %add_add_fusion.refs_11_.refs_0_), channel_id=1, source_target_pairs={{0,8},{2,10},{4,12},{6,14},{8,0},{10,2},{12,4},{14,6},{16,24},{18,... | collective-permute-start | bytes 589832 | tf_op jit(solution)/shard_map/ppermute | solution.py:343
  106.1 7.1 %collective-permute-start.25 = (f32[1,3,64,256]{3,2,1,0:T(8,128)S(1)}, f32[1,3,64,256]{3,2,1,0:T(8,128)S(1)}, u32[]{:S(2)}, u32[]{:S(2)}) collective-permute-start(f32[1,3,64,256]{3,2,1,0:T(8,128)S(1)} %collective-permute-done.24.refs_13_), channel_id=1, source_target_pairs={{0,8},{2,10},{4,12},{6,14},{8,0},{10,2},{12,4},{14,6},{16,24},{18,... | collective-permute-start | bytes 589832 | tf_op jit(solution)/shard_map/ppermute | solution.py:343
  116.1 30.8 %collective-permute-start.29 = (f32[2,256,256]{2,1,0:T(8,128)S(1)}, f32[2,256,256]{2,1,0:T(8,128)S(1)}, u32[]{:S(2)}, u32[]{:S(2)}) collective-permute-start(f32[2,256,256]{2,1,0:T(8,128)S(1)} %get-tuple-element.190), channel_id=1, source_target_pairs={{0,2},{2,0},{4,6},{6,4},{8,10},{10,8},{12,14},{14,12},{16,18},{18,... | collective-permute-start | bytes 1572872 | tf_op jit(solution)/shard_map/ppermute | solution.py:343
  116.5 30.4 %collective-permute-start.30 = (f32[2,256,256]{2,1,0:T(8,128)S(1)}, f32[2,256,256]{2,1,0:T(8,128)S(1)}, u32[]{:S(2)}, u32[]{:S(2)}) collective-permute-start(f32[2,256,256]{2,1,0:T(8,128)S(1)} %get-tuple-element.191), channel_id=1, source_target_pairs={{0,4},{2,6},{4,0},{6,2},{8,12},{10,14},{12,8},{14,10},{16,20},{18,... | collective-permute-start | bytes 1572872 | tf_op jit(solution)/shard_map/ppermute | solution.py:343
  116.8 30.1 %collective-permute-start.31 = (f32[2,256,256]{2,1,0:T(8,128)S(1)}, f32[2,256,256]{2,1,0:T(8,128)S(1)}, u32[]{:S(2)}, u32[]{:S(2)}) collective-permute-start(f32[2,256,256]{2,1,0:T(8,128)S(1)} %get-tuple-element.192), channel_id=1, source_target_pairs={{0,6},{2,4},{4,2},{6,0},{8,14},{10,12},{12,10},{14,8},{16,22},{18,... | collective-permute-start | bytes 1572872 | tf_op jit(solution)/shard_map/ppermute | solution.py:343
  119.7 7.8 %collective-permute-start.33 = (f32[1,3,64,256]{3,2,1,0:T(8,128)S(1)}, f32[1,3,64,256]{3,2,1,0:T(8,128)S(1)}, u32[]{:S(2)}, u32[]{:S(2)}) collective-permute-start(f32[1,3,64,256]{3,2,1,0:T(8,128)S(1)} %get-tuple-element.196), channel_id=1, source_target_pairs={{0,8},{2,10},{4,12},{6,14},{8,0},{10,2},{12,4},{14,6},{16,24},{18,... | collective-permute-start | bytes 589832 | tf_op jit(solution)/shard_map/ppermute | solution.py:343
  119.7 11.3 %collective-permute-start.32 = (f32[1,3,64,256]{3,2,1,0:T(8,128)S(1)}, f32[1,3,64,256]{3,2,1,0:T(8,128)S(1)}, u32[]{:S(2)}, u32[]{:S(2)}) collective-permute-start(f32[1,3,64,256]{3,2,1,0:T(8,128)S(1)} %get-tuple-element.194), channel_id=1, source_target_pairs={{0,8},{2,10},{4,12},{6,14},{8,0},{10,2},{12,4},{14,6},{16,24},{18,... | collective-permute-start | bytes 589832 | tf_op jit(solution)/shard_map/ppermute | solution.py:343
  127.5 8.3 %collective-permute-start.34 = (f32[1,3,64,256]{3,2,1,0:T(8,128)S(1)}, f32[1,3,64,256]{3,2,1,0:T(8,128)S(1)}, u32[]{:S(2)}, u32[]{:S(2)}) collective-permute-start(f32[1,3,64,256]{3,2,1,0:T(8,128)S(1)} %add.40), channel_id=1, source_target_pairs={{0,16},{2,18},{4,20},{6,22},{8,24},{10,26},{12,28},{14,30},{16,0},... | collective-permute-start | bytes 589832 | tf_op jit(solution)/shard_map/ppermute | solution.py:343
  136.4 5.6 %collective-permute-start.35 = (f32[1,3,16,256]{3,2,1,0:T(8,128)S(1)}, f32[1,3,16,256]{3,2,1,0:T(8,128)S(1)}, u32[]{:S(2)}, u32[]{:S(2)}) collective-permute-start(f32[1,3,16,256]{3,2,1,0:T(8,128)S(1)} %get-tuple-element.198), channel_id=1, source_target_pairs={{0,2},{2,0},{4,6},{6,4},{8,10},{10,8},{12,14},{14,12},{16,18},{18,... | collective-permute-start | bytes 147464 | tf_op jit(solution)/shard_map/ppermute | solution.py:343
  136.9 5.0 %collective-permute-start.36 = (f32[1,3,16,256]{3,2,1,0:T(8,128)S(1)}, f32[1,3,16,256]{3,2,1,0:T(8,128)S(1)}, u32[]{:S(2)}, u32[]{:S(2)}) collective-permute-start(f32[1,3,16,256]{3,2,1,0:T(8,128)S(1)} %get-tuple-element.199), channel_id=1, source_target_pairs={{0,4},{2,6},{4,0},{6,2},{8,12},{10,14},{12,8},{14,10},{16,20},{18,... | collective-permute-start | bytes 147464 | tf_op jit(solution)/shard_map/ppermute | solution.py:343
  141.9 5.0 %collective-permute-start.37 = (f32[1,3,16,256]{3,2,1,0:T(8,128)S(1)}, f32[1,3,16,256]{3,2,1,0:T(8,128)S(1)}, u32[]{:S(2)}, u32[]{:S(2)}) collective-permute-start(f32[1,3,16,256]{3,2,1,0:T(8,128)S(1)} %get-tuple-element.200), channel_id=1, source_target_pairs={{0,6},{2,4},{4,2},{6,0},{8,14},{10,12},{12,10},{14,8},{16,22},{18,... | collective-permute-start | bytes 147464 | tf_op jit(solution)/shard_map/ppermute | solution.py:343

commit v12 on v8

--- a/solution.py
+++ b/solution.py
@@ -11,7 +11,7 @@
 F32 = jnp.float32
 BF16 = jnp.bfloat16
 LANES = 128
-VMEM_LIMIT = 24 * 1024 * 1024
+MIB = 1024 * 1024
 
 
 def mm(a, b):
@@ -26,7 +26,7 @@
     return lax.dot_general(a, b, (((0,), (0,)), ((), ())), preferred_element_type=F32)
 
 
-def call(body, out_shape, scratch, flops, *args):
+def call(body, out_shape, scratch, flops, *args, mib=16):
     smem = pl.BlockSpec(memory_space=pltpu.SMEM)
     vmem = pl.BlockSpec(memory_space=pltpu.VMEM)
     size = sum(a.size * a.dtype.itemsize for a in args)
@@ -37,7 +37,7 @@
         in_specs=[smem if a.dtype == jnp.int32 else vmem for a in args],
         out_specs=[vmem] * len(out_shape),
         scratch_shapes=scratch,
-        compiler_params=pltpu.CompilerParams(vmem_limit_bytes=VMEM_LIMIT),
+        compiler_params=pltpu.CompilerParams(vmem_limit_bytes=mib * MIB),
         cost_estimate=pl.CostEstimate(flops=flops, bytes_accessed=size, transcendentals=0),
     )(*args)
 
@@ -65,16 +65,16 @@
     outs, scratch = rest[:groups], rest[groups]
     tokens, heads, width = x.shape
     put_rows(scratch, x[...].astype(F32).reshape(tokens * heads, width))
-    for step in range(groups):
-        outs[step][...] = take_head(scratch, place[0] ^ step, tokens, heads)
+    for step, out in enumerate(outs):
+        out[...] = take_head(scratch, place[0] ^ step, tokens, heads).astype(out.dtype)
 
 
 def split_scaled_kernel(groups, place, x, r, *rest):
     outs = rest[:groups]
     split_kernel(groups, place, x, *rest)
     for step in range(groups):
-        scaled = outs[step][...] * rate_column(r, place[0] ^ step)
-        outs[step][...] = scaled.astype(BF16).astype(F32)
+        scaled = outs[step][...].astype(F32) * rate_column(r, place[0] ^ step)
+        outs[step][...] = scaled.astype(BF16).astype(outs[step].dtype)
 
 
 def split_apply_kernel(groups, place, q, cot, gain, scale, *rest):
@@ -358,7 +358,9 @@
     square = pltpu.VMEM((3, hidden, width), F32)
 
     def split(body, *args):
-        return call(functools.partial(body, groups), pieces, [scratch], 16 * flops, place, *args)
+        outs = [shape(tokens, width, dtype=BF16)] + pieces[1:]
+        body = functools.partial(body, groups)
+        return call(body, outs, [scratch], 16 * flops, place, *args, mib=8)
 
     k_in = in_plane(split(split_kernel, keys[0]))
     s_in = in_plane(split(split_scaled_kernel, values[0], rates[0]))
@@ -380,8 +382,10 @@
         [shape(2, tokens, width)] * groups + [shape(8, width)],
         [scratch], flops // 8, place, queries[0], cotangent[0], gain, own_scale,
     )
-    q_in = in_plane(q_out)
+    q_in = in_plane(q_out[:-1])
     new = functools.reduce(jnp.add, scatter(terms, depth, groups))
+    new, q_in, q_last = after(new, q_in, q_out[-1])
+    q_in.append(move(q_last, "ctx", groups - 1))
     new = gather(new, depth, groups)
     *passed, stats = call(
         functools.partial(apply_kernel, groups, depth),
@@ -414,7 +418,7 @@
     out = call(
         functools.partial(update_back_kernel, groups, depth, scale),
         [shape(2, tokens, width)] * groups + slices, [square] * 2, 12 * flops,
-        place, *early, *saved, *parts, *own,
+        place, *early, *saved, *parts, *own, mib=24,
     )
     back = in_plane(out[:groups])
     ends = scatter(out[groups:], depth, groups, one_by_one=False)

time: 146 us -> 146 us (level)
  waiting for transfers between devices: 75 us -> 78.4 us
  starting transfers between devices: 46.3 us -> 43.5 us
    ppermute x37, waiting for transfers between devices: 75 us -> 78.4 us  [move(): lax.ppermute(x, axis, [(c, c ^ step) for c in range(lax.axis_size(axis))])]
    ppermute x37, starting transfers between devices: 46.3 us -> 43.5 us  [move(): lax.ppermute(x, axis, [(c, c ^ step) for c in range(lax.axis_size(axis))])]
  transfers between devices with their start and end apart: 37 -> 37, of which waited for: 22 -> 25; matrix products, arithmetic and copies ran while one was open for 1% -> 1% of each run, Pallas kernels for 5% -> 5%
where the time goes in v12:
time: 146 us
  waiting for transfers between devices  78.4 us (54%)
  starting transfers between devices  43.5 us (30%)
  Pallas kernels  19.8 us (14%)
  local copies, waits for them, and re-layouts  3.52 us (2%)
    ppermute x37, waiting for transfers between devices, move(): lax.ppermute(x, axis, [(c, c ^ step) for c in range(lax.axis_size(axis))])  78.4 us
    ppermute x37, starting transfers between devices, move(): lax.ppermute(x, axis, [(c, c ^ step) for c in range(lax.axis_size(axis))])  43.5 us
    pallas_call x11, Pallas kernels, call(): pl.pallas_call(body, out_shape=out_shape, in_specs=[smem if a.dtype == jn...  19.8 us
  transfers between devices with their start and end apart: 37, of which 25 were waited for; matrix products, arithmetic and copies ran while one was open for 1% of the time, Pallas kernels for 5%

profile of v12, /device:TPU:0, one launch (start us, length us, event | category | flops | bytes accessed | tf_op | source)
XLA Modules:
  0.0 146.2 jit_solution(6516030961577883182)
XLA Ops:
  0.7 1.1 copy-done.5
  1.8 0.9 shard_map.145
  2.8 3.0 %collective-permute-start = (f32[256,256]{1,0:T(8,128)S(1)}, f32[256,256]{1,0:T(8,128)S(1)}, u32[]{:S(2)}, u32[]{:S(2)}) collective-permute-start(f32[256,256]{1,0:T(8,128)S(1)} %get-tuple-element.109), channel_id=1, source_target_pairs={{0,2},{2,0},{4,6},{6,4},{8,10},{10,8},{12,14},{14,12},{16,18},{18,... | collective-permute-start | bytes 786440 | tf_op jit(solution)/shard_map/ppermute | solution.py:320
  5.8 1.5 %collective-permute-start.1 = (f32[256,256]{1,0:T(8,128)S(1)}, f32[256,256]{1,0:T(8,128)S(1)}, u32[]{:S(2)}, u32[]{:S(2)}) collective-permute-start(f32[256,256]{1,0:T(8,128)S(1)} %get-tuple-element.110), channel_id=1, source_target_pairs={{0,4},{2,6},{4,0},{6,2},{8,12},{10,14},{12,8},{14,10},{16,20},{18,... | collective-permute-start | bytes 786440 | tf_op jit(solution)/shard_map/ppermute | solution.py:320
  7.3 1.8 %shard_map.146 = (bf16[256,256]{1,0:T(8,128)(2,1)S(1)}, f32[256,256]{1,0:T(8,128)}, f32[256,256]{1,0:T(8,128)}, f32[256,256]{1,0:T(8,128)S(1)}) custom-call(s32[2]{0:T(128)S(1)} %pad_add_fusion.place, bf16[256,4,256]{2,1,0:T(4,128)(2,1)S(1)} %bitcast.22, f32[4,256]{1,0:T(4,128)S(1)} %bitcast.19), custom_call_target="tpu_custom_call" | custom-call | flops 2147483648 | bytes 1445896 | tf_op jit(solution)/shard_map/pallas_call | solution.py:34
  9.1 0.7 copy-done.7
  9.8 1.9 %collective-permute-start.3 = (f32[256,256]{1,0:T(8,128)}, f32[256,256]{1,0:T(8,128)S(1)}, u32[]{:S(2)}, u32[]{:S(2)}) collective-permute-start(f32[256,256]{1,0:T(8,128)} %get-tuple-element.113), channel_id=1, source_target_pairs={{0,2},{2,0},{4,6},{6,4},{8,10},{10,8},{12,14},{14,12},{16,18},{18,... | collective-permute-start | bytes 786440 | tf_op jit(solution)/shard_map/ppermute | solution.py:320
  11.7 1.5 %collective-permute-start.4 = (f32[256,256]{1,0:T(8,128)}, f32[256,256]{1,0:T(8,128)S(1)}, u32[]{:S(2)}, u32[]{:S(2)}) collective-permute-start(f32[256,256]{1,0:T(8,128)} %get-tuple-element.114), channel_id=1, source_target_pairs={{0,4},{2,6},{4,0},{6,2},{8,12},{10,14},{12,8},{14,10},{16,20},{18,... | collective-permute-start | bytes 786440 | tf_op jit(solution)/shard_map/ppermute | solution.py:320
  13.2 2.7 %collective-permute-start.5 = (f32[256,256]{1,0:T(8,128)S(1)}, f32[256,256]{1,0:T(8,128)S(1)}, u32[]{:S(2)}, u32[]{:S(2)}) collective-permute-start(f32[256,256]{1,0:T(8,128)S(1)} %get-tuple-element.115), channel_id=1, source_target_pairs={{0,6},{2,4},{4,2},{6,0},{8,14},{10,12},{12,10},{14,8},{16,22},{18,... | collective-permute-start | bytes 786440 | tf_op jit(solution)/shard_map/ppermute | solution.py:320
  15.9 1.1 dynamic-slice_bitcast_fusion
  17.1 2.7 %collective-permute-done.1.refs_2_ = f32[256,256]{1,0:T(8,128)S(1)} collective-permute-done((f32[256,256]{1,0:T(8,128)S(1)}, f32[256,256]{1,0:T(8,128)S(1)}, u32[]{:S(2)}, u32[]{:S(2)}) %collective-permute-start.1) | collective-permute-done | bytes 262176 | tf_op jit(solution)/shard_map/ppermute | solution.py:320
  20.1 4.1 %collective-permute-done.3.refs_5_ = f32[256,256]{1,0:T(8,128)S(1)} collective-permute-done((f32[256,256]{1,0:T(8,128)}, f32[256,256]{1,0:T(8,128)S(1)}, u32[]{:S(2)}, u32[]{:S(2)}) %collective-permute-start.3) | collective-permute-done | bytes 262176 | tf_op jit(solution)/shard_map/ppermute | solution.py:320
  24.2 6.2 %collective-permute-done.4.refs_6_ = f32[256,256]{1,0:T(8,128)S(1)} collective-permute-done((f32[256,256]{1,0:T(8,128)}, f32[256,256]{1,0:T(8,128)S(1)}, u32[]{:S(2)}, u32[]{:S(2)}) %collective-permute-start.4) | collective-permute-done | bytes 262176 | tf_op jit(solution)/shard_map/ppermute | solution.py:320
  30.4 2.2 %shard_map.148 = (bf16[4,256,256]{2,1,0:T(8,128)(2,1)S(1)}, bf16[4,256,256]{2,1,0:T(8,128)(2,1)S(1)}, f32[1,3,64,256]{3,2,1,0:T(8,128)S(1)}, f32[1,3,64,256]{3,2...) custom-call(s32[2]{0:T(128)S(1)} %pad_add_fusion.place, ...), custom_call_target="tpu_custom_call" | custom-call | flops 805306368 | bytes 4456456 | tf_op jit(solution)/shard_map/pallas_call | solution.py:34
  32.6 1.6 %collective-permute-start.6 = (f32[1,3,64,256]{3,2,1,0:T(8,128)S(1)}, f32[1,3,64,256]{3,2,1,0:T(8,128)S(1)}, u32[]{:S(2)}, u32[]{:S(2)}) collective-permute-start(f32[1,3,64,256]{3,2,1,0:T(8,128)S(1)} %get-tuple-element.128), channel_id=1, source_target_pairs={{0,8},{2,10},{4,12},{6,14},{8,0},{10,2},{12,4},{14,6},{16,24},{18,... | collective-permute-start | bytes 589832 | tf_op jit(solution)/shard_map/ppermute | solution.py:320
  34.9 1.9 %shard_map.147 = (f32[2,256,256]{2,1,0:T(8,128)S(1)}, f32[2,256,256]{2,1,0:T(8,128)S(1)}, f32[2,256,256]{2,1,0:T(8,128)S(1)}, f32[2,256,256]{2,1,0:T(8,128)S(1)}, f32[8,256]{1,0:T(8,128)S(1)}) custom-call(s32[2]{0:T(128)S(1)} %pad_add_fusion.place, bf16[256,4,256]{2,1,0:T(4,128)(2,1)S(1)} %bitcast.17, bf16[256,4,256]{2,1,0:T(4,128)(2,1)S(1)} %bitcast.18, ...), custom_call_target="tpu_custom_call" | custom-call | flops 16777216 | bytes 3158028 | tf_op jit(solution)/shard_map/pallas_call | solution.py:34
  36.8 1.3 collective-permute-start.9
  38.1 0.8 collective-permute-start.10
  39.0 2.7 %collective-permute-start.8 = (f32[1,3,64,256]{3,2,1,0:T(8,128)S(1)}, f32[1,3,64,256]{3,2,1,0:T(8,128)S(1)}, u32[]{:S(2)}, u32[]{:S(2)}) collective-permute-start(f32[1,3,64,256]{3,2,1,0:T(8,128)S(1)} %add.34), channel_id=1, source_target_pairs={{0,16},{2,18},{4,20},{6,22},{8,24},{10,26},{12,28},{14,30},{16,0},... | collective-permute-start | bytes 589832 | tf_op jit(solution)/shard_map/ppermute | solution.py:320
  41.6 1.0 collective-permute-start.7
  42.6 6.3 %collective-permute-done.8 = f32[1,3,64,256]{3,2,1,0:T(8,128)S(1)} collective-permute-done((f32[1,3,64,256]{3,2,1,0:T(8,128)S(1)}, f32[1,3,64,256]{3,2,1,0:T(8,128)S(1)}, u32[]{:S(2)}, u32[]{:S(2)}) %collective-permute-start.8) | collective-permute-done | bytes 196640 | tf_op jit(solution)/shard_map/ppermute | solution.py:320
  49.0 0.9 collective-permute-done.7
  50.4 1.1 collective-permute-start.11
  51.5 2.0 %collective-permute-start.13 = (f32[1,3,64,256]{3,2,1,0:T(8,128)S(1)}, f32[1,3,64,256]{3,2,1,0:T(8,128)S(1)}, u32[]{:S(2)}, u32[]{:S(2)}) collective-permute-start(f32[1,3,64,256]{3,2,1,0:T(8,128)S(1)} %add_add_fusion.1.refs_4_), channel_id=1, source_target_pairs={{0,16},{2,18},{4,20},{6,22},{8,24},{10,26},{12,28},{14,30},{16,0},... | collective-permute-start | bytes 589832 | tf_op jit(solution)/shard_map/ppermute | solution.py:320
  53.5 0.8 collective-permute-start.12
  54.3 7.1 %collective-permute-done.13.refs_6_ = f32[1,3,64,256]{3,2,1,0:T(8,128)S(1)} collective-permute-done((f32[1,3,64,256]{3,2,1,0:T(8,128)S(1)}, f32[1,3,64,256]{3,2,1,0:T(8,128)S(1)}, u32[]{:S(2)}, u32[]{:S(2)}) %collective-permute-start.13) | collective-permute-done | bytes 196640 | tf_op jit(solution)/shard_map/ppermute | solution.py:320
  61.6 5.5 %collective-permute-done.14.refs_7_ = f32[1,3,64,256]{3,2,1,0:T(8,128)S(1)} collective-permute-done((f32[1,3,64,256]{3,2,1,0:T(8,128)S(1)}, f32[1,3,64,256]{3,2,1,0:T(8,128)S(1)}, u32[]{:S(2)}, u32[]{:S(2)}) %collective-permute-start.14) | collective-permute-done | bytes 196640 | tf_op jit(solution)/shard_map/ppermute | solution.py:320
  67.1 1.8 %shard_map.149 = (f32[4,256,256]{2,1,0:T(8,128)S(1)}, f32[4,256,256]{2,1,0:T(8,128)S(1)}, bf16[4,256,256]{2,1,0:T(8,128)(2,1)S(1)}, f32[4,256,256]{2,1,0:T(8,128...) custom-call(s32[2]{0:T(128)S(1)} %pad_add_fusion.place, f32[8,256]{1,0:T(8,128)S(1)} %get-tuple-element.118.scale_row, ...), custom_call_target="tpu_custom_call" | custom-call | flops 402653184 | bytes 6963208 | tf_op jit(solution)/shard_map/pallas_call | solution.py:34
  68.9 1.2 collective-permute-done.15
  70.1 1.3 collective-permute-start.18
  71.4 1.5 %collective-permute-start.17 = (f32[2,4,256]{2,1,0:T(4,128)S(1)}, f32[2,4,256]{2,1,0:T(4,128)S(1)}, u32[]{:S(2)}, u32[]{:S(2)}) collective-permute-start(f32[2,4,256]{2,1,0:T(4,128)S(1)} %add.36.refs_4_), channel_id=1, source_target_pairs={{0,4},{2,6},{4,0},{6,2},{8,12},{10,14},{12,8},{14,10},{16,20},{18,... | collective-permute-start | bytes 24584 | tf_op jit(solution)/shard_map/ppermute | solution.py:320
  72.9 0.7 collective-permute-start.16
  73.6 1.1 collective-permute-done.18.refs_7_
  75.1 1.5 %collective-permute-done.16.refs_5_ = f32[2,4,256]{2,1,0:T(4,128)S(1)} collective-permute-done((f32[2,4,256]{2,1,0:T(4,128)S(1)}, f32[2,4,256]{2,1,0:T(4,128)S(1)}, u32[]{:S(2)}, u32[]{:S(2)}) %collective-permute-start.16) | collective-permute-done | bytes 8224 | tf_op jit(solution)/shard_map/ppermute | solution.py:320
  76.6 2.1 %shard_map.150 = (f32[256,256]{1,0:T(8,128)S(1)}, f32[256,256]{1,0:T(8,128)S(1)}, f32[256,256]{1,0:T(8,128)S(1)}, f32[256,256]{1,0:T(8,128)S(1)}, f32[1,3,64,256...) custom-call(s32[2]{0:T(128)S(1)} %pad_add_fusion.place, ...), custom_call_target="tpu_custom_call" | custom-call | flops 805306368 | bytes 8036360 | tf_op jit(solution)/shard_map/pallas_call | solution.py:34
  79.0 5.4 %collective-permute-done.19 = f32[1,3,64,256]{3,2,1,0:T(8,128)S(1)} collective-permute-done((f32[1,3,64,256]{3,2,1,0:T(8,128)S(1)}, f32[1,3,64,256]{3,2,1,0:T(8,128)S(1)}, u32[]{:S(2)}, u32[]{:S(2)}) %collective-permute-start.19) | collective-permute-done | bytes 196640 | tf_op jit(solution)/shard_map/ppermute | solution.py:320
  84.4 0.7 collective-permute-start.21
  85.2 1.8 %collective-permute-start.20 = (f32[1,3,64,256]{3,2,1,0:T(8,128)S(1)}, f32[1,3,64,256]{3,2,1,0:T(8,128)S(1)}, u32[]{:S(2)}, u32[]{:S(2)}) collective-permute-start(f32[1,3,64,256]{3,2,1,0:T(8,128)S(1)} %get-tuple-element.161), channel_id=1, source_target_pairs={{0,8},{2,10},{4,12},{6,14},{8,0},{10,2},{12,4},{14,6},{16,24},{18,... | collective-permute-start | bytes 589832 | tf_op jit(solution)/shard_map/ppermute | solution.py:320
  87.0 6.6 %collective-permute-done.21 = f32[1,3,64,256]{3,2,1,0:T(8,128)S(1)} collective-permute-done((f32[1,3,64,256]{3,2,1,0:T(8,128)S(1)}, f32[1,3,64,256]{3,2,1,0:T(8,128)S(1)}, u32[]{:S(2)}, u32[]{:S(2)}) %collective-permute-start.21) | collective-permute-done | bytes 196640 | tf_op jit(solution)/shard_map/ppermute | solution.py:320
  93.7 0.7 collective-permute-start.23
  94.4 0.8 collective-permute-start.25
  95.2 1.2 collective-permute-start.26
  96.3 1.5 %collective-permute-start.27 = (f32[256,256]{1,0:T(8,128)S(1)}, f32[256,256]{1,0:T(8,128)S(1)}, u32[]{:S(2)}, u32[]{:S(2)}) collective-permute-start(f32[256,256]{1,0:T(8,128)S(1)} %get-tuple-element.167), channel_id=1, source_target_pairs={{0,6},{2,4},{4,2},{6,0},{8,14},{10,12},{12,10},{14,8},{16,22},{18,... | collective-permute-start | bytes 786440 | tf_op jit(solution)/shard_map/ppermute | solution.py:320
  97.9 1.8 %collective-permute-start.22 = (f32[1,3,64,256]{3,2,1,0:T(8,128)S(1)}, f32[1,3,64,256]{3,2,1,0:T(8,128)S(1)}, u32[]{:S(2)}, u32[]{:S(2)}) collective-permute-start(f32[1,3,64,256]{3,2,1,0:T(8,128)S(1)} %add_add_fusion.refs_11_.refs_0_), channel_id=1, source_target_pairs={{0,8},{2,10},{4,12},{6,14},{8,0},{10,2},{12,4},{14,6},{16,24},{18,... | collective-permute-start | bytes 589832 | tf_op jit(solution)/shard_map/ppermute | solution.py:320
  99.6 3.7 %collective-permute-done.23.refs_13_ = f32[1,3,64,256]{3,2,1,0:T(8,128)S(1)} collective-permute-done((f32[1,3,64,256]{3,2,1,0:T(8,128)S(1)}, f32[1,3,64,256]{3,2,1,0:T(8,128)S(1)}, u32[]{:S(2)}, u32[]{:S(2)}) %collective-permute-start.23) | collective-permute-done | bytes 196640 | tf_op jit(solution)/shard_map/ppermute | solution.py:320
  103.3 1.1 shard_map.152
  104.4 2.4 %collective-permute-done.26.refs_2_ = f32[256,256]{1,0:T(8,128)S(1)} collective-permute-done((f32[256,256]{1,0:T(8,128)S(1)}, f32[256,256]{1,0:T(8,128)S(1)}, u32[]{:S(2)}, u32[]{:S(2)}) %collective-permute-start.26) | collective-permute-done | bytes 262176 | tf_op jit(solution)/shard_map/ppermute | solution.py:320
  106.9 1.7 %shard_map.151 = bf16[256,4,256]{2,1,0:T(4,128)(2,1)} custom-call(s32[2]{0:T(128)S(1)} %pad_add_fusion.place, f32[256,256]{1,0:T(8,128)S(1)} %get-tuple-element.164.refs_0_, f32[256,256]{1,0:T(8,128)S(1)} %collective-permute-done.25.refs_1_, f32[256,256]{1,0:T(8,128)S(1)} %collective-permute-done.26.refs_2_, f32[256,256]{1,0:T(8,128)S(1)} %collective-permute-done.27.refs_3_), custom_call_target="tpu_custom_call" | custom-call | flops 8388608 | bytes 1572872 | tf_op jit(solution)/shard_map/pallas_call | solution.py:34
  108.6 1.0 collective-permute-done.24.refs_14_
  109.6 3.2 %shard_map.153 = (f32[2,256,256]{2,1,0:T(8,128)S(1)}, f32[2,256,256]{2,1,0:T(8,128)S(1)}, f32[2,256,256]{2,1,0:T(8,128)S(1)}, f32[2,256,256]{2,1,0:T(8,128)S(1)}...) custom-call(s32[2]{0:T(128)S(1)} %pad_add_fusion.place, ...), custom_call_target="tpu_custom_call" | custom-call | flops 1610612736 | bytes 13369352 | tf_op jit(solution)/shard_map/pallas_call | solution.py:34
  112.8 2.5 %collective-permute-start.28 = (f32[2,256,256]{2,1,0:T(8,128)S(1)}, f32[2,256,256]{2,1,0:T(8,128)S(1)}, u32[]{:S(2)}, u32[]{:S(2)}) collective-permute-start(f32[2,256,256]{2,1,0:T(8,128)S(1)} %get-tuple-element.194), channel_id=1, source_target_pairs={{0,2},{2,0},{4,6},{6,4},{8,10},{10,8},{12,14},{14,12},{16,18},{18,... | collective-permute-start | bytes 1572872 | tf_op jit(solution)/shard_map/ppermute | solution.py:320
  115.3 1.5 collective-permute-start.30
  116.8 1.3 collective-permute-start.32
  118.1 0.7 collective-permute-start.31
  118.8 6.0 %collective-permute-done.32 = f32[1,3,64,256]{3,2,1,0:T(8,128)S(1)} collective-permute-done((f32[1,3,64,256]{3,2,1,0:T(8,128)S(1)}, f32[1,3,64,256]{3,2,1,0:T(8,128)S(1)}, u32[]{:S(2)}, u32[]{:S(2)}) %collective-permute-start.32) | collective-permute-done | bytes 196640 | tf_op jit(solution)/shard_map/ppermute | solution.py:320
  124.9 3.6 %collective-permute-done.31.refs_2_ = f32[1,3,64,256]{3,2,1,0:T(8,128)S(1)} collective-permute-done((f32[1,3,64,256]{3,2,1,0:T(8,128)S(1)}, f32[1,3,64,256]{3,2,1,0:T(8,128)S(1)}, u32[]{:S(2)}, u32[]{:S(2)}) %collective-permute-start.31) | collective-permute-done | bytes 196640 | tf_op jit(solution)/shard_map/ppermute | solution.py:320
  128.5 5.1 %collective-permute-done.33.refs_3_ = f32[1,3,64,256]{3,2,1,0:T(8,128)S(1)} collective-permute-done((f32[1,3,64,256]{3,2,1,0:T(8,128)S(1)}, f32[1,3,64,256]{3,2,1,0:T(8,128)S(1)}, u32[]{:S(2)}, u32[]{:S(2)}) %collective-permute-start.33) | collective-permute-done | bytes 196640 | tf_op jit(solution)/shard_map/ppermute | solution.py:320
  133.5 0.6 shard_map.154
  134.1 1.4 collective-permute-start.34
  135.6 0.6 collective-permute-start.35
  136.2 2.6 %collective-permute-done.34.refs_5_ = f32[1,3,16,256]{3,2,1,0:T(8,128)S(1)} collective-permute-done((f32[1,3,16,256]{3,2,1,0:T(8,128)S(1)}, f32[1,3,16,256]{3,2,1,0:T(8,128)S(1)}, u32[]{:S(2)}, u32[]{:S(2)}) %collective-permute-start.34) | collective-permute-done | bytes 49184 | tf_op jit(solution)/shard_map/ppermute | solution.py:320
  138.8 0.9 collective-permute-start.36
  140.2 3.6 %collective-permute-done.36.refs_7_ = f32[1,3,16,256]{3,2,1,0:T(8,128)S(1)} collective-permute-done((f32[1,3,16,256]{3,2,1,0:T(8,128)S(1)}, f32[1,3,16,256]{3,2,1,0:T(8,128)S(1)}, u32[]{:S(2)}, u32[]{:S(2)}) %collective-permute-start.36) | collective-permute-done | bytes 49184 | tf_op jit(solution)/shard_map/ppermute | solution.py:320
  143.8 2.4 %shard_map.155 = (bf16[256,4,256]{2,1,0:T(4,128)(2,1)}, bf16[256,4,256]{2,1,0:T(4,128)(2,1)}, f32[4,16,256]{2,1,0:T(8,128)}, f32[4,16,256]{2,1,0:T(8,128)}, f32[4,16,256]{2,1,0:T(8,128)}) custom-call(s32[2]{0:T(128)S(1)} %pad_add_fusion.place, f32[4,256]{1,0:T(4,128)S(1)} %bitcast.20, f32[2,256,256]{2,1,0:T(8,128)S(1)} %get-tuple-element.193.refs_0_, ...), custom_call_target="tpu_custom_call" | custom-call | flops 16777216 | bytes 3543048 | tf_op jit(solution)/shard_map/pallas_call | solution.py:34
  (51 shorter events, 3.5 us)
Async XLA Ops:
  0.6 15.3 %copy-start = (f32[4,256,256]{2,1,0:T(8,128)S(1)}, f32[4,256,256]{2,1,0:T(8,128)}, u32[]{:S(2)}) copy-start(f32[4,256,256]{2,1,0:T(8,128)} %param.16) | copy-start | bytes 3145732
  0.7 1.1 copy-start.5
  1.8 5.5 %copy-start.6 = (bf16[1,256,4,256]{3,2,1,0:T(4,128)(2,1)S(1)}, bf16[1,256,4,256]{3,2,1,0:T(4,128)(2,1)}, u32[]{:S(2)}) copy-start(bf16[1,256,4,256]{3,2,1,0:T(4,128)(2,1)} %param.12) | copy-start | bytes 1572868
  2.7 4.6 %copy-start.4 = (f32[1,4,256]{2,1,0:T(4,128)S(1)}, f32[1,4,256]{2,1,0:T(4,128)}, u32[]{:S(2)}) copy-start(f32[1,4,256]{2,1,0:T(4,128)} %param.13) | copy-start | bytes 12292
  2.8 10.5 %collective-permute-start = (f32[256,256]{1,0:T(8,128)S(1)}, f32[256,256]{1,0:T(8,128)S(1)}, u32[]{:S(2)}, u32[]{:S(2)}) collective-permute-start(f32[256,256]{1,0:T(8,128)S(1)} %get-tuple-element.109), channel_id=1, source_target_pairs={{0,2},{2,0},{4,6},{6,4},{8,10},{10,8},{12,14},{14,12},{16,18},{18,... | collective-permute-start | bytes 786440 | tf_op jit(solution)/shard_map/ppermute | solution.py:320
  5.8 14.0 %collective-permute-start.1 = (f32[256,256]{1,0:T(8,128)S(1)}, f32[256,256]{1,0:T(8,128)S(1)}, u32[]{:S(2)}, u32[]{:S(2)}) collective-permute-start(f32[256,256]{1,0:T(8,128)S(1)} %get-tuple-element.110), channel_id=1, source_target_pairs={{0,4},{2,6},{4,0},{6,2},{8,12},{10,14},{12,8},{14,10},{16,20},{18,... | collective-permute-start | bytes 786440 | tf_op jit(solution)/shard_map/ppermute | solution.py:320
  7.3 12.8 %collective-permute-start.2 = (f32[256,256]{1,0:T(8,128)S(1)}, f32[256,256]{1,0:T(8,128)S(1)}, u32[]{:S(2)}, u32[]{:S(2)}) collective-permute-start(f32[256,256]{1,0:T(8,128)S(1)} %get-tuple-element.111), channel_id=1, source_target_pairs={{0,6},{2,4},{4,2},{6,0},{8,14},{10,12},{12,10},{14,8},{16,22},{18,... | collective-permute-start | bytes 786440 | tf_op jit(solution)/shard_map/ppermute | solution.py:320
  9.1 0.7 copy-start.7
  9.8 14.4 %collective-permute-start.3 = (f32[256,256]{1,0:T(8,128)}, f32[256,256]{1,0:T(8,128)S(1)}, u32[]{:S(2)}, u32[]{:S(2)}) collective-permute-start(f32[256,256]{1,0:T(8,128)} %get-tuple-element.113), channel_id=1, source_target_pairs={{0,2},{2,0},{4,6},{6,4},{8,10},{10,8},{12,14},{14,12},{16,18},{18,... | collective-permute-start | bytes 786440 | tf_op jit(solution)/shard_map/ppermute | solution.py:320
  11.7 18.7 %collective-permute-start.4 = (f32[256,256]{1,0:T(8,128)}, f32[256,256]{1,0:T(8,128)S(1)}, u32[]{:S(2)}, u32[]{:S(2)}) collective-permute-start(f32[256,256]{1,0:T(8,128)} %get-tuple-element.114), channel_id=1, source_target_pairs={{0,4},{2,6},{4,0},{6,2},{8,12},{10,14},{12,8},{14,10},{16,20},{18,... | collective-permute-start | bytes 786440 | tf_op jit(solution)/shard_map/ppermute | solution.py:320
  13.2 17.1 %collective-permute-start.5 = (f32[256,256]{1,0:T(8,128)S(1)}, f32[256,256]{1,0:T(8,128)S(1)}, u32[]{:S(2)}, u32[]{:S(2)}) collective-permute-start(f32[256,256]{1,0:T(8,128)S(1)} %get-tuple-element.115), channel_id=1, source_target_pairs={{0,6},{2,4},{4,2},{6,0},{8,14},{10,12},{12,10},{14,8},{16,22},{18,... | collective-permute-start | bytes 786440 | tf_op jit(solution)/shard_map/ppermute | solution.py:320
  15.9 14.5 %copy-start.8 = (bf16[256,256]{1,0:T(8,128)(2,1)S(1)}, bf16[256,256]{1,0:T(8,128)(2,1)}, u32[]{:S(2)}) copy-start(bf16[256,256]{1,0:T(8,128)(2,1)} %copy-done.7) | copy-start | bytes 393220
  30.4 4.5 %copy-start.1 = (bf16[1,256,4,256]{3,2,1,0:T(4,128)(2,1)S(1)}, bf16[1,256,4,256]{3,2,1,0:T(4,128)(2,1)}, u32[]{:S(2)}) copy-start(bf16[1,256,4,256]{3,2,1,0:T(4,128)(2,1)} %param.10) | copy-start | bytes 1572868
  30.4 4.5 %copy-start.2 = (bf16[1,256,4,256]{3,2,1,0:T(4,128)(2,1)S(1)}, bf16[1,256,4,256]{3,2,1,0:T(4,128)(2,1)}, u32[]{:S(2)}) copy-start(bf16[1,256,4,256]{3,2,1,0:T(4,128)(2,1)} %param.19) | copy-start | bytes 1572868
  32.6 1.7 %copy-start.9 = (f32[4]{0:T(128)S(1)}, f32[4]{0:T(128)}, u32[]{:S(2)}) copy-start(f32[4]{0:T(128)} %param.14) | copy-start | bytes 52
  32.6 2.2 %copy-start.3 = (f32[4,256]{1,0:T(4,128)S(1)}, f32[4,256]{1,0:T(4,128)}, u32[]{:S(2)}) copy-start(f32[4,256]{1,0:T(4,128)} %gain.1) | copy-start | bytes 12292
  32.6 6.3 %collective-permute-start.6 = (f32[1,3,64,256]{3,2,1,0:T(8,128)S(1)}, f32[1,3,64,256]{3,2,1,0:T(8,128)S(1)}, u32[]{:S(2)}, u32[]{:S(2)}) collective-permute-start(f32[1,3,64,256]{3,2,1,0:T(8,128)S(1)} %get-tuple-element.128), channel_id=1, source_target_pairs={{0,8},{2,10},{4,12},{6,14},{8,0},{10,2},{12,4},{14,6},{16,24},{18,... | collective-permute-start | bytes 589832 | tf_op jit(solution)/shard_map/ppermute | solution.py:320
  36.8 13.1 %collective-permute-start.9 = (f32[2,256,256]{2,1,0:T(8,128)S(1)}, f32[2,256,256]{2,1,0:T(8,128)S(1)}, u32[]{:S(2)}, u32[]{:S(2)}) collective-permute-start(f32[2,256,256]{2,1,0:T(8,128)S(1)} %get-tuple-element.134), channel_id=1, source_target_pairs={{0,2},{2,0},{4,6},{6,4},{8,10},{10,8},{12,14},{14,12},{16,18},{18,... | collective-permute-start | bytes 1572872 | tf_op jit(solution)/shard_map/ppermute | solution.py:320
  38.1 12.2 %collective-permute-start.10 = (f32[2,256,256]{2,1,0:T(8,128)S(1)}, f32[2,256,256]{2,1,0:T(8,128)S(1)}, u32[]{:S(2)}, u32[]{:S(2)}) collective-permute-start(f32[2,256,256]{2,1,0:T(8,128)S(1)} %get-tuple-element.135), channel_id=1, source_target_pairs={{0,4},{2,6},{4,0},{6,2},{8,12},{10,14},{12,8},{14,10},{16,20},{18,... | collective-permute-start | bytes 1572872 | tf_op jit(solution)/shard_map/ppermute | solution.py:320
  39.0 10.0 %collective-permute-start.8 = (f32[1,3,64,256]{3,2,1,0:T(8,128)S(1)}, f32[1,3,64,256]{3,2,1,0:T(8,128)S(1)}, u32[]{:S(2)}, u32[]{:S(2)}) collective-permute-start(f32[1,3,64,256]{3,2,1,0:T(8,128)S(1)} %add.34), channel_id=1, source_target_pairs={{0,16},{2,18},{4,20},{6,22},{8,24},{10,26},{12,28},{14,30},{16,0},... | collective-permute-start | bytes 589832 | tf_op jit(solution)/shard_map/ppermute | solution.py:320
  41.6 8.2 %collective-permute-start.7 = (f32[1,3,64,256]{3,2,1,0:T(8,128)S(1)}, f32[1,3,64,256]{3,2,1,0:T(8,128)S(1)}, u32[]{:S(2)}, u32[]{:S(2)}) collective-permute-start(f32[1,3,64,256]{3,2,1,0:T(8,128)S(1)} %get-tuple-element.130), channel_id=1, source_target_pairs={{0,8},{2,10},{4,12},{6,14},{8,0},{10,2},{12,4},{14,6},{16,24},{18,... | collective-permute-start | bytes 589832 | tf_op jit(solution)/shard_map/ppermute | solution.py:320
  50.4 16.7 %collective-permute-start.11 = (f32[2,256,256]{2,1,0:T(8,128)S(1)}, f32[2,256,256]{2,1,0:T(8,128)S(1)}, u32[]{:S(2)}, u32[]{:S(2)}) collective-permute-start(f32[2,256,256]{2,1,0:T(8,128)S(1)} %get-tuple-element.140), channel_id=1, source_target_pairs={{0,6},{2,4},{4,2},{6,0},{8,14},{10,12},{12,10},{14,8},{16,22},{18,... | collective-permute-start | bytes 1572872 | tf_op jit(solution)/shard_map/ppermute | solution.py:320
  51.5 9.9 %collective-permute-start.13 = (f32[1,3,64,256]{3,2,1,0:T(8,128)S(1)}, f32[1,3,64,256]{3,2,1,0:T(8,128)S(1)}, u32[]{:S(2)}, u32[]{:S(2)}) collective-permute-start(f32[1,3,64,256]{3,2,1,0:T(8,128)S(1)} %add_add_fusion.1.refs_4_), channel_id=1, source_target_pairs={{0,16},{2,18},{4,20},{6,22},{8,24},{10,26},{12,28},{14,30},{16,0},... | collective-permute-start | bytes 589832 | tf_op jit(solution)/shard_map/ppermute | solution.py:320
  53.5 8.2 %collective-permute-start.12 = (f32[1,3,64,256]{3,2,1,0:T(8,128)S(1)}, f32[1,3,64,256]{3,2,1,0:T(8,128)S(1)}, u32[]{:S(2)}, u32[]{:S(2)}) collective-permute-start(f32[1,3,64,256]{3,2,1,0:T(8,128)S(1)} %add_add_fusion.1.refs_4_), channel_id=1, source_target_pairs={{0,8},{2,10},{4,12},{6,14},{8,0},{10,2},{12,4},{14,6},{16,24},{18,... | collective-permute-start | bytes 589832 | tf_op jit(solution)/shard_map/ppermute | solution.py:320
  61.4 5.7 %collective-permute-start.14 = (f32[1,3,64,256]{3,2,1,0:T(8,128)S(1)}, f32[1,3,64,256]{3,2,1,0:T(8,128)S(1)}, u32[]{:S(2)}, u32[]{:S(2)}) collective-permute-start(f32[1,3,64,256]{3,2,1,0:T(8,128)S(1)} %collective-permute-done.13.refs_6_), channel_id=1, source_target_pairs={{0,8},{2,10},{4,12},{6,14},{8,0},{10,2},{12,4},{14,6},{16,24},{18,... | collective-permute-start | bytes 589832 | tf_op jit(solution)/shard_map/ppermute | solution.py:320
  68.9 1.2 collective-permute-start.15
  70.1 4.5 %collective-permute-start.18 = (f32[2,4,256]{2,1,0:T(4,128)S(1)}, f32[2,4,256]{2,1,0:T(4,128)S(1)}, u32[]{:S(2)}, u32[]{:S(2)}) collective-permute-start(f32[2,4,256]{2,1,0:T(4,128)S(1)} %add.36.refs_4_), channel_id=1, source_target_pairs={{0,6},{2,4},{4,2},{6,0},{8,14},{10,12},{12,10},{14,8},{16,22},{18,... | collective-permute-start | bytes 24584 | tf_op jit(solution)/shard_map/ppermute | solution.py:320
  71.4 3.7 %collective-permute-start.17 = (f32[2,4,256]{2,1,0:T(4,128)S(1)}, f32[2,4,256]{2,1,0:T(4,128)S(1)}, u32[]{:S(2)}, u32[]{:S(2)}) collective-permute-start(f32[2,4,256]{2,1,0:T(4,128)S(1)} %add.36.refs_4_), channel_id=1, source_target_pairs={{0,4},{2,6},{4,0},{6,2},{8,12},{10,14},{12,8},{14,10},{16,20},{18,... | collective-permute-start | bytes 24584 | tf_op jit(solution)/shard_map/ppermute | solution.py:320
  72.9 3.7 %collective-permute-start.16 = (f32[2,4,256]{2,1,0:T(4,128)S(1)}, f32[2,4,256]{2,1,0:T(4,128)S(1)}, u32[]{:S(2)}, u32[]{:S(2)}) collective-permute-start(f32[2,4,256]{2,1,0:T(4,128)S(1)} %add.36.refs_4_), channel_id=1, source_target_pairs={{0,2},{2,0},{4,6},{6,4},{8,10},{10,8},{12,14},{14,12},{16,18},{18,... | collective-permute-start | bytes 24584 | tf_op jit(solution)/shard_map/ppermute | solution.py:320
  78.7 5.7 %collective-permute-start.19 = (f32[1,3,64,256]{3,2,1,0:T(8,128)S(1)}, f32[1,3,64,256]{3,2,1,0:T(8,128)S(1)}, u32[]{:S(2)}, u32[]{:S(2)}) collective-permute-start(f32[1,3,64,256]{3,2,1,0:T(8,128)S(1)} %get-tuple-element.159), channel_id=1, source_target_pairs={{0,8},{2,10},{4,12},{6,14},{8,0},{10,2},{12,4},{14,6},{16,24},{18,... | collective-permute-start | bytes 589832 | tf_op jit(solution)/shard_map/ppermute | solution.py:320
  84.4 9.2 %collective-permute-start.21 = (f32[1,3,64,256]{3,2,1,0:T(8,128)S(1)}, f32[1,3,64,256]{3,2,1,0:T(8,128)S(1)}, u32[]{:S(2)}, u32[]{:S(2)}) collective-permute-start(f32[1,3,64,256]{3,2,1,0:T(8,128)S(1)} %add.38), channel_id=1, source_target_pairs={{0,16},{2,18},{4,20},{6,22},{8,24},{10,26},{12,28},{14,30},{16,0},... | collective-permute-start | bytes 589832 | tf_op jit(solution)/shard_map/ppermute | solution.py:320
  85.2 8.4 %collective-permute-start.20 = (f32[1,3,64,256]{3,2,1,0:T(8,128)S(1)}, f32[1,3,64,256]{3,2,1,0:T(8,128)S(1)}, u32[]{:S(2)}, u32[]{:S(2)}) collective-permute-start(f32[1,3,64,256]{3,2,1,0:T(8,128)S(1)} %get-tuple-element.161), channel_id=1, source_target_pairs={{0,8},{2,10},{4,12},{6,14},{8,0},{10,2},{12,4},{14,6},{16,24},{18,... | collective-permute-start | bytes 589832 | tf_op jit(solution)/shard_map/ppermute | solution.py:320
  93.7 9.6 %collective-permute-start.23 = (f32[1,3,64,256]{3,2,1,0:T(8,128)S(1)}, f32[1,3,64,256]{3,2,1,0:T(8,128)S(1)}, u32[]{:S(2)}, u32[]{:S(2)}) collective-permute-start(f32[1,3,64,256]{3,2,1,0:T(8,128)S(1)} %add_add_fusion.refs_11_.refs_0_), channel_id=1, source_target_pairs={{0,16},{2,18},{4,20},{6,22},{8,24},{10,26},{12,28},{14,30},{16,0},... | collective-permute-start | bytes 589832 | tf_op jit(solution)/shard_map/ppermute | solution.py:320
  94.4 10.0 %collective-permute-start.25 = (f32[256,256]{1,0:T(8,128)S(1)}, f32[256,256]{1,0:T(8,128)S(1)}, u32[]{:S(2)}, u32[]{:S(2)}) collective-permute-start(f32[256,256]{1,0:T(8,128)S(1)} %get-tuple-element.165), channel_id=1, source_target_pairs={{0,2},{2,0},{4,6},{6,4},{8,10},{10,8},{12,14},{14,12},{16,18},{18,... | collective-permute-start | bytes 786440 | tf_op jit(solution)/shard_map/ppermute | solution.py:320
  95.2 11.7 %collective-permute-start.26 = (f32[256,256]{1,0:T(8,128)S(1)}, f32[256,256]{1,0:T(8,128)S(1)}, u32[]{:S(2)}, u32[]{:S(2)}) collective-permute-start(f32[256,256]{1,0:T(8,128)S(1)} %get-tuple-element.166), channel_id=1, source_target_pairs={{0,4},{2,6},{4,0},{6,2},{8,12},{10,14},{12,8},{14,10},{16,20},{18,... | collective-permute-start | bytes 786440 | tf_op jit(solution)/shard_map/ppermute | solution.py:320
  96.3 10.5 %collective-permute-start.27 = (f32[256,256]{1,0:T(8,128)S(1)}, f32[256,256]{1,0:T(8,128)S(1)}, u32[]{:S(2)}, u32[]{:S(2)}) collective-permute-start(f32[256,256]{1,0:T(8,128)S(1)} %get-tuple-element.167), channel_id=1, source_target_pairs={{0,6},{2,4},{4,2},{6,0},{8,14},{10,12},{12,10},{14,8},{16,22},{18,... | collective-permute-start | bytes 786440 | tf_op jit(solution)/shard_map/ppermute | solution.py:320
  97.9 10.7 %collective-permute-start.22 = (f32[1,3,64,256]{3,2,1,0:T(8,128)S(1)}, f32[1,3,64,256]{3,2,1,0:T(8,128)S(1)}, u32[]{:S(2)}, u32[]{:S(2)}) collective-permute-start(f32[1,3,64,256]{3,2,1,0:T(8,128)S(1)} %add_add_fusion.refs_11_.refs_0_), channel_id=1, source_target_pairs={{0,8},{2,10},{4,12},{6,14},{8,0},{10,2},{12,4},{14,6},{16,24},{18,... | collective-permute-start | bytes 589832 | tf_op jit(solution)/shard_map/ppermute | solution.py:320
  103.3 6.3 %collective-permute-start.24 = (f32[1,3,64,256]{3,2,1,0:T(8,128)S(1)}, f32[1,3,64,256]{3,2,1,0:T(8,128)S(1)}, u32[]{:S(2)}, u32[]{:S(2)}) collective-permute-start(f32[1,3,64,256]{3,2,1,0:T(8,128)S(1)} %collective-permute-done.23.refs_13_), channel_id=1, source_target_pairs={{0,8},{2,10},{4,12},{6,14},{8,0},{10,2},{12,4},{14,6},{16,24},{18,... | collective-permute-start | bytes 589832 | tf_op jit(solution)/shard_map/ppermute | solution.py:320
  112.8 31.0 %collective-permute-start.28 = (f32[2,256,256]{2,1,0:T(8,128)S(1)}, f32[2,256,256]{2,1,0:T(8,128)S(1)}, u32[]{:S(2)}, u32[]{:S(2)}) collective-permute-start(f32[2,256,256]{2,1,0:T(8,128)S(1)} %get-tuple-element.194), channel_id=1, source_target_pairs={{0,2},{2,0},{4,6},{6,4},{8,10},{10,8},{12,14},{14,12},{16,18},{18,... | collective-permute-start | bytes 1572872 | tf_op jit(solution)/shard_map/ppermute | solution.py:320
  115.2 28.5 %collective-permute-start.29 = (f32[2,256,256]{2,1,0:T(8,128)S(1)}, f32[2,256,256]{2,1,0:T(8,128)S(1)}, u32[]{:S(2)}, u32[]{:S(2)}) collective-permute-start(f32[2,256,256]{2,1,0:T(8,128)S(1)} %get-tuple-element.195), channel_id=1, source_target_pairs={{0,4},{2,6},{4,0},{6,2},{8,12},{10,14},{12,8},{14,10},{16,20},{18,... | collective-permute-start | bytes 1572872 | tf_op jit(solution)/shard_map/ppermute | solution.py:320
  115.3 28.5 %collective-permute-start.30 = (f32[2,256,256]{2,1,0:T(8,128)S(1)}, f32[2,256,256]{2,1,0:T(8,128)S(1)}, u32[]{:S(2)}, u32[]{:S(2)}) collective-permute-start(f32[2,256,256]{2,1,0:T(8,128)S(1)} %get-tuple-element.196), channel_id=1, source_target_pairs={{0,6},{2,4},{4,2},{6,0},{8,14},{10,12},{12,10},{14,8},{16,22},{18,... | collective-permute-start | bytes 1572872 | tf_op jit(solution)/shard_map/ppermute | solution.py:320
  116.8 8.0 %collective-permute-start.32 = (f32[1,3,64,256]{3,2,1,0:T(8,128)S(1)}, f32[1,3,64,256]{3,2,1,0:T(8,128)S(1)}, u32[]{:S(2)}, u32[]{:S(2)}) collective-permute-start(f32[1,3,64,256]{3,2,1,0:T(8,128)S(1)} %get-tuple-element.200), channel_id=1, source_target_pairs={{0,8},{2,10},{4,12},{6,14},{8,0},{10,2},{12,4},{14,6},{16,24},{18,... | collective-permute-start | bytes 589832 | tf_op jit(solution)/shard_map/ppermute | solution.py:320
  118.1 10.4 %collective-permute-start.31 = (f32[1,3,64,256]{3,2,1,0:T(8,128)S(1)}, f32[1,3,64,256]{3,2,1,0:T(8,128)S(1)}, u32[]{:S(2)}, u32[]{:S(2)}) collective-permute-start(f32[1,3,64,256]{3,2,1,0:T(8,128)S(1)} %get-tuple-element.198), channel_id=1, source_target_pairs={{0,8},{2,10},{4,12},{6,14},{8,0},{10,2},{12,4},{14,6},{16,24},{18,... | collective-permute-start | bytes 589832 | tf_op jit(solution)/shard_map/ppermute | solution.py:320
  124.8 8.7 %collective-permute-start.33 = (f32[1,3,64,256]{3,2,1,0:T(8,128)S(1)}, f32[1,3,64,256]{3,2,1,0:T(8,128)S(1)}, u32[]{:S(2)}, u32[]{:S(2)}) collective-permute-start(f32[1,3,64,256]{3,2,1,0:T(8,128)S(1)} %add.40), channel_id=1, source_target_pairs={{0,16},{2,18},{4,20},{6,22},{8,24},{10,26},{12,28},{14,30},{16,0},... | collective-permute-start | bytes 589832 | tf_op jit(solution)/shard_map/ppermute | solution.py:320
  134.1 4.6 %collective-permute-start.34 = (f32[1,3,16,256]{3,2,1,0:T(8,128)S(1)}, f32[1,3,16,256]{3,2,1,0:T(8,128)S(1)}, u32[]{:S(2)}, u32[]{:S(2)}) collective-permute-start(f32[1,3,16,256]{3,2,1,0:T(8,128)S(1)} %get-tuple-element.202), channel_id=1, source_target_pairs={{0,2},{2,0},{4,6},{6,4},{8,10},{10,8},{12,14},{14,12},{16,18},{18,... | collective-permute-start | bytes 147464 | tf_op jit(solution)/shard_map/ppermute | solution.py:320
  135.6 4.6 %collective-permute-start.35 = (f32[1,3,16,256]{3,2,1,0:T(8,128)S(1)}, f32[1,3,16,256]{3,2,1,0:T(8,128)S(1)}, u32[]{:S(2)}, u32[]{:S(2)}) collective-permute-start(f32[1,3,16,256]{3,2,1,0:T(8,128)S(1)} %get-tuple-element.203), channel_id=1, source_target_pairs={{0,4},{2,6},{4,0},{6,2},{8,12},{10,14},{12,8},{14,10},{16,20},{18,... | collective-permute-start | bytes 147464 | tf_op jit(solution)/shard_map/ppermute | solution.py:320
  138.8 5.0 %collective-permute-start.36 = (f32[1,3,16,256]{3,2,1,0:T(8,128)S(1)}, f32[1,3,16,256]{3,2,1,0:T(8,128)S(1)}, u32[]{:S(2)}, u32[]{:S(2)}) collective-permute-start(f32[1,3,16,256]{3,2,1,0:T(8,128)S(1)} %get-tuple-element.204), channel_id=1, source_target_pairs={{0,6},{2,4},{4,2},{6,0},{8,14},{10,12},{12,10},{14,8},{16,22},{18,... | collective-permute-start | bytes 147464 | tf_op jit(solution)/shard_map/ppermute | solution.py:320

commit v13 on v12

--- a/solution.py
+++ b/solution.py
@@ -84,6 +84,22 @@
     split_kernel(groups, place, cot, *[out.at[1] for out in outs], scratch)
     for step in range(groups):
         outs[step][1] *= gain[pl.ds(place[0] ^ step, 1), :]
+
+
+def packing(groups):
+    if groups == 4:
+        return [[(0, 0), (0, 1)], [(1, 0), (1, 1), (3, 0)], [(2, 0), (2, 1), (3, 1)]]
+    return [[(step, 0), (step, 1)] for step in range(groups)]
+
+
+def unpacked(groups, refs):
+    found = {}
+    for ref, members in zip(refs, packing(groups)):
+        for i, member in enumerate(members):
+            found[member] = ref.at[i]
+    for i, ref in enumerate(refs[len(packing(groups)) :]):
+        found[(groups - 1, i)] = ref
+    return [(found[(step, 0)], found[(step, 1)]) for step in range(groups)]
 
 
 def rate_column(r, head):
@@ -235,7 +251,8 @@
     dact_r, third_r, activ_r, deriv_r, slope_r, second_r, dfirst_r, dthird_r, act_r = kept
     parts, refs = refs[:depth], refs[depth:]
     w_gate, w_out, w_up = refs[:3]
-    outs, slices = refs[3 : groups + 3], refs[groups + 3 : -2]
+    packed = len(packing(groups))
+    outs, slices = unpacked(groups, refs[3 : packed + 3]), refs[packed + 3 : -2]
     whole, sums = refs[-2:]
     assemble(place, parts, whole)
     gate_b, out_b, up_b = (w[...].astype(BF16) for w in (w_gate, w_out, w_up))
@@ -252,13 +269,13 @@
         bar_df_dact = bar_dfirst * dact
         bar_third = (bar_df_dact * deriv + bar_act * activ).astype(BF16)
         bar_first = (bar_activ * deriv + bar_df_dact * second_r[step]).astype(BF16)
-        outs[step][0] = (
+        outs[step][0][...] = (
             mm_t(dfirst_r[step], cot_gate)
             + mm_t(dthird_r[step], cot_up)
             + mm_t(bar_first, gate_b)
             + mm_t(bar_third, up_b)
         )
-        outs[step][1] = mm(act_r[step], cot_out) + mm(bar_dact, out_b)
+        outs[step][1][...] = mm(act_r[step], cot_out) + mm(bar_dact, out_b)
         total[0] += tmm(keys, bar_first)
         total[1] += tmm(bar_dact, scaled)
         total[2] += tmm(keys, bar_third)
@@ -276,14 +293,13 @@
 
 
 def join_update_kernel(groups, place, r, *refs):
-    pieces, parts = refs[:groups], refs[groups : 2 * groups]
-    out_k, out_v = refs[2 * groups : 2 * groups + 2]
-    grads, (sk, sv) = refs[2 * groups + 2 : -2], refs[-2:]
+    (out_k, out_v, *grads), (sk, sv) = refs[-7:-2], refs[-2:]
+    pieces, parts = unpacked(groups, refs[: -7 - groups]), refs[-7 - groups : -7]
     tokens, heads, width = out_k.shape
     for step, piece in enumerate(pieces):
         head = place[0] ^ step
-        put_head(sk, head, piece[0], tokens, heads)
-        put_head(sv, head, piece[1] * rate_column(r, head), tokens, heads)
+        put_head(sk, head, piece[0][...], tokens, heads)
+        put_head(sv, head, piece[1][...] * rate_column(r, head), tokens, heads)
         for i, grad in enumerate(grads):
             grad[head] = parts[step][0, i]
     out_k[...] = rows_of(sk).reshape(tokens, heads, width).astype(BF16)
@@ -325,12 +341,11 @@
     def forwarded(got):
         return [got[:1]] if got.shape[0] == 1 else [got[i : i + 1] for i in range(got.shape[0])]
 
-    def scatter(outs, count, unit, one_by_one=True):
+    def scatter(outs, count, unit):
         outs = list(outs)
         evens = list(range(2, count, 2))
         via = forwarded(move(outs.pop(0), "ctx", unit)) if evens else []
-        if one_by_one:
-            via, outs[0] = after(via, outs[0])
+        via, outs[0] = after(via, outs[0])
         first = [move(outs[0], "ctx", unit)] if count > 1 else []
         even = [move(p + v, "ctx", r * unit) for p, v, r in zip(outs[1:], via, evens)]
         return [outs[-1]] + first + even
@@ -417,11 +432,15 @@
     rows = hidden // depth
     out = call(
         functools.partial(update_back_kernel, groups, depth, scale),
-        [shape(2, tokens, width)] * groups + slices, [square] * 2, 12 * flops,
+        [kept(len(members)) for members in packing(groups)] + slices, [square] * 2, 12 * flops,
         place, *early, *saved, *parts, *own, mib=24,
     )
-    back = in_plane(out[:groups])
-    ends = scatter(out[groups:], depth, groups, one_by_one=False)
+    packed = len(packing(groups))
+    back = in_plane(out[:packed])
+    ends = scatter(out[packed:], depth, groups)
+    if groups == 4:
+        ends, back = after(ends, back)
+        back += [move(back[1][2], "ctx", 2), move(back[2][2], "ctx", 1)]
     own_rows = rows // groups
     sent = call(
         functools.partial(rows_kernel, groups),

time: 146 us -> 146 us (level)
  waiting for transfers between devices: 78.4 us -> 76.4 us
  starting transfers between devices: 43.5 us -> 45.1 us
    ppermute x37 -> x38, waiting for transfers between devices: 78.4 us -> 76.4 us  [move(): lax.ppermute(x, axis, [(c, c ^ step) for c in range(lax.axis_size(axis))])]
    ppermute x37 -> x38, starting transfers between devices: 43.5 us -> 45.1 us  [move(): lax.ppermute(x, axis, [(c, c ^ step) for c in range(lax.axis_size(axis))])]
  transfers between devices with their start and end apart: 37 -> 38, of which waited for: 25 -> 26; matrix products, arithmetic and copies ran while one was open for 1% -> 1% of each run, Pallas kernels for 5% -> 5%
where the time goes in v13:
time: 146 us
  waiting for transfers between devices  76.4 us (52%)
  starting transfers between devices  45.1 us (31%)
  Pallas kernels  19.5 us (13%)
  local copies, waits for them, and re-layouts  3.56 us (2%)
    ppermute x38, waiting for transfers between devices, move(): lax.ppermute(x, axis, [(c, c ^ step) for c in range(lax.axis_size(axis))])  76.4 us
    ppermute x38, starting transfers between devices, move(): lax.ppermute(x, axis, [(c, c ^ step) for c in range(lax.axis_size(axis))])  45.1 us
    pallas_call x11, Pallas kernels, call(): pl.pallas_call(body, out_shape=out_shape, in_specs=[smem if a.dtype == jn...  19.5 us
  transfers between devices with their start and end apart: 38, of which 26 were waited for; matrix products, arithmetic and copies ran while one was open for 1% of the time, Pallas kernels for 5%

profile of v13, /device:TPU:0, one launch (start us, length us, event | category | flops | bytes accessed | tf_op | source)
XLA Modules:
  0.0 145.6 jit_solution(13546064829785290833)
XLA Ops:
  0.7 1.1 copy-done.5
  1.8 0.9 shard_map.145
  2.8 3.0 %collective-permute-start = (f32[256,256]{1,0:T(8,128)S(1)}, f32[256,256]{1,0:T(8,128)S(1)}, u32[]{:S(2)}, u32[]{:S(2)}) collective-permute-start(f32[256,256]{1,0:T(8,128)S(1)} %get-tuple-element.116), channel_id=1, source_target_pairs={{0,2},{2,0},{4,6},{6,4},{8,10},{10,8},{12,14},{14,12},{16,18},{18,... | collective-permute-start | bytes 786440 | tf_op jit(solution)/shard_map/ppermute | solution.py:336
  5.8 1.5 %collective-permute-start.1 = (f32[256,256]{1,0:T(8,128)S(1)}, f32[256,256]{1,0:T(8,128)S(1)}, u32[]{:S(2)}, u32[]{:S(2)}) collective-permute-start(f32[256,256]{1,0:T(8,128)S(1)} %get-tuple-element.117), channel_id=1, source_target_pairs={{0,4},{2,6},{4,0},{6,2},{8,12},{10,14},{12,8},{14,10},{16,20},{18,... | collective-permute-start | bytes 786440 | tf_op jit(solution)/shard_map/ppermute | solution.py:336
  7.3 1.8 %shard_map.146 = (bf16[256,256]{1,0:T(8,128)(2,1)S(1)}, f32[256,256]{1,0:T(8,128)}, f32[256,256]{1,0:T(8,128)}, f32[256,256]{1,0:T(8,128)S(1)}) custom-call(s32[2]{0:T(128)S(1)} %pad_add_fusion.place, bf16[256,4,256]{2,1,0:T(4,128)(2,1)S(1)} %bitcast.26, f32[4,256]{1,0:T(4,128)S(1)} %bitcast.23), custom_call_target="tpu_custom_call" | custom-call | flops 2147483648 | bytes 1445896 | tf_op jit(solution)/shard_map/pallas_call | solution.py:34
  9.1 0.7 copy-done.7
  9.8 1.9 %collective-permute-start.3 = (f32[256,256]{1,0:T(8,128)}, f32[256,256]{1,0:T(8,128)S(1)}, u32[]{:S(2)}, u32[]{:S(2)}) collective-permute-start(f32[256,256]{1,0:T(8,128)} %get-tuple-element.120), channel_id=1, source_target_pairs={{0,2},{2,0},{4,6},{6,4},{8,10},{10,8},{12,14},{14,12},{16,18},{18,... | collective-permute-start | bytes 786440 | tf_op jit(solution)/shard_map/ppermute | solution.py:336
  11.7 1.5 %collective-permute-start.4 = (f32[256,256]{1,0:T(8,128)}, f32[256,256]{1,0:T(8,128)S(1)}, u32[]{:S(2)}, u32[]{:S(2)}) collective-permute-start(f32[256,256]{1,0:T(8,128)} %get-tuple-element.121), channel_id=1, source_target_pairs={{0,4},{2,6},{4,0},{6,2},{8,12},{10,14},{12,8},{14,10},{16,20},{18,... | collective-permute-start | bytes 786440 | tf_op jit(solution)/shard_map/ppermute | solution.py:336
  13.2 2.7 %collective-permute-start.5 = (f32[256,256]{1,0:T(8,128)S(1)}, f32[256,256]{1,0:T(8,128)S(1)}, u32[]{:S(2)}, u32[]{:S(2)}) collective-permute-start(f32[256,256]{1,0:T(8,128)S(1)} %get-tuple-element.122), channel_id=1, source_target_pairs={{0,6},{2,4},{4,2},{6,0},{8,14},{10,12},{12,10},{14,8},{16,22},{18,... | collective-permute-start | bytes 786440 | tf_op jit(solution)/shard_map/ppermute | solution.py:336
  15.9 1.1 dynamic-slice_bitcast_fusion
  17.1 2.7 %collective-permute-done.1.refs_2_ = f32[256,256]{1,0:T(8,128)S(1)} collective-permute-done((f32[256,256]{1,0:T(8,128)S(1)}, f32[256,256]{1,0:T(8,128)S(1)}, u32[]{:S(2)}, u32[]{:S(2)}) %collective-permute-start.1) | collective-permute-done | bytes 262176 | tf_op jit(solution)/shard_map/ppermute | solution.py:336
  20.1 4.1 %collective-permute-done.3.refs_5_ = f32[256,256]{1,0:T(8,128)S(1)} collective-permute-done((f32[256,256]{1,0:T(8,128)}, f32[256,256]{1,0:T(8,128)S(1)}, u32[]{:S(2)}, u32[]{:S(2)}) %collective-permute-start.3) | collective-permute-done | bytes 262176 | tf_op jit(solution)/shard_map/ppermute | solution.py:336
  24.2 6.2 %collective-permute-done.4.refs_6_ = f32[256,256]{1,0:T(8,128)S(1)} collective-permute-done((f32[256,256]{1,0:T(8,128)}, f32[256,256]{1,0:T(8,128)S(1)}, u32[]{:S(2)}, u32[]{:S(2)}) %collective-permute-start.4) | collective-permute-done | bytes 262176 | tf_op jit(solution)/shard_map/ppermute | solution.py:336
  30.4 2.2 %shard_map.148 = (bf16[4,256,256]{2,1,0:T(8,128)(2,1)S(1)}, bf16[4,256,256]{2,1,0:T(8,128)(2,1)S(1)}, f32[1,3,64,256]{3,2,1,0:T(8,128)S(1)}, f32[1,3,64,256]{3,2...) custom-call(s32[2]{0:T(128)S(1)} %pad_add_fusion.place, ...), custom_call_target="tpu_custom_call" | custom-call | flops 805306368 | bytes 4456456 | tf_op jit(solution)/shard_map/pallas_call | solution.py:34
  32.6 1.6 %collective-permute-start.6 = (f32[1,3,64,256]{3,2,1,0:T(8,128)S(1)}, f32[1,3,64,256]{3,2,1,0:T(8,128)S(1)}, u32[]{:S(2)}, u32[]{:S(2)}) collective-permute-start(f32[1,3,64,256]{3,2,1,0:T(8,128)S(1)} %get-tuple-element.135), channel_id=1, source_target_pairs={{0,8},{2,10},{4,12},{6,14},{8,0},{10,2},{12,4},{14,6},{16,24},{18,... | collective-permute-start | bytes 589832 | tf_op jit(solution)/shard_map/ppermute | solution.py:336
  34.9 1.9 %shard_map.147 = (f32[2,256,256]{2,1,0:T(8,128)S(1)}, f32[2,256,256]{2,1,0:T(8,128)S(1)}, f32[2,256,256]{2,1,0:T(8,128)S(1)}, f32[2,256,256]{2,1,0:T(8,128)S(1)}, f32[8,256]{1,0:T(8,128)S(1)}) custom-call(s32[2]{0:T(128)S(1)} %pad_add_fusion.place, bf16[256,4,256]{2,1,0:T(4,128)(2,1)S(1)} %bitcast.21, bf16[256,4,256]{2,1,0:T(4,128)(2,1)S(1)} %bitcast.22, ...), custom_call_target="tpu_custom_call" | custom-call | flops 16777216 | bytes 3158028 | tf_op jit(solution)/shard_map/pallas_call | solution.py:34
  36.8 1.3 collective-permute-start.9
  38.1 0.8 collective-permute-start.10
  39.0 2.7 %collective-permute-start.8 = (f32[1,3,64,256]{3,2,1,0:T(8,128)S(1)}, f32[1,3,64,256]{3,2,1,0:T(8,128)S(1)}, u32[]{:S(2)}, u32[]{:S(2)}) collective-permute-start(f32[1,3,64,256]{3,2,1,0:T(8,128)S(1)} %add.34), channel_id=1, source_target_pairs={{0,16},{2,18},{4,20},{6,22},{8,24},{10,26},{12,28},{14,30},{16,0},... | collective-permute-start | bytes 589832 | tf_op jit(solution)/shard_map/ppermute | solution.py:336
  41.6 1.0 collective-permute-start.7
  42.6 6.4 %collective-permute-done.8 = f32[1,3,64,256]{3,2,1,0:T(8,128)S(1)} collective-permute-done((f32[1,3,64,256]{3,2,1,0:T(8,128)S(1)}, f32[1,3,64,256]{3,2,1,0:T(8,128)S(1)}, u32[]{:S(2)}, u32[]{:S(2)}) %collective-permute-start.8) | collective-permute-done | bytes 196640 | tf_op jit(solution)/shard_map/ppermute | solution.py:336
  49.0 0.9 collective-permute-done.7
  50.4 1.1 collective-permute-start.11
  51.5 2.0 %collective-permute-start.13 = (f32[1,3,64,256]{3,2,1,0:T(8,128)S(1)}, f32[1,3,64,256]{3,2,1,0:T(8,128)S(1)}, u32[]{:S(2)}, u32[]{:S(2)}) collective-permute-start(f32[1,3,64,256]{3,2,1,0:T(8,128)S(1)} %add_add_fusion.1.refs_4_), channel_id=1, source_target_pairs={{0,16},{2,18},{4,20},{6,22},{8,24},{10,26},{12,28},{14,30},{16,0},... | collective-permute-start | bytes 589832 | tf_op jit(solution)/shard_map/ppermute | solution.py:336
  53.5 0.8 collective-permute-start.12
  54.3 7.0 %collective-permute-done.13.refs_6_ = f32[1,3,64,256]{3,2,1,0:T(8,128)S(1)} collective-permute-done((f32[1,3,64,256]{3,2,1,0:T(8,128)S(1)}, f32[1,3,64,256]{3,2,1,0:T(8,128)S(1)}, u32[]{:S(2)}, u32[]{:S(2)}) %collective-permute-start.13) | collective-permute-done | bytes 196640 | tf_op jit(solution)/shard_map/ppermute | solution.py:336
  61.6 5.5 %collective-permute-done.14.refs_7_ = f32[1,3,64,256]{3,2,1,0:T(8,128)S(1)} collective-permute-done((f32[1,3,64,256]{3,2,1,0:T(8,128)S(1)}, f32[1,3,64,256]{3,2,1,0:T(8,128)S(1)}, u32[]{:S(2)}, u32[]{:S(2)}) %collective-permute-start.14) | collective-permute-done | bytes 196640 | tf_op jit(solution)/shard_map/ppermute | solution.py:336
  67.1 1.8 %shard_map.149 = (f32[4,256,256]{2,1,0:T(8,128)S(1)}, f32[4,256,256]{2,1,0:T(8,128)S(1)}, bf16[4,256,256]{2,1,0:T(8,128)(2,1)S(1)}, f32[4,256,256]{2,1,0:T(8,128...) custom-call(s32[2]{0:T(128)S(1)} %pad_add_fusion.place, f32[8,256]{1,0:T(8,128)S(1)} %get-tuple-element.125.scale_row, ...), custom_call_target="tpu_custom_call" | custom-call | flops 402653184 | bytes 6963208 | tf_op jit(solution)/shard_map/pallas_call | solution.py:34
  68.9 1.2 collective-permute-done.15
  70.1 1.4 collective-permute-start.18
  71.5 1.5 %collective-permute-start.17 = (f32[2,4,256]{2,1,0:T(4,128)S(1)}, f32[2,4,256]{2,1,0:T(4,128)S(1)}, u32[]{:S(2)}, u32[]{:S(2)}) collective-permute-start(f32[2,4,256]{2,1,0:T(4,128)S(1)} %add.36.refs_4_), channel_id=1, source_target_pairs={{0,4},{2,6},{4,0},{6,2},{8,12},{10,14},{12,8},{14,10},{16,20},{18,... | collective-permute-start | bytes 24584 | tf_op jit(solution)/shard_map/ppermute | solution.py:336
  72.9 0.6 collective-permute-start.16
  73.6 1.1 collective-permute-done.18.refs_7_
  75.1 1.5 %collective-permute-done.16.refs_5_ = f32[2,4,256]{2,1,0:T(4,128)S(1)} collective-permute-done((f32[2,4,256]{2,1,0:T(4,128)S(1)}, f32[2,4,256]{2,1,0:T(4,128)S(1)}, u32[]{:S(2)}, u32[]{:S(2)}) %collective-permute-start.16) | collective-permute-done | bytes 8224 | tf_op jit(solution)/shard_map/ppermute | solution.py:336
  76.6 2.1 %shard_map.150 = (f32[256,256]{1,0:T(8,128)S(1)}, f32[256,256]{1,0:T(8,128)S(1)}, f32[256,256]{1,0:T(8,128)S(1)}, f32[256,256]{1,0:T(8,128)S(1)}, f32[1,3,64,256...) custom-call(s32[2]{0:T(128)S(1)} %pad_add_fusion.place, ...), custom_call_target="tpu_custom_call" | custom-call | flops 805306368 | bytes 8036360 | tf_op jit(solution)/shard_map/pallas_call | solution.py:34
  79.0 5.4 %collective-permute-done.19 = f32[1,3,64,256]{3,2,1,0:T(8,128)S(1)} collective-permute-done((f32[1,3,64,256]{3,2,1,0:T(8,128)S(1)}, f32[1,3,64,256]{3,2,1,0:T(8,128)S(1)}, u32[]{:S(2)}, u32[]{:S(2)}) %collective-permute-start.19) | collective-permute-done | bytes 196640 | tf_op jit(solution)/shard_map/ppermute | solution.py:336
  84.5 0.7 collective-permute-start.21
  85.2 1.9 %collective-permute-start.20 = (f32[1,3,64,256]{3,2,1,0:T(8,128)S(1)}, f32[1,3,64,256]{3,2,1,0:T(8,128)S(1)}, u32[]{:S(2)}, u32[]{:S(2)}) collective-permute-start(f32[1,3,64,256]{3,2,1,0:T(8,128)S(1)} %get-tuple-element.168), channel_id=1, source_target_pairs={{0,8},{2,10},{4,12},{6,14},{8,0},{10,2},{12,4},{14,6},{16,24},{18,... | collective-permute-start | bytes 589832 | tf_op jit(solution)/shard_map/ppermute | solution.py:336
  87.1 6.6 %collective-permute-done.21 = f32[1,3,64,256]{3,2,1,0:T(8,128)S(1)} collective-permute-done((f32[1,3,64,256]{3,2,1,0:T(8,128)S(1)}, f32[1,3,64,256]{3,2,1,0:T(8,128)S(1)}, u32[]{:S(2)}, u32[]{:S(2)}) %collective-permute-start.21) | collective-permute-done | bytes 196640 | tf_op jit(solution)/shard_map/ppermute | solution.py:336
  93.7 0.7 collective-permute-start.23
  94.4 0.8 collective-permute-start.25
  95.2 1.2 collective-permute-start.26
  96.4 1.6 %collective-permute-start.27 = (f32[256,256]{1,0:T(8,128)S(1)}, f32[256,256]{1,0:T(8,128)S(1)}, u32[]{:S(2)}, u32[]{:S(2)}) collective-permute-start(f32[256,256]{1,0:T(8,128)S(1)} %get-tuple-element.174), channel_id=1, source_target_pairs={{0,6},{2,4},{4,2},{6,0},{8,14},{10,12},{12,10},{14,8},{16,22},{18,... | collective-permute-start | bytes 786440 | tf_op jit(solution)/shard_map/ppermute | solution.py:336
  97.9 1.8 %collective-permute-start.22 = (f32[1,3,64,256]{3,2,1,0:T(8,128)S(1)}, f32[1,3,64,256]{3,2,1,0:T(8,128)S(1)}, u32[]{:S(2)}, u32[]{:S(2)}) collective-permute-start(f32[1,3,64,256]{3,2,1,0:T(8,128)S(1)} %add_add_fusion.refs_11_.refs_0_), channel_id=1, source_target_pairs={{0,8},{2,10},{4,12},{6,14},{8,0},{10,2},{12,4},{14,6},{16,24},{18,... | collective-permute-start | bytes 589832 | tf_op jit(solution)/shard_map/ppermute | solution.py:336
  99.7 3.7 %collective-permute-done.23.refs_13_ = f32[1,3,64,256]{3,2,1,0:T(8,128)S(1)} collective-permute-done((f32[1,3,64,256]{3,2,1,0:T(8,128)S(1)}, f32[1,3,64,256]{3,2,1,0:T(8,128)S(1)}, u32[]{:S(2)}, u32[]{:S(2)}) %collective-permute-start.23) | collective-permute-done | bytes 196640 | tf_op jit(solution)/shard_map/ppermute | solution.py:336
  103.3 1.0 shard_map.152
  104.4 2.5 %collective-permute-done.26.refs_2_ = f32[256,256]{1,0:T(8,128)S(1)} collective-permute-done((f32[256,256]{1,0:T(8,128)S(1)}, f32[256,256]{1,0:T(8,128)S(1)}, u32[]{:S(2)}, u32[]{:S(2)}) %collective-permute-start.26) | collective-permute-done | bytes 262176 | tf_op jit(solution)/shard_map/ppermute | solution.py:336
  106.9 1.7 %shard_map.151 = bf16[256,4,256]{2,1,0:T(4,128)(2,1)} custom-call(s32[2]{0:T(128)S(1)} %pad_add_fusion.place, f32[256,256]{1,0:T(8,128)S(1)} %get-tuple-element.171.refs_0_, f32[256,256]{1,0:T(8,128)S(1)} %collective-permute-done.25.refs_1_, f32[256,256]{1,0:T(8,128)S(1)} %collective-permute-done.26.refs_2_, f32[256,256]{1,0:T(8,128)S(1)} %collective-permute-done.27.refs_3_), custom_call_target="tpu_custom_call" | custom-call | flops 8388608 | bytes 1572872 | tf_op jit(solution)/shard_map/pallas_call | solution.py:34
  108.6 1.0 collective-permute-done.24.refs_14_
  109.6 3.0 %shard_map.153 = (f32[2,256,256]{2,1,0:T(8,128)S(1)}, f32[3,256,256]{2,1,0:T(8,128)S(1)}, f32[3,256,256]{2,1,0:T(8,128)S(1)}, f32[1,3,64,256]{3,2,1,0:T(8,128)S(...) custom-call(s32[2]{0:T(128)S(1)} %pad_add_fusion.place, ...), custom_call_target="tpu_custom_call" | custom-call | flops 1610612736 | bytes 13369352 | tf_op jit(solution)/shard_map/pallas_call | solution.py:34
  112.6 2.5 %collective-permute-start.31 = (f32[3,256,256]{2,1,0:T(8,128)S(1)}, f32[3,256,256]{2,1,0:T(8,128)S(1)}, u32[]{:S(2)}, u32[]{:S(2)}) collective-permute-start(f32[3,256,256]{2,1,0:T(8,128)S(1)} %get-tuple-element.207), channel_id=1, source_target_pairs={{0,2},{2,0},{4,6},{6,4},{8,10},{10,8},{12,14},{14,12},{16,18},{18,... | collective-permute-start | bytes 2359304 | tf_op jit(solution)/shard_map/ppermute | solution.py:336
  115.2 1.4 collective-permute-start.28
  116.6 4.2 %collective-permute-done.28 = f32[1,3,64,256]{3,2,1,0:T(8,128)S(1)} collective-permute-done((f32[1,3,64,256]{3,2,1,0:T(8,128)S(1)}, f32[1,3,64,256]{3,2,1,0:T(8,128)S(1)}, u32[]{:S(2)}, u32[]{:S(2)}) %collective-permute-start.28) | collective-permute-done | bytes 196640 | tf_op jit(solution)/shard_map/ppermute | solution.py:336
  120.9 1.1 collective-permute-start.30
  122.0 0.9 collective-permute-start.29
  123.0 7.5 %collective-permute-done.30.refs_3_ = f32[1,3,64,256]{3,2,1,0:T(8,128)S(1)} collective-permute-done((f32[1,3,64,256]{3,2,1,0:T(8,128)S(1)}, f32[1,3,64,256]{3,2,1,0:T(8,128)S(1)}, u32[]{:S(2)}, u32[]{:S(2)}) %collective-permute-start.30) | collective-permute-done | bytes 196640 | tf_op jit(solution)/shard_map/ppermute | solution.py:336
  130.5 1.4 collective-permute-done.31.refs_1_
  131.9 1.5 %collective-permute-done.32.refs_2_ = f32[3,256,256]{2,1,0:T(8,128)S(1)} collective-permute-done((f32[3,256,256]{2,1,0:T(8,128)S(1)}, f32[3,256,256]{2,1,0:T(8,128)S(1)}, u32[]{:S(2)}, u32[]{:S(2)}) %collective-permute-start.32) | collective-permute-done | bytes 786464 | tf_op jit(solution)/shard_map/ppermute | solution.py:336
  134.4 0.6 shard_map.154
  135.0 1.4 collective-permute-start.35
  136.5 1.7 %collective-permute-start.36 = (f32[1,3,16,256]{3,2,1,0:T(8,128)S(1)}, f32[1,3,16,256]{3,2,1,0:T(8,128)S(1)}, u32[]{:S(2)}, u32[]{:S(2)}) collective-permute-start(f32[1,3,16,256]{3,2,1,0:T(8,128)S(1)} %get-tuple-element.217), channel_id=1, source_target_pairs={{0,4},{2,6},{4,0},{6,2},{8,12},{10,14},{12,8},{14,10},{16,20},{18,... | collective-permute-start | bytes 147464 | tf_op jit(solution)/shard_map/ppermute | solution.py:336
  138.6 2.6 %collective-permute-done.35.refs_6_ = f32[1,3,16,256]{3,2,1,0:T(8,128)S(1)} collective-permute-done((f32[1,3,16,256]{3,2,1,0:T(8,128)S(1)}, f32[1,3,16,256]{3,2,1,0:T(8,128)S(1)}, u32[]{:S(2)}, u32[]{:S(2)}) %collective-permute-start.35) | collective-permute-done | bytes 49184 | tf_op jit(solution)/shard_map/ppermute | solution.py:336
  141.6 1.7 %collective-permute-done.37.refs_8_ = f32[1,3,16,256]{3,2,1,0:T(8,128)S(1)} collective-permute-done((f32[1,3,16,256]{3,2,1,0:T(8,128)S(1)}, f32[1,3,16,256]{3,2,1,0:T(8,128)S(1)}, u32[]{:S(2)}, u32[]{:S(2)}) %collective-permute-start.37) | collective-permute-done | bytes 49184 | tf_op jit(solution)/shard_map/ppermute | solution.py:336
  143.2 2.4 %shard_map.155 = (bf16[256,4,256]{2,1,0:T(4,128)(2,1)}, bf16[256,4,256]{2,1,0:T(4,128)(2,1)}, f32[4,16,256]{2,1,0:T(8,128)}, f32[4,16,256]{2,1,0:T(8,128)}, f32[4,16,256]{2,1,0:T(8,128)}) custom-call(s32[2]{0:T(128)S(1)} %pad_add_fusion.place, f32[4,256]{1,0:T(4,128)S(1)} %bitcast.24, f32[2,256,256]{2,1,0:T(8,128)S(1)} %get-tuple-element.209.refs_0_, ...), custom_call_target="tpu_custom_call" | custom-call | flops 16777216 | bytes 4067336 | tf_op jit(solution)/shard_map/pallas_call | solution.py:34
  (55 shorter events, 4.7 us)
Async XLA Ops:
  0.6 15.3 %copy-start = (f32[4,256,256]{2,1,0:T(8,128)S(1)}, f32[4,256,256]{2,1,0:T(8,128)}, u32[]{:S(2)}) copy-start(f32[4,256,256]{2,1,0:T(8,128)} %param.16) | copy-start | bytes 3145732
  0.7 1.1 copy-start.5
  1.8 5.5 %copy-start.6 = (bf16[1,256,4,256]{3,2,1,0:T(4,128)(2,1)S(1)}, bf16[1,256,4,256]{3,2,1,0:T(4,128)(2,1)}, u32[]{:S(2)}) copy-start(bf16[1,256,4,256]{3,2,1,0:T(4,128)(2,1)} %param.12) | copy-start | bytes 1572868
  2.7 4.6 %copy-start.4 = (f32[1,4,256]{2,1,0:T(4,128)S(1)}, f32[1,4,256]{2,1,0:T(4,128)}, u32[]{:S(2)}) copy-start(f32[1,4,256]{2,1,0:T(4,128)} %param.13) | copy-start | bytes 12292
  2.8 10.5 %collective-permute-start = (f32[256,256]{1,0:T(8,128)S(1)}, f32[256,256]{1,0:T(8,128)S(1)}, u32[]{:S(2)}, u32[]{:S(2)}) collective-permute-start(f32[256,256]{1,0:T(8,128)S(1)} %get-tuple-element.116), channel_id=1, source_target_pairs={{0,2},{2,0},{4,6},{6,4},{8,10},{10,8},{12,14},{14,12},{16,18},{18,... | collective-permute-start | bytes 786440 | tf_op jit(solution)/shard_map/ppermute | solution.py:336
  5.8 14.0 %collective-permute-start.1 = (f32[256,256]{1,0:T(8,128)S(1)}, f32[256,256]{1,0:T(8,128)S(1)}, u32[]{:S(2)}, u32[]{:S(2)}) collective-permute-start(f32[256,256]{1,0:T(8,128)S(1)} %get-tuple-element.117), channel_id=1, source_target_pairs={{0,4},{2,6},{4,0},{6,2},{8,12},{10,14},{12,8},{14,10},{16,20},{18,... | collective-permute-start | bytes 786440 | tf_op jit(solution)/shard_map/ppermute | solution.py:336
  7.3 12.8 %collective-permute-start.2 = (f32[256,256]{1,0:T(8,128)S(1)}, f32[256,256]{1,0:T(8,128)S(1)}, u32[]{:S(2)}, u32[]{:S(2)}) collective-permute-start(f32[256,256]{1,0:T(8,128)S(1)} %get-tuple-element.118), channel_id=1, source_target_pairs={{0,6},{2,4},{4,2},{6,0},{8,14},{10,12},{12,10},{14,8},{16,22},{18,... | collective-permute-start | bytes 786440 | tf_op jit(solution)/shard_map/ppermute | solution.py:336
  9.1 0.7 copy-start.7
  9.8 14.4 %collective-permute-start.3 = (f32[256,256]{1,0:T(8,128)}, f32[256,256]{1,0:T(8,128)S(1)}, u32[]{:S(2)}, u32[]{:S(2)}) collective-permute-start(f32[256,256]{1,0:T(8,128)} %get-tuple-element.120), channel_id=1, source_target_pairs={{0,2},{2,0},{4,6},{6,4},{8,10},{10,8},{12,14},{14,12},{16,18},{18,... | collective-permute-start | bytes 786440 | tf_op jit(solution)/shard_map/ppermute | solution.py:336
  11.7 18.7 %collective-permute-start.4 = (f32[256,256]{1,0:T(8,128)}, f32[256,256]{1,0:T(8,128)S(1)}, u32[]{:S(2)}, u32[]{:S(2)}) collective-permute-start(f32[256,256]{1,0:T(8,128)} %get-tuple-element.121), channel_id=1, source_target_pairs={{0,4},{2,6},{4,0},{6,2},{8,12},{10,14},{12,8},{14,10},{16,20},{18,... | collective-permute-start | bytes 786440 | tf_op jit(solution)/shard_map/ppermute | solution.py:336
  13.2 17.1 %collective-permute-start.5 = (f32[256,256]{1,0:T(8,128)S(1)}, f32[256,256]{1,0:T(8,128)S(1)}, u32[]{:S(2)}, u32[]{:S(2)}) collective-permute-start(f32[256,256]{1,0:T(8,128)S(1)} %get-tuple-element.122), channel_id=1, source_target_pairs={{0,6},{2,4},{4,2},{6,0},{8,14},{10,12},{12,10},{14,8},{16,22},{18,... | collective-permute-start | bytes 786440 | tf_op jit(solution)/shard_map/ppermute | solution.py:336
  15.9 14.5 %copy-start.8 = (bf16[256,256]{1,0:T(8,128)(2,1)S(1)}, bf16[256,256]{1,0:T(8,128)(2,1)}, u32[]{:S(2)}) copy-start(bf16[256,256]{1,0:T(8,128)(2,1)} %copy-done.7) | copy-start | bytes 393220
  30.4 4.5 %copy-start.1 = (bf16[1,256,4,256]{3,2,1,0:T(4,128)(2,1)S(1)}, bf16[1,256,4,256]{3,2,1,0:T(4,128)(2,1)}, u32[]{:S(2)}) copy-start(bf16[1,256,4,256]{3,2,1,0:T(4,128)(2,1)} %param.10) | copy-start | bytes 1572868
  30.4 4.5 %copy-start.2 = (bf16[1,256,4,256]{3,2,1,0:T(4,128)(2,1)S(1)}, bf16[1,256,4,256]{3,2,1,0:T(4,128)(2,1)}, u32[]{:S(2)}) copy-start(bf16[1,256,4,256]{3,2,1,0:T(4,128)(2,1)} %param.19) | copy-start | bytes 1572868
  32.6 1.7 %copy-start.9 = (f32[4]{0:T(128)S(1)}, f32[4]{0:T(128)}, u32[]{:S(2)}) copy-start(f32[4]{0:T(128)} %param.14) | copy-start | bytes 52
  32.6 2.2 %copy-start.3 = (f32[4,256]{1,0:T(4,128)S(1)}, f32[4,256]{1,0:T(4,128)}, u32[]{:S(2)}) copy-start(f32[4,256]{1,0:T(4,128)} %gain.1) | copy-start | bytes 12292
  32.6 6.3 %collective-permute-start.6 = (f32[1,3,64,256]{3,2,1,0:T(8,128)S(1)}, f32[1,3,64,256]{3,2,1,0:T(8,128)S(1)}, u32[]{:S(2)}, u32[]{:S(2)}) collective-permute-start(f32[1,3,64,256]{3,2,1,0:T(8,128)S(1)} %get-tuple-element.135), channel_id=1, source_target_pairs={{0,8},{2,10},{4,12},{6,14},{8,0},{10,2},{12,4},{14,6},{16,24},{18,... | collective-permute-start | bytes 589832 | tf_op jit(solution)/shard_map/ppermute | solution.py:336
  36.8 13.1 %collective-permute-start.9 = (f32[2,256,256]{2,1,0:T(8,128)S(1)}, f32[2,256,256]{2,1,0:T(8,128)S(1)}, u32[]{:S(2)}, u32[]{:S(2)}) collective-permute-start(f32[2,256,256]{2,1,0:T(8,128)S(1)} %get-tuple-element.141), channel_id=1, source_target_pairs={{0,2},{2,0},{4,6},{6,4},{8,10},{10,8},{12,14},{14,12},{16,18},{18,... | collective-permute-start | bytes 1572872 | tf_op jit(solution)/shard_map/ppermute | solution.py:336
  38.1 12.2 %collective-permute-start.10 = (f32[2,256,256]{2,1,0:T(8,128)S(1)}, f32[2,256,256]{2,1,0:T(8,128)S(1)}, u32[]{:S(2)}, u32[]{:S(2)}) collective-permute-start(f32[2,256,256]{2,1,0:T(8,128)S(1)} %get-tuple-element.142), channel_id=1, source_target_pairs={{0,4},{2,6},{4,0},{6,2},{8,12},{10,14},{12,8},{14,10},{16,20},{18,... | collective-permute-start | bytes 1572872 | tf_op jit(solution)/shard_map/ppermute | solution.py:336
  39.0 10.0 %collective-permute-start.8 = (f32[1,3,64,256]{3,2,1,0:T(8,128)S(1)}, f32[1,3,64,256]{3,2,1,0:T(8,128)S(1)}, u32[]{:S(2)}, u32[]{:S(2)}) collective-permute-start(f32[1,3,64,256]{3,2,1,0:T(8,128)S(1)} %add.34), channel_id=1, source_target_pairs={{0,16},{2,18},{4,20},{6,22},{8,24},{10,26},{12,28},{14,30},{16,0},... | collective-permute-start | bytes 589832 | tf_op jit(solution)/shard_map/ppermute | solution.py:336
  41.6 8.2 %collective-permute-start.7 = (f32[1,3,64,256]{3,2,1,0:T(8,128)S(1)}, f32[1,3,64,256]{3,2,1,0:T(8,128)S(1)}, u32[]{:S(2)}, u32[]{:S(2)}) collective-permute-start(f32[1,3,64,256]{3,2,1,0:T(8,128)S(1)} %get-tuple-element.137), channel_id=1, source_target_pairs={{0,8},{2,10},{4,12},{6,14},{8,0},{10,2},{12,4},{14,6},{16,24},{18,... | collective-permute-start | bytes 589832 | tf_op jit(solution)/shard_map/ppermute | solution.py:336
  50.4 16.7 %collective-permute-start.11 = (f32[2,256,256]{2,1,0:T(8,128)S(1)}, f32[2,256,256]{2,1,0:T(8,128)S(1)}, u32[]{:S(2)}, u32[]{:S(2)}) collective-permute-start(f32[2,256,256]{2,1,0:T(8,128)S(1)} %get-tuple-element.147), channel_id=1, source_target_pairs={{0,6},{2,4},{4,2},{6,0},{8,14},{10,12},{12,10},{14,8},{16,22},{18,... | collective-permute-start | bytes 1572872 | tf_op jit(solution)/shard_map/ppermute | solution.py:336
  51.5 9.9 %collective-permute-start.13 = (f32[1,3,64,256]{3,2,1,0:T(8,128)S(1)}, f32[1,3,64,256]{3,2,1,0:T(8,128)S(1)}, u32[]{:S(2)}, u32[]{:S(2)}) collective-permute-start(f32[1,3,64,256]{3,2,1,0:T(8,128)S(1)} %add_add_fusion.1.refs_4_), channel_id=1, source_target_pairs={{0,16},{2,18},{4,20},{6,22},{8,24},{10,26},{12,28},{14,30},{16,0},... | collective-permute-start | bytes 589832 | tf_op jit(solution)/shard_map/ppermute | solution.py:336
  53.5 8.2 %collective-permute-start.12 = (f32[1,3,64,256]{3,2,1,0:T(8,128)S(1)}, f32[1,3,64,256]{3,2,1,0:T(8,128)S(1)}, u32[]{:S(2)}, u32[]{:S(2)}) collective-permute-start(f32[1,3,64,256]{3,2,1,0:T(8,128)S(1)} %add_add_fusion.1.refs_4_), channel_id=1, source_target_pairs={{0,8},{2,10},{4,12},{6,14},{8,0},{10,2},{12,4},{14,6},{16,24},{18,... | collective-permute-start | bytes 589832 | tf_op jit(solution)/shard_map/ppermute | solution.py:336
  61.4 5.7 %collective-permute-start.14 = (f32[1,3,64,256]{3,2,1,0:T(8,128)S(1)}, f32[1,3,64,256]{3,2,1,0:T(8,128)S(1)}, u32[]{:S(2)}, u32[]{:S(2)}) collective-permute-start(f32[1,3,64,256]{3,2,1,0:T(8,128)S(1)} %collective-permute-done.13.refs_6_), channel_id=1, source_target_pairs={{0,8},{2,10},{4,12},{6,14},{8,0},{10,2},{12,4},{14,6},{16,24},{18,... | collective-permute-start | bytes 589832 | tf_op jit(solution)/shard_map/ppermute | solution.py:336
  68.9 1.2 collective-permute-start.15
  70.1 4.5 %collective-permute-start.18 = (f32[2,4,256]{2,1,0:T(4,128)S(1)}, f32[2,4,256]{2,1,0:T(4,128)S(1)}, u32[]{:S(2)}, u32[]{:S(2)}) collective-permute-start(f32[2,4,256]{2,1,0:T(4,128)S(1)} %add.36.refs_4_), channel_id=1, source_target_pairs={{0,6},{2,4},{4,2},{6,0},{8,14},{10,12},{12,10},{14,8},{16,22},{18,... | collective-permute-start | bytes 24584 | tf_op jit(solution)/shard_map/ppermute | solution.py:336
  71.5 3.7 %collective-permute-start.17 = (f32[2,4,256]{2,1,0:T(4,128)S(1)}, f32[2,4,256]{2,1,0:T(4,128)S(1)}, u32[]{:S(2)}, u32[]{:S(2)}) collective-permute-start(f32[2,4,256]{2,1,0:T(4,128)S(1)} %add.36.refs_4_), channel_id=1, source_target_pairs={{0,4},{2,6},{4,0},{6,2},{8,12},{10,14},{12,8},{14,10},{16,20},{18,... | collective-permute-start | bytes 24584 | tf_op jit(solution)/shard_map/ppermute | solution.py:336
  72.9 3.7 %collective-permute-start.16 = (f32[2,4,256]{2,1,0:T(4,128)S(1)}, f32[2,4,256]{2,1,0:T(4,128)S(1)}, u32[]{:S(2)}, u32[]{:S(2)}) collective-permute-start(f32[2,4,256]{2,1,0:T(4,128)S(1)} %add.36.refs_4_), channel_id=1, source_target_pairs={{0,2},{2,0},{4,6},{6,4},{8,10},{10,8},{12,14},{14,12},{16,18},{18,... | collective-permute-start | bytes 24584 | tf_op jit(solution)/shard_map/ppermute | solution.py:336
  78.7 5.7 %collective-permute-start.19 = (f32[1,3,64,256]{3,2,1,0:T(8,128)S(1)}, f32[1,3,64,256]{3,2,1,0:T(8,128)S(1)}, u32[]{:S(2)}, u32[]{:S(2)}) collective-permute-start(f32[1,3,64,256]{3,2,1,0:T(8,128)S(1)} %get-tuple-element.166), channel_id=1, source_target_pairs={{0,8},{2,10},{4,12},{6,14},{8,0},{10,2},{12,4},{14,6},{16,24},{18,... | collective-permute-start | bytes 589832 | tf_op jit(solution)/shard_map/ppermute | solution.py:336
  84.5 9.2 %collective-permute-start.21 = (f32[1,3,64,256]{3,2,1,0:T(8,128)S(1)}, f32[1,3,64,256]{3,2,1,0:T(8,128)S(1)}, u32[]{:S(2)}, u32[]{:S(2)}) collective-permute-start(f32[1,3,64,256]{3,2,1,0:T(8,128)S(1)} %add.38), channel_id=1, source_target_pairs={{0,16},{2,18},{4,20},{6,22},{8,24},{10,26},{12,28},{14,30},{16,0},... | collective-permute-start | bytes 589832 | tf_op jit(solution)/shard_map/ppermute | solution.py:336
  85.2 8.5 %collective-permute-start.20 = (f32[1,3,64,256]{3,2,1,0:T(8,128)S(1)}, f32[1,3,64,256]{3,2,1,0:T(8,128)S(1)}, u32[]{:S(2)}, u32[]{:S(2)}) collective-permute-start(f32[1,3,64,256]{3,2,1,0:T(8,128)S(1)} %get-tuple-element.168), channel_id=1, source_target_pairs={{0,8},{2,10},{4,12},{6,14},{8,0},{10,2},{12,4},{14,6},{16,24},{18,... | collective-permute-start | bytes 589832 | tf_op jit(solution)/shard_map/ppermute | solution.py:336
  93.7 9.6 %collective-permute-start.23 = (f32[1,3,64,256]{3,2,1,0:T(8,128)S(1)}, f32[1,3,64,256]{3,2,1,0:T(8,128)S(1)}, u32[]{:S(2)}, u32[]{:S(2)}) collective-permute-start(f32[1,3,64,256]{3,2,1,0:T(8,128)S(1)} %add_add_fusion.refs_11_.refs_0_), channel_id=1, source_target_pairs={{0,16},{2,18},{4,20},{6,22},{8,24},{10,26},{12,28},{14,30},{16,0},... | collective-permute-start | bytes 589832 | tf_op jit(solution)/shard_map/ppermute | solution.py:336
  94.4 10.0 %collective-permute-start.25 = (f32[256,256]{1,0:T(8,128)S(1)}, f32[256,256]{1,0:T(8,128)S(1)}, u32[]{:S(2)}, u32[]{:S(2)}) collective-permute-start(f32[256,256]{1,0:T(8,128)S(1)} %get-tuple-element.172), channel_id=1, source_target_pairs={{0,2},{2,0},{4,6},{6,4},{8,10},{10,8},{12,14},{14,12},{16,18},{18,... | collective-permute-start | bytes 786440 | tf_op jit(solution)/shard_map/ppermute | solution.py:336
  95.2 11.7 %collective-permute-start.26 = (f32[256,256]{1,0:T(8,128)S(1)}, f32[256,256]{1,0:T(8,128)S(1)}, u32[]{:S(2)}, u32[]{:S(2)}) collective-permute-start(f32[256,256]{1,0:T(8,128)S(1)} %get-tuple-element.173), channel_id=1, source_target_pairs={{0,4},{2,6},{4,0},{6,2},{8,12},{10,14},{12,8},{14,10},{16,20},{18,... | collective-permute-start | bytes 786440 | tf_op jit(solution)/shard_map/ppermute | solution.py:336
  96.4 10.5 %collective-permute-start.27 = (f32[256,256]{1,0:T(8,128)S(1)}, f32[256,256]{1,0:T(8,128)S(1)}, u32[]{:S(2)}, u32[]{:S(2)}) collective-permute-start(f32[256,256]{1,0:T(8,128)S(1)} %get-tuple-element.174), channel_id=1, source_target_pairs={{0,6},{2,4},{4,2},{6,0},{8,14},{10,12},{12,10},{14,8},{16,22},{18,... | collective-permute-start | bytes 786440 | tf_op jit(solution)/shard_map/ppermute | solution.py:336
  97.9 10.7 %collective-permute-start.22 = (f32[1,3,64,256]{3,2,1,0:T(8,128)S(1)}, f32[1,3,64,256]{3,2,1,0:T(8,128)S(1)}, u32[]{:S(2)}, u32[]{:S(2)}) collective-permute-start(f32[1,3,64,256]{3,2,1,0:T(8,128)S(1)} %add_add_fusion.refs_11_.refs_0_), channel_id=1, source_target_pairs={{0,8},{2,10},{4,12},{6,14},{8,0},{10,2},{12,4},{14,6},{16,24},{18,... | collective-permute-start | bytes 589832 | tf_op jit(solution)/shard_map/ppermute | solution.py:336
  103.3 6.3 %collective-permute-start.24 = (f32[1,3,64,256]{3,2,1,0:T(8,128)S(1)}, f32[1,3,64,256]{3,2,1,0:T(8,128)S(1)}, u32[]{:S(2)}, u32[]{:S(2)}) collective-permute-start(f32[1,3,64,256]{3,2,1,0:T(8,128)S(1)} %collective-permute-done.23.refs_13_), channel_id=1, source_target_pairs={{0,8},{2,10},{4,12},{6,14},{8,0},{10,2},{12,4},{14,6},{16,24},{18,... | collective-permute-start | bytes 589832 | tf_op jit(solution)/shard_map/ppermute | solution.py:336
  112.6 19.3 %collective-permute-start.31 = (f32[3,256,256]{2,1,0:T(8,128)S(1)}, f32[3,256,256]{2,1,0:T(8,128)S(1)}, u32[]{:S(2)}, u32[]{:S(2)}) collective-permute-start(f32[3,256,256]{2,1,0:T(8,128)S(1)} %get-tuple-element.207), channel_id=1, source_target_pairs={{0,2},{2,0},{4,6},{6,4},{8,10},{10,8},{12,14},{14,12},{16,18},{18,... | collective-permute-start | bytes 2359304 | tf_op jit(solution)/shard_map/ppermute | solution.py:336
  115.1 18.3 %collective-permute-start.32 = (f32[3,256,256]{2,1,0:T(8,128)S(1)}, f32[3,256,256]{2,1,0:T(8,128)S(1)}, u32[]{:S(2)}, u32[]{:S(2)}) collective-permute-start(f32[3,256,256]{2,1,0:T(8,128)S(1)} %get-tuple-element.208), channel_id=1, source_target_pairs={{0,4},{2,6},{4,0},{6,2},{8,12},{10,14},{12,8},{14,10},{16,20},{18,... | collective-permute-start | bytes 2359304 | tf_op jit(solution)/shard_map/ppermute | solution.py:336
  115.2 5.7 %collective-permute-start.28 = (f32[1,3,64,256]{3,2,1,0:T(8,128)S(1)}, f32[1,3,64,256]{3,2,1,0:T(8,128)S(1)}, u32[]{:S(2)}, u32[]{:S(2)}) collective-permute-start(f32[1,3,64,256]{3,2,1,0:T(8,128)S(1)} %get-tuple-element.201), channel_id=1, source_target_pairs={{0,8},{2,10},{4,12},{6,14},{8,0},{10,2},{12,4},{14,6},{16,24},{18,... | collective-permute-start | bytes 589832 | tf_op jit(solution)/shard_map/ppermute | solution.py:336
  120.9 9.6 %collective-permute-start.30 = (f32[1,3,64,256]{3,2,1,0:T(8,128)S(1)}, f32[1,3,64,256]{3,2,1,0:T(8,128)S(1)}, u32[]{:S(2)}, u32[]{:S(2)}) collective-permute-start(f32[1,3,64,256]{3,2,1,0:T(8,128)S(1)} %add.40), channel_id=1, source_target_pairs={{0,16},{2,18},{4,20},{6,22},{8,24},{10,26},{12,28},{14,30},{16,0},... | collective-permute-start | bytes 589832 | tf_op jit(solution)/shard_map/ppermute | solution.py:336
  122.0 8.5 %collective-permute-start.29 = (f32[1,3,64,256]{3,2,1,0:T(8,128)S(1)}, f32[1,3,64,256]{3,2,1,0:T(8,128)S(1)}, u32[]{:S(2)}, u32[]{:S(2)}) collective-permute-start(f32[1,3,64,256]{3,2,1,0:T(8,128)S(1)} %get-tuple-element.203), channel_id=1, source_target_pairs={{0,8},{2,10},{4,12},{6,14},{8,0},{10,2},{12,4},{14,6},{16,24},{18,... | collective-permute-start | bytes 589832 | tf_op jit(solution)/shard_map/ppermute | solution.py:336
  133.4 9.8 %collective-permute-start.34 = (f32[256,256]{1,0:T(8,128)S(1)}, f32[256,256]{1,0:T(8,128)S(1)}, u32[]{:S(2)}, u32[]{:S(2)}) collective-permute-start(f32[256,256]{1,0:T(8,128)S(1)} %slice_bitcast_fusion), channel_id=1, source_target_pairs={{0,2},{2,0},{4,6},{6,4},{8,10},{10,8},{12,14},{14,12},{16,18},{18,... | collective-permute-start | bytes 786440 | tf_op jit(solution)/shard_map/ppermute | solution.py:336
  133.8 9.4 %collective-permute-start.33 = (f32[256,256]{1,0:T(8,128)S(1)}, f32[256,256]{1,0:T(8,128)S(1)}, u32[]{:S(2)}, u32[]{:S(2)}) collective-permute-start(f32[256,256]{1,0:T(8,128)S(1)} %slice_bitcast_fusion.1), channel_id=1, source_target_pairs={{0,4},{2,6},{4,0},{6,2},{8,12},{10,14},{12,8},{14,10},{16,20},{18,... | collective-permute-start | bytes 786440 | tf_op jit(solution)/shard_map/ppermute | solution.py:336
  135.0 6.2 %collective-permute-start.35 = (f32[1,3,16,256]{3,2,1,0:T(8,128)S(1)}, f32[1,3,16,256]{3,2,1,0:T(8,128)S(1)}, u32[]{:S(2)}, u32[]{:S(2)}) collective-permute-start(f32[1,3,16,256]{3,2,1,0:T(8,128)S(1)} %get-tuple-element.216), channel_id=1, source_target_pairs={{0,2},{2,0},{4,6},{6,4},{8,10},{10,8},{12,14},{14,12},{16,18},{18,... | collective-permute-start | bytes 147464 | tf_op jit(solution)/shard_map/ppermute | solution.py:336
  136.5 5.1 %collective-permute-start.36 = (f32[1,3,16,256]{3,2,1,0:T(8,128)S(1)}, f32[1,3,16,256]{3,2,1,0:T(8,128)S(1)}, u32[]{:S(2)}, u32[]{:S(2)}) collective-permute-start(f32[1,3,16,256]{3,2,1,0:T(8,128)S(1)} %get-tuple-element.217), channel_id=1, source_target_pairs={{0,4},{2,6},{4,0},{6,2},{8,12},{10,14},{12,8},{14,10},{16,20},{18,... | collective-permute-start | bytes 147464 | tf_op jit(solution)/shard_map/ppermute | solution.py:336
  138.2 5.0 %collective-permute-start.37 = (f32[1,3,16,256]{3,2,1,0:T(8,128)S(1)}, f32[1,3,16,256]{3,2,1,0:T(8,128)S(1)}, u32[]{:S(2)}, u32[]{:S(2)}) collective-permute-start(f32[1,3,16,256]{3,2,1,0:T(8,128)S(1)} %get-tuple-element.218), channel_id=1, source_target_pairs={{0,6},{2,4},{4,2},{6,0},{8,14},{10,12},{12,10},{14,8},{16,22},{18,... | collective-permute-start | bytes 147464 | tf_op jit(solution)/shard_map/ppermute | solution.py:336

commit v14 on v13

--- a/solution.py
+++ b/solution.py
@@ -191,34 +191,35 @@
         stats[1, pl.ds(source, 1), :] = both[1:2, :]
 
 
-def apply_back_kernel(groups, depth, count, place, scale_row, *refs):
-    pieces, stats = refs[:groups], refs[groups : 2 * groups]
-    activ_ref, slope_ref, hidden_ref, os_ref, new_b = refs[2 * groups : 2 * groups + 5]
-    outs = refs[2 * groups + 5 : 3 * groups + 5]
-    slices, sums, both = refs[3 * groups + 5 : -2], refs[-2], refs[-1]
-    total_stats = stats[0][...]
-    for other in stats[1:]:
-        total_stats += other[...]
-    both[...] = total_stats
+def apply_back_kernel(groups, depth, count, place, scale_row, stats, *refs):
+    pieces, refs = refs[:groups], refs[groups:]
+    activ_ref, slope_ref, hidden_ref, os_ref, new_b = refs[:5]
+    dfirst_ref, dthird_ref, slices, sums = refs[5], refs[6], refs[7:-1], refs[-1]
     total = [0.0, 0.0, 0.0]
     for step in range(groups):
         queries = pieces[step][0].astype(BF16)
         source = place[0] ^ step
-        sq = rate_column(both.at[0], source)
-        ps = rate_column(both.at[1], source)
+        sq = rate_column(stats.at[0], source)
+        ps = rate_column(stats.at[1], source)
         inv = lax.rsqrt(sq / count + 1e-06)
         dos = inv * pieces[step][1] - os_ref[step] * (inv * inv * inv * ps / count)
         dout = (dos * scale_row[0:1, :]).astype(BF16)
         dhidden = mm_t(dout, new_b[1])
         dthird = (dhidden * activ_ref[step]).astype(BF16)
         dfirst = (dhidden * slope_ref[step]).astype(BF16)
-        outs[step][...] = mm_t(dfirst, new_b[0]) + mm_t(dthird, new_b[2])
+        dfirst_ref[step] = dfirst
+        dthird_ref[step] = dthird
         total[0] += tmm(queries, dfirst)
         total[1] += tmm(hidden_ref[step], dout)
         total[2] += tmm(queries, dthird)
     for i in range(3):
         sums[i] = total[i]
     send_slices(sums, slices, place[1], depth)
+
+
+def query_back_kernel(dfirst, dthird, new_b, *outs):
+    for step, out in enumerate(outs):
+        out[...] = mm_t(dfirst[step], new_b[0]) + mm_t(dthird[step], new_b[2])
 
 
 def update_keep_kernel(k_kept, s_kept, w_gate, w_out, w_up, *outs):
@@ -293,17 +294,21 @@
 
 
 def join_update_kernel(groups, place, r, *refs):
-    (out_k, out_v, *grads), (sk, sv) = refs[-7:-2], refs[-2:]
-    pieces, parts = unpacked(groups, refs[: -7 - groups]), refs[-7 - groups : -7]
+    pieces, (out_k, out_v, sk, sv) = unpacked(groups, refs[:-4]), refs[-4:]
     tokens, heads, width = out_k.shape
     for step, piece in enumerate(pieces):
         head = place[0] ^ step
         put_head(sk, head, piece[0][...], tokens, heads)
         put_head(sv, head, piece[1][...] * rate_column(r, head), tokens, heads)
-        for i, grad in enumerate(grads):
-            grad[head] = parts[step][0, i]
     out_k[...] = rows_of(sk).reshape(tokens, heads, width).astype(BF16)
     out_v[...] = rows_of(sv).reshape(tokens, heads, width).astype(BF16)
+
+
+def join_rows_kernel(groups, place, *refs):
+    parts, grads = refs[:groups], refs[groups:]
+    for step, part in enumerate(parts):
+        for i, grad in enumerate(grads):
+            grad[place[0] ^ step] = part[0, i]
 
 
 def rows_kernel(groups, place, *refs):
@@ -408,25 +413,30 @@
         + [shape(3, hidden, width, dtype=BF16), shape(2, groups, tokens)],
         [square], 3 * flops, place, scale_row, *q_in, *new,
     )
-    bit = 1
-    while bit < head_axis:
-        stats = stats + move(stats, "head", bit)
-        bit *= 2
+    for axis, size in (("head", lax.axis_size("head")), ("ctx", groups)):
+        bit = 1
+        while bit < size:
+            stats = stats + move(stats, axis, bit)
+            bit *= 2
     out = call(
-        functools.partial(apply_back_kernel, groups, depth, count), pieces + slices,
-        [square, pltpu.VMEM((2, groups, tokens), F32)], 6 * flops,
-        place, scale_row, *q_in, *in_plane([stats] * groups), *passed,
-    )
+        functools.partial(apply_back_kernel, groups, depth, count),
+        [kept(groups, dtype=BF16)] * 2 + slices, [square], 6 * flops,
+        place, scale_row, stats, *q_in, *passed,
+    )
+    q_sent = call(
+        query_back_kernel, [shape(tokens, width)] * groups, [], 2 * flops, *out[:2], passed[-1]
+    )
+    out = out[2:]
     out, early = after(out, early)
     saved = call(
         update_keep_kernel, [kept(groups)] * 6 + [kept(groups, dtype=BF16)] * 3, [], 3 * flops,
         *early, *own,
     )
-    part = functools.reduce(jnp.add, scatter(out[groups:], depth, groups))
+    part = functools.reduce(jnp.add, scatter(out, depth, groups))
     parts = gather(part, depth, groups)
     (grad_q,) = call(
         functools.partial(join_query_kernel, groups), [joined], [scratch], flops // 16,
-        place, *in_plane(out[:groups]),
+        place, *in_plane(q_sent),
     )
     parts, grad_q, saved = after(parts, grad_q, saved)
     rows = hidden // depth
@@ -447,10 +457,14 @@
         [shape(1, 3, own_rows, width)] * groups,
         [pltpu.VMEM((3, rows, width), F32)], flops // 100, place, part, *ends,
     )
-    grad_k, grad_v, *grads = call(
-        functools.partial(join_update_kernel, groups),
-        [joined] * 2 + [shape(heads, own_rows, width)] * 3, [scratch] * 2, flops // 8,
-        place, rates[0], *back, *in_plane(sent),
+    grad_k, grad_v = call(
+        functools.partial(join_update_kernel, groups), [joined] * 2, [scratch] * 2, flops // 8,
+        place, rates[0], *back,
+    )
+    got, grad_k, grad_v = after(in_plane(sent), grad_k, grad_v)
+    grads = call(
+        functools.partial(join_rows_kernel, groups), [shape(heads, own_rows, width)] * 3, [],
+        flops // 100, place, *got,
     )
     if lax.axis_size("batch") > 1:
         grads = [lax.psum_scatter(x, "batch", scatter_dimension=1, tiled=True) for x in grads]

time: 146 us -> 143 us (0.979)
  waiting for transfers between devices: 76.4 us -> 69.5 us
  starting transfers between devices: 45.1 us -> 47.9 us
  Pallas kernels: 19.5 us -> 21.1 us
    ppermute x38 -> x37, waiting for transfers between devices: 76.4 us -> 69.5 us  [move(): lax.ppermute(x, axis, [(c, c ^ step) for c in range(lax.axis_size(axis))])]
    ppermute x38 -> x37, starting transfers between devices: 45.1 us -> 47.9 us  [move(): lax.ppermute(x, axis, [(c, c ^ step) for c in range(lax.axis_size(axis))])]
    pallas_call x11 -> x13, Pallas kernels: 19.5 us -> 21.1 us  [call(): pl.pallas_call(body, out_shape=out_shape, in_specs=[smem if a.dtype == jn...]
  transfers between devices with their start and end apart: 38 -> 37, of which waited for: 26 -> 22; matrix products, arithmetic and copies ran while one was open for 1% -> 1% of each run, Pallas kernels for 5% -> 7%
where the time goes in v14:
time: 143 us
  waiting for transfers between devices  69.5 us (49%)
  starting transfers between devices  47.9 us (33%)
  Pallas kernels  21.1 us (15%)
  local copies, waits for them, and re-layouts  3.56 us (2%)
    ppermute x37, waiting for transfers between devices, move(): lax.ppermute(x, axis, [(c, c ^ step) for c in range(lax.axis_size(axis))])  69.5 us
    ppermute x37, starting transfers between devices, move(): lax.ppermute(x, axis, [(c, c ^ step) for c in range(lax.axis_size(axis))])  47.9 us
    pallas_call x13, Pallas kernels, call(): pl.pallas_call(body, out_shape=out_shape, in_specs=[smem if a.dtype == jn...  21.1 us
  transfers between devices with their start and end apart: 37, of which 22 were waited for; matrix products, arithmetic and copies ran while one was open for 1% of the time, Pallas kernels for 7%

profile of v14, /device:TPU:0, one launch (start us, length us, event | category | flops | bytes accessed | tf_op | source)
XLA Modules:
  0.0 143.2 jit_solution(8523703445260805510)
XLA Ops:
  0.7 1.1 copy-done.5
  1.8 0.9 shard_map.145
  2.8 3.0 %collective-permute-start = (f32[256,256]{1,0:T(8,128)S(1)}, f32[256,256]{1,0:T(8,128)S(1)}, u32[]{:S(2)}, u32[]{:S(2)}) collective-permute-start(f32[256,256]{1,0:T(8,128)S(1)} %get-tuple-element.120), channel_id=1, source_target_pairs={{0,2},{2,0},{4,6},{6,4},{8,10},{10,8},{12,14},{14,12},{16,18},{18,... | collective-permute-start | bytes 786440 | tf_op jit(solution)/shard_map/ppermute | solution.py:341
  5.8 1.5 %collective-permute-start.1 = (f32[256,256]{1,0:T(8,128)S(1)}, f32[256,256]{1,0:T(8,128)S(1)}, u32[]{:S(2)}, u32[]{:S(2)}) collective-permute-start(f32[256,256]{1,0:T(8,128)S(1)} %get-tuple-element.121), channel_id=1, source_target_pairs={{0,4},{2,6},{4,0},{6,2},{8,12},{10,14},{12,8},{14,10},{16,20},{18,... | collective-permute-start | bytes 786440 | tf_op jit(solution)/shard_map/ppermute | solution.py:341
  7.3 1.8 %shard_map.146 = (bf16[256,256]{1,0:T(8,128)(2,1)S(1)}, f32[256,256]{1,0:T(8,128)}, f32[256,256]{1,0:T(8,128)}, f32[256,256]{1,0:T(8,128)S(1)}) custom-call(s32[2]{0:T(128)S(1)} %pad_add_fusion.place, bf16[256,4,256]{2,1,0:T(4,128)(2,1)S(1)} %bitcast.26, f32[4,256]{1,0:T(4,128)S(1)} %bitcast.23), custom_call_target="tpu_custom_call" | custom-call | flops 2147483648 | bytes 1445896 | tf_op jit(solution)/shard_map/pallas_call | solution.py:34
  9.1 0.7 copy-done.7
  9.8 1.9 %collective-permute-start.3 = (f32[256,256]{1,0:T(8,128)}, f32[256,256]{1,0:T(8,128)S(1)}, u32[]{:S(2)}, u32[]{:S(2)}) collective-permute-start(f32[256,256]{1,0:T(8,128)} %get-tuple-element.124), channel_id=1, source_target_pairs={{0,2},{2,0},{4,6},{6,4},{8,10},{10,8},{12,14},{14,12},{16,18},{18,... | collective-permute-start | bytes 786440 | tf_op jit(solution)/shard_map/ppermute | solution.py:341
  11.7 1.5 %collective-permute-start.4 = (f32[256,256]{1,0:T(8,128)}, f32[256,256]{1,0:T(8,128)S(1)}, u32[]{:S(2)}, u32[]{:S(2)}) collective-permute-start(f32[256,256]{1,0:T(8,128)} %get-tuple-element.125), channel_id=1, source_target_pairs={{0,4},{2,6},{4,0},{6,2},{8,12},{10,14},{12,8},{14,10},{16,20},{18,... | collective-permute-start | bytes 786440 | tf_op jit(solution)/shard_map/ppermute | solution.py:341
  13.2 2.7 %collective-permute-start.5 = (f32[256,256]{1,0:T(8,128)S(1)}, f32[256,256]{1,0:T(8,128)S(1)}, u32[]{:S(2)}, u32[]{:S(2)}) collective-permute-start(f32[256,256]{1,0:T(8,128)S(1)} %get-tuple-element.126), channel_id=1, source_target_pairs={{0,6},{2,4},{4,2},{6,0},{8,14},{10,12},{12,10},{14,8},{16,22},{18,... | collective-permute-start | bytes 786440 | tf_op jit(solution)/shard_map/ppermute | solution.py:341
  15.9 1.1 dynamic-slice_bitcast_fusion
  17.1 2.7 %collective-permute-done.1.refs_2_ = f32[256,256]{1,0:T(8,128)S(1)} collective-permute-done((f32[256,256]{1,0:T(8,128)S(1)}, f32[256,256]{1,0:T(8,128)S(1)}, u32[]{:S(2)}, u32[]{:S(2)}) %collective-permute-start.1) | collective-permute-done | bytes 262176 | tf_op jit(solution)/shard_map/ppermute | solution.py:341
  20.1 4.1 %collective-permute-done.3.refs_5_ = f32[256,256]{1,0:T(8,128)S(1)} collective-permute-done((f32[256,256]{1,0:T(8,128)}, f32[256,256]{1,0:T(8,128)S(1)}, u32[]{:S(2)}, u32[]{:S(2)}) %collective-permute-start.3) | collective-permute-done | bytes 262176 | tf_op jit(solution)/shard_map/ppermute | solution.py:341
  24.2 6.2 %collective-permute-done.4.refs_6_ = f32[256,256]{1,0:T(8,128)S(1)} collective-permute-done((f32[256,256]{1,0:T(8,128)}, f32[256,256]{1,0:T(8,128)S(1)}, u32[]{:S(2)}, u32[]{:S(2)}) %collective-permute-start.4) | collective-permute-done | bytes 262176 | tf_op jit(solution)/shard_map/ppermute | solution.py:341
  30.4 2.2 %shard_map.148 = (bf16[4,256,256]{2,1,0:T(8,128)(2,1)S(1)}, bf16[4,256,256]{2,1,0:T(8,128)(2,1)S(1)}, f32[1,3,64,256]{3,2,1,0:T(8,128)S(1)}, f32[1,3,64,256]{3,2...) custom-call(s32[2]{0:T(128)S(1)} %pad_add_fusion.place, ...), custom_call_target="tpu_custom_call" | custom-call | flops 805306368 | bytes 4456456 | tf_op jit(solution)/shard_map/pallas_call | solution.py:34
  32.6 1.6 %collective-permute-start.6 = (f32[1,3,64,256]{3,2,1,0:T(8,128)S(1)}, f32[1,3,64,256]{3,2,1,0:T(8,128)S(1)}, u32[]{:S(2)}, u32[]{:S(2)}) collective-permute-start(f32[1,3,64,256]{3,2,1,0:T(8,128)S(1)} %get-tuple-element.139), channel_id=1, source_target_pairs={{0,8},{2,10},{4,12},{6,14},{8,0},{10,2},{12,4},{14,6},{16,24},{18,... | collective-permute-start | bytes 589832 | tf_op jit(solution)/shard_map/ppermute | solution.py:341
  34.3 0.6 dynamic_slice.14
  34.9 1.9 %shard_map.147 = (f32[2,256,256]{2,1,0:T(8,128)S(1)}, f32[2,256,256]{2,1,0:T(8,128)S(1)}, f32[2,256,256]{2,1,0:T(8,128)S(1)}, f32[2,256,256]{2,1,0:T(8,128)S(1)}, f32[8,256]{1,0:T(8,128)S(1)}) custom-call(s32[2]{0:T(128)S(1)} %pad_add_fusion.place, bf16[256,4,256]{2,1,0:T(4,128)(2,1)S(1)} %bitcast.21, bf16[256,4,256]{2,1,0:T(4,128)(2,1)S(1)} %bitcast.22, ...), custom_call_target="tpu_custom_call" | custom-call | flops 16777216 | bytes 3158028 | tf_op jit(solution)/shard_map/pallas_call | solution.py:34
  36.8 1.3 collective-permute-start.9
  38.1 0.8 collective-permute-start.10
  39.0 2.7 %collective-permute-start.8 = (f32[1,3,64,256]{3,2,1,0:T(8,128)S(1)}, f32[1,3,64,256]{3,2,1,0:T(8,128)S(1)}, u32[]{:S(2)}, u32[]{:S(2)}) collective-permute-start(f32[1,3,64,256]{3,2,1,0:T(8,128)S(1)} %add.40), channel_id=1, source_target_pairs={{0,16},{2,18},{4,20},{6,22},{8,24},{10,26},{12,28},{14,30},{16,0},... | collective-permute-start | bytes 589832 | tf_op jit(solution)/shard_map/ppermute | solution.py:341
  41.6 1.0 collective-permute-start.7
  42.6 6.3 %collective-permute-done.8 = f32[1,3,64,256]{3,2,1,0:T(8,128)S(1)} collective-permute-done((f32[1,3,64,256]{3,2,1,0:T(8,128)S(1)}, f32[1,3,64,256]{3,2,1,0:T(8,128)S(1)}, u32[]{:S(2)}, u32[]{:S(2)}) %collective-permute-start.8) | collective-permute-done | bytes 196640 | tf_op jit(solution)/shard_map/ppermute | solution.py:341
  49.0 0.9 collective-permute-done.7
  50.4 1.1 collective-permute-start.11
  51.5 2.0 %collective-permute-start.13 = (f32[1,3,64,256]{3,2,1,0:T(8,128)S(1)}, f32[1,3,64,256]{3,2,1,0:T(8,128)S(1)}, u32[]{:S(2)}, u32[]{:S(2)}) collective-permute-start(f32[1,3,64,256]{3,2,1,0:T(8,128)S(1)} %add_add_fusion.1.refs_4_), channel_id=1, source_target_pairs={{0,16},{2,18},{4,20},{6,22},{8,24},{10,26},{12,28},{14,30},{16,0},... | collective-permute-start | bytes 589832 | tf_op jit(solution)/shard_map/ppermute | solution.py:341
  53.5 0.8 collective-permute-start.12
  54.3 7.1 %collective-permute-done.13.refs_6_ = f32[1,3,64,256]{3,2,1,0:T(8,128)S(1)} collective-permute-done((f32[1,3,64,256]{3,2,1,0:T(8,128)S(1)}, f32[1,3,64,256]{3,2,1,0:T(8,128)S(1)}, u32[]{:S(2)}, u32[]{:S(2)}) %collective-permute-start.13) | collective-permute-done | bytes 196640 | tf_op jit(solution)/shard_map/ppermute | solution.py:341
  61.6 5.5 %collective-permute-done.14.refs_7_ = f32[1,3,64,256]{3,2,1,0:T(8,128)S(1)} collective-permute-done((f32[1,3,64,256]{3,2,1,0:T(8,128)S(1)}, f32[1,3,64,256]{3,2,1,0:T(8,128)S(1)}, u32[]{:S(2)}, u32[]{:S(2)}) %collective-permute-start.14) | collective-permute-done | bytes 196640 | tf_op jit(solution)/shard_map/ppermute | solution.py:341
  67.1 1.8 %shard_map.149 = (f32[4,256,256]{2,1,0:T(8,128)S(1)}, f32[4,256,256]{2,1,0:T(8,128)S(1)}, bf16[4,256,256]{2,1,0:T(8,128)(2,1)S(1)}, f32[4,256,256]{2,1,0:T(8,128...) custom-call(s32[2]{0:T(128)S(1)} %pad_add_fusion.place, f32[8,256]{1,0:T(8,128)S(1)} %get-tuple-element.129.scale_row, ...), custom_call_target="tpu_custom_call" | custom-call | flops 402653184 | bytes 6963208 | tf_op jit(solution)/shard_map/pallas_call | solution.py:34
  68.9 1.2 collective-permute-done.15
  70.1 1.4 collective-permute-start.16
  71.5 2.3 %collective-permute-done.16 = f32[2,4,256]{2,1,0:T(4,128)S(1)} collective-permute-done((f32[2,4,256]{2,1,0:T(4,128)S(1)}, f32[2,4,256]{2,1,0:T(4,128)S(1)}, u32[]{:S(2)}, u32[]{:S(2)}) %collective-permute-start.16) | collective-permute-done | bytes 8224 | tf_op jit(solution)/shard_map/ppermute | solution.py:341
  73.7 0.5 collective-permute-start.17
  74.2 3.2 %collective-permute-done.17 = f32[2,4,256]{2,1,0:T(4,128)S(1)} collective-permute-done((f32[2,4,256]{2,1,0:T(4,128)S(1)}, f32[2,4,256]{2,1,0:T(4,128)S(1)}, u32[]{:S(2)}, u32[]{:S(2)}) %collective-permute-start.17) | collective-permute-done | bytes 8224 | tf_op jit(solution)/shard_map/ppermute | solution.py:341
  77.4 2.0 %shard_map.150 = (bf16[4,256,256]{2,1,0:T(8,128)(2,1)S(1)}, bf16[4,256,256]{2,1,0:T(8,128)(2,1)S(1)}, f32[1,3,64,256]{3,2,1,0:T(8,128)S(1)}, f32[1,3,64,256]{3,2...) custom-call(s32[2]{0:T(128)S(1)} %pad_add_fusion.place, ...), custom_call_target="tpu_custom_call" | custom-call | flops 805306368 | bytes 8011784 | tf_op jit(solution)/shard_map/pallas_call | solution.py:34
  79.8 5.4 %collective-permute-done.18 = f32[1,3,64,256]{3,2,1,0:T(8,128)S(1)} collective-permute-done((f32[1,3,64,256]{3,2,1,0:T(8,128)S(1)}, f32[1,3,64,256]{3,2,1,0:T(8,128)S(1)}, u32[]{:S(2)}, u32[]{:S(2)}) %collective-permute-start.18) | collective-permute-done | bytes 196640 | tf_op jit(solution)/shard_map/ppermute | solution.py:341
  85.2 0.7 collective-permute-start.20
  85.9 1.8 %collective-permute-start.19 = (f32[1,3,64,256]{3,2,1,0:T(8,128)S(1)}, f32[1,3,64,256]{3,2,1,0:T(8,128)S(1)}, u32[]{:S(2)}, u32[]{:S(2)}) collective-permute-start(f32[1,3,64,256]{3,2,1,0:T(8,128)S(1)} %get-tuple-element.168), channel_id=1, source_target_pairs={{0,8},{2,10},{4,12},{6,14},{8,0},{10,2},{12,4},{14,6},{16,24},{18,... | collective-permute-start | bytes 589832 | tf_op jit(solution)/shard_map/ppermute | solution.py:341
  87.7 8.9 %collective-permute-done.20 = f32[1,3,64,256]{3,2,1,0:T(8,128)S(1)} collective-permute-done((f32[1,3,64,256]{3,2,1,0:T(8,128)S(1)}, f32[1,3,64,256]{3,2,1,0:T(8,128)S(1)}, u32[]{:S(2)}, u32[]{:S(2)}) %collective-permute-start.20) | collective-permute-done | bytes 196640 | tf_op jit(solution)/shard_map/ppermute | solution.py:341
  96.8 0.5 shard_map.151
  97.2 1.6 %collective-permute-start.24 = (f32[256,256]{1,0:T(8,128)S(1)}, f32[256,256]{1,0:T(8,128)S(1)}, u32[]{:S(2)}, u32[]{:S(2)}) collective-permute-start(f32[256,256]{1,0:T(8,128)S(1)} %get-tuple-element.174), channel_id=1, source_target_pairs={{0,2},{2,0},{4,6},{6,4},{8,10},{10,8},{12,14},{14,12},{16,18},{18,... | collective-permute-start | bytes 786440 | tf_op jit(solution)/shard_map/ppermute | solution.py:341
  98.8 2.0 %collective-permute-start.26 = (f32[256,256]{1,0:T(8,128)S(1)}, f32[256,256]{1,0:T(8,128)S(1)}, u32[]{:S(2)}, u32[]{:S(2)}) collective-permute-start(f32[256,256]{1,0:T(8,128)S(1)} %get-tuple-element.176), channel_id=1, source_target_pairs={{0,6},{2,4},{4,2},{6,0},{8,14},{10,12},{12,10},{14,8},{16,22},{18,... | collective-permute-start | bytes 786440 | tf_op jit(solution)/shard_map/ppermute | solution.py:341
  100.8 3.2 %collective-permute-start.21 = (f32[1,3,64,256]{3,2,1,0:T(8,128)S(1)}, f32[1,3,64,256]{3,2,1,0:T(8,128)S(1)}, u32[]{:S(2)}, u32[]{:S(2)}) collective-permute-start(f32[1,3,64,256]{3,2,1,0:T(8,128)S(1)} %add_add_fusion.refs_11_.refs_0_), channel_id=1, source_target_pairs={{0,8},{2,10},{4,12},{6,14},{8,0},{10,2},{12,4},{14,6},{16,24},{18,... | collective-permute-start | bytes 589832 | tf_op jit(solution)/shard_map/ppermute | solution.py:341
  104.0 0.9 collective-permute-done.22.refs_13_
  105.0 1.0 shard_map.153
  106.0 2.0 %collective-permute-done.25.refs_2_ = f32[256,256]{1,0:T(8,128)S(1)} collective-permute-done((f32[256,256]{1,0:T(8,128)S(1)}, f32[256,256]{1,0:T(8,128)S(1)}, u32[]{:S(2)}, u32[]{:S(2)}) %collective-permute-start.25) | collective-permute-done | bytes 262176 | tf_op jit(solution)/shard_map/ppermute | solution.py:341
  108.0 1.7 %shard_map.152 = bf16[256,4,256]{2,1,0:T(4,128)(2,1)} custom-call(s32[2]{0:T(128)S(1)} %pad_add_fusion.place, f32[256,256]{1,0:T(8,128)S(1)} %get-tuple-element.173.refs_0_, f32[256,256]{1,0:T(8,128)S(1)} %collective-permute-done.24.refs_1_, f32[256,256]{1,0:T(8,128)S(1)} %collective-permute-done.25.refs_2_, f32[256,256]{1,0:T(8,128)S(1)} %collective-permute-done.26.refs_3_), custom_call_target="tpu_custom_call" | custom-call | flops 8388608 | bytes 1572872 | tf_op jit(solution)/shard_map/pallas_call | solution.py:34
  109.7 0.8 collective-permute-done.23.refs_14_
  110.6 3.0 %shard_map.154 = (f32[2,256,256]{2,1,0:T(8,128)S(1)}, f32[3,256,256]{2,1,0:T(8,128)S(1)}, f32[3,256,256]{2,1,0:T(8,128)S(1)}, f32[1,3,64,256]{3,2,1,0:T(8,128)S(...) custom-call(s32[2]{0:T(128)S(1)} %pad_add_fusion.place, ...), custom_call_target="tpu_custom_call" | custom-call | flops 1610612736 | bytes 13369352 | tf_op jit(solution)/shard_map/pallas_call | solution.py:34
  113.6 1.5 %collective-permute-start.30 = (f32[3,256,256]{2,1,0:T(8,128)S(1)}, f32[3,256,256]{2,1,0:T(8,128)S(1)}, u32[]{:S(2)}, u32[]{:S(2)}) collective-permute-start(f32[3,256,256]{2,1,0:T(8,128)S(1)} %get-tuple-element.209), channel_id=1, source_target_pairs={{0,2},{2,0},{4,6},{6,4},{8,10},{10,8},{12,14},{14,12},{16,18},{18,... | collective-permute-start | bytes 2359304 | tf_op jit(solution)/shard_map/ppermute | solution.py:341
  115.2 4.1 %collective-permute-start.27 = (f32[1,3,64,256]{3,2,1,0:T(8,128)S(1)}, f32[1,3,64,256]{3,2,1,0:T(8,128)S(1)}, u32[]{:S(2)}, u32[]{:S(2)}) collective-permute-start(f32[1,3,64,256]{3,2,1,0:T(8,128)S(1)} %get-tuple-element.203), channel_id=1, source_target_pairs={{0,8},{2,10},{4,12},{6,14},{8,0},{10,2},{12,4},{14,6},{16,24},{18,... | collective-permute-start | bytes 589832 | tf_op jit(solution)/shard_map/ppermute | solution.py:341
  119.3 4.0 %collective-permute-done.27 = f32[1,3,64,256]{3,2,1,0:T(8,128)S(1)} collective-permute-done((f32[1,3,64,256]{3,2,1,0:T(8,128)S(1)}, f32[1,3,64,256]{3,2,1,0:T(8,128)S(1)}, u32[]{:S(2)}, u32[]{:S(2)}) %collective-permute-start.27) | collective-permute-done | bytes 196640 | tf_op jit(solution)/shard_map/ppermute | solution.py:341
  123.3 1.2 collective-permute-start.29
  124.6 1.8 %collective-permute-start.28 = (f32[1,3,64,256]{3,2,1,0:T(8,128)S(1)}, f32[1,3,64,256]{3,2,1,0:T(8,128)S(1)}, u32[]{:S(2)}, u32[]{:S(2)}) collective-permute-start(f32[1,3,64,256]{3,2,1,0:T(8,128)S(1)} %get-tuple-element.205), channel_id=1, source_target_pairs={{0,8},{2,10},{4,12},{6,14},{8,0},{10,2},{12,4},{14,6},{16,24},{18,... | collective-permute-start | bytes 589832 | tf_op jit(solution)/shard_map/ppermute | solution.py:341
  126.4 5.7 %collective-permute-done.29.refs_3_ = f32[1,3,64,256]{3,2,1,0:T(8,128)S(1)} collective-permute-done((f32[1,3,64,256]{3,2,1,0:T(8,128)S(1)}, f32[1,3,64,256]{3,2,1,0:T(8,128)S(1)}, u32[]{:S(2)}, u32[]{:S(2)}) %collective-permute-start.29) | collective-permute-done | bytes 196640 | tf_op jit(solution)/shard_map/ppermute | solution.py:341
  132.2 1.0 collective-permute-start.36
  133.2 0.8 collective-permute-start.35
  134.0 0.6 shard_map.155
  134.6 1.5 %collective-permute-start.32 = (f32[1,3,16,256]{3,2,1,0:T(8,128)S(1)}, f32[1,3,16,256]{3,2,1,0:T(8,128)S(1)}, u32[]{:S(2)}, u32[]{:S(2)}) collective-permute-start(f32[1,3,16,256]{3,2,1,0:T(8,128)S(1)} %get-tuple-element.215), channel_id=1, source_target_pairs={{0,2},{2,0},{4,6},{6,4},{8,10},{10,8},{12,14},{14,12},{16,18},{18,... | collective-permute-start | bytes 147464 | tf_op jit(solution)/shard_map/ppermute | solution.py:341
  136.1 0.8 collective-permute-start.33
  136.9 1.2 collective-permute-start.34
  138.6 1.0 collective-permute-done.35.refs_3_
  139.6 2.4 %shard_map.156 = (bf16[256,4,256]{2,1,0:T(4,128)(2,1)}, bf16[256,4,256]{2,1,0:T(4,128)(2,1)}) custom-call(s32[2]{0:T(128)S(1)} %pad_add_fusion.place, f32[4,256]{1,0:T(4,128)S(1)} %bitcast.24, f32[2,256,256]{2,1,0:T(8,128)S(1)} %get-tuple-element.218.refs_0_, f32[3,256,256]{2,1,0:T(8,128)S(1)} %collective-permute-done.30.refs_1_, ...), custom_call_target="tpu_custom_call" | custom-call | flops 16777216 | bytes 3674120 | tf_op jit(solution)/shard_map/pallas_call | solution.py:34
  142.0 1.2 shard_map.157
  (57 shorter events, 2.5 us)
Async XLA Ops:
  0.6 15.3 %copy-start = (f32[4,256,256]{2,1,0:T(8,128)S(1)}, f32[4,256,256]{2,1,0:T(8,128)}, u32[]{:S(2)}) copy-start(f32[4,256,256]{2,1,0:T(8,128)} %param.16) | copy-start | bytes 3145732
  0.7 1.1 copy-start.5
  1.8 5.5 %copy-start.6 = (bf16[1,256,4,256]{3,2,1,0:T(4,128)(2,1)S(1)}, bf16[1,256,4,256]{3,2,1,0:T(4,128)(2,1)}, u32[]{:S(2)}) copy-start(bf16[1,256,4,256]{3,2,1,0:T(4,128)(2,1)} %param.12) | copy-start | bytes 1572868
  2.7 4.6 %copy-start.4 = (f32[1,4,256]{2,1,0:T(4,128)S(1)}, f32[1,4,256]{2,1,0:T(4,128)}, u32[]{:S(2)}) copy-start(f32[1,4,256]{2,1,0:T(4,128)} %param.13) | copy-start | bytes 12292
  2.8 10.5 %collective-permute-start = (f32[256,256]{1,0:T(8,128)S(1)}, f32[256,256]{1,0:T(8,128)S(1)}, u32[]{:S(2)}, u32[]{:S(2)}) collective-permute-start(f32[256,256]{1,0:T(8,128)S(1)} %get-tuple-element.120), channel_id=1, source_target_pairs={{0,2},{2,0},{4,6},{6,4},{8,10},{10,8},{12,14},{14,12},{16,18},{18,... | collective-permute-start | bytes 786440 | tf_op jit(solution)/shard_map/ppermute | solution.py:341
  5.8 14.0 %collective-permute-start.1 = (f32[256,256]{1,0:T(8,128)S(1)}, f32[256,256]{1,0:T(8,128)S(1)}, u32[]{:S(2)}, u32[]{:S(2)}) collective-permute-start(f32[256,256]{1,0:T(8,128)S(1)} %get-tuple-element.121), channel_id=1, source_target_pairs={{0,4},{2,6},{4,0},{6,2},{8,12},{10,14},{12,8},{14,10},{16,20},{18,... | collective-permute-start | bytes 786440 | tf_op jit(solution)/shard_map/ppermute | solution.py:341
  7.3 12.8 %collective-permute-start.2 = (f32[256,256]{1,0:T(8,128)S(1)}, f32[256,256]{1,0:T(8,128)S(1)}, u32[]{:S(2)}, u32[]{:S(2)}) collective-permute-start(f32[256,256]{1,0:T(8,128)S(1)} %get-tuple-element.122), channel_id=1, source_target_pairs={{0,6},{2,4},{4,2},{6,0},{8,14},{10,12},{12,10},{14,8},{16,22},{18,... | collective-permute-start | bytes 786440 | tf_op jit(solution)/shard_map/ppermute | solution.py:341
  9.1 0.7 copy-start.7
  9.8 14.4 %collective-permute-start.3 = (f32[256,256]{1,0:T(8,128)}, f32[256,256]{1,0:T(8,128)S(1)}, u32[]{:S(2)}, u32[]{:S(2)}) collective-permute-start(f32[256,256]{1,0:T(8,128)} %get-tuple-element.124), channel_id=1, source_target_pairs={{0,2},{2,0},{4,6},{6,4},{8,10},{10,8},{12,14},{14,12},{16,18},{18,... | collective-permute-start | bytes 786440 | tf_op jit(solution)/shard_map/ppermute | solution.py:341
  11.7 18.7 %collective-permute-start.4 = (f32[256,256]{1,0:T(8,128)}, f32[256,256]{1,0:T(8,128)S(1)}, u32[]{:S(2)}, u32[]{:S(2)}) collective-permute-start(f32[256,256]{1,0:T(8,128)} %get-tuple-element.125), channel_id=1, source_target_pairs={{0,4},{2,6},{4,0},{6,2},{8,12},{10,14},{12,8},{14,10},{16,20},{18,... | collective-permute-start | bytes 786440 | tf_op jit(solution)/shard_map/ppermute | solution.py:341
  13.2 17.1 %collective-permute-start.5 = (f32[256,256]{1,0:T(8,128)S(1)}, f32[256,256]{1,0:T(8,128)S(1)}, u32[]{:S(2)}, u32[]{:S(2)}) collective-permute-start(f32[256,256]{1,0:T(8,128)S(1)} %get-tuple-element.126), channel_id=1, source_target_pairs={{0,6},{2,4},{4,2},{6,0},{8,14},{10,12},{12,10},{14,8},{16,22},{18,... | collective-permute-start | bytes 786440 | tf_op jit(solution)/shard_map/ppermute | solution.py:341
  15.9 14.5 %copy-start.8 = (bf16[256,256]{1,0:T(8,128)(2,1)S(1)}, bf16[256,256]{1,0:T(8,128)(2,1)}, u32[]{:S(2)}) copy-start(bf16[256,256]{1,0:T(8,128)(2,1)} %copy-done.7) | copy-start | bytes 393220
  30.4 4.5 %copy-start.1 = (bf16[1,256,4,256]{3,2,1,0:T(4,128)(2,1)S(1)}, bf16[1,256,4,256]{3,2,1,0:T(4,128)(2,1)}, u32[]{:S(2)}) copy-start(bf16[1,256,4,256]{3,2,1,0:T(4,128)(2,1)} %param.10) | copy-start | bytes 1572868
  30.4 4.5 %copy-start.2 = (bf16[1,256,4,256]{3,2,1,0:T(4,128)(2,1)S(1)}, bf16[1,256,4,256]{3,2,1,0:T(4,128)(2,1)}, u32[]{:S(2)}) copy-start(bf16[1,256,4,256]{3,2,1,0:T(4,128)(2,1)} %param.19) | copy-start | bytes 1572868
  32.6 1.7 %copy-start.9 = (f32[4]{0:T(128)S(1)}, f32[4]{0:T(128)}, u32[]{:S(2)}) copy-start(f32[4]{0:T(128)} %param.14) | copy-start | bytes 52
  32.6 2.2 %copy-start.3 = (f32[4,256]{1,0:T(4,128)S(1)}, f32[4,256]{1,0:T(4,128)}, u32[]{:S(2)}) copy-start(f32[4,256]{1,0:T(4,128)} %gain.1) | copy-start | bytes 12292
  32.6 6.3 %collective-permute-start.6 = (f32[1,3,64,256]{3,2,1,0:T(8,128)S(1)}, f32[1,3,64,256]{3,2,1,0:T(8,128)S(1)}, u32[]{:S(2)}, u32[]{:S(2)}) collective-permute-start(f32[1,3,64,256]{3,2,1,0:T(8,128)S(1)} %get-tuple-element.139), channel_id=1, source_target_pairs={{0,8},{2,10},{4,12},{6,14},{8,0},{10,2},{12,4},{14,6},{16,24},{18,... | collective-permute-start | bytes 589832 | tf_op jit(solution)/shard_map/ppermute | solution.py:341
  36.8 13.1 %collective-permute-start.9 = (f32[2,256,256]{2,1,0:T(8,128)S(1)}, f32[2,256,256]{2,1,0:T(8,128)S(1)}, u32[]{:S(2)}, u32[]{:S(2)}) collective-permute-start(f32[2,256,256]{2,1,0:T(8,128)S(1)} %get-tuple-element.145), channel_id=1, source_target_pairs={{0,2},{2,0},{4,6},{6,4},{8,10},{10,8},{12,14},{14,12},{16,18},{18,... | collective-permute-start | bytes 1572872 | tf_op jit(solution)/shard_map/ppermute | solution.py:341
  38.1 12.2 %collective-permute-start.10 = (f32[2,256,256]{2,1,0:T(8,128)S(1)}, f32[2,256,256]{2,1,0:T(8,128)S(1)}, u32[]{:S(2)}, u32[]{:S(2)}) collective-permute-start(f32[2,256,256]{2,1,0:T(8,128)S(1)} %get-tuple-element.146), channel_id=1, source_target_pairs={{0,4},{2,6},{4,0},{6,2},{8,12},{10,14},{12,8},{14,10},{16,20},{18,... | collective-permute-start | bytes 1572872 | tf_op jit(solution)/shard_map/ppermute | solution.py:341
  39.0 10.0 %collective-permute-start.8 = (f32[1,3,64,256]{3,2,1,0:T(8,128)S(1)}, f32[1,3,64,256]{3,2,1,0:T(8,128)S(1)}, u32[]{:S(2)}, u32[]{:S(2)}) collective-permute-start(f32[1,3,64,256]{3,2,1,0:T(8,128)S(1)} %add.40), channel_id=1, source_target_pairs={{0,16},{2,18},{4,20},{6,22},{8,24},{10,26},{12,28},{14,30},{16,0},... | collective-permute-start | bytes 589832 | tf_op jit(solution)/shard_map/ppermute | solution.py:341
  41.6 8.2 %collective-permute-start.7 = (f32[1,3,64,256]{3,2,1,0:T(8,128)S(1)}, f32[1,3,64,256]{3,2,1,0:T(8,128)S(1)}, u32[]{:S(2)}, u32[]{:S(2)}) collective-permute-start(f32[1,3,64,256]{3,2,1,0:T(8,128)S(1)} %get-tuple-element.141), channel_id=1, source_target_pairs={{0,8},{2,10},{4,12},{6,14},{8,0},{10,2},{12,4},{14,6},{16,24},{18,... | collective-permute-start | bytes 589832 | tf_op jit(solution)/shard_map/ppermute | solution.py:341
  50.4 16.7 %collective-permute-start.11 = (f32[2,256,256]{2,1,0:T(8,128)S(1)}, f32[2,256,256]{2,1,0:T(8,128)S(1)}, u32[]{:S(2)}, u32[]{:S(2)}) collective-permute-start(f32[2,256,256]{2,1,0:T(8,128)S(1)} %get-tuple-element.151), channel_id=1, source_target_pairs={{0,6},{2,4},{4,2},{6,0},{8,14},{10,12},{12,10},{14,8},{16,22},{18,... | collective-permute-start | bytes 1572872 | tf_op jit(solution)/shard_map/ppermute | solution.py:341
  51.5 9.9 %collective-permute-start.13 = (f32[1,3,64,256]{3,2,1,0:T(8,128)S(1)}, f32[1,3,64,256]{3,2,1,0:T(8,128)S(1)}, u32[]{:S(2)}, u32[]{:S(2)}) collective-permute-start(f32[1,3,64,256]{3,2,1,0:T(8,128)S(1)} %add_add_fusion.1.refs_4_), channel_id=1, source_target_pairs={{0,16},{2,18},{4,20},{6,22},{8,24},{10,26},{12,28},{14,30},{16,0},... | collective-permute-start | bytes 589832 | tf_op jit(solution)/shard_map/ppermute | solution.py:341
  53.5 8.2 %collective-permute-start.12 = (f32[1,3,64,256]{3,2,1,0:T(8,128)S(1)}, f32[1,3,64,256]{3,2,1,0:T(8,128)S(1)}, u32[]{:S(2)}, u32[]{:S(2)}) collective-permute-start(f32[1,3,64,256]{3,2,1,0:T(8,128)S(1)} %add_add_fusion.1.refs_4_), channel_id=1, source_target_pairs={{0,8},{2,10},{4,12},{6,14},{8,0},{10,2},{12,4},{14,6},{16,24},{18,... | collective-permute-start | bytes 589832 | tf_op jit(solution)/shard_map/ppermute | solution.py:341
  61.4 5.7 %collective-permute-start.14 = (f32[1,3,64,256]{3,2,1,0:T(8,128)S(1)}, f32[1,3,64,256]{3,2,1,0:T(8,128)S(1)}, u32[]{:S(2)}, u32[]{:S(2)}) collective-permute-start(f32[1,3,64,256]{3,2,1,0:T(8,128)S(1)} %collective-permute-done.13.refs_6_), channel_id=1, source_target_pairs={{0,8},{2,10},{4,12},{6,14},{8,0},{10,2},{12,4},{14,6},{16,24},{18,... | collective-permute-start | bytes 589832 | tf_op jit(solution)/shard_map/ppermute | solution.py:341
  68.9 1.2 collective-permute-start.15
  70.1 3.7 %collective-permute-start.16 = (f32[2,4,256]{2,1,0:T(4,128)S(1)}, f32[2,4,256]{2,1,0:T(4,128)S(1)}, u32[]{:S(2)}, u32[]{:S(2)}) collective-permute-start(f32[2,4,256]{2,1,0:T(4,128)S(1)} %add.42), channel_id=1, source_target_pairs={{0,2},{2,0},{4,6},{6,4},{8,10},{10,8},{12,14},{14,12},{16,18},{18,... | collective-permute-start | bytes 24584 | tf_op jit(solution)/shard_map/ppermute | solution.py:341
  73.7 3.7 %collective-permute-start.17 = (f32[2,4,256]{2,1,0:T(4,128)S(1)}, f32[2,4,256]{2,1,0:T(4,128)S(1)}, u32[]{:S(2)}, u32[]{:S(2)}) collective-permute-start(f32[2,4,256]{2,1,0:T(4,128)S(1)} %add.43), channel_id=1, source_target_pairs={{0,4},{2,6},{4,0},{6,2},{8,12},{10,14},{12,8},{14,10},{16,20},{18,... | collective-permute-start | bytes 24584 | tf_op jit(solution)/shard_map/ppermute | solution.py:341
  79.4 5.7 %collective-permute-start.18 = (f32[1,3,64,256]{3,2,1,0:T(8,128)S(1)}, f32[1,3,64,256]{3,2,1,0:T(8,128)S(1)}, u32[]{:S(2)}, u32[]{:S(2)}) collective-permute-start(f32[1,3,64,256]{3,2,1,0:T(8,128)S(1)} %get-tuple-element.166), channel_id=1, source_target_pairs={{0,8},{2,10},{4,12},{6,14},{8,0},{10,2},{12,4},{14,6},{16,24},{18,... | collective-permute-start | bytes 589832 | tf_op jit(solution)/shard_map/ppermute | solution.py:341
  85.2 11.5 %collective-permute-start.20 = (f32[1,3,64,256]{3,2,1,0:T(8,128)S(1)}, f32[1,3,64,256]{3,2,1,0:T(8,128)S(1)}, u32[]{:S(2)}, u32[]{:S(2)}) collective-permute-start(f32[1,3,64,256]{3,2,1,0:T(8,128)S(1)} %add.46), channel_id=1, source_target_pairs={{0,16},{2,18},{4,20},{6,22},{8,24},{10,26},{12,28},{14,30},{16,0},... | collective-permute-start | bytes 589832 | tf_op jit(solution)/shard_map/ppermute | solution.py:341
  85.9 10.8 %collective-permute-start.19 = (f32[1,3,64,256]{3,2,1,0:T(8,128)S(1)}, f32[1,3,64,256]{3,2,1,0:T(8,128)S(1)}, u32[]{:S(2)}, u32[]{:S(2)}) collective-permute-start(f32[1,3,64,256]{3,2,1,0:T(8,128)S(1)} %get-tuple-element.168), channel_id=1, source_target_pairs={{0,8},{2,10},{4,12},{6,14},{8,0},{10,2},{12,4},{14,6},{16,24},{18,... | collective-permute-start | bytes 589832 | tf_op jit(solution)/shard_map/ppermute | solution.py:341
  96.7 8.2 %collective-permute-start.22 = (f32[1,3,64,256]{3,2,1,0:T(8,128)S(1)}, f32[1,3,64,256]{3,2,1,0:T(8,128)S(1)}, u32[]{:S(2)}, u32[]{:S(2)}) collective-permute-start(f32[1,3,64,256]{3,2,1,0:T(8,128)S(1)} %add_add_fusion.refs_11_.refs_0_), channel_id=1, source_target_pairs={{0,16},{2,18},{4,20},{6,22},{8,24},{10,26},{12,28},{14,30},{16,0},... | collective-permute-start | bytes 589832 | tf_op jit(solution)/shard_map/ppermute | solution.py:341
  97.2 8.8 %collective-permute-start.24 = (f32[256,256]{1,0:T(8,128)S(1)}, f32[256,256]{1,0:T(8,128)S(1)}, u32[]{:S(2)}, u32[]{:S(2)}) collective-permute-start(f32[256,256]{1,0:T(8,128)S(1)} %get-tuple-element.174), channel_id=1, source_target_pairs={{0,2},{2,0},{4,6},{6,4},{8,10},{10,8},{12,14},{14,12},{16,18},{18,... | collective-permute-start | bytes 786440 | tf_op jit(solution)/shard_map/ppermute | solution.py:341
  98.8 9.2 %collective-permute-start.25 = (f32[256,256]{1,0:T(8,128)S(1)}, f32[256,256]{1,0:T(8,128)S(1)}, u32[]{:S(2)}, u32[]{:S(2)}) collective-permute-start(f32[256,256]{1,0:T(8,128)S(1)} %get-tuple-element.175), channel_id=1, source_target_pairs={{0,4},{2,6},{4,0},{6,2},{8,12},{10,14},{12,8},{14,10},{16,20},{18,... | collective-permute-start | bytes 786440 | tf_op jit(solution)/shard_map/ppermute | solution.py:341
  98.8 9.2 %collective-permute-start.26 = (f32[256,256]{1,0:T(8,128)S(1)}, f32[256,256]{1,0:T(8,128)S(1)}, u32[]{:S(2)}, u32[]{:S(2)}) collective-permute-start(f32[256,256]{1,0:T(8,128)S(1)} %get-tuple-element.176), channel_id=1, source_target_pairs={{0,6},{2,4},{4,2},{6,0},{8,14},{10,12},{12,10},{14,8},{16,22},{18,... | collective-permute-start | bytes 786440 | tf_op jit(solution)/shard_map/ppermute | solution.py:341
  100.8 8.9 %collective-permute-start.21 = (f32[1,3,64,256]{3,2,1,0:T(8,128)S(1)}, f32[1,3,64,256]{3,2,1,0:T(8,128)S(1)}, u32[]{:S(2)}, u32[]{:S(2)}) collective-permute-start(f32[1,3,64,256]{3,2,1,0:T(8,128)S(1)} %add_add_fusion.refs_11_.refs_0_), channel_id=1, source_target_pairs={{0,8},{2,10},{4,12},{6,14},{8,0},{10,2},{12,4},{14,6},{16,24},{18,... | collective-permute-start | bytes 589832 | tf_op jit(solution)/shard_map/ppermute | solution.py:341
  104.9 5.7 %collective-permute-start.23 = (f32[1,3,64,256]{3,2,1,0:T(8,128)S(1)}, f32[1,3,64,256]{3,2,1,0:T(8,128)S(1)}, u32[]{:S(2)}, u32[]{:S(2)}) collective-permute-start(f32[1,3,64,256]{3,2,1,0:T(8,128)S(1)} %collective-permute-done.22.refs_13_), channel_id=1, source_target_pairs={{0,8},{2,10},{4,12},{6,14},{8,0},{10,2},{12,4},{14,6},{16,24},{18,... | collective-permute-start | bytes 589832 | tf_op jit(solution)/shard_map/ppermute | solution.py:341
  113.6 18.5 %collective-permute-start.30 = (f32[3,256,256]{2,1,0:T(8,128)S(1)}, f32[3,256,256]{2,1,0:T(8,128)S(1)}, u32[]{:S(2)}, u32[]{:S(2)}) collective-permute-start(f32[3,256,256]{2,1,0:T(8,128)S(1)} %get-tuple-element.209), channel_id=1, source_target_pairs={{0,2},{2,0},{4,6},{6,4},{8,10},{10,8},{12,14},{14,12},{16,18},{18,... | collective-permute-start | bytes 2359304 | tf_op jit(solution)/shard_map/ppermute | solution.py:341
  115.1 17.0 %collective-permute-start.31 = (f32[3,256,256]{2,1,0:T(8,128)S(1)}, f32[3,256,256]{2,1,0:T(8,128)S(1)}, u32[]{:S(2)}, u32[]{:S(2)}) collective-permute-start(f32[3,256,256]{2,1,0:T(8,128)S(1)} %get-tuple-element.210), channel_id=1, source_target_pairs={{0,4},{2,6},{4,0},{6,2},{8,12},{10,14},{12,8},{14,10},{16,20},{18,... | collective-permute-start | bytes 2359304 | tf_op jit(solution)/shard_map/ppermute | solution.py:341
  115.2 8.1 %collective-permute-start.27 = (f32[1,3,64,256]{3,2,1,0:T(8,128)S(1)}, f32[1,3,64,256]{3,2,1,0:T(8,128)S(1)}, u32[]{:S(2)}, u32[]{:S(2)}) collective-permute-start(f32[1,3,64,256]{3,2,1,0:T(8,128)S(1)} %get-tuple-element.203), channel_id=1, source_target_pairs={{0,8},{2,10},{4,12},{6,14},{8,0},{10,2},{12,4},{14,6},{16,24},{18,... | collective-permute-start | bytes 589832 | tf_op jit(solution)/shard_map/ppermute | solution.py:341
  123.3 8.7 %collective-permute-start.29 = (f32[1,3,64,256]{3,2,1,0:T(8,128)S(1)}, f32[1,3,64,256]{3,2,1,0:T(8,128)S(1)}, u32[]{:S(2)}, u32[]{:S(2)}) collective-permute-start(f32[1,3,64,256]{3,2,1,0:T(8,128)S(1)} %add.48), channel_id=1, source_target_pairs={{0,16},{2,18},{4,20},{6,22},{8,24},{10,26},{12,28},{14,30},{16,0},... | collective-permute-start | bytes 589832 | tf_op jit(solution)/shard_map/ppermute | solution.py:341
  124.6 7.5 %collective-permute-start.28 = (f32[1,3,64,256]{3,2,1,0:T(8,128)S(1)}, f32[1,3,64,256]{3,2,1,0:T(8,128)S(1)}, u32[]{:S(2)}, u32[]{:S(2)}) collective-permute-start(f32[1,3,64,256]{3,2,1,0:T(8,128)S(1)} %get-tuple-element.205), channel_id=1, source_target_pairs={{0,8},{2,10},{4,12},{6,14},{8,0},{10,2},{12,4},{14,6},{16,24},{18,... | collective-permute-start | bytes 589832 | tf_op jit(solution)/shard_map/ppermute | solution.py:341
  132.2 6.4 %collective-permute-start.36 = (f32[256,256]{1,0:T(8,128)S(1)}, f32[256,256]{1,0:T(8,128)S(1)}, u32[]{:S(2)}, u32[]{:S(2)}) collective-permute-start(f32[256,256]{1,0:T(8,128)S(1)} %slice_bitcast_fusion), channel_id=1, source_target_pairs={{0,2},{2,0},{4,6},{6,4},{8,10},{10,8},{12,14},{14,12},{16,18},{18,... | collective-permute-start | bytes 786440 | tf_op jit(solution)/shard_map/ppermute | solution.py:341
  133.2 6.4 %collective-permute-start.35 = (f32[256,256]{1,0:T(8,128)S(1)}, f32[256,256]{1,0:T(8,128)S(1)}, u32[]{:S(2)}, u32[]{:S(2)}) collective-permute-start(f32[256,256]{1,0:T(8,128)S(1)} %slice_bitcast_fusion.1), channel_id=1, source_target_pairs={{0,4},{2,6},{4,0},{6,2},{8,12},{10,14},{12,8},{14,10},{16,20},{18,... | collective-permute-start | bytes 786440 | tf_op jit(solution)/shard_map/ppermute | solution.py:341
  134.6 7.3 %collective-permute-start.32 = (f32[1,3,16,256]{3,2,1,0:T(8,128)S(1)}, f32[1,3,16,256]{3,2,1,0:T(8,128)S(1)}, u32[]{:S(2)}, u32[]{:S(2)}) collective-permute-start(f32[1,3,16,256]{3,2,1,0:T(8,128)S(1)} %get-tuple-element.215), channel_id=1, source_target_pairs={{0,2},{2,0},{4,6},{6,4},{8,10},{10,8},{12,14},{14,12},{16,18},{18,... | collective-permute-start | bytes 147464 | tf_op jit(solution)/shard_map/ppermute | solution.py:341
  136.1 5.9 %collective-permute-start.33 = (f32[1,3,16,256]{3,2,1,0:T(8,128)S(1)}, f32[1,3,16,256]{3,2,1,0:T(8,128)S(1)}, u32[]{:S(2)}, u32[]{:S(2)}) collective-permute-start(f32[1,3,16,256]{3,2,1,0:T(8,128)S(1)} %get-tuple-element.216), channel_id=1, source_target_pairs={{0,4},{2,6},{4,0},{6,2},{8,12},{10,14},{12,8},{14,10},{16,20},{18,... | collective-permute-start | bytes 147464 | tf_op jit(solution)/shard_map/ppermute | solution.py:341
  136.9 5.0 %collective-permute-start.34 = (f32[1,3,16,256]{3,2,1,0:T(8,128)S(1)}, f32[1,3,16,256]{3,2,1,0:T(8,128)S(1)}, u32[]{:S(2)}, u32[]{:S(2)}) collective-permute-start(f32[1,3,16,256]{3,2,1,0:T(8,128)S(1)} %get-tuple-element.217), channel_id=1, source_target_pairs={{0,6},{2,4},{4,2},{6,0},{8,14},{10,12},{12,10},{14,8},{16,22},{18,... | collective-permute-start | bytes 147464 | tf_op jit(solution)/shard_map/ppermute | solution.py:341

commit v15 on v14

--- a/solution.py
+++ b/solution.py
@@ -78,12 +78,13 @@
 
 
 def split_apply_kernel(groups, place, q, cot, gain, scale, *rest):
-    outs, scale_row, scratch = rest[:groups], rest[groups], rest[groups + 1]
+    outs, scale_row, scratch = rest[:-2], rest[-2], rest[-1]
     scale_row[...] = jnp.broadcast_to(scale[...], scale_row.shape)
-    split_kernel(groups, place, q, *[out.at[0] for out in outs], scratch)
-    split_kernel(groups, place, cot, *[out.at[1] for out in outs], scratch)
+    pieces = query_refs(groups, outs)
+    split_kernel(groups, place, q, *[one for one, _ in pieces], scratch)
+    split_kernel(groups, place, cot, *[two for _, two in pieces], scratch)
     for step in range(groups):
-        outs[step][1] *= gain[pl.ds(place[0] ^ step, 1), :]
+        pieces[step][1][...] *= gain[pl.ds(place[0] ^ step, 1), :]
 
 
 def packing(groups):
@@ -158,19 +159,28 @@
 
 def assemble(place, parts, whole):
     rows = parts[0].shape[2]
-    for step, part in enumerate(parts):
-        at = pl.multiple_of((place[1] ^ step) * rows, rows)
-        whole[:, pl.ds(at, rows), :] = part[0]
+    for i, part in enumerate(parts):
+        at = pl.multiple_of((place[1] ^ (i if i < 2 else i // 2 + 1)) * rows, rows)
+        low, high = {3: (0, 3), 2: (0, 2), 1: (2, 3)}[part.shape[1]]
+        whole[low:high, pl.ds(at, rows), :] = part[0]
+
+
+def gathered(depth):
+    return max(2 * depth - 2, depth)
+
+
+def query_refs(groups, refs):
+    return [(ref.at[0], ref.at[1]) for ref in refs[:groups]]
 
 
 def apply_kernel(groups, depth, place, scale_row, *refs):
-    pieces = refs[:groups]
-    parts = refs[groups : groups + depth]
-    activ_ref, slope_ref, hidden_ref, os_ref, new_b, stats, whole = refs[groups + depth :]
+    pieces, refs = query_refs(groups, refs), refs[groups:]
+    parts = refs[: gathered(depth)]
+    activ_ref, slope_ref, hidden_ref, os_ref, new_b, stats, whole = refs[gathered(depth) :]
     assemble(place, parts, whole)
     new_b[...] = whole[...].astype(BF16)
     for step in range(groups):
-        queries = pieces[step][0].astype(BF16)
+        queries = pieces[step][0][...].astype(BF16)
         tokens = queries.shape[0]
         first = mm(queries, new_b[0])
         third = mm(queries, new_b[2])
@@ -183,7 +193,7 @@
         hidden_ref[step] = hidden
         os_ref[step] = scaled
         sq = jnp.sum(scaled * scaled, axis=1, keepdims=True)
-        ps = jnp.sum(scaled * pieces[step][1], axis=1, keepdims=True)
+        ps = jnp.sum(scaled * pieces[step][1][...], axis=1, keepdims=True)
         lane = lax.broadcasted_iota(jnp.int32, (tokens, LANES), 1)
         both = jnp.where(lane == 0, sq, jnp.where(lane == 1, ps, 0.0)).T
         source = place[0] ^ step
@@ -192,17 +202,17 @@
 
 
 def apply_back_kernel(groups, depth, count, place, scale_row, stats, *refs):
-    pieces, refs = refs[:groups], refs[groups:]
+    pieces, refs = query_refs(groups, refs), refs[groups:]
     activ_ref, slope_ref, hidden_ref, os_ref, new_b = refs[:5]
     dfirst_ref, dthird_ref, slices, sums = refs[5], refs[6], refs[7:-1], refs[-1]
     total = [0.0, 0.0, 0.0]
     for step in range(groups):
-        queries = pieces[step][0].astype(BF16)
+        queries = pieces[step][0][...].astype(BF16)
         source = place[0] ^ step
         sq = rate_column(stats.at[0], source)
         ps = rate_column(stats.at[1], source)
         inv = lax.rsqrt(sq / count + 1e-06)
-        dos = inv * pieces[step][1] - os_ref[step] * (inv * inv * inv * ps / count)
+        dos = inv * pieces[step][1][...] - os_ref[step] * (inv * inv * inv * ps / count)
         dout = (dos * scale_row[0:1, :]).astype(BF16)
         dhidden = mm_t(dout, new_b[1])
         dthird = (dhidden * activ_ref[step]).astype(BF16)
@@ -250,7 +260,7 @@
     (k_kept, s_kept), refs = refs[:2], refs[2:]
     kept, refs = refs[:9], refs[9:]
     dact_r, third_r, activ_r, deriv_r, slope_r, second_r, dfirst_r, dthird_r, act_r = kept
-    parts, refs = refs[:depth], refs[depth:]
+    parts, refs = refs[: gathered(depth)], refs[gathered(depth) :]
     w_gate, w_out, w_up = refs[:3]
     packed = len(packing(groups))
     outs, slices = unpacked(groups, refs[3 : packed + 3]), refs[packed + 3 : -2]
@@ -356,12 +366,10 @@
         return [outs[-1]] + first + even
 
     def gather(part, count, unit):
-        got = [part] * count
-        for r in [2 * i for i in range(1, count // 2)]:
-            got[r] = move(part, "ctx", r * unit)
-            got[r + 1] = move(got[r], "ctx", unit)
-        if count > 1:
-            got[1] = move(part, "ctx", unit)
+        got = [part, move(part, "ctx", unit)][:count]
+        for r in range(2, count, 2):
+            sent = [move(part[:, i : i + 2], "ctx", r * unit) for i in (0, 2)]
+            got += sent + [move(x, "ctx", unit) for x in sent]
         return got
 
     def after(x, *others):
@@ -434,11 +442,12 @@
     )
     part = functools.reduce(jnp.add, scatter(out, depth, groups))
     parts = gather(part, depth, groups)
+    q_back = in_plane(q_sent)
+    parts, saved, q_back = after(parts, saved, q_back)
     (grad_q,) = call(
         functools.partial(join_query_kernel, groups), [joined], [scratch], flops // 16,
-        place, *in_plane(q_sent),
-    )
-    parts, grad_q, saved = after(parts, grad_q, saved)
+        place, *q_back,
+    )
     rows = hidden // depth
     out = call(
         functools.partial(update_back_kernel, groups, depth, scale),
@@ -449,7 +458,7 @@
     back = in_plane(out[:packed])
     ends = scatter(out[packed:], depth, groups)
     if groups == 4:
-        ends, back = after(ends, back)
+        ends, back, grad_q = after(ends, back, grad_q)
         back += [move(back[1][2], "ctx", 2), move(back[2][2], "ctx", 1)]
     own_rows = rows // groups
     sent = call(

time: 143 us -> 144 us (level)
  starting transfers between devices: 47.9 us -> 53.5 us
  waiting for transfers between devices: 69.5 us -> 64.1 us
    ppermute x37 -> x41, starting transfers between devices: 47.9 us -> 53.5 us  [move(): lax.ppermute(x, axis, [(c, c ^ step) for c in range(lax.axis_size(axis))])]
    ppermute x37 -> x41, waiting for transfers between devices: 69.5 us -> 64.1 us  [move(): lax.ppermute(x, axis, [(c, c ^ step) for c in range(lax.axis_size(axis))])]
  transfers between devices with their start and end apart: 37 -> 41, of which waited for: 22 -> 22; matrix products, arithmetic and copies ran while one was open for 1% -> 1% of each run, Pallas kernels for 7% -> 7%
where the time goes in v15:
time: 144 us
  waiting for transfers between devices  64.1 us (45%)
  starting transfers between devices  53.5 us (37%)
  Pallas kernels  21.2 us (15%)
  local copies, waits for them, and re-layouts  4.2 us (3%)
    ppermute x41, waiting for transfers between devices, move(): lax.ppermute(x, axis, [(c, c ^ step) for c in range(lax.axis_size(axis))])  64.1 us
    ppermute x41, starting transfers between devices, move(): lax.ppermute(x, axis, [(c, c ^ step) for c in range(lax.axis_size(axis))])  53.5 us
    pallas_call x13, Pallas kernels, call(): pl.pallas_call(body, out_shape=out_shape, in_specs=[smem if a.dtype == jn...  21.2 us
  transfers between devices with their start and end apart: 41, of which 22 were waited for; matrix products, arithmetic and copies ran while one was open for 1% of the time, Pallas kernels for 7%

profile of v15, /device:TPU:0, one launch (start us, length us, event | category | flops | bytes accessed | tf_op | source)
XLA Modules:
  0.0 144.2 jit_solution(16451539936384143235)
XLA Ops:
  0.7 0.7 copy-done.4
  1.4 1.0 copy-done.5
  2.5 1.1 shard_map.146
  3.6 3.0 %collective-permute-start.3 = (f32[256,256]{1,0:T(8,128)S(1)}, f32[256,256]{1,0:T(8,128)S(1)}, u32[]{:S(2)}, u32[]{:S(2)}) collective-permute-start(f32[256,256]{1,0:T(8,128)S(1)} %get-tuple-element.130), channel_id=1, source_target_pairs={{0,2},{2,0},{4,6},{6,4},{8,10},{10,8},{12,14},{14,12},{16,18},{18,... | collective-permute-start | bytes 786440 | tf_op jit(solution)/shard_map/ppermute | solution.py:351
  6.6 1.5 %collective-permute-start.4 = (f32[256,256]{1,0:T(8,128)S(1)}, f32[256,256]{1,0:T(8,128)S(1)}, u32[]{:S(2)}, u32[]{:S(2)}) collective-permute-start(f32[256,256]{1,0:T(8,128)S(1)} %get-tuple-element.131), channel_id=1, source_target_pairs={{0,4},{2,6},{4,0},{6,2},{8,12},{10,14},{12,8},{14,10},{16,20},{18,... | collective-permute-start | bytes 786440 | tf_op jit(solution)/shard_map/ppermute | solution.py:351
  8.1 1.7 %shard_map.145 = (bf16[256,256]{1,0:T(8,128)(2,1)S(1)}, f32[256,256]{1,0:T(8,128)}, f32[256,256]{1,0:T(8,128)}, f32[256,256]{1,0:T(8,128)S(1)}) custom-call(s32[2]{0:T(128)S(1)} %pad_add_fusion.place, bf16[256,4,256]{2,1,0:T(4,128)(2,1)S(1)} %bitcast.26), custom_call_target="tpu_custom_call" | custom-call | flops 2147483648 | bytes 1441800 | tf_op jit(solution)/shard_map/pallas_call | solution.py:34
  9.8 0.7 copy-done.7
  10.4 1.9 %collective-permute-start = (f32[256,256]{1,0:T(8,128)}, f32[256,256]{1,0:T(8,128)S(1)}, u32[]{:S(2)}, u32[]{:S(2)}) collective-permute-start(f32[256,256]{1,0:T(8,128)} %get-tuple-element.126), channel_id=1, source_target_pairs={{0,2},{2,0},{4,6},{6,4},{8,10},{10,8},{12,14},{14,12},{16,18},{18,... | collective-permute-start | bytes 786440 | tf_op jit(solution)/shard_map/ppermute | solution.py:351
  12.4 1.5 %collective-permute-start.1 = (f32[256,256]{1,0:T(8,128)}, f32[256,256]{1,0:T(8,128)S(1)}, u32[]{:S(2)}, u32[]{:S(2)}) collective-permute-start(f32[256,256]{1,0:T(8,128)} %get-tuple-element.127), channel_id=1, source_target_pairs={{0,4},{2,6},{4,0},{6,2},{8,12},{10,14},{12,8},{14,10},{16,20},{18,... | collective-permute-start | bytes 786440 | tf_op jit(solution)/shard_map/ppermute | solution.py:351
  13.9 2.8 %collective-permute-start.2 = (f32[256,256]{1,0:T(8,128)S(1)}, f32[256,256]{1,0:T(8,128)S(1)}, u32[]{:S(2)}, u32[]{:S(2)}) collective-permute-start(f32[256,256]{1,0:T(8,128)S(1)} %get-tuple-element.128), channel_id=1, source_target_pairs={{0,6},{2,4},{4,2},{6,0},{8,14},{10,12},{12,10},{14,8},{16,22},{18,... | collective-permute-start | bytes 786440 | tf_op jit(solution)/shard_map/ppermute | solution.py:351
  16.7 1.1 dynamic-slice_bitcast_fusion
  17.9 2.8 %collective-permute-done.4.refs_6_ = f32[256,256]{1,0:T(8,128)S(1)} collective-permute-done((f32[256,256]{1,0:T(8,128)S(1)}, f32[256,256]{1,0:T(8,128)S(1)}, u32[]{:S(2)}, u32[]{:S(2)}) %collective-permute-start.4) | collective-permute-done | bytes 262176 | tf_op jit(solution)/shard_map/ppermute | solution.py:351
  20.9 4.1 %collective-permute-done.refs_1_ = f32[256,256]{1,0:T(8,128)S(1)} collective-permute-done((f32[256,256]{1,0:T(8,128)}, f32[256,256]{1,0:T(8,128)S(1)}, u32[]{:S(2)}, u32[]{:S(2)}) %collective-permute-start) | collective-permute-done | bytes 262176 | tf_op jit(solution)/shard_map/ppermute | solution.py:351
  25.0 6.2 %collective-permute-done.1.refs_2_ = f32[256,256]{1,0:T(8,128)S(1)} collective-permute-done((f32[256,256]{1,0:T(8,128)}, f32[256,256]{1,0:T(8,128)S(1)}, u32[]{:S(2)}, u32[]{:S(2)}) %collective-permute-start.1) | collective-permute-done | bytes 262176 | tf_op jit(solution)/shard_map/ppermute | solution.py:351
  31.2 2.2 %shard_map.148 = (bf16[4,256,256]{2,1,0:T(8,128)(2,1)S(1)}, bf16[4,256,256]{2,1,0:T(8,128)(2,1)S(1)}, f32[1,3,64,256]{3,2,1,0:T(8,128)S(1)}, f32[1,3,64,256]{3,2...) custom-call(s32[2]{0:T(128)S(1)} %pad_add_fusion.place, bf16[256,256]{1,0:T(8,128)(2,1)S(1)} %copy-done.8, ...), custom_call_target="tpu_custom_call" | custom-call | flops 805306368 | bytes 4456456 | tf_op jit(solution)/shard_map/pallas_call | solution.py:34
  33.4 1.6 %collective-permute-start.6 = (f32[1,3,64,256]{3,2,1,0:T(8,128)S(1)}, f32[1,3,64,256]{3,2,1,0:T(8,128)S(1)}, u32[]{:S(2)}, u32[]{:S(2)}) collective-permute-start(f32[1,3,64,256]{3,2,1,0:T(8,128)S(1)} %get-tuple-element.145), channel_id=1, source_target_pairs={{0,8},{2,10},{4,12},{6,14},{8,0},{10,2},{12,4},{14,6},{16,24},{18,... | collective-permute-start | bytes 589832 | tf_op jit(solution)/shard_map/ppermute | solution.py:351
  35.1 0.6 dynamic_slice.14
  35.7 1.9 %shard_map.147 = (f32[2,256,256]{2,1,0:T(8,128)S(1)}, f32[2,256,256]{2,1,0:T(8,128)S(1)}, f32[2,256,256]{2,1,0:T(8,128)S(1)}, f32[2,256,256]{2,1,0:T(8,128)S(1)}, f32[8,256]{1,0:T(8,128)S(1)}) custom-call(s32[2]{0:T(128)S(1)} %pad_add_fusion.place, bf16[256,4,256]{2,1,0:T(4,128)(2,1)S(1)} %bitcast.21, bf16[256,4,256]{2,1,0:T(4,128)(2,1)S(1)} %bitcast.22, ...), custom_call_target="tpu_custom_call" | custom-call | flops 16777216 | bytes 3158028 | tf_op jit(solution)/shard_map/pallas_call | solution.py:34
  37.6 1.6 %collective-permute-start.10 = (f32[2,256,256]{2,1,0:T(8,128)S(1)}, f32[2,256,256]{2,1,0:T(8,128)S(1)}, u32[]{:S(2)}, u32[]{:S(2)}) collective-permute-start(f32[2,256,256]{2,1,0:T(8,128)S(1)} %get-tuple-element.152), channel_id=1, source_target_pairs={{0,4},{2,6},{4,0},{6,2},{8,12},{10,14},{12,8},{14,10},{16,20},{18,... | collective-permute-start | bytes 1572872 | tf_op jit(solution)/shard_map/ppermute | solution.py:351
  39.8 2.7 %collective-permute-start.8 = (f32[1,3,64,256]{3,2,1,0:T(8,128)S(1)}, f32[1,3,64,256]{3,2,1,0:T(8,128)S(1)}, u32[]{:S(2)}, u32[]{:S(2)}) collective-permute-start(f32[1,3,64,256]{3,2,1,0:T(8,128)S(1)} %add.40), channel_id=1, source_target_pairs={{0,16},{2,18},{4,20},{6,22},{8,24},{10,26},{12,28},{14,30},{16,0},... | collective-permute-start | bytes 589832 | tf_op jit(solution)/shard_map/ppermute | solution.py:351
  42.4 1.0 collective-permute-start.7
  43.4 6.4 %collective-permute-done.8 = f32[1,3,64,256]{3,2,1,0:T(8,128)S(1)} collective-permute-done((f32[1,3,64,256]{3,2,1,0:T(8,128)S(1)}, f32[1,3,64,256]{3,2,1,0:T(8,128)S(1)}, u32[]{:S(2)}, u32[]{:S(2)}) %collective-permute-start.8) | collective-permute-done | bytes 196640 | tf_op jit(solution)/shard_map/ppermute | solution.py:351
  49.8 0.9 collective-permute-done.7
  50.7 1.9 %collective-permute-start.11 = (f32[2,256,256]{2,1,0:T(8,128)S(1)}, f32[2,256,256]{2,1,0:T(8,128)S(1)}, u32[]{:S(2)}, u32[]{:S(2)}) collective-permute-start(f32[2,256,256]{2,1,0:T(8,128)S(1)} %get-tuple-element.157), channel_id=1, source_target_pairs={{0,6},{2,4},{4,2},{6,0},{8,14},{10,12},{12,10},{14,8},{16,22},{18,... | collective-permute-start | bytes 1572872 | tf_op jit(solution)/shard_map/ppermute | solution.py:351
  52.6 2.7 %collective-permute-start.13 = (f32[1,2,64,256]{3,2,1,0:T(8,128)S(1)}, f32[1,2,64,256]{3,2,1,0:T(8,128)S(1)}, u32[]{:S(2)}, u32[]{:S(2)}) collective-permute-start(f32[1,2,64,256]{3,2,1,0:T(8,128)S(1)} %slice.18), channel_id=1, source_target_pairs={{0,16},{2,18},{4,20},{6,22},{8,24},{10,26},{12,28},{14,30},{16,0},... | collective-permute-start | bytes 393224 | tf_op jit(solution)/shard_map/ppermute | solution.py:351
  55.3 0.8 collective-permute-start.12
  56.5 4.4 %collective-permute-done.13.refs_6_ = f32[1,2,64,256]{3,2,1,0:T(8,128)S(1)} collective-permute-done((f32[1,2,64,256]{3,2,1,0:T(8,128)S(1)}, f32[1,2,64,256]{3,2,1,0:T(8,128)S(1)}, u32[]{:S(2)}, u32[]{:S(2)}) %collective-permute-start.13) | collective-permute-done | bytes 131104 | tf_op jit(solution)/shard_map/ppermute | solution.py:351
  60.9 2.4 %collective-permute-done.14.refs_7_ = f32[1,1,64,256]{3,2,1,0:T(8,128)S(1)} collective-permute-done((f32[1,1,64,256]{3,2,1,0:T(8,128)S(1)}, f32[1,1,64,256]{3,2,1,0:T(8,128)S(1)}, u32[]{:S(2)}, u32[]{:S(2)}) %collective-permute-start.14) | collective-permute-done | bytes 65568 | tf_op jit(solution)/shard_map/ppermute | solution.py:351
  63.2 1.9 %collective-permute-start.16 = (f32[1,1,64,256]{3,2,1,0:T(8,128)S(1)}, f32[1,1,64,256]{3,2,1,0:T(8,128)S(1)}, u32[]{:S(2)}, u32[]{:S(2)}) collective-permute-start(f32[1,1,64,256]{3,2,1,0:T(8,128)S(1)} %collective-permute-done.14.refs_7_), channel_id=1, source_target_pairs={{0,8},{2,10},{4,12},{6,14},{8,0},{10,2},{12,4},{14,6},{16,24},{18,... | collective-permute-start | bytes 196616 | tf_op jit(solution)/shard_map/ppermute | solution.py:351
  65.1 2.4 %collective-permute-done.16.refs_9_ = f32[1,1,64,256]{3,2,1,0:T(8,128)S(1)} collective-permute-done((f32[1,1,64,256]{3,2,1,0:T(8,128)S(1)}, f32[1,1,64,256]{3,2,1,0:T(8,128)S(1)}, u32[]{:S(2)}, u32[]{:S(2)}) %collective-permute-start.16) | collective-permute-done | bytes 65568 | tf_op jit(solution)/shard_map/ppermute | solution.py:351
  67.5 1.8 %shard_map.149 = (f32[4,256,256]{2,1,0:T(8,128)S(1)}, f32[4,256,256]{2,1,0:T(8,128)S(1)}, bf16[4,256,256]{2,1,0:T(8,128)(2,1)S(1)}, f32[4,256,256]{2,1,0:T(8,128...) custom-call(s32[2]{0:T(128)S(1)} %pad_add_fusion.place, f32[8,256]{1,0:T(8,128)S(1)} %get-tuple-element.135.scale_row, ...), custom_call_target="tpu_custom_call" | custom-call | flops 402653184 | bytes 6963208 | tf_op jit(solution)/shard_map/pallas_call | solution.py:34
  69.3 1.2 collective-permute-done.17
  70.5 1.0 collective-permute-start.18
  71.5 2.6 %collective-permute-done.18 = f32[2,4,256]{2,1,0:T(4,128)S(1)} collective-permute-done((f32[2,4,256]{2,1,0:T(4,128)S(1)}, f32[2,4,256]{2,1,0:T(4,128)S(1)}, u32[]{:S(2)}, u32[]{:S(2)}) %collective-permute-start.18) | collective-permute-done | bytes 8224 | tf_op jit(solution)/shard_map/ppermute | solution.py:351
  74.2 1.4 collective-permute-start.19
  75.5 2.3 %collective-permute-done.19 = f32[2,4,256]{2,1,0:T(4,128)S(1)} collective-permute-done((f32[2,4,256]{2,1,0:T(4,128)S(1)}, f32[2,4,256]{2,1,0:T(4,128)S(1)}, u32[]{:S(2)}, u32[]{:S(2)}) %collective-permute-start.19) | collective-permute-done | bytes 8224 | tf_op jit(solution)/shard_map/ppermute | solution.py:351
  77.8 2.0 %shard_map.150 = (bf16[4,256,256]{2,1,0:T(8,128)(2,1)S(1)}, bf16[4,256,256]{2,1,0:T(8,128)(2,1)S(1)}, f32[1,3,64,256]{3,2,1,0:T(8,128)S(1)}, f32[1,3,64,256]{3,2...) custom-call(s32[2]{0:T(128)S(1)} %pad_add_fusion.place, ...), custom_call_target="tpu_custom_call" | custom-call | flops 805306368 | bytes 8011784 | tf_op jit(solution)/shard_map/pallas_call | solution.py:34
  79.8 2.0 %collective-permute-start.20 = (f32[1,3,64,256]{3,2,1,0:T(8,128)S(1)}, f32[1,3,64,256]{3,2,1,0:T(8,128)S(1)}, u32[]{:S(2)}, u32[]{:S(2)}) collective-permute-start(f32[1,3,64,256]{3,2,1,0:T(8,128)S(1)} %get-tuple-element.174), channel_id=1, source_target_pairs={{0,8},{2,10},{4,12},{6,14},{8,0},{10,2},{12,4},{14,6},{16,24},{18,... | collective-permute-start | bytes 589832 | tf_op jit(solution)/shard_map/ppermute | solution.py:351
  81.8 3.8 %collective-permute-done.20 = f32[1,3,64,256]{3,2,1,0:T(8,128)S(1)} collective-permute-done((f32[1,3,64,256]{3,2,1,0:T(8,128)S(1)}, f32[1,3,64,256]{3,2,1,0:T(8,128)S(1)}, u32[]{:S(2)}, u32[]{:S(2)}) %collective-permute-start.20) | collective-permute-done | bytes 196640 | tf_op jit(solution)/shard_map/ppermute | solution.py:351
  85.6 4.6 %collective-permute-start.22 = (f32[1,3,64,256]{3,2,1,0:T(8,128)S(1)}, f32[1,3,64,256]{3,2,1,0:T(8,128)S(1)}, u32[]{:S(2)}, u32[]{:S(2)}) collective-permute-start(f32[1,3,64,256]{3,2,1,0:T(8,128)S(1)} %add.46), channel_id=1, source_target_pairs={{0,16},{2,18},{4,20},{6,22},{8,24},{10,26},{12,28},{14,30},{16,0},... | collective-permute-start | bytes 589832 | tf_op jit(solution)/shard_map/ppermute | solution.py:351
  91.3 3.0 %collective-permute-start.30 = (f32[256,256]{1,0:T(8,128)S(1)}, f32[256,256]{1,0:T(8,128)S(1)}, u32[]{:S(2)}, u32[]{:S(2)}) collective-permute-start(f32[256,256]{1,0:T(8,128)S(1)} %get-tuple-element.193), channel_id=1, source_target_pairs={{0,6},{2,4},{4,2},{6,0},{8,14},{10,12},{12,10},{14,8},{16,22},{18,... | collective-permute-start | bytes 786440 | tf_op jit(solution)/shard_map/ppermute | solution.py:351
  94.3 3.2 %collective-permute-done.22 = f32[1,3,64,256]{3,2,1,0:T(8,128)S(1)} collective-permute-done((f32[1,3,64,256]{3,2,1,0:T(8,128)S(1)}, f32[1,3,64,256]{3,2,1,0:T(8,128)S(1)}, u32[]{:S(2)}, u32[]{:S(2)}) %collective-permute-start.22) | collective-permute-done | bytes 196640 | tf_op jit(solution)/shard_map/ppermute | solution.py:351
  97.5 2.3 %collective-permute-done.21 = f32[1,3,64,256]{3,2,1,0:T(8,128)S(1)} collective-permute-done((f32[1,3,64,256]{3,2,1,0:T(8,128)S(1)}, f32[1,3,64,256]{3,2,1,0:T(8,128)S(1)}, u32[]{:S(2)}, u32[]{:S(2)}) %collective-permute-start.21) | collective-permute-done | bytes 196640 | tf_op jit(solution)/shard_map/ppermute | solution.py:351
  100.0 2.9 %collective-permute-start.25 = (f32[1,1,64,256]{3,2,1,0:T(8,128)S(1)}, f32[1,1,64,256]{3,2,1,0:T(8,128)S(1)}, u32[]{:S(2)}, u32[]{:S(2)}) collective-permute-start(f32[1,1,64,256]{3,2,1,0:T(8,128)S(1)} %slice.25), channel_id=1, source_target_pairs={{0,16},{2,18},{4,20},{6,22},{8,24},{10,26},{12,28},{14,30},{16,0},... | collective-permute-start | bytes 196616 | tf_op jit(solution)/shard_map/ppermute | solution.py:351
  102.9 3.8 %collective-permute-done.24.refs_13_ = f32[1,2,64,256]{3,2,1,0:T(8,128)S(1)} collective-permute-done((f32[1,2,64,256]{3,2,1,0:T(8,128)S(1)}, f32[1,2,64,256]{3,2,1,0:T(8,128)S(1)}, u32[]{:S(2)}, u32[]{:S(2)}) %collective-permute-start.24) | collective-permute-done | bytes 131104 | tf_op jit(solution)/shard_map/ppermute | solution.py:351
  106.7 0.7 collective-permute-done.25.refs_14_
  107.4 2.0 %collective-permute-start.27 = (f32[1,1,64,256]{3,2,1,0:T(8,128)S(1)}, f32[1,1,64,256]{3,2,1,0:T(8,128)S(1)}, u32[]{:S(2)}, u32[]{:S(2)}) collective-permute-start(f32[1,1,64,256]{3,2,1,0:T(8,128)S(1)} %collective-permute-done.25.refs_14_), channel_id=1, source_target_pairs={{0,8},{2,10},{4,12},{6,14},{8,0},{10,2},{12,4},{14,6},{16,24},{18,... | collective-permute-start | bytes 196616 | tf_op jit(solution)/shard_map/ppermute | solution.py:351
  109.4 1.0 shard_map.151
  110.5 1.9 %collective-permute-done.27.refs_16_ = f32[1,1,64,256]{3,2,1,0:T(8,128)S(1)} collective-permute-done((f32[1,1,64,256]{3,2,1,0:T(8,128)S(1)}, f32[1,1,64,256]{3,2,1,0:T(8,128)S(1)}, u32[]{:S(2)}, u32[]{:S(2)}) %collective-permute-start.27) | collective-permute-done | bytes 65568 | tf_op jit(solution)/shard_map/ppermute | solution.py:351
  112.4 3.0 %shard_map.153 = (f32[2,256,256]{2,1,0:T(8,128)S(1)}, f32[3,256,256]{2,1,0:T(8,128)S(1)}, f32[3,256,256]{2,1,0:T(8,128)S(1)}, f32[1,3,64,256]{3,2,1,0:T(8,128)S(...) custom-call(s32[2]{0:T(128)S(1)} %pad_add_fusion.place, ...), custom_call_target="tpu_custom_call" | custom-call | flops 1610612736 | bytes 13369352 | tf_op jit(solution)/shard_map/pallas_call | solution.py:34
  115.5 2.0 %collective-permute-start.31 = (f32[1,3,64,256]{3,2,1,0:T(8,128)S(1)}, f32[1,3,64,256]{3,2,1,0:T(8,128)S(1)}, u32[]{:S(2)}, u32[]{:S(2)}) collective-permute-start(f32[1,3,64,256]{3,2,1,0:T(8,128)S(1)} %get-tuple-element.210), channel_id=1, source_target_pairs={{0,8},{2,10},{4,12},{6,14},{8,0},{10,2},{12,4},{14,6},{16,24},{18,... | collective-permute-start | bytes 589832 | tf_op jit(solution)/shard_map/ppermute | solution.py:351
  117.5 6.7 %collective-permute-done.31 = f32[1,3,64,256]{3,2,1,0:T(8,128)S(1)} collective-permute-done((f32[1,3,64,256]{3,2,1,0:T(8,128)S(1)}, f32[1,3,64,256]{3,2,1,0:T(8,128)S(1)}, u32[]{:S(2)}, u32[]{:S(2)}) %collective-permute-start.31) | collective-permute-done | bytes 196640 | tf_op jit(solution)/shard_map/ppermute | solution.py:351
  124.2 1.0 collective-permute-start.33
  125.3 1.0 collective-permute-start.32
  126.3 1.7 %shard_map.154 = bf16[256,4,256]{2,1,0:T(4,128)(2,1)} custom-call(s32[2]{0:T(128)S(1)} %pad_add_fusion.place, f32[256,256]{1,0:T(8,128)S(1)} %get-tuple-element.218.refs_0_, f32[256,256]{1,0:T(8,128)S(1)} %collective-permute-done.28.refs_1_, f32[256,256]{1,0:T(8,128)S(1)} %collective-permute-done.29.refs_2_, f32[256,256]{1,0:T(8,128)S(1)} %collective-permute-done.30.refs_3_), custom_call_target="tpu_custom_call" | custom-call | flops 8388608 | bytes 1572872 | tf_op jit(solution)/shard_map/pallas_call | solution.py:34
  128.0 5.0 %collective-permute-done.33.refs_3_ = f32[1,3,64,256]{3,2,1,0:T(8,128)S(1)} collective-permute-done((f32[1,3,64,256]{3,2,1,0:T(8,128)S(1)}, f32[1,3,64,256]{3,2,1,0:T(8,128)S(1)}, u32[]{:S(2)}, u32[]{:S(2)}) %collective-permute-start.33) | collective-permute-done | bytes 196640 | tf_op jit(solution)/shard_map/ppermute | solution.py:351
  133.1 0.7 collective-permute-start.39
  133.8 1.7 %collective-permute-start.40 = (f32[256,256]{1,0:T(8,128)S(1)}, f32[256,256]{1,0:T(8,128)S(1)}, u32[]{:S(2)}, u32[]{:S(2)}) collective-permute-start(f32[256,256]{1,0:T(8,128)S(1)} %slice_bitcast_fusion), channel_id=1, source_target_pairs={{0,2},{2,0},{4,6},{6,4},{8,10},{10,8},{12,14},{14,12},{16,18},{18,... | collective-permute-start | bytes 786440 | tf_op jit(solution)/shard_map/ppermute | solution.py:351
  135.5 0.6 shard_map.155
  136.6 1.4 collective-permute-start.37
  138.0 1.7 %collective-permute-start.38 = (f32[1,3,16,256]{3,2,1,0:T(8,128)S(1)}, f32[1,3,16,256]{3,2,1,0:T(8,128)S(1)}, u32[]{:S(2)}, u32[]{:S(2)}) collective-permute-start(f32[1,3,16,256]{3,2,1,0:T(8,128)S(1)} %get-tuple-element.229), channel_id=1, source_target_pairs={{0,6},{2,4},{4,2},{6,0},{8,14},{10,12},{12,10},{14,8},{16,22},{18,... | collective-permute-start | bytes 147464 | tf_op jit(solution)/shard_map/ppermute | solution.py:351
  139.6 0.6 collective-permute-done.40.refs_4_
  140.2 2.4 %shard_map.156 = (bf16[256,4,256]{2,1,0:T(4,128)(2,1)}, bf16[256,4,256]{2,1,0:T(4,128)(2,1)}) custom-call(s32[2]{0:T(128)S(1)} %pad_add_fusion.place, f32[4,256]{1,0:T(4,128)S(1)} %bitcast.24, f32[2,256,256]{2,1,0:T(8,128)S(1)} %get-tuple-element.230.refs_0_, f32[3,256,256]{2,1,0:T(8,128)S(1)} %collective-permute-done.34.refs_1_, ...), custom_call_target="tpu_custom_call" | custom-call | flops 16777216 | bytes 3674120 | tf_op jit(solution)/shard_map/pallas_call | solution.py:34
  143.0 1.2 shard_map.157
  (69 shorter events, 3.7 us)
Async XLA Ops:
  0.6 16.1 %copy-start = (f32[4,256,256]{2,1,0:T(8,128)S(1)}, f32[4,256,256]{2,1,0:T(8,128)}, u32[]{:S(2)}) copy-start(f32[4,256,256]{2,1,0:T(8,128)} %param.16) | copy-start | bytes 3145732
  0.7 0.8 copy-start.4
  1.4 1.0 copy-start.5
  2.5 5.6 %copy-start.6 = (bf16[1,256,4,256]{3,2,1,0:T(4,128)(2,1)S(1)}, bf16[1,256,4,256]{3,2,1,0:T(4,128)(2,1)}, u32[]{:S(2)}) copy-start(bf16[1,256,4,256]{3,2,1,0:T(4,128)(2,1)} %param.11) | copy-start | bytes 1572868
  3.6 10.4 %collective-permute-start.3 = (f32[256,256]{1,0:T(8,128)S(1)}, f32[256,256]{1,0:T(8,128)S(1)}, u32[]{:S(2)}, u32[]{:S(2)}) collective-permute-start(f32[256,256]{1,0:T(8,128)S(1)} %get-tuple-element.130), channel_id=1, source_target_pairs={{0,2},{2,0},{4,6},{6,4},{8,10},{10,8},{12,14},{14,12},{16,18},{18,... | collective-permute-start | bytes 786440 | tf_op jit(solution)/shard_map/ppermute | solution.py:351
  6.6 14.1 %collective-permute-start.4 = (f32[256,256]{1,0:T(8,128)S(1)}, f32[256,256]{1,0:T(8,128)S(1)}, u32[]{:S(2)}, u32[]{:S(2)}) collective-permute-start(f32[256,256]{1,0:T(8,128)S(1)} %get-tuple-element.131), channel_id=1, source_target_pairs={{0,4},{2,6},{4,0},{6,2},{8,12},{10,14},{12,8},{14,10},{16,20},{18,... | collective-permute-start | bytes 786440 | tf_op jit(solution)/shard_map/ppermute | solution.py:351
  8.1 12.8 %collective-permute-start.5 = (f32[256,256]{1,0:T(8,128)S(1)}, f32[256,256]{1,0:T(8,128)S(1)}, u32[]{:S(2)}, u32[]{:S(2)}) collective-permute-start(f32[256,256]{1,0:T(8,128)S(1)} %get-tuple-element.132), channel_id=1, source_target_pairs={{0,6},{2,4},{4,2},{6,0},{8,14},{10,12},{12,10},{14,8},{16,22},{18,... | collective-permute-start | bytes 786440 | tf_op jit(solution)/shard_map/ppermute | solution.py:351
  9.8 0.7 copy-start.7
  10.4 14.5 %collective-permute-start = (f32[256,256]{1,0:T(8,128)}, f32[256,256]{1,0:T(8,128)S(1)}, u32[]{:S(2)}, u32[]{:S(2)}) collective-permute-start(f32[256,256]{1,0:T(8,128)} %get-tuple-element.126), channel_id=1, source_target_pairs={{0,2},{2,0},{4,6},{6,4},{8,10},{10,8},{12,14},{14,12},{16,18},{18,... | collective-permute-start | bytes 786440 | tf_op jit(solution)/shard_map/ppermute | solution.py:351
  12.4 18.8 %collective-permute-start.1 = (f32[256,256]{1,0:T(8,128)}, f32[256,256]{1,0:T(8,128)S(1)}, u32[]{:S(2)}, u32[]{:S(2)}) collective-permute-start(f32[256,256]{1,0:T(8,128)} %get-tuple-element.127), channel_id=1, source_target_pairs={{0,4},{2,6},{4,0},{6,2},{8,12},{10,14},{12,8},{14,10},{16,20},{18,... | collective-permute-start | bytes 786440 | tf_op jit(solution)/shard_map/ppermute | solution.py:351
  13.9 17.3 %collective-permute-start.2 = (f32[256,256]{1,0:T(8,128)S(1)}, f32[256,256]{1,0:T(8,128)S(1)}, u32[]{:S(2)}, u32[]{:S(2)}) collective-permute-start(f32[256,256]{1,0:T(8,128)S(1)} %get-tuple-element.128), channel_id=1, source_target_pairs={{0,6},{2,4},{4,2},{6,0},{8,14},{10,12},{12,10},{14,8},{16,22},{18,... | collective-permute-start | bytes 786440 | tf_op jit(solution)/shard_map/ppermute | solution.py:351
  16.7 14.5 %copy-start.8 = (bf16[256,256]{1,0:T(8,128)(2,1)S(1)}, bf16[256,256]{1,0:T(8,128)(2,1)}, u32[]{:S(2)}) copy-start(bf16[256,256]{1,0:T(8,128)(2,1)} %copy-done.7) | copy-start | bytes 393220
  31.2 4.5 %copy-start.1 = (bf16[1,256,4,256]{3,2,1,0:T(4,128)(2,1)S(1)}, bf16[1,256,4,256]{3,2,1,0:T(4,128)(2,1)}, u32[]{:S(2)}) copy-start(bf16[1,256,4,256]{3,2,1,0:T(4,128)(2,1)} %param.10) | copy-start | bytes 1572868
  31.2 4.5 %copy-start.2 = (bf16[1,256,4,256]{3,2,1,0:T(4,128)(2,1)S(1)}, bf16[1,256,4,256]{3,2,1,0:T(4,128)(2,1)}, u32[]{:S(2)}) copy-start(bf16[1,256,4,256]{3,2,1,0:T(4,128)(2,1)} %param.19) | copy-start | bytes 1572868
  33.4 1.7 %copy-start.9 = (f32[4]{0:T(128)S(1)}, f32[4]{0:T(128)}, u32[]{:S(2)}) copy-start(f32[4]{0:T(128)} %param.14) | copy-start | bytes 52
  33.4 2.2 %copy-start.3 = (f32[4,256]{1,0:T(4,128)S(1)}, f32[4,256]{1,0:T(4,128)}, u32[]{:S(2)}) copy-start(f32[4,256]{1,0:T(4,128)} %gain.1) | copy-start | bytes 12292
  33.4 6.3 %collective-permute-start.6 = (f32[1,3,64,256]{3,2,1,0:T(8,128)S(1)}, f32[1,3,64,256]{3,2,1,0:T(8,128)S(1)}, u32[]{:S(2)}, u32[]{:S(2)}) collective-permute-start(f32[1,3,64,256]{3,2,1,0:T(8,128)S(1)} %get-tuple-element.145), channel_id=1, source_target_pairs={{0,8},{2,10},{4,12},{6,14},{8,0},{10,2},{12,4},{14,6},{16,24},{18,... | collective-permute-start | bytes 589832 | tf_op jit(solution)/shard_map/ppermute | solution.py:351
  37.6 13.1 %collective-permute-start.10 = (f32[2,256,256]{2,1,0:T(8,128)S(1)}, f32[2,256,256]{2,1,0:T(8,128)S(1)}, u32[]{:S(2)}, u32[]{:S(2)}) collective-permute-start(f32[2,256,256]{2,1,0:T(8,128)S(1)} %get-tuple-element.152), channel_id=1, source_target_pairs={{0,4},{2,6},{4,0},{6,2},{8,12},{10,14},{12,8},{14,10},{16,20},{18,... | collective-permute-start | bytes 1572872 | tf_op jit(solution)/shard_map/ppermute | solution.py:351
  39.2 11.5 %collective-permute-start.9 = (f32[2,256,256]{2,1,0:T(8,128)S(1)}, f32[2,256,256]{2,1,0:T(8,128)S(1)}, u32[]{:S(2)}, u32[]{:S(2)}) collective-permute-start(f32[2,256,256]{2,1,0:T(8,128)S(1)} %get-tuple-element.151), channel_id=1, source_target_pairs={{0,2},{2,0},{4,6},{6,4},{8,10},{10,8},{12,14},{14,12},{16,18},{18,... | collective-permute-start | bytes 1572872 | tf_op jit(solution)/shard_map/ppermute | solution.py:351
  39.8 10.0 %collective-permute-start.8 = (f32[1,3,64,256]{3,2,1,0:T(8,128)S(1)}, f32[1,3,64,256]{3,2,1,0:T(8,128)S(1)}, u32[]{:S(2)}, u32[]{:S(2)}) collective-permute-start(f32[1,3,64,256]{3,2,1,0:T(8,128)S(1)} %add.40), channel_id=1, source_target_pairs={{0,16},{2,18},{4,20},{6,22},{8,24},{10,26},{12,28},{14,30},{16,0},... | collective-permute-start | bytes 589832 | tf_op jit(solution)/shard_map/ppermute | solution.py:351
  42.4 8.2 %collective-permute-start.7 = (f32[1,3,64,256]{3,2,1,0:T(8,128)S(1)}, f32[1,3,64,256]{3,2,1,0:T(8,128)S(1)}, u32[]{:S(2)}, u32[]{:S(2)}) collective-permute-start(f32[1,3,64,256]{3,2,1,0:T(8,128)S(1)} %get-tuple-element.147), channel_id=1, source_target_pairs={{0,8},{2,10},{4,12},{6,14},{8,0},{10,2},{12,4},{14,6},{16,24},{18,... | collective-permute-start | bytes 589832 | tf_op jit(solution)/shard_map/ppermute | solution.py:351
  50.7 16.8 %collective-permute-start.11 = (f32[2,256,256]{2,1,0:T(8,128)S(1)}, f32[2,256,256]{2,1,0:T(8,128)S(1)}, u32[]{:S(2)}, u32[]{:S(2)}) collective-permute-start(f32[2,256,256]{2,1,0:T(8,128)S(1)} %get-tuple-element.157), channel_id=1, source_target_pairs={{0,6},{2,4},{4,2},{6,0},{8,14},{10,12},{12,10},{14,8},{16,22},{18,... | collective-permute-start | bytes 1572872 | tf_op jit(solution)/shard_map/ppermute | solution.py:351
  52.6 8.2 %collective-permute-start.13 = (f32[1,2,64,256]{3,2,1,0:T(8,128)S(1)}, f32[1,2,64,256]{3,2,1,0:T(8,128)S(1)}, u32[]{:S(2)}, u32[]{:S(2)}) collective-permute-start(f32[1,2,64,256]{3,2,1,0:T(8,128)S(1)} %slice.18), channel_id=1, source_target_pairs={{0,16},{2,18},{4,20},{6,22},{8,24},{10,26},{12,28},{14,30},{16,0},... | collective-permute-start | bytes 393224 | tf_op jit(solution)/shard_map/ppermute | solution.py:351
  55.3 12.2 %collective-permute-start.12 = (f32[1,3,64,256]{3,2,1,0:T(8,128)S(1)}, f32[1,3,64,256]{3,2,1,0:T(8,128)S(1)}, u32[]{:S(2)}, u32[]{:S(2)}) collective-permute-start(f32[1,3,64,256]{3,2,1,0:T(8,128)S(1)} %add_add_fusion.1.refs_4_), channel_id=1, source_target_pairs={{0,8},{2,10},{4,12},{6,14},{8,0},{10,2},{12,4},{14,6},{16,24},{18,... | collective-permute-start | bytes 589832 | tf_op jit(solution)/shard_map/ppermute | solution.py:351
  56.2 7.1 %collective-permute-start.14 = (f32[1,1,64,256]{3,2,1,0:T(8,128)S(1)}, f32[1,1,64,256]{3,2,1,0:T(8,128)S(1)}, u32[]{:S(2)}, u32[]{:S(2)}) collective-permute-start(f32[1,1,64,256]{3,2,1,0:T(8,128)S(1)} %slice.19), channel_id=1, source_target_pairs={{0,16},{2,18},{4,20},{6,22},{8,24},{10,26},{12,28},{14,30},{16,0},... | collective-permute-start | bytes 196616 | tf_op jit(solution)/shard_map/ppermute | solution.py:351
  60.9 6.6 %collective-permute-start.15 = (f32[1,2,64,256]{3,2,1,0:T(8,128)S(1)}, f32[1,2,64,256]{3,2,1,0:T(8,128)S(1)}, u32[]{:S(2)}, u32[]{:S(2)}) collective-permute-start(f32[1,2,64,256]{3,2,1,0:T(8,128)S(1)} %collective-permute-done.13.refs_6_), channel_id=1, source_target_pairs={{0,8},{2,10},{4,12},{6,14},{8,0},{10,2},{12,4},{14,6},{16,24},{18,... | collective-permute-start | bytes 393224 | tf_op jit(solution)/shard_map/ppermute | solution.py:351
  63.2 4.3 %collective-permute-start.16 = (f32[1,1,64,256]{3,2,1,0:T(8,128)S(1)}, f32[1,1,64,256]{3,2,1,0:T(8,128)S(1)}, u32[]{:S(2)}, u32[]{:S(2)}) collective-permute-start(f32[1,1,64,256]{3,2,1,0:T(8,128)S(1)} %collective-permute-done.14.refs_7_), channel_id=1, source_target_pairs={{0,8},{2,10},{4,12},{6,14},{8,0},{10,2},{12,4},{14,6},{16,24},{18,... | collective-permute-start | bytes 196616 | tf_op jit(solution)/shard_map/ppermute | solution.py:351
  69.3 1.2 collective-permute-start.17
  70.5 3.7 %collective-permute-start.18 = (f32[2,4,256]{2,1,0:T(4,128)S(1)}, f32[2,4,256]{2,1,0:T(4,128)S(1)}, u32[]{:S(2)}, u32[]{:S(2)}) collective-permute-start(f32[2,4,256]{2,1,0:T(4,128)S(1)} %add.42), channel_id=1, source_target_pairs={{0,2},{2,0},{4,6},{6,4},{8,10},{10,8},{12,14},{14,12},{16,18},{18,... | collective-permute-start | bytes 24584 | tf_op jit(solution)/shard_map/ppermute | solution.py:351
  74.2 3.7 %collective-permute-start.19 = (f32[2,4,256]{2,1,0:T(4,128)S(1)}, f32[2,4,256]{2,1,0:T(4,128)S(1)}, u32[]{:S(2)}, u32[]{:S(2)}) collective-permute-start(f32[2,4,256]{2,1,0:T(4,128)S(1)} %add.43), channel_id=1, source_target_pairs={{0,4},{2,6},{4,0},{6,2},{8,12},{10,14},{12,8},{14,10},{16,20},{18,... | collective-permute-start | bytes 24584 | tf_op jit(solution)/shard_map/ppermute | solution.py:351
  79.8 5.7 %collective-permute-start.20 = (f32[1,3,64,256]{3,2,1,0:T(8,128)S(1)}, f32[1,3,64,256]{3,2,1,0:T(8,128)S(1)}, u32[]{:S(2)}, u32[]{:S(2)}) collective-permute-start(f32[1,3,64,256]{3,2,1,0:T(8,128)S(1)} %get-tuple-element.174), channel_id=1, source_target_pairs={{0,8},{2,10},{4,12},{6,14},{8,0},{10,2},{12,4},{14,6},{16,24},{18,... | collective-permute-start | bytes 589832 | tf_op jit(solution)/shard_map/ppermute | solution.py:351
  85.6 11.9 %collective-permute-start.22 = (f32[1,3,64,256]{3,2,1,0:T(8,128)S(1)}, f32[1,3,64,256]{3,2,1,0:T(8,128)S(1)}, u32[]{:S(2)}, u32[]{:S(2)}) collective-permute-start(f32[1,3,64,256]{3,2,1,0:T(8,128)S(1)} %add.46), channel_id=1, source_target_pairs={{0,16},{2,18},{4,20},{6,22},{8,24},{10,26},{12,28},{14,30},{16,0},... | collective-permute-start | bytes 589832 | tf_op jit(solution)/shard_map/ppermute | solution.py:351
  90.2 9.5 %collective-permute-start.21 = (f32[1,3,64,256]{3,2,1,0:T(8,128)S(1)}, f32[1,3,64,256]{3,2,1,0:T(8,128)S(1)}, u32[]{:S(2)}, u32[]{:S(2)}) collective-permute-start(f32[1,3,64,256]{3,2,1,0:T(8,128)S(1)} %get-tuple-element.176), channel_id=1, source_target_pairs={{0,8},{2,10},{4,12},{6,14},{8,0},{10,2},{12,4},{14,6},{16,24},{18,... | collective-permute-start | bytes 589832 | tf_op jit(solution)/shard_map/ppermute | solution.py:351
  90.7 9.3 %collective-permute-start.28 = (f32[256,256]{1,0:T(8,128)S(1)}, f32[256,256]{1,0:T(8,128)S(1)}, u32[]{:S(2)}, u32[]{:S(2)}) collective-permute-start(f32[256,256]{1,0:T(8,128)S(1)} %get-tuple-element.191), channel_id=1, source_target_pairs={{0,2},{2,0},{4,6},{6,4},{8,10},{10,8},{12,14},{14,12},{16,18},{18,... | collective-permute-start | bytes 786440 | tf_op jit(solution)/shard_map/ppermute | solution.py:351
  90.8 19.7 %collective-permute-start.29 = (f32[256,256]{1,0:T(8,128)S(1)}, f32[256,256]{1,0:T(8,128)S(1)}, u32[]{:S(2)}, u32[]{:S(2)}) collective-permute-start(f32[256,256]{1,0:T(8,128)S(1)} %get-tuple-element.192), channel_id=1, source_target_pairs={{0,4},{2,6},{4,0},{6,2},{8,12},{10,14},{12,8},{14,10},{16,20},{18,... | collective-permute-start | bytes 786440 | tf_op jit(solution)/shard_map/ppermute | solution.py:351
  91.3 19.2 %collective-permute-start.30 = (f32[256,256]{1,0:T(8,128)S(1)}, f32[256,256]{1,0:T(8,128)S(1)}, u32[]{:S(2)}, u32[]{:S(2)}) collective-permute-start(f32[256,256]{1,0:T(8,128)S(1)} %get-tuple-element.193), channel_id=1, source_target_pairs={{0,6},{2,4},{4,2},{6,0},{8,14},{10,12},{12,10},{14,8},{16,22},{18,... | collective-permute-start | bytes 786440 | tf_op jit(solution)/shard_map/ppermute | solution.py:351
  99.8 6.9 %collective-permute-start.24 = (f32[1,2,64,256]{3,2,1,0:T(8,128)S(1)}, f32[1,2,64,256]{3,2,1,0:T(8,128)S(1)}, u32[]{:S(2)}, u32[]{:S(2)}) collective-permute-start(f32[1,2,64,256]{3,2,1,0:T(8,128)S(1)} %slice.24), channel_id=1, source_target_pairs={{0,16},{2,18},{4,20},{6,22},{8,24},{10,26},{12,28},{14,30},{16,0},... | collective-permute-start | bytes 393224 | tf_op jit(solution)/shard_map/ppermute | solution.py:351
  99.9 12.5 %collective-permute-start.23 = (f32[1,3,64,256]{3,2,1,0:T(8,128)S(1)}, f32[1,3,64,256]{3,2,1,0:T(8,128)S(1)}, u32[]{:S(2)}, u32[]{:S(2)}) collective-permute-start(f32[1,3,64,256]{3,2,1,0:T(8,128)S(1)} %add_add_fusion.refs_11_.refs_0_), channel_id=1, source_target_pairs={{0,8},{2,10},{4,12},{6,14},{8,0},{10,2},{12,4},{14,6},{16,24},{18,... | collective-permute-start | bytes 589832 | tf_op jit(solution)/shard_map/ppermute | solution.py:351
  100.0 7.4 %collective-permute-start.25 = (f32[1,1,64,256]{3,2,1,0:T(8,128)S(1)}, f32[1,1,64,256]{3,2,1,0:T(8,128)S(1)}, u32[]{:S(2)}, u32[]{:S(2)}) collective-permute-start(f32[1,1,64,256]{3,2,1,0:T(8,128)S(1)} %slice.25), channel_id=1, source_target_pairs={{0,16},{2,18},{4,20},{6,22},{8,24},{10,26},{12,28},{14,30},{16,0},... | collective-permute-start | bytes 196616 | tf_op jit(solution)/shard_map/ppermute | solution.py:351
  106.7 5.7 %collective-permute-start.26 = (f32[1,2,64,256]{3,2,1,0:T(8,128)S(1)}, f32[1,2,64,256]{3,2,1,0:T(8,128)S(1)}, u32[]{:S(2)}, u32[]{:S(2)}) collective-permute-start(f32[1,2,64,256]{3,2,1,0:T(8,128)S(1)} %collective-permute-done.24.refs_13_), channel_id=1, source_target_pairs={{0,8},{2,10},{4,12},{6,14},{8,0},{10,2},{12,4},{14,6},{16,24},{18,... | collective-permute-start | bytes 393224 | tf_op jit(solution)/shard_map/ppermute | solution.py:351
  107.4 5.0 %collective-permute-start.27 = (f32[1,1,64,256]{3,2,1,0:T(8,128)S(1)}, f32[1,1,64,256]{3,2,1,0:T(8,128)S(1)}, u32[]{:S(2)}, u32[]{:S(2)}) collective-permute-start(f32[1,1,64,256]{3,2,1,0:T(8,128)S(1)} %collective-permute-done.25.refs_14_), channel_id=1, source_target_pairs={{0,8},{2,10},{4,12},{6,14},{8,0},{10,2},{12,4},{14,6},{16,24},{18,... | collective-permute-start | bytes 196616 | tf_op jit(solution)/shard_map/ppermute | solution.py:351
  115.4 17.7 %collective-permute-start.34 = (f32[3,256,256]{2,1,0:T(8,128)S(1)}, f32[3,256,256]{2,1,0:T(8,128)S(1)}, u32[]{:S(2)}, u32[]{:S(2)}) collective-permute-start(f32[3,256,256]{2,1,0:T(8,128)S(1)} %get-tuple-element.216), channel_id=1, source_target_pairs={{0,2},{2,0},{4,6},{6,4},{8,10},{10,8},{12,14},{14,12},{16,18},{18,... | collective-permute-start | bytes 2359304 | tf_op jit(solution)/shard_map/ppermute | solution.py:351
  115.5 17.6 %collective-permute-start.35 = (f32[3,256,256]{2,1,0:T(8,128)S(1)}, f32[3,256,256]{2,1,0:T(8,128)S(1)}, u32[]{:S(2)}, u32[]{:S(2)}) collective-permute-start(f32[3,256,256]{2,1,0:T(8,128)S(1)} %get-tuple-element.217), channel_id=1, source_target_pairs={{0,4},{2,6},{4,0},{6,2},{8,12},{10,14},{12,8},{14,10},{16,20},{18,... | collective-permute-start | bytes 2359304 | tf_op jit(solution)/shard_map/ppermute | solution.py:351
  115.5 8.7 %collective-permute-start.31 = (f32[1,3,64,256]{3,2,1,0:T(8,128)S(1)}, f32[1,3,64,256]{3,2,1,0:T(8,128)S(1)}, u32[]{:S(2)}, u32[]{:S(2)}) collective-permute-start(f32[1,3,64,256]{3,2,1,0:T(8,128)S(1)} %get-tuple-element.210), channel_id=1, source_target_pairs={{0,8},{2,10},{4,12},{6,14},{8,0},{10,2},{12,4},{14,6},{16,24},{18,... | collective-permute-start | bytes 589832 | tf_op jit(solution)/shard_map/ppermute | solution.py:351
  124.2 8.8 %collective-permute-start.33 = (f32[1,3,64,256]{3,2,1,0:T(8,128)S(1)}, f32[1,3,64,256]{3,2,1,0:T(8,128)S(1)}, u32[]{:S(2)}, u32[]{:S(2)}) collective-permute-start(f32[1,3,64,256]{3,2,1,0:T(8,128)S(1)} %add.48), channel_id=1, source_target_pairs={{0,16},{2,18},{4,20},{6,22},{8,24},{10,26},{12,28},{14,30},{16,0},... | collective-permute-start | bytes 589832 | tf_op jit(solution)/shard_map/ppermute | solution.py:351
  125.3 7.8 %collective-permute-start.32 = (f32[1,3,64,256]{3,2,1,0:T(8,128)S(1)}, f32[1,3,64,256]{3,2,1,0:T(8,128)S(1)}, u32[]{:S(2)}, u32[]{:S(2)}) collective-permute-start(f32[1,3,64,256]{3,2,1,0:T(8,128)S(1)} %get-tuple-element.212), channel_id=1, source_target_pairs={{0,8},{2,10},{4,12},{6,14},{8,0},{10,2},{12,4},{14,6},{16,24},{18,... | collective-permute-start | bytes 589832 | tf_op jit(solution)/shard_map/ppermute | solution.py:351
  133.1 6.6 %collective-permute-start.39 = (f32[256,256]{1,0:T(8,128)S(1)}, f32[256,256]{1,0:T(8,128)S(1)}, u32[]{:S(2)}, u32[]{:S(2)}) collective-permute-start(f32[256,256]{1,0:T(8,128)S(1)} %slice_bitcast_fusion.1), channel_id=1, source_target_pairs={{0,4},{2,6},{4,0},{6,2},{8,12},{10,14},{12,8},{14,10},{16,20},{18,... | collective-permute-start | bytes 786440 | tf_op jit(solution)/shard_map/ppermute | solution.py:351
  133.8 6.4 %collective-permute-start.40 = (f32[256,256]{1,0:T(8,128)S(1)}, f32[256,256]{1,0:T(8,128)S(1)}, u32[]{:S(2)}, u32[]{:S(2)}) collective-permute-start(f32[256,256]{1,0:T(8,128)S(1)} %slice_bitcast_fusion), channel_id=1, source_target_pairs={{0,2},{2,0},{4,6},{6,4},{8,10},{10,8},{12,14},{14,12},{16,18},{18,... | collective-permute-start | bytes 786440 | tf_op jit(solution)/shard_map/ppermute | solution.py:351
  136.1 6.6 %collective-permute-start.36 = (f32[1,3,16,256]{3,2,1,0:T(8,128)S(1)}, f32[1,3,16,256]{3,2,1,0:T(8,128)S(1)}, u32[]{:S(2)}, u32[]{:S(2)}) collective-permute-start(f32[1,3,16,256]{3,2,1,0:T(8,128)S(1)} %get-tuple-element.227), channel_id=1, source_target_pairs={{0,2},{2,0},{4,6},{6,4},{8,10},{10,8},{12,14},{14,12},{16,18},{18,... | collective-permute-start | bytes 147464 | tf_op jit(solution)/shard_map/ppermute | solution.py:351
  136.6 6.1 %collective-permute-start.37 = (f32[1,3,16,256]{3,2,1,0:T(8,128)S(1)}, f32[1,3,16,256]{3,2,1,0:T(8,128)S(1)}, u32[]{:S(2)}, u32[]{:S(2)}) collective-permute-start(f32[1,3,16,256]{3,2,1,0:T(8,128)S(1)} %get-tuple-element.228), channel_id=1, source_target_pairs={{0,4},{2,6},{4,0},{6,2},{8,12},{10,14},{12,8},{14,10},{16,20},{18,... | collective-permute-start | bytes 147464 | tf_op jit(solution)/shard_map/ppermute | solution.py:351
  138.0 5.0 %collective-permute-start.38 = (f32[1,3,16,256]{3,2,1,0:T(8,128)S(1)}, f32[1,3,16,256]{3,2,1,0:T(8,128)S(1)}, u32[]{:S(2)}, u32[]{:S(2)}) collective-permute-start(f32[1,3,16,256]{3,2,1,0:T(8,128)S(1)} %get-tuple-element.229), channel_id=1, source_target_pairs={{0,6},{2,4},{4,2},{6,0},{8,14},{10,12},{12,10},{14,8},{16,22},{18,... | collective-permute-start | bytes 147464 | tf_op jit(solution)/shard_map/ppermute | solution.py:351

commit v16 on v15

--- a/solution.py
+++ b/solution.py
@@ -122,7 +122,7 @@
 
 def update_sums(keys_in, scaled_in, weights, key_kept, scaled_kept):
     gate_b, out_b, up_b = (w[...].astype(BF16) for w in weights)
-    total = [0.0, 0.0, 0.0]
+    acts, dfirsts, dthirds = [], [], []
     for step, (key, value) in enumerate(zip(keys_in, scaled_in)):
         keys = key[...].astype(BF16)
         scaled = value[...].astype(BF16)
@@ -137,10 +137,15 @@
         deriv = sig * (1.0 + first * (1.0 - sig))
         dfirst = (dact * third * deriv).astype(BF16)
         dthird = (dact * activ).astype(BF16)
-        total[0] += tmm(keys, dfirst)
-        total[1] += tmm(act, scaled)
-        total[2] += tmm(keys, dthird)
-    return total
+        acts.append(act)
+        dfirsts.append(dfirst)
+        dthirds.append(dthird)
+    keys, scaled = tokens_of(key_kept), tokens_of(scaled_kept)
+    return (
+        tmm(keys, jnp.concatenate(dfirsts)),
+        tmm(jnp.concatenate(acts), scaled),
+        tmm(keys, jnp.concatenate(dthirds)),
+    )
 
 
 def update_kernel(count, depth, scale, place, *refs):
@@ -159,24 +164,23 @@
 
 def assemble(place, parts, whole):
     rows = parts[0].shape[2]
-    for i, part in enumerate(parts):
-        at = pl.multiple_of((place[1] ^ (i if i < 2 else i // 2 + 1)) * rows, rows)
-        low, high = {3: (0, 3), 2: (0, 2), 1: (2, 3)}[part.shape[1]]
-        whole[low:high, pl.ds(at, rows), :] = part[0]
-
-
-def gathered(depth):
-    return max(2 * depth - 2, depth)
+    for step, part in enumerate(parts):
+        at = pl.multiple_of((place[1] ^ step) * rows, rows)
+        whole[:, pl.ds(at, rows), :] = part[0]
 
 
 def query_refs(groups, refs):
-    return [(ref.at[0], ref.at[1]) for ref in refs[:groups]]
+    return [(ref.at[0], ref.at[1]) for ref in refs[: groups - 1]] + [refs[groups - 1 : groups + 1]]
+
+
+def tokens_of(ref):
+    return ref[...].reshape(ref.shape[0] * ref.shape[1], ref.shape[2])
 
 
 def apply_kernel(groups, depth, place, scale_row, *refs):
-    pieces, refs = query_refs(groups, refs), refs[groups:]
-    parts = refs[: gathered(depth)]
-    activ_ref, slope_ref, hidden_ref, os_ref, new_b, stats, whole = refs[gathered(depth) :]
+    pieces, refs = query_refs(groups, refs), refs[groups + 1 :]
+    parts = refs[:depth]
+    activ_ref, slope_ref, hidden_ref, os_ref, new_b, stats, whole = refs[depth:]
     assemble(place, parts, whole)
     new_b[...] = whole[...].astype(BF16)
     for step in range(groups):
@@ -201,16 +205,17 @@
         stats[1, pl.ds(source, 1), :] = both[1:2, :]
 
 
-def apply_back_kernel(groups, depth, count, place, scale_row, stats, *refs):
-    pieces, refs = query_refs(groups, refs), refs[groups:]
+def apply_back_kernel(groups, depth, count, place, scale_row, *refs):
+    stats, refs = refs[:groups], refs[groups:]
+    pieces, refs = query_refs(groups, refs), refs[groups + 1 :]
     activ_ref, slope_ref, hidden_ref, os_ref, new_b = refs[:5]
-    dfirst_ref, dthird_ref, slices, sums = refs[5], refs[6], refs[7:-1], refs[-1]
-    total = [0.0, 0.0, 0.0]
+    dfirst_ref, dthird_ref, slices, sums, both = refs[5], refs[6], refs[7:-2], refs[-2], refs[-1]
+    both[...] = functools.reduce(jnp.add, [ref[...] for ref in stats])
+    douts = []
     for step in range(groups):
-        queries = pieces[step][0][...].astype(BF16)
         source = place[0] ^ step
-        sq = rate_column(stats.at[0], source)
-        ps = rate_column(stats.at[1], source)
+        sq = rate_column(both.at[0], source)
+        ps = rate_column(both.at[1], source)
         inv = lax.rsqrt(sq / count + 1e-06)
         dos = inv * pieces[step][1][...] - os_ref[step] * (inv * inv * inv * ps / count)
         dout = (dos * scale_row[0:1, :]).astype(BF16)
@@ -219,11 +224,11 @@
         dfirst = (dhidden * slope_ref[step]).astype(BF16)
         dfirst_ref[step] = dfirst
         dthird_ref[step] = dthird
-        total[0] += tmm(queries, dfirst)
-        total[1] += tmm(hidden_ref[step], dout)
-        total[2] += tmm(queries, dthird)
-    for i in range(3):
-        sums[i] = total[i]
+        douts.append(dout)
+    queries = jnp.concatenate([piece[0][...].astype(BF16) for piece in pieces])
+    sums[0] = tmm(queries, tokens_of(dfirst_ref))
+    sums[1] = tmm(tokens_of(hidden_ref), jnp.concatenate(douts))
+    sums[2] = tmm(queries, tokens_of(dthird_ref))
     send_slices(sums, slices, place[1], depth)
 
 
@@ -260,7 +265,7 @@
     (k_kept, s_kept), refs = refs[:2], refs[2:]
     kept, refs = refs[:9], refs[9:]
     dact_r, third_r, activ_r, deriv_r, slope_r, second_r, dfirst_r, dthird_r, act_r = kept
-    parts, refs = refs[: gathered(depth)], refs[gathered(depth) :]
+    parts, refs = refs[:depth], refs[depth:]
     w_gate, w_out, w_up = refs[:3]
     packed = len(packing(groups))
     outs, slices = unpacked(groups, refs[3 : packed + 3]), refs[packed + 3 : -2]
@@ -268,7 +273,7 @@
     assemble(place, parts, whole)
     gate_b, out_b, up_b = (w[...].astype(BF16) for w in (w_gate, w_out, w_up))
     cot_gate, cot_out, cot_up = ((whole[i] * scale).astype(BF16) for i in range(3))
-    total = [0.0, 0.0, 0.0]
+    firsts, thirds, dacts = [], [], []
     for step in range(groups):
         keys, scaled = k_kept[step], s_kept[step]
         bar_dfirst = mm(keys, cot_gate)
@@ -287,11 +292,13 @@
             + mm_t(bar_third, up_b)
         )
         outs[step][1][...] = mm(act_r[step], cot_out) + mm(bar_dact, out_b)
-        total[0] += tmm(keys, bar_first)
-        total[1] += tmm(bar_dact, scaled)
-        total[2] += tmm(keys, bar_third)
-    for i in range(3):
-        sums[i] = total[i]
+        firsts.append(bar_first)
+        thirds.append(bar_third)
+        dacts.append(bar_dact)
+    keys = tokens_of(k_kept)
+    sums[0] = tmm(keys, jnp.concatenate(firsts))
+    sums[1] = tmm(jnp.concatenate(dacts), tokens_of(s_kept))
+    sums[2] = tmm(keys, jnp.concatenate(thirds))
     send_slices(sums, slices, place[1], depth)
 
 
@@ -366,10 +373,12 @@
         return [outs[-1]] + first + even
 
     def gather(part, count, unit):
-        got = [part, move(part, "ctx", unit)][:count]
-        for r in range(2, count, 2):
-            sent = [move(part[:, i : i + 2], "ctx", r * unit) for i in (0, 2)]
-            got += sent + [move(x, "ctx", unit) for x in sent]
+        got = [part] * count
+        for r in [2 * i for i in range(1, count // 2)]:
+            got[r] = move(part, "ctx", r * unit)
+            got[r + 1] = move(got[r], "ctx", unit)
+        if count > 1:
+            got[1] = move(part, "ctx", unit)
         return got
 
     def after(x, *others):
@@ -407,13 +416,13 @@
     early, terms = out[:2], out[2:]
     *q_out, scale_row = call(
         functools.partial(split_apply_kernel, groups),
-        [shape(2, tokens, width)] * groups + [shape(8, width)],
+        [shape(2, tokens, width)] * (groups - 1) + [shape(tokens, width)] * 2 + [shape(8, width)],
         [scratch], flops // 8, place, queries[0], cotangent[0], gain, own_scale,
     )
-    q_in = in_plane(q_out[:-1])
+    q_in = in_plane(q_out[:-2])
     new = functools.reduce(jnp.add, scatter(terms, depth, groups))
-    new, q_in, q_last = after(new, q_in, q_out[-1])
-    q_in.append(move(q_last, "ctx", groups - 1))
+    new, q_in, q_last = after(new, q_in, q_out[-2:])
+    q_in += [move(x, "ctx", groups - 1) for x in q_last]
     new = gather(new, depth, groups)
     *passed, stats = call(
         functools.partial(apply_kernel, groups, depth),
@@ -421,15 +430,15 @@
         + [shape(3, hidden, width, dtype=BF16), shape(2, groups, tokens)],
         [square], 3 * flops, place, scale_row, *q_in, *new,
     )
-    for axis, size in (("head", lax.axis_size("head")), ("ctx", groups)):
-        bit = 1
-        while bit < size:
-            stats = stats + move(stats, axis, bit)
-            bit *= 2
+    bit = 1
+    while bit < head_axis:
+        stats = stats + move(stats, "head", bit)
+        bit *= 2
     out = call(
         functools.partial(apply_back_kernel, groups, depth, count),
-        [kept(groups, dtype=BF16)] * 2 + slices, [square], 6 * flops,
-        place, scale_row, stats, *q_in, *passed,
+        [kept(groups, dtype=BF16)] * 2 + slices,
+        [square, pltpu.VMEM((2, groups, tokens), F32)], 6 * flops,
+        place, scale_row, *in_plane([stats] * groups), *q_in, *passed,
     )
     q_sent = call(
         query_back_kernel, [shape(tokens, width)] * groups, [], 2 * flops, *out[:2], passed[-1]

time: 144 us -> 144 us (level)
  starting transfers between devices: 53.5 us -> 46.6 us
  waiting for transfers between devices: 64.1 us -> 70.9 us
    ppermute x41 -> x39, starting transfers between devices: 53.5 us -> 46.6 us  [move(): lax.ppermute(x, axis, [(c, c ^ step) for c in range(lax.axis_size(axis))])]
    ppermute x41 -> x39, waiting for transfers between devices: 64.1 us -> 70.9 us  [move(): lax.ppermute(x, axis, [(c, c ^ step) for c in range(lax.axis_size(axis))])]
  transfers between devices with their start and end apart: 41 -> 39, of which waited for: 22 -> 25; matrix products, arithmetic and copies ran while one was open for 1% -> 1% of each run, Pallas kernels for 7% -> 7%
where the time goes in v16:
time: 144 us
  waiting for transfers between devices  70.9 us (49%)
  starting transfers between devices  46.6 us (32%)
  Pallas kernels  21.1 us (15%)
  local copies, waits for them, and re-layouts  4.17 us (3%)
    ppermute x39, waiting for transfers between devices, move(): lax.ppermute(x, axis, [(c, c ^ step) for c in range(lax.axis_size(axis))])  70.9 us
    ppermute x39, starting transfers between devices, move(): lax.ppermute(x, axis, [(c, c ^ step) for c in range(lax.axis_size(axis))])  46.6 us
    pallas_call x13, Pallas kernels, call(): pl.pallas_call(body, out_shape=out_shape, in_specs=[smem if a.dtype == jn...  21.1 us
  transfers between devices with their start and end apart: 39, of which 25 were waited for; matrix products, arithmetic and copies ran while one was open for 1% of the time, Pallas kernels for 7%

profile of v16, /device:TPU:0, one launch (start us, length us, event | category | flops | bytes accessed | tf_op | source)
XLA Modules:
  0.0 143.8 jit_solution(10918732229778161160)
XLA Ops:
  0.7 0.7 copy-done.4
  1.4 1.0 copy-done.5
  2.5 1.1 shard_map.146
  3.6 3.0 %collective-permute-start.3 = (f32[256,256]{1,0:T(8,128)S(1)}, f32[256,256]{1,0:T(8,128)S(1)}, u32[]{:S(2)}, u32[]{:S(2)}) collective-permute-start(f32[256,256]{1,0:T(8,128)S(1)} %get-tuple-element.130), channel_id=1, source_target_pairs={{0,2},{2,0},{4,6},{6,4},{8,10},{10,8},{12,14},{14,12},{16,18},{18,... | collective-permute-start | bytes 786440 | tf_op jit(solution)/shard_map/ppermute | solution.py:358
  6.6 1.5 %collective-permute-start.4 = (f32[256,256]{1,0:T(8,128)S(1)}, f32[256,256]{1,0:T(8,128)S(1)}, u32[]{:S(2)}, u32[]{:S(2)}) collective-permute-start(f32[256,256]{1,0:T(8,128)S(1)} %get-tuple-element.131), channel_id=1, source_target_pairs={{0,4},{2,6},{4,0},{6,2},{8,12},{10,14},{12,8},{14,10},{16,20},{18,... | collective-permute-start | bytes 786440 | tf_op jit(solution)/shard_map/ppermute | solution.py:358
  8.1 1.7 %shard_map.145 = (bf16[256,256]{1,0:T(8,128)(2,1)S(1)}, f32[256,256]{1,0:T(8,128)}, f32[256,256]{1,0:T(8,128)}, f32[256,256]{1,0:T(8,128)S(1)}) custom-call(s32[2]{0:T(128)S(1)} %pad_add_fusion.place, bf16[256,4,256]{2,1,0:T(4,128)(2,1)S(1)} %bitcast.26), custom_call_target="tpu_custom_call" | custom-call | flops 2147483648 | bytes 1441800 | tf_op jit(solution)/shard_map/pallas_call | solution.py:34
  9.8 0.7 copy-done.7
  10.4 1.9 %collective-permute-start = (f32[256,256]{1,0:T(8,128)}, f32[256,256]{1,0:T(8,128)S(1)}, u32[]{:S(2)}, u32[]{:S(2)}) collective-permute-start(f32[256,256]{1,0:T(8,128)} %get-tuple-element.126), channel_id=1, source_target_pairs={{0,2},{2,0},{4,6},{6,4},{8,10},{10,8},{12,14},{14,12},{16,18},{18,... | collective-permute-start | bytes 786440 | tf_op jit(solution)/shard_map/ppermute | solution.py:358
  12.4 1.5 %collective-permute-start.1 = (f32[256,256]{1,0:T(8,128)}, f32[256,256]{1,0:T(8,128)S(1)}, u32[]{:S(2)}, u32[]{:S(2)}) collective-permute-start(f32[256,256]{1,0:T(8,128)} %get-tuple-element.127), channel_id=1, source_target_pairs={{0,4},{2,6},{4,0},{6,2},{8,12},{10,14},{12,8},{14,10},{16,20},{18,... | collective-permute-start | bytes 786440 | tf_op jit(solution)/shard_map/ppermute | solution.py:358
  13.9 2.8 %collective-permute-start.2 = (f32[256,256]{1,0:T(8,128)S(1)}, f32[256,256]{1,0:T(8,128)S(1)}, u32[]{:S(2)}, u32[]{:S(2)}) collective-permute-start(f32[256,256]{1,0:T(8,128)S(1)} %get-tuple-element.128), channel_id=1, source_target_pairs={{0,6},{2,4},{4,2},{6,0},{8,14},{10,12},{12,10},{14,8},{16,22},{18,... | collective-permute-start | bytes 786440 | tf_op jit(solution)/shard_map/ppermute | solution.py:358
  16.7 1.1 dynamic-slice_bitcast_fusion
  17.9 2.8 %collective-permute-done.4.refs_6_ = f32[256,256]{1,0:T(8,128)S(1)} collective-permute-done((f32[256,256]{1,0:T(8,128)S(1)}, f32[256,256]{1,0:T(8,128)S(1)}, u32[]{:S(2)}, u32[]{:S(2)}) %collective-permute-start.4) | collective-permute-done | bytes 262176 | tf_op jit(solution)/shard_map/ppermute | solution.py:358
  20.9 4.1 %collective-permute-done.refs_1_ = f32[256,256]{1,0:T(8,128)S(1)} collective-permute-done((f32[256,256]{1,0:T(8,128)}, f32[256,256]{1,0:T(8,128)S(1)}, u32[]{:S(2)}, u32[]{:S(2)}) %collective-permute-start) | collective-permute-done | bytes 262176 | tf_op jit(solution)/shard_map/ppermute | solution.py:358
  25.0 6.2 %collective-permute-done.1.refs_2_ = f32[256,256]{1,0:T(8,128)S(1)} collective-permute-done((f32[256,256]{1,0:T(8,128)}, f32[256,256]{1,0:T(8,128)S(1)}, u32[]{:S(2)}, u32[]{:S(2)}) %collective-permute-start.1) | collective-permute-done | bytes 262176 | tf_op jit(solution)/shard_map/ppermute | solution.py:358
  31.2 2.0 %shard_map.148 = (bf16[4,256,256]{2,1,0:T(8,128)(2,1)S(1)}, bf16[4,256,256]{2,1,0:T(8,128)(2,1)S(1)}, f32[1,3,64,256]{3,2,1,0:T(8,128)S(1)}, f32[1,3,64,256]{3,2...) custom-call(s32[2]{0:T(128)S(1)} %pad_add_fusion.place, bf16[256,256]{1,0:T(8,128)(2,1)S(1)} %copy-done.8, ...), custom_call_target="tpu_custom_call" | custom-call | flops 805306368 | bytes 4456456 | tf_op jit(solution)/shard_map/pallas_call | solution.py:34
  33.2 1.6 %collective-permute-start.6 = (f32[1,3,64,256]{3,2,1,0:T(8,128)S(1)}, f32[1,3,64,256]{3,2,1,0:T(8,128)S(1)}, u32[]{:S(2)}, u32[]{:S(2)}) collective-permute-start(f32[1,3,64,256]{3,2,1,0:T(8,128)S(1)} %get-tuple-element.145), channel_id=1, source_target_pairs={{0,8},{2,10},{4,12},{6,14},{8,0},{10,2},{12,4},{14,6},{16,24},{18,... | collective-permute-start | bytes 589832 | tf_op jit(solution)/shard_map/ppermute | solution.py:358
  35.4 1.9 %shard_map.147 = (f32[2,256,256]{2,1,0:T(8,128)S(1)}, f32[2,256,256]{2,1,0:T(8,128)S(1)}, f32[2,256,256]{2,1,0:T(8,128)S(1)}, f32[256,256]{1,0:T(8,128)S(1)}, f3...) custom-call(s32[2]{0:T(128)S(1)} %pad_add_fusion.place, bf16[256,4,256]{2,1,0:T(4,128)(2,1)S(1)} %bitcast.21, ...), custom_call_target="tpu_custom_call" | custom-call | flops 16777216 | bytes 3158028 | tf_op jit(solution)/shard_map/pallas_call | solution.py:34
  37.4 1.6 %collective-permute-start.10 = (f32[2,256,256]{2,1,0:T(8,128)S(1)}, f32[2,256,256]{2,1,0:T(8,128)S(1)}, u32[]{:S(2)}, u32[]{:S(2)}) collective-permute-start(f32[2,256,256]{2,1,0:T(8,128)S(1)} %get-tuple-element.152), channel_id=1, source_target_pairs={{0,4},{2,6},{4,0},{6,2},{8,12},{10,14},{12,8},{14,10},{16,20},{18,... | collective-permute-start | bytes 1572872 | tf_op jit(solution)/shard_map/ppermute | solution.py:358
  39.5 2.7 %collective-permute-start.8 = (f32[1,3,64,256]{3,2,1,0:T(8,128)S(1)}, f32[1,3,64,256]{3,2,1,0:T(8,128)S(1)}, u32[]{:S(2)}, u32[]{:S(2)}) collective-permute-start(f32[1,3,64,256]{3,2,1,0:T(8,128)S(1)} %add.34), channel_id=1, source_target_pairs={{0,16},{2,18},{4,20},{6,22},{8,24},{10,26},{12,28},{14,30},{16,0},... | collective-permute-start | bytes 589832 | tf_op jit(solution)/shard_map/ppermute | solution.py:358
  42.2 1.0 collective-permute-start.7
  43.2 6.4 %collective-permute-done.8 = f32[1,3,64,256]{3,2,1,0:T(8,128)S(1)} collective-permute-done((f32[1,3,64,256]{3,2,1,0:T(8,128)S(1)}, f32[1,3,64,256]{3,2,1,0:T(8,128)S(1)}, u32[]{:S(2)}, u32[]{:S(2)}) %collective-permute-start.8) | collective-permute-done | bytes 196640 | tf_op jit(solution)/shard_map/ppermute | solution.py:358
  49.6 0.9 collective-permute-done.7
  50.5 2.1 %collective-permute-start.14 = (f32[1,3,64,256]{3,2,1,0:T(8,128)S(1)}, f32[1,3,64,256]{3,2,1,0:T(8,128)S(1)}, u32[]{:S(2)}, u32[]{:S(2)}) collective-permute-start(f32[1,3,64,256]{3,2,1,0:T(8,128)S(1)} %add_add_fusion.1.refs_5_), channel_id=1, source_target_pairs={{0,16},{2,18},{4,20},{6,22},{8,24},{10,26},{12,28},{14,30},{16,0},... | collective-permute-start | bytes 589832 | tf_op jit(solution)/shard_map/ppermute | solution.py:358
  52.6 2.4 %collective-permute-start.11 = (f32[256,256]{1,0:T(8,128)S(1)}, f32[256,256]{1,0:T(8,128)S(1)}, u32[]{:S(2)}, u32[]{:S(2)}) collective-permute-start(f32[256,256]{1,0:T(8,128)S(1)} %get-tuple-element.158), channel_id=1, source_target_pairs={{0,6},{2,4},{4,2},{6,0},{8,14},{10,12},{12,10},{14,8},{16,22},{18,... | collective-permute-start | bytes 786440 | tf_op jit(solution)/shard_map/ppermute | solution.py:358
  55.5 0.8 collective-permute-start.13
  56.4 4.3 %collective-permute-done.14.refs_7_ = f32[1,3,64,256]{3,2,1,0:T(8,128)S(1)} collective-permute-done((f32[1,3,64,256]{3,2,1,0:T(8,128)S(1)}, f32[1,3,64,256]{3,2,1,0:T(8,128)S(1)}, u32[]{:S(2)}, u32[]{:S(2)}) %collective-permute-start.14) | collective-permute-done | bytes 196640 | tf_op jit(solution)/shard_map/ppermute | solution.py:358
  60.6 2.2 %collective-permute-done.13.refs_6_ = f32[1,3,64,256]{3,2,1,0:T(8,128)S(1)} collective-permute-done((f32[1,3,64,256]{3,2,1,0:T(8,128)S(1)}, f32[1,3,64,256]{3,2,1,0:T(8,128)S(1)}, u32[]{:S(2)}, u32[]{:S(2)}) %collective-permute-start.13) | collective-permute-done | bytes 196640 | tf_op jit(solution)/shard_map/ppermute | solution.py:358
  62.9 1.5 %collective-permute-done.12.refs_4_.refs_8_ = f32[256,256]{1,0:T(8,128)S(1)} collective-permute-done((f32[256,256]{1,0:T(8,128)S(1)}, f32[256,256]{1,0:T(8,128)S(1)}, u32[]{:S(2)}, u32[]{:S(2)}) %collective-permute-start.12) | collective-permute-done | bytes 262176 | tf_op jit(solution)/shard_map/ppermute | solution.py:358
  64.4 2.5 %collective-permute-done.15.refs_8_ = f32[1,3,64,256]{3,2,1,0:T(8,128)S(1)} collective-permute-done((f32[1,3,64,256]{3,2,1,0:T(8,128)S(1)}, f32[1,3,64,256]{3,2,1,0:T(8,128)S(1)}, u32[]{:S(2)}, u32[]{:S(2)}) %collective-permute-start.15) | collective-permute-done | bytes 196640 | tf_op jit(solution)/shard_map/ppermute | solution.py:358
  66.9 1.8 %shard_map.149 = (f32[4,256,256]{2,1,0:T(8,128)S(1)}, f32[4,256,256]{2,1,0:T(8,128)S(1)}, bf16[4,256,256]{2,1,0:T(8,128)(2,1)S(1)}, f32[4,256,256]{2,1,0:T(8,128...) custom-call(s32[2]{0:T(128)S(1)} %pad_add_fusion.place, f32[8,256]{1,0:T(8,128)S(1)} %get-tuple-element.135.scale_row, ...), custom_call_target="tpu_custom_call" | custom-call | flops 402653184 | bytes 6963208 | tf_op jit(solution)/shard_map/pallas_call | solution.py:34
  68.7 1.2 collective-permute-done.16
  70.4 1.6 %collective-permute-start.18 = (f32[2,4,256]{2,1,0:T(4,128)S(1)}, f32[2,4,256]{2,1,0:T(4,128)S(1)}, u32[]{:S(2)}, u32[]{:S(2)}) collective-permute-start(f32[2,4,256]{2,1,0:T(4,128)S(1)} %add.36.refs_0_), channel_id=1, source_target_pairs={{0,4},{2,6},{4,0},{6,2},{8,12},{10,14},{12,8},{14,10},{16,20},{18,... | collective-permute-start | bytes 24584 | tf_op jit(solution)/shard_map/ppermute | solution.py:358
  72.0 1.4 collective-permute-start.19
  74.1 2.4 %collective-permute-done.19.refs_3_ = f32[2,4,256]{2,1,0:T(4,128)S(1)} collective-permute-done((f32[2,4,256]{2,1,0:T(4,128)S(1)}, f32[2,4,256]{2,1,0:T(4,128)S(1)}, u32[]{:S(2)}, u32[]{:S(2)}) %collective-permute-start.19) | collective-permute-done | bytes 8224 | tf_op jit(solution)/shard_map/ppermute | solution.py:358
  76.5 2.1 %shard_map.150 = (bf16[4,256,256]{2,1,0:T(8,128)(2,1)S(1)}, bf16[4,256,256]{2,1,0:T(8,128)(2,1)S(1)}, f32[1,3,64,256]{3,2,1,0:T(8,128)S(1)}, f32[1,3,64,256]{3,2...) custom-call(s32[2]{0:T(128)S(1)} %pad_add_fusion.place, ...), custom_call_target="tpu_custom_call" | custom-call | flops 805306368 | bytes 8036360 | tf_op jit(solution)/shard_map/pallas_call | solution.py:34
  79.1 5.3 %collective-permute-done.20 = f32[1,3,64,256]{3,2,1,0:T(8,128)S(1)} collective-permute-done((f32[1,3,64,256]{3,2,1,0:T(8,128)S(1)}, f32[1,3,64,256]{3,2,1,0:T(8,128)S(1)}, u32[]{:S(2)}, u32[]{:S(2)}) %collective-permute-start.20) | collective-permute-done | bytes 196640 | tf_op jit(solution)/shard_map/ppermute | solution.py:358
  84.4 0.9 collective-permute-start.22
  85.3 2.0 %collective-permute-start.21 = (f32[1,3,64,256]{3,2,1,0:T(8,128)S(1)}, f32[1,3,64,256]{3,2,1,0:T(8,128)S(1)}, u32[]{:S(2)}, u32[]{:S(2)}) collective-permute-start(f32[1,3,64,256]{3,2,1,0:T(8,128)S(1)} %get-tuple-element.178), channel_id=1, source_target_pairs={{0,8},{2,10},{4,12},{6,14},{8,0},{10,2},{12,4},{14,6},{16,24},{18,... | collective-permute-start | bytes 589832 | tf_op jit(solution)/shard_map/ppermute | solution.py:358
  87.4 6.3 %collective-permute-done.22 = f32[1,3,64,256]{3,2,1,0:T(8,128)S(1)} collective-permute-done((f32[1,3,64,256]{3,2,1,0:T(8,128)S(1)}, f32[1,3,64,256]{3,2,1,0:T(8,128)S(1)}, u32[]{:S(2)}, u32[]{:S(2)}) %collective-permute-start.22) | collective-permute-done | bytes 196640 | tf_op jit(solution)/shard_map/ppermute | solution.py:358
  93.7 0.6 collective-permute-start.24
  94.8 1.3 collective-permute-start.26
  96.7 1.6 %collective-permute-start.28 = (f32[256,256]{1,0:T(8,128)S(1)}, f32[256,256]{1,0:T(8,128)S(1)}, u32[]{:S(2)}, u32[]{:S(2)}) collective-permute-start(f32[256,256]{1,0:T(8,128)S(1)} %get-tuple-element.195), channel_id=1, source_target_pairs={{0,6},{2,4},{4,2},{6,0},{8,14},{10,12},{12,10},{14,8},{16,22},{18,... | collective-permute-start | bytes 786440 | tf_op jit(solution)/shard_map/ppermute | solution.py:358
  98.3 2.1 %collective-permute-start.23 = (f32[1,3,64,256]{3,2,1,0:T(8,128)S(1)}, f32[1,3,64,256]{3,2,1,0:T(8,128)S(1)}, u32[]{:S(2)}, u32[]{:S(2)}) collective-permute-start(f32[1,3,64,256]{3,2,1,0:T(8,128)S(1)} %add_add_fusion.refs_11_.refs_0_), channel_id=1, source_target_pairs={{0,8},{2,10},{4,12},{6,14},{8,0},{10,2},{12,4},{14,6},{16,24},{18,... | collective-permute-start | bytes 589832 | tf_op jit(solution)/shard_map/ppermute | solution.py:358
  100.5 3.2 %collective-permute-done.24.refs_13_ = f32[1,3,64,256]{3,2,1,0:T(8,128)S(1)} collective-permute-done((f32[1,3,64,256]{3,2,1,0:T(8,128)S(1)}, f32[1,3,64,256]{3,2,1,0:T(8,128)S(1)}, u32[]{:S(2)}, u32[]{:S(2)}) %collective-permute-start.24) | collective-permute-done | bytes 196640 | tf_op jit(solution)/shard_map/ppermute | solution.py:358
  103.7 1.0 shard_map.151
  104.8 2.7 %collective-permute-done.27.refs_2_ = f32[256,256]{1,0:T(8,128)S(1)} collective-permute-done((f32[256,256]{1,0:T(8,128)S(1)}, f32[256,256]{1,0:T(8,128)S(1)}, u32[]{:S(2)}, u32[]{:S(2)}) %collective-permute-start.27) | collective-permute-done | bytes 262176 | tf_op jit(solution)/shard_map/ppermute | solution.py:358
  107.5 2.9 %collective-permute-done.25.refs_14_ = f32[1,3,64,256]{3,2,1,0:T(8,128)S(1)} collective-permute-done((f32[1,3,64,256]{3,2,1,0:T(8,128)S(1)}, f32[1,3,64,256]{3,2,1,0:T(8,128)S(1)}, u32[]{:S(2)}, u32[]{:S(2)}) %collective-permute-start.25) | collective-permute-done | bytes 196640 | tf_op jit(solution)/shard_map/ppermute | solution.py:358
  110.4 3.0 %shard_map.153 = (f32[2,256,256]{2,1,0:T(8,128)S(1)}, f32[3,256,256]{2,1,0:T(8,128)S(1)}, f32[3,256,256]{2,1,0:T(8,128)S(1)}, f32[1,3,64,256]{3,2,1,0:T(8,128)S(...) custom-call(s32[2]{0:T(128)S(1)} %pad_add_fusion.place, ...), custom_call_target="tpu_custom_call" | custom-call | flops 1610612736 | bytes 13369352 | tf_op jit(solution)/shard_map/pallas_call | solution.py:34
  113.4 1.1 collective-permute-start.32
  115.4 5.4 %collective-permute-done.29 = f32[1,3,64,256]{3,2,1,0:T(8,128)S(1)} collective-permute-done((f32[1,3,64,256]{3,2,1,0:T(8,128)S(1)}, f32[1,3,64,256]{3,2,1,0:T(8,128)S(1)}, u32[]{:S(2)}, u32[]{:S(2)}) %collective-permute-start.29) | collective-permute-done | bytes 196640 | tf_op jit(solution)/shard_map/ppermute | solution.py:358
  121.3 2.0 %collective-permute-start.30 = (f32[1,3,64,256]{3,2,1,0:T(8,128)S(1)}, f32[1,3,64,256]{3,2,1,0:T(8,128)S(1)}, u32[]{:S(2)}, u32[]{:S(2)}) collective-permute-start(f32[1,3,64,256]{3,2,1,0:T(8,128)S(1)} %get-tuple-element.212), channel_id=1, source_target_pairs={{0,8},{2,10},{4,12},{6,14},{8,0},{10,2},{12,4},{14,6},{16,24},{18,... | collective-permute-start | bytes 589832 | tf_op jit(solution)/shard_map/ppermute | solution.py:358
  123.3 1.7 %shard_map.154 = bf16[256,4,256]{2,1,0:T(4,128)(2,1)} custom-call(s32[2]{0:T(128)S(1)} %pad_add_fusion.place, f32[256,256]{1,0:T(8,128)S(1)} %get-tuple-element.218.refs_0_, f32[256,256]{1,0:T(8,128)S(1)} %collective-permute-done.26.refs_1_, f32[256,256]{1,0:T(8,128)S(1)} %collective-permute-done.27.refs_2_, f32[256,256]{1,0:T(8,128)S(1)} %collective-permute-done.28.refs_3_), custom_call_target="tpu_custom_call" | custom-call | flops 8388608 | bytes 1572872 | tf_op jit(solution)/shard_map/pallas_call | solution.py:34
  125.0 5.2 %collective-permute-done.31.refs_3_ = f32[1,3,64,256]{3,2,1,0:T(8,128)S(1)} collective-permute-done((f32[1,3,64,256]{3,2,1,0:T(8,128)S(1)}, f32[1,3,64,256]{3,2,1,0:T(8,128)S(1)}, u32[]{:S(2)}, u32[]{:S(2)}) %collective-permute-start.31) | collective-permute-done | bytes 196640 | tf_op jit(solution)/shard_map/ppermute | solution.py:358
  130.2 1.7 %collective-permute-done.32.refs_1_ = f32[3,256,256]{2,1,0:T(8,128)S(1)} collective-permute-done((f32[3,256,256]{2,1,0:T(8,128)S(1)}, f32[3,256,256]{2,1,0:T(8,128)S(1)}, u32[]{:S(2)}, u32[]{:S(2)}) %collective-permute-start.32) | collective-permute-done | bytes 786464 | tf_op jit(solution)/shard_map/ppermute | solution.py:358
  131.9 0.8 collective-permute-done.33.refs_2_
  132.7 0.6 collective-permute-start.37
  133.4 0.8 collective-permute-start.38
  134.1 0.6 shard_map.155
  134.7 1.4 collective-permute-start.34
  136.1 1.5 %collective-permute-start.35 = (f32[1,3,16,256]{3,2,1,0:T(8,128)S(1)}, f32[1,3,16,256]{3,2,1,0:T(8,128)S(1)}, u32[]{:S(2)}, u32[]{:S(2)}) collective-permute-start(f32[1,3,16,256]{3,2,1,0:T(8,128)S(1)} %get-tuple-element.228), channel_id=1, source_target_pairs={{0,4},{2,6},{4,0},{6,2},{8,12},{10,14},{12,8},{14,10},{16,20},{18,... | collective-permute-start | bytes 147464 | tf_op jit(solution)/shard_map/ppermute | solution.py:358
  137.6 0.7 collective-permute-start.36
  138.3 1.5 %collective-permute-done.37.refs_3_ = f32[256,256]{1,0:T(8,128)S(1)} collective-permute-done((f32[256,256]{1,0:T(8,128)S(1)}, f32[256,256]{1,0:T(8,128)S(1)}, u32[]{:S(2)}, u32[]{:S(2)}) %collective-permute-start.37) | collective-permute-done | bytes 262176 | tf_op jit(solution)/shard_map/ppermute | solution.py:358
  140.2 2.4 %shard_map.156 = (bf16[256,4,256]{2,1,0:T(4,128)(2,1)}, bf16[256,4,256]{2,1,0:T(4,128)(2,1)}) custom-call(s32[2]{0:T(128)S(1)} %pad_add_fusion.place, f32[4,256]{1,0:T(4,128)S(1)} %bitcast.24, f32[2,256,256]{2,1,0:T(8,128)S(1)} %get-tuple-element.230.refs_0_, f32[3,256,256]{2,1,0:T(8,128)S(1)} %collective-permute-done.32.refs_1_, ...), custom_call_target="tpu_custom_call" | custom-call | flops 16777216 | bytes 3674120 | tf_op jit(solution)/shard_map/pallas_call | solution.py:34
  142.6 1.2 shard_map.157
  (59 shorter events, 6.7 us)
Async XLA Ops:
  0.6 16.1 %copy-start = (f32[4,256,256]{2,1,0:T(8,128)S(1)}, f32[4,256,256]{2,1,0:T(8,128)}, u32[]{:S(2)}) copy-start(f32[4,256,256]{2,1,0:T(8,128)} %param.16) | copy-start | bytes 3145732
  0.7 0.8 copy-start.4
  1.4 1.0 copy-start.5
  2.5 5.6 %copy-start.6 = (bf16[1,256,4,256]{3,2,1,0:T(4,128)(2,1)S(1)}, bf16[1,256,4,256]{3,2,1,0:T(4,128)(2,1)}, u32[]{:S(2)}) copy-start(bf16[1,256,4,256]{3,2,1,0:T(4,128)(2,1)} %param.11) | copy-start | bytes 1572868
  3.6 10.4 %collective-permute-start.3 = (f32[256,256]{1,0:T(8,128)S(1)}, f32[256,256]{1,0:T(8,128)S(1)}, u32[]{:S(2)}, u32[]{:S(2)}) collective-permute-start(f32[256,256]{1,0:T(8,128)S(1)} %get-tuple-element.130), channel_id=1, source_target_pairs={{0,2},{2,0},{4,6},{6,4},{8,10},{10,8},{12,14},{14,12},{16,18},{18,... | collective-permute-start | bytes 786440 | tf_op jit(solution)/shard_map/ppermute | solution.py:358
  6.6 14.1 %collective-permute-start.4 = (f32[256,256]{1,0:T(8,128)S(1)}, f32[256,256]{1,0:T(8,128)S(1)}, u32[]{:S(2)}, u32[]{:S(2)}) collective-permute-start(f32[256,256]{1,0:T(8,128)S(1)} %get-tuple-element.131), channel_id=1, source_target_pairs={{0,4},{2,6},{4,0},{6,2},{8,12},{10,14},{12,8},{14,10},{16,20},{18,... | collective-permute-start | bytes 786440 | tf_op jit(solution)/shard_map/ppermute | solution.py:358
  8.1 12.8 %collective-permute-start.5 = (f32[256,256]{1,0:T(8,128)S(1)}, f32[256,256]{1,0:T(8,128)S(1)}, u32[]{:S(2)}, u32[]{:S(2)}) collective-permute-start(f32[256,256]{1,0:T(8,128)S(1)} %get-tuple-element.132), channel_id=1, source_target_pairs={{0,6},{2,4},{4,2},{6,0},{8,14},{10,12},{12,10},{14,8},{16,22},{18,... | collective-permute-start | bytes 786440 | tf_op jit(solution)/shard_map/ppermute | solution.py:358
  9.8 0.7 copy-start.7
  10.4 14.5 %collective-permute-start = (f32[256,256]{1,0:T(8,128)}, f32[256,256]{1,0:T(8,128)S(1)}, u32[]{:S(2)}, u32[]{:S(2)}) collective-permute-start(f32[256,256]{1,0:T(8,128)} %get-tuple-element.126), channel_id=1, source_target_pairs={{0,2},{2,0},{4,6},{6,4},{8,10},{10,8},{12,14},{14,12},{16,18},{18,... | collective-permute-start | bytes 786440 | tf_op jit(solution)/shard_map/ppermute | solution.py:358
  12.4 18.8 %collective-permute-start.1 = (f32[256,256]{1,0:T(8,128)}, f32[256,256]{1,0:T(8,128)S(1)}, u32[]{:S(2)}, u32[]{:S(2)}) collective-permute-start(f32[256,256]{1,0:T(8,128)} %get-tuple-element.127), channel_id=1, source_target_pairs={{0,4},{2,6},{4,0},{6,2},{8,12},{10,14},{12,8},{14,10},{16,20},{18,... | collective-permute-start | bytes 786440 | tf_op jit(solution)/shard_map/ppermute | solution.py:358
  13.9 17.3 %collective-permute-start.2 = (f32[256,256]{1,0:T(8,128)S(1)}, f32[256,256]{1,0:T(8,128)S(1)}, u32[]{:S(2)}, u32[]{:S(2)}) collective-permute-start(f32[256,256]{1,0:T(8,128)S(1)} %get-tuple-element.128), channel_id=1, source_target_pairs={{0,6},{2,4},{4,2},{6,0},{8,14},{10,12},{12,10},{14,8},{16,22},{18,... | collective-permute-start | bytes 786440 | tf_op jit(solution)/shard_map/ppermute | solution.py:358
  16.7 14.5 %copy-start.8 = (bf16[256,256]{1,0:T(8,128)(2,1)S(1)}, bf16[256,256]{1,0:T(8,128)(2,1)}, u32[]{:S(2)}) copy-start(bf16[256,256]{1,0:T(8,128)(2,1)} %copy-done.7) | copy-start | bytes 393220
  31.2 4.2 %copy-start.1 = (bf16[1,256,4,256]{3,2,1,0:T(4,128)(2,1)S(1)}, bf16[1,256,4,256]{3,2,1,0:T(4,128)(2,1)}, u32[]{:S(2)}) copy-start(bf16[1,256,4,256]{3,2,1,0:T(4,128)(2,1)} %param.10) | copy-start | bytes 1572868
  31.2 4.2 %copy-start.2 = (bf16[1,256,4,256]{3,2,1,0:T(4,128)(2,1)S(1)}, bf16[1,256,4,256]{3,2,1,0:T(4,128)(2,1)}, u32[]{:S(2)}) copy-start(bf16[1,256,4,256]{3,2,1,0:T(4,128)(2,1)} %param.19) | copy-start | bytes 1572868
  33.2 1.7 %copy-start.9 = (f32[4]{0:T(128)S(1)}, f32[4]{0:T(128)}, u32[]{:S(2)}) copy-start(f32[4]{0:T(128)} %param.14) | copy-start | bytes 52
  33.2 2.2 %copy-start.3 = (f32[4,256]{1,0:T(4,128)S(1)}, f32[4,256]{1,0:T(4,128)}, u32[]{:S(2)}) copy-start(f32[4,256]{1,0:T(4,128)} %gain.1) | copy-start | bytes 12292
  33.2 6.3 %collective-permute-start.6 = (f32[1,3,64,256]{3,2,1,0:T(8,128)S(1)}, f32[1,3,64,256]{3,2,1,0:T(8,128)S(1)}, u32[]{:S(2)}, u32[]{:S(2)}) collective-permute-start(f32[1,3,64,256]{3,2,1,0:T(8,128)S(1)} %get-tuple-element.145), channel_id=1, source_target_pairs={{0,8},{2,10},{4,12},{6,14},{8,0},{10,2},{12,4},{14,6},{16,24},{18,... | collective-permute-start | bytes 589832 | tf_op jit(solution)/shard_map/ppermute | solution.py:358
  37.4 13.1 %collective-permute-start.10 = (f32[2,256,256]{2,1,0:T(8,128)S(1)}, f32[2,256,256]{2,1,0:T(8,128)S(1)}, u32[]{:S(2)}, u32[]{:S(2)}) collective-permute-start(f32[2,256,256]{2,1,0:T(8,128)S(1)} %get-tuple-element.152), channel_id=1, source_target_pairs={{0,4},{2,6},{4,0},{6,2},{8,12},{10,14},{12,8},{14,10},{16,20},{18,... | collective-permute-start | bytes 1572872 | tf_op jit(solution)/shard_map/ppermute | solution.py:358
  39.0 11.5 %collective-permute-start.9 = (f32[2,256,256]{2,1,0:T(8,128)S(1)}, f32[2,256,256]{2,1,0:T(8,128)S(1)}, u32[]{:S(2)}, u32[]{:S(2)}) collective-permute-start(f32[2,256,256]{2,1,0:T(8,128)S(1)} %get-tuple-element.151), channel_id=1, source_target_pairs={{0,2},{2,0},{4,6},{6,4},{8,10},{10,8},{12,14},{14,12},{16,18},{18,... | collective-permute-start | bytes 1572872 | tf_op jit(solution)/shard_map/ppermute | solution.py:358
  39.5 10.0 %collective-permute-start.8 = (f32[1,3,64,256]{3,2,1,0:T(8,128)S(1)}, f32[1,3,64,256]{3,2,1,0:T(8,128)S(1)}, u32[]{:S(2)}, u32[]{:S(2)}) collective-permute-start(f32[1,3,64,256]{3,2,1,0:T(8,128)S(1)} %add.34), channel_id=1, source_target_pairs={{0,16},{2,18},{4,20},{6,22},{8,24},{10,26},{12,28},{14,30},{16,0},... | collective-permute-start | bytes 589832 | tf_op jit(solution)/shard_map/ppermute | solution.py:358
  42.2 8.2 %collective-permute-start.7 = (f32[1,3,64,256]{3,2,1,0:T(8,128)S(1)}, f32[1,3,64,256]{3,2,1,0:T(8,128)S(1)}, u32[]{:S(2)}, u32[]{:S(2)}) collective-permute-start(f32[1,3,64,256]{3,2,1,0:T(8,128)S(1)} %get-tuple-element.147), channel_id=1, source_target_pairs={{0,8},{2,10},{4,12},{6,14},{8,0},{10,2},{12,4},{14,6},{16,24},{18,... | collective-permute-start | bytes 589832 | tf_op jit(solution)/shard_map/ppermute | solution.py:358
  50.5 10.1 %collective-permute-start.14 = (f32[1,3,64,256]{3,2,1,0:T(8,128)S(1)}, f32[1,3,64,256]{3,2,1,0:T(8,128)S(1)}, u32[]{:S(2)}, u32[]{:S(2)}) collective-permute-start(f32[1,3,64,256]{3,2,1,0:T(8,128)S(1)} %add_add_fusion.1.refs_5_), channel_id=1, source_target_pairs={{0,16},{2,18},{4,20},{6,22},{8,24},{10,26},{12,28},{14,30},{16,0},... | collective-permute-start | bytes 589832 | tf_op jit(solution)/shard_map/ppermute | solution.py:358
  52.6 10.3 %collective-permute-start.11 = (f32[256,256]{1,0:T(8,128)S(1)}, f32[256,256]{1,0:T(8,128)S(1)}, u32[]{:S(2)}, u32[]{:S(2)}) collective-permute-start(f32[256,256]{1,0:T(8,128)S(1)} %get-tuple-element.158), channel_id=1, source_target_pairs={{0,6},{2,4},{4,2},{6,0},{8,14},{10,12},{12,10},{14,8},{16,22},{18,... | collective-permute-start | bytes 786440 | tf_op jit(solution)/shard_map/ppermute | solution.py:358
  55.0 9.4 %collective-permute-start.12 = (f32[256,256]{1,0:T(8,128)S(1)}, f32[256,256]{1,0:T(8,128)S(1)}, u32[]{:S(2)}, u32[]{:S(2)}) collective-permute-start(f32[256,256]{1,0:T(8,128)S(1)} %get-tuple-element.159), channel_id=1, source_target_pairs={{0,6},{2,4},{4,2},{6,0},{8,14},{10,12},{12,10},{14,8},{16,22},{18,... | collective-permute-start | bytes 786440 | tf_op jit(solution)/shard_map/ppermute | solution.py:358
  55.5 7.3 %collective-permute-start.13 = (f32[1,3,64,256]{3,2,1,0:T(8,128)S(1)}, f32[1,3,64,256]{3,2,1,0:T(8,128)S(1)}, u32[]{:S(2)}, u32[]{:S(2)}) collective-permute-start(f32[1,3,64,256]{3,2,1,0:T(8,128)S(1)} %add_add_fusion.1.refs_5_), channel_id=1, source_target_pairs={{0,8},{2,10},{4,12},{6,14},{8,0},{10,2},{12,4},{14,6},{16,24},{18,... | collective-permute-start | bytes 589832 | tf_op jit(solution)/shard_map/ppermute | solution.py:358
  60.6 6.3 %collective-permute-start.15 = (f32[1,3,64,256]{3,2,1,0:T(8,128)S(1)}, f32[1,3,64,256]{3,2,1,0:T(8,128)S(1)}, u32[]{:S(2)}, u32[]{:S(2)}) collective-permute-start(f32[1,3,64,256]{3,2,1,0:T(8,128)S(1)} %collective-permute-done.14.refs_7_), channel_id=1, source_target_pairs={{0,8},{2,10},{4,12},{6,14},{8,0},{10,2},{12,4},{14,6},{16,24},{18,... | collective-permute-start | bytes 589832 | tf_op jit(solution)/shard_map/ppermute | solution.py:358
  68.7 1.2 collective-permute-start.16
  69.9 3.7 %collective-permute-start.17 = (f32[2,4,256]{2,1,0:T(4,128)S(1)}, f32[2,4,256]{2,1,0:T(4,128)S(1)}, u32[]{:S(2)}, u32[]{:S(2)}) collective-permute-start(f32[2,4,256]{2,1,0:T(4,128)S(1)} %add.36.refs_0_), channel_id=1, source_target_pairs={{0,2},{2,0},{4,6},{6,4},{8,10},{10,8},{12,14},{14,12},{16,18},{18,... | collective-permute-start | bytes 24584 | tf_op jit(solution)/shard_map/ppermute | solution.py:358
  70.4 3.7 %collective-permute-start.18 = (f32[2,4,256]{2,1,0:T(4,128)S(1)}, f32[2,4,256]{2,1,0:T(4,128)S(1)}, u32[]{:S(2)}, u32[]{:S(2)}) collective-permute-start(f32[2,4,256]{2,1,0:T(4,128)S(1)} %add.36.refs_0_), channel_id=1, source_target_pairs={{0,4},{2,6},{4,0},{6,2},{8,12},{10,14},{12,8},{14,10},{16,20},{18,... | collective-permute-start | bytes 24584 | tf_op jit(solution)/shard_map/ppermute | solution.py:358
  72.0 4.5 %collective-permute-start.19 = (f32[2,4,256]{2,1,0:T(4,128)S(1)}, f32[2,4,256]{2,1,0:T(4,128)S(1)}, u32[]{:S(2)}, u32[]{:S(2)}) collective-permute-start(f32[2,4,256]{2,1,0:T(4,128)S(1)} %add.36.refs_0_), channel_id=1, source_target_pairs={{0,6},{2,4},{4,2},{6,0},{8,14},{10,12},{12,10},{14,8},{16,22},{18,... | collective-permute-start | bytes 24584 | tf_op jit(solution)/shard_map/ppermute | solution.py:358
  78.7 5.7 %collective-permute-start.20 = (f32[1,3,64,256]{3,2,1,0:T(8,128)S(1)}, f32[1,3,64,256]{3,2,1,0:T(8,128)S(1)}, u32[]{:S(2)}, u32[]{:S(2)}) collective-permute-start(f32[1,3,64,256]{3,2,1,0:T(8,128)S(1)} %get-tuple-element.176), channel_id=1, source_target_pairs={{0,8},{2,10},{4,12},{6,14},{8,0},{10,2},{12,4},{14,6},{16,24},{18,... | collective-permute-start | bytes 589832 | tf_op jit(solution)/shard_map/ppermute | solution.py:358
  84.4 9.2 %collective-permute-start.22 = (f32[1,3,64,256]{3,2,1,0:T(8,128)S(1)}, f32[1,3,64,256]{3,2,1,0:T(8,128)S(1)}, u32[]{:S(2)}, u32[]{:S(2)}) collective-permute-start(f32[1,3,64,256]{3,2,1,0:T(8,128)S(1)} %add.38), channel_id=1, source_target_pairs={{0,16},{2,18},{4,20},{6,22},{8,24},{10,26},{12,28},{14,30},{16,0},... | collective-permute-start | bytes 589832 | tf_op jit(solution)/shard_map/ppermute | solution.py:358
  85.3 8.3 %collective-permute-start.21 = (f32[1,3,64,256]{3,2,1,0:T(8,128)S(1)}, f32[1,3,64,256]{3,2,1,0:T(8,128)S(1)}, u32[]{:S(2)}, u32[]{:S(2)}) collective-permute-start(f32[1,3,64,256]{3,2,1,0:T(8,128)S(1)} %get-tuple-element.178), channel_id=1, source_target_pairs={{0,8},{2,10},{4,12},{6,14},{8,0},{10,2},{12,4},{14,6},{16,24},{18,... | collective-permute-start | bytes 589832 | tf_op jit(solution)/shard_map/ppermute | solution.py:358
  93.7 10.0 %collective-permute-start.24 = (f32[1,3,64,256]{3,2,1,0:T(8,128)S(1)}, f32[1,3,64,256]{3,2,1,0:T(8,128)S(1)}, u32[]{:S(2)}, u32[]{:S(2)}) collective-permute-start(f32[1,3,64,256]{3,2,1,0:T(8,128)S(1)} %add_add_fusion.refs_11_.refs_0_), channel_id=1, source_target_pairs={{0,16},{2,18},{4,20},{6,22},{8,24},{10,26},{12,28},{14,30},{16,0},... | collective-permute-start | bytes 589832 | tf_op jit(solution)/shard_map/ppermute | solution.py:358
  94.8 10.0 %collective-permute-start.26 = (f32[256,256]{1,0:T(8,128)S(1)}, f32[256,256]{1,0:T(8,128)S(1)}, u32[]{:S(2)}, u32[]{:S(2)}) collective-permute-start(f32[256,256]{1,0:T(8,128)S(1)} %get-tuple-element.193), channel_id=1, source_target_pairs={{0,2},{2,0},{4,6},{6,4},{8,10},{10,8},{12,14},{14,12},{16,18},{18,... | collective-permute-start | bytes 786440 | tf_op jit(solution)/shard_map/ppermute | solution.py:358
  96.1 11.4 %collective-permute-start.27 = (f32[256,256]{1,0:T(8,128)S(1)}, f32[256,256]{1,0:T(8,128)S(1)}, u32[]{:S(2)}, u32[]{:S(2)}) collective-permute-start(f32[256,256]{1,0:T(8,128)S(1)} %get-tuple-element.194), channel_id=1, source_target_pairs={{0,4},{2,6},{4,0},{6,2},{8,12},{10,14},{12,8},{14,10},{16,20},{18,... | collective-permute-start | bytes 786440 | tf_op jit(solution)/shard_map/ppermute | solution.py:358
  96.7 10.8 %collective-permute-start.28 = (f32[256,256]{1,0:T(8,128)S(1)}, f32[256,256]{1,0:T(8,128)S(1)}, u32[]{:S(2)}, u32[]{:S(2)}) collective-permute-start(f32[256,256]{1,0:T(8,128)S(1)} %get-tuple-element.195), channel_id=1, source_target_pairs={{0,6},{2,4},{4,2},{6,0},{8,14},{10,12},{12,10},{14,8},{16,22},{18,... | collective-permute-start | bytes 786440 | tf_op jit(solution)/shard_map/ppermute | solution.py:358
  98.3 9.2 %collective-permute-start.23 = (f32[1,3,64,256]{3,2,1,0:T(8,128)S(1)}, f32[1,3,64,256]{3,2,1,0:T(8,128)S(1)}, u32[]{:S(2)}, u32[]{:S(2)}) collective-permute-start(f32[1,3,64,256]{3,2,1,0:T(8,128)S(1)} %add_add_fusion.refs_11_.refs_0_), channel_id=1, source_target_pairs={{0,8},{2,10},{4,12},{6,14},{8,0},{10,2},{12,4},{14,6},{16,24},{18,... | collective-permute-start | bytes 589832 | tf_op jit(solution)/shard_map/ppermute | solution.py:358
  103.7 6.7 %collective-permute-start.25 = (f32[1,3,64,256]{3,2,1,0:T(8,128)S(1)}, f32[1,3,64,256]{3,2,1,0:T(8,128)S(1)}, u32[]{:S(2)}, u32[]{:S(2)}) collective-permute-start(f32[1,3,64,256]{3,2,1,0:T(8,128)S(1)} %collective-permute-done.24.refs_13_), channel_id=1, source_target_pairs={{0,8},{2,10},{4,12},{6,14},{8,0},{10,2},{12,4},{14,6},{16,24},{18,... | collective-permute-start | bytes 589832 | tf_op jit(solution)/shard_map/ppermute | solution.py:358
  113.4 18.5 %collective-permute-start.32 = (f32[3,256,256]{2,1,0:T(8,128)S(1)}, f32[3,256,256]{2,1,0:T(8,128)S(1)}, u32[]{:S(2)}, u32[]{:S(2)}) collective-permute-start(f32[3,256,256]{2,1,0:T(8,128)S(1)} %get-tuple-element.216), channel_id=1, source_target_pairs={{0,2},{2,0},{4,6},{6,4},{8,10},{10,8},{12,14},{14,12},{16,18},{18,... | collective-permute-start | bytes 2359304 | tf_op jit(solution)/shard_map/ppermute | solution.py:358
  114.6 18.1 %collective-permute-start.33 = (f32[3,256,256]{2,1,0:T(8,128)S(1)}, f32[3,256,256]{2,1,0:T(8,128)S(1)}, u32[]{:S(2)}, u32[]{:S(2)}) collective-permute-start(f32[3,256,256]{2,1,0:T(8,128)S(1)} %get-tuple-element.217), channel_id=1, source_target_pairs={{0,4},{2,6},{4,0},{6,2},{8,12},{10,14},{12,8},{14,10},{16,20},{18,... | collective-permute-start | bytes 2359304 | tf_op jit(solution)/shard_map/ppermute | solution.py:358
  115.1 5.7 %collective-permute-start.29 = (f32[1,3,64,256]{3,2,1,0:T(8,128)S(1)}, f32[1,3,64,256]{3,2,1,0:T(8,128)S(1)}, u32[]{:S(2)}, u32[]{:S(2)}) collective-permute-start(f32[1,3,64,256]{3,2,1,0:T(8,128)S(1)} %get-tuple-element.210), channel_id=1, source_target_pairs={{0,8},{2,10},{4,12},{6,14},{8,0},{10,2},{12,4},{14,6},{16,24},{18,... | collective-permute-start | bytes 589832 | tf_op jit(solution)/shard_map/ppermute | solution.py:358
  120.8 9.4 %collective-permute-start.31 = (f32[1,3,64,256]{3,2,1,0:T(8,128)S(1)}, f32[1,3,64,256]{3,2,1,0:T(8,128)S(1)}, u32[]{:S(2)}, u32[]{:S(2)}) collective-permute-start(f32[1,3,64,256]{3,2,1,0:T(8,128)S(1)} %add.40), channel_id=1, source_target_pairs={{0,16},{2,18},{4,20},{6,22},{8,24},{10,26},{12,28},{14,30},{16,0},... | collective-permute-start | bytes 589832 | tf_op jit(solution)/shard_map/ppermute | solution.py:358
  121.3 8.9 %collective-permute-start.30 = (f32[1,3,64,256]{3,2,1,0:T(8,128)S(1)}, f32[1,3,64,256]{3,2,1,0:T(8,128)S(1)}, u32[]{:S(2)}, u32[]{:S(2)}) collective-permute-start(f32[1,3,64,256]{3,2,1,0:T(8,128)S(1)} %get-tuple-element.212), channel_id=1, source_target_pairs={{0,8},{2,10},{4,12},{6,14},{8,0},{10,2},{12,4},{14,6},{16,24},{18,... | collective-permute-start | bytes 589832 | tf_op jit(solution)/shard_map/ppermute | solution.py:358
  132.7 7.1 %collective-permute-start.37 = (f32[256,256]{1,0:T(8,128)S(1)}, f32[256,256]{1,0:T(8,128)S(1)}, u32[]{:S(2)}, u32[]{:S(2)}) collective-permute-start(f32[256,256]{1,0:T(8,128)S(1)} %slice_bitcast_fusion.1), channel_id=1, source_target_pairs={{0,4},{2,6},{4,0},{6,2},{8,12},{10,14},{12,8},{14,10},{16,20},{18,... | collective-permute-start | bytes 786440 | tf_op jit(solution)/shard_map/ppermute | solution.py:358
  133.4 6.8 %collective-permute-start.38 = (f32[256,256]{1,0:T(8,128)S(1)}, f32[256,256]{1,0:T(8,128)S(1)}, u32[]{:S(2)}, u32[]{:S(2)}) collective-permute-start(f32[256,256]{1,0:T(8,128)S(1)} %slice_bitcast_fusion), channel_id=1, source_target_pairs={{0,2},{2,0},{4,6},{6,4},{8,10},{10,8},{12,14},{14,12},{16,18},{18,... | collective-permute-start | bytes 786440 | tf_op jit(solution)/shard_map/ppermute | solution.py:358
  134.7 7.8 %collective-permute-start.34 = (f32[1,3,16,256]{3,2,1,0:T(8,128)S(1)}, f32[1,3,16,256]{3,2,1,0:T(8,128)S(1)}, u32[]{:S(2)}, u32[]{:S(2)}) collective-permute-start(f32[1,3,16,256]{3,2,1,0:T(8,128)S(1)} %get-tuple-element.227), channel_id=1, source_target_pairs={{0,2},{2,0},{4,6},{6,4},{8,10},{10,8},{12,14},{14,12},{16,18},{18,... | collective-permute-start | bytes 147464 | tf_op jit(solution)/shard_map/ppermute | solution.py:358
  136.1 6.4 %collective-permute-start.35 = (f32[1,3,16,256]{3,2,1,0:T(8,128)S(1)}, f32[1,3,16,256]{3,2,1,0:T(8,128)S(1)}, u32[]{:S(2)}, u32[]{:S(2)}) collective-permute-start(f32[1,3,16,256]{3,2,1,0:T(8,128)S(1)} %get-tuple-element.228), channel_id=1, source_target_pairs={{0,4},{2,6},{4,0},{6,2},{8,12},{10,14},{12,8},{14,10},{16,20},{18,... | collective-permute-start | bytes 147464 | tf_op jit(solution)/shard_map/ppermute | solution.py:358
  137.6 5.0 %collective-permute-start.36 = (f32[1,3,16,256]{3,2,1,0:T(8,128)S(1)}, f32[1,3,16,256]{3,2,1,0:T(8,128)S(1)}, u32[]{:S(2)}, u32[]{:S(2)}) collective-permute-start(f32[1,3,16,256]{3,2,1,0:T(8,128)S(1)} %get-tuple-element.229), channel_id=1, source_target_pairs={{0,6},{2,4},{4,2},{6,0},{8,14},{10,12},{12,10},{14,8},{16,22},{18,... | collective-permute-start | bytes 147464 | tf_op jit(solution)/shard_map/ppermute | solution.py:358

commit v17 on v16

--- a/solution.py
+++ b/solution.py
@@ -97,7 +97,7 @@
     found = {}
     for ref, members in zip(refs, packing(groups)):
         for i, member in enumerate(members):
-            found[member] = ref.at[i]
+            found[member] = ref.at[i] if ref is not None else None
     for i, ref in enumerate(refs[len(packing(groups)) :]):
         found[(groups - 1, i)] = ref
     return [(found[(step, 0)], found[(step, 1)]) for step in range(groups)]
@@ -261,20 +261,12 @@
         act_r[step] = (activ * third).astype(BF16)
 
 
-def update_back_kernel(groups, depth, scale, place, *refs):
-    (k_kept, s_kept), refs = refs[:2], refs[2:]
-    kept, refs = refs[:9], refs[9:]
-    dact_r, third_r, activ_r, deriv_r, slope_r, second_r, dfirst_r, dthird_r, act_r = kept
-    parts, refs = refs[:depth], refs[depth:]
-    w_gate, w_out, w_up = refs[:3]
-    packed = len(packing(groups))
-    outs, slices = unpacked(groups, refs[3 : packed + 3]), refs[packed + 3 : -2]
-    whole, sums = refs[-2:]
-    assemble(place, parts, whole)
-    gate_b, out_b, up_b = (w[...].astype(BF16) for w in (w_gate, w_out, w_up))
-    cot_gate, cot_out, cot_up = ((whole[i] * scale).astype(BF16) for i in range(3))
+def update_back_steps(steps, outs, refs, weights, cots):
+    k_kept, s_kept, dact_r, third_r, activ_r, deriv_r, slope_r, second_r, dfirst_r, dthird_r, act_r = refs
+    gate_b, out_b, up_b = weights
+    cot_gate, cot_out, cot_up = cots
     firsts, thirds, dacts = [], [], []
-    for step in range(groups):
+    for step in steps:
         keys, scaled = k_kept[step], s_kept[step]
         bar_dfirst = mm(keys, cot_gate)
         bar_dthird = mm(keys, cot_up)
@@ -295,10 +287,38 @@
         firsts.append(bar_first)
         thirds.append(bar_third)
         dacts.append(bar_dact)
-    keys = tokens_of(k_kept)
-    sums[0] = tmm(keys, jnp.concatenate(firsts))
-    sums[1] = tmm(jnp.concatenate(dacts), tokens_of(s_kept))
-    sums[2] = tmm(keys, jnp.concatenate(thirds))
+    return firsts, thirds, dacts
+
+
+def update_away_kernel(groups, depth, scale, place, *refs):
+    kept, refs = refs[:11], refs[11:]
+    parts, refs = refs[:depth], refs[depth:]
+    weights = [w[...].astype(BF16) for w in refs[:3]]
+    outs, (cots, firsts, thirds, dacts, whole) = refs[3:-5], refs[-5:]
+    assemble(place, parts, whole)
+    cots[...] = (whole[...] * scale).astype(BF16)
+    outs = unpacked(groups, [None] + list(outs))
+    found = update_back_steps(range(1, groups), outs, kept, weights, [cots[i] for i in range(3)])
+    for to, values in zip((firsts, thirds, dacts), found):
+        for i, value in enumerate(values):
+            to[i] = value
+
+
+def update_home_kernel(depth, place, *refs):
+    kept, refs = refs[:11], refs[11:]
+    weights = [w[...].astype(BF16) for w in refs[:3]]
+    cots, firsts, thirds, dacts = refs[3:7]
+    out, slices, sums = refs[7], refs[8:-1], refs[-1]
+    outs = [(out.at[0], out.at[1])]
+    found = update_back_steps([0], outs, kept, weights, [cots[i] for i in range(3)])
+    first, third, dact = (
+        jnp.concatenate(mine + [tokens_of(ref)])
+        for mine, ref in zip(found, (firsts, thirds, dacts))
+    )
+    keys = tokens_of(kept[0])
+    sums[0] = tmm(keys, first)
+    sums[1] = tmm(dact, tokens_of(kept[1]))
+    sums[2] = tmm(keys, third)
     send_slices(sums, slices, place[1], depth)
 
 
@@ -400,6 +420,7 @@
         return call(body, outs, [scratch], 16 * flops, place, *args, mib=8)
 
     k_in = in_plane(split(split_kernel, keys[0]))
+    k_in[0], values, rates = after(k_in[0], values, rates)
     s_in = in_plane(split(split_scaled_kernel, values[0], rates[0]))
     own = [lax.dynamic_index_in_dim(w, mine, 0, keepdims=False) for w in (w_gate, w_out, w_up)]
     own_scale = lax.dynamic_index_in_dim(head_scale, mine, 0, keepdims=True)[None, :]
@@ -458,14 +479,18 @@
         place, *q_back,
     )
     rows = hidden // depth
-    out = call(
-        functools.partial(update_back_kernel, groups, depth, scale),
-        [kept(len(members)) for members in packing(groups)] + slices, [square] * 2, 12 * flops,
-        place, *early, *saved, *parts, *own, mib=24,
-    )
-    packed = len(packing(groups))
-    back = in_plane(out[:packed])
-    ends = scatter(out[packed:], depth, groups)
+    away = [kept(len(members)) for members in packing(groups)[1:]]
+    *sent, cots, firsts, thirds, dacts = call(
+        functools.partial(update_away_kernel, groups, depth, scale),
+        away + [shape(3, hidden, width, dtype=BF16)] + [kept(groups - 1, dtype=BF16)] * 3,
+        [square], 9 * flops, place, *early, *saved, *parts, *own, mib=24,
+    )
+    mine_back, *ends = call(
+        functools.partial(update_home_kernel, depth), [kept(2)] + slices, [square], 5 * flops,
+        place, *early, *saved, *own, cots, firsts, thirds, dacts,
+    )
+    back = in_plane([mine_back] + sent)
+    ends = scatter(ends, depth, groups)
     if groups == 4:
         ends, back, grad_q = after(ends, back, grad_q)
         back += [move(back[1][2], "ctx", 2), move(back[2][2], "ctx", 1)]

time: 144 us -> 146 us (1.014)
  starting transfers between devices: 46.6 us -> 50.1 us
  waiting for transfers between devices: 70.9 us -> 68.8 us
    ppermute x39, starting transfers between devices: 46.6 us -> 50.1 us  [move(): lax.ppermute(x, axis, [(c, c ^ step) for c in range(lax.axis_size(axis))])]
    ppermute x39, waiting for transfers between devices: 70.9 us -> 68.8 us  [move(): lax.ppermute(x, axis, [(c, c ^ step) for c in range(lax.axis_size(axis))])]
    pallas_call x13 -> x14, Pallas kernels: 21.1 us -> 21.9 us  [call(): pl.pallas_call(body, out_shape=out_shape, in_specs=[smem if a.dtype == jn...]
  transfers between devices with their start and end apart: 39 -> 39, of which waited for: 25 -> 27; matrix products, arithmetic and copies ran while one was open for 1% -> 1% of each run, Pallas kernels for 7% -> 8%
where the time goes in v17:
time: 146 us; the launch traced here: 145 us
  waiting for transfers between devices  68.8 us (47%)
  starting transfers between devices  50.1 us (34%)
  Pallas kernels  21.9 us (15%)
  local copies, waits for them, and re-layouts  3.56 us (2%)
    ppermute x39, waiting for transfers between devices, move(): lax.ppermute(x, axis, [(c, c ^ step) for c in range(lax.axis_size(axis))])  68.8 us
    ppermute x39, starting transfers between devices, move(): lax.ppermute(x, axis, [(c, c ^ step) for c in range(lax.axis_size(axis))])  50.1 us
    pallas_call x14, Pallas kernels, call(): pl.pallas_call(body, out_shape=out_shape, in_specs=[smem if a.dtype == jn...  21.9 us
  transfers between devices with their start and end apart: 39, of which 27 were waited for; matrix products, arithmetic and copies ran while one was open for 1% of the time, Pallas kernels for 8%

profile of v17, /device:TPU:0, one launch (start us, length us, event | category | flops | bytes accessed | tf_op | source)
XLA Modules:
  0.0 145.5 jit_solution(11818403339222159140)
XLA Ops:
  0.7 1.1 copy-done.5
  1.8 0.9 shard_map.145
  2.7 3.0 %collective-permute-start = (f32[256,256]{1,0:T(8,128)S(1)}, f32[256,256]{1,0:T(8,128)S(1)}, u32[]{:S(2)}, u32[]{:S(2)}) collective-permute-start(f32[256,256]{1,0:T(8,128)S(1)} %get-tuple-element.134), channel_id=1, source_target_pairs={{0,2},{2,0},{4,6},{6,4},{8,10},{10,8},{12,14},{14,12},{16,18},{18,... | collective-permute-start | bytes 786440 | tf_op jit(solution)/shard_map/ppermute | solution.py:378
  5.8 1.5 %collective-permute-start.1 = (f32[256,256]{1,0:T(8,128)S(1)}, f32[256,256]{1,0:T(8,128)S(1)}, u32[]{:S(2)}, u32[]{:S(2)}) collective-permute-start(f32[256,256]{1,0:T(8,128)S(1)} %get-tuple-element.135), channel_id=1, source_target_pairs={{0,4},{2,6},{4,0},{6,2},{8,12},{10,14},{12,8},{14,10},{16,20},{18,... | collective-permute-start | bytes 786440 | tf_op jit(solution)/shard_map/ppermute | solution.py:378
  7.3 1.8 %shard_map.146 = (bf16[256,256]{1,0:T(8,128)(2,1)S(1)}, f32[256,256]{1,0:T(8,128)}, f32[256,256]{1,0:T(8,128)}, f32[256,256]{1,0:T(8,128)S(1)}) custom-call(s32[2]{0:T(128)S(1)} %pad_add_fusion.place, bf16[256,4,256]{2,1,0:T(4,128)(2,1)S(1)} %bitcast.26, f32[4,256]{1,0:T(4,128)S(1)} %bitcast.23), custom_call_target="tpu_custom_call" | custom-call | flops 2147483648 | bytes 1445896 | tf_op jit(solution)/shard_map/pallas_call | solution.py:34
  9.8 1.9 %collective-permute-start.3 = (f32[256,256]{1,0:T(8,128)}, f32[256,256]{1,0:T(8,128)S(1)}, u32[]{:S(2)}, u32[]{:S(2)}) collective-permute-start(f32[256,256]{1,0:T(8,128)} %get-tuple-element.140), channel_id=1, source_target_pairs={{0,2},{2,0},{4,6},{6,4},{8,10},{10,8},{12,14},{14,12},{16,18},{18,... | collective-permute-start | bytes 786440 | tf_op jit(solution)/shard_map/ppermute | solution.py:378
  11.7 1.5 %collective-permute-start.4 = (f32[256,256]{1,0:T(8,128)}, f32[256,256]{1,0:T(8,128)S(1)}, u32[]{:S(2)}, u32[]{:S(2)}) collective-permute-start(f32[256,256]{1,0:T(8,128)} %get-tuple-element.141), channel_id=1, source_target_pairs={{0,4},{2,6},{4,0},{6,2},{8,12},{10,14},{12,8},{14,10},{16,20},{18,... | collective-permute-start | bytes 786440 | tf_op jit(solution)/shard_map/ppermute | solution.py:378
  13.2 2.7 %collective-permute-start.5 = (f32[256,256]{1,0:T(8,128)S(1)}, f32[256,256]{1,0:T(8,128)S(1)}, u32[]{:S(2)}, u32[]{:S(2)}) collective-permute-start(f32[256,256]{1,0:T(8,128)S(1)} %get-tuple-element.142), channel_id=1, source_target_pairs={{0,6},{2,4},{4,2},{6,0},{8,14},{10,12},{12,10},{14,8},{16,22},{18,... | collective-permute-start | bytes 786440 | tf_op jit(solution)/shard_map/ppermute | solution.py:378
  15.9 1.1 dynamic-slice_bitcast_fusion
  17.0 2.7 %collective-permute-done.1.refs_2_ = f32[256,256]{1,0:T(8,128)S(1)} collective-permute-done((f32[256,256]{1,0:T(8,128)S(1)}, f32[256,256]{1,0:T(8,128)S(1)}, u32[]{:S(2)}, u32[]{:S(2)}) %collective-permute-start.1) | collective-permute-done | bytes 262176 | tf_op jit(solution)/shard_map/ppermute | solution.py:378
  20.1 4.1 %collective-permute-done.3.refs_5_ = f32[256,256]{1,0:T(8,128)S(1)} collective-permute-done((f32[256,256]{1,0:T(8,128)}, f32[256,256]{1,0:T(8,128)S(1)}, u32[]{:S(2)}, u32[]{:S(2)}) %collective-permute-start.3) | collective-permute-done | bytes 262176 | tf_op jit(solution)/shard_map/ppermute | solution.py:378
  24.2 6.2 %collective-permute-done.4.refs_6_ = f32[256,256]{1,0:T(8,128)S(1)} collective-permute-done((f32[256,256]{1,0:T(8,128)}, f32[256,256]{1,0:T(8,128)S(1)}, u32[]{:S(2)}, u32[]{:S(2)}) %collective-permute-start.4) | collective-permute-done | bytes 262176 | tf_op jit(solution)/shard_map/ppermute | solution.py:378
  30.4 2.0 %shard_map.148 = (bf16[4,256,256]{2,1,0:T(8,128)(2,1)S(1)}, bf16[4,256,256]{2,1,0:T(8,128)(2,1)S(1)}, f32[1,3,64,256]{3,2,1,0:T(8,128)S(1)}, f32[1,3,64,256]{3,2...) custom-call(s32[2]{0:T(128)S(1)} %pad_add_fusion.place, ...), custom_call_target="tpu_custom_call" | custom-call | flops 805306368 | bytes 4456456 | tf_op jit(solution)/shard_map/pallas_call | solution.py:34
  32.4 1.6 %collective-permute-start.6 = (f32[1,3,64,256]{3,2,1,0:T(8,128)S(1)}, f32[1,3,64,256]{3,2,1,0:T(8,128)S(1)}, u32[]{:S(2)}, u32[]{:S(2)}) collective-permute-start(f32[1,3,64,256]{3,2,1,0:T(8,128)S(1)} %get-tuple-element.155), channel_id=1, source_target_pairs={{0,8},{2,10},{4,12},{6,14},{8,0},{10,2},{12,4},{14,6},{16,24},{18,... | collective-permute-start | bytes 589832 | tf_op jit(solution)/shard_map/ppermute | solution.py:378
  34.6 1.9 %shard_map.147 = (f32[2,256,256]{2,1,0:T(8,128)S(1)}, f32[2,256,256]{2,1,0:T(8,128)S(1)}, f32[2,256,256]{2,1,0:T(8,128)S(1)}, f32[256,256]{1,0:T(8,128)S(1)}, f3...) custom-call(s32[2]{0:T(128)S(1)} %pad_add_fusion.place, bf16[256,4,256]{2,1,0:T(4,128)(2,1)S(1)} %bitcast.21, ...), custom_call_target="tpu_custom_call" | custom-call | flops 16777216 | bytes 3158028 | tf_op jit(solution)/shard_map/pallas_call | solution.py:34
  36.6 1.3 collective-permute-start.9
  37.9 0.8 collective-permute-start.10
  38.7 2.7 %collective-permute-start.8 = (f32[1,3,64,256]{3,2,1,0:T(8,128)S(1)}, f32[1,3,64,256]{3,2,1,0:T(8,128)S(1)}, u32[]{:S(2)}, u32[]{:S(2)}) collective-permute-start(f32[1,3,64,256]{3,2,1,0:T(8,128)S(1)} %add.34), channel_id=1, source_target_pairs={{0,16},{2,18},{4,20},{6,22},{8,24},{10,26},{12,28},{14,30},{16,0},... | collective-permute-start | bytes 589832 | tf_op jit(solution)/shard_map/ppermute | solution.py:378
  41.4 1.0 collective-permute-start.7
  42.4 6.3 %collective-permute-done.8 = f32[1,3,64,256]{3,2,1,0:T(8,128)S(1)} collective-permute-done((f32[1,3,64,256]{3,2,1,0:T(8,128)S(1)}, f32[1,3,64,256]{3,2,1,0:T(8,128)S(1)}, u32[]{:S(2)}, u32[]{:S(2)}) %collective-permute-start.8) | collective-permute-done | bytes 196640 | tf_op jit(solution)/shard_map/ppermute | solution.py:378
  48.7 0.9 collective-permute-done.7
  50.1 2.6 %collective-permute-start.14 = (f32[1,3,64,256]{3,2,1,0:T(8,128)S(1)}, f32[1,3,64,256]{3,2,1,0:T(8,128)S(1)}, u32[]{:S(2)}, u32[]{:S(2)}) collective-permute-start(f32[1,3,64,256]{3,2,1,0:T(8,128)S(1)} %add_add_fusion.1.refs_5_), channel_id=1, source_target_pairs={{0,16},{2,18},{4,20},{6,22},{8,24},{10,26},{12,28},{14,30},{16,0},... | collective-permute-start | bytes 589832 | tf_op jit(solution)/shard_map/ppermute | solution.py:378
  53.2 2.4 %collective-permute-start.12 = (f32[256,256]{1,0:T(8,128)S(1)}, f32[256,256]{1,0:T(8,128)S(1)}, u32[]{:S(2)}, u32[]{:S(2)}) collective-permute-start(f32[256,256]{1,0:T(8,128)S(1)} %get-tuple-element.169), channel_id=1, source_target_pairs={{0,6},{2,4},{4,2},{6,0},{8,14},{10,12},{12,10},{14,8},{16,22},{18,... | collective-permute-start | bytes 786440 | tf_op jit(solution)/shard_map/ppermute | solution.py:378
  55.6 0.8 collective-permute-start.13
  56.5 3.3 %collective-permute-done.14.refs_7_ = f32[1,3,64,256]{3,2,1,0:T(8,128)S(1)} collective-permute-done((f32[1,3,64,256]{3,2,1,0:T(8,128)S(1)}, f32[1,3,64,256]{3,2,1,0:T(8,128)S(1)}, u32[]{:S(2)}, u32[]{:S(2)}) %collective-permute-start.14) | collective-permute-done | bytes 196640 | tf_op jit(solution)/shard_map/ppermute | solution.py:378
  59.9 3.1 %collective-permute-done.13.refs_6_ = f32[1,3,64,256]{3,2,1,0:T(8,128)S(1)} collective-permute-done((f32[1,3,64,256]{3,2,1,0:T(8,128)S(1)}, f32[1,3,64,256]{3,2,1,0:T(8,128)S(1)}, u32[]{:S(2)}, u32[]{:S(2)}) %collective-permute-start.13) | collective-permute-done | bytes 196640 | tf_op jit(solution)/shard_map/ppermute | solution.py:378
  63.0 1.6 %collective-permute-done.12.refs_4_.refs_8_ = f32[256,256]{1,0:T(8,128)S(1)} collective-permute-done((f32[256,256]{1,0:T(8,128)S(1)}, f32[256,256]{1,0:T(8,128)S(1)}, u32[]{:S(2)}, u32[]{:S(2)}) %collective-permute-start.12) | collective-permute-done | bytes 262176 | tf_op jit(solution)/shard_map/ppermute | solution.py:378
  64.7 1.4 collective-permute-done.15.refs_8_
  66.1 1.8 %shard_map.149 = (f32[4,256,256]{2,1,0:T(8,128)S(1)}, f32[4,256,256]{2,1,0:T(8,128)S(1)}, bf16[4,256,256]{2,1,0:T(8,128)(2,1)S(1)}, f32[4,256,256]{2,1,0:T(8,128...) custom-call(s32[2]{0:T(128)S(1)} %pad_add_fusion.place, f32[8,256]{1,0:T(8,128)S(1)} %get-tuple-element.145.scale_row, ...), custom_call_target="tpu_custom_call" | custom-call | flops 402653184 | bytes 6963208 | tf_op jit(solution)/shard_map/pallas_call | solution.py:34
  67.9 1.2 collective-permute-done.16
  69.1 1.5 %collective-permute-start.19 = (f32[2,4,256]{2,1,0:T(4,128)S(1)}, f32[2,4,256]{2,1,0:T(4,128)S(1)}, u32[]{:S(2)}, u32[]{:S(2)}) collective-permute-start(f32[2,4,256]{2,1,0:T(4,128)S(1)} %add.36.refs_0_), channel_id=1, source_target_pairs={{0,6},{2,4},{4,2},{6,0},{8,14},{10,12},{12,10},{14,8},{16,22},{18,... | collective-permute-start | bytes 24584 | tf_op jit(solution)/shard_map/ppermute | solution.py:378
  71.1 1.5 %collective-permute-start.17 = (f32[2,4,256]{2,1,0:T(4,128)S(1)}, f32[2,4,256]{2,1,0:T(4,128)S(1)}, u32[]{:S(2)}, u32[]{:S(2)}) collective-permute-start(f32[2,4,256]{2,1,0:T(4,128)S(1)} %add.36.refs_0_), channel_id=1, source_target_pairs={{0,2},{2,0},{4,6},{6,4},{8,10},{10,8},{12,14},{14,12},{16,18},{18,... | collective-permute-start | bytes 24584 | tf_op jit(solution)/shard_map/ppermute | solution.py:378
  72.6 1.1 collective-permute-done.19.refs_3_
  74.7 2.1 %shard_map.150 = (bf16[4,256,256]{2,1,0:T(8,128)(2,1)S(1)}, bf16[4,256,256]{2,1,0:T(8,128)(2,1)S(1)}, f32[1,3,64,256]{3,2,1,0:T(8,128)S(1)}, f32[1,3,64,256]{3,2...) custom-call(s32[2]{0:T(128)S(1)} %pad_add_fusion.place, ...), custom_call_target="tpu_custom_call" | custom-call | flops 805306368 | bytes 8036360 | tf_op jit(solution)/shard_map/pallas_call | solution.py:34
  76.9 0.8 collective-permute-start.20
  77.7 4.9 %collective-permute-done.20 = f32[1,3,64,256]{3,2,1,0:T(8,128)S(1)} collective-permute-done((f32[1,3,64,256]{3,2,1,0:T(8,128)S(1)}, f32[1,3,64,256]{3,2,1,0:T(8,128)S(1)}, u32[]{:S(2)}, u32[]{:S(2)}) %collective-permute-start.20) | collective-permute-done | bytes 196640 | tf_op jit(solution)/shard_map/ppermute | solution.py:378
  82.6 2.0 %collective-permute-start.22 = (f32[1,3,64,256]{3,2,1,0:T(8,128)S(1)}, f32[1,3,64,256]{3,2,1,0:T(8,128)S(1)}, u32[]{:S(2)}, u32[]{:S(2)}) collective-permute-start(f32[1,3,64,256]{3,2,1,0:T(8,128)S(1)} %add.38), channel_id=1, source_target_pairs={{0,16},{2,18},{4,20},{6,22},{8,24},{10,26},{12,28},{14,30},{16,0},... | collective-permute-start | bytes 589832 | tf_op jit(solution)/shard_map/ppermute | solution.py:378
  84.6 1.9 %collective-permute-start.21 = (f32[1,3,64,256]{3,2,1,0:T(8,128)S(1)}, f32[1,3,64,256]{3,2,1,0:T(8,128)S(1)}, u32[]{:S(2)}, u32[]{:S(2)}) collective-permute-start(f32[1,3,64,256]{3,2,1,0:T(8,128)S(1)} %get-tuple-element.188), channel_id=1, source_target_pairs={{0,8},{2,10},{4,12},{6,14},{8,0},{10,2},{12,4},{14,6},{16,24},{18,... | collective-permute-start | bytes 589832 | tf_op jit(solution)/shard_map/ppermute | solution.py:378
  86.5 5.9 %collective-permute-done.22 = f32[1,3,64,256]{3,2,1,0:T(8,128)S(1)} collective-permute-done((f32[1,3,64,256]{3,2,1,0:T(8,128)S(1)}, f32[1,3,64,256]{3,2,1,0:T(8,128)S(1)}, u32[]{:S(2)}, u32[]{:S(2)}) %collective-permute-start.22) | collective-permute-done | bytes 196640 | tf_op jit(solution)/shard_map/ppermute | solution.py:378
  93.7 1.0 collective-permute-start.26
  94.8 1.3 collective-permute-start.27
  96.1 1.2 collective-permute-start.28
  97.3 2.3 %collective-permute-start.23 = (f32[1,3,64,256]{3,2,1,0:T(8,128)S(1)}, f32[1,3,64,256]{3,2,1,0:T(8,128)S(1)}, u32[]{:S(2)}, u32[]{:S(2)}) collective-permute-start(f32[1,3,64,256]{3,2,1,0:T(8,128)S(1)} %add_add_fusion.refs_11_.refs_0_), channel_id=1, source_target_pairs={{0,8},{2,10},{4,12},{6,14},{8,0},{10,2},{12,4},{14,6},{16,24},{18,... | collective-permute-start | bytes 589832 | tf_op jit(solution)/shard_map/ppermute | solution.py:378
  99.6 3.2 %collective-permute-done.24.refs_13_ = f32[1,3,64,256]{3,2,1,0:T(8,128)S(1)} collective-permute-done((f32[1,3,64,256]{3,2,1,0:T(8,128)S(1)}, f32[1,3,64,256]{3,2,1,0:T(8,128)S(1)}, u32[]{:S(2)}, u32[]{:S(2)}) %collective-permute-start.24) | collective-permute-done | bytes 196640 | tf_op jit(solution)/shard_map/ppermute | solution.py:378
  102.8 1.1 shard_map.151
  103.9 1.3 collective-permute-done.27.refs_2_
  105.2 1.6 %collective-permute-done.28.refs_3_ = f32[256,256]{1,0:T(8,128)S(1)} collective-permute-done((f32[256,256]{1,0:T(8,128)S(1)}, f32[256,256]{1,0:T(8,128)S(1)}, u32[]{:S(2)}, u32[]{:S(2)}) %collective-permute-start.28) | collective-permute-done | bytes 262176 | tf_op jit(solution)/shard_map/ppermute | solution.py:378
  106.7 2.8 %collective-permute-done.25.refs_14_ = f32[1,3,64,256]{3,2,1,0:T(8,128)S(1)} collective-permute-done((f32[1,3,64,256]{3,2,1,0:T(8,128)S(1)}, f32[1,3,64,256]{3,2,1,0:T(8,128)S(1)}, u32[]{:S(2)}, u32[]{:S(2)}) %collective-permute-start.25) | collective-permute-done | bytes 196640 | tf_op jit(solution)/shard_map/ppermute | solution.py:378
  109.5 2.1 %shard_map.153 = (f32[3,256,256]{2,1,0:T(8,128)S(1)}, f32[3,256,256]{2,1,0:T(8,128)S(1)}, bf16[3,256,256]{2,1,0:T(8,128)(2,1)S(1)}, bf16[3,256,256]{2,1,0:T(8,12...) custom-call(s32[2]{0:T(128)S(1)} %pad_add_fusion.place, ...), custom_call_target="tpu_custom_call" | custom-call | flops 1207959552 | bytes 13631496 | tf_op jit(solution)/shard_map/pallas_call | solution.py:34
  111.6 1.9 %collective-permute-start.32 = (f32[3,256,256]{2,1,0:T(8,128)S(1)}, f32[3,256,256]{2,1,0:T(8,128)S(1)}, u32[]{:S(2)}, u32[]{:S(2)}) collective-permute-start(f32[3,256,256]{2,1,0:T(8,128)S(1)} %get-tuple-element.230), channel_id=1, source_target_pairs={{0,2},{2,0},{4,6},{6,4},{8,10},{10,8},{12,14},{14,12},{16,18},{18,... | collective-permute-start | bytes 2359304 | tf_op jit(solution)/shard_map/ppermute | solution.py:378
  113.7 1.7 %shard_map.154 = (f32[2,256,256]{2,1,0:T(8,128)S(1)}, f32[1,3,64,256]{3,2,1,0:T(8,128)S(1)}, f32[1,3,64,256]{3,2,1,0:T(8,128)S(1)}, f32[1,3,64,256]{3,2,1,0:T(8,128)S(1)}, f32[1,3,64,256]{3,2,1,0:T(8,128)S(1)}) custom-call(s32[2]{0:T(128)S(1)} %pad_add_fusion.place, bf16[4,256,256]{2,1,0:T(8,128)(2,1)S(1)} %get-tuple-element.183.k_kept.refs_0_, ...), custom_call_target="tpu_custom_call" | custom-call | flops 671088640 | bytes 12582920 | tf_op jit(solution)/shard_map/pallas_call | solution.py:34
  115.5 5.9 %collective-permute-done.29 = f32[1,3,64,256]{3,2,1,0:T(8,128)S(1)} collective-permute-done((f32[1,3,64,256]{3,2,1,0:T(8,128)S(1)}, f32[1,3,64,256]{3,2,1,0:T(8,128)S(1)}, u32[]{:S(2)}, u32[]{:S(2)}) %collective-permute-start.29) | collective-permute-done | bytes 196640 | tf_op jit(solution)/shard_map/ppermute | solution.py:378
  121.4 0.9 collective-permute-start.31
  122.3 1.7 %collective-permute-start.30 = (f32[1,3,64,256]{3,2,1,0:T(8,128)S(1)}, f32[1,3,64,256]{3,2,1,0:T(8,128)S(1)}, u32[]{:S(2)}, u32[]{:S(2)}) collective-permute-start(f32[1,3,64,256]{3,2,1,0:T(8,128)S(1)} %get-tuple-element.226), channel_id=1, source_target_pairs={{0,8},{2,10},{4,12},{6,14},{8,0},{10,2},{12,4},{14,6},{16,24},{18,... | collective-permute-start | bytes 589832 | tf_op jit(solution)/shard_map/ppermute | solution.py:378
  124.0 1.7 %shard_map.155 = bf16[256,4,256]{2,1,0:T(4,128)(2,1)} custom-call(s32[2]{0:T(128)S(1)} %pad_add_fusion.place, f32[256,256]{1,0:T(8,128)S(1)} %get-tuple-element.232.refs_0_, f32[256,256]{1,0:T(8,128)S(1)} %collective-permute-done.26.refs_1_, f32[256,256]{1,0:T(8,128)S(1)} %collective-permute-done.27.refs_2_, f32[256,256]{1,0:T(8,128)S(1)} %collective-permute-done.28.refs_3_), custom_call_target="tpu_custom_call" | custom-call | flops 8388608 | bytes 1572872 | tf_op jit(solution)/shard_map/pallas_call | solution.py:34
  125.8 5.8 %collective-permute-done.31.refs_3_ = f32[1,3,64,256]{3,2,1,0:T(8,128)S(1)} collective-permute-done((f32[1,3,64,256]{3,2,1,0:T(8,128)S(1)}, f32[1,3,64,256]{3,2,1,0:T(8,128)S(1)}, u32[]{:S(2)}, u32[]{:S(2)}) %collective-permute-start.31) | collective-permute-done | bytes 196640 | tf_op jit(solution)/shard_map/ppermute | solution.py:378
  131.7 1.4 collective-permute-start.38
  133.2 1.1 collective-permute-start.37
  135.3 1.2 collective-permute-start.35
  136.5 1.9 %collective-permute-start.36 = (f32[1,3,16,256]{3,2,1,0:T(8,128)S(1)}, f32[1,3,16,256]{3,2,1,0:T(8,128)S(1)}, u32[]{:S(2)}, u32[]{:S(2)}) collective-permute-start(f32[1,3,16,256]{3,2,1,0:T(8,128)S(1)} %get-tuple-element.243), channel_id=1, source_target_pairs={{0,6},{2,4},{4,2},{6,0},{8,14},{10,12},{12,10},{14,8},{16,22},{18,... | collective-permute-start | bytes 147464 | tf_op jit(solution)/shard_map/ppermute | solution.py:378
  138.4 1.9 %collective-permute-done.38.refs_4_ = f32[256,256]{1,0:T(8,128)S(1)} collective-permute-done((f32[256,256]{1,0:T(8,128)S(1)}, f32[256,256]{1,0:T(8,128)S(1)}, u32[]{:S(2)}, u32[]{:S(2)}) %collective-permute-start.38) | collective-permute-done | bytes 262176 | tf_op jit(solution)/shard_map/ppermute | solution.py:378
  140.4 1.5 %collective-permute-done.37.refs_3_ = f32[256,256]{1,0:T(8,128)S(1)} collective-permute-done((f32[256,256]{1,0:T(8,128)S(1)}, f32[256,256]{1,0:T(8,128)S(1)}, u32[]{:S(2)}, u32[]{:S(2)}) %collective-permute-start.37) | collective-permute-done | bytes 262176 | tf_op jit(solution)/shard_map/ppermute | solution.py:378
  141.8 2.4 %shard_map.157 = (bf16[256,4,256]{2,1,0:T(4,128)(2,1)}, bf16[256,4,256]{2,1,0:T(4,128)(2,1)}) custom-call(s32[2]{0:T(128)S(1)} %pad_add_fusion.place, f32[4,256]{1,0:T(4,128)S(1)} %bitcast.24, f32[2,256,256]{2,1,0:T(8,128)S(1)} %get-tuple-element.244.refs_0_, f32[3,256,256]{2,1,0:T(8,128)S(1)} %collective-permute-done.32.refs_1_, ...), custom_call_target="tpu_custom_call" | custom-call | flops 16777216 | bytes 3674120 | tf_op jit(solution)/shard_map/pallas_call | solution.py:34
  144.2 1.2 shard_map.158
  (60 shorter events, 7.4 us)
Async XLA Ops:
  0.6 15.3 %copy-start = (f32[4,256,256]{2,1,0:T(8,128)S(1)}, f32[4,256,256]{2,1,0:T(8,128)}, u32[]{:S(2)}) copy-start(f32[4,256,256]{2,1,0:T(8,128)} %param.16) | copy-start | bytes 3145732
  0.7 1.1 copy-start.5
  1.8 5.5 %copy-start.6 = (bf16[1,256,4,256]{3,2,1,0:T(4,128)(2,1)S(1)}, bf16[1,256,4,256]{3,2,1,0:T(4,128)(2,1)}, u32[]{:S(2)}) copy-start(bf16[1,256,4,256]{3,2,1,0:T(4,128)(2,1)} %param.12) | copy-start | bytes 1572868
  2.7 10.5 %collective-permute-start = (f32[256,256]{1,0:T(8,128)S(1)}, f32[256,256]{1,0:T(8,128)S(1)}, u32[]{:S(2)}, u32[]{:S(2)}) collective-permute-start(f32[256,256]{1,0:T(8,128)S(1)} %get-tuple-element.134), channel_id=1, source_target_pairs={{0,2},{2,0},{4,6},{6,4},{8,10},{10,8},{12,14},{14,12},{16,18},{18,... | collective-permute-start | bytes 786440 | tf_op jit(solution)/shard_map/ppermute | solution.py:378
  5.7 1.6 %copy-start.4 = (f32[1,4,256]{2,1,0:T(4,128)S(1)}, f32[1,4,256]{2,1,0:T(4,128)}, u32[]{:S(2)}) copy-start(f32[1,4,256]{2,1,0:T(4,128)} %param.13) | copy-start | bytes 12292
  5.8 14.0 %collective-permute-start.1 = (f32[256,256]{1,0:T(8,128)S(1)}, f32[256,256]{1,0:T(8,128)S(1)}, u32[]{:S(2)}, u32[]{:S(2)}) collective-permute-start(f32[256,256]{1,0:T(8,128)S(1)} %get-tuple-element.135), channel_id=1, source_target_pairs={{0,4},{2,6},{4,0},{6,2},{8,12},{10,14},{12,8},{14,10},{16,20},{18,... | collective-permute-start | bytes 786440 | tf_op jit(solution)/shard_map/ppermute | solution.py:378
  7.3 12.8 %collective-permute-start.2 = (f32[256,256]{1,0:T(8,128)S(1)}, f32[256,256]{1,0:T(8,128)S(1)}, u32[]{:S(2)}, u32[]{:S(2)}) collective-permute-start(f32[256,256]{1,0:T(8,128)S(1)} %get-tuple-element.136), channel_id=1, source_target_pairs={{0,6},{2,4},{4,2},{6,0},{8,14},{10,12},{12,10},{14,8},{16,22},{18,... | collective-permute-start | bytes 786440 | tf_op jit(solution)/shard_map/ppermute | solution.py:378
  9.1 0.7 copy-start.7
  9.8 14.4 %collective-permute-start.3 = (f32[256,256]{1,0:T(8,128)}, f32[256,256]{1,0:T(8,128)S(1)}, u32[]{:S(2)}, u32[]{:S(2)}) collective-permute-start(f32[256,256]{1,0:T(8,128)} %get-tuple-element.140), channel_id=1, source_target_pairs={{0,2},{2,0},{4,6},{6,4},{8,10},{10,8},{12,14},{14,12},{16,18},{18,... | collective-permute-start | bytes 786440 | tf_op jit(solution)/shard_map/ppermute | solution.py:378
  11.7 18.7 %collective-permute-start.4 = (f32[256,256]{1,0:T(8,128)}, f32[256,256]{1,0:T(8,128)S(1)}, u32[]{:S(2)}, u32[]{:S(2)}) collective-permute-start(f32[256,256]{1,0:T(8,128)} %get-tuple-element.141), channel_id=1, source_target_pairs={{0,4},{2,6},{4,0},{6,2},{8,12},{10,14},{12,8},{14,10},{16,20},{18,... | collective-permute-start | bytes 786440 | tf_op jit(solution)/shard_map/ppermute | solution.py:378
  13.2 17.1 %collective-permute-start.5 = (f32[256,256]{1,0:T(8,128)S(1)}, f32[256,256]{1,0:T(8,128)S(1)}, u32[]{:S(2)}, u32[]{:S(2)}) collective-permute-start(f32[256,256]{1,0:T(8,128)S(1)} %get-tuple-element.142), channel_id=1, source_target_pairs={{0,6},{2,4},{4,2},{6,0},{8,14},{10,12},{12,10},{14,8},{16,22},{18,... | collective-permute-start | bytes 786440 | tf_op jit(solution)/shard_map/ppermute | solution.py:378
  15.9 14.5 %copy-start.8 = (bf16[256,256]{1,0:T(8,128)(2,1)S(1)}, bf16[256,256]{1,0:T(8,128)(2,1)}, u32[]{:S(2)}) copy-start(bf16[256,256]{1,0:T(8,128)(2,1)} %copy-done.7) | copy-start | bytes 393220
  30.4 4.2 %copy-start.1 = (bf16[1,256,4,256]{3,2,1,0:T(4,128)(2,1)S(1)}, bf16[1,256,4,256]{3,2,1,0:T(4,128)(2,1)}, u32[]{:S(2)}) copy-start(bf16[1,256,4,256]{3,2,1,0:T(4,128)(2,1)} %param.10) | copy-start | bytes 1572868
  30.4 4.2 %copy-start.2 = (bf16[1,256,4,256]{3,2,1,0:T(4,128)(2,1)S(1)}, bf16[1,256,4,256]{3,2,1,0:T(4,128)(2,1)}, u32[]{:S(2)}) copy-start(bf16[1,256,4,256]{3,2,1,0:T(4,128)(2,1)} %param.19) | copy-start | bytes 1572868
  32.4 1.7 %copy-start.9 = (f32[4]{0:T(128)S(1)}, f32[4]{0:T(128)}, u32[]{:S(2)}) copy-start(f32[4]{0:T(128)} %param.14) | copy-start | bytes 52
  32.4 2.2 %copy-start.3 = (f32[4,256]{1,0:T(4,128)S(1)}, f32[4,256]{1,0:T(4,128)}, u32[]{:S(2)}) copy-start(f32[4,256]{1,0:T(4,128)} %gain.1) | copy-start | bytes 12292
  32.4 6.3 %collective-permute-start.6 = (f32[1,3,64,256]{3,2,1,0:T(8,128)S(1)}, f32[1,3,64,256]{3,2,1,0:T(8,128)S(1)}, u32[]{:S(2)}, u32[]{:S(2)}) collective-permute-start(f32[1,3,64,256]{3,2,1,0:T(8,128)S(1)} %get-tuple-element.155), channel_id=1, source_target_pairs={{0,8},{2,10},{4,12},{6,14},{8,0},{10,2},{12,4},{14,6},{16,24},{18,... | collective-permute-start | bytes 589832 | tf_op jit(solution)/shard_map/ppermute | solution.py:378
  36.6 13.1 %collective-permute-start.9 = (f32[2,256,256]{2,1,0:T(8,128)S(1)}, f32[2,256,256]{2,1,0:T(8,128)S(1)}, u32[]{:S(2)}, u32[]{:S(2)}) collective-permute-start(f32[2,256,256]{2,1,0:T(8,128)S(1)} %get-tuple-element.161), channel_id=1, source_target_pairs={{0,2},{2,0},{4,6},{6,4},{8,10},{10,8},{12,14},{14,12},{16,18},{18,... | collective-permute-start | bytes 1572872 | tf_op jit(solution)/shard_map/ppermute | solution.py:378
  37.9 12.2 %collective-permute-start.10 = (f32[2,256,256]{2,1,0:T(8,128)S(1)}, f32[2,256,256]{2,1,0:T(8,128)S(1)}, u32[]{:S(2)}, u32[]{:S(2)}) collective-permute-start(f32[2,256,256]{2,1,0:T(8,128)S(1)} %get-tuple-element.162), channel_id=1, source_target_pairs={{0,4},{2,6},{4,0},{6,2},{8,12},{10,14},{12,8},{14,10},{16,20},{18,... | collective-permute-start | bytes 1572872 | tf_op jit(solution)/shard_map/ppermute | solution.py:378
  38.7 10.0 %collective-permute-start.8 = (f32[1,3,64,256]{3,2,1,0:T(8,128)S(1)}, f32[1,3,64,256]{3,2,1,0:T(8,128)S(1)}, u32[]{:S(2)}, u32[]{:S(2)}) collective-permute-start(f32[1,3,64,256]{3,2,1,0:T(8,128)S(1)} %add.34), channel_id=1, source_target_pairs={{0,16},{2,18},{4,20},{6,22},{8,24},{10,26},{12,28},{14,30},{16,0},... | collective-permute-start | bytes 589832 | tf_op jit(solution)/shard_map/ppermute | solution.py:378
  41.4 8.2 %collective-permute-start.7 = (f32[1,3,64,256]{3,2,1,0:T(8,128)S(1)}, f32[1,3,64,256]{3,2,1,0:T(8,128)S(1)}, u32[]{:S(2)}, u32[]{:S(2)}) collective-permute-start(f32[1,3,64,256]{3,2,1,0:T(8,128)S(1)} %get-tuple-element.157), channel_id=1, source_target_pairs={{0,8},{2,10},{4,12},{6,14},{8,0},{10,2},{12,4},{14,6},{16,24},{18,... | collective-permute-start | bytes 589832 | tf_op jit(solution)/shard_map/ppermute | solution.py:378
  50.1 9.7 %collective-permute-start.14 = (f32[1,3,64,256]{3,2,1,0:T(8,128)S(1)}, f32[1,3,64,256]{3,2,1,0:T(8,128)S(1)}, u32[]{:S(2)}, u32[]{:S(2)}) collective-permute-start(f32[1,3,64,256]{3,2,1,0:T(8,128)S(1)} %add_add_fusion.1.refs_5_), channel_id=1, source_target_pairs={{0,16},{2,18},{4,20},{6,22},{8,24},{10,26},{12,28},{14,30},{16,0},... | collective-permute-start | bytes 589832 | tf_op jit(solution)/shard_map/ppermute | solution.py:378
  52.7 10.3 %collective-permute-start.11 = (f32[256,256]{1,0:T(8,128)S(1)}, f32[256,256]{1,0:T(8,128)S(1)}, u32[]{:S(2)}, u32[]{:S(2)}) collective-permute-start(f32[256,256]{1,0:T(8,128)S(1)} %get-tuple-element.168), channel_id=1, source_target_pairs={{0,6},{2,4},{4,2},{6,0},{8,14},{10,12},{12,10},{14,8},{16,22},{18,... | collective-permute-start | bytes 786440 | tf_op jit(solution)/shard_map/ppermute | solution.py:378
  53.2 11.4 %collective-permute-start.12 = (f32[256,256]{1,0:T(8,128)S(1)}, f32[256,256]{1,0:T(8,128)S(1)}, u32[]{:S(2)}, u32[]{:S(2)}) collective-permute-start(f32[256,256]{1,0:T(8,128)S(1)} %get-tuple-element.169), channel_id=1, source_target_pairs={{0,6},{2,4},{4,2},{6,0},{8,14},{10,12},{12,10},{14,8},{16,22},{18,... | collective-permute-start | bytes 786440 | tf_op jit(solution)/shard_map/ppermute | solution.py:378
  55.6 7.4 %collective-permute-start.13 = (f32[1,3,64,256]{3,2,1,0:T(8,128)S(1)}, f32[1,3,64,256]{3,2,1,0:T(8,128)S(1)}, u32[]{:S(2)}, u32[]{:S(2)}) collective-permute-start(f32[1,3,64,256]{3,2,1,0:T(8,128)S(1)} %add_add_fusion.1.refs_5_), channel_id=1, source_target_pairs={{0,8},{2,10},{4,12},{6,14},{8,0},{10,2},{12,4},{14,6},{16,24},{18,... | collective-permute-start | bytes 589832 | tf_op jit(solution)/shard_map/ppermute | solution.py:378
  59.8 6.3 %collective-permute-start.15 = (f32[1,3,64,256]{3,2,1,0:T(8,128)S(1)}, f32[1,3,64,256]{3,2,1,0:T(8,128)S(1)}, u32[]{:S(2)}, u32[]{:S(2)}) collective-permute-start(f32[1,3,64,256]{3,2,1,0:T(8,128)S(1)} %collective-permute-done.14.refs_7_), channel_id=1, source_target_pairs={{0,8},{2,10},{4,12},{6,14},{8,0},{10,2},{12,4},{14,6},{16,24},{18,... | collective-permute-start | bytes 589832 | tf_op jit(solution)/shard_map/ppermute | solution.py:378
  67.8 1.2 collective-permute-start.16
  69.1 4.5 %collective-permute-start.19 = (f32[2,4,256]{2,1,0:T(4,128)S(1)}, f32[2,4,256]{2,1,0:T(4,128)S(1)}, u32[]{:S(2)}, u32[]{:S(2)}) collective-permute-start(f32[2,4,256]{2,1,0:T(4,128)S(1)} %add.36.refs_0_), channel_id=1, source_target_pairs={{0,6},{2,4},{4,2},{6,0},{8,14},{10,12},{12,10},{14,8},{16,22},{18,... | collective-permute-start | bytes 24584 | tf_op jit(solution)/shard_map/ppermute | solution.py:378
  70.6 3.7 %collective-permute-start.18 = (f32[2,4,256]{2,1,0:T(4,128)S(1)}, f32[2,4,256]{2,1,0:T(4,128)S(1)}, u32[]{:S(2)}, u32[]{:S(2)}) collective-permute-start(f32[2,4,256]{2,1,0:T(4,128)S(1)} %add.36.refs_0_), channel_id=1, source_target_pairs={{0,4},{2,6},{4,0},{6,2},{8,12},{10,14},{12,8},{14,10},{16,20},{18,... | collective-permute-start | bytes 24584 | tf_op jit(solution)/shard_map/ppermute | solution.py:378
  71.1 3.7 %collective-permute-start.17 = (f32[2,4,256]{2,1,0:T(4,128)S(1)}, f32[2,4,256]{2,1,0:T(4,128)S(1)}, u32[]{:S(2)}, u32[]{:S(2)}) collective-permute-start(f32[2,4,256]{2,1,0:T(4,128)S(1)} %add.36.refs_0_), channel_id=1, source_target_pairs={{0,2},{2,0},{4,6},{6,4},{8,10},{10,8},{12,14},{14,12},{16,18},{18,... | collective-permute-start | bytes 24584 | tf_op jit(solution)/shard_map/ppermute | solution.py:378
  76.9 5.7 %collective-permute-start.20 = (f32[1,3,64,256]{3,2,1,0:T(8,128)S(1)}, f32[1,3,64,256]{3,2,1,0:T(8,128)S(1)}, u32[]{:S(2)}, u32[]{:S(2)}) collective-permute-start(f32[1,3,64,256]{3,2,1,0:T(8,128)S(1)} %get-tuple-element.186), channel_id=1, source_target_pairs={{0,8},{2,10},{4,12},{6,14},{8,0},{10,2},{12,4},{14,6},{16,24},{18,... | collective-permute-start | bytes 589832 | tf_op jit(solution)/shard_map/ppermute | solution.py:378
  82.6 9.7 %collective-permute-start.22 = (f32[1,3,64,256]{3,2,1,0:T(8,128)S(1)}, f32[1,3,64,256]{3,2,1,0:T(8,128)S(1)}, u32[]{:S(2)}, u32[]{:S(2)}) collective-permute-start(f32[1,3,64,256]{3,2,1,0:T(8,128)S(1)} %add.38), channel_id=1, source_target_pairs={{0,16},{2,18},{4,20},{6,22},{8,24},{10,26},{12,28},{14,30},{16,0},... | collective-permute-start | bytes 589832 | tf_op jit(solution)/shard_map/ppermute | solution.py:378
  84.6 8.0 %collective-permute-start.21 = (f32[1,3,64,256]{3,2,1,0:T(8,128)S(1)}, f32[1,3,64,256]{3,2,1,0:T(8,128)S(1)}, u32[]{:S(2)}, u32[]{:S(2)}) collective-permute-start(f32[1,3,64,256]{3,2,1,0:T(8,128)S(1)} %get-tuple-element.188), channel_id=1, source_target_pairs={{0,8},{2,10},{4,12},{6,14},{8,0},{10,2},{12,4},{14,6},{16,24},{18,... | collective-permute-start | bytes 589832 | tf_op jit(solution)/shard_map/ppermute | solution.py:378
  92.6 10.1 %collective-permute-start.24 = (f32[1,3,64,256]{3,2,1,0:T(8,128)S(1)}, f32[1,3,64,256]{3,2,1,0:T(8,128)S(1)}, u32[]{:S(2)}, u32[]{:S(2)}) collective-permute-start(f32[1,3,64,256]{3,2,1,0:T(8,128)S(1)} %add_add_fusion.refs_11_.refs_0_), channel_id=1, source_target_pairs={{0,16},{2,18},{4,20},{6,22},{8,24},{10,26},{12,28},{14,30},{16,0},... | collective-permute-start | bytes 589832 | tf_op jit(solution)/shard_map/ppermute | solution.py:378
  93.7 10.1 %collective-permute-start.26 = (f32[256,256]{1,0:T(8,128)S(1)}, f32[256,256]{1,0:T(8,128)S(1)}, u32[]{:S(2)}, u32[]{:S(2)}) collective-permute-start(f32[256,256]{1,0:T(8,128)S(1)} %get-tuple-element.203), channel_id=1, source_target_pairs={{0,2},{2,0},{4,6},{6,4},{8,10},{10,8},{12,14},{14,12},{16,18},{18,... | collective-permute-start | bytes 786440 | tf_op jit(solution)/shard_map/ppermute | solution.py:378
  94.8 10.4 %collective-permute-start.27 = (f32[256,256]{1,0:T(8,128)S(1)}, f32[256,256]{1,0:T(8,128)S(1)}, u32[]{:S(2)}, u32[]{:S(2)}) collective-permute-start(f32[256,256]{1,0:T(8,128)S(1)} %get-tuple-element.204), channel_id=1, source_target_pairs={{0,4},{2,6},{4,0},{6,2},{8,12},{10,14},{12,8},{14,10},{16,20},{18,... | collective-permute-start | bytes 786440 | tf_op jit(solution)/shard_map/ppermute | solution.py:378
  96.1 10.6 %collective-permute-start.28 = (f32[256,256]{1,0:T(8,128)S(1)}, f32[256,256]{1,0:T(8,128)S(1)}, u32[]{:S(2)}, u32[]{:S(2)}) collective-permute-start(f32[256,256]{1,0:T(8,128)S(1)} %get-tuple-element.205), channel_id=1, source_target_pairs={{0,6},{2,4},{4,2},{6,0},{8,14},{10,12},{12,10},{14,8},{16,22},{18,... | collective-permute-start | bytes 786440 | tf_op jit(solution)/shard_map/ppermute | solution.py:378
  97.3 9.4 %collective-permute-start.23 = (f32[1,3,64,256]{3,2,1,0:T(8,128)S(1)}, f32[1,3,64,256]{3,2,1,0:T(8,128)S(1)}, u32[]{:S(2)}, u32[]{:S(2)}) collective-permute-start(f32[1,3,64,256]{3,2,1,0:T(8,128)S(1)} %add_add_fusion.refs_11_.refs_0_), channel_id=1, source_target_pairs={{0,8},{2,10},{4,12},{6,14},{8,0},{10,2},{12,4},{14,6},{16,24},{18,... | collective-permute-start | bytes 589832 | tf_op jit(solution)/shard_map/ppermute | solution.py:378
  102.8 6.8 %collective-permute-start.25 = (f32[1,3,64,256]{3,2,1,0:T(8,128)S(1)}, f32[1,3,64,256]{3,2,1,0:T(8,128)S(1)}, u32[]{:S(2)}, u32[]{:S(2)}) collective-permute-start(f32[1,3,64,256]{3,2,1,0:T(8,128)S(1)} %collective-permute-done.24.refs_13_), channel_id=1, source_target_pairs={{0,8},{2,10},{4,12},{6,14},{8,0},{10,2},{12,4},{14,6},{16,24},{18,... | collective-permute-start | bytes 589832 | tf_op jit(solution)/shard_map/ppermute | solution.py:378
  111.6 20.0 %collective-permute-start.32 = (f32[3,256,256]{2,1,0:T(8,128)S(1)}, f32[3,256,256]{2,1,0:T(8,128)S(1)}, u32[]{:S(2)}, u32[]{:S(2)}) collective-permute-start(f32[3,256,256]{2,1,0:T(8,128)S(1)} %get-tuple-element.230), channel_id=1, source_target_pairs={{0,2},{2,0},{4,6},{6,4},{8,10},{10,8},{12,14},{14,12},{16,18},{18,... | collective-permute-start | bytes 2359304 | tf_op jit(solution)/shard_map/ppermute | solution.py:378
  113.5 18.2 %collective-permute-start.33 = (f32[3,256,256]{2,1,0:T(8,128)S(1)}, f32[3,256,256]{2,1,0:T(8,128)S(1)}, u32[]{:S(2)}, u32[]{:S(2)}) collective-permute-start(f32[3,256,256]{2,1,0:T(8,128)S(1)} %get-tuple-element.231), channel_id=1, source_target_pairs={{0,4},{2,6},{4,0},{6,2},{8,12},{10,14},{12,8},{14,10},{16,20},{18,... | collective-permute-start | bytes 2359304 | tf_op jit(solution)/shard_map/ppermute | solution.py:378
  115.5 5.9 %collective-permute-start.29 = (f32[1,3,64,256]{3,2,1,0:T(8,128)S(1)}, f32[1,3,64,256]{3,2,1,0:T(8,128)S(1)}, u32[]{:S(2)}, u32[]{:S(2)}) collective-permute-start(f32[1,3,64,256]{3,2,1,0:T(8,128)S(1)} %get-tuple-element.224), channel_id=1, source_target_pairs={{0,8},{2,10},{4,12},{6,14},{8,0},{10,2},{12,4},{14,6},{16,24},{18,... | collective-permute-start | bytes 589832 | tf_op jit(solution)/shard_map/ppermute | solution.py:378
  121.4 10.2 %collective-permute-start.31 = (f32[1,3,64,256]{3,2,1,0:T(8,128)S(1)}, f32[1,3,64,256]{3,2,1,0:T(8,128)S(1)}, u32[]{:S(2)}, u32[]{:S(2)}) collective-permute-start(f32[1,3,64,256]{3,2,1,0:T(8,128)S(1)} %add.40), channel_id=1, source_target_pairs={{0,16},{2,18},{4,20},{6,22},{8,24},{10,26},{12,28},{14,30},{16,0},... | collective-permute-start | bytes 589832 | tf_op jit(solution)/shard_map/ppermute | solution.py:378
  122.3 9.3 %collective-permute-start.30 = (f32[1,3,64,256]{3,2,1,0:T(8,128)S(1)}, f32[1,3,64,256]{3,2,1,0:T(8,128)S(1)}, u32[]{:S(2)}, u32[]{:S(2)}) collective-permute-start(f32[1,3,64,256]{3,2,1,0:T(8,128)S(1)} %get-tuple-element.226), channel_id=1, source_target_pairs={{0,8},{2,10},{4,12},{6,14},{8,0},{10,2},{12,4},{14,6},{16,24},{18,... | collective-permute-start | bytes 589832 | tf_op jit(solution)/shard_map/ppermute | solution.py:378
  131.7 8.6 %collective-permute-start.38 = (f32[256,256]{1,0:T(8,128)S(1)}, f32[256,256]{1,0:T(8,128)S(1)}, u32[]{:S(2)}, u32[]{:S(2)}) collective-permute-start(f32[256,256]{1,0:T(8,128)S(1)} %slice_bitcast_fusion), channel_id=1, source_target_pairs={{0,2},{2,0},{4,6},{6,4},{8,10},{10,8},{12,14},{14,12},{16,18},{18,... | collective-permute-start | bytes 786440 | tf_op jit(solution)/shard_map/ppermute | solution.py:378
  133.2 8.7 %collective-permute-start.37 = (f32[256,256]{1,0:T(8,128)S(1)}, f32[256,256]{1,0:T(8,128)S(1)}, u32[]{:S(2)}, u32[]{:S(2)}) collective-permute-start(f32[256,256]{1,0:T(8,128)S(1)} %slice_bitcast_fusion.1), channel_id=1, source_target_pairs={{0,4},{2,6},{4,0},{6,2},{8,12},{10,14},{12,8},{14,10},{16,20},{18,... | collective-permute-start | bytes 786440 | tf_op jit(solution)/shard_map/ppermute | solution.py:378
  134.9 9.3 %collective-permute-start.34 = (f32[1,3,16,256]{3,2,1,0:T(8,128)S(1)}, f32[1,3,16,256]{3,2,1,0:T(8,128)S(1)}, u32[]{:S(2)}, u32[]{:S(2)}) collective-permute-start(f32[1,3,16,256]{3,2,1,0:T(8,128)S(1)} %get-tuple-element.241), channel_id=1, source_target_pairs={{0,2},{2,0},{4,6},{6,4},{8,10},{10,8},{12,14},{14,12},{16,18},{18,... | collective-permute-start | bytes 147464 | tf_op jit(solution)/shard_map/ppermute | solution.py:378
  135.3 8.9 %collective-permute-start.35 = (f32[1,3,16,256]{3,2,1,0:T(8,128)S(1)}, f32[1,3,16,256]{3,2,1,0:T(8,128)S(1)}, u32[]{:S(2)}, u32[]{:S(2)}) collective-permute-start(f32[1,3,16,256]{3,2,1,0:T(8,128)S(1)} %get-tuple-element.242), channel_id=1, source_target_pairs={{0,4},{2,6},{4,0},{6,2},{8,12},{10,14},{12,8},{14,10},{16,20},{18,... | collective-permute-start | bytes 147464 | tf_op jit(solution)/shard_map/ppermute | solution.py:378
  136.5 7.7 %collective-permute-start.36 = (f32[1,3,16,256]{3,2,1,0:T(8,128)S(1)}, f32[1,3,16,256]{3,2,1,0:T(8,128)S(1)}, u32[]{:S(2)}, u32[]{:S(2)}) collective-permute-start(f32[1,3,16,256]{3,2,1,0:T(8,128)S(1)} %get-tuple-element.243), channel_id=1, source_target_pairs={{0,6},{2,4},{4,2},{6,0},{8,14},{10,12},{12,10},{14,8},{16,22},{18,... | collective-permute-start | bytes 147464 | tf_op jit(solution)/shard_map/ppermute | solution.py:378

commit v18 on v16

--- a/solution.py
+++ b/solution.py
@@ -170,7 +170,7 @@
 
 
 def query_refs(groups, refs):
-    return [(ref.at[0], ref.at[1]) for ref in refs[: groups - 1]] + [refs[groups - 1 : groups + 1]]
+    return [(ref.at[0], ref.at[1]) for ref in refs[:groups]]
 
 
 def tokens_of(ref):
@@ -178,7 +178,7 @@
 
 
 def apply_kernel(groups, depth, place, scale_row, *refs):
-    pieces, refs = query_refs(groups, refs), refs[groups + 1 :]
+    pieces, refs = query_refs(groups, refs), refs[groups:]
     parts = refs[:depth]
     activ_ref, slope_ref, hidden_ref, os_ref, new_b, stats, whole = refs[depth:]
     assemble(place, parts, whole)
@@ -207,7 +207,7 @@
 
 def apply_back_kernel(groups, depth, count, place, scale_row, *refs):
     stats, refs = refs[:groups], refs[groups:]
-    pieces, refs = query_refs(groups, refs), refs[groups + 1 :]
+    pieces, refs = query_refs(groups, refs), refs[groups:]
     activ_ref, slope_ref, hidden_ref, os_ref, new_b = refs[:5]
     dfirst_ref, dthird_ref, slices, sums, both = refs[5], refs[6], refs[7:-2], refs[-2], refs[-1]
     both[...] = functools.reduce(jnp.add, [ref[...] for ref in stats])
@@ -416,13 +416,13 @@
     early, terms = out[:2], out[2:]
     *q_out, scale_row = call(
         functools.partial(split_apply_kernel, groups),
-        [shape(2, tokens, width)] * (groups - 1) + [shape(tokens, width)] * 2 + [shape(8, width)],
+        [shape(2, tokens, width)] * groups + [shape(8, width)],
         [scratch], flops // 8, place, queries[0], cotangent[0], gain, own_scale,
     )
-    q_in = in_plane(q_out[:-2])
+    q_in = in_plane(q_out[:-1])
     new = functools.reduce(jnp.add, scatter(terms, depth, groups))
-    new, q_in, q_last = after(new, q_in, q_out[-2:])
-    q_in += [move(x, "ctx", groups - 1) for x in q_last]
+    new, q_in, q_last = after(new, q_in, q_out[-1])
+    q_in.append(move(q_last, "ctx", groups - 1))
     new = gather(new, depth, groups)
     *passed, stats = call(
         functools.partial(apply_kernel, groups, depth),

time: 144 us -> 145 us (level)
    ppermute x39 -> x38, starting transfers between devices: 46.6 us -> 47.8 us  [move(): lax.ppermute(x, axis, [(c, c ^ step) for c in range(lax.axis_size(axis))])]
    ppermute x39 -> x38, waiting for transfers between devices: 70.9 us -> 71.1 us  [move(): lax.ppermute(x, axis, [(c, c ^ step) for c in range(lax.axis_size(axis))])]
  transfers between devices with their start and end apart: 39 -> 38, of which waited for: 25 -> 24; matrix products, arithmetic and copies ran while one was open for 1% -> 1% of each run, Pallas kernels for 7% -> 7%
where the time goes in v18:
time: 145 us
  waiting for transfers between devices  71.1 us (49%)
  starting transfers between devices  47.8 us (33%)
  Pallas kernels  21.1 us (15%)
  local copies, waits for them, and re-layouts  4.17 us (3%)
    ppermute x38, waiting for transfers between devices, move(): lax.ppermute(x, axis, [(c, c ^ step) for c in range(lax.axis_size(axis))])  71.1 us
    ppermute x38, starting transfers between devices, move(): lax.ppermute(x, axis, [(c, c ^ step) for c in range(lax.axis_size(axis))])  47.8 us
    pallas_call x13, Pallas kernels, call(): pl.pallas_call(body, out_shape=out_shape, in_specs=[smem if a.dtype == jn...  21.1 us
  transfers between devices with their start and end apart: 38, of which 24 were waited for; matrix products, arithmetic and copies ran while one was open for 1% of the time, Pallas kernels for 7%

profile of v18, /device:TPU:0, one launch (start us, length us, event | category | flops | bytes accessed | tf_op | source)
XLA Modules:
  0.0 145.2 jit_solution(11039891094214994799)
XLA Ops:
  0.7 0.7 copy-done.4
  1.4 1.0 copy-done.5
  2.5 1.1 shard_map.146
  3.6 3.0 %collective-permute-start.3 = (f32[256,256]{1,0:T(8,128)S(1)}, f32[256,256]{1,0:T(8,128)S(1)}, u32[]{:S(2)}, u32[]{:S(2)}) collective-permute-start(f32[256,256]{1,0:T(8,128)S(1)} %get-tuple-element.128), channel_id=1, source_target_pairs={{0,2},{2,0},{4,6},{6,4},{8,10},{10,8},{12,14},{14,12},{16,18},{18,... | collective-permute-start | bytes 786440 | tf_op jit(solution)/shard_map/ppermute | solution.py:358
  6.6 1.5 %collective-permute-start.4 = (f32[256,256]{1,0:T(8,128)S(1)}, f32[256,256]{1,0:T(8,128)S(1)}, u32[]{:S(2)}, u32[]{:S(2)}) collective-permute-start(f32[256,256]{1,0:T(8,128)S(1)} %get-tuple-element.129), channel_id=1, source_target_pairs={{0,4},{2,6},{4,0},{6,2},{8,12},{10,14},{12,8},{14,10},{16,20},{18,... | collective-permute-start | bytes 786440 | tf_op jit(solution)/shard_map/ppermute | solution.py:358
  8.1 1.7 %shard_map.145 = (bf16[256,256]{1,0:T(8,128)(2,1)S(1)}, f32[256,256]{1,0:T(8,128)}, f32[256,256]{1,0:T(8,128)}, f32[256,256]{1,0:T(8,128)S(1)}) custom-call(s32[2]{0:T(128)S(1)} %pad_add_fusion.place, bf16[256,4,256]{2,1,0:T(4,128)(2,1)S(1)} %bitcast.26), custom_call_target="tpu_custom_call" | custom-call | flops 2147483648 | bytes 1441800 | tf_op jit(solution)/shard_map/pallas_call | solution.py:34
  9.8 0.7 copy-done.7
  10.4 1.9 %collective-permute-start = (f32[256,256]{1,0:T(8,128)}, f32[256,256]{1,0:T(8,128)S(1)}, u32[]{:S(2)}, u32[]{:S(2)}) collective-permute-start(f32[256,256]{1,0:T(8,128)} %get-tuple-element.124), channel_id=1, source_target_pairs={{0,2},{2,0},{4,6},{6,4},{8,10},{10,8},{12,14},{14,12},{16,18},{18,... | collective-permute-start | bytes 786440 | tf_op jit(solution)/shard_map/ppermute | solution.py:358
  12.4 1.5 %collective-permute-start.1 = (f32[256,256]{1,0:T(8,128)}, f32[256,256]{1,0:T(8,128)S(1)}, u32[]{:S(2)}, u32[]{:S(2)}) collective-permute-start(f32[256,256]{1,0:T(8,128)} %get-tuple-element.125), channel_id=1, source_target_pairs={{0,4},{2,6},{4,0},{6,2},{8,12},{10,14},{12,8},{14,10},{16,20},{18,... | collective-permute-start | bytes 786440 | tf_op jit(solution)/shard_map/ppermute | solution.py:358
  13.9 2.8 %collective-permute-start.2 = (f32[256,256]{1,0:T(8,128)S(1)}, f32[256,256]{1,0:T(8,128)S(1)}, u32[]{:S(2)}, u32[]{:S(2)}) collective-permute-start(f32[256,256]{1,0:T(8,128)S(1)} %get-tuple-element.126), channel_id=1, source_target_pairs={{0,6},{2,4},{4,2},{6,0},{8,14},{10,12},{12,10},{14,8},{16,22},{18,... | collective-permute-start | bytes 786440 | tf_op jit(solution)/shard_map/ppermute | solution.py:358
  16.7 1.1 dynamic-slice_bitcast_fusion
  17.9 2.8 %collective-permute-done.4.refs_6_ = f32[256,256]{1,0:T(8,128)S(1)} collective-permute-done((f32[256,256]{1,0:T(8,128)S(1)}, f32[256,256]{1,0:T(8,128)S(1)}, u32[]{:S(2)}, u32[]{:S(2)}) %collective-permute-start.4) | collective-permute-done | bytes 262176 | tf_op jit(solution)/shard_map/ppermute | solution.py:358
  20.9 4.1 %collective-permute-done.refs_1_ = f32[256,256]{1,0:T(8,128)S(1)} collective-permute-done((f32[256,256]{1,0:T(8,128)}, f32[256,256]{1,0:T(8,128)S(1)}, u32[]{:S(2)}, u32[]{:S(2)}) %collective-permute-start) | collective-permute-done | bytes 262176 | tf_op jit(solution)/shard_map/ppermute | solution.py:358
  25.0 6.2 %collective-permute-done.1.refs_2_ = f32[256,256]{1,0:T(8,128)S(1)} collective-permute-done((f32[256,256]{1,0:T(8,128)}, f32[256,256]{1,0:T(8,128)S(1)}, u32[]{:S(2)}, u32[]{:S(2)}) %collective-permute-start.1) | collective-permute-done | bytes 262176 | tf_op jit(solution)/shard_map/ppermute | solution.py:358
  31.2 2.0 %shard_map.148 = (bf16[4,256,256]{2,1,0:T(8,128)(2,1)S(1)}, bf16[4,256,256]{2,1,0:T(8,128)(2,1)S(1)}, f32[1,3,64,256]{3,2,1,0:T(8,128)S(1)}, f32[1,3,64,256]{3,2...) custom-call(s32[2]{0:T(128)S(1)} %pad_add_fusion.place, bf16[256,256]{1,0:T(8,128)(2,1)S(1)} %copy-done.8, ...), custom_call_target="tpu_custom_call" | custom-call | flops 805306368 | bytes 4456456 | tf_op jit(solution)/shard_map/pallas_call | solution.py:34
  33.2 1.6 %collective-permute-start.6 = (f32[1,3,64,256]{3,2,1,0:T(8,128)S(1)}, f32[1,3,64,256]{3,2,1,0:T(8,128)S(1)}, u32[]{:S(2)}, u32[]{:S(2)}) collective-permute-start(f32[1,3,64,256]{3,2,1,0:T(8,128)S(1)} %get-tuple-element.143), channel_id=1, source_target_pairs={{0,8},{2,10},{4,12},{6,14},{8,0},{10,2},{12,4},{14,6},{16,24},{18,... | collective-permute-start | bytes 589832 | tf_op jit(solution)/shard_map/ppermute | solution.py:358
  35.4 1.9 %shard_map.147 = (f32[2,256,256]{2,1,0:T(8,128)S(1)}, f32[2,256,256]{2,1,0:T(8,128)S(1)}, f32[2,256,256]{2,1,0:T(8,128)S(1)}, f32[2,256,256]{2,1,0:T(8,128)S(1)}, f32[8,256]{1,0:T(8,128)S(1)}) custom-call(s32[2]{0:T(128)S(1)} %pad_add_fusion.place, bf16[256,4,256]{2,1,0:T(4,128)(2,1)S(1)} %bitcast.21, bf16[256,4,256]{2,1,0:T(4,128)(2,1)S(1)} %bitcast.22, ...), custom_call_target="tpu_custom_call" | custom-call | flops 16777216 | bytes 3158028 | tf_op jit(solution)/shard_map/pallas_call | solution.py:34
  37.4 1.6 %collective-permute-start.10 = (f32[2,256,256]{2,1,0:T(8,128)S(1)}, f32[2,256,256]{2,1,0:T(8,128)S(1)}, u32[]{:S(2)}, u32[]{:S(2)}) collective-permute-start(f32[2,256,256]{2,1,0:T(8,128)S(1)} %get-tuple-element.150), channel_id=1, source_target_pairs={{0,4},{2,6},{4,0},{6,2},{8,12},{10,14},{12,8},{14,10},{16,20},{18,... | collective-permute-start | bytes 1572872 | tf_op jit(solution)/shard_map/ppermute | solution.py:358
  39.5 2.7 %collective-permute-start.8 = (f32[1,3,64,256]{3,2,1,0:T(8,128)S(1)}, f32[1,3,64,256]{3,2,1,0:T(8,128)S(1)}, u32[]{:S(2)}, u32[]{:S(2)}) collective-permute-start(f32[1,3,64,256]{3,2,1,0:T(8,128)S(1)} %add.34), channel_id=1, source_target_pairs={{0,16},{2,18},{4,20},{6,22},{8,24},{10,26},{12,28},{14,30},{16,0},... | collective-permute-start | bytes 589832 | tf_op jit(solution)/shard_map/ppermute | solution.py:358
  42.2 1.0 collective-permute-start.7
  43.2 6.4 %collective-permute-done.8 = f32[1,3,64,256]{3,2,1,0:T(8,128)S(1)} collective-permute-done((f32[1,3,64,256]{3,2,1,0:T(8,128)S(1)}, f32[1,3,64,256]{3,2,1,0:T(8,128)S(1)}, u32[]{:S(2)}, u32[]{:S(2)}) %collective-permute-start.8) | collective-permute-done | bytes 196640 | tf_op jit(solution)/shard_map/ppermute | solution.py:358
  49.6 0.9 collective-permute-done.7
  50.5 1.9 %collective-permute-start.11 = (f32[2,256,256]{2,1,0:T(8,128)S(1)}, f32[2,256,256]{2,1,0:T(8,128)S(1)}, u32[]{:S(2)}, u32[]{:S(2)}) collective-permute-start(f32[2,256,256]{2,1,0:T(8,128)S(1)} %get-tuple-element.155), channel_id=1, source_target_pairs={{0,6},{2,4},{4,2},{6,0},{8,14},{10,12},{12,10},{14,8},{16,22},{18,... | collective-permute-start | bytes 1572872 | tf_op jit(solution)/shard_map/ppermute | solution.py:358
  52.4 2.6 %collective-permute-start.13 = (f32[1,3,64,256]{3,2,1,0:T(8,128)S(1)}, f32[1,3,64,256]{3,2,1,0:T(8,128)S(1)}, u32[]{:S(2)}, u32[]{:S(2)}) collective-permute-start(f32[1,3,64,256]{3,2,1,0:T(8,128)S(1)} %add_add_fusion.1.refs_4_), channel_id=1, source_target_pairs={{0,16},{2,18},{4,20},{6,22},{8,24},{10,26},{12,28},{14,30},{16,0},... | collective-permute-start | bytes 589832 | tf_op jit(solution)/shard_map/ppermute | solution.py:358
  55.0 0.8 collective-permute-start.12
  55.8 6.1 %collective-permute-done.13.refs_6_ = f32[1,3,64,256]{3,2,1,0:T(8,128)S(1)} collective-permute-done((f32[1,3,64,256]{3,2,1,0:T(8,128)S(1)}, f32[1,3,64,256]{3,2,1,0:T(8,128)S(1)}, u32[]{:S(2)}, u32[]{:S(2)}) %collective-permute-start.13) | collective-permute-done | bytes 196640 | tf_op jit(solution)/shard_map/ppermute | solution.py:358
  62.6 5.1 %collective-permute-done.14.refs_7_ = f32[1,3,64,256]{3,2,1,0:T(8,128)S(1)} collective-permute-done((f32[1,3,64,256]{3,2,1,0:T(8,128)S(1)}, f32[1,3,64,256]{3,2,1,0:T(8,128)S(1)}, u32[]{:S(2)}, u32[]{:S(2)}) %collective-permute-start.14) | collective-permute-done | bytes 196640 | tf_op jit(solution)/shard_map/ppermute | solution.py:358
  67.6 1.8 %shard_map.149 = (f32[4,256,256]{2,1,0:T(8,128)S(1)}, f32[4,256,256]{2,1,0:T(8,128)S(1)}, bf16[4,256,256]{2,1,0:T(8,128)(2,1)S(1)}, f32[4,256,256]{2,1,0:T(8,128...) custom-call(s32[2]{0:T(128)S(1)} %pad_add_fusion.place, f32[8,256]{1,0:T(8,128)S(1)} %get-tuple-element.133.scale_row, ...), custom_call_target="tpu_custom_call" | custom-call | flops 402653184 | bytes 6963208 | tf_op jit(solution)/shard_map/pallas_call | solution.py:34
  69.5 1.2 collective-permute-done.15
  70.6 1.4 collective-permute-start.16
  72.6 1.5 %collective-permute-start.18 = (f32[2,4,256]{2,1,0:T(4,128)S(1)}, f32[2,4,256]{2,1,0:T(4,128)S(1)}, u32[]{:S(2)}, u32[]{:S(2)}) collective-permute-start(f32[2,4,256]{2,1,0:T(4,128)S(1)} %add.36.refs_0_), channel_id=1, source_target_pairs={{0,6},{2,4},{4,2},{6,0},{8,14},{10,12},{12,10},{14,8},{16,22},{18,... | collective-permute-start | bytes 24584 | tf_op jit(solution)/shard_map/ppermute | solution.py:358
  74.3 1.4 collective-permute-done.17.refs_2_
  75.7 1.5 %collective-permute-done.18.refs_3_ = f32[2,4,256]{2,1,0:T(4,128)S(1)} collective-permute-done((f32[2,4,256]{2,1,0:T(4,128)S(1)}, f32[2,4,256]{2,1,0:T(4,128)S(1)}, u32[]{:S(2)}, u32[]{:S(2)}) %collective-permute-start.18) | collective-permute-done | bytes 8224 | tf_op jit(solution)/shard_map/ppermute | solution.py:358
  77.2 2.1 %shard_map.150 = (bf16[4,256,256]{2,1,0:T(8,128)(2,1)S(1)}, bf16[4,256,256]{2,1,0:T(8,128)(2,1)S(1)}, f32[1,3,64,256]{3,2,1,0:T(8,128)S(1)}, f32[1,3,64,256]{3,2...) custom-call(s32[2]{0:T(128)S(1)} %pad_add_fusion.place, ...), custom_call_target="tpu_custom_call" | custom-call | flops 805306368 | bytes 8036360 | tf_op jit(solution)/shard_map/pallas_call | solution.py:34
  79.6 5.4 %collective-permute-done.19 = f32[1,3,64,256]{3,2,1,0:T(8,128)S(1)} collective-permute-done((f32[1,3,64,256]{3,2,1,0:T(8,128)S(1)}, f32[1,3,64,256]{3,2,1,0:T(8,128)S(1)}, u32[]{:S(2)}, u32[]{:S(2)}) %collective-permute-start.19) | collective-permute-done | bytes 196640 | tf_op jit(solution)/shard_map/ppermute | solution.py:358
  85.0 0.9 collective-permute-start.21
  86.0 1.7 %collective-permute-start.20 = (f32[1,3,64,256]{3,2,1,0:T(8,128)S(1)}, f32[1,3,64,256]{3,2,1,0:T(8,128)S(1)}, u32[]{:S(2)}, u32[]{:S(2)}) collective-permute-start(f32[1,3,64,256]{3,2,1,0:T(8,128)S(1)} %get-tuple-element.174), channel_id=1, source_target_pairs={{0,8},{2,10},{4,12},{6,14},{8,0},{10,2},{12,4},{14,6},{16,24},{18,... | collective-permute-start | bytes 589832 | tf_op jit(solution)/shard_map/ppermute | solution.py:358
  87.7 6.4 %collective-permute-done.21 = f32[1,3,64,256]{3,2,1,0:T(8,128)S(1)} collective-permute-done((f32[1,3,64,256]{3,2,1,0:T(8,128)S(1)}, f32[1,3,64,256]{3,2,1,0:T(8,128)S(1)}, u32[]{:S(2)}, u32[]{:S(2)}) %collective-permute-start.21) | collective-permute-done | bytes 196640 | tf_op jit(solution)/shard_map/ppermute | solution.py:358
  94.2 0.6 collective-permute-start.23
  95.3 1.5 %collective-permute-start.25 = (f32[256,256]{1,0:T(8,128)S(1)}, f32[256,256]{1,0:T(8,128)S(1)}, u32[]{:S(2)}, u32[]{:S(2)}) collective-permute-start(f32[256,256]{1,0:T(8,128)S(1)} %get-tuple-element.189), channel_id=1, source_target_pairs={{0,2},{2,0},{4,6},{6,4},{8,10},{10,8},{12,14},{14,12},{16,18},{18,... | collective-permute-start | bytes 786440 | tf_op jit(solution)/shard_map/ppermute | solution.py:358
  96.8 1.0 collective-permute-start.26
  97.8 1.1 collective-permute-start.27
  98.8 2.2 %collective-permute-start.22 = (f32[1,3,64,256]{3,2,1,0:T(8,128)S(1)}, f32[1,3,64,256]{3,2,1,0:T(8,128)S(1)}, u32[]{:S(2)}, u32[]{:S(2)}) collective-permute-start(f32[1,3,64,256]{3,2,1,0:T(8,128)S(1)} %add_add_fusion.refs_11_.refs_0_), channel_id=1, source_target_pairs={{0,8},{2,10},{4,12},{6,14},{8,0},{10,2},{12,4},{14,6},{16,24},{18,... | collective-permute-start | bytes 589832 | tf_op jit(solution)/shard_map/ppermute | solution.py:358
  101.1 2.9 %collective-permute-done.23.refs_13_ = f32[1,3,64,256]{3,2,1,0:T(8,128)S(1)} collective-permute-done((f32[1,3,64,256]{3,2,1,0:T(8,128)S(1)}, f32[1,3,64,256]{3,2,1,0:T(8,128)S(1)}, u32[]{:S(2)}, u32[]{:S(2)}) %collective-permute-start.23) | collective-permute-done | bytes 196640 | tf_op jit(solution)/shard_map/ppermute | solution.py:358
  104.0 1.0 shard_map.151
  105.1 2.9 %collective-permute-done.26.refs_2_ = f32[256,256]{1,0:T(8,128)S(1)} collective-permute-done((f32[256,256]{1,0:T(8,128)S(1)}, f32[256,256]{1,0:T(8,128)S(1)}, u32[]{:S(2)}, u32[]{:S(2)}) %collective-permute-start.26) | collective-permute-done | bytes 262176 | tf_op jit(solution)/shard_map/ppermute | solution.py:358
  108.0 2.6 %collective-permute-done.24.refs_14_ = f32[1,3,64,256]{3,2,1,0:T(8,128)S(1)} collective-permute-done((f32[1,3,64,256]{3,2,1,0:T(8,128)S(1)}, f32[1,3,64,256]{3,2,1,0:T(8,128)S(1)}, u32[]{:S(2)}, u32[]{:S(2)}) %collective-permute-start.24) | collective-permute-done | bytes 196640 | tf_op jit(solution)/shard_map/ppermute | solution.py:358
  110.6 3.0 %shard_map.153 = (f32[2,256,256]{2,1,0:T(8,128)S(1)}, f32[3,256,256]{2,1,0:T(8,128)S(1)}, f32[3,256,256]{2,1,0:T(8,128)S(1)}, f32[1,3,64,256]{3,2,1,0:T(8,128)S(...) custom-call(s32[2]{0:T(128)S(1)} %pad_add_fusion.place, ...), custom_call_target="tpu_custom_call" | custom-call | flops 1610612736 | bytes 13369352 | tf_op jit(solution)/shard_map/pallas_call | solution.py:34
  113.7 2.8 %collective-permute-start.32 = (f32[3,256,256]{2,1,0:T(8,128)S(1)}, f32[3,256,256]{2,1,0:T(8,128)S(1)}, u32[]{:S(2)}, u32[]{:S(2)}) collective-permute-start(f32[3,256,256]{2,1,0:T(8,128)S(1)} %get-tuple-element.213), channel_id=1, source_target_pairs={{0,4},{2,6},{4,0},{6,2},{8,12},{10,14},{12,8},{14,10},{16,20},{18,... | collective-permute-start | bytes 2359304 | tf_op jit(solution)/shard_map/ppermute | solution.py:358
  116.5 5.7 %collective-permute-done.28 = f32[1,3,64,256]{3,2,1,0:T(8,128)S(1)} collective-permute-done((f32[1,3,64,256]{3,2,1,0:T(8,128)S(1)}, f32[1,3,64,256]{3,2,1,0:T(8,128)S(1)}, u32[]{:S(2)}, u32[]{:S(2)}) %collective-permute-start.28) | collective-permute-done | bytes 196640 | tf_op jit(solution)/shard_map/ppermute | solution.py:358
  122.6 2.0 %collective-permute-start.29 = (f32[1,3,64,256]{3,2,1,0:T(8,128)S(1)}, f32[1,3,64,256]{3,2,1,0:T(8,128)S(1)}, u32[]{:S(2)}, u32[]{:S(2)}) collective-permute-start(f32[1,3,64,256]{3,2,1,0:T(8,128)S(1)} %get-tuple-element.208), channel_id=1, source_target_pairs={{0,8},{2,10},{4,12},{6,14},{8,0},{10,2},{12,4},{14,6},{16,24},{18,... | collective-permute-start | bytes 589832 | tf_op jit(solution)/shard_map/ppermute | solution.py:358
  124.6 1.7 %shard_map.154 = bf16[256,4,256]{2,1,0:T(4,128)(2,1)} custom-call(s32[2]{0:T(128)S(1)} %pad_add_fusion.place, f32[256,256]{1,0:T(8,128)S(1)} %get-tuple-element.214.refs_0_, f32[256,256]{1,0:T(8,128)S(1)} %collective-permute-done.25.refs_1_, f32[256,256]{1,0:T(8,128)S(1)} %collective-permute-done.26.refs_2_, f32[256,256]{1,0:T(8,128)S(1)} %collective-permute-done.27.refs_3_), custom_call_target="tpu_custom_call" | custom-call | flops 8388608 | bytes 1572872 | tf_op jit(solution)/shard_map/pallas_call | solution.py:34
  126.4 5.0 %collective-permute-done.30.refs_3_ = f32[1,3,64,256]{3,2,1,0:T(8,128)S(1)} collective-permute-done((f32[1,3,64,256]{3,2,1,0:T(8,128)S(1)}, f32[1,3,64,256]{3,2,1,0:T(8,128)S(1)}, u32[]{:S(2)}, u32[]{:S(2)}) %collective-permute-start.30) | collective-permute-done | bytes 196640 | tf_op jit(solution)/shard_map/ppermute | solution.py:358
  131.4 0.6 collective-permute-done.31.refs_1_
  132.1 0.8 collective-permute-done.32.refs_2_
  132.9 1.8 %collective-permute-start.36 = (f32[256,256]{1,0:T(8,128)S(1)}, f32[256,256]{1,0:T(8,128)S(1)}, u32[]{:S(2)}, u32[]{:S(2)}) collective-permute-start(f32[256,256]{1,0:T(8,128)S(1)} %slice_bitcast_fusion.1), channel_id=1, source_target_pairs={{0,4},{2,6},{4,0},{6,2},{8,12},{10,14},{12,8},{14,10},{16,20},{18,... | collective-permute-start | bytes 786440 | tf_op jit(solution)/shard_map/ppermute | solution.py:358
  134.7 0.6 collective-permute-start.37
  135.3 0.6 shard_map.155
  135.9 1.6 %collective-permute-start.33 = (f32[1,3,16,256]{3,2,1,0:T(8,128)S(1)}, f32[1,3,16,256]{3,2,1,0:T(8,128)S(1)}, u32[]{:S(2)}, u32[]{:S(2)}) collective-permute-start(f32[1,3,16,256]{3,2,1,0:T(8,128)S(1)} %get-tuple-element.223), channel_id=1, source_target_pairs={{0,2},{2,0},{4,6},{6,4},{8,10},{10,8},{12,14},{14,12},{16,18},{18,... | collective-permute-start | bytes 147464 | tf_op jit(solution)/shard_map/ppermute | solution.py:358
  137.8 1.7 %collective-permute-start.35 = (f32[1,3,16,256]{3,2,1,0:T(8,128)S(1)}, f32[1,3,16,256]{3,2,1,0:T(8,128)S(1)}, u32[]{:S(2)}, u32[]{:S(2)}) collective-permute-start(f32[1,3,16,256]{3,2,1,0:T(8,128)S(1)} %get-tuple-element.225), channel_id=1, source_target_pairs={{0,6},{2,4},{4,2},{6,0},{8,14},{10,12},{12,10},{14,8},{16,22},{18,... | collective-permute-start | bytes 147464 | tf_op jit(solution)/shard_map/ppermute | solution.py:358
  139.5 0.9 collective-permute-done.36.refs_3_
  140.4 1.1 collective-permute-done.37.refs_4_
  141.5 2.4 %shard_map.156 = (bf16[256,4,256]{2,1,0:T(4,128)(2,1)}, bf16[256,4,256]{2,1,0:T(4,128)(2,1)}) custom-call(s32[2]{0:T(128)S(1)} %pad_add_fusion.place, f32[4,256]{1,0:T(4,128)S(1)} %bitcast.24, f32[2,256,256]{2,1,0:T(8,128)S(1)} %get-tuple-element.226.refs_0_, f32[3,256,256]{2,1,0:T(8,128)S(1)} %collective-permute-done.31.refs_1_, ...), custom_call_target="tpu_custom_call" | custom-call | flops 16777216 | bytes 3674120 | tf_op jit(solution)/shard_map/pallas_call | solution.py:34
  143.9 1.2 shard_map.157
  (57 shorter events, 4.7 us)
Async XLA Ops:
  0.6 16.1 %copy-start = (f32[4,256,256]{2,1,0:T(8,128)S(1)}, f32[4,256,256]{2,1,0:T(8,128)}, u32[]{:S(2)}) copy-start(f32[4,256,256]{2,1,0:T(8,128)} %param.16) | copy-start | bytes 3145732
  0.7 0.8 copy-start.4
  1.4 1.0 copy-start.5
  2.5 5.6 %copy-start.6 = (bf16[1,256,4,256]{3,2,1,0:T(4,128)(2,1)S(1)}, bf16[1,256,4,256]{3,2,1,0:T(4,128)(2,1)}, u32[]{:S(2)}) copy-start(bf16[1,256,4,256]{3,2,1,0:T(4,128)(2,1)} %param.11) | copy-start | bytes 1572868
  3.6 10.4 %collective-permute-start.3 = (f32[256,256]{1,0:T(8,128)S(1)}, f32[256,256]{1,0:T(8,128)S(1)}, u32[]{:S(2)}, u32[]{:S(2)}) collective-permute-start(f32[256,256]{1,0:T(8,128)S(1)} %get-tuple-element.128), channel_id=1, source_target_pairs={{0,2},{2,0},{4,6},{6,4},{8,10},{10,8},{12,14},{14,12},{16,18},{18,... | collective-permute-start | bytes 786440 | tf_op jit(solution)/shard_map/ppermute | solution.py:358
  6.6 14.1 %collective-permute-start.4 = (f32[256,256]{1,0:T(8,128)S(1)}, f32[256,256]{1,0:T(8,128)S(1)}, u32[]{:S(2)}, u32[]{:S(2)}) collective-permute-start(f32[256,256]{1,0:T(8,128)S(1)} %get-tuple-element.129), channel_id=1, source_target_pairs={{0,4},{2,6},{4,0},{6,2},{8,12},{10,14},{12,8},{14,10},{16,20},{18,... | collective-permute-start | bytes 786440 | tf_op jit(solution)/shard_map/ppermute | solution.py:358
  8.1 12.8 %collective-permute-start.5 = (f32[256,256]{1,0:T(8,128)S(1)}, f32[256,256]{1,0:T(8,128)S(1)}, u32[]{:S(2)}, u32[]{:S(2)}) collective-permute-start(f32[256,256]{1,0:T(8,128)S(1)} %get-tuple-element.130), channel_id=1, source_target_pairs={{0,6},{2,4},{4,2},{6,0},{8,14},{10,12},{12,10},{14,8},{16,22},{18,... | collective-permute-start | bytes 786440 | tf_op jit(solution)/shard_map/ppermute | solution.py:358
  9.8 0.7 copy-start.7
  10.4 14.5 %collective-permute-start = (f32[256,256]{1,0:T(8,128)}, f32[256,256]{1,0:T(8,128)S(1)}, u32[]{:S(2)}, u32[]{:S(2)}) collective-permute-start(f32[256,256]{1,0:T(8,128)} %get-tuple-element.124), channel_id=1, source_target_pairs={{0,2},{2,0},{4,6},{6,4},{8,10},{10,8},{12,14},{14,12},{16,18},{18,... | collective-permute-start | bytes 786440 | tf_op jit(solution)/shard_map/ppermute | solution.py:358
  12.4 18.8 %collective-permute-start.1 = (f32[256,256]{1,0:T(8,128)}, f32[256,256]{1,0:T(8,128)S(1)}, u32[]{:S(2)}, u32[]{:S(2)}) collective-permute-start(f32[256,256]{1,0:T(8,128)} %get-tuple-element.125), channel_id=1, source_target_pairs={{0,4},{2,6},{4,0},{6,2},{8,12},{10,14},{12,8},{14,10},{16,20},{18,... | collective-permute-start | bytes 786440 | tf_op jit(solution)/shard_map/ppermute | solution.py:358
  13.9 17.3 %collective-permute-start.2 = (f32[256,256]{1,0:T(8,128)S(1)}, f32[256,256]{1,0:T(8,128)S(1)}, u32[]{:S(2)}, u32[]{:S(2)}) collective-permute-start(f32[256,256]{1,0:T(8,128)S(1)} %get-tuple-element.126), channel_id=1, source_target_pairs={{0,6},{2,4},{4,2},{6,0},{8,14},{10,12},{12,10},{14,8},{16,22},{18,... | collective-permute-start | bytes 786440 | tf_op jit(solution)/shard_map/ppermute | solution.py:358
  16.7 14.5 %copy-start.8 = (bf16[256,256]{1,0:T(8,128)(2,1)S(1)}, bf16[256,256]{1,0:T(8,128)(2,1)}, u32[]{:S(2)}) copy-start(bf16[256,256]{1,0:T(8,128)(2,1)} %copy-done.7) | copy-start | bytes 393220
  31.2 4.2 %copy-start.1 = (bf16[1,256,4,256]{3,2,1,0:T(4,128)(2,1)S(1)}, bf16[1,256,4,256]{3,2,1,0:T(4,128)(2,1)}, u32[]{:S(2)}) copy-start(bf16[1,256,4,256]{3,2,1,0:T(4,128)(2,1)} %param.10) | copy-start | bytes 1572868
  31.2 4.2 %copy-start.2 = (bf16[1,256,4,256]{3,2,1,0:T(4,128)(2,1)S(1)}, bf16[1,256,4,256]{3,2,1,0:T(4,128)(2,1)}, u32[]{:S(2)}) copy-start(bf16[1,256,4,256]{3,2,1,0:T(4,128)(2,1)} %param.19) | copy-start | bytes 1572868
  33.2 1.7 %copy-start.9 = (f32[4]{0:T(128)S(1)}, f32[4]{0:T(128)}, u32[]{:S(2)}) copy-start(f32[4]{0:T(128)} %param.14) | copy-start | bytes 52
  33.2 2.2 %copy-start.3 = (f32[4,256]{1,0:T(4,128)S(1)}, f32[4,256]{1,0:T(4,128)}, u32[]{:S(2)}) copy-start(f32[4,256]{1,0:T(4,128)} %gain.1) | copy-start | bytes 12292
  33.2 6.3 %collective-permute-start.6 = (f32[1,3,64,256]{3,2,1,0:T(8,128)S(1)}, f32[1,3,64,256]{3,2,1,0:T(8,128)S(1)}, u32[]{:S(2)}, u32[]{:S(2)}) collective-permute-start(f32[1,3,64,256]{3,2,1,0:T(8,128)S(1)} %get-tuple-element.143), channel_id=1, source_target_pairs={{0,8},{2,10},{4,12},{6,14},{8,0},{10,2},{12,4},{14,6},{16,24},{18,... | collective-permute-start | bytes 589832 | tf_op jit(solution)/shard_map/ppermute | solution.py:358
  37.4 13.1 %collective-permute-start.10 = (f32[2,256,256]{2,1,0:T(8,128)S(1)}, f32[2,256,256]{2,1,0:T(8,128)S(1)}, u32[]{:S(2)}, u32[]{:S(2)}) collective-permute-start(f32[2,256,256]{2,1,0:T(8,128)S(1)} %get-tuple-element.150), channel_id=1, source_target_pairs={{0,4},{2,6},{4,0},{6,2},{8,12},{10,14},{12,8},{14,10},{16,20},{18,... | collective-permute-start | bytes 1572872 | tf_op jit(solution)/shard_map/ppermute | solution.py:358
  39.0 11.5 %collective-permute-start.9 = (f32[2,256,256]{2,1,0:T(8,128)S(1)}, f32[2,256,256]{2,1,0:T(8,128)S(1)}, u32[]{:S(2)}, u32[]{:S(2)}) collective-permute-start(f32[2,256,256]{2,1,0:T(8,128)S(1)} %get-tuple-element.149), channel_id=1, source_target_pairs={{0,2},{2,0},{4,6},{6,4},{8,10},{10,8},{12,14},{14,12},{16,18},{18,... | collective-permute-start | bytes 1572872 | tf_op jit(solution)/shard_map/ppermute | solution.py:358
  39.5 10.0 %collective-permute-start.8 = (f32[1,3,64,256]{3,2,1,0:T(8,128)S(1)}, f32[1,3,64,256]{3,2,1,0:T(8,128)S(1)}, u32[]{:S(2)}, u32[]{:S(2)}) collective-permute-start(f32[1,3,64,256]{3,2,1,0:T(8,128)S(1)} %add.34), channel_id=1, source_target_pairs={{0,16},{2,18},{4,20},{6,22},{8,24},{10,26},{12,28},{14,30},{16,0},... | collective-permute-start | bytes 589832 | tf_op jit(solution)/shard_map/ppermute | solution.py:358
  42.2 8.2 %collective-permute-start.7 = (f32[1,3,64,256]{3,2,1,0:T(8,128)S(1)}, f32[1,3,64,256]{3,2,1,0:T(8,128)S(1)}, u32[]{:S(2)}, u32[]{:S(2)}) collective-permute-start(f32[1,3,64,256]{3,2,1,0:T(8,128)S(1)} %get-tuple-element.145), channel_id=1, source_target_pairs={{0,8},{2,10},{4,12},{6,14},{8,0},{10,2},{12,4},{14,6},{16,24},{18,... | collective-permute-start | bytes 589832 | tf_op jit(solution)/shard_map/ppermute | solution.py:358
  50.5 17.2 %collective-permute-start.11 = (f32[2,256,256]{2,1,0:T(8,128)S(1)}, f32[2,256,256]{2,1,0:T(8,128)S(1)}, u32[]{:S(2)}, u32[]{:S(2)}) collective-permute-start(f32[2,256,256]{2,1,0:T(8,128)S(1)} %get-tuple-element.155), channel_id=1, source_target_pairs={{0,6},{2,4},{4,2},{6,0},{8,14},{10,12},{12,10},{14,8},{16,22},{18,... | collective-permute-start | bytes 1572872 | tf_op jit(solution)/shard_map/ppermute | solution.py:358
  52.4 9.6 %collective-permute-start.13 = (f32[1,3,64,256]{3,2,1,0:T(8,128)S(1)}, f32[1,3,64,256]{3,2,1,0:T(8,128)S(1)}, u32[]{:S(2)}, u32[]{:S(2)}) collective-permute-start(f32[1,3,64,256]{3,2,1,0:T(8,128)S(1)} %add_add_fusion.1.refs_4_), channel_id=1, source_target_pairs={{0,16},{2,18},{4,20},{6,22},{8,24},{10,26},{12,28},{14,30},{16,0},... | collective-permute-start | bytes 589832 | tf_op jit(solution)/shard_map/ppermute | solution.py:358
  55.0 7.6 %collective-permute-start.12 = (f32[1,3,64,256]{3,2,1,0:T(8,128)S(1)}, f32[1,3,64,256]{3,2,1,0:T(8,128)S(1)}, u32[]{:S(2)}, u32[]{:S(2)}) collective-permute-start(f32[1,3,64,256]{3,2,1,0:T(8,128)S(1)} %add_add_fusion.1.refs_4_), channel_id=1, source_target_pairs={{0,8},{2,10},{4,12},{6,14},{8,0},{10,2},{12,4},{14,6},{16,24},{18,... | collective-permute-start | bytes 589832 | tf_op jit(solution)/shard_map/ppermute | solution.py:358
  62.0 5.7 %collective-permute-start.14 = (f32[1,3,64,256]{3,2,1,0:T(8,128)S(1)}, f32[1,3,64,256]{3,2,1,0:T(8,128)S(1)}, u32[]{:S(2)}, u32[]{:S(2)}) collective-permute-start(f32[1,3,64,256]{3,2,1,0:T(8,128)S(1)} %collective-permute-done.13.refs_6_), channel_id=1, source_target_pairs={{0,8},{2,10},{4,12},{6,14},{8,0},{10,2},{12,4},{14,6},{16,24},{18,... | collective-permute-start | bytes 589832 | tf_op jit(solution)/shard_map/ppermute | solution.py:358
  69.4 1.2 collective-permute-start.15
  70.6 3.7 %collective-permute-start.16 = (f32[2,4,256]{2,1,0:T(4,128)S(1)}, f32[2,4,256]{2,1,0:T(4,128)S(1)}, u32[]{:S(2)}, u32[]{:S(2)}) collective-permute-start(f32[2,4,256]{2,1,0:T(4,128)S(1)} %add.36.refs_0_), channel_id=1, source_target_pairs={{0,2},{2,0},{4,6},{6,4},{8,10},{10,8},{12,14},{14,12},{16,18},{18,... | collective-permute-start | bytes 24584 | tf_op jit(solution)/shard_map/ppermute | solution.py:358
  72.0 3.7 %collective-permute-start.17 = (f32[2,4,256]{2,1,0:T(4,128)S(1)}, f32[2,4,256]{2,1,0:T(4,128)S(1)}, u32[]{:S(2)}, u32[]{:S(2)}) collective-permute-start(f32[2,4,256]{2,1,0:T(4,128)S(1)} %add.36.refs_0_), channel_id=1, source_target_pairs={{0,4},{2,6},{4,0},{6,2},{8,12},{10,14},{12,8},{14,10},{16,20},{18,... | collective-permute-start | bytes 24584 | tf_op jit(solution)/shard_map/ppermute | solution.py:358
  72.6 4.5 %collective-permute-start.18 = (f32[2,4,256]{2,1,0:T(4,128)S(1)}, f32[2,4,256]{2,1,0:T(4,128)S(1)}, u32[]{:S(2)}, u32[]{:S(2)}) collective-permute-start(f32[2,4,256]{2,1,0:T(4,128)S(1)} %add.36.refs_0_), channel_id=1, source_target_pairs={{0,6},{2,4},{4,2},{6,0},{8,14},{10,12},{12,10},{14,8},{16,22},{18,... | collective-permute-start | bytes 24584 | tf_op jit(solution)/shard_map/ppermute | solution.py:358
  79.3 5.7 %collective-permute-start.19 = (f32[1,3,64,256]{3,2,1,0:T(8,128)S(1)}, f32[1,3,64,256]{3,2,1,0:T(8,128)S(1)}, u32[]{:S(2)}, u32[]{:S(2)}) collective-permute-start(f32[1,3,64,256]{3,2,1,0:T(8,128)S(1)} %get-tuple-element.172), channel_id=1, source_target_pairs={{0,8},{2,10},{4,12},{6,14},{8,0},{10,2},{12,4},{14,6},{16,24},{18,... | collective-permute-start | bytes 589832 | tf_op jit(solution)/shard_map/ppermute | solution.py:358
  85.0 9.1 %collective-permute-start.21 = (f32[1,3,64,256]{3,2,1,0:T(8,128)S(1)}, f32[1,3,64,256]{3,2,1,0:T(8,128)S(1)}, u32[]{:S(2)}, u32[]{:S(2)}) collective-permute-start(f32[1,3,64,256]{3,2,1,0:T(8,128)S(1)} %add.38), channel_id=1, source_target_pairs={{0,16},{2,18},{4,20},{6,22},{8,24},{10,26},{12,28},{14,30},{16,0},... | collective-permute-start | bytes 589832 | tf_op jit(solution)/shard_map/ppermute | solution.py:358
  86.0 8.2 %collective-permute-start.20 = (f32[1,3,64,256]{3,2,1,0:T(8,128)S(1)}, f32[1,3,64,256]{3,2,1,0:T(8,128)S(1)}, u32[]{:S(2)}, u32[]{:S(2)}) collective-permute-start(f32[1,3,64,256]{3,2,1,0:T(8,128)S(1)} %get-tuple-element.174), channel_id=1, source_target_pairs={{0,8},{2,10},{4,12},{6,14},{8,0},{10,2},{12,4},{14,6},{16,24},{18,... | collective-permute-start | bytes 589832 | tf_op jit(solution)/shard_map/ppermute | solution.py:358
  94.2 9.8 %collective-permute-start.23 = (f32[1,3,64,256]{3,2,1,0:T(8,128)S(1)}, f32[1,3,64,256]{3,2,1,0:T(8,128)S(1)}, u32[]{:S(2)}, u32[]{:S(2)}) collective-permute-start(f32[1,3,64,256]{3,2,1,0:T(8,128)S(1)} %add_add_fusion.refs_11_.refs_0_), channel_id=1, source_target_pairs={{0,16},{2,18},{4,20},{6,22},{8,24},{10,26},{12,28},{14,30},{16,0},... | collective-permute-start | bytes 589832 | tf_op jit(solution)/shard_map/ppermute | solution.py:358
  95.3 9.8 %collective-permute-start.25 = (f32[256,256]{1,0:T(8,128)S(1)}, f32[256,256]{1,0:T(8,128)S(1)}, u32[]{:S(2)}, u32[]{:S(2)}) collective-permute-start(f32[256,256]{1,0:T(8,128)S(1)} %get-tuple-element.189), channel_id=1, source_target_pairs={{0,2},{2,0},{4,6},{6,4},{8,10},{10,8},{12,14},{14,12},{16,18},{18,... | collective-permute-start | bytes 786440 | tf_op jit(solution)/shard_map/ppermute | solution.py:358
  96.8 11.2 %collective-permute-start.26 = (f32[256,256]{1,0:T(8,128)S(1)}, f32[256,256]{1,0:T(8,128)S(1)}, u32[]{:S(2)}, u32[]{:S(2)}) collective-permute-start(f32[256,256]{1,0:T(8,128)S(1)} %get-tuple-element.190), channel_id=1, source_target_pairs={{0,4},{2,6},{4,0},{6,2},{8,12},{10,14},{12,8},{14,10},{16,20},{18,... | collective-permute-start | bytes 786440 | tf_op jit(solution)/shard_map/ppermute | solution.py:358
  97.8 10.2 %collective-permute-start.27 = (f32[256,256]{1,0:T(8,128)S(1)}, f32[256,256]{1,0:T(8,128)S(1)}, u32[]{:S(2)}, u32[]{:S(2)}) collective-permute-start(f32[256,256]{1,0:T(8,128)S(1)} %get-tuple-element.191), channel_id=1, source_target_pairs={{0,6},{2,4},{4,2},{6,0},{8,14},{10,12},{12,10},{14,8},{16,22},{18,... | collective-permute-start | bytes 786440 | tf_op jit(solution)/shard_map/ppermute | solution.py:358
  98.8 9.2 %collective-permute-start.22 = (f32[1,3,64,256]{3,2,1,0:T(8,128)S(1)}, f32[1,3,64,256]{3,2,1,0:T(8,128)S(1)}, u32[]{:S(2)}, u32[]{:S(2)}) collective-permute-start(f32[1,3,64,256]{3,2,1,0:T(8,128)S(1)} %add_add_fusion.refs_11_.refs_0_), channel_id=1, source_target_pairs={{0,8},{2,10},{4,12},{6,14},{8,0},{10,2},{12,4},{14,6},{16,24},{18,... | collective-permute-start | bytes 589832 | tf_op jit(solution)/shard_map/ppermute | solution.py:358
  104.0 6.6 %collective-permute-start.24 = (f32[1,3,64,256]{3,2,1,0:T(8,128)S(1)}, f32[1,3,64,256]{3,2,1,0:T(8,128)S(1)}, u32[]{:S(2)}, u32[]{:S(2)}) collective-permute-start(f32[1,3,64,256]{3,2,1,0:T(8,128)S(1)} %collective-permute-done.23.refs_13_), channel_id=1, source_target_pairs={{0,8},{2,10},{4,12},{6,14},{8,0},{10,2},{12,4},{14,6},{16,24},{18,... | collective-permute-start | bytes 589832 | tf_op jit(solution)/shard_map/ppermute | solution.py:358
  113.7 18.4 %collective-permute-start.31 = (f32[3,256,256]{2,1,0:T(8,128)S(1)}, f32[3,256,256]{2,1,0:T(8,128)S(1)}, u32[]{:S(2)}, u32[]{:S(2)}) collective-permute-start(f32[3,256,256]{2,1,0:T(8,128)S(1)} %get-tuple-element.212), channel_id=1, source_target_pairs={{0,2},{2,0},{4,6},{6,4},{8,10},{10,8},{12,14},{14,12},{16,18},{18,... | collective-permute-start | bytes 2359304 | tf_op jit(solution)/shard_map/ppermute | solution.py:358
  113.7 19.1 %collective-permute-start.32 = (f32[3,256,256]{2,1,0:T(8,128)S(1)}, f32[3,256,256]{2,1,0:T(8,128)S(1)}, u32[]{:S(2)}, u32[]{:S(2)}) collective-permute-start(f32[3,256,256]{2,1,0:T(8,128)S(1)} %get-tuple-element.213), channel_id=1, source_target_pairs={{0,4},{2,6},{4,0},{6,2},{8,12},{10,14},{12,8},{14,10},{16,20},{18,... | collective-permute-start | bytes 2359304 | tf_op jit(solution)/shard_map/ppermute | solution.py:358
  116.5 5.7 %collective-permute-start.28 = (f32[1,3,64,256]{3,2,1,0:T(8,128)S(1)}, f32[1,3,64,256]{3,2,1,0:T(8,128)S(1)}, u32[]{:S(2)}, u32[]{:S(2)}) collective-permute-start(f32[1,3,64,256]{3,2,1,0:T(8,128)S(1)} %get-tuple-element.206), channel_id=1, source_target_pairs={{0,8},{2,10},{4,12},{6,14},{8,0},{10,2},{12,4},{14,6},{16,24},{18,... | collective-permute-start | bytes 589832 | tf_op jit(solution)/shard_map/ppermute | solution.py:358
  122.2 9.2 %collective-permute-start.30 = (f32[1,3,64,256]{3,2,1,0:T(8,128)S(1)}, f32[1,3,64,256]{3,2,1,0:T(8,128)S(1)}, u32[]{:S(2)}, u32[]{:S(2)}) collective-permute-start(f32[1,3,64,256]{3,2,1,0:T(8,128)S(1)} %add.40), channel_id=1, source_target_pairs={{0,16},{2,18},{4,20},{6,22},{8,24},{10,26},{12,28},{14,30},{16,0},... | collective-permute-start | bytes 589832 | tf_op jit(solution)/shard_map/ppermute | solution.py:358
  122.6 8.8 %collective-permute-start.29 = (f32[1,3,64,256]{3,2,1,0:T(8,128)S(1)}, f32[1,3,64,256]{3,2,1,0:T(8,128)S(1)}, u32[]{:S(2)}, u32[]{:S(2)}) collective-permute-start(f32[1,3,64,256]{3,2,1,0:T(8,128)S(1)} %get-tuple-element.208), channel_id=1, source_target_pairs={{0,8},{2,10},{4,12},{6,14},{8,0},{10,2},{12,4},{14,6},{16,24},{18,... | collective-permute-start | bytes 589832 | tf_op jit(solution)/shard_map/ppermute | solution.py:358
  132.9 7.5 %collective-permute-start.36 = (f32[256,256]{1,0:T(8,128)S(1)}, f32[256,256]{1,0:T(8,128)S(1)}, u32[]{:S(2)}, u32[]{:S(2)}) collective-permute-start(f32[256,256]{1,0:T(8,128)S(1)} %slice_bitcast_fusion.1), channel_id=1, source_target_pairs={{0,4},{2,6},{4,0},{6,2},{8,12},{10,14},{12,8},{14,10},{16,20},{18,... | collective-permute-start | bytes 786440 | tf_op jit(solution)/shard_map/ppermute | solution.py:358
  134.7 6.8 %collective-permute-start.37 = (f32[256,256]{1,0:T(8,128)S(1)}, f32[256,256]{1,0:T(8,128)S(1)}, u32[]{:S(2)}, u32[]{:S(2)}) collective-permute-start(f32[256,256]{1,0:T(8,128)S(1)} %slice_bitcast_fusion), channel_id=1, source_target_pairs={{0,2},{2,0},{4,6},{6,4},{8,10},{10,8},{12,14},{14,12},{16,18},{18,... | collective-permute-start | bytes 786440 | tf_op jit(solution)/shard_map/ppermute | solution.py:358
  135.9 8.0 %collective-permute-start.33 = (f32[1,3,16,256]{3,2,1,0:T(8,128)S(1)}, f32[1,3,16,256]{3,2,1,0:T(8,128)S(1)}, u32[]{:S(2)}, u32[]{:S(2)}) collective-permute-start(f32[1,3,16,256]{3,2,1,0:T(8,128)S(1)} %get-tuple-element.223), channel_id=1, source_target_pairs={{0,2},{2,0},{4,6},{6,4},{8,10},{10,8},{12,14},{14,12},{16,18},{18,... | collective-permute-start | bytes 147464 | tf_op jit(solution)/shard_map/ppermute | solution.py:358
  137.5 6.4 %collective-permute-start.34 = (f32[1,3,16,256]{3,2,1,0:T(8,128)S(1)}, f32[1,3,16,256]{3,2,1,0:T(8,128)S(1)}, u32[]{:S(2)}, u32[]{:S(2)}) collective-permute-start(f32[1,3,16,256]{3,2,1,0:T(8,128)S(1)} %get-tuple-element.224), channel_id=1, source_target_pairs={{0,4},{2,6},{4,0},{6,2},{8,12},{10,14},{12,8},{14,10},{16,20},{18,... | collective-permute-start | bytes 147464 | tf_op jit(solution)/shard_map/ppermute | solution.py:358
  137.8 6.2 %collective-permute-start.35 = (f32[1,3,16,256]{3,2,1,0:T(8,128)S(1)}, f32[1,3,16,256]{3,2,1,0:T(8,128)S(1)}, u32[]{:S(2)}, u32[]{:S(2)}) collective-permute-start(f32[1,3,16,256]{3,2,1,0:T(8,128)S(1)} %get-tuple-element.225), channel_id=1, source_target_pairs={{0,6},{2,4},{4,2},{6,0},{8,14},{10,12},{12,10},{14,8},{16,22},{18,... | collective-permute-start | bytes 147464 | tf_op jit(solution)/shard_map/ppermute | solution.py:358

commit v19 on v16

--- a/solution.py
+++ b/solution.py
@@ -451,12 +451,11 @@
     )
     part = functools.reduce(jnp.add, scatter(out, depth, groups))
     parts = gather(part, depth, groups)
-    q_back = in_plane(q_sent)
-    parts, saved, q_back = after(parts, saved, q_back)
     (grad_q,) = call(
         functools.partial(join_query_kernel, groups), [joined], [scratch], flops // 16,
-        place, *q_back,
-    )
+        place, *in_plane(q_sent),
+    )
+    parts, grad_q, saved = after(parts, grad_q, saved)
     rows = hidden // depth
     out = call(
         functools.partial(update_back_kernel, groups, depth, scale),
@@ -467,7 +466,7 @@
     back = in_plane(out[:packed])
     ends = scatter(out[packed:], depth, groups)
     if groups == 4:
-        ends, back, grad_q = after(ends, back, grad_q)
+        ends, back = after(ends, back)
         back += [move(back[1][2], "ctx", 2), move(back[2][2], "ctx", 1)]
     own_rows = rows // groups
     sent = call(

time: 144 us -> 145 us (level)
  starting transfers between devices: 46.6 us -> 51.5 us
  waiting for transfers between devices: 70.9 us -> 67.3 us
    ppermute x39, starting transfers between devices: 46.6 us -> 51.5 us  [move(): lax.ppermute(x, axis, [(c, c ^ step) for c in range(lax.axis_size(axis))])]
    ppermute x39, waiting for transfers between devices: 70.9 us -> 67.3 us  [move(): lax.ppermute(x, axis, [(c, c ^ step) for c in range(lax.axis_size(axis))])]
  transfers between devices with their start and end apart: 39 -> 39, of which waited for: 25 -> 28; matrix products, arithmetic and copies ran while one was open for 1% -> 1% of each run, Pallas kernels for 7% -> 7%
where the time goes in v19:
time: 145 us; the launch traced here: 144 us
  waiting for transfers between devices  67.3 us (46%)
  starting transfers between devices  51.5 us (36%)
  Pallas kernels  21 us (14%)
  local copies, waits for them, and re-layouts  3.56 us (2%)
    ppermute x39, waiting for transfers between devices, move(): lax.ppermute(x, axis, [(c, c ^ step) for c in range(lax.axis_size(axis))])  67.3 us
    ppermute x39, starting transfers between devices, move(): lax.ppermute(x, axis, [(c, c ^ step) for c in range(lax.axis_size(axis))])  51.5 us
    pallas_call x13, Pallas kernels, call(): pl.pallas_call(body, out_shape=out_shape, in_specs=[smem if a.dtype == jn...  21 us
  transfers between devices with their start and end apart: 39, of which 28 were waited for; matrix products, arithmetic and copies ran while one was open for 1% of the time, Pallas kernels for 7%

profile of v19, /device:TPU:0, one launch (start us, length us, event | category | flops | bytes accessed | tf_op | source)
XLA Modules:
  0.0 144.4 jit_solution(12146463759119229427)
XLA Ops:
  0.7 1.1 copy-done.5
  1.8 0.9 shard_map.145
  2.8 3.0 %collective-permute-start = (f32[256,256]{1,0:T(8,128)S(1)}, f32[256,256]{1,0:T(8,128)S(1)}, u32[]{:S(2)}, u32[]{:S(2)}) collective-permute-start(f32[256,256]{1,0:T(8,128)S(1)} %get-tuple-element.122), channel_id=1, source_target_pairs={{0,2},{2,0},{4,6},{6,4},{8,10},{10,8},{12,14},{14,12},{16,18},{18,... | collective-permute-start | bytes 786440 | tf_op jit(solution)/shard_map/ppermute | solution.py:358
  5.8 1.5 %collective-permute-start.1 = (f32[256,256]{1,0:T(8,128)S(1)}, f32[256,256]{1,0:T(8,128)S(1)}, u32[]{:S(2)}, u32[]{:S(2)}) collective-permute-start(f32[256,256]{1,0:T(8,128)S(1)} %get-tuple-element.123), channel_id=1, source_target_pairs={{0,4},{2,6},{4,0},{6,2},{8,12},{10,14},{12,8},{14,10},{16,20},{18,... | collective-permute-start | bytes 786440 | tf_op jit(solution)/shard_map/ppermute | solution.py:358
  7.3 1.8 %shard_map.146 = (bf16[256,256]{1,0:T(8,128)(2,1)S(1)}, f32[256,256]{1,0:T(8,128)}, f32[256,256]{1,0:T(8,128)}, f32[256,256]{1,0:T(8,128)S(1)}) custom-call(s32[2]{0:T(128)S(1)} %pad_add_fusion.place, bf16[256,4,256]{2,1,0:T(4,128)(2,1)S(1)} %bitcast.26, f32[4,256]{1,0:T(4,128)S(1)} %bitcast.23), custom_call_target="tpu_custom_call" | custom-call | flops 2147483648 | bytes 1445896 | tf_op jit(solution)/shard_map/pallas_call | solution.py:34
  9.8 1.9 %collective-permute-start.3 = (f32[256,256]{1,0:T(8,128)}, f32[256,256]{1,0:T(8,128)S(1)}, u32[]{:S(2)}, u32[]{:S(2)}) collective-permute-start(f32[256,256]{1,0:T(8,128)} %get-tuple-element.126), channel_id=1, source_target_pairs={{0,2},{2,0},{4,6},{6,4},{8,10},{10,8},{12,14},{14,12},{16,18},{18,... | collective-permute-start | bytes 786440 | tf_op jit(solution)/shard_map/ppermute | solution.py:358
  11.7 1.5 %collective-permute-start.4 = (f32[256,256]{1,0:T(8,128)}, f32[256,256]{1,0:T(8,128)S(1)}, u32[]{:S(2)}, u32[]{:S(2)}) collective-permute-start(f32[256,256]{1,0:T(8,128)} %get-tuple-element.127), channel_id=1, source_target_pairs={{0,4},{2,6},{4,0},{6,2},{8,12},{10,14},{12,8},{14,10},{16,20},{18,... | collective-permute-start | bytes 786440 | tf_op jit(solution)/shard_map/ppermute | solution.py:358
  13.2 2.7 %collective-permute-start.5 = (f32[256,256]{1,0:T(8,128)S(1)}, f32[256,256]{1,0:T(8,128)S(1)}, u32[]{:S(2)}, u32[]{:S(2)}) collective-permute-start(f32[256,256]{1,0:T(8,128)S(1)} %get-tuple-element.128), channel_id=1, source_target_pairs={{0,6},{2,4},{4,2},{6,0},{8,14},{10,12},{12,10},{14,8},{16,22},{18,... | collective-permute-start | bytes 786440 | tf_op jit(solution)/shard_map/ppermute | solution.py:358
  15.9 1.1 dynamic-slice_bitcast_fusion
  17.1 2.7 %collective-permute-done.1.refs_2_ = f32[256,256]{1,0:T(8,128)S(1)} collective-permute-done((f32[256,256]{1,0:T(8,128)S(1)}, f32[256,256]{1,0:T(8,128)S(1)}, u32[]{:S(2)}, u32[]{:S(2)}) %collective-permute-start.1) | collective-permute-done | bytes 262176 | tf_op jit(solution)/shard_map/ppermute | solution.py:358
  20.1 4.1 %collective-permute-done.3.refs_5_ = f32[256,256]{1,0:T(8,128)S(1)} collective-permute-done((f32[256,256]{1,0:T(8,128)}, f32[256,256]{1,0:T(8,128)S(1)}, u32[]{:S(2)}, u32[]{:S(2)}) %collective-permute-start.3) | collective-permute-done | bytes 262176 | tf_op jit(solution)/shard_map/ppermute | solution.py:358
  24.2 6.2 %collective-permute-done.4.refs_6_ = f32[256,256]{1,0:T(8,128)S(1)} collective-permute-done((f32[256,256]{1,0:T(8,128)}, f32[256,256]{1,0:T(8,128)S(1)}, u32[]{:S(2)}, u32[]{:S(2)}) %collective-permute-start.4) | collective-permute-done | bytes 262176 | tf_op jit(solution)/shard_map/ppermute | solution.py:358
  30.4 2.0 %shard_map.148 = (bf16[4,256,256]{2,1,0:T(8,128)(2,1)S(1)}, bf16[4,256,256]{2,1,0:T(8,128)(2,1)S(1)}, f32[1,3,64,256]{3,2,1,0:T(8,128)S(1)}, f32[1,3,64,256]{3,2...) custom-call(s32[2]{0:T(128)S(1)} %pad_add_fusion.place, ...), custom_call_target="tpu_custom_call" | custom-call | flops 805306368 | bytes 4456456 | tf_op jit(solution)/shard_map/pallas_call | solution.py:34
  32.4 1.6 %collective-permute-start.6 = (f32[1,3,64,256]{3,2,1,0:T(8,128)S(1)}, f32[1,3,64,256]{3,2,1,0:T(8,128)S(1)}, u32[]{:S(2)}, u32[]{:S(2)}) collective-permute-start(f32[1,3,64,256]{3,2,1,0:T(8,128)S(1)} %get-tuple-element.141), channel_id=1, source_target_pairs={{0,8},{2,10},{4,12},{6,14},{8,0},{10,2},{12,4},{14,6},{16,24},{18,... | collective-permute-start | bytes 589832 | tf_op jit(solution)/shard_map/ppermute | solution.py:358
  34.6 1.9 %shard_map.147 = (f32[2,256,256]{2,1,0:T(8,128)S(1)}, f32[2,256,256]{2,1,0:T(8,128)S(1)}, f32[2,256,256]{2,1,0:T(8,128)S(1)}, f32[256,256]{1,0:T(8,128)S(1)}, f3...) custom-call(s32[2]{0:T(128)S(1)} %pad_add_fusion.place, bf16[256,4,256]{2,1,0:T(4,128)(2,1)S(1)} %bitcast.21, ...), custom_call_target="tpu_custom_call" | custom-call | flops 16777216 | bytes 3158028 | tf_op jit(solution)/shard_map/pallas_call | solution.py:34
  36.6 1.3 collective-permute-start.9
  37.9 0.8 collective-permute-start.10
  38.7 2.7 %collective-permute-start.8 = (f32[1,3,64,256]{3,2,1,0:T(8,128)S(1)}, f32[1,3,64,256]{3,2,1,0:T(8,128)S(1)}, u32[]{:S(2)}, u32[]{:S(2)}) collective-permute-start(f32[1,3,64,256]{3,2,1,0:T(8,128)S(1)} %add.34), channel_id=1, source_target_pairs={{0,16},{2,18},{4,20},{6,22},{8,24},{10,26},{12,28},{14,30},{16,0},... | collective-permute-start | bytes 589832 | tf_op jit(solution)/shard_map/ppermute | solution.py:358
  41.4 1.0 collective-permute-start.7
  42.4 6.4 %collective-permute-done.8 = f32[1,3,64,256]{3,2,1,0:T(8,128)S(1)} collective-permute-done((f32[1,3,64,256]{3,2,1,0:T(8,128)S(1)}, f32[1,3,64,256]{3,2,1,0:T(8,128)S(1)}, u32[]{:S(2)}, u32[]{:S(2)}) %collective-permute-start.8) | collective-permute-done | bytes 196640 | tf_op jit(solution)/shard_map/ppermute | solution.py:358
  48.8 0.9 collective-permute-done.7
  50.1 2.6 %collective-permute-start.14 = (f32[1,3,64,256]{3,2,1,0:T(8,128)S(1)}, f32[1,3,64,256]{3,2,1,0:T(8,128)S(1)}, u32[]{:S(2)}, u32[]{:S(2)}) collective-permute-start(f32[1,3,64,256]{3,2,1,0:T(8,128)S(1)} %add_add_fusion.1.refs_5_), channel_id=1, source_target_pairs={{0,16},{2,18},{4,20},{6,22},{8,24},{10,26},{12,28},{14,30},{16,0},... | collective-permute-start | bytes 589832 | tf_op jit(solution)/shard_map/ppermute | solution.py:358
  53.3 2.4 %collective-permute-start.12 = (f32[256,256]{1,0:T(8,128)S(1)}, f32[256,256]{1,0:T(8,128)S(1)}, u32[]{:S(2)}, u32[]{:S(2)}) collective-permute-start(f32[256,256]{1,0:T(8,128)S(1)} %get-tuple-element.155), channel_id=1, source_target_pairs={{0,6},{2,4},{4,2},{6,0},{8,14},{10,12},{12,10},{14,8},{16,22},{18,... | collective-permute-start | bytes 786440 | tf_op jit(solution)/shard_map/ppermute | solution.py:358
  55.7 0.8 collective-permute-start.13
  56.5 3.3 %collective-permute-done.14.refs_7_ = f32[1,3,64,256]{3,2,1,0:T(8,128)S(1)} collective-permute-done((f32[1,3,64,256]{3,2,1,0:T(8,128)S(1)}, f32[1,3,64,256]{3,2,1,0:T(8,128)S(1)}, u32[]{:S(2)}, u32[]{:S(2)}) %collective-permute-start.14) | collective-permute-done | bytes 196640 | tf_op jit(solution)/shard_map/ppermute | solution.py:358
  60.0 3.0 %collective-permute-done.13.refs_6_ = f32[1,3,64,256]{3,2,1,0:T(8,128)S(1)} collective-permute-done((f32[1,3,64,256]{3,2,1,0:T(8,128)S(1)}, f32[1,3,64,256]{3,2,1,0:T(8,128)S(1)}, u32[]{:S(2)}, u32[]{:S(2)}) %collective-permute-start.13) | collective-permute-done | bytes 196640 | tf_op jit(solution)/shard_map/ppermute | solution.py:358
  63.0 1.7 %collective-permute-done.12.refs_4_.refs_8_ = f32[256,256]{1,0:T(8,128)S(1)} collective-permute-done((f32[256,256]{1,0:T(8,128)S(1)}, f32[256,256]{1,0:T(8,128)S(1)}, u32[]{:S(2)}, u32[]{:S(2)}) %collective-permute-start.12) | collective-permute-done | bytes 262176 | tf_op jit(solution)/shard_map/ppermute | solution.py:358
  64.7 1.4 collective-permute-done.15.refs_8_
  66.1 1.8 %shard_map.149 = (f32[4,256,256]{2,1,0:T(8,128)S(1)}, f32[4,256,256]{2,1,0:T(8,128)S(1)}, bf16[4,256,256]{2,1,0:T(8,128)(2,1)S(1)}, f32[4,256,256]{2,1,0:T(8,128...) custom-call(s32[2]{0:T(128)S(1)} %pad_add_fusion.place, f32[8,256]{1,0:T(8,128)S(1)} %get-tuple-element.131.scale_row, ...), custom_call_target="tpu_custom_call" | custom-call | flops 402653184 | bytes 6963208 | tf_op jit(solution)/shard_map/pallas_call | solution.py:34
  67.9 1.2 collective-permute-done.16
  69.1 1.5 %collective-permute-start.19 = (f32[2,4,256]{2,1,0:T(4,128)S(1)}, f32[2,4,256]{2,1,0:T(4,128)S(1)}, u32[]{:S(2)}, u32[]{:S(2)}) collective-permute-start(f32[2,4,256]{2,1,0:T(4,128)S(1)} %add.36.refs_0_), channel_id=1, source_target_pairs={{0,6},{2,4},{4,2},{6,0},{8,14},{10,12},{12,10},{14,8},{16,22},{18,... | collective-permute-start | bytes 24584 | tf_op jit(solution)/shard_map/ppermute | solution.py:358
  71.1 1.5 %collective-permute-start.17 = (f32[2,4,256]{2,1,0:T(4,128)S(1)}, f32[2,4,256]{2,1,0:T(4,128)S(1)}, u32[]{:S(2)}, u32[]{:S(2)}) collective-permute-start(f32[2,4,256]{2,1,0:T(4,128)S(1)} %add.36.refs_0_), channel_id=1, source_target_pairs={{0,2},{2,0},{4,6},{6,4},{8,10},{10,8},{12,14},{14,12},{16,18},{18,... | collective-permute-start | bytes 24584 | tf_op jit(solution)/shard_map/ppermute | solution.py:358
  72.6 1.1 collective-permute-done.19.refs_3_
  74.7 2.1 %shard_map.150 = (bf16[4,256,256]{2,1,0:T(8,128)(2,1)S(1)}, bf16[4,256,256]{2,1,0:T(8,128)(2,1)S(1)}, f32[1,3,64,256]{3,2,1,0:T(8,128)S(1)}, f32[1,3,64,256]{3,2...) custom-call(s32[2]{0:T(128)S(1)} %pad_add_fusion.place, ...), custom_call_target="tpu_custom_call" | custom-call | flops 805306368 | bytes 8036360 | tf_op jit(solution)/shard_map/pallas_call | solution.py:34
  76.9 0.8 collective-permute-start.20
  77.7 4.9 %collective-permute-done.20 = f32[1,3,64,256]{3,2,1,0:T(8,128)S(1)} collective-permute-done((f32[1,3,64,256]{3,2,1,0:T(8,128)S(1)}, f32[1,3,64,256]{3,2,1,0:T(8,128)S(1)}, u32[]{:S(2)}, u32[]{:S(2)}) %collective-permute-start.20) | collective-permute-done | bytes 196640 | tf_op jit(solution)/shard_map/ppermute | solution.py:358
  82.6 2.0 %collective-permute-start.22 = (f32[1,3,64,256]{3,2,1,0:T(8,128)S(1)}, f32[1,3,64,256]{3,2,1,0:T(8,128)S(1)}, u32[]{:S(2)}, u32[]{:S(2)}) collective-permute-start(f32[1,3,64,256]{3,2,1,0:T(8,128)S(1)} %add.38), channel_id=1, source_target_pairs={{0,16},{2,18},{4,20},{6,22},{8,24},{10,26},{12,28},{14,30},{16,0},... | collective-permute-start | bytes 589832 | tf_op jit(solution)/shard_map/ppermute | solution.py:358
  84.6 1.9 %collective-permute-start.21 = (f32[1,3,64,256]{3,2,1,0:T(8,128)S(1)}, f32[1,3,64,256]{3,2,1,0:T(8,128)S(1)}, u32[]{:S(2)}, u32[]{:S(2)}) collective-permute-start(f32[1,3,64,256]{3,2,1,0:T(8,128)S(1)} %get-tuple-element.172), channel_id=1, source_target_pairs={{0,8},{2,10},{4,12},{6,14},{8,0},{10,2},{12,4},{14,6},{16,24},{18,... | collective-permute-start | bytes 589832 | tf_op jit(solution)/shard_map/ppermute | solution.py:358
  86.5 5.9 %collective-permute-done.22 = f32[1,3,64,256]{3,2,1,0:T(8,128)S(1)} collective-permute-done((f32[1,3,64,256]{3,2,1,0:T(8,128)S(1)}, f32[1,3,64,256]{3,2,1,0:T(8,128)S(1)}, u32[]{:S(2)}, u32[]{:S(2)}) %collective-permute-start.22) | collective-permute-done | bytes 196640 | tf_op jit(solution)/shard_map/ppermute | solution.py:358
  93.7 1.0 collective-permute-start.26
  94.7 1.3 collective-permute-start.27
  96.1 1.2 collective-permute-start.28
  97.3 2.3 %collective-permute-start.23 = (f32[1,3,64,256]{3,2,1,0:T(8,128)S(1)}, f32[1,3,64,256]{3,2,1,0:T(8,128)S(1)}, u32[]{:S(2)}, u32[]{:S(2)}) collective-permute-start(f32[1,3,64,256]{3,2,1,0:T(8,128)S(1)} %add_add_fusion.refs_11_.refs_0_), channel_id=1, source_target_pairs={{0,8},{2,10},{4,12},{6,14},{8,0},{10,2},{12,4},{14,6},{16,24},{18,... | collective-permute-start | bytes 589832 | tf_op jit(solution)/shard_map/ppermute | solution.py:358
  99.6 3.2 %collective-permute-done.24.refs_13_ = f32[1,3,64,256]{3,2,1,0:T(8,128)S(1)} collective-permute-done((f32[1,3,64,256]{3,2,1,0:T(8,128)S(1)}, f32[1,3,64,256]{3,2,1,0:T(8,128)S(1)}, u32[]{:S(2)}, u32[]{:S(2)}) %collective-permute-start.24) | collective-permute-done | bytes 196640 | tf_op jit(solution)/shard_map/ppermute | solution.py:358
  102.8 1.0 shard_map.153
  103.8 1.3 collective-permute-done.27.refs_2_
  105.2 1.5 %collective-permute-done.28.refs_3_ = f32[256,256]{1,0:T(8,128)S(1)} collective-permute-done((f32[256,256]{1,0:T(8,128)S(1)}, f32[256,256]{1,0:T(8,128)S(1)}, u32[]{:S(2)}, u32[]{:S(2)}) %collective-permute-start.28) | collective-permute-done | bytes 262176 | tf_op jit(solution)/shard_map/ppermute | solution.py:358
  106.7 1.7 %shard_map.152 = bf16[256,4,256]{2,1,0:T(4,128)(2,1)} custom-call(s32[2]{0:T(128)S(1)} %pad_add_fusion.place, f32[256,256]{1,0:T(8,128)S(1)} %get-tuple-element.177.refs_0_, f32[256,256]{1,0:T(8,128)S(1)} %collective-permute-done.26.refs_1_, f32[256,256]{1,0:T(8,128)S(1)} %collective-permute-done.27.refs_2_, f32[256,256]{1,0:T(8,128)S(1)} %collective-permute-done.28.refs_3_), custom_call_target="tpu_custom_call" | custom-call | flops 8388608 | bytes 1572872 | tf_op jit(solution)/shard_map/pallas_call | solution.py:34
  108.5 1.0 collective-permute-done.25.refs_14_
  109.5 3.0 %shard_map.154 = (f32[2,256,256]{2,1,0:T(8,128)S(1)}, f32[3,256,256]{2,1,0:T(8,128)S(1)}, f32[3,256,256]{2,1,0:T(8,128)S(1)}, f32[1,3,64,256]{3,2,1,0:T(8,128)S(...) custom-call(s32[2]{0:T(128)S(1)} %pad_add_fusion.place, ...), custom_call_target="tpu_custom_call" | custom-call | flops 1610612736 | bytes 13369352 | tf_op jit(solution)/shard_map/pallas_call | solution.py:34
  112.5 1.9 %collective-permute-start.32 = (f32[3,256,256]{2,1,0:T(8,128)S(1)}, f32[3,256,256]{2,1,0:T(8,128)S(1)}, u32[]{:S(2)}, u32[]{:S(2)}) collective-permute-start(f32[3,256,256]{2,1,0:T(8,128)S(1)} %get-tuple-element.213), channel_id=1, source_target_pairs={{0,2},{2,0},{4,6},{6,4},{8,10},{10,8},{12,14},{14,12},{16,18},{18,... | collective-permute-start | bytes 2359304 | tf_op jit(solution)/shard_map/ppermute | solution.py:358
  114.6 1.5 %collective-permute-start.29 = (f32[1,3,64,256]{3,2,1,0:T(8,128)S(1)}, f32[1,3,64,256]{3,2,1,0:T(8,128)S(1)}, u32[]{:S(2)}, u32[]{:S(2)}) collective-permute-start(f32[1,3,64,256]{3,2,1,0:T(8,128)S(1)} %get-tuple-element.207), channel_id=1, source_target_pairs={{0,8},{2,10},{4,12},{6,14},{8,0},{10,2},{12,4},{14,6},{16,24},{18,... | collective-permute-start | bytes 589832 | tf_op jit(solution)/shard_map/ppermute | solution.py:358
  116.1 4.4 %collective-permute-done.29 = f32[1,3,64,256]{3,2,1,0:T(8,128)S(1)} collective-permute-done((f32[1,3,64,256]{3,2,1,0:T(8,128)S(1)}, f32[1,3,64,256]{3,2,1,0:T(8,128)S(1)}, u32[]{:S(2)}, u32[]{:S(2)}) %collective-permute-start.29) | collective-permute-done | bytes 196640 | tf_op jit(solution)/shard_map/ppermute | solution.py:358
  120.5 1.7 %collective-permute-start.31 = (f32[1,3,64,256]{3,2,1,0:T(8,128)S(1)}, f32[1,3,64,256]{3,2,1,0:T(8,128)S(1)}, u32[]{:S(2)}, u32[]{:S(2)}) collective-permute-start(f32[1,3,64,256]{3,2,1,0:T(8,128)S(1)} %add.40), channel_id=1, source_target_pairs={{0,16},{2,18},{4,20},{6,22},{8,24},{10,26},{12,28},{14,30},{16,0},... | collective-permute-start | bytes 589832 | tf_op jit(solution)/shard_map/ppermute | solution.py:358
  122.2 0.9 collective-permute-start.30
  123.1 7.1 %collective-permute-done.31.refs_3_ = f32[1,3,64,256]{3,2,1,0:T(8,128)S(1)} collective-permute-done((f32[1,3,64,256]{3,2,1,0:T(8,128)S(1)}, f32[1,3,64,256]{3,2,1,0:T(8,128)S(1)}, u32[]{:S(2)}, u32[]{:S(2)}) %collective-permute-start.31) | collective-permute-done | bytes 196640 | tf_op jit(solution)/shard_map/ppermute | solution.py:358
  130.2 0.9 collective-permute-done.32.refs_1_
  131.2 1.5 %collective-permute-done.33.refs_2_ = f32[3,256,256]{2,1,0:T(8,128)S(1)} collective-permute-done((f32[3,256,256]{2,1,0:T(8,128)S(1)}, f32[3,256,256]{2,1,0:T(8,128)S(1)}, u32[]{:S(2)}, u32[]{:S(2)}) %collective-permute-start.33) | collective-permute-done | bytes 786464 | tf_op jit(solution)/shard_map/ppermute | solution.py:358
  133.5 1.7 %collective-permute-start.37 = (f32[256,256]{1,0:T(8,128)S(1)}, f32[256,256]{1,0:T(8,128)S(1)}, u32[]{:S(2)}, u32[]{:S(2)}) collective-permute-start(f32[256,256]{1,0:T(8,128)S(1)} %slice_bitcast_fusion.1), channel_id=1, source_target_pairs={{0,4},{2,6},{4,0},{6,2},{8,12},{10,14},{12,8},{14,10},{16,20},{18,... | collective-permute-start | bytes 786440 | tf_op jit(solution)/shard_map/ppermute | solution.py:358
  136.2 1.3 collective-permute-start.35
  137.5 1.9 %collective-permute-start.36 = (f32[1,3,16,256]{3,2,1,0:T(8,128)S(1)}, f32[1,3,16,256]{3,2,1,0:T(8,128)S(1)}, u32[]{:S(2)}, u32[]{:S(2)}) collective-permute-start(f32[1,3,16,256]{3,2,1,0:T(8,128)S(1)} %get-tuple-element.221), channel_id=1, source_target_pairs={{0,6},{2,4},{4,2},{6,0},{8,14},{10,12},{12,10},{14,8},{16,22},{18,... | collective-permute-start | bytes 147464 | tf_op jit(solution)/shard_map/ppermute | solution.py:358
  140.0 0.8 collective-permute-done.37.refs_3_
  140.8 2.4 %shard_map.156 = (bf16[256,4,256]{2,1,0:T(4,128)(2,1)}, bf16[256,4,256]{2,1,0:T(4,128)(2,1)}) custom-call(s32[2]{0:T(128)S(1)} %pad_add_fusion.place, f32[4,256]{1,0:T(4,128)S(1)} %bitcast.24, f32[2,256,256]{2,1,0:T(8,128)S(1)} %get-tuple-element.222.refs_0_, f32[3,256,256]{2,1,0:T(8,128)S(1)} %collective-permute-done.32.refs_1_, ...), custom_call_target="tpu_custom_call" | custom-call | flops 16777216 | bytes 3674120 | tf_op jit(solution)/shard_map/pallas_call | solution.py:34
  143.2 1.2 shard_map.157
  (59 shorter events, 8.6 us)
Async XLA Ops:
  0.6 15.3 %copy-start = (f32[4,256,256]{2,1,0:T(8,128)S(1)}, f32[4,256,256]{2,1,0:T(8,128)}, u32[]{:S(2)}) copy-start(f32[4,256,256]{2,1,0:T(8,128)} %param.16) | copy-start | bytes 3145732
  0.7 1.1 copy-start.5
  1.8 5.5 %copy-start.6 = (bf16[1,256,4,256]{3,2,1,0:T(4,128)(2,1)S(1)}, bf16[1,256,4,256]{3,2,1,0:T(4,128)(2,1)}, u32[]{:S(2)}) copy-start(bf16[1,256,4,256]{3,2,1,0:T(4,128)(2,1)} %param.12) | copy-start | bytes 1572868
  2.7 4.6 %copy-start.4 = (f32[1,4,256]{2,1,0:T(4,128)S(1)}, f32[1,4,256]{2,1,0:T(4,128)}, u32[]{:S(2)}) copy-start(f32[1,4,256]{2,1,0:T(4,128)} %param.13) | copy-start | bytes 12292
  2.8 10.5 %collective-permute-start = (f32[256,256]{1,0:T(8,128)S(1)}, f32[256,256]{1,0:T(8,128)S(1)}, u32[]{:S(2)}, u32[]{:S(2)}) collective-permute-start(f32[256,256]{1,0:T(8,128)S(1)} %get-tuple-element.122), channel_id=1, source_target_pairs={{0,2},{2,0},{4,6},{6,4},{8,10},{10,8},{12,14},{14,12},{16,18},{18,... | collective-permute-start | bytes 786440 | tf_op jit(solution)/shard_map/ppermute | solution.py:358
  5.8 14.0 %collective-permute-start.1 = (f32[256,256]{1,0:T(8,128)S(1)}, f32[256,256]{1,0:T(8,128)S(1)}, u32[]{:S(2)}, u32[]{:S(2)}) collective-permute-start(f32[256,256]{1,0:T(8,128)S(1)} %get-tuple-element.123), channel_id=1, source_target_pairs={{0,4},{2,6},{4,0},{6,2},{8,12},{10,14},{12,8},{14,10},{16,20},{18,... | collective-permute-start | bytes 786440 | tf_op jit(solution)/shard_map/ppermute | solution.py:358
  7.3 12.8 %collective-permute-start.2 = (f32[256,256]{1,0:T(8,128)S(1)}, f32[256,256]{1,0:T(8,128)S(1)}, u32[]{:S(2)}, u32[]{:S(2)}) collective-permute-start(f32[256,256]{1,0:T(8,128)S(1)} %get-tuple-element.124), channel_id=1, source_target_pairs={{0,6},{2,4},{4,2},{6,0},{8,14},{10,12},{12,10},{14,8},{16,22},{18,... | collective-permute-start | bytes 786440 | tf_op jit(solution)/shard_map/ppermute | solution.py:358
  9.1 0.7 copy-start.7
  9.8 14.4 %collective-permute-start.3 = (f32[256,256]{1,0:T(8,128)}, f32[256,256]{1,0:T(8,128)S(1)}, u32[]{:S(2)}, u32[]{:S(2)}) collective-permute-start(f32[256,256]{1,0:T(8,128)} %get-tuple-element.126), channel_id=1, source_target_pairs={{0,2},{2,0},{4,6},{6,4},{8,10},{10,8},{12,14},{14,12},{16,18},{18,... | collective-permute-start | bytes 786440 | tf_op jit(solution)/shard_map/ppermute | solution.py:358
  11.7 18.7 %collective-permute-start.4 = (f32[256,256]{1,0:T(8,128)}, f32[256,256]{1,0:T(8,128)S(1)}, u32[]{:S(2)}, u32[]{:S(2)}) collective-permute-start(f32[256,256]{1,0:T(8,128)} %get-tuple-element.127), channel_id=1, source_target_pairs={{0,4},{2,6},{4,0},{6,2},{8,12},{10,14},{12,8},{14,10},{16,20},{18,... | collective-permute-start | bytes 786440 | tf_op jit(solution)/shard_map/ppermute | solution.py:358
  13.2 17.1 %collective-permute-start.5 = (f32[256,256]{1,0:T(8,128)S(1)}, f32[256,256]{1,0:T(8,128)S(1)}, u32[]{:S(2)}, u32[]{:S(2)}) collective-permute-start(f32[256,256]{1,0:T(8,128)S(1)} %get-tuple-element.128), channel_id=1, source_target_pairs={{0,6},{2,4},{4,2},{6,0},{8,14},{10,12},{12,10},{14,8},{16,22},{18,... | collective-permute-start | bytes 786440 | tf_op jit(solution)/shard_map/ppermute | solution.py:358
  15.9 14.5 %copy-start.8 = (bf16[256,256]{1,0:T(8,128)(2,1)S(1)}, bf16[256,256]{1,0:T(8,128)(2,1)}, u32[]{:S(2)}) copy-start(bf16[256,256]{1,0:T(8,128)(2,1)} %copy-done.7) | copy-start | bytes 393220
  30.4 4.2 %copy-start.1 = (bf16[1,256,4,256]{3,2,1,0:T(4,128)(2,1)S(1)}, bf16[1,256,4,256]{3,2,1,0:T(4,128)(2,1)}, u32[]{:S(2)}) copy-start(bf16[1,256,4,256]{3,2,1,0:T(4,128)(2,1)} %param.10) | copy-start | bytes 1572868
  30.4 4.2 %copy-start.2 = (bf16[1,256,4,256]{3,2,1,0:T(4,128)(2,1)S(1)}, bf16[1,256,4,256]{3,2,1,0:T(4,128)(2,1)}, u32[]{:S(2)}) copy-start(bf16[1,256,4,256]{3,2,1,0:T(4,128)(2,1)} %param.19) | copy-start | bytes 1572868
  32.4 1.7 %copy-start.9 = (f32[4]{0:T(128)S(1)}, f32[4]{0:T(128)}, u32[]{:S(2)}) copy-start(f32[4]{0:T(128)} %param.14) | copy-start | bytes 52
  32.4 2.2 %copy-start.3 = (f32[4,256]{1,0:T(4,128)S(1)}, f32[4,256]{1,0:T(4,128)}, u32[]{:S(2)}) copy-start(f32[4,256]{1,0:T(4,128)} %gain.1) | copy-start | bytes 12292
  32.4 6.3 %collective-permute-start.6 = (f32[1,3,64,256]{3,2,1,0:T(8,128)S(1)}, f32[1,3,64,256]{3,2,1,0:T(8,128)S(1)}, u32[]{:S(2)}, u32[]{:S(2)}) collective-permute-start(f32[1,3,64,256]{3,2,1,0:T(8,128)S(1)} %get-tuple-element.141), channel_id=1, source_target_pairs={{0,8},{2,10},{4,12},{6,14},{8,0},{10,2},{12,4},{14,6},{16,24},{18,... | collective-permute-start | bytes 589832 | tf_op jit(solution)/shard_map/ppermute | solution.py:358
  36.6 13.1 %collective-permute-start.9 = (f32[2,256,256]{2,1,0:T(8,128)S(1)}, f32[2,256,256]{2,1,0:T(8,128)S(1)}, u32[]{:S(2)}, u32[]{:S(2)}) collective-permute-start(f32[2,256,256]{2,1,0:T(8,128)S(1)} %get-tuple-element.147), channel_id=1, source_target_pairs={{0,2},{2,0},{4,6},{6,4},{8,10},{10,8},{12,14},{14,12},{16,18},{18,... | collective-permute-start | bytes 1572872 | tf_op jit(solution)/shard_map/ppermute | solution.py:358
  37.9 12.2 %collective-permute-start.10 = (f32[2,256,256]{2,1,0:T(8,128)S(1)}, f32[2,256,256]{2,1,0:T(8,128)S(1)}, u32[]{:S(2)}, u32[]{:S(2)}) collective-permute-start(f32[2,256,256]{2,1,0:T(8,128)S(1)} %get-tuple-element.148), channel_id=1, source_target_pairs={{0,4},{2,6},{4,0},{6,2},{8,12},{10,14},{12,8},{14,10},{16,20},{18,... | collective-permute-start | bytes 1572872 | tf_op jit(solution)/shard_map/ppermute | solution.py:358
  38.7 10.0 %collective-permute-start.8 = (f32[1,3,64,256]{3,2,1,0:T(8,128)S(1)}, f32[1,3,64,256]{3,2,1,0:T(8,128)S(1)}, u32[]{:S(2)}, u32[]{:S(2)}) collective-permute-start(f32[1,3,64,256]{3,2,1,0:T(8,128)S(1)} %add.34), channel_id=1, source_target_pairs={{0,16},{2,18},{4,20},{6,22},{8,24},{10,26},{12,28},{14,30},{16,0},... | collective-permute-start | bytes 589832 | tf_op jit(solution)/shard_map/ppermute | solution.py:358
  41.4 8.2 %collective-permute-start.7 = (f32[1,3,64,256]{3,2,1,0:T(8,128)S(1)}, f32[1,3,64,256]{3,2,1,0:T(8,128)S(1)}, u32[]{:S(2)}, u32[]{:S(2)}) collective-permute-start(f32[1,3,64,256]{3,2,1,0:T(8,128)S(1)} %get-tuple-element.143), channel_id=1, source_target_pairs={{0,8},{2,10},{4,12},{6,14},{8,0},{10,2},{12,4},{14,6},{16,24},{18,... | collective-permute-start | bytes 589832 | tf_op jit(solution)/shard_map/ppermute | solution.py:358
  50.1 9.7 %collective-permute-start.14 = (f32[1,3,64,256]{3,2,1,0:T(8,128)S(1)}, f32[1,3,64,256]{3,2,1,0:T(8,128)S(1)}, u32[]{:S(2)}, u32[]{:S(2)}) collective-permute-start(f32[1,3,64,256]{3,2,1,0:T(8,128)S(1)} %add_add_fusion.1.refs_5_), channel_id=1, source_target_pairs={{0,16},{2,18},{4,20},{6,22},{8,24},{10,26},{12,28},{14,30},{16,0},... | collective-permute-start | bytes 589832 | tf_op jit(solution)/shard_map/ppermute | solution.py:358
  52.7 10.3 %collective-permute-start.11 = (f32[256,256]{1,0:T(8,128)S(1)}, f32[256,256]{1,0:T(8,128)S(1)}, u32[]{:S(2)}, u32[]{:S(2)}) collective-permute-start(f32[256,256]{1,0:T(8,128)S(1)} %get-tuple-element.154), channel_id=1, source_target_pairs={{0,6},{2,4},{4,2},{6,0},{8,14},{10,12},{12,10},{14,8},{16,22},{18,... | collective-permute-start | bytes 786440 | tf_op jit(solution)/shard_map/ppermute | solution.py:358
  53.3 11.4 %collective-permute-start.12 = (f32[256,256]{1,0:T(8,128)S(1)}, f32[256,256]{1,0:T(8,128)S(1)}, u32[]{:S(2)}, u32[]{:S(2)}) collective-permute-start(f32[256,256]{1,0:T(8,128)S(1)} %get-tuple-element.155), channel_id=1, source_target_pairs={{0,6},{2,4},{4,2},{6,0},{8,14},{10,12},{12,10},{14,8},{16,22},{18,... | collective-permute-start | bytes 786440 | tf_op jit(solution)/shard_map/ppermute | solution.py:358
  55.7 7.3 %collective-permute-start.13 = (f32[1,3,64,256]{3,2,1,0:T(8,128)S(1)}, f32[1,3,64,256]{3,2,1,0:T(8,128)S(1)}, u32[]{:S(2)}, u32[]{:S(2)}) collective-permute-start(f32[1,3,64,256]{3,2,1,0:T(8,128)S(1)} %add_add_fusion.1.refs_5_), channel_id=1, source_target_pairs={{0,8},{2,10},{4,12},{6,14},{8,0},{10,2},{12,4},{14,6},{16,24},{18,... | collective-permute-start | bytes 589832 | tf_op jit(solution)/shard_map/ppermute | solution.py:358
  59.8 6.3 %collective-permute-start.15 = (f32[1,3,64,256]{3,2,1,0:T(8,128)S(1)}, f32[1,3,64,256]{3,2,1,0:T(8,128)S(1)}, u32[]{:S(2)}, u32[]{:S(2)}) collective-permute-start(f32[1,3,64,256]{3,2,1,0:T(8,128)S(1)} %collective-permute-done.14.refs_7_), channel_id=1, source_target_pairs={{0,8},{2,10},{4,12},{6,14},{8,0},{10,2},{12,4},{14,6},{16,24},{18,... | collective-permute-start | bytes 589832 | tf_op jit(solution)/shard_map/ppermute | solution.py:358
  67.9 1.2 collective-permute-start.16
  69.1 4.5 %collective-permute-start.19 = (f32[2,4,256]{2,1,0:T(4,128)S(1)}, f32[2,4,256]{2,1,0:T(4,128)S(1)}, u32[]{:S(2)}, u32[]{:S(2)}) collective-permute-start(f32[2,4,256]{2,1,0:T(4,128)S(1)} %add.36.refs_0_), channel_id=1, source_target_pairs={{0,6},{2,4},{4,2},{6,0},{8,14},{10,12},{12,10},{14,8},{16,22},{18,... | collective-permute-start | bytes 24584 | tf_op jit(solution)/shard_map/ppermute | solution.py:358
  70.6 3.7 %collective-permute-start.18 = (f32[2,4,256]{2,1,0:T(4,128)S(1)}, f32[2,4,256]{2,1,0:T(4,128)S(1)}, u32[]{:S(2)}, u32[]{:S(2)}) collective-permute-start(f32[2,4,256]{2,1,0:T(4,128)S(1)} %add.36.refs_0_), channel_id=1, source_target_pairs={{0,4},{2,6},{4,0},{6,2},{8,12},{10,14},{12,8},{14,10},{16,20},{18,... | collective-permute-start | bytes 24584 | tf_op jit(solution)/shard_map/ppermute | solution.py:358
  71.1 3.7 %collective-permute-start.17 = (f32[2,4,256]{2,1,0:T(4,128)S(1)}, f32[2,4,256]{2,1,0:T(4,128)S(1)}, u32[]{:S(2)}, u32[]{:S(2)}) collective-permute-start(f32[2,4,256]{2,1,0:T(4,128)S(1)} %add.36.refs_0_), channel_id=1, source_target_pairs={{0,2},{2,0},{4,6},{6,4},{8,10},{10,8},{12,14},{14,12},{16,18},{18,... | collective-permute-start | bytes 24584 | tf_op jit(solution)/shard_map/ppermute | solution.py:358
  76.9 5.7 %collective-permute-start.20 = (f32[1,3,64,256]{3,2,1,0:T(8,128)S(1)}, f32[1,3,64,256]{3,2,1,0:T(8,128)S(1)}, u32[]{:S(2)}, u32[]{:S(2)}) collective-permute-start(f32[1,3,64,256]{3,2,1,0:T(8,128)S(1)} %get-tuple-element.170), channel_id=1, source_target_pairs={{0,8},{2,10},{4,12},{6,14},{8,0},{10,2},{12,4},{14,6},{16,24},{18,... | collective-permute-start | bytes 589832 | tf_op jit(solution)/shard_map/ppermute | solution.py:358
  82.6 9.7 %collective-permute-start.22 = (f32[1,3,64,256]{3,2,1,0:T(8,128)S(1)}, f32[1,3,64,256]{3,2,1,0:T(8,128)S(1)}, u32[]{:S(2)}, u32[]{:S(2)}) collective-permute-start(f32[1,3,64,256]{3,2,1,0:T(8,128)S(1)} %add.38), channel_id=1, source_target_pairs={{0,16},{2,18},{4,20},{6,22},{8,24},{10,26},{12,28},{14,30},{16,0},... | collective-permute-start | bytes 589832 | tf_op jit(solution)/shard_map/ppermute | solution.py:358
  84.6 8.0 %collective-permute-start.21 = (f32[1,3,64,256]{3,2,1,0:T(8,128)S(1)}, f32[1,3,64,256]{3,2,1,0:T(8,128)S(1)}, u32[]{:S(2)}, u32[]{:S(2)}) collective-permute-start(f32[1,3,64,256]{3,2,1,0:T(8,128)S(1)} %get-tuple-element.172), channel_id=1, source_target_pairs={{0,8},{2,10},{4,12},{6,14},{8,0},{10,2},{12,4},{14,6},{16,24},{18,... | collective-permute-start | bytes 589832 | tf_op jit(solution)/shard_map/ppermute | solution.py:358
  92.6 10.1 %collective-permute-start.24 = (f32[1,3,64,256]{3,2,1,0:T(8,128)S(1)}, f32[1,3,64,256]{3,2,1,0:T(8,128)S(1)}, u32[]{:S(2)}, u32[]{:S(2)}) collective-permute-start(f32[1,3,64,256]{3,2,1,0:T(8,128)S(1)} %add_add_fusion.refs_11_.refs_0_), channel_id=1, source_target_pairs={{0,16},{2,18},{4,20},{6,22},{8,24},{10,26},{12,28},{14,30},{16,0},... | collective-permute-start | bytes 589832 | tf_op jit(solution)/shard_map/ppermute | solution.py:358
  93.7 10.1 %collective-permute-start.26 = (f32[256,256]{1,0:T(8,128)S(1)}, f32[256,256]{1,0:T(8,128)S(1)}, u32[]{:S(2)}, u32[]{:S(2)}) collective-permute-start(f32[256,256]{1,0:T(8,128)S(1)} %get-tuple-element.178), channel_id=1, source_target_pairs={{0,2},{2,0},{4,6},{6,4},{8,10},{10,8},{12,14},{14,12},{16,18},{18,... | collective-permute-start | bytes 786440 | tf_op jit(solution)/shard_map/ppermute | solution.py:358
  94.7 10.4 %collective-permute-start.27 = (f32[256,256]{1,0:T(8,128)S(1)}, f32[256,256]{1,0:T(8,128)S(1)}, u32[]{:S(2)}, u32[]{:S(2)}) collective-permute-start(f32[256,256]{1,0:T(8,128)S(1)} %get-tuple-element.179), channel_id=1, source_target_pairs={{0,4},{2,6},{4,0},{6,2},{8,12},{10,14},{12,8},{14,10},{16,20},{18,... | collective-permute-start | bytes 786440 | tf_op jit(solution)/shard_map/ppermute | solution.py:358
  96.1 10.6 %collective-permute-start.28 = (f32[256,256]{1,0:T(8,128)S(1)}, f32[256,256]{1,0:T(8,128)S(1)}, u32[]{:S(2)}, u32[]{:S(2)}) collective-permute-start(f32[256,256]{1,0:T(8,128)S(1)} %get-tuple-element.180), channel_id=1, source_target_pairs={{0,6},{2,4},{4,2},{6,0},{8,14},{10,12},{12,10},{14,8},{16,22},{18,... | collective-permute-start | bytes 786440 | tf_op jit(solution)/shard_map/ppermute | solution.py:358
  97.3 11.2 %collective-permute-start.23 = (f32[1,3,64,256]{3,2,1,0:T(8,128)S(1)}, f32[1,3,64,256]{3,2,1,0:T(8,128)S(1)}, u32[]{:S(2)}, u32[]{:S(2)}) collective-permute-start(f32[1,3,64,256]{3,2,1,0:T(8,128)S(1)} %add_add_fusion.refs_11_.refs_0_), channel_id=1, source_target_pairs={{0,8},{2,10},{4,12},{6,14},{8,0},{10,2},{12,4},{14,6},{16,24},{18,... | collective-permute-start | bytes 589832 | tf_op jit(solution)/shard_map/ppermute | solution.py:358
  102.8 6.7 %collective-permute-start.25 = (f32[1,3,64,256]{3,2,1,0:T(8,128)S(1)}, f32[1,3,64,256]{3,2,1,0:T(8,128)S(1)}, u32[]{:S(2)}, u32[]{:S(2)}) collective-permute-start(f32[1,3,64,256]{3,2,1,0:T(8,128)S(1)} %collective-permute-done.24.refs_13_), channel_id=1, source_target_pairs={{0,8},{2,10},{4,12},{6,14},{8,0},{10,2},{12,4},{14,6},{16,24},{18,... | collective-permute-start | bytes 589832 | tf_op jit(solution)/shard_map/ppermute | solution.py:358
  112.5 18.6 %collective-permute-start.32 = (f32[3,256,256]{2,1,0:T(8,128)S(1)}, f32[3,256,256]{2,1,0:T(8,128)S(1)}, u32[]{:S(2)}, u32[]{:S(2)}) collective-permute-start(f32[3,256,256]{2,1,0:T(8,128)S(1)} %get-tuple-element.213), channel_id=1, source_target_pairs={{0,2},{2,0},{4,6},{6,4},{8,10},{10,8},{12,14},{14,12},{16,18},{18,... | collective-permute-start | bytes 2359304 | tf_op jit(solution)/shard_map/ppermute | solution.py:358
  114.4 18.2 %collective-permute-start.33 = (f32[3,256,256]{2,1,0:T(8,128)S(1)}, f32[3,256,256]{2,1,0:T(8,128)S(1)}, u32[]{:S(2)}, u32[]{:S(2)}) collective-permute-start(f32[3,256,256]{2,1,0:T(8,128)S(1)} %get-tuple-element.214), channel_id=1, source_target_pairs={{0,4},{2,6},{4,0},{6,2},{8,12},{10,14},{12,8},{14,10},{16,20},{18,... | collective-permute-start | bytes 2359304 | tf_op jit(solution)/shard_map/ppermute | solution.py:358
  114.6 5.9 %collective-permute-start.29 = (f32[1,3,64,256]{3,2,1,0:T(8,128)S(1)}, f32[1,3,64,256]{3,2,1,0:T(8,128)S(1)}, u32[]{:S(2)}, u32[]{:S(2)}) collective-permute-start(f32[1,3,64,256]{3,2,1,0:T(8,128)S(1)} %get-tuple-element.207), channel_id=1, source_target_pairs={{0,8},{2,10},{4,12},{6,14},{8,0},{10,2},{12,4},{14,6},{16,24},{18,... | collective-permute-start | bytes 589832 | tf_op jit(solution)/shard_map/ppermute | solution.py:358
  120.5 9.7 %collective-permute-start.31 = (f32[1,3,64,256]{3,2,1,0:T(8,128)S(1)}, f32[1,3,64,256]{3,2,1,0:T(8,128)S(1)}, u32[]{:S(2)}, u32[]{:S(2)}) collective-permute-start(f32[1,3,64,256]{3,2,1,0:T(8,128)S(1)} %add.40), channel_id=1, source_target_pairs={{0,16},{2,18},{4,20},{6,22},{8,24},{10,26},{12,28},{14,30},{16,0},... | collective-permute-start | bytes 589832 | tf_op jit(solution)/shard_map/ppermute | solution.py:358
  122.2 8.1 %collective-permute-start.30 = (f32[1,3,64,256]{3,2,1,0:T(8,128)S(1)}, f32[1,3,64,256]{3,2,1,0:T(8,128)S(1)}, u32[]{:S(2)}, u32[]{:S(2)}) collective-permute-start(f32[1,3,64,256]{3,2,1,0:T(8,128)S(1)} %get-tuple-element.209), channel_id=1, source_target_pairs={{0,8},{2,10},{4,12},{6,14},{8,0},{10,2},{12,4},{14,6},{16,24},{18,... | collective-permute-start | bytes 589832 | tf_op jit(solution)/shard_map/ppermute | solution.py:358
  132.7 7.3 %collective-permute-start.38 = (f32[256,256]{1,0:T(8,128)S(1)}, f32[256,256]{1,0:T(8,128)S(1)}, u32[]{:S(2)}, u32[]{:S(2)}) collective-permute-start(f32[256,256]{1,0:T(8,128)S(1)} %slice_bitcast_fusion), channel_id=1, source_target_pairs={{0,2},{2,0},{4,6},{6,4},{8,10},{10,8},{12,14},{14,12},{16,18},{18,... | collective-permute-start | bytes 786440 | tf_op jit(solution)/shard_map/ppermute | solution.py:358
  133.5 7.3 %collective-permute-start.37 = (f32[256,256]{1,0:T(8,128)S(1)}, f32[256,256]{1,0:T(8,128)S(1)}, u32[]{:S(2)}, u32[]{:S(2)}) collective-permute-start(f32[256,256]{1,0:T(8,128)S(1)} %slice_bitcast_fusion.1), channel_id=1, source_target_pairs={{0,4},{2,6},{4,0},{6,2},{8,12},{10,14},{12,8},{14,10},{16,20},{18,... | collective-permute-start | bytes 786440 | tf_op jit(solution)/shard_map/ppermute | solution.py:358
  135.8 7.4 %collective-permute-start.34 = (f32[1,3,16,256]{3,2,1,0:T(8,128)S(1)}, f32[1,3,16,256]{3,2,1,0:T(8,128)S(1)}, u32[]{:S(2)}, u32[]{:S(2)}) collective-permute-start(f32[1,3,16,256]{3,2,1,0:T(8,128)S(1)} %get-tuple-element.219), channel_id=1, source_target_pairs={{0,2},{2,0},{4,6},{6,4},{8,10},{10,8},{12,14},{14,12},{16,18},{18,... | collective-permute-start | bytes 147464 | tf_op jit(solution)/shard_map/ppermute | solution.py:358
  136.2 7.0 %collective-permute-start.35 = (f32[1,3,16,256]{3,2,1,0:T(8,128)S(1)}, f32[1,3,16,256]{3,2,1,0:T(8,128)S(1)}, u32[]{:S(2)}, u32[]{:S(2)}) collective-permute-start(f32[1,3,16,256]{3,2,1,0:T(8,128)S(1)} %get-tuple-element.220), channel_id=1, source_target_pairs={{0,4},{2,6},{4,0},{6,2},{8,12},{10,14},{12,8},{14,10},{16,20},{18,... | collective-permute-start | bytes 147464 | tf_op jit(solution)/shard_map/ppermute | solution.py:358
  137.5 5.7 %collective-permute-start.36 = (f32[1,3,16,256]{3,2,1,0:T(8,128)S(1)}, f32[1,3,16,256]{3,2,1,0:T(8,128)S(1)}, u32[]{:S(2)}, u32[]{:S(2)}) collective-permute-start(f32[1,3,16,256]{3,2,1,0:T(8,128)S(1)} %get-tuple-element.221), channel_id=1, source_target_pairs={{0,6},{2,4},{4,2},{6,0},{8,14},{10,12},{12,10},{14,8},{16,22},{18,... | collective-permute-start | bytes 147464 | tf_op jit(solution)/shard_map/ppermute | solution.py:358

commit v20 on v14

--- a/solution.py
+++ b/solution.py
@@ -44,7 +44,7 @@
 
 def put_rows(scratch, x):
     for i in range(scratch.shape[0]):
-        scratch[i] = x[:, i * LANES : (i + 1) * LANES]
+        scratch[i, : x.shape[0], :] = x[:, i * LANES : (i + 1) * LANES]
 
 
 def take_head(scratch, head, tokens, heads):
@@ -57,8 +57,8 @@
         scratch[i, pl.ds(head, tokens, stride=heads), :] = x[:, i * LANES : (i + 1) * LANES]
 
 
-def rows_of(scratch):
-    return jnp.concatenate([scratch[i] for i in range(scratch.shape[0])], axis=1)
+def rows_of(scratch, rows):
+    return jnp.concatenate([scratch[i, :rows, :] for i in range(scratch.shape[0])], axis=1)
 
 
 def split_kernel(groups, place, x, *rest):
@@ -290,7 +290,7 @@
     tokens, heads, width = out.shape
     for step, piece in enumerate(pieces):
         put_head(scratch, place[0] ^ step, piece[...], tokens, heads)
-    out[...] = rows_of(scratch).reshape(tokens, heads, width).astype(BF16)
+    out[...] = rows_of(scratch, tokens * heads).reshape(tokens, heads, width).astype(BF16)
 
 
 def join_update_kernel(groups, place, r, *refs):
@@ -300,8 +300,8 @@
         head = place[0] ^ step
         put_head(sk, head, piece[0][...], tokens, heads)
         put_head(sv, head, piece[1][...] * rate_column(r, head), tokens, heads)
-    out_k[...] = rows_of(sk).reshape(tokens, heads, width).astype(BF16)
-    out_v[...] = rows_of(sv).reshape(tokens, heads, width).astype(BF16)
+    out_k[...] = rows_of(sk, tokens * heads).reshape(tokens, heads, width).astype(BF16)
+    out_v[...] = rows_of(sv, tokens * heads).reshape(tokens, heads, width).astype(BF16)
 
 
 def join_rows_kernel(groups, place, *refs):
@@ -374,7 +374,7 @@
     pieces = [shape(tokens, width)] * groups
     slices = [shape(len(m), 3, hidden // depth, width) for m in send_groups(depth)]
     joined = shape(tokens, heads, width, dtype=BF16)
-    scratch = pltpu.VMEM((width // LANES, tokens * heads, LANES), F32)
+    scratch = pltpu.VMEM((width // LANES, tokens * heads + 8 * heads, LANES), F32)
     square = pltpu.VMEM((3, hidden, width), F32)
 
     def split(body, *args):

time: 143 us -> 143 us (level)
  no operation moved by 1% of the time
where the time goes in v20:
time: 143 us
  waiting for transfers between devices  69.5 us (49%)
  starting transfers between devices  47.9 us (33%)
  Pallas kernels  21.1 us (15%)
  local copies, waits for them, and re-layouts  3.56 us (2%)
    ppermute x37, waiting for transfers between devices, move(): lax.ppermute(x, axis, [(c, c ^ step) for c in range(lax.axis_size(axis))])  69.5 us
    ppermute x37, starting transfers between devices, move(): lax.ppermute(x, axis, [(c, c ^ step) for c in range(lax.axis_size(axis))])  47.9 us
    pallas_call x13, Pallas kernels, call(): pl.pallas_call(body, out_shape=out_shape, in_specs=[smem if a.dtype == jn...  21.1 us
  transfers between devices with their start and end apart: 37, of which 22 were waited for; matrix products, arithmetic and copies ran while one was open for 1% of the time, Pallas kernels for 7%

profile of v20, /device:TPU:0, one launch (start us, length us, event | category | flops | bytes accessed | tf_op | source)
XLA Modules:
  0.0 143.2 jit_solution(15706402862580985157)
XLA Ops:
  0.7 1.1 copy-done.5
  1.8 0.9 shard_map.145
  2.8 3.0 %collective-permute-start = (f32[256,256]{1,0:T(8,128)S(1)}, f32[256,256]{1,0:T(8,128)S(1)}, u32[]{:S(2)}, u32[]{:S(2)}) collective-permute-start(f32[256,256]{1,0:T(8,128)S(1)} %get-tuple-element.120), channel_id=1, source_target_pairs={{0,2},{2,0},{4,6},{6,4},{8,10},{10,8},{12,14},{14,12},{16,18},{18,... | collective-permute-start | bytes 786440 | tf_op jit(solution)/shard_map/ppermute | solution.py:341
  5.8 1.5 %collective-permute-start.1 = (f32[256,256]{1,0:T(8,128)S(1)}, f32[256,256]{1,0:T(8,128)S(1)}, u32[]{:S(2)}, u32[]{:S(2)}) collective-permute-start(f32[256,256]{1,0:T(8,128)S(1)} %get-tuple-element.121), channel_id=1, source_target_pairs={{0,4},{2,6},{4,0},{6,2},{8,12},{10,14},{12,8},{14,10},{16,20},{18,... | collective-permute-start | bytes 786440 | tf_op jit(solution)/shard_map/ppermute | solution.py:341
  7.3 1.8 %shard_map.146 = (bf16[256,256]{1,0:T(8,128)(2,1)S(1)}, f32[256,256]{1,0:T(8,128)}, f32[256,256]{1,0:T(8,128)}, f32[256,256]{1,0:T(8,128)S(1)}) custom-call(s32[2]{0:T(128)S(1)} %pad_add_fusion.place, bf16[256,4,256]{2,1,0:T(4,128)(2,1)S(1)} %bitcast.26, f32[4,256]{1,0:T(4,128)S(1)} %bitcast.23), custom_call_target="tpu_custom_call" | custom-call | flops 2147483648 | bytes 1445896 | tf_op jit(solution)/shard_map/pallas_call | solution.py:34
  9.1 0.7 copy-done.7
  9.8 1.9 %collective-permute-start.3 = (f32[256,256]{1,0:T(8,128)}, f32[256,256]{1,0:T(8,128)S(1)}, u32[]{:S(2)}, u32[]{:S(2)}) collective-permute-start(f32[256,256]{1,0:T(8,128)} %get-tuple-element.124), channel_id=1, source_target_pairs={{0,2},{2,0},{4,6},{6,4},{8,10},{10,8},{12,14},{14,12},{16,18},{18,... | collective-permute-start | bytes 786440 | tf_op jit(solution)/shard_map/ppermute | solution.py:341
  11.7 1.5 %collective-permute-start.4 = (f32[256,256]{1,0:T(8,128)}, f32[256,256]{1,0:T(8,128)S(1)}, u32[]{:S(2)}, u32[]{:S(2)}) collective-permute-start(f32[256,256]{1,0:T(8,128)} %get-tuple-element.125), channel_id=1, source_target_pairs={{0,4},{2,6},{4,0},{6,2},{8,12},{10,14},{12,8},{14,10},{16,20},{18,... | collective-permute-start | bytes 786440 | tf_op jit(solution)/shard_map/ppermute | solution.py:341
  13.2 2.7 %collective-permute-start.5 = (f32[256,256]{1,0:T(8,128)S(1)}, f32[256,256]{1,0:T(8,128)S(1)}, u32[]{:S(2)}, u32[]{:S(2)}) collective-permute-start(f32[256,256]{1,0:T(8,128)S(1)} %get-tuple-element.126), channel_id=1, source_target_pairs={{0,6},{2,4},{4,2},{6,0},{8,14},{10,12},{12,10},{14,8},{16,22},{18,... | collective-permute-start | bytes 786440 | tf_op jit(solution)/shard_map/ppermute | solution.py:341
  15.9 1.1 dynamic-slice_bitcast_fusion
  17.1 2.7 %collective-permute-done.1.refs_2_ = f32[256,256]{1,0:T(8,128)S(1)} collective-permute-done((f32[256,256]{1,0:T(8,128)S(1)}, f32[256,256]{1,0:T(8,128)S(1)}, u32[]{:S(2)}, u32[]{:S(2)}) %collective-permute-start.1) | collective-permute-done | bytes 262176 | tf_op jit(solution)/shard_map/ppermute | solution.py:341
  20.1 4.1 %collective-permute-done.3.refs_5_ = f32[256,256]{1,0:T(8,128)S(1)} collective-permute-done((f32[256,256]{1,0:T(8,128)}, f32[256,256]{1,0:T(8,128)S(1)}, u32[]{:S(2)}, u32[]{:S(2)}) %collective-permute-start.3) | collective-permute-done | bytes 262176 | tf_op jit(solution)/shard_map/ppermute | solution.py:341
  24.2 6.2 %collective-permute-done.4.refs_6_ = f32[256,256]{1,0:T(8,128)S(1)} collective-permute-done((f32[256,256]{1,0:T(8,128)}, f32[256,256]{1,0:T(8,128)S(1)}, u32[]{:S(2)}, u32[]{:S(2)}) %collective-permute-start.4) | collective-permute-done | bytes 262176 | tf_op jit(solution)/shard_map/ppermute | solution.py:341
  30.4 2.2 %shard_map.148 = (bf16[4,256,256]{2,1,0:T(8,128)(2,1)S(1)}, bf16[4,256,256]{2,1,0:T(8,128)(2,1)S(1)}, f32[1,3,64,256]{3,2,1,0:T(8,128)S(1)}, f32[1,3,64,256]{3,2...) custom-call(s32[2]{0:T(128)S(1)} %pad_add_fusion.place, ...), custom_call_target="tpu_custom_call" | custom-call | flops 805306368 | bytes 4456456 | tf_op jit(solution)/shard_map/pallas_call | solution.py:34
  32.6 1.6 %collective-permute-start.6 = (f32[1,3,64,256]{3,2,1,0:T(8,128)S(1)}, f32[1,3,64,256]{3,2,1,0:T(8,128)S(1)}, u32[]{:S(2)}, u32[]{:S(2)}) collective-permute-start(f32[1,3,64,256]{3,2,1,0:T(8,128)S(1)} %get-tuple-element.139), channel_id=1, source_target_pairs={{0,8},{2,10},{4,12},{6,14},{8,0},{10,2},{12,4},{14,6},{16,24},{18,... | collective-permute-start | bytes 589832 | tf_op jit(solution)/shard_map/ppermute | solution.py:341
  34.3 0.6 dynamic_slice.14
  34.9 1.9 %shard_map.147 = (f32[2,256,256]{2,1,0:T(8,128)S(1)}, f32[2,256,256]{2,1,0:T(8,128)S(1)}, f32[2,256,256]{2,1,0:T(8,128)S(1)}, f32[2,256,256]{2,1,0:T(8,128)S(1)}, f32[8,256]{1,0:T(8,128)S(1)}) custom-call(s32[2]{0:T(128)S(1)} %pad_add_fusion.place, bf16[256,4,256]{2,1,0:T(4,128)(2,1)S(1)} %bitcast.21, bf16[256,4,256]{2,1,0:T(4,128)(2,1)S(1)} %bitcast.22, ...), custom_call_target="tpu_custom_call" | custom-call | flops 16777216 | bytes 3158028 | tf_op jit(solution)/shard_map/pallas_call | solution.py:34
  36.8 1.3 collective-permute-start.9
  38.1 0.8 collective-permute-start.10
  39.0 2.7 %collective-permute-start.8 = (f32[1,3,64,256]{3,2,1,0:T(8,128)S(1)}, f32[1,3,64,256]{3,2,1,0:T(8,128)S(1)}, u32[]{:S(2)}, u32[]{:S(2)}) collective-permute-start(f32[1,3,64,256]{3,2,1,0:T(8,128)S(1)} %add.40), channel_id=1, source_target_pairs={{0,16},{2,18},{4,20},{6,22},{8,24},{10,26},{12,28},{14,30},{16,0},... | collective-permute-start | bytes 589832 | tf_op jit(solution)/shard_map/ppermute | solution.py:341
  41.6 1.0 collective-permute-start.7
  42.6 6.3 %collective-permute-done.8 = f32[1,3,64,256]{3,2,1,0:T(8,128)S(1)} collective-permute-done((f32[1,3,64,256]{3,2,1,0:T(8,128)S(1)}, f32[1,3,64,256]{3,2,1,0:T(8,128)S(1)}, u32[]{:S(2)}, u32[]{:S(2)}) %collective-permute-start.8) | collective-permute-done | bytes 196640 | tf_op jit(solution)/shard_map/ppermute | solution.py:341
  49.0 0.9 collective-permute-done.7
  50.4 1.1 collective-permute-start.11
  51.5 2.0 %collective-permute-start.13 = (f32[1,3,64,256]{3,2,1,0:T(8,128)S(1)}, f32[1,3,64,256]{3,2,1,0:T(8,128)S(1)}, u32[]{:S(2)}, u32[]{:S(2)}) collective-permute-start(f32[1,3,64,256]{3,2,1,0:T(8,128)S(1)} %add_add_fusion.1.refs_4_), channel_id=1, source_target_pairs={{0,16},{2,18},{4,20},{6,22},{8,24},{10,26},{12,28},{14,30},{16,0},... | collective-permute-start | bytes 589832 | tf_op jit(solution)/shard_map/ppermute | solution.py:341
  53.5 0.8 collective-permute-start.12
  54.3 7.1 %collective-permute-done.13.refs_6_ = f32[1,3,64,256]{3,2,1,0:T(8,128)S(1)} collective-permute-done((f32[1,3,64,256]{3,2,1,0:T(8,128)S(1)}, f32[1,3,64,256]{3,2,1,0:T(8,128)S(1)}, u32[]{:S(2)}, u32[]{:S(2)}) %collective-permute-start.13) | collective-permute-done | bytes 196640 | tf_op jit(solution)/shard_map/ppermute | solution.py:341
  61.6 5.5 %collective-permute-done.14.refs_7_ = f32[1,3,64,256]{3,2,1,0:T(8,128)S(1)} collective-permute-done((f32[1,3,64,256]{3,2,1,0:T(8,128)S(1)}, f32[1,3,64,256]{3,2,1,0:T(8,128)S(1)}, u32[]{:S(2)}, u32[]{:S(2)}) %collective-permute-start.14) | collective-permute-done | bytes 196640 | tf_op jit(solution)/shard_map/ppermute | solution.py:341
  67.1 1.8 %shard_map.149 = (f32[4,256,256]{2,1,0:T(8,128)S(1)}, f32[4,256,256]{2,1,0:T(8,128)S(1)}, bf16[4,256,256]{2,1,0:T(8,128)(2,1)S(1)}, f32[4,256,256]{2,1,0:T(8,128...) custom-call(s32[2]{0:T(128)S(1)} %pad_add_fusion.place, f32[8,256]{1,0:T(8,128)S(1)} %get-tuple-element.129.scale_row, ...), custom_call_target="tpu_custom_call" | custom-call | flops 402653184 | bytes 6963208 | tf_op jit(solution)/shard_map/pallas_call | solution.py:34
  68.9 1.2 collective-permute-done.15
  70.1 1.4 collective-permute-start.16
  71.5 2.3 %collective-permute-done.16 = f32[2,4,256]{2,1,0:T(4,128)S(1)} collective-permute-done((f32[2,4,256]{2,1,0:T(4,128)S(1)}, f32[2,4,256]{2,1,0:T(4,128)S(1)}, u32[]{:S(2)}, u32[]{:S(2)}) %collective-permute-start.16) | collective-permute-done | bytes 8224 | tf_op jit(solution)/shard_map/ppermute | solution.py:341
  73.7 0.5 collective-permute-start.17
  74.2 3.2 %collective-permute-done.17 = f32[2,4,256]{2,1,0:T(4,128)S(1)} collective-permute-done((f32[2,4,256]{2,1,0:T(4,128)S(1)}, f32[2,4,256]{2,1,0:T(4,128)S(1)}, u32[]{:S(2)}, u32[]{:S(2)}) %collective-permute-start.17) | collective-permute-done | bytes 8224 | tf_op jit(solution)/shard_map/ppermute | solution.py:341
  77.4 2.0 %shard_map.150 = (bf16[4,256,256]{2,1,0:T(8,128)(2,1)S(1)}, bf16[4,256,256]{2,1,0:T(8,128)(2,1)S(1)}, f32[1,3,64,256]{3,2,1,0:T(8,128)S(1)}, f32[1,3,64,256]{3,2...) custom-call(s32[2]{0:T(128)S(1)} %pad_add_fusion.place, ...), custom_call_target="tpu_custom_call" | custom-call | flops 805306368 | bytes 8011784 | tf_op jit(solution)/shard_map/pallas_call | solution.py:34
  79.8 5.4 %collective-permute-done.18 = f32[1,3,64,256]{3,2,1,0:T(8,128)S(1)} collective-permute-done((f32[1,3,64,256]{3,2,1,0:T(8,128)S(1)}, f32[1,3,64,256]{3,2,1,0:T(8,128)S(1)}, u32[]{:S(2)}, u32[]{:S(2)}) %collective-permute-start.18) | collective-permute-done | bytes 196640 | tf_op jit(solution)/shard_map/ppermute | solution.py:341
  85.2 0.7 collective-permute-start.20
  85.9 1.8 %collective-permute-start.19 = (f32[1,3,64,256]{3,2,1,0:T(8,128)S(1)}, f32[1,3,64,256]{3,2,1,0:T(8,128)S(1)}, u32[]{:S(2)}, u32[]{:S(2)}) collective-permute-start(f32[1,3,64,256]{3,2,1,0:T(8,128)S(1)} %get-tuple-element.168), channel_id=1, source_target_pairs={{0,8},{2,10},{4,12},{6,14},{8,0},{10,2},{12,4},{14,6},{16,24},{18,... | collective-permute-start | bytes 589832 | tf_op jit(solution)/shard_map/ppermute | solution.py:341
  87.7 8.9 %collective-permute-done.20 = f32[1,3,64,256]{3,2,1,0:T(8,128)S(1)} collective-permute-done((f32[1,3,64,256]{3,2,1,0:T(8,128)S(1)}, f32[1,3,64,256]{3,2,1,0:T(8,128)S(1)}, u32[]{:S(2)}, u32[]{:S(2)}) %collective-permute-start.20) | collective-permute-done | bytes 196640 | tf_op jit(solution)/shard_map/ppermute | solution.py:341
  96.8 0.5 shard_map.151
  97.2 1.6 %collective-permute-start.24 = (f32[256,256]{1,0:T(8,128)S(1)}, f32[256,256]{1,0:T(8,128)S(1)}, u32[]{:S(2)}, u32[]{:S(2)}) collective-permute-start(f32[256,256]{1,0:T(8,128)S(1)} %get-tuple-element.174), channel_id=1, source_target_pairs={{0,2},{2,0},{4,6},{6,4},{8,10},{10,8},{12,14},{14,12},{16,18},{18,... | collective-permute-start | bytes 786440 | tf_op jit(solution)/shard_map/ppermute | solution.py:341
  98.8 2.0 %collective-permute-start.26 = (f32[256,256]{1,0:T(8,128)S(1)}, f32[256,256]{1,0:T(8,128)S(1)}, u32[]{:S(2)}, u32[]{:S(2)}) collective-permute-start(f32[256,256]{1,0:T(8,128)S(1)} %get-tuple-element.176), channel_id=1, source_target_pairs={{0,6},{2,4},{4,2},{6,0},{8,14},{10,12},{12,10},{14,8},{16,22},{18,... | collective-permute-start | bytes 786440 | tf_op jit(solution)/shard_map/ppermute | solution.py:341
  100.8 3.2 %collective-permute-start.21 = (f32[1,3,64,256]{3,2,1,0:T(8,128)S(1)}, f32[1,3,64,256]{3,2,1,0:T(8,128)S(1)}, u32[]{:S(2)}, u32[]{:S(2)}) collective-permute-start(f32[1,3,64,256]{3,2,1,0:T(8,128)S(1)} %add_add_fusion.refs_11_.refs_0_), channel_id=1, source_target_pairs={{0,8},{2,10},{4,12},{6,14},{8,0},{10,2},{12,4},{14,6},{16,24},{18,... | collective-permute-start | bytes 589832 | tf_op jit(solution)/shard_map/ppermute | solution.py:341
  104.0 0.9 collective-permute-done.22.refs_13_
  105.0 1.0 shard_map.153
  106.0 2.0 %collective-permute-done.25.refs_2_ = f32[256,256]{1,0:T(8,128)S(1)} collective-permute-done((f32[256,256]{1,0:T(8,128)S(1)}, f32[256,256]{1,0:T(8,128)S(1)}, u32[]{:S(2)}, u32[]{:S(2)}) %collective-permute-start.25) | collective-permute-done | bytes 262176 | tf_op jit(solution)/shard_map/ppermute | solution.py:341
  108.0 1.7 %shard_map.152 = bf16[256,4,256]{2,1,0:T(4,128)(2,1)} custom-call(s32[2]{0:T(128)S(1)} %pad_add_fusion.place, f32[256,256]{1,0:T(8,128)S(1)} %get-tuple-element.173.refs_0_, f32[256,256]{1,0:T(8,128)S(1)} %collective-permute-done.24.refs_1_, f32[256,256]{1,0:T(8,128)S(1)} %collective-permute-done.25.refs_2_, f32[256,256]{1,0:T(8,128)S(1)} %collective-permute-done.26.refs_3_), custom_call_target="tpu_custom_call" | custom-call | flops 8388608 | bytes 1572872 | tf_op jit(solution)/shard_map/pallas_call | solution.py:34
  109.7 0.8 collective-permute-done.23.refs_14_
  110.6 3.0 %shard_map.154 = (f32[2,256,256]{2,1,0:T(8,128)S(1)}, f32[3,256,256]{2,1,0:T(8,128)S(1)}, f32[3,256,256]{2,1,0:T(8,128)S(1)}, f32[1,3,64,256]{3,2,1,0:T(8,128)S(...) custom-call(s32[2]{0:T(128)S(1)} %pad_add_fusion.place, ...), custom_call_target="tpu_custom_call" | custom-call | flops 1610612736 | bytes 13369352 | tf_op jit(solution)/shard_map/pallas_call | solution.py:34
  113.6 1.5 %collective-permute-start.30 = (f32[3,256,256]{2,1,0:T(8,128)S(1)}, f32[3,256,256]{2,1,0:T(8,128)S(1)}, u32[]{:S(2)}, u32[]{:S(2)}) collective-permute-start(f32[3,256,256]{2,1,0:T(8,128)S(1)} %get-tuple-element.209), channel_id=1, source_target_pairs={{0,2},{2,0},{4,6},{6,4},{8,10},{10,8},{12,14},{14,12},{16,18},{18,... | collective-permute-start | bytes 2359304 | tf_op jit(solution)/shard_map/ppermute | solution.py:341
  115.2 4.1 %collective-permute-start.27 = (f32[1,3,64,256]{3,2,1,0:T(8,128)S(1)}, f32[1,3,64,256]{3,2,1,0:T(8,128)S(1)}, u32[]{:S(2)}, u32[]{:S(2)}) collective-permute-start(f32[1,3,64,256]{3,2,1,0:T(8,128)S(1)} %get-tuple-element.203), channel_id=1, source_target_pairs={{0,8},{2,10},{4,12},{6,14},{8,0},{10,2},{12,4},{14,6},{16,24},{18,... | collective-permute-start | bytes 589832 | tf_op jit(solution)/shard_map/ppermute | solution.py:341
  119.3 4.0 %collective-permute-done.27 = f32[1,3,64,256]{3,2,1,0:T(8,128)S(1)} collective-permute-done((f32[1,3,64,256]{3,2,1,0:T(8,128)S(1)}, f32[1,3,64,256]{3,2,1,0:T(8,128)S(1)}, u32[]{:S(2)}, u32[]{:S(2)}) %collective-permute-start.27) | collective-permute-done | bytes 196640 | tf_op jit(solution)/shard_map/ppermute | solution.py:341
  123.3 1.2 collective-permute-start.29
  124.6 1.8 %collective-permute-start.28 = (f32[1,3,64,256]{3,2,1,0:T(8,128)S(1)}, f32[1,3,64,256]{3,2,1,0:T(8,128)S(1)}, u32[]{:S(2)}, u32[]{:S(2)}) collective-permute-start(f32[1,3,64,256]{3,2,1,0:T(8,128)S(1)} %get-tuple-element.205), channel_id=1, source_target_pairs={{0,8},{2,10},{4,12},{6,14},{8,0},{10,2},{12,4},{14,6},{16,24},{18,... | collective-permute-start | bytes 589832 | tf_op jit(solution)/shard_map/ppermute | solution.py:341
  126.4 5.7 %collective-permute-done.29.refs_3_ = f32[1,3,64,256]{3,2,1,0:T(8,128)S(1)} collective-permute-done((f32[1,3,64,256]{3,2,1,0:T(8,128)S(1)}, f32[1,3,64,256]{3,2,1,0:T(8,128)S(1)}, u32[]{:S(2)}, u32[]{:S(2)}) %collective-permute-start.29) | collective-permute-done | bytes 196640 | tf_op jit(solution)/shard_map/ppermute | solution.py:341
  132.2 1.0 collective-permute-start.36
  133.2 0.8 collective-permute-start.35
  134.0 0.6 shard_map.155
  134.6 1.5 %collective-permute-start.32 = (f32[1,3,16,256]{3,2,1,0:T(8,128)S(1)}, f32[1,3,16,256]{3,2,1,0:T(8,128)S(1)}, u32[]{:S(2)}, u32[]{:S(2)}) collective-permute-start(f32[1,3,16,256]{3,2,1,0:T(8,128)S(1)} %get-tuple-element.215), channel_id=1, source_target_pairs={{0,2},{2,0},{4,6},{6,4},{8,10},{10,8},{12,14},{14,12},{16,18},{18,... | collective-permute-start | bytes 147464 | tf_op jit(solution)/shard_map/ppermute | solution.py:341
  136.1 0.8 collective-permute-start.33
  136.9 1.2 collective-permute-start.34
  138.6 1.0 collective-permute-done.35.refs_3_
  139.6 2.4 %shard_map.156 = (bf16[256,4,256]{2,1,0:T(4,128)(2,1)}, bf16[256,4,256]{2,1,0:T(4,128)(2,1)}) custom-call(s32[2]{0:T(128)S(1)} %pad_add_fusion.place, f32[4,256]{1,0:T(4,128)S(1)} %bitcast.24, f32[2,256,256]{2,1,0:T(8,128)S(1)} %get-tuple-element.218.refs_0_, f32[3,256,256]{2,1,0:T(8,128)S(1)} %collective-permute-done.30.refs_1_, ...), custom_call_target="tpu_custom_call" | custom-call | flops 16777216 | bytes 3674120 | tf_op jit(solution)/shard_map/pallas_call | solution.py:34
  142.0 1.2 shard_map.157
  (57 shorter events, 2.5 us)
Async XLA Ops:
  0.6 15.3 %copy-start = (f32[4,256,256]{2,1,0:T(8,128)S(1)}, f32[4,256,256]{2,1,0:T(8,128)}, u32[]{:S(2)}) copy-start(f32[4,256,256]{2,1,0:T(8,128)} %param.16) | copy-start | bytes 3145732
  0.7 1.1 copy-start.5
  1.8 5.5 %copy-start.6 = (bf16[1,256,4,256]{3,2,1,0:T(4,128)(2,1)S(1)}, bf16[1,256,4,256]{3,2,1,0:T(4,128)(2,1)}, u32[]{:S(2)}) copy-start(bf16[1,256,4,256]{3,2,1,0:T(4,128)(2,1)} %param.12) | copy-start | bytes 1572868
  2.7 4.6 %copy-start.4 = (f32[1,4,256]{2,1,0:T(4,128)S(1)}, f32[1,4,256]{2,1,0:T(4,128)}, u32[]{:S(2)}) copy-start(f32[1,4,256]{2,1,0:T(4,128)} %param.13) | copy-start | bytes 12292
  2.8 10.5 %collective-permute-start = (f32[256,256]{1,0:T(8,128)S(1)}, f32[256,256]{1,0:T(8,128)S(1)}, u32[]{:S(2)}, u32[]{:S(2)}) collective-permute-start(f32[256,256]{1,0:T(8,128)S(1)} %get-tuple-element.120), channel_id=1, source_target_pairs={{0,2},{2,0},{4,6},{6,4},{8,10},{10,8},{12,14},{14,12},{16,18},{18,... | collective-permute-start | bytes 786440 | tf_op jit(solution)/shard_map/ppermute | solution.py:341
  5.8 14.0 %collective-permute-start.1 = (f32[256,256]{1,0:T(8,128)S(1)}, f32[256,256]{1,0:T(8,128)S(1)}, u32[]{:S(2)}, u32[]{:S(2)}) collective-permute-start(f32[256,256]{1,0:T(8,128)S(1)} %get-tuple-element.121), channel_id=1, source_target_pairs={{0,4},{2,6},{4,0},{6,2},{8,12},{10,14},{12,8},{14,10},{16,20},{18,... | collective-permute-start | bytes 786440 | tf_op jit(solution)/shard_map/ppermute | solution.py:341
  7.3 12.8 %collective-permute-start.2 = (f32[256,256]{1,0:T(8,128)S(1)}, f32[256,256]{1,0:T(8,128)S(1)}, u32[]{:S(2)}, u32[]{:S(2)}) collective-permute-start(f32[256,256]{1,0:T(8,128)S(1)} %get-tuple-element.122), channel_id=1, source_target_pairs={{0,6},{2,4},{4,2},{6,0},{8,14},{10,12},{12,10},{14,8},{16,22},{18,... | collective-permute-start | bytes 786440 | tf_op jit(solution)/shard_map/ppermute | solution.py:341
  9.1 0.7 copy-start.7
  9.8 14.4 %collective-permute-start.3 = (f32[256,256]{1,0:T(8,128)}, f32[256,256]{1,0:T(8,128)S(1)}, u32[]{:S(2)}, u32[]{:S(2)}) collective-permute-start(f32[256,256]{1,0:T(8,128)} %get-tuple-element.124), channel_id=1, source_target_pairs={{0,2},{2,0},{4,6},{6,4},{8,10},{10,8},{12,14},{14,12},{16,18},{18,... | collective-permute-start | bytes 786440 | tf_op jit(solution)/shard_map/ppermute | solution.py:341
  11.7 18.7 %collective-permute-start.4 = (f32[256,256]{1,0:T(8,128)}, f32[256,256]{1,0:T(8,128)S(1)}, u32[]{:S(2)}, u32[]{:S(2)}) collective-permute-start(f32[256,256]{1,0:T(8,128)} %get-tuple-element.125), channel_id=1, source_target_pairs={{0,4},{2,6},{4,0},{6,2},{8,12},{10,14},{12,8},{14,10},{16,20},{18,... | collective-permute-start | bytes 786440 | tf_op jit(solution)/shard_map/ppermute | solution.py:341
  13.2 17.1 %collective-permute-start.5 = (f32[256,256]{1,0:T(8,128)S(1)}, f32[256,256]{1,0:T(8,128)S(1)}, u32[]{:S(2)}, u32[]{:S(2)}) collective-permute-start(f32[256,256]{1,0:T(8,128)S(1)} %get-tuple-element.126), channel_id=1, source_target_pairs={{0,6},{2,4},{4,2},{6,0},{8,14},{10,12},{12,10},{14,8},{16,22},{18,... | collective-permute-start | bytes 786440 | tf_op jit(solution)/shard_map/ppermute | solution.py:341
  15.9 14.5 %copy-start.8 = (bf16[256,256]{1,0:T(8,128)(2,1)S(1)}, bf16[256,256]{1,0:T(8,128)(2,1)}, u32[]{:S(2)}) copy-start(bf16[256,256]{1,0:T(8,128)(2,1)} %copy-done.7) | copy-start | bytes 393220
  30.4 4.5 %copy-start.1 = (bf16[1,256,4,256]{3,2,1,0:T(4,128)(2,1)S(1)}, bf16[1,256,4,256]{3,2,1,0:T(4,128)(2,1)}, u32[]{:S(2)}) copy-start(bf16[1,256,4,256]{3,2,1,0:T(4,128)(2,1)} %param.10) | copy-start | bytes 1572868
  30.4 4.5 %copy-start.2 = (bf16[1,256,4,256]{3,2,1,0:T(4,128)(2,1)S(1)}, bf16[1,256,4,256]{3,2,1,0:T(4,128)(2,1)}, u32[]{:S(2)}) copy-start(bf16[1,256,4,256]{3,2,1,0:T(4,128)(2,1)} %param.19) | copy-start | bytes 1572868
  32.6 1.7 %copy-start.9 = (f32[4]{0:T(128)S(1)}, f32[4]{0:T(128)}, u32[]{:S(2)}) copy-start(f32[4]{0:T(128)} %param.14) | copy-start | bytes 52
  32.6 2.2 %copy-start.3 = (f32[4,256]{1,0:T(4,128)S(1)}, f32[4,256]{1,0:T(4,128)}, u32[]{:S(2)}) copy-start(f32[4,256]{1,0:T(4,128)} %gain.1) | copy-start | bytes 12292
  32.6 6.3 %collective-permute-start.6 = (f32[1,3,64,256]{3,2,1,0:T(8,128)S(1)}, f32[1,3,64,256]{3,2,1,0:T(8,128)S(1)}, u32[]{:S(2)}, u32[]{:S(2)}) collective-permute-start(f32[1,3,64,256]{3,2,1,0:T(8,128)S(1)} %get-tuple-element.139), channel_id=1, source_target_pairs={{0,8},{2,10},{4,12},{6,14},{8,0},{10,2},{12,4},{14,6},{16,24},{18,... | collective-permute-start | bytes 589832 | tf_op jit(solution)/shard_map/ppermute | solution.py:341
  36.8 13.1 %collective-permute-start.9 = (f32[2,256,256]{2,1,0:T(8,128)S(1)}, f32[2,256,256]{2,1,0:T(8,128)S(1)}, u32[]{:S(2)}, u32[]{:S(2)}) collective-permute-start(f32[2,256,256]{2,1,0:T(8,128)S(1)} %get-tuple-element.145), channel_id=1, source_target_pairs={{0,2},{2,0},{4,6},{6,4},{8,10},{10,8},{12,14},{14,12},{16,18},{18,... | collective-permute-start | bytes 1572872 | tf_op jit(solution)/shard_map/ppermute | solution.py:341
  38.1 12.2 %collective-permute-start.10 = (f32[2,256,256]{2,1,0:T(8,128)S(1)}, f32[2,256,256]{2,1,0:T(8,128)S(1)}, u32[]{:S(2)}, u32[]{:S(2)}) collective-permute-start(f32[2,256,256]{2,1,0:T(8,128)S(1)} %get-tuple-element.146), channel_id=1, source_target_pairs={{0,4},{2,6},{4,0},{6,2},{8,12},{10,14},{12,8},{14,10},{16,20},{18,... | collective-permute-start | bytes 1572872 | tf_op jit(solution)/shard_map/ppermute | solution.py:341
  39.0 10.0 %collective-permute-start.8 = (f32[1,3,64,256]{3,2,1,0:T(8,128)S(1)}, f32[1,3,64,256]{3,2,1,0:T(8,128)S(1)}, u32[]{:S(2)}, u32[]{:S(2)}) collective-permute-start(f32[1,3,64,256]{3,2,1,0:T(8,128)S(1)} %add.40), channel_id=1, source_target_pairs={{0,16},{2,18},{4,20},{6,22},{8,24},{10,26},{12,28},{14,30},{16,0},... | collective-permute-start | bytes 589832 | tf_op jit(solution)/shard_map/ppermute | solution.py:341
  41.6 8.2 %collective-permute-start.7 = (f32[1,3,64,256]{3,2,1,0:T(8,128)S(1)}, f32[1,3,64,256]{3,2,1,0:T(8,128)S(1)}, u32[]{:S(2)}, u32[]{:S(2)}) collective-permute-start(f32[1,3,64,256]{3,2,1,0:T(8,128)S(1)} %get-tuple-element.141), channel_id=1, source_target_pairs={{0,8},{2,10},{4,12},{6,14},{8,0},{10,2},{12,4},{14,6},{16,24},{18,... | collective-permute-start | bytes 589832 | tf_op jit(solution)/shard_map/ppermute | solution.py:341
  50.4 16.7 %collective-permute-start.11 = (f32[2,256,256]{2,1,0:T(8,128)S(1)}, f32[2,256,256]{2,1,0:T(8,128)S(1)}, u32[]{:S(2)}, u32[]{:S(2)}) collective-permute-start(f32[2,256,256]{2,1,0:T(8,128)S(1)} %get-tuple-element.151), channel_id=1, source_target_pairs={{0,6},{2,4},{4,2},{6,0},{8,14},{10,12},{12,10},{14,8},{16,22},{18,... | collective-permute-start | bytes 1572872 | tf_op jit(solution)/shard_map/ppermute | solution.py:341
  51.5 9.9 %collective-permute-start.13 = (f32[1,3,64,256]{3,2,1,0:T(8,128)S(1)}, f32[1,3,64,256]{3,2,1,0:T(8,128)S(1)}, u32[]{:S(2)}, u32[]{:S(2)}) collective-permute-start(f32[1,3,64,256]{3,2,1,0:T(8,128)S(1)} %add_add_fusion.1.refs_4_), channel_id=1, source_target_pairs={{0,16},{2,18},{4,20},{6,22},{8,24},{10,26},{12,28},{14,30},{16,0},... | collective-permute-start | bytes 589832 | tf_op jit(solution)/shard_map/ppermute | solution.py:341
  53.5 8.2 %collective-permute-start.12 = (f32[1,3,64,256]{3,2,1,0:T(8,128)S(1)}, f32[1,3,64,256]{3,2,1,0:T(8,128)S(1)}, u32[]{:S(2)}, u32[]{:S(2)}) collective-permute-start(f32[1,3,64,256]{3,2,1,0:T(8,128)S(1)} %add_add_fusion.1.refs_4_), channel_id=1, source_target_pairs={{0,8},{2,10},{4,12},{6,14},{8,0},{10,2},{12,4},{14,6},{16,24},{18,... | collective-permute-start | bytes 589832 | tf_op jit(solution)/shard_map/ppermute | solution.py:341
  61.4 5.7 %collective-permute-start.14 = (f32[1,3,64,256]{3,2,1,0:T(8,128)S(1)}, f32[1,3,64,256]{3,2,1,0:T(8,128)S(1)}, u32[]{:S(2)}, u32[]{:S(2)}) collective-permute-start(f32[1,3,64,256]{3,2,1,0:T(8,128)S(1)} %collective-permute-done.13.refs_6_), channel_id=1, source_target_pairs={{0,8},{2,10},{4,12},{6,14},{8,0},{10,2},{12,4},{14,6},{16,24},{18,... | collective-permute-start | bytes 589832 | tf_op jit(solution)/shard_map/ppermute | solution.py:341
  68.9 1.2 collective-permute-start.15
  70.1 3.7 %collective-permute-start.16 = (f32[2,4,256]{2,1,0:T(4,128)S(1)}, f32[2,4,256]{2,1,0:T(4,128)S(1)}, u32[]{:S(2)}, u32[]{:S(2)}) collective-permute-start(f32[2,4,256]{2,1,0:T(4,128)S(1)} %add.42), channel_id=1, source_target_pairs={{0,2},{2,0},{4,6},{6,4},{8,10},{10,8},{12,14},{14,12},{16,18},{18,... | collective-permute-start | bytes 24584 | tf_op jit(solution)/shard_map/ppermute | solution.py:341
  73.7 3.7 %collective-permute-start.17 = (f32[2,4,256]{2,1,0:T(4,128)S(1)}, f32[2,4,256]{2,1,0:T(4,128)S(1)}, u32[]{:S(2)}, u32[]{:S(2)}) collective-permute-start(f32[2,4,256]{2,1,0:T(4,128)S(1)} %add.43), channel_id=1, source_target_pairs={{0,4},{2,6},{4,0},{6,2},{8,12},{10,14},{12,8},{14,10},{16,20},{18,... | collective-permute-start | bytes 24584 | tf_op jit(solution)/shard_map/ppermute | solution.py:341
  79.4 5.7 %collective-permute-start.18 = (f32[1,3,64,256]{3,2,1,0:T(8,128)S(1)}, f32[1,3,64,256]{3,2,1,0:T(8,128)S(1)}, u32[]{:S(2)}, u32[]{:S(2)}) collective-permute-start(f32[1,3,64,256]{3,2,1,0:T(8,128)S(1)} %get-tuple-element.166), channel_id=1, source_target_pairs={{0,8},{2,10},{4,12},{6,14},{8,0},{10,2},{12,4},{14,6},{16,24},{18,... | collective-permute-start | bytes 589832 | tf_op jit(solution)/shard_map/ppermute | solution.py:341
  85.2 11.5 %collective-permute-start.20 = (f32[1,3,64,256]{3,2,1,0:T(8,128)S(1)}, f32[1,3,64,256]{3,2,1,0:T(8,128)S(1)}, u32[]{:S(2)}, u32[]{:S(2)}) collective-permute-start(f32[1,3,64,256]{3,2,1,0:T(8,128)S(1)} %add.46), channel_id=1, source_target_pairs={{0,16},{2,18},{4,20},{6,22},{8,24},{10,26},{12,28},{14,30},{16,0},... | collective-permute-start | bytes 589832 | tf_op jit(solution)/shard_map/ppermute | solution.py:341
  85.9 10.8 %collective-permute-start.19 = (f32[1,3,64,256]{3,2,1,0:T(8,128)S(1)}, f32[1,3,64,256]{3,2,1,0:T(8,128)S(1)}, u32[]{:S(2)}, u32[]{:S(2)}) collective-permute-start(f32[1,3,64,256]{3,2,1,0:T(8,128)S(1)} %get-tuple-element.168), channel_id=1, source_target_pairs={{0,8},{2,10},{4,12},{6,14},{8,0},{10,2},{12,4},{14,6},{16,24},{18,... | collective-permute-start | bytes 589832 | tf_op jit(solution)/shard_map/ppermute | solution.py:341
  96.7 8.2 %collective-permute-start.22 = (f32[1,3,64,256]{3,2,1,0:T(8,128)S(1)}, f32[1,3,64,256]{3,2,1,0:T(8,128)S(1)}, u32[]{:S(2)}, u32[]{:S(2)}) collective-permute-start(f32[1,3,64,256]{3,2,1,0:T(8,128)S(1)} %add_add_fusion.refs_11_.refs_0_), channel_id=1, source_target_pairs={{0,16},{2,18},{4,20},{6,22},{8,24},{10,26},{12,28},{14,30},{16,0},... | collective-permute-start | bytes 589832 | tf_op jit(solution)/shard_map/ppermute | solution.py:341
  97.2 8.8 %collective-permute-start.24 = (f32[256,256]{1,0:T(8,128)S(1)}, f32[256,256]{1,0:T(8,128)S(1)}, u32[]{:S(2)}, u32[]{:S(2)}) collective-permute-start(f32[256,256]{1,0:T(8,128)S(1)} %get-tuple-element.174), channel_id=1, source_target_pairs={{0,2},{2,0},{4,6},{6,4},{8,10},{10,8},{12,14},{14,12},{16,18},{18,... | collective-permute-start | bytes 786440 | tf_op jit(solution)/shard_map/ppermute | solution.py:341
  98.8 9.2 %collective-permute-start.25 = (f32[256,256]{1,0:T(8,128)S(1)}, f32[256,256]{1,0:T(8,128)S(1)}, u32[]{:S(2)}, u32[]{:S(2)}) collective-permute-start(f32[256,256]{1,0:T(8,128)S(1)} %get-tuple-element.175), channel_id=1, source_target_pairs={{0,4},{2,6},{4,0},{6,2},{8,12},{10,14},{12,8},{14,10},{16,20},{18,... | collective-permute-start | bytes 786440 | tf_op jit(solution)/shard_map/ppermute | solution.py:341
  98.8 9.2 %collective-permute-start.26 = (f32[256,256]{1,0:T(8,128)S(1)}, f32[256,256]{1,0:T(8,128)S(1)}, u32[]{:S(2)}, u32[]{:S(2)}) collective-permute-start(f32[256,256]{1,0:T(8,128)S(1)} %get-tuple-element.176), channel_id=1, source_target_pairs={{0,6},{2,4},{4,2},{6,0},{8,14},{10,12},{12,10},{14,8},{16,22},{18,... | collective-permute-start | bytes 786440 | tf_op jit(solution)/shard_map/ppermute | solution.py:341
  100.8 8.9 %collective-permute-start.21 = (f32[1,3,64,256]{3,2,1,0:T(8,128)S(1)}, f32[1,3,64,256]{3,2,1,0:T(8,128)S(1)}, u32[]{:S(2)}, u32[]{:S(2)}) collective-permute-start(f32[1,3,64,256]{3,2,1,0:T(8,128)S(1)} %add_add_fusion.refs_11_.refs_0_), channel_id=1, source_target_pairs={{0,8},{2,10},{4,12},{6,14},{8,0},{10,2},{12,4},{14,6},{16,24},{18,... | collective-permute-start | bytes 589832 | tf_op jit(solution)/shard_map/ppermute | solution.py:341
  104.9 5.7 %collective-permute-start.23 = (f32[1,3,64,256]{3,2,1,0:T(8,128)S(1)}, f32[1,3,64,256]{3,2,1,0:T(8,128)S(1)}, u32[]{:S(2)}, u32[]{:S(2)}) collective-permute-start(f32[1,3,64,256]{3,2,1,0:T(8,128)S(1)} %collective-permute-done.22.refs_13_), channel_id=1, source_target_pairs={{0,8},{2,10},{4,12},{6,14},{8,0},{10,2},{12,4},{14,6},{16,24},{18,... | collective-permute-start | bytes 589832 | tf_op jit(solution)/shard_map/ppermute | solution.py:341
  113.6 18.5 %collective-permute-start.30 = (f32[3,256,256]{2,1,0:T(8,128)S(1)}, f32[3,256,256]{2,1,0:T(8,128)S(1)}, u32[]{:S(2)}, u32[]{:S(2)}) collective-permute-start(f32[3,256,256]{2,1,0:T(8,128)S(1)} %get-tuple-element.209), channel_id=1, source_target_pairs={{0,2},{2,0},{4,6},{6,4},{8,10},{10,8},{12,14},{14,12},{16,18},{18,... | collective-permute-start | bytes 2359304 | tf_op jit(solution)/shard_map/ppermute | solution.py:341
  115.1 17.0 %collective-permute-start.31 = (f32[3,256,256]{2,1,0:T(8,128)S(1)}, f32[3,256,256]{2,1,0:T(8,128)S(1)}, u32[]{:S(2)}, u32[]{:S(2)}) collective-permute-start(f32[3,256,256]{2,1,0:T(8,128)S(1)} %get-tuple-element.210), channel_id=1, source_target_pairs={{0,4},{2,6},{4,0},{6,2},{8,12},{10,14},{12,8},{14,10},{16,20},{18,... | collective-permute-start | bytes 2359304 | tf_op jit(solution)/shard_map/ppermute | solution.py:341
  115.2 8.1 %collective-permute-start.27 = (f32[1,3,64,256]{3,2,1,0:T(8,128)S(1)}, f32[1,3,64,256]{3,2,1,0:T(8,128)S(1)}, u32[]{:S(2)}, u32[]{:S(2)}) collective-permute-start(f32[1,3,64,256]{3,2,1,0:T(8,128)S(1)} %get-tuple-element.203), channel_id=1, source_target_pairs={{0,8},{2,10},{4,12},{6,14},{8,0},{10,2},{12,4},{14,6},{16,24},{18,... | collective-permute-start | bytes 589832 | tf_op jit(solution)/shard_map/ppermute | solution.py:341
  123.3 8.7 %collective-permute-start.29 = (f32[1,3,64,256]{3,2,1,0:T(8,128)S(1)}, f32[1,3,64,256]{3,2,1,0:T(8,128)S(1)}, u32[]{:S(2)}, u32[]{:S(2)}) collective-permute-start(f32[1,3,64,256]{3,2,1,0:T(8,128)S(1)} %add.48), channel_id=1, source_target_pairs={{0,16},{2,18},{4,20},{6,22},{8,24},{10,26},{12,28},{14,30},{16,0},... | collective-permute-start | bytes 589832 | tf_op jit(solution)/shard_map/ppermute | solution.py:341
  124.6 7.5 %collective-permute-start.28 = (f32[1,3,64,256]{3,2,1,0:T(8,128)S(1)}, f32[1,3,64,256]{3,2,1,0:T(8,128)S(1)}, u32[]{:S(2)}, u32[]{:S(2)}) collective-permute-start(f32[1,3,64,256]{3,2,1,0:T(8,128)S(1)} %get-tuple-element.205), channel_id=1, source_target_pairs={{0,8},{2,10},{4,12},{6,14},{8,0},{10,2},{12,4},{14,6},{16,24},{18,... | collective-permute-start | bytes 589832 | tf_op jit(solution)/shard_map/ppermute | solution.py:341
  132.2 6.4 %collective-permute-start.36 = (f32[256,256]{1,0:T(8,128)S(1)}, f32[256,256]{1,0:T(8,128)S(1)}, u32[]{:S(2)}, u32[]{:S(2)}) collective-permute-start(f32[256,256]{1,0:T(8,128)S(1)} %slice_bitcast_fusion), channel_id=1, source_target_pairs={{0,2},{2,0},{4,6},{6,4},{8,10},{10,8},{12,14},{14,12},{16,18},{18,... | collective-permute-start | bytes 786440 | tf_op jit(solution)/shard_map/ppermute | solution.py:341
  133.2 6.4 %collective-permute-start.35 = (f32[256,256]{1,0:T(8,128)S(1)}, f32[256,256]{1,0:T(8,128)S(1)}, u32[]{:S(2)}, u32[]{:S(2)}) collective-permute-start(f32[256,256]{1,0:T(8,128)S(1)} %slice_bitcast_fusion.1), channel_id=1, source_target_pairs={{0,4},{2,6},{4,0},{6,2},{8,12},{10,14},{12,8},{14,10},{16,20},{18,... | collective-permute-start | bytes 786440 | tf_op jit(solution)/shard_map/ppermute | solution.py:341
  134.6 7.3 %collective-permute-start.32 = (f32[1,3,16,256]{3,2,1,0:T(8,128)S(1)}, f32[1,3,16,256]{3,2,1,0:T(8,128)S(1)}, u32[]{:S(2)}, u32[]{:S(2)}) collective-permute-start(f32[1,3,16,256]{3,2,1,0:T(8,128)S(1)} %get-tuple-element.215), channel_id=1, source_target_pairs={{0,2},{2,0},{4,6},{6,4},{8,10},{10,8},{12,14},{14,12},{16,18},{18,... | collective-permute-start | bytes 147464 | tf_op jit(solution)/shard_map/ppermute | solution.py:341
  136.1 5.9 %collective-permute-start.33 = (f32[1,3,16,256]{3,2,1,0:T(8,128)S(1)}, f32[1,3,16,256]{3,2,1,0:T(8,128)S(1)}, u32[]{:S(2)}, u32[]{:S(2)}) collective-permute-start(f32[1,3,16,256]{3,2,1,0:T(8,128)S(1)} %get-tuple-element.216), channel_id=1, source_target_pairs={{0,4},{2,6},{4,0},{6,2},{8,12},{10,14},{12,8},{14,10},{16,20},{18,... | collective-permute-start | bytes 147464 | tf_op jit(solution)/shard_map/ppermute | solution.py:341
  136.9 5.0 %collective-permute-start.34 = (f32[1,3,16,256]{3,2,1,0:T(8,128)S(1)}, f32[1,3,16,256]{3,2,1,0:T(8,128)S(1)}, u32[]{:S(2)}, u32[]{:S(2)}) collective-permute-start(f32[1,3,16,256]{3,2,1,0:T(8,128)S(1)} %get-tuple-element.217), channel_id=1, source_target_pairs={{0,6},{2,4},{4,2},{6,0},{8,14},{10,12},{12,10},{14,8},{16,22},{18,... | collective-permute-start | bytes 147464 | tf_op jit(solution)/shard_map/ppermute | solution.py:341
